TPU v7x, 32 devices: a whole 2x2x4 slice. The times are simulated.
32 devices in a mesh: expert: 8 (over y, x, core), replica: 4 (over z).
Axes of the slice: x: 2, y: 2, z: 4, core: 2. Of those that a mesh axis runs over, the one named last changes fastest.
Arguments:
- tokens: bfloat16 [4096, 2048], P(('replica', 'expert')), parts along dimension 0, may hold values from -6 to 6
- expert_ids: int32 [4096, 8], P(('replica', 'expert')), parts along dimension 0, may hold values from 0 to 127, all different within a row; in each aligned block of 128 rows (0 to 127, 128 to 255, ...) at most 12 rows name the same one
- combine: float32 [4096, 8], P(('replica', 'expert')), parts along dimension 0, may hold values from 0.25 to 1
- old_gate: bfloat16 [1536, 2048], P('expert'), may hold values from -0.125 to 0.125
- old_up: bfloat16 [1536, 2048], P('expert'), may hold values from -0.125 to 0.125
- old_down: bfloat16 [1536, 2048], P('expert'), may hold values from -0.21875 to 0.21875
- move_plan: int32 [2, 3, 96], replicated, may hold values from -1 to 191, as said below
Outputs:
- mixed: bfloat16 [4096, 2048], P(('replica', 'expert')), parts along dimension 0
- arrived: bfloat16 [12, 768, 2048], P('replica', 'expert'), parts along dimension 0
There are 4 independent parts, one for each index of `replica`. A program takes and returns all parts, laid end to end along the dimension named above; an argument that names none is the same for every part. Nothing has to cross between parts.
Inputs may be any that keep to these rules, and one draw needn't show every extreme that they name: `expert_ids`: each row names 8 different experts; among the 128 rows of one device no expert is named more than 12 times, a bound that some block reaches. `move_plan`: in each group the non-negative entries over the three survivors name every one of the leaving device's 192 rows exactly once; each survivor's entries fill its slots from the first, -1 after them; every survivor receives at least 24 rows; in every draw some survivor receives 96 rows.
All inputs are finite; a program needn't handle non-finite values.
Results may differ from a plain program's by a relative error of at most 0.0058.
Values may be sent and summed in bfloat16 or wider, within the bound.
No kernel may reach another device: no remote copies, remote signals or barrier semaphores. Data moves between devices by JAX's collectives and lax.ppermute only.
A program may use at most 128 MiB of HBM per device.

v0:
```python
import jax
import jax.numpy as jnp
from jax import lax
from jax.sharding import PartitionSpec as P

CAP = 12


def shifted(block, axis, distance):
    devices = range(lax.axis_size(axis))
    route = [(i - distance, i) for i in devices if i - distance in devices]
    return lax.ppermute(block, axis, route)


def project(row_block, weights):
    numbers = (((1,), (1,)), ((), ()))
    gate_value = lax.dot_general(row_block, weights[0], numbers, preferred_element_type=jnp.float32)
    up_value = lax.dot_general(row_block, weights[1], numbers, preferred_element_type=jnp.float32)
    hidden = (jax.nn.silu(gate_value) * up_value).astype(jnp.bfloat16)
    return jnp.dot(hidden, weights[2], preferred_element_type=jnp.float32)


def select_rows(resident, plan_row):
    gathered = jnp.take(resident, jnp.maximum(plan_row, 0), axis=1)
    return jnp.where((plan_row >= 0)[None, :, None], gathered, jnp.zeros((), resident.dtype))


def on_device(tokens, expert_ids, combine, old_gate, old_up, old_down, move_plan):
    device_index = lax.axis_index("expert")
    group_index = device_index // 4
    position = device_index % 4
    resident = jnp.stack([old_gate, old_up, old_down], axis=0)
    group_plan = lax.dynamic_index_in_dim(move_plan, group_index, 0, keepdims=False)
    leaving = position == 3
    arrived = jnp.zeros((3, move_plan.shape[2], resident.shape[2]), resident.dtype)
    for offset in (1, 2, 3):
        parcel = jnp.where(
            leaving, select_rows(resident, group_plan[3 - offset]), jnp.zeros((), resident.dtype)
        )
        landed = shifted(parcel, "expert", -offset)
        arrived = arrived + landed
    tok_count, top_count = expert_ids.shape
    model_width = tokens.shape[1]
    experts_here = move_plan.shape[0]
    slot_total = experts_here * CAP
    flat_ids = expert_ids.reshape(-1)
    in_window = flat_ids < experts_here
    onehot = (flat_ids[:, None] == jnp.arange(experts_here, dtype=jnp.int32)[None, :]).astype(
        jnp.int32
    )
    slot_rank = jnp.sum(jnp.cumsum(onehot, axis=0) * onehot, axis=1) - 1
    slot_index = jnp.where(in_window, flat_ids * CAP + slot_rank, slot_total)
    source_token = (
        jnp.zeros((slot_total,), jnp.int32)
        .at[slot_index]
        .set(jnp.arange(flat_ids.shape[0], dtype=jnp.int32) // top_count, mode="drop")
    )
    filled = jnp.zeros((slot_total,), jnp.bool_).at[slot_index].set(True, mode="drop")
    slot_token_rows = jnp.where(
        filled[:, None], jnp.take(tokens, source_token, axis=0), jnp.zeros((), tokens.dtype)
    )
    slot_token_rows = slot_token_rows.reshape(experts_here, CAP, model_width)
    held_rows = jnp.concatenate([resident, arrived], axis=1)
    remaining_device = (jnp.arange(4) < 3).reshape(1, 4, 1, 1)
    departing_rows = jnp.where(
        remaining_device, slot_token_rows[:, None], jnp.zeros((), tokens.dtype)
    ).reshape(experts_here * 4, CAP, model_width)
    incoming = lax.all_to_all(departing_rows, "expert", split_axis=0, concat_axis=0, tiled=True)
    sources = incoming.shape[0]
    slot_count = incoming.shape[1]
    row_block = incoming.reshape(sources * slot_count, model_width)
    partial_value = (
        project(row_block, held_rows).astype(jnp.bfloat16).reshape(sources, slot_count, model_width)
    )
    returned = lax.all_to_all(partial_value, "expert", split_axis=0, concat_axis=0, tiled=True)
    summed = jnp.sum(
        returned.reshape(experts_here, 4, CAP, model_width)[:, :3].astype(jnp.float32), axis=1
    )
    weight_flat = jnp.where(in_window, combine.reshape(-1), jnp.zeros((), combine.dtype))
    picked = jnp.take(
        summed.reshape(slot_total, model_width), jnp.minimum(slot_index, slot_total - 1), axis=0
    )
    mixed = jnp.sum(
        (picked * weight_flat[:, None]).reshape(tok_count, top_count, model_width), axis=1
    )
    return (mixed.astype(jnp.bfloat16), arrived)


def solution(mesh):
    placed = (
        P(("replica", "expert"), None),
        P(("replica", "expert"), None),
        P(("replica", "expert"), None),
        P("expert", None),
        P("expert", None),
        P("expert", None),
        P(),
    )
    return jax.shard_map(
        on_device,
        mesh=mesh,
        in_specs=placed,
        out_specs=(P(("replica", "expert"), None), P("replica", "expert", None)),
        check_vma=False,
    )
```

profile of v0, /device:TPU:0, one launch (start us, length us, event | category | flops | bytes accessed | tf_op | source)
XLA Modules:
  0.0 154.0 jit_solution(3413484184409860233)
XLA Ops:
  0.7 0.8 compare_and_fusion.3
  2.2 2.3 %copy.47 = bf16[1,192,2048]{2,0,1:T(2,128)(2,1)S(1)} copy(bf16[1,192,2048]{2,1,0:T(8,128)(2,1)} %bitcast.69) | data formatting | bytes 1572864 | tf_op jit(solution)/shard_map/stack | solution.py:32
  4.6 2.4 %copy.48 = bf16[1,192,2048]{2,0,1:T(2,128)(2,1)} copy(bf16[1,192,2048]{2,1,0:T(8,128)(2,1)S(1)} %bitcast.70) | data formatting | bytes 1572864 | tf_op jit(solution)/shard_map/stack | solution.py:32
  7.0 2.4 %copy.49 = bf16[1,192,2048]{2,0,1:T(2,128)(2,1)} copy(bf16[1,192,2048]{2,1,0:T(8,128)(2,1)S(1)} %bitcast.71) | data formatting | bytes 1572864 | tf_op jit(solution)/shard_map/stack | solution.py:32
  9.4 7.6 %pad_maximum_fusion.1 = bf16[3,192,2048]{2,0,1:T(4,128)(2,1)} fusion(bf16[1,192,2048]{2,0,1:T(2,128)(2,1)} %copy.49, bf16[1,192,2048]{2,0,1:T(2,128)(2,1)} %copy.48, bf16[1,192,2048]{2,0,1:T(2,128)(2,1)S(1)} %copy.47), kind=kLoop, calls=%fused_computation.11 | loop fusion | flops 7077888 | bytes 4718592 | tf_op jit(solution)/shard_map/stack | solution.py:32
  17.0 3.8 %gather_fusion.2 = bf16[96,3,2048]{2,1,0:T(4,128)(2,1)S(1)} fusion(bf16[3,192,2048]{2,0,1:T(4,128)(2,1)} %pad_maximum_fusion.1, s32[1024]{0:T(1024)S(1)} %pad_clamp_fusion.2), kind=kCustom, calls=%fused_computation.clone | custom fusion | bytes 2359680 | tf_op jit(solution)/shard_map/jit(_take)/gather | solution.py:24
  20.8 1.7 %fusion.4 = bf16[3,96,2048]{2,0,1:T(4,128)(2,1)S(1)} fusion(bf16[96,3,2048]{2,1,0:T(4,128)(2,1)S(1)} %gather_fusion.2, pred[96]{0:T(512)(128)(4,1)S(1)} %get-tuple-element.13, pred[96]{0:T(512)(128)(4,1)S(1)} %get-tuple-element.24, pred[]{:T(512)S(6)} %eq.35), kind=kLoop, calls=%fused_computation.18 | loop fusion | flops 1769472 | bytes 2359489 | tf_op jit(solution)/shard_map/jit(_where)/select_n | solution.py:37
  22.5 1.9 %copy.50 = bf16[3,96,2048]{2,1,0:T(8,128)(2,1)} copy(bf16[3,96,2048]{2,0,1:T(4,128)(2,1)S(1)} %fusion.4) | data formatting | bytes 2359296 | tf_op jit(solution)/shard_map/jit(_where)/select_n | solution.py:37
  24.3 1.5 collective-permute-start
  25.8 3.8 %gather_fusion.3 = bf16[96,3,2048]{2,1,0:T(4,128)(2,1)S(1)} fusion(bf16[3,192,2048]{2,0,1:T(4,128)(2,1)} %pad_maximum_fusion.1, s32[1024]{0:T(1024)S(1)} %pad_clamp_fusion.1), kind=kCustom, calls=%fused_computation.1.clone | custom fusion | bytes 2359680 | tf_op jit(solution)/shard_map/jit(_take)/gather | solution.py:24
  29.6 1.7 %fusion.3 = bf16[3,96,2048]{2,0,1:T(4,128)(2,1)S(1)} fusion(bf16[96,3,2048]{2,1,0:T(4,128)(2,1)S(1)} %gather_fusion.3, pred[96]{0:T(512)(128)(4,1)S(1)} %get-tuple-element.27, pred[96]{0:T(512)(128)(4,1)S(1)} %get-tuple-element.25, pred[]{:T(512)S(6)} %eq.35), kind=kLoop, calls=%fused_computation.16 | loop fusion | flops 1769472 | bytes 2359489 | tf_op jit(solution)/shard_map/jit(_where)/select_n | solution.py:37
  31.3 2.0 %copy.51 = bf16[3,96,2048]{2,1,0:T(8,128)(2,1)} copy(bf16[3,96,2048]{2,0,1:T(4,128)(2,1)S(1)} %fusion.3) | data formatting | bytes 2359296 | tf_op jit(solution)/shard_map/jit(_where)/select_n | solution.py:37
  33.3 1.3 collective-permute-start.1
  34.6 3.8 %gather_fusion.4 = bf16[96,3,2048]{2,1,0:T(4,128)(2,1)S(1)} fusion(bf16[3,192,2048]{2,0,1:T(4,128)(2,1)} %pad_maximum_fusion.1, s32[1024]{0:T(1024)S(1)} %pad_clamp_fusion), kind=kCustom, calls=%fused_computation.2.clone | custom fusion | bytes 2359680 | tf_op jit(solution)/shard_map/jit(_take)/gather | solution.py:24
  38.4 1.7 %fusion.2 = bf16[3,96,2048]{2,0,1:T(4,128)(2,1)S(1)} fusion(bf16[96,3,2048]{2,1,0:T(4,128)(2,1)S(1)} %gather_fusion.4, pred[96]{0:T(512)(128)(4,1)S(1)} %get-tuple-element.29, pred[96]{0:T(512)(128)(4,1)S(1)} %get-tuple-element.26, pred[]{:T(512)S(6)} %eq.35), kind=kLoop, calls=%fused_computation.14 | loop fusion | flops 1769472 | bytes 2359489 | tf_op jit(solution)/shard_map/jit(_where)/select_n | solution.py:37
  40.1 1.9 %copy.54 = bf16[3,96,2048]{2,1,0:T(8,128)(2,1)} copy(bf16[3,96,2048]{2,0,1:T(4,128)(2,1)S(1)} %fusion.2) | data formatting | bytes 2359296 | tf_op jit(solution)/shard_map/jit(_where)/select_n | solution.py:37
  42.0 1.3 collective-permute-start.2
  45.3 4.3 %scatter_custom_fusion.1 = s32[24]{0:T(128)S(1)} fusion(s32[1024]{0:T(1024)S(1)} %bitcast.74, s32[1024]{0:T(1024)S(1)} %add_select_fusion, s32[]{:T(128)} %constant.100.clone.1), kind=kCustom, calls=%fused_computation.79 | custom fusion | bytes 100 | tf_op jit(solution)/shard_map/scatter | solution.py:56
  50.4 4.3 %scatter_custom_fusion = pred[24]{0:T(512)(128)(4,1)S(1)} fusion(s32[1024]{0:T(1024)S(1)} %bitcast.75, pred[1024]{0:T(1024)(128)(4,1)S(1)} %broadcast.237, pred[]{:T(512)} %constant.105.clone.1), kind=kCustom, calls=%fused_computation.73 | custom fusion | bytes 25 | tf_op jit(solution)/shard_map/scatter | solution.py:58
  55.2 32.9 %all_to_all.10 = bf16[8,12,2048]{2,1,0:T(8,128)(2,1)S(1)} all-to-all(bf16[8,12,2048]{2,1,0:T(8,128)(2,1)S(1)} %bitcast_select_fusion.4), channel_id=1, replica_groups=mesh['expert'=8,'replica'=4] {'expert'}, dimensions={0} | all-to-all | bytes 786432 | tf_op jit(solution)/shard_map/all_to_all | solution.py:68
  88.1 0.8 reshape.208
  88.9 8.1 %copy_add_fusion = bf16[3,96,2048]{2,0,1:T(4,128)(2,1)S(1)} fusion(bf16[3,96,2048]{2,1,0:T(8,128)(2,1)} %collective-permute-done.2, bf16[3,96,2048]{2,1,0:T(8,128)(2,1)} %collective-permute-done.1, bf16[3,96,2048]{2,1,0:T(8,128)(2,1)S(1)} %collective-permute-done), kind=kLoop, calls=%fused_computation.19 | loop fusion | flops 1179648 | bytes 4718592 | tf_op jit(solution)/shard_map/add | solution.py:41
  97.1 6.5 %pad_maximum_fusion = bf16[3,288,2048]{2,0,1:T(4,128)(2,1)S(1)} fusion(bf16[3,96,2048]{2,0,1:T(4,128)(2,1)S(1)} %copy_add_fusion, bf16[1,192,2048]{2,0,1:T(2,128)(2,1)S(1)} %copy-done.4, bf16[1,192,2048]{2,0,1:T(2,128)(2,1)S(1)} %copy-done.3, bf16[1,192,2048]{2,0,1:T(2,128)(2,1)S(1)} %copy-done.2), kind=kLoop, calls=%fused_computation.10 | loop fusion | flops 14155776 | bytes 7077888 | tf_op jit(solution)/shard_map/concatenate | solution.py:63
  103.6 6.0 %fusion.28 = (bf16[1,288,2048]{2,0,1:T(2,128)(2,1)}, bf16[1,288,2048]{2,0,1:T(2,128)(2,1)}, bf16[1,288,2048]{2,0,1:T(2,128)(2,1)S(1)}) fusion(bf16[3,288,2048]{2,0,1:T(4,128)(2,1)S(1)} %pad_maximum_fusion), kind=kLoop, calls=%fused_computation.82 | loop fusion | bytes 7077888 | tf_op jit(solution)/shard_map/slice | solution.py:17
  109.6 0.9 fusion.7
  110.5 3.9 %convolution_convert_fusion = bf16[96,2048]{1,0:T(8,128)(2,1)S(1)} fusion(bf16[1,288,2048]{2,0,1:T(2,128)(2,1)} %get-tuple-element.20, f32[96,288]{1,0:T(8,128)S(1)} %fusion.7, bf16[96,2048]{1,0:T(8,128)(2,1)S(1)} %copy-done.7, bf16[1,288,2048]{2,0,1:T(2,128)(2,1)} %get-tuple-element.19), kind=kOutput, calls=%fused_computation.12 | convolution fusion | flops 226854912 | bytes 3256320 | tf_op jit(solution)/shard_map/dot_general | solution.py:20
  114.4 0.9 reshape.209
  115.3 15.3 %all-to-all-start.1 = ((bf16[8,12,2048]{2,1,0:T(8,128)(2,1)}), bf16[8,12,2048]{2,1,0:T(8,128)(2,1)S(1)}, u32[]{:S(2)}, u32[]{:S(2)}) async-start(bf16[8,12,2048]{2,1,0:T(8,128)(2,1)} %reshape.209), calls=%async_computation.1 | async-start | bytes 1048576 | tf_op jit(solution)/shard_map/all_to_all | solution.py:75
  130.9 1.9 %copy.57 = bf16[3,96,2048]{2,1,0:T(8,128)(2,1)} copy(bf16[3,96,2048]{2,0,1:T(4,128)(2,1)S(1)} %copy_add_fusion) | data formatting | bytes 2359296
  132.7 7.6 %all-to-all-done.1 = bf16[8,12,2048]{2,1,0:T(8,128)(2,1)S(1)} async-done(((bf16[8,12,2048]{2,1,0:T(8,128)(2,1)}), bf16[8,12,2048]{2,1,0:T(8,128)(2,1)S(1)}, u32[]{:S(2)}, u32[]{:S(2)}) %all-to-all-start.1) | async-done | bytes 393248 | tf_op jit(solution)/shard_map/all_to_all | solution.py:75
  140.5 6.8 %gather_fusion.1 = f32[1024,2048]{1,0:T(8,128)} fusion(f32[24,2048]{1,0:T(8,128)S(1)} %reshape.211, s32[1024]{0:T(1024)S(1)} %broadcast_clamp_fusion), kind=kCustom, calls=%fused_computation.4 | custom fusion | bytes 16781312 | tf_op jit(solution)/shard_map/jit(_take)/gather | solution.py:80
  147.2 6.8 %fusion.1 = bf16[128,2048]{1,0:T(8,128)(2,1)} fusion(f32[1024,2048]{1,0:T(8,128)} %gather_fusion.1, f32[128,8]{1,0:T(8,128)S(1)} %copy.56, pred[128,8]{1,0:T(8,128)(4,1)S(1)} %copy.44), kind=kLoop, calls=%fused_computation.9 | loop fusion | flops 6029312 | bytes 8918016 | tf_op jit(solution)/shard_map/reduce_sum | solution.py:83
  (66 shorter events, 4.3 us)
Async XLA Ops:
  0.6 49.0 %copy-start = (bf16[128,2048]{1,0:T(8,128)(2,1)S(1)}, bf16[128,2048]{1,0:T(8,128)(2,1)}, u32[]{:S(2)}) copy-start(bf16[128,2048]{1,0:T(8,128)(2,1)} %param.9) | copy-start | bytes 1572868
  0.6 4.0 %copy-start.5 = (bf16[192,2048]{1,0:T(8,128)(2,1)S(1)}, bf16[192,2048]{1,0:T(8,128)(2,1)}, u32[]{:S(2)}) copy-start(bf16[192,2048]{1,0:T(8,128)(2,1)} %param.13) | copy-start | bytes 2359300
  4.6 4.8 %copy-start.1 = (bf16[1,192,2048]{2,0,1:T(2,128)(2,1)}, bf16[1,192,2048]{2,0,1:T(2,128)(2,1)S(1)}, u32[]{:S(2)}) copy-start(bf16[1,192,2048]{2,0,1:T(2,128)(2,1)S(1)} %copy.47) | copy-start | bytes 2359300
  4.6 2.4 %copy-start.6 = (bf16[192,2048]{1,0:T(8,128)(2,1)S(1)}, bf16[192,2048]{1,0:T(8,128)(2,1)}, u32[]{:S(2)}) copy-start(bf16[192,2048]{1,0:T(8,128)(2,1)} %param.14) | copy-start | bytes 2359300
  24.3 64.6 %collective-permute-start = (bf16[3,96,2048]{2,1,0:T(8,128)(2,1)}, bf16[3,96,2048]{2,1,0:T(8,128)(2,1)S(1)}, u32[]{:S(2)}, u32[]{:S(2)}) collective-permute-start(bf16[3,96,2048]{2,1,0:T(8,128)(2,1)} %copy.50), channel_id=1, source_target_pairs={{4,0},{8,4},{12,8},{16,12},{20,16},{24,20},{28,24},{5,1},{9,5},{13... | collective-permute-start | bytes 3538952 | tf_op jit(solution)/shard_map/ppermute | solution.py:12
  33.3 55.6 %collective-permute-start.1 = (bf16[3,96,2048]{2,1,0:T(8,128)(2,1)}, bf16[3,96,2048]{2,1,0:T(8,128)(2,1)}, u32[]{:S(2)}, u32[]{:S(2)}) collective-permute-start(bf16[3,96,2048]{2,1,0:T(8,128)(2,1)} %copy.51), channel_id=1, source_target_pairs={{8,0},{12,4},{16,8},{20,12},{24,16},{28,20},{9,1},{13,5},{17,9},{2... | collective-permute-start | bytes 3538952 | tf_op jit(solution)/shard_map/ppermute | solution.py:12
  40.1 3.2 %copy-start.8 = (s32[128,8]{0,1:T(8,128)S(1)}, s32[128,8]{0,1:T(8,128)}, u32[]{:S(2)}) copy-start(s32[128,8]{0,1:T(8,128)} %param.10) | copy-start | bytes 12292
  42.0 47.0 %collective-permute-start.2 = (bf16[3,96,2048]{2,1,0:T(8,128)(2,1)}, bf16[3,96,2048]{2,1,0:T(8,128)(2,1)}, u32[]{:S(2)}, u32[]{:S(2)}) collective-permute-start(bf16[3,96,2048]{2,1,0:T(8,128)(2,1)} %copy.54), channel_id=1, source_target_pairs={{12,0},{16,4},{20,8},{24,12},{28,16},{13,1},{17,5},{21,9},{25,13},... | collective-permute-start | bytes 3538952 | tf_op jit(solution)/shard_map/ppermute | solution.py:12
  88.9 8.2 %copy-start.2 = (bf16[1,192,2048]{2,0,1:T(2,128)(2,1)S(1)}, bf16[1,192,2048]{2,0,1:T(2,128)(2,1)}, u32[]{:S(2)}) copy-start(bf16[1,192,2048]{2,0,1:T(2,128)(2,1)} %copy-done.1) | copy-start | bytes 2359300
  88.9 8.2 %copy-start.3 = (bf16[1,192,2048]{2,0,1:T(2,128)(2,1)S(1)}, bf16[1,192,2048]{2,0,1:T(2,128)(2,1)}, u32[]{:S(2)}) copy-start(bf16[1,192,2048]{2,0,1:T(2,128)(2,1)} %copy.48) | copy-start | bytes 2359300
  88.9 8.2 %copy-start.4 = (bf16[1,192,2048]{2,0,1:T(2,128)(2,1)S(1)}, bf16[1,192,2048]{2,0,1:T(2,128)(2,1)}, u32[]{:S(2)}) copy-start(bf16[1,192,2048]{2,0,1:T(2,128)(2,1)} %copy.49) | copy-start | bytes 2359300
  103.6 6.0 %copy-start.7 = (bf16[96,2048]{1,0:T(8,128)(2,1)S(1)}, bf16[96,2048]{1,0:T(8,128)(2,1)}, u32[]{:S(2)}) copy-start(bf16[96,2048]{1,0:T(8,128)(2,1)} %reshape.208) | copy-start | bytes 1179652
  114.4 16.2 %copy-start.9 = (f32[128,8]{0,1:T(8,128)S(1)}, f32[128,8]{0,1:T(8,128)}, u32[]{:S(2)}) copy-start(f32[128,8]{0,1:T(8,128)} %param.11) | copy-start | bytes 12292
  115.3 25.1 %all-to-all-start.1 = ((bf16[8,12,2048]{2,1,0:T(8,128)(2,1)}), bf16[8,12,2048]{2,1,0:T(8,128)(2,1)S(1)}, u32[]{:S(2)}, u32[]{:S(2)}) async-start(bf16[8,12,2048]{2,1,0:T(8,128)(2,1)} %reshape.209), calls=%async_computation.1 | async-start | bytes 1048576 | tf_op jit(solution)/shard_map/all_to_all | solution.py:75
where the time goes:
time: 154 us
  local copies, waits for them, and re-layouts  51.4 us (33%)
  other arithmetic  36.9 us (24%)
  blocking collectives  32.9 us (21%)
  starting transfers between devices  19.3 us (13%)
  waiting for transfers between devices  7.63 us (5%)
  matrix products  4.79 us (3%)
    all_to_all x1, blocking collectives, on_device(): lax.all_to_all(departing_rows, 'expert', split_axis=0, concat_axis=0, til...  32.9 us
    all_to_all x1, starting transfers between devices, on_device(): lax.all_to_all(partial_value, 'expert', split_axis=0, concat_axis=0, tile...  15.3 us
    gather x3, local copies, waits for them, and re-layouts, select_rows(): gathered = jnp.take(resident, jnp.maximum(plan_row, 0), axis=1)  11.3 us
    add x1, other arithmetic, on_device(): arrived = arrived + landed  8.13 us
    another operation x1, other arithmetic, on_device(): resident = jnp.stack([old_gate, old_up, old_down], axis=0)  7.63 us
    all_to_all x1, waiting for transfers between devices, on_device(): lax.all_to_all(partial_value, 'expert', split_axis=0, concat_axis=0, tile...  7.62 us
    another operation x3, local copies, waits for them, and re-layouts, on_device(): resident = jnp.stack([old_gate, old_up, old_down], axis=0)  7.09 us
    gather x1, local copies, waits for them, and re-layouts, on_device(): jnp.take(summed.reshape(slot_total, model_width), jnp.minimum(slot_index,...  6.76 us
  transfers between devices with their start and end apart: 4, of which 1 were waited for; matrix products, arithmetic and copies ran while one was open for 19% of the time, Pallas kernels for 0%

commit v1 on v0

v1 whole, which is shorter than its diff:
```python
import functools

import jax
import jax.numpy as jnp
from jax import lax
from jax.experimental import pallas as pl
from jax.experimental.pallas import tpu as pltpu
from jax.sharding import PartitionSpec as P

CAP = 12
SLOTS = 16
GROUP = 4
BF16 = jnp.bfloat16
F32 = jnp.float32
VMEM = pl.BlockSpec(memory_space=pltpu.VMEM)
SMEM = pl.BlockSpec(memory_space=pltpu.SMEM)
HBM = pl.BlockSpec(memory_space=pl.ANY)


def params():
    return pltpu.CompilerParams(vmem_limit_bytes=40 * 1024 * 1024)


def slot_matrix(ids, group, experts):
    tok = ids.shape[1]
    member = []
    for j in range(experts):
        expert = lax.rem(group + j, experts)
        named = jnp.where(ids == expert, 1.0, 0.0)
        member.append(jnp.sum(named, axis=0, keepdims=True))
    member = jnp.concatenate(member, axis=0)
    row = lax.broadcasted_iota(jnp.int32, (tok, tok), 0)
    col = lax.broadcasted_iota(jnp.int32, (tok, tok), 1)
    upto = jnp.where(row <= col, 1.0, 0.0).astype(BF16)
    rank = jnp.dot(member.astype(BF16), upto, preferred_element_type=F32)
    place = jnp.where(member > 0, rank - 1.0, -1.0).astype(jnp.int32)
    slot = lax.broadcasted_iota(jnp.int32, (SLOTS, tok), 0)
    blocks = [jnp.where(slot == place[j : j + 1, :], 1.0, 0.0) for j in range(experts)]
    return jnp.concatenate(blocks, axis=0)


def dispatch_kernel(experts, where_ref, ids_ref, tok_ref, own_ref, other_ref):
    chosen = slot_matrix(ids_ref[...], where_ref[0], experts).astype(BF16)
    rows = jnp.dot(chosen, tok_ref[...], preferred_element_type=F32).astype(BF16)
    own_ref[...] = rows[:SLOTS]
    other_ref[...] = rows[SLOTS:].reshape(other_ref.shape)


def select_kernel(where_ref, plan_ref, gate_ref, up_ref, down_ref, *out_refs):
    group = where_ref[0]
    rows = gate_ref.shape[0]
    most = plan_ref.shape[2]

    @pl.when(where_ref[1] == GROUP - 1)
    def _():
        number = lax.broadcasted_iota(jnp.int32, (rows, most), 0)
        for p in range(GROUP - 1):
            plan = plan_ref[p, pl.ds(group, 1), :]
            pick = jnp.where(number == plan, 1.0, 0.0).astype(BF16)
            for m, ref in enumerate((gate_ref, up_ref, down_ref)):
                out_refs[p][m] = lax.dot_general(
                    pick, ref[...], (((0,), (0,)), ((), ())), preferred_element_type=F32
                ).astype(BF16)


def merge_kernel(where_ref, first_ref, second_ref, third_ref, out_ref, sems):
    position = where_ref[1]
    for p, ref in ((1, second_ref), (2, third_ref)):

        @pl.when(position == p)
        def _():
            copies = [
                pltpu.make_async_copy(ref.at[m], out_ref.at[m], sems.at[m]) for m in range(3)
            ]
            for copy in copies:
                copy.start()
            for copy in copies:
                copy.wait()


def expert_kernel(*refs):
    x_refs, (gate_ref, up_ref, down_ref), out_refs = refs[:4], refs[4:7], refs[7:]
    rows = x_refs[0].shape[0]
    x = jnp.concatenate([ref[...] for ref in x_refs], axis=0)
    numbers = (((1,), (1,)), ((), ()))
    gate_value = lax.dot_general(x, gate_ref[...], numbers, preferred_element_type=F32)
    up_value = lax.dot_general(x, up_ref[...], numbers, preferred_element_type=F32)
    hidden = (gate_value / (1.0 + jnp.exp(-gate_value)) * up_value).astype(BF16)
    partial = jnp.dot(hidden, down_ref[...], preferred_element_type=F32).astype(BF16)
    for k, ref in enumerate(out_refs):
        ref[...] = partial[k * rows : (k + 1) * rows]


def combine_kernel(experts, where_ref, ids_ref, weight_ref, own_ref, back_ref, out_ref):
    ids = ids_ref[...]
    group = where_ref[0]
    chosen = slot_matrix(ids, group, experts)
    scale = []
    for j in range(experts):
        expert = lax.rem(group + j, experts)
        weight = jnp.sum(
            jnp.where(ids == expert, weight_ref[...], 0.0), axis=0, keepdims=True
        )
        block = chosen[j * SLOTS : (j + 1) * SLOTS]
        scale.append(jnp.sum(block * weight, axis=1, keepdims=True))
    scale = jnp.concatenate(scale, axis=0)
    back = back_ref[...].reshape(-1, back_ref.shape[-1]).astype(F32)
    value = jnp.concatenate([own_ref[...], back], axis=0) * scale
    high = value.astype(BF16)
    rest = value - high.astype(F32)
    middle = rest.astype(BF16)
    low = (rest - middle.astype(F32)).astype(BF16)
    parts = jnp.concatenate([high, middle, low], axis=0)
    chosen = chosen.astype(BF16)
    chosen = jnp.concatenate([chosen] * 3, axis=0)
    out_ref[...] = lax.dot_general(
        chosen, parts, (((0,), (0,)), ((), ())), preferred_element_type=F32
    ).astype(BF16)


def on_device(tokens, expert_ids, combine, old_gate, old_up, old_down, move_plan):
    devices = lax.axis_size("expert")
    experts = move_plan.shape[0]
    most = move_plan.shape[2]
    width = tokens.shape[1]
    device = lax.axis_index("expert")
    group, position = device // GROUP, device % GROUP
    where = jnp.stack([group, position]).astype(jnp.int32)
    ids = expert_ids.T
    weights = combine.T
    plan = jnp.transpose(move_plan, (1, 0, 2))

    def shape(*dims, dtype=BF16):
        return jax.ShapeDtypeStruct(dims, dtype)

    def permute(block, target):
        return lax.ppermute(block, "expert", [(i, target(i)) for i in range(devices)])

    own, others = pl.pallas_call(
        functools.partial(dispatch_kernel, experts),
        out_shape=(shape(SLOTS, width), shape(experts - 1, SLOTS, width)),
        in_specs=[SMEM, VMEM, VMEM],
        out_specs=(VMEM, VMEM),
        compiler_params=params(),
        name="dispatch",
    )(where, ids, tokens)

    chosen = pl.pallas_call(
        select_kernel,
        out_shape=[shape(3, most, width)] * 3,
        in_specs=[SMEM, VMEM, VMEM, VMEM, VMEM],
        out_specs=[VMEM] * 3,
        compiler_params=params(),
        name="select",
    )(where, plan, old_gate, old_up, old_down)

    across = [
        permute(others[j - 1], lambda i: (i + GROUP * j) % devices) for j in range(1, experts)
    ]
    here = jnp.concatenate([own] + across, axis=0)
    rows = [here] + [permute(here, lambda i: i ^ k) for k in (1, 2, 3)]

    landed = [
        lax.ppermute(
            chosen[p],
            "expert",
            [(GROUP * e + GROUP - 1, GROUP * e + p) for e in range(experts)],
        )
        for p in range(GROUP - 1)
    ]

    step = min(experts * SLOTS, 32)
    row_spec = pl.BlockSpec((step, width), lambda i: (i, 0))
    whole_spec = pl.BlockSpec(old_gate.shape, lambda i: (0, 0))
    partial = pl.pallas_call(
        expert_kernel,
        grid=(experts * SLOTS // step,),
        out_shape=[shape(experts * SLOTS, width)] * 4,
        in_specs=[row_spec] * 4 + [whole_spec] * 3,
        out_specs=[row_spec] * 4,
        compiler_params=params(),
        name="expert",
    )(*rows, old_gate, old_up, old_down)
    total = partial[0].astype(F32)
    for k in (1, 2, 3):
        total = total + permute(partial[k], lambda i: i ^ k).astype(F32)
    total = total.reshape(experts, SLOTS, width)
    back = jnp.stack(
        [
            permute(total[j].astype(BF16), lambda i: (i - GROUP * j) % devices)
            for j in range(1, experts)
        ]
    )
    mixed = pl.pallas_call(
        functools.partial(combine_kernel, experts),
        out_shape=shape(tokens.shape[0], width),
        in_specs=[SMEM, VMEM, VMEM, VMEM, VMEM],
        out_specs=VMEM,
        compiler_params=params(),
        name="combine",
    )(where, ids, weights, total[0], back)

    arrived = pl.pallas_call(
        merge_kernel,
        out_shape=shape(3, most, width),
        in_specs=[SMEM, HBM, HBM, HBM],
        out_specs=HBM,
        input_output_aliases={1: 0},
        scratch_shapes=[pltpu.SemaphoreType.DMA((3,))],
        compiler_params=params(),
        name="merge",
    )(where, *landed)
    return mixed, arrived


def solution(mesh):
    placed = (
        P(("replica", "expert"), None),
        P(("replica", "expert"), None),
        P(("replica", "expert"), None),
        P("expert", None),
        P("expert", None),
        P("expert", None),
        P(),
    )
    return jax.shard_map(
        on_device,
        mesh=mesh,
        in_specs=placed,
        out_specs=(P(("replica", "expert"), None), P("replica", "expert", None)),
        check_vma=False,
    )
```

time: 154 us -> 61.4 us (0.40)
  local copies, waits for them, and re-layouts: 51.4 us -> 5.14 us
  other arithmetic: 36.9 us -> 0.14 us
  blocking collectives: 32.9 us -> 0 us
  waiting for transfers between devices: 7.63 us -> 37.9 us
  starting transfers between devices: 19.3 us -> 12.3 us
  Pallas kernels: 0 us -> 4.82 us
  matrix products: 4.79 us -> 0 us
    ppermute x3 -> x11, waiting for transfers between devices: 0.01 us -> 37.9 us  [the longest x8 37.9 us: permute(): lax.ppermute(block, 'expert', [(i, target(i)) for i in range(devices)])]
    all_to_all x1 -> x0, blocking collectives: 32.9 us -> none  [on_device(): lax.all_to_all(departing_rows, 'expert', split_axis=0, concat_axis=0, til...]
    gather x6 -> x0, local copies, waits for them, and re-layouts: 18.8 us -> none  [the longest x3 11.3 us: select_rows(): gathered = jnp.take(resident, jnp.maximum(plan_row, 0), axis=1)]
    all_to_all x1 -> x0, starting transfers between devices: 15.3 us -> none  [on_device(): lax.all_to_all(partial_value, 'expert', split_axis=0, concat_axis=0, tile...]
    scatter x2 -> x0, local copies, waits for them, and re-layouts: 8.64 us -> none  [the longest x1 4.34 us: on_device(): jnp.zeros((slot_total,), jnp.bool_).at[slot_index].set(True, mode='drop')]
    another operation x3 -> x1, other arithmetic: 8.4 us -> 0.08 us  [on_device(): where = jnp.stack([group, position]).astype(jnp.int32)]
    ppermute x3 -> x11, starting transfers between devices: 4.02 us -> 12.3 us  [the longest x8 9.52 us: permute(): lax.ppermute(block, 'expert', [(i, target(i)) for i in range(devices)])]
    add x1, other arithmetic: 8.13 us -> 0.06 us  [on_device(): total = total + permute(partial[k], lambda i: i ^ k).astype(F32)]
  transfers between devices with their start and end apart: 4 -> 11, of which waited for: 1 -> 7; matrix products, arithmetic and copies ran while one was open for 19% -> 0% of each run, Pallas kernels for 0% -> 6%
where the time goes in v1:
time: 61.4 us; the launch traced here: 61.1 us
  waiting for transfers between devices  37.9 us (62%)
  starting transfers between devices  12.3 us (20%)
  local copies, waits for them, and re-layouts  5.14 us (8%)
  Pallas kernels  4.82 us (8%)
  between operations  0.78 us (1%)
    ppermute x8, waiting for transfers between devices, permute(): lax.ppermute(block, 'expert', [(i, target(i)) for i in range(devices)])  37.9 us
    ppermute x8, starting transfers between devices, permute(): lax.ppermute(block, 'expert', [(i, target(i)) for i in range(devices)])  9.52 us
    unnamed x18, local copies, waits for them, and re-layouts  5.12 us
    ppermute x3, starting transfers between devices, on_device(): lax.ppermute(chosen[p], 'expert', [(GROUP * e + GROUP - 1, GROUP * e + p)...  2.76 us
    pallas_call x1, Pallas kernels, on_device(): pl.pallas_call(functools.partial(combine_kernel, experts), out_shape=shap...  1.91 us
  transfers between devices with their start and end apart: 11, of which 7 were waited for; matrix products, arithmetic and copies ran while one was open for 0% of the time, Pallas kernels for 6%

profile of v1, /device:TPU:0, one launch (start us, length us, event | category | flops | bytes accessed | tf_op | source)
XLA Modules:
  0.0 61.1 jit_solution(10760614140121053412)
XLA Ops:
  0.6 0.1 pad_add_fusion.where_ref
  0.7 1.1 %copy-done = bf16[192,2048]{1,0:T(8,128)(2,1)S(1)} copy-done((bf16[192,2048]{1,0:T(8,128)(2,1)S(1)}, bf16[192,2048]{1,0:T(8,128)(2,1)}, u32[]{:S(2)}) %copy-start) | copy-done | bytes 786456
  1.9 1.1 %copy-done.2 = bf16[192,2048]{1,0:T(8,128)(2,1)S(1)} copy-done((bf16[192,2048]{1,0:T(8,128)(2,1)S(1)}, bf16[192,2048]{1,0:T(8,128)(2,1)}, u32[]{:S(2)}) %copy-start.2) | copy-done | bytes 786456
  3.0 1.1 %copy-done.3 = bf16[192,2048]{1,0:T(8,128)(2,1)S(1)} copy-done((bf16[192,2048]{1,0:T(8,128)(2,1)S(1)}, bf16[192,2048]{1,0:T(8,128)(2,1)}, u32[]{:S(2)}) %copy-start.3) | copy-done | bytes 786456
  4.1 0.7 %copy-done.7 = s32[2,3,96]{2,0,1:T(2,128)S(1)} copy-done((s32[2,3,96]{2,0,1:T(2,128)S(1)}, s32[2,3,96]{2,0,1:T(2,128)}, u32[]{:S(2)}) %copy-start.7) | copy-done | bytes 2328
  4.8 0.5 select.7
  5.4 0.7 %collective-permute-start.10 = (bf16[3,96,2048]{2,1,0:T(8,128)(2,1)S(1)}, bf16[3,96,2048]{2,1,0:T(8,128)(2,1)S(1)}, u32[]{:S(2)}, u32[]{:S(2)}) collective-permute-start(bf16[3,96,2048]{2,1,0:T(8,128)(2,1)S(1)} %get-tuple-element.19), channel_id=1, source_target_pairs={{12,8},{28,24},{13,9},{29,25},{14,10},{30,26},{15,11},{31,27}} | collective-permute-start | bytes 3538952 | tf_op jit(solution)/shard_map/ppermute | solution.py:164
  6.1 1.3 %collective-permute-start.8 = (bf16[3,96,2048]{2,1,0:T(8,128)(2,1)S(1)}, bf16[3,96,2048]{2,1,0:T(8,128)(2,1)S(1)}, u32[]{:S(2)}, u32[]{:S(2)}) collective-permute-start(bf16[3,96,2048]{2,1,0:T(8,128)(2,1)S(1)} %get-tuple-element.17), channel_id=1, source_target_pairs={{12,0},{28,16},{13,1},{29,17},{14,2},{30,18},{15,3},{31,19}} | collective-permute-start | bytes 3538952 | tf_op jit(solution)/shard_map/ppermute | solution.py:164
  7.4 0.7 %collective-permute-start.9 = (bf16[3,96,2048]{2,1,0:T(8,128)(2,1)S(1)}, bf16[3,96,2048]{2,1,0:T(8,128)(2,1)S(1)}, u32[]{:S(2)}, u32[]{:S(2)}) collective-permute-start(bf16[3,96,2048]{2,1,0:T(8,128)(2,1)S(1)} %get-tuple-element.18), channel_id=1, source_target_pairs={{12,4},{28,20},{13,5},{29,21},{14,6},{30,22},{15,7},{31,23}} | collective-permute-start | bytes 3538952 | tf_op jit(solution)/shard_map/ppermute | solution.py:164
  8.2 0.9 %dispatch.1 = (bf16[16,2048]{1,0:T(8,128)(2,1)S(1)}, bf16[1,16,2048]{2,1,0:T(8,128)(2,1)S(1)}) custom-call(s32[2]{0:T(128)S(1)} %pad_add_fusion.where_ref, s32[8,128]{1,0:T(8,128)S(1)} %bitcast.8, bf16[128,2048]{1,0:T(8,128)(2,1)S(1)} %copy-done.4), custom_call_target="tpu_custom_call" | custom-call | tf_op jit(solution)/shard_map/dispatch/pallas_call | solution.py:139
  9.1 3.0 %collective-permute-start = (bf16[16,2048]{1,0:T(8,128)(2,1)S(1)}, bf16[16,2048]{1,0:T(8,128)(2,1)S(1)}, u32[]{:S(2)}, u32[]{:S(2)}) collective-permute-start(bf16[16,2048]{1,0:T(8,128)(2,1)S(1)} %bitcast.12), channel_id=1, source_target_pairs={{0,16},{4,20},{8,24},{12,28},{16,0},{20,4},{24,8},{28,12},{1,17},{... | collective-permute-start | bytes 196616 | tf_op jit(solution)/shard_map/ppermute | solution.py:137
  12.1 2.2 %collective-permute-done = bf16[16,2048]{1,0:T(8,128)(2,1)S(1)} collective-permute-done((bf16[16,2048]{1,0:T(8,128)(2,1)S(1)}, bf16[16,2048]{1,0:T(8,128)(2,1)S(1)}, u32[]{:S(2)}, u32[]{:S(2)}) %collective-permute-start) | collective-permute-done | bytes 65568 | tf_op jit(solution)/shard_map/ppermute | solution.py:137
  14.3 0.0 collective-permute-start.1
  14.3 3.3 %collective-permute-start.2 = (bf16[32,2048]{1,0:T(8,128)(2,1)S(1)}, bf16[32,2048]{1,0:T(8,128)(2,1)S(1)}, u32[]{:S(2)}, u32[]{:S(2)}) collective-permute-start(bf16[32,2048]{1,0:T(8,128)(2,1)S(1)} %constant_dynamic-update-slice_fusion.refs_0_), channel_id=1, source_target_pairs={{0,8},{4,12},{8,0},{12,4},{16,24},{20,28},{24,16},{28,20},{1,9},{5... | collective-permute-start | bytes 393224 | tf_op jit(solution)/shard_map/ppermute | solution.py:137
  17.6 0.0 collective-permute-done.1.refs_1_
  17.6 0.9 %collective-permute-start.3 = (bf16[32,2048]{1,0:T(8,128)(2,1)S(1)}, bf16[32,2048]{1,0:T(8,128)(2,1)S(1)}, u32[]{:S(2)}, u32[]{:S(2)}) collective-permute-start(bf16[32,2048]{1,0:T(8,128)(2,1)S(1)} %constant_dynamic-update-slice_fusion.refs_0_), channel_id=1, source_target_pairs={{0,12},{4,8},{8,4},{12,0},{16,28},{20,24},{24,20},{28,16},{1,13},{... | collective-permute-start | bytes 393224 | tf_op jit(solution)/shard_map/ppermute | solution.py:137
  18.6 3.5 %collective-permute-done.2.refs_2_ = bf16[32,2048]{1,0:T(8,128)(2,1)S(1)} collective-permute-done((bf16[32,2048]{1,0:T(8,128)(2,1)S(1)}, bf16[32,2048]{1,0:T(8,128)(2,1)S(1)}, u32[]{:S(2)}, u32[]{:S(2)}) %collective-permute-start.2) | collective-permute-done | bytes 131104 | tf_op jit(solution)/shard_map/ppermute | solution.py:137
  22.0 21.8 %collective-permute-done.3.refs_3_ = bf16[32,2048]{1,0:T(8,128)(2,1)S(1)} collective-permute-done((bf16[32,2048]{1,0:T(8,128)(2,1)S(1)}, bf16[32,2048]{1,0:T(8,128)(2,1)S(1)}, u32[]{:S(2)}, u32[]{:S(2)}) %collective-permute-start.3) | collective-permute-done | bytes 131104 | tf_op jit(solution)/shard_map/ppermute | solution.py:137
  43.8 0.9 %expert.1 = (bf16[32,2048]{1,0:T(8,128)(2,1)S(1)}, bf16[32,2048]{1,0:T(8,128)(2,1)S(1)}, bf16[32,2048]{1,0:T(8,128)(2,1)S(1)}, bf16[32,2048]{1,0:T(8,128)(2,1)S(1)}) custom-call(bf16[32,2048]{1,0:T(8,128)(2,1)S(1)} %constant_dynamic-update-slice_fusion.refs_0_, bf16[32,2048]{1,0:T(8,128)(2,1)S(1)} %collective-permute-done.1.refs_1_, ...), custom_call_target="tpu_custom_call" | custom-call | tf_op jit(solution)/shard_map/expert/pallas_call | solution.py:175
  44.8 0.0 copy-start.6
  44.8 0.1 collective-permute-start.4
  44.8 0.1 collective-permute-start.5
  44.9 1.3 %collective-permute-done.4 = bf16[32,2048]{1,0:T(8,128)(2,1)S(1)} collective-permute-done((bf16[32,2048]{1,0:T(8,128)(2,1)S(1)}, bf16[32,2048]{1,0:T(8,128)(2,1)S(1)}, u32[]{:S(2)}, u32[]{:S(2)}) %collective-permute-start.4) | collective-permute-done | bytes 131104 | tf_op jit(solution)/shard_map/ppermute | solution.py:137
  46.2 0.5 collective-permute-start.6
  46.7 4.5 %collective-permute-done.5 = bf16[32,2048]{1,0:T(8,128)(2,1)S(1)} collective-permute-done((bf16[32,2048]{1,0:T(8,128)(2,1)S(1)}, bf16[32,2048]{1,0:T(8,128)(2,1)S(1)}, u32[]{:S(2)}, u32[]{:S(2)}) %collective-permute-start.5) | collective-permute-done | bytes 131104 | tf_op jit(solution)/shard_map/ppermute | solution.py:137
  51.2 1.9 %collective-permute-done.6 = bf16[32,2048]{1,0:T(8,128)(2,1)S(1)} collective-permute-done((bf16[32,2048]{1,0:T(8,128)(2,1)S(1)}, bf16[32,2048]{1,0:T(8,128)(2,1)S(1)}, u32[]{:S(2)}, u32[]{:S(2)}) %collective-permute-start.6) | collective-permute-done | bytes 131104 | tf_op jit(solution)/shard_map/ppermute | solution.py:137
  53.1 0.1 convert_add_fusion
  53.2 1.6 %collective-permute-start.7 = (bf16[16,2048]{1,0:T(8,128)(2,1)S(1)}, bf16[16,2048]{1,0:T(8,128)(2,1)S(1)}, u32[]{:S(2)}, u32[]{:S(2)}) collective-permute-start(bf16[16,2048]{1,0:T(8,128)(2,1)S(1)} %slice.14), channel_id=1, source_target_pairs={{0,16},{4,20},{8,24},{12,28},{16,0},{20,4},{24,8},{28,12},{1,17},{... | collective-permute-start | bytes 196616 | tf_op jit(solution)/shard_map/ppermute | solution.py:137
  54.8 2.7 %collective-permute-done.7 = bf16[16,2048]{1,0:T(8,128)(2,1)S(1)} collective-permute-done((bf16[16,2048]{1,0:T(8,128)(2,1)S(1)}, bf16[16,2048]{1,0:T(8,128)(2,1)S(1)}, u32[]{:S(2)}, u32[]{:S(2)}) %collective-permute-start.7) | collective-permute-done | bytes 65568 | tf_op jit(solution)/shard_map/ppermute | solution.py:137
  57.5 1.9 %combine.1 = bf16[128,2048]{1,0:T(8,128)(2,1)} custom-call(s32[2]{0:T(128)S(1)} %pad_add_fusion.where_ref, s32[8,128]{1,0:T(8,128)S(1)} %bitcast.9, f32[8,128]{1,0:T(8,128)S(1)} %bitcast.10, f32[16,2048]{1,0:T(8,128)S(1)} %slice.11.own_ref, bf16[1,16,2048]{2,1,0:T(8,128)(2,1)S(1)} %bitcast.7), custom_call_target="tpu_custom_call" | custom-call | tf_op jit(solution)/shard_map/combine/pallas_call | solution.py:194
  59.5 0.6 merge.1
  60.1 1.0 %copy.13 = bf16[3,96,2048]{2,1,0:T(8,128)(2,1)} copy(bf16[3,96,2048]{2,1,0:T(8,128)(2,1)S(1)} %merge.1) | data formatting | bytes 2359296
  (18 shorter events, 0.1 us)
Async XLA Ops:
  0.7 1.1 %copy-start = (bf16[192,2048]{1,0:T(8,128)(2,1)S(1)}, bf16[192,2048]{1,0:T(8,128)(2,1)}, u32[]{:S(2)}) copy-start(bf16[192,2048]{1,0:T(8,128)(2,1)} %gate_ref.1) | copy-start | bytes 2359300
  1.9 1.1 %copy-start.2 = (bf16[192,2048]{1,0:T(8,128)(2,1)S(1)}, bf16[192,2048]{1,0:T(8,128)(2,1)}, u32[]{:S(2)}) copy-start(bf16[192,2048]{1,0:T(8,128)(2,1)} %up_ref.1) | copy-start | bytes 2359300
  3.0 1.1 %copy-start.3 = (bf16[192,2048]{1,0:T(8,128)(2,1)S(1)}, bf16[192,2048]{1,0:T(8,128)(2,1)}, u32[]{:S(2)}) copy-start(bf16[192,2048]{1,0:T(8,128)(2,1)} %down_ref.1) | copy-start | bytes 2359300
  4.1 0.7 %copy-start.7 = (s32[2,3,96]{2,0,1:T(2,128)S(1)}, s32[2,3,96]{2,0,1:T(2,128)}, u32[]{:S(2)}) copy-start(s32[2,3,96]{2,0,1:T(2,128)} %param.13) | copy-start | bytes 6916
  4.8 3.4 %copy-start.4 = (bf16[128,2048]{1,0:T(8,128)(2,1)S(1)}, bf16[128,2048]{1,0:T(8,128)(2,1)}, u32[]{:S(2)}) copy-start(bf16[128,2048]{1,0:T(8,128)(2,1)} %tok_ref.1) | copy-start | bytes 1572868
  4.8 3.4 %copy-start.5 = (s32[128,8]{0,1:T(8,128)S(1)}, s32[128,8]{0,1:T(8,128)}, u32[]{:S(2)}) copy-start(s32[128,8]{0,1:T(8,128)} %param.8) | copy-start | bytes 12292
  4.8 39.0 %copy-start.1 = (bf16[192,2048]{1,0:T(8,128)(2,1)S(1)}, bf16[192,2048]{1,0:T(8,128)(2,1)}, u32[]{:S(2)}) copy-start(bf16[192,2048]{1,0:T(8,128)(2,1)} %gate_ref.1) | copy-start | bytes 2359300
  5.4 54.1 %collective-permute-start.10 = (bf16[3,96,2048]{2,1,0:T(8,128)(2,1)S(1)}, bf16[3,96,2048]{2,1,0:T(8,128)(2,1)S(1)}, u32[]{:S(2)}, u32[]{:S(2)}) collective-permute-start(bf16[3,96,2048]{2,1,0:T(8,128)(2,1)S(1)} %get-tuple-element.19), channel_id=1, source_target_pairs={{12,8},{28,24},{13,9},{29,25},{14,10},{30,26},{15,11},{31,27}} | collective-permute-start | bytes 3538952 | tf_op jit(solution)/shard_map/ppermute | solution.py:164
  6.1 53.3 %collective-permute-start.8 = (bf16[3,96,2048]{2,1,0:T(8,128)(2,1)S(1)}, bf16[3,96,2048]{2,1,0:T(8,128)(2,1)S(1)}, u32[]{:S(2)}, u32[]{:S(2)}) collective-permute-start(bf16[3,96,2048]{2,1,0:T(8,128)(2,1)S(1)} %get-tuple-element.17), channel_id=1, source_target_pairs={{12,0},{28,16},{13,1},{29,17},{14,2},{30,18},{15,3},{31,19}} | collective-permute-start | bytes 3538952 | tf_op jit(solution)/shard_map/ppermute | solution.py:164
  7.4 52.0 %collective-permute-start.9 = (bf16[3,96,2048]{2,1,0:T(8,128)(2,1)S(1)}, bf16[3,96,2048]{2,1,0:T(8,128)(2,1)S(1)}, u32[]{:S(2)}, u32[]{:S(2)}) collective-permute-start(bf16[3,96,2048]{2,1,0:T(8,128)(2,1)S(1)} %get-tuple-element.18), channel_id=1, source_target_pairs={{12,4},{28,20},{13,5},{29,21},{14,6},{30,22},{15,7},{31,23}} | collective-permute-start | bytes 3538952 | tf_op jit(solution)/shard_map/ppermute | solution.py:164
  9.1 5.3 %collective-permute-start = (bf16[16,2048]{1,0:T(8,128)(2,1)S(1)}, bf16[16,2048]{1,0:T(8,128)(2,1)S(1)}, u32[]{:S(2)}, u32[]{:S(2)}) collective-permute-start(bf16[16,2048]{1,0:T(8,128)(2,1)S(1)} %bitcast.12), channel_id=1, source_target_pairs={{0,16},{4,20},{8,24},{12,28},{16,0},{20,4},{24,8},{28,12},{1,17},{... | collective-permute-start | bytes 196616 | tf_op jit(solution)/shard_map/ppermute | solution.py:137
  14.3 3.3 %collective-permute-start.1 = (bf16[32,2048]{1,0:T(8,128)(2,1)S(1)}, bf16[32,2048]{1,0:T(8,128)(2,1)S(1)}, u32[]{:S(2)}, u32[]{:S(2)}) collective-permute-start(bf16[32,2048]{1,0:T(8,128)(2,1)S(1)} %constant_dynamic-update-slice_fusion.refs_0_), channel_id=1, source_target_pairs={{0,4},{4,0},{8,12},{12,8},{16,20},{20,16},{24,28},{28,24},{1,5},{5... | collective-permute-start | bytes 393224 | tf_op jit(solution)/shard_map/ppermute | solution.py:137
  14.3 7.7 %collective-permute-start.2 = (bf16[32,2048]{1,0:T(8,128)(2,1)S(1)}, bf16[32,2048]{1,0:T(8,128)(2,1)S(1)}, u32[]{:S(2)}, u32[]{:S(2)}) collective-permute-start(bf16[32,2048]{1,0:T(8,128)(2,1)S(1)} %constant_dynamic-update-slice_fusion.refs_0_), channel_id=1, source_target_pairs={{0,8},{4,12},{8,0},{12,4},{16,24},{20,28},{24,16},{28,20},{1,9},{5... | collective-permute-start | bytes 393224 | tf_op jit(solution)/shard_map/ppermute | solution.py:137
  17.6 26.2 %collective-permute-start.3 = (bf16[32,2048]{1,0:T(8,128)(2,1)S(1)}, bf16[32,2048]{1,0:T(8,128)(2,1)S(1)}, u32[]{:S(2)}, u32[]{:S(2)}) collective-permute-start(bf16[32,2048]{1,0:T(8,128)(2,1)S(1)} %constant_dynamic-update-slice_fusion.refs_0_), channel_id=1, source_target_pairs={{0,12},{4,8},{8,4},{12,0},{16,28},{20,24},{24,20},{28,16},{1,13},{... | collective-permute-start | bytes 393224 | tf_op jit(solution)/shard_map/ppermute | solution.py:137
  44.8 12.8 %copy-start.6 = (f32[128,8]{0,1:T(8,128)S(1)}, f32[128,8]{0,1:T(8,128)}, u32[]{:S(2)}) copy-start(f32[128,8]{0,1:T(8,128)} %param.9) | copy-start | bytes 12292
  44.8 1.4 %collective-permute-start.4 = (bf16[32,2048]{1,0:T(8,128)(2,1)S(1)}, bf16[32,2048]{1,0:T(8,128)(2,1)S(1)}, u32[]{:S(2)}, u32[]{:S(2)}) collective-permute-start(bf16[32,2048]{1,0:T(8,128)(2,1)S(1)} %get-tuple-element.14), channel_id=1, source_target_pairs={{0,4},{4,0},{8,12},{12,8},{16,20},{20,16},{24,28},{28,24},{1,5},{5... | collective-permute-start | bytes 393224 | tf_op jit(solution)/shard_map/ppermute | solution.py:137
  44.8 6.4 %collective-permute-start.5 = (bf16[32,2048]{1,0:T(8,128)(2,1)S(1)}, bf16[32,2048]{1,0:T(8,128)(2,1)S(1)}, u32[]{:S(2)}, u32[]{:S(2)}) collective-permute-start(bf16[32,2048]{1,0:T(8,128)(2,1)S(1)} %get-tuple-element.15), channel_id=1, source_target_pairs={{0,8},{4,12},{8,0},{12,4},{16,24},{20,28},{24,16},{28,20},{1,9},{5... | collective-permute-start | bytes 393224 | tf_op jit(solution)/shard_map/ppermute | solution.py:137
  46.2 6.9 %collective-permute-start.6 = (bf16[32,2048]{1,0:T(8,128)(2,1)S(1)}, bf16[32,2048]{1,0:T(8,128)(2,1)S(1)}, u32[]{:S(2)}, u32[]{:S(2)}) collective-permute-start(bf16[32,2048]{1,0:T(8,128)(2,1)S(1)} %get-tuple-element.16), channel_id=1, source_target_pairs={{0,12},{4,8},{8,4},{12,0},{16,28},{20,24},{24,20},{28,16},{1,13},{... | collective-permute-start | bytes 393224 | tf_op jit(solution)/shard_map/ppermute | solution.py:137
  53.2 4.3 %collective-permute-start.7 = (bf16[16,2048]{1,0:T(8,128)(2,1)S(1)}, bf16[16,2048]{1,0:T(8,128)(2,1)S(1)}, u32[]{:S(2)}, u32[]{:S(2)}) collective-permute-start(bf16[16,2048]{1,0:T(8,128)(2,1)S(1)} %slice.14), channel_id=1, source_target_pairs={{0,16},{4,20},{8,24},{12,28},{16,0},{20,4},{24,8},{28,12},{1,17},{... | collective-permute-start | bytes 196616 | tf_op jit(solution)/shard_map/ppermute | solution.py:137

commit v2 on v1

v2 whole, which is shorter than its diff:
```python
import functools

import jax
import jax.numpy as jnp
from jax import lax
from jax.experimental import pallas as pl
from jax.experimental.pallas import tpu as pltpu
from jax.sharding import PartitionSpec as P

CAP = 12
SLOTS = 16
GROUP = 4
BF16 = jnp.bfloat16
F32 = jnp.float32
VMEM = pl.BlockSpec(memory_space=pltpu.VMEM)
SMEM = pl.BlockSpec(memory_space=pltpu.SMEM)
HBM = pl.BlockSpec(memory_space=pl.ANY)


def params(megabytes=40):
    return pltpu.CompilerParams(vmem_limit_bytes=megabytes * 1024 * 1024)


def slot_matrix(ids, group, experts):
    tok = ids.shape[1]
    member = []
    for j in range(experts):
        expert = lax.rem(group + j, experts)
        named = jnp.where(ids == expert, 1.0, 0.0)
        member.append(jnp.sum(named, axis=0, keepdims=True))
    member = jnp.concatenate(member, axis=0)
    row = lax.broadcasted_iota(jnp.int32, (tok, tok), 0)
    col = lax.broadcasted_iota(jnp.int32, (tok, tok), 1)
    upto = jnp.where(row <= col, 1.0, 0.0).astype(BF16)
    rank = jnp.dot(member.astype(BF16), upto, preferred_element_type=F32)
    place = jnp.where(member > 0, rank - 1.0, -1.0).astype(jnp.int32)
    slot = lax.broadcasted_iota(jnp.int32, (SLOTS, tok), 0)
    blocks = [jnp.where(slot == place[j : j + 1, :], 1.0, 0.0) for j in range(experts)]
    return jnp.concatenate(blocks, axis=0)


def dispatch_kernel(experts, where_ref, ids_ref, tok_hbm, *refs):
    out_refs, (tok_ref, sem) = refs[:experts], refs[experts:]
    copy = pltpu.make_async_copy(tok_hbm, tok_ref, sem)
    copy.start()
    chosen = slot_matrix(ids_ref[...], where_ref[0], experts).astype(BF16)
    copy.wait()
    rows = jnp.dot(chosen, tok_ref[...], preferred_element_type=F32).astype(BF16)
    for j, ref in enumerate(out_refs):
        ref[...] = rows[j * SLOTS : (j + 1) * SLOTS]


def pick_rows(number, plan, held_ref):
    pick = jnp.where(number == plan, 1.0, 0.0).astype(BF16)
    return lax.dot_general(
        pick, held_ref[...], (((0,), (0,)), ((), ())), preferred_element_type=F32
    ).astype(BF16)


def select_kernel(wanted, where_ref, plan_ref, gate_hbm, up_hbm, down_hbm, after_ref, *refs):
    out_refs, (held_ref, sems) = refs[: len(wanted)], refs[len(wanted) :]
    group = where_ref[0]
    rows = held_ref.shape[1]
    parity = where_ref[2]

    @pl.when(where_ref[1] == GROUP - 1)
    def _():
        copies = [
            pltpu.make_async_copy(ref, held_ref.at[m], sems.at[m])
            for m, ref in enumerate((gate_hbm, up_hbm, down_hbm))
        ]
        for copy in copies:
            copy.start()
        plans = []
        for survivor, first, count in wanted:
            plan = plan_ref[survivor, pl.ds(group, 1), :]
            if first is None:
                plan = jnp.where(parity == 0, plan[:, :count], plan[:, count : 2 * count])
            else:
                plan = plan[:, first : first + count]
            plans.append(plan)
        width = sum(count for _, _, count in wanted)
        number = lax.broadcasted_iota(jnp.int32, (rows, width), 0)
        pick = jnp.where(number == jnp.concatenate(plans, axis=1), 1.0, 0.0).astype(BF16)
        for m, copy in enumerate(copies):
            copy.wait()
            found = lax.dot_general(
                pick, held_ref[m], (((0,), (0,)), ((), ())), preferred_element_type=F32
            ).astype(BF16)
            start = 0
            for (_, _, count), ref in zip(wanted, out_refs):
                ref[m] = found[start : start + count]
                start += count


def merge_kernel(part, where_ref, *refs):
    shared, swapped, straight, near = refs[0:2], refs[2:4], refs[4:6], refs[6]
    out_ref, sems = refs[7:]
    position, parity = where_ref[1], where_ref[2]

    def move(pieces):
        copies = []
        for ref, first, count in pieces:
            for m in range(3):
                copies.append(
                    pltpu.make_async_copy(
                        ref.at[m], out_ref.at[m, pl.ds(first, count)], sems.at[len(copies)]
                    )
                )
        for copy in copies:
            copy.start()
        for copy in copies:
            copy.wait()

    for p in range(2):
        for even in range(2):
            mine = position == 1 if p == 1 else jnp.logical_or(position == 0, position == 3)

            @pl.when(jnp.logical_and(mine, parity == even))
            def _():
                move(
                    [
                        (shared[p], part * even, part),
                        (swapped[p], part * (1 - even), part),
                        (straight[p], 2 * part, out_ref.shape[1] - 2 * part),
                    ]
                )

    @pl.when(position == 2)
    def _():
        move([(near, 0, out_ref.shape[1])])


def expert_kernel(pieces, *refs):
    x_refs, (gate_ref, up_ref, down_ref), out_refs = (
        refs[:pieces],
        refs[pieces : pieces + 3],
        refs[pieces + 3 :],
    )
    x = jnp.concatenate([ref[...] for ref in x_refs], axis=0)
    numbers = (((1,), (1,)), ((), ()))
    gate_value = lax.dot_general(x, gate_ref[...], numbers, preferred_element_type=F32)
    up_value = lax.dot_general(x, up_ref[...], numbers, preferred_element_type=F32)
    hidden = (gate_value / (1.0 + jnp.exp(-gate_value)) * up_value).astype(BF16)
    partial = jnp.dot(hidden, down_ref[...], preferred_element_type=F32).astype(BF16)
    for k, ref in enumerate(out_refs):
        ref[...] = partial[k * SLOTS : (k + 1) * SLOTS]


def combine_kernel(experts, where_ref, ids_ref, weight_ref, *refs):
    piece_refs, out_ref = refs[: experts * GROUP], refs[experts * GROUP]
    ids = ids_ref[...]
    group = where_ref[0]
    tok = ids.shape[0]
    row = lax.broadcasted_iota(jnp.int32, (tok, tok), 0)
    col = lax.broadcasted_iota(jnp.int32, (tok, tok), 1)
    upto = jnp.where(col <= row, 1.0, 0.0).astype(BF16)
    slot = lax.broadcasted_iota(jnp.int32, (tok, GROUP * SLOTS), 1) % SLOTS
    mixed = None
    for j in range(experts):
        named = ids == lax.rem(group + j, experts)
        member = jnp.sum(jnp.where(named, 1.0, 0.0), axis=1, keepdims=True)
        weight = jnp.sum(jnp.where(named, weight_ref[...], 0.0), axis=1, keepdims=True)
        rank = jnp.dot(upto, member.astype(BF16), preferred_element_type=F32)
        place = jnp.where(member > 0, rank - 1.0, -1.0).astype(jnp.int32)
        chosen = jnp.where(slot == place, 1.0, 0.0).astype(BF16)
        parts = [ref[...] for ref in piece_refs[j * GROUP : (j + 1) * GROUP]]
        found = jnp.dot(
            chosen, jnp.concatenate(parts, axis=0), preferred_element_type=F32
        )
        term = weight * found
        mixed = term if mixed is None else mixed + term
    out_ref[...] = mixed.astype(BF16)


def on_device(tokens, expert_ids, combine, old_gate, old_up, old_down, move_plan):
    devices = lax.axis_size("expert")
    replicas = lax.axis_size("replica")
    experts = move_plan.shape[0]
    most = move_plan.shape[2]
    width = tokens.shape[1]
    device = lax.axis_index("expert")
    group, position = device // GROUP, device % GROUP
    parity = lax.axis_index("replica") % 2
    where = jnp.stack([group, position, parity]).astype(jnp.int32)
    plan = jnp.transpose(move_plan, (1, 0, 2))
    weights = (old_gate, old_up, old_down)
    part = most // 3
    rest = most - 2 * part

    def shape(*dims, dtype=BF16):
        return jax.ShapeDtypeStruct(dims, dtype)

    def send(block, j, k):
        route = []
        for i in range(devices):
            g, p = i // GROUP, i % GROUP
            route.append((i, GROUP * ((g + j) % experts) + (p ^ k)))
        return lax.ppermute(block, "expert", route)

    def migrate(block, survivor):
        route = [(GROUP * e + GROUP - 1, GROUP * e + survivor) for e in range(experts)]
        return lax.ppermute(block, "expert", route)

    def swap(block, survivor):
        route = []
        for r in range(replicas):
            for e in range(experts):
                i = GROUP * e + survivor
                route.append((i * replicas + r, i * replicas + (r ^ 1)))
        return lax.ppermute(block, ("expert", "replica"), route)

    def select(wanted, after, name):
        return pl.pallas_call(
            functools.partial(select_kernel, wanted),
            out_shape=[shape(3, count, width) for _, _, count in wanted],
            in_specs=[SMEM, VMEM, HBM, HBM, HBM, HBM],
            out_specs=[VMEM] * len(wanted),
            scratch_shapes=[
                pltpu.VMEM((3,) + old_gate.shape, BF16),
                pltpu.SemaphoreType.DMA((3,)),
            ],
            compiler_params=params(60),
            name=name,
        )(where, plan, *weights, after)

    parcels = pl.pallas_call(
        functools.partial(dispatch_kernel, experts),
        out_shape=[shape(SLOTS, width)] * experts,
        in_specs=[SMEM, VMEM, HBM],
        out_specs=[VMEM] * experts,
        scratch_shapes=[pltpu.VMEM(tokens.shape, BF16), pltpu.SemaphoreType.DMA],
        compiler_params=params(60),
        name="dispatch",
    )(where, expert_ids.T, tokens)

    pairs = [(j, k) for j in range(experts) for k in range(GROUP)]
    rows = [parcels[0]] + [send(parcels[j], j, k) for j, k in pairs[1:]]

    first = select(
        [(0, None, part), (1, None, part), (2, 0, most)], parcels[0], "select_first"
    )
    shared = [migrate(first[p], p) for p in range(2)]
    near = migrate(first[2], 2)

    pieces = len(pairs)
    partial = pl.pallas_call(
        functools.partial(expert_kernel, pieces),
        out_shape=[shape(SLOTS, width)] * pieces,
        in_specs=[VMEM] * (pieces + 3),
        out_specs=[VMEM] * pieces,
        compiler_params=params(),
        name="expert",
    )(*rows, *weights)
    back = [partial[0]] + [
        send(block, -j, k) for (j, k), block in zip(pairs[1:], partial[1:])
    ]

    last = select([(0, 2 * part, rest), (1, 2 * part, rest)], back[1], "select_last")
    straight = [migrate(last[p], p) for p in range(2)]
    swapped = [swap(shared[p], p) for p in range(2)]

    mixed = pl.pallas_call(
        functools.partial(combine_kernel, experts),
        out_shape=shape(tokens.shape[0], width),
        in_specs=[SMEM, VMEM, VMEM] + [VMEM] * pieces,
        out_specs=VMEM,
        compiler_params=params(),
        name="combine",
    )(where, expert_ids, combine, *back)

    arrived = pl.pallas_call(
        functools.partial(merge_kernel, part),
        out_shape=shape(3, most, width),
        in_specs=[SMEM] + [HBM] * 7,
        out_specs=HBM,
        scratch_shapes=[pltpu.SemaphoreType.DMA((9,))],
        compiler_params=params(),
        name="merge",
    )(where, *shared, *swapped, *straight, near)
    return mixed, arrived


def solution(mesh):
    placed = (
        P(("replica", "expert"), None),
        P(("replica", "expert"), None),
        P(("replica", "expert"), None),
        P("expert", None),
        P("expert", None),
        P("expert", None),
        P(),
    )
    return jax.shard_map(
        on_device,
        mesh=mesh,
        in_specs=placed,
        out_specs=(P(("replica", "expert"), None), P("replica", "expert", None)),
        check_vma=False,
    )
```

time: 61.4 us -> 78.5 us (1.28)
  the two profiles are of different devices: /device:TPU:0 before, /device:TPU:1 now
where the time goes in v2:
time: 78.5 us; the launch traced here: 78 us
  starting transfers between devices  25.3 us (32%)
  Pallas kernels  23.9 us (30%)
  waiting for transfers between devices  22.5 us (29%)
  local copies, waits for them, and re-layouts  4.82 us (6%)
  between operations  0.88 us (1%)
    ppermute x14, waiting for transfers between devices, send(): return lax.ppermute(block, 'expert', route)  19.2 us
    ppermute x14, starting transfers between devices, send(): return lax.ppermute(block, 'expert', route)  16.7 us
    pallas_call x1, Pallas kernels, on_device(): pl.pallas_call(functools.partial(merge_kernel, part), out_shape=shape(3,...  13.7 us
    unnamed x32, local copies, waits for them, and re-layouts  4.82 us
    ppermute x5, starting transfers between devices, migrate(): return lax.ppermute(block, 'expert', route)  4.65 us
    ppermute x2, starting transfers between devices, swap(): return lax.ppermute(block, ('expert', 'replica'), route)  3.89 us
    pallas_call x2, Pallas kernels, select(): pl.pallas_call(functools.partial(select_kernel, wanted), out_shape=[shape...  3.79 us
    pallas_call x1, Pallas kernels, on_device(): pl.pallas_call(functools.partial(dispatch_kernel, experts), out_shape=[sh...  2.61 us
  transfers between devices with their start and end apart: 21, of which 10 were waited for; matrix products, arithmetic and copies ran while one was open for 0% of the time, Pallas kernels for 7%

profile of v2, /device:TPU:1, one launch (start us, length us, event | category | flops | bytes accessed | tf_op | source)
XLA Modules:
  0.0 78.0 jit_solution(10553180507444106091)
XLA Ops:
  1.3 2.6 %dispatch.1 = (bf16[16,2048]{1,0:T(8,128)(2,1)}, bf16[16,2048]{1,0:T(8,128)(2,1)}) custom-call(s32[3]{0:T(128)} %pad_add_fusion.where_ref, s32[8,128]{1,0:T(8,128)} %bitcast.5, bf16[128,2048]{1,0:T(8,128)(2,1)} %tok_hbm.1), custom_call_target="tpu_custom_call" | custom-call | tf_op jit(solution)/shard_map/dispatch/pallas_call | solution.py:227
  4.0 2.2 %select_first.1 = (bf16[3,32,2048]{2,1,0:T(8,128)(2,1)}, bf16[3,32,2048]{2,1,0:T(8,128)(2,1)}, bf16[3,96,2048]{2,1,0:T(8,128)(2,1)}) custom-call(s32[3]{0:T(128)} %pad_add_fusion.where_ref, s32[3,2,96]{2,1,0:T(2,128)} %bitcast.6, bf16[192,2048]{1,0:T(8,128)(2,1)} %gate_hbm.3, bf16[192,2048]{1,0:T(8,128)(2,1)} %up_hbm.3, bf16[192,2048]{1,0:T(8,128)(2,1)} %down_hbm.3, ...), custom_call_target="tpu_custom_call" | custom-call | tf_op jit(solution)/shard_map/select_first/pallas_call | solution.py:214
  6.1 0.7 collective-permute-start.20
  7.0 4.8 %collective-permute-start.1 = (bf16[16,2048]{1,0:T(8,128)(2,1)S(1)}, bf16[16,2048]{1,0:T(8,128)(2,1)S(1)}, u32[]{:S(2)}, u32[]{:S(2)}) collective-permute-start(bf16[16,2048]{1,0:T(8,128)(2,1)S(1)} %copy-done.5), channel_id=1, source_target_pairs={{0,8},{4,12},{8,0},{12,4},{16,24},{20,28},{24,16},{28,20},{1,9},{5... | collective-permute-start | bytes 196616 | tf_op jit(solution)/shard_map/ppermute | solution.py:199
  12.2 1.2 %collective-permute-start.3 = (bf16[16,2048]{1,0:T(8,128)(2,1)}, bf16[16,2048]{1,0:T(8,128)(2,1)S(1)}, u32[]{:S(2)}, u32[]{:S(2)}) collective-permute-start(bf16[16,2048]{1,0:T(8,128)(2,1)} %get-tuple-element.18), channel_id=1, source_target_pairs={{0,16},{4,20},{8,24},{12,28},{16,0},{20,4},{24,8},{28,12},{1,17},{... | collective-permute-start | bytes 196616 | tf_op jit(solution)/shard_map/ppermute | solution.py:199
  13.4 0.8 collective-permute-start.4
  14.2 0.7 collective-permute-start.14
  14.9 1.6 %collective-permute-done.2.refs_3_ = bf16[16,2048]{1,0:T(8,128)(2,1)S(1)} collective-permute-done((bf16[16,2048]{1,0:T(8,128)(2,1)S(1)}, bf16[16,2048]{1,0:T(8,128)(2,1)S(1)}, u32[]{:S(2)}, u32[]{:S(2)}) %collective-permute-start.2) | collective-permute-done | bytes 65568 | tf_op jit(solution)/shard_map/ppermute | solution.py:199
  16.5 1.3 %collective-permute-start.15 = (bf16[3,32,2048]{2,1,0:T(8,128)(2,1)}, bf16[3,32,2048]{2,1,0:T(8,128)(2,1)}, u32[]{:S(2)}, u32[]{:S(2)}) collective-permute-start(bf16[3,32,2048]{2,1,0:T(8,128)(2,1)} %get-tuple-element.28), channel_id=1, source_target_pairs={{12,4},{28,20},{13,5},{29,21},{14,6},{30,22},{15,7},{31,23}} | collective-permute-start | bytes 1179656 | tf_op jit(solution)/shard_map/ppermute | solution.py:203
  17.8 3.8 %collective-permute-start.5 = (bf16[16,2048]{1,0:T(8,128)(2,1)}, bf16[16,2048]{1,0:T(8,128)(2,1)S(1)}, u32[]{:S(2)}, u32[]{:S(2)}) collective-permute-start(bf16[16,2048]{1,0:T(8,128)(2,1)} %get-tuple-element.18), channel_id=1, source_target_pairs={{0,24},{4,28},{8,16},{12,20},{16,8},{20,12},{24,0},{28,4},{1,25},{... | collective-permute-start | bytes 196616 | tf_op jit(solution)/shard_map/ppermute | solution.py:199
  21.6 9.2 %collective-permute-done.5.refs_6_ = bf16[16,2048]{1,0:T(8,128)(2,1)S(1)} collective-permute-done((bf16[16,2048]{1,0:T(8,128)(2,1)}, bf16[16,2048]{1,0:T(8,128)(2,1)S(1)}, u32[]{:S(2)}, u32[]{:S(2)}) %collective-permute-start.5) | collective-permute-done | bytes 65568 | tf_op jit(solution)/shard_map/ppermute | solution.py:199
  30.8 1.5 %expert.1 = (bf16[16,2048]{1,0:T(8,128)(2,1)S(1)}, bf16[16,2048]{1,0:T(8,128)(2,1)S(1)}, bf16[16,2048]{1,0:T(8,128)(2,1)}, bf16[16,2048]{1,0:T(8,128)(2,1)}, bf1...) custom-call(bf16[16,2048]{1,0:T(8,128)(2,1)S(1)} %copy-done.5, ...), custom_call_target="tpu_custom_call" | custom-call | tf_op jit(solution)/shard_map/expert/pallas_call | solution.py:247
  32.3 1.4 %collective-permute-start.7 = (bf16[16,2048]{1,0:T(8,128)(2,1)S(1)}, bf16[16,2048]{1,0:T(8,128)(2,1)S(1)}, u32[]{:S(2)}, u32[]{:S(2)}) collective-permute-start(bf16[16,2048]{1,0:T(8,128)(2,1)S(1)} %get-tuple-element.20), channel_id=1, source_target_pairs={{0,4},{4,0},{8,12},{12,8},{16,20},{20,16},{24,28},{28,24},{1,5},{5... | collective-permute-start | bytes 196616 | tf_op jit(solution)/shard_map/ppermute | solution.py:199
  33.9 0.7 collective-permute-done.7.refs_1_.after_ref
  34.6 0.7 collective-permute-start.11
  35.3 2.1 %collective-permute-done.10.refs_4_ = bf16[16,2048]{1,0:T(8,128)(2,1)S(1)} collective-permute-done((bf16[16,2048]{1,0:T(8,128)(2,1)S(1)}, bf16[16,2048]{1,0:T(8,128)(2,1)S(1)}, u32[]{:S(2)}, u32[]{:S(2)}) %collective-permute-start.10) | collective-permute-done | bytes 65568 | tf_op jit(solution)/shard_map/ppermute | solution.py:199
  37.4 1.5 %collective-permute-done.11.refs_5_ = bf16[16,2048]{1,0:T(8,128)(2,1)S(1)} collective-permute-done((bf16[16,2048]{1,0:T(8,128)(2,1)S(1)}, bf16[16,2048]{1,0:T(8,128)(2,1)S(1)}, u32[]{:S(2)}, u32[]{:S(2)}) %collective-permute-start.11) | collective-permute-done | bytes 65568 | tf_op jit(solution)/shard_map/ppermute | solution.py:199
  38.9 2.1 %collective-permute-start.13 = (bf16[16,2048]{1,0:T(8,128)(2,1)S(1)}, bf16[16,2048]{1,0:T(8,128)(2,1)S(1)}, u32[]{:S(2)}, u32[]{:S(2)}) collective-permute-start(bf16[16,2048]{1,0:T(8,128)(2,1)S(1)} %get-tuple-element.26), channel_id=1, source_target_pairs={{0,28},{4,24},{8,20},{12,16},{16,12},{20,8},{24,4},{28,0},{1,29},{... | collective-permute-start | bytes 196616 | tf_op jit(solution)/shard_map/ppermute | solution.py:199
  41.4 3.3 %collective-permute-done.13.refs_7_ = bf16[16,2048]{1,0:T(8,128)(2,1)S(1)} collective-permute-done((bf16[16,2048]{1,0:T(8,128)(2,1)S(1)}, bf16[16,2048]{1,0:T(8,128)(2,1)S(1)}, u32[]{:S(2)}, u32[]{:S(2)}) %collective-permute-start.13) | collective-permute-done | bytes 65568 | tf_op jit(solution)/shard_map/ppermute | solution.py:199
  44.7 1.2 %collective-permute-start.9 = (bf16[16,2048]{1,0:T(8,128)(2,1)}, bf16[16,2048]{1,0:T(8,128)(2,1)S(1)}, u32[]{:S(2)}, u32[]{:S(2)}) collective-permute-start(bf16[16,2048]{1,0:T(8,128)(2,1)} %get-tuple-element.22), channel_id=1, source_target_pairs={{0,12},{4,8},{8,4},{12,0},{16,28},{20,24},{24,20},{28,16},{1,13},{... | collective-permute-start | bytes 196616 | tf_op jit(solution)/shard_map/ppermute | solution.py:199
  45.9 1.6 %select_last.1 = (bf16[3,32,2048]{2,1,0:T(8,128)(2,1)}, bf16[3,32,2048]{2,1,0:T(8,128)(2,1)}) custom-call(s32[3]{0:T(128)} %pad_add_fusion.where_ref, s32[3,2,96]{2,1,0:T(2,128)} %bitcast.7, bf16[192,2048]{1,0:T(8,128)(2,1)} %gate_hbm.3, bf16[192,2048]{1,0:T(8,128)(2,1)} %up_hbm.3, bf16[192,2048]{1,0:T(8,128)(2,1)} %down_hbm.3, bf16[16,2048]{1,0:T(8,128)(2,1)} %copy-done.3), custom_call_target="tpu_custom_call" | custom-call | tf_op jit(solution)/shard_map/select_last/pallas_call | solution.py:214
  49.9 1.3 %collective-permute-start.19 = (bf16[3,32,2048]{2,1,0:T(8,128)(2,1)}, bf16[3,32,2048]{2,1,0:T(8,128)(2,1)S(1)}, u32[]{:S(2)}, u32[]{:S(2)}) collective-permute-start(bf16[3,32,2048]{2,1,0:T(8,128)(2,1)} %get-tuple-element.30), channel_id=1, source_target_pairs={{12,4},{28,20},{13,5},{29,21},{14,6},{30,22},{15,7},{31,23}} | collective-permute-start | bytes 1179656 | tf_op jit(solution)/shard_map/ppermute | solution.py:203
  51.2 0.7 collective-permute-start.16
  51.9 3.2 %collective-permute-start.17 = (bf16[3,32,2048]{2,1,0:T(8,128)(2,1)}, bf16[3,32,2048]{2,1,0:T(8,128)(2,1)S(1)}, u32[]{:S(2)}, u32[]{:S(2)}) collective-permute-start(bf16[3,32,2048]{2,1,0:T(8,128)(2,1)} %collective-permute-done.15.refs_1_), channel_id=1, source_target_pairs={{4,5},{20,21},{5,4},{21,20},{6,7},{22,23},{7,6},{23,22}} | collective-permute-start | bytes 1179656 | tf_op jit(solution)/shard_map/ppermute | solution.py:211
  55.4 0.8 %copy-done.4 = bf16[16,2048]{1,0:T(8,128)(2,1)S(1)} copy-done((bf16[16,2048]{1,0:T(8,128)(2,1)S(1)}, bf16[16,2048]{1,0:T(8,128)(2,1)}, u32[]{:S(2)}) %copy-start.4) | copy-done | bytes 65560
  56.2 0.8 %copy-done.7 = bf16[16,2048]{1,0:T(8,128)(2,1)S(1)} copy-done((bf16[16,2048]{1,0:T(8,128)(2,1)S(1)}, bf16[16,2048]{1,0:T(8,128)(2,1)}, u32[]{:S(2)}) %copy-start.7) | copy-done | bytes 65560
  57.0 0.8 %copy-done.9 = bf16[16,2048]{1,0:T(8,128)(2,1)S(1)} copy-done((bf16[16,2048]{1,0:T(8,128)(2,1)S(1)}, bf16[16,2048]{1,0:T(8,128)(2,1)}, u32[]{:S(2)}) %copy-start.9) | copy-done | bytes 65560
  57.9 0.8 %copy-done.11 = bf16[16,2048]{1,0:T(8,128)(2,1)S(1)} copy-done((bf16[16,2048]{1,0:T(8,128)(2,1)S(1)}, bf16[16,2048]{1,0:T(8,128)(2,1)}, u32[]{:S(2)}) %copy-start.11) | copy-done | bytes 65560
  58.7 2.3 %combine.1 = bf16[128,2048]{1,0:T(8,128)(2,1)} custom-call(s32[3]{0:T(128)S(1)} %copy-done.12, s32[128,8]{1,0:T(8,128)S(1)} %copy.9.ids_ref, f32[128,8]{1,0:T(8,128)S(1)} %copy.10.weight_ref, bf16[16,2048]{1,0:T(8,128)(2,1)S(1)} %get-tuple-element.19.refs_0_, bf16[16,2048]{1,0:T(8,128)(2,1)S(1)} %copy-done.4, bf16[16,2048]{1,0:T(8,128)(2,1)S(1)} %copy-done.9, ...), custom_call_target="tpu_custom_call" | custom-call | tf_op jit(solution)/shard_map/combine/pallas_call | solution.py:263
  61.0 2.0 %collective-permute-done.19.refs_5_ = bf16[3,32,2048]{2,1,0:T(8,128)(2,1)S(1)} collective-permute-done((bf16[3,32,2048]{2,1,0:T(8,128)(2,1)}, bf16[3,32,2048]{2,1,0:T(8,128)(2,1)S(1)}, u32[]{:S(2)}, u32[]{:S(2)}) %collective-permute-start.19) | collective-permute-done | bytes 393248 | tf_op jit(solution)/shard_map/ppermute | solution.py:203
  63.0 1.3 %collective-permute-done.17.refs_3_ = bf16[3,32,2048]{2,1,0:T(8,128)(2,1)S(1)} collective-permute-done((bf16[3,32,2048]{2,1,0:T(8,128)(2,1)}, bf16[3,32,2048]{2,1,0:T(8,128)(2,1)S(1)}, u32[]{:S(2)}, u32[]{:S(2)}) %collective-permute-start.17) | collective-permute-done | bytes 393248 | tf_op jit(solution)/shard_map/ppermute | solution.py:211
  64.3 13.7 %merge.1 = bf16[3,96,2048]{2,1,0:T(8,128)(2,1)} custom-call(s32[3]{0:T(128)S(1)} %copy-done.12, bf16[3,32,2048]{2,1,0:T(8,128)(2,1)S(1)} %collective-permute-done.14.refs_0_, bf16[3,32,2048]{2,1,0:T(8,128)(2,1)} %collective-permute-done.15.refs_1_, bf16[3,32,2048]{2,1,0:T(8,128)(2,1)S(1)} %collective-permute-done.16.refs_2_, ...), custom_call_target="tpu_custom_call" | custom-call | tf_op jit(solution)/shard_map/merge/pallas_call | solution.py:272
  (49 shorter events, 4.3 us)
Async XLA Ops:
  3.9 3.0 %copy-start.5 = (bf16[16,2048]{1,0:T(8,128)(2,1)S(1)}, bf16[16,2048]{1,0:T(8,128)(2,1)}, u32[]{:S(2)}) copy-start(bf16[16,2048]{1,0:T(8,128)(2,1)} %get-tuple-element.17.refs_0_.after_ref) | copy-start | bytes 196612
  3.9 26.8 %copy-start = (bf16[192,2048]{1,0:T(8,128)(2,1)S(1)}, bf16[192,2048]{1,0:T(8,128)(2,1)}, u32[]{:S(2)}) copy-start(bf16[192,2048]{1,0:T(8,128)(2,1)} %gate_hbm.3) | copy-start | bytes 2359300
  3.9 26.8 %copy-start.1 = (bf16[192,2048]{1,0:T(8,128)(2,1)S(1)}, bf16[192,2048]{1,0:T(8,128)(2,1)}, u32[]{:S(2)}) copy-start(bf16[192,2048]{1,0:T(8,128)(2,1)} %up_hbm.3) | copy-start | bytes 2359300
  3.9 26.8 %copy-start.2 = (bf16[192,2048]{1,0:T(8,128)(2,1)S(1)}, bf16[192,2048]{1,0:T(8,128)(2,1)}, u32[]{:S(2)}) copy-start(bf16[192,2048]{1,0:T(8,128)(2,1)} %down_hbm.3) | copy-start | bytes 2359300
  6.1 58.2 %collective-permute-start.20 = (bf16[3,96,2048]{2,1,0:T(8,128)(2,1)}, bf16[3,96,2048]{2,1,0:T(8,128)(2,1)S(1)}, u32[]{:S(2)}, u32[]{:S(2)}) collective-permute-start(bf16[3,96,2048]{2,1,0:T(8,128)(2,1)} %get-tuple-element.31), channel_id=1, source_target_pairs={{12,8},{28,24},{13,9},{29,25},{14,10},{30,26},{15,11},{31,27}} | collective-permute-start | bytes 3538952 | tf_op jit(solution)/shard_map/ppermute | solution.py:203
  6.9 6.5 %collective-permute-start = (bf16[16,2048]{1,0:T(8,128)(2,1)S(1)}, bf16[16,2048]{1,0:T(8,128)(2,1)S(1)}, u32[]{:S(2)}, u32[]{:S(2)}) collective-permute-start(bf16[16,2048]{1,0:T(8,128)(2,1)S(1)} %copy-done.5), channel_id=1, source_target_pairs={{0,4},{4,0},{8,12},{12,8},{16,20},{20,16},{24,28},{28,24},{1,5},{5... | collective-permute-start | bytes 196616 | tf_op jit(solution)/shard_map/ppermute | solution.py:199
  7.0 7.2 %collective-permute-start.1 = (bf16[16,2048]{1,0:T(8,128)(2,1)S(1)}, bf16[16,2048]{1,0:T(8,128)(2,1)S(1)}, u32[]{:S(2)}, u32[]{:S(2)}) collective-permute-start(bf16[16,2048]{1,0:T(8,128)(2,1)S(1)} %copy-done.5), channel_id=1, source_target_pairs={{0,8},{4,12},{8,0},{12,4},{16,24},{20,28},{24,16},{28,20},{1,9},{5... | collective-permute-start | bytes 196616 | tf_op jit(solution)/shard_map/ppermute | solution.py:199
  11.8 4.7 %collective-permute-start.2 = (bf16[16,2048]{1,0:T(8,128)(2,1)S(1)}, bf16[16,2048]{1,0:T(8,128)(2,1)S(1)}, u32[]{:S(2)}, u32[]{:S(2)}) collective-permute-start(bf16[16,2048]{1,0:T(8,128)(2,1)S(1)} %copy-done.5), channel_id=1, source_target_pairs={{0,12},{4,8},{8,4},{12,0},{16,28},{20,24},{24,20},{28,16},{1,13},{... | collective-permute-start | bytes 196616 | tf_op jit(solution)/shard_map/ppermute | solution.py:199
  12.2 5.6 %collective-permute-start.3 = (bf16[16,2048]{1,0:T(8,128)(2,1)}, bf16[16,2048]{1,0:T(8,128)(2,1)S(1)}, u32[]{:S(2)}, u32[]{:S(2)}) collective-permute-start(bf16[16,2048]{1,0:T(8,128)(2,1)} %get-tuple-element.18), channel_id=1, source_target_pairs={{0,16},{4,20},{8,24},{12,28},{16,0},{20,4},{24,8},{28,12},{1,17},{... | collective-permute-start | bytes 196616 | tf_op jit(solution)/shard_map/ppermute | solution.py:199
  13.4 8.2 %collective-permute-start.4 = (bf16[16,2048]{1,0:T(8,128)(2,1)}, bf16[16,2048]{1,0:T(8,128)(2,1)S(1)}, u32[]{:S(2)}, u32[]{:S(2)}) collective-permute-start(bf16[16,2048]{1,0:T(8,128)(2,1)} %get-tuple-element.18), channel_id=1, source_target_pairs={{0,20},{4,16},{8,28},{12,24},{16,4},{20,0},{24,12},{28,8},{1,21},{... | collective-permute-start | bytes 196616 | tf_op jit(solution)/shard_map/ppermute | solution.py:199
  14.2 37.0 %collective-permute-start.14 = (bf16[3,32,2048]{2,1,0:T(8,128)(2,1)}, bf16[3,32,2048]{2,1,0:T(8,128)(2,1)S(1)}, u32[]{:S(2)}, u32[]{:S(2)}) collective-permute-start(bf16[3,32,2048]{2,1,0:T(8,128)(2,1)} %get-tuple-element.27), channel_id=1, source_target_pairs={{12,0},{28,16},{13,1},{29,17},{14,2},{30,18},{15,3},{31,19}} | collective-permute-start | bytes 1179656 | tf_op jit(solution)/shard_map/ppermute | solution.py:203
  16.5 35.4 %collective-permute-start.15 = (bf16[3,32,2048]{2,1,0:T(8,128)(2,1)}, bf16[3,32,2048]{2,1,0:T(8,128)(2,1)}, u32[]{:S(2)}, u32[]{:S(2)}) collective-permute-start(bf16[3,32,2048]{2,1,0:T(8,128)(2,1)} %get-tuple-element.28), channel_id=1, source_target_pairs={{12,4},{28,20},{13,5},{29,21},{14,6},{30,22},{15,7},{31,23}} | collective-permute-start | bytes 1179656 | tf_op jit(solution)/shard_map/ppermute | solution.py:203
  17.8 13.0 %collective-permute-start.5 = (bf16[16,2048]{1,0:T(8,128)(2,1)}, bf16[16,2048]{1,0:T(8,128)(2,1)S(1)}, u32[]{:S(2)}, u32[]{:S(2)}) collective-permute-start(bf16[16,2048]{1,0:T(8,128)(2,1)} %get-tuple-element.18), channel_id=1, source_target_pairs={{0,24},{4,28},{8,16},{12,20},{16,8},{20,12},{24,0},{28,4},{1,25},{... | collective-permute-start | bytes 196616 | tf_op jit(solution)/shard_map/ppermute | solution.py:199
  21.6 9.2 %collective-permute-start.6 = (bf16[16,2048]{1,0:T(8,128)(2,1)}, bf16[16,2048]{1,0:T(8,128)(2,1)S(1)}, u32[]{:S(2)}, u32[]{:S(2)}) collective-permute-start(bf16[16,2048]{1,0:T(8,128)(2,1)} %get-tuple-element.18), channel_id=1, source_target_pairs={{0,28},{4,24},{8,20},{12,16},{16,12},{20,8},{24,4},{28,0},{1,29},{... | collective-permute-start | bytes 196616 | tf_op jit(solution)/shard_map/ppermute | solution.py:199
  32.3 2.3 %collective-permute-start.7 = (bf16[16,2048]{1,0:T(8,128)(2,1)S(1)}, bf16[16,2048]{1,0:T(8,128)(2,1)S(1)}, u32[]{:S(2)}, u32[]{:S(2)}) collective-permute-start(bf16[16,2048]{1,0:T(8,128)(2,1)S(1)} %get-tuple-element.20), channel_id=1, source_target_pairs={{0,4},{4,0},{8,12},{12,8},{16,20},{20,16},{24,28},{28,24},{1,5},{5... | collective-permute-start | bytes 196616 | tf_op jit(solution)/shard_map/ppermute | solution.py:199
  33.7 3.7 %collective-permute-start.10 = (bf16[16,2048]{1,0:T(8,128)(2,1)S(1)}, bf16[16,2048]{1,0:T(8,128)(2,1)S(1)}, u32[]{:S(2)}, u32[]{:S(2)}) collective-permute-start(bf16[16,2048]{1,0:T(8,128)(2,1)S(1)} %get-tuple-element.23), channel_id=1, source_target_pairs={{0,16},{4,20},{8,24},{12,28},{16,0},{20,4},{24,8},{28,12},{1,17},{... | collective-permute-start | bytes 196616 | tf_op jit(solution)/shard_map/ppermute | solution.py:199
  34.6 11.3 %copy-start.3 = (bf16[16,2048]{1,0:T(8,128)(2,1)}, bf16[16,2048]{1,0:T(8,128)(2,1)S(1)}, u32[]{:S(2)}) copy-start(bf16[16,2048]{1,0:T(8,128)(2,1)S(1)} %collective-permute-done.7.refs_1_.after_ref) | copy-start | bytes 196612
  34.6 4.3 %collective-permute-start.11 = (bf16[16,2048]{1,0:T(8,128)(2,1)S(1)}, bf16[16,2048]{1,0:T(8,128)(2,1)S(1)}, u32[]{:S(2)}, u32[]{:S(2)}) collective-permute-start(bf16[16,2048]{1,0:T(8,128)(2,1)S(1)} %get-tuple-element.24), channel_id=1, source_target_pairs={{0,20},{4,16},{8,28},{12,24},{16,4},{20,0},{24,12},{28,8},{1,21},{... | collective-permute-start | bytes 196616 | tf_op jit(solution)/shard_map/ppermute | solution.py:199
  37.4 4.0 %collective-permute-start.12 = (bf16[16,2048]{1,0:T(8,128)(2,1)S(1)}, bf16[16,2048]{1,0:T(8,128)(2,1)S(1)}, u32[]{:S(2)}, u32[]{:S(2)}) collective-permute-start(bf16[16,2048]{1,0:T(8,128)(2,1)S(1)} %get-tuple-element.25), channel_id=1, source_target_pairs={{0,24},{4,28},{8,16},{12,20},{16,8},{20,12},{24,0},{28,4},{1,25},{... | collective-permute-start | bytes 196616 | tf_op jit(solution)/shard_map/ppermute | solution.py:199
  38.9 5.8 %collective-permute-start.13 = (bf16[16,2048]{1,0:T(8,128)(2,1)S(1)}, bf16[16,2048]{1,0:T(8,128)(2,1)S(1)}, u32[]{:S(2)}, u32[]{:S(2)}) collective-permute-start(bf16[16,2048]{1,0:T(8,128)(2,1)S(1)} %get-tuple-element.26), channel_id=1, source_target_pairs={{0,28},{4,24},{8,20},{12,16},{16,12},{20,8},{24,4},{28,0},{1,29},{... | collective-permute-start | bytes 196616 | tf_op jit(solution)/shard_map/ppermute | solution.py:199
  41.4 6.1 %collective-permute-start.8 = (bf16[16,2048]{1,0:T(8,128)(2,1)}, bf16[16,2048]{1,0:T(8,128)(2,1)S(1)}, u32[]{:S(2)}, u32[]{:S(2)}) collective-permute-start(bf16[16,2048]{1,0:T(8,128)(2,1)} %get-tuple-element.21), channel_id=1, source_target_pairs={{0,8},{4,12},{8,0},{12,4},{16,24},{20,28},{24,16},{28,20},{1,9},{5... | collective-permute-start | bytes 196616 | tf_op jit(solution)/shard_map/ppermute | solution.py:199
  44.7 2.8 %copy-start.6 = (bf16[16,2048]{1,0:T(8,128)(2,1)}, bf16[16,2048]{1,0:T(8,128)(2,1)S(1)}, u32[]{:S(2)}) copy-start(bf16[16,2048]{1,0:T(8,128)(2,1)S(1)} %collective-permute-done.13.refs_7_) | copy-start | bytes 196612
  44.7 10.4 %copy-start.13 = (s32[128,8]{0,1:T(8,128)S(1)}, s32[128,8]{0,1:T(8,128)}, u32[]{:S(2)}) copy-start(s32[128,8]{0,1:T(8,128)} %param.8) | copy-start | bytes 12292
  44.7 10.5 %copy-start.14 = (f32[128,8]{0,1:T(8,128)S(1)}, f32[128,8]{0,1:T(8,128)}, u32[]{:S(2)}) copy-start(f32[128,8]{0,1:T(8,128)} %param.9) | copy-start | bytes 12292
  44.7 10.6 %copy-start.12 = (s32[3]{0:T(128)S(1)}, s32[3]{0:T(128)}, u32[]{:S(2)}) copy-start(s32[3]{0:T(128)} %pad_add_fusion.where_ref) | copy-start | bytes 40
  44.7 4.6 %collective-permute-start.9 = (bf16[16,2048]{1,0:T(8,128)(2,1)}, bf16[16,2048]{1,0:T(8,128)(2,1)S(1)}, u32[]{:S(2)}, u32[]{:S(2)}) collective-permute-start(bf16[16,2048]{1,0:T(8,128)(2,1)} %get-tuple-element.22), channel_id=1, source_target_pairs={{0,12},{4,8},{8,4},{12,0},{16,28},{20,24},{24,20},{28,16},{1,13},{... | collective-permute-start | bytes 196616 | tf_op jit(solution)/shard_map/ppermute | solution.py:199
  48.2 12.8 %collective-permute-start.18 = (bf16[3,32,2048]{2,1,0:T(8,128)(2,1)}, bf16[3,32,2048]{2,1,0:T(8,128)(2,1)S(1)}, u32[]{:S(2)}, u32[]{:S(2)}) collective-permute-start(bf16[3,32,2048]{2,1,0:T(8,128)(2,1)} %get-tuple-element.29), channel_id=1, source_target_pairs={{12,0},{28,16},{13,1},{29,17},{14,2},{30,18},{15,3},{31,19}} | collective-permute-start | bytes 1179656 | tf_op jit(solution)/shard_map/ppermute | solution.py:203
  49.9 13.1 %collective-permute-start.19 = (bf16[3,32,2048]{2,1,0:T(8,128)(2,1)}, bf16[3,32,2048]{2,1,0:T(8,128)(2,1)S(1)}, u32[]{:S(2)}, u32[]{:S(2)}) collective-permute-start(bf16[3,32,2048]{2,1,0:T(8,128)(2,1)} %get-tuple-element.30), channel_id=1, source_target_pairs={{12,4},{28,20},{13,5},{29,21},{14,6},{30,22},{15,7},{31,23}} | collective-permute-start | bytes 1179656 | tf_op jit(solution)/shard_map/ppermute | solution.py:203
  51.2 11.8 %collective-permute-start.16 = (bf16[3,32,2048]{2,1,0:T(8,128)(2,1)S(1)}, bf16[3,32,2048]{2,1,0:T(8,128)(2,1)S(1)}, u32[]{:S(2)}, u32[]{:S(2)}) collective-permute-start(bf16[3,32,2048]{2,1,0:T(8,128)(2,1)S(1)} %collective-permute-done.14.refs_0_), channel_id=1, source_target_pairs={{0,1},{16,17},{1,0},{17,16},{2,3},{18,19},{3,2},{19,18}} | collective-permute-start | bytes 1179656 | tf_op jit(solution)/shard_map/ppermute | solution.py:211
  51.9 12.4 %collective-permute-start.17 = (bf16[3,32,2048]{2,1,0:T(8,128)(2,1)}, bf16[3,32,2048]{2,1,0:T(8,128)(2,1)S(1)}, u32[]{:S(2)}, u32[]{:S(2)}) collective-permute-start(bf16[3,32,2048]{2,1,0:T(8,128)(2,1)} %collective-permute-done.15.refs_1_), channel_id=1, source_target_pairs={{4,5},{20,21},{5,4},{21,20},{6,7},{22,23},{7,6},{23,22}} | collective-permute-start | bytes 1179656 | tf_op jit(solution)/shard_map/ppermute | solution.py:211
  55.3 0.8 %copy-start.4 = (bf16[16,2048]{1,0:T(8,128)(2,1)S(1)}, bf16[16,2048]{1,0:T(8,128)(2,1)}, u32[]{:S(2)}) copy-start(bf16[16,2048]{1,0:T(8,128)(2,1)} %copy-done.3) | copy-start | bytes 196612
  56.2 0.8 %copy-start.7 = (bf16[16,2048]{1,0:T(8,128)(2,1)S(1)}, bf16[16,2048]{1,0:T(8,128)(2,1)}, u32[]{:S(2)}) copy-start(bf16[16,2048]{1,0:T(8,128)(2,1)} %copy-done.6) | copy-start | bytes 196612
  (4 other events, 2.9 us)

commit v3 on v2

v3 whole, which is shorter than its diff:
```python
import functools

import jax
import jax.numpy as jnp
from jax import lax
from jax.experimental import pallas as pl
from jax.experimental.pallas import tpu as pltpu
from jax.sharding import PartitionSpec as P

CAP = 12
SLOTS = 16
GROUP = 4
BF16 = jnp.bfloat16
F32 = jnp.float32
VMEM = pl.BlockSpec(memory_space=pltpu.VMEM)
SMEM = pl.BlockSpec(memory_space=pltpu.SMEM)
HBM = pl.BlockSpec(memory_space=pl.ANY)


def params(megabytes=40):
    return pltpu.CompilerParams(vmem_limit_bytes=megabytes * 1024 * 1024)


def slot_matrix(ids, group, experts):
    tok = ids.shape[1]
    member = []
    for j in range(experts):
        expert = lax.rem(group + j, experts)
        named = jnp.where(ids == expert, 1.0, 0.0)
        member.append(jnp.sum(named, axis=0, keepdims=True))
    member = jnp.concatenate(member, axis=0)
    row = lax.broadcasted_iota(jnp.int32, (tok, tok), 0)
    col = lax.broadcasted_iota(jnp.int32, (tok, tok), 1)
    upto = jnp.where(row <= col, 1.0, 0.0).astype(BF16)
    rank = jnp.dot(member.astype(BF16), upto, preferred_element_type=F32)
    place = jnp.where(member > 0, rank - 1.0, -1.0).astype(jnp.int32)
    slot = lax.broadcasted_iota(jnp.int32, (SLOTS, tok), 0)
    blocks = [jnp.where(slot == place[j : j + 1, :], 1.0, 0.0) for j in range(experts)]
    return jnp.concatenate(blocks, axis=0)


def dispatch_kernel(experts, where_ref, ids_ref, tok_hbm, *refs):
    out_refs, (tok_ref, sem) = refs[:experts], refs[experts:]
    copy = pltpu.make_async_copy(tok_hbm, tok_ref, sem)
    copy.start()
    chosen = slot_matrix(ids_ref[...], where_ref[0], experts).astype(BF16)
    copy.wait()
    rows = jnp.dot(chosen, tok_ref[...], preferred_element_type=F32).astype(BF16)
    for j, ref in enumerate(out_refs):
        ref[...] = rows[j * SLOTS : (j + 1) * SLOTS]


def select_kernel(replicas, where_ref, plan_ref, gate_hbm, up_hbm, down_hbm, after_ref, *refs):
    out_refs, (held_ref, sems) = refs[: GROUP - 1], refs[GROUP - 1 :]
    rows = held_ref.shape[1]
    share = out_refs[0].shape[1]

    @pl.when(where_ref[1] == GROUP - 1)
    def _():
        copies = [
            pltpu.make_async_copy(ref, held_ref.at[m], sems.at[m])
            for m, ref in enumerate((gate_hbm, up_hbm, down_hbm))
        ]
        for copy in copies:
            copy.start()
        plans = []
        for survivor in range(GROUP - 1):
            whole = plan_ref[survivor, pl.ds(where_ref[0], 1), :]
            plan = whole[:, :share]
            for r in range(1, replicas):
                part = whole[:, r * share : (r + 1) * share]
                plan = jnp.where(where_ref[2] == r, part, plan)
            plans.append(plan)
        number = lax.broadcasted_iota(jnp.int32, (rows, share * len(plans)), 0)
        pick = jnp.where(number == jnp.concatenate(plans, axis=1), 1.0, 0.0).astype(BF16)
        for m, copy in enumerate(copies):
            copy.wait()
            found = lax.dot_general(
                pick, held_ref[m], (((0,), (0,)), ((), ())), preferred_element_type=F32
            )
            for p, ref in enumerate(out_refs):
                ref[m] = found[p * share : (p + 1) * share].astype(BF16)


def expert_kernel(*refs):
    x_refs, (gate_ref, up_ref, down_ref), out_refs = refs[:4], refs[4:7], refs[7:]
    rows = x_refs[0].shape[0]
    x = jnp.concatenate([ref[...] for ref in x_refs], axis=0)
    numbers = (((1,), (1,)), ((), ()))
    gate_value = lax.dot_general(x, gate_ref[...], numbers, preferred_element_type=F32)
    up_value = lax.dot_general(x, up_ref[...], numbers, preferred_element_type=F32)
    hidden = (gate_value / (1.0 + jnp.exp(-gate_value)) * up_value).astype(BF16)
    partial = jnp.dot(hidden, down_ref[...], preferred_element_type=F32).astype(BF16)
    for k, ref in enumerate(out_refs):
        ref[...] = partial[k * rows : (k + 1) * rows]


def combine_kernel(experts, where_ref, ids_ref, weight_ref, *refs):
    near_refs, back_refs, out_ref = refs[:GROUP], refs[GROUP:-1], refs[-1]
    ids = ids_ref[...]
    group = where_ref[0]
    tok = ids.shape[0]
    row = lax.broadcasted_iota(jnp.int32, (tok, tok), 0)
    col = lax.broadcasted_iota(jnp.int32, (tok, tok), 1)
    upto = jnp.where(col <= row, 1.0, 0.0).astype(BF16)
    mixed = None
    for j in range(experts):
        named = ids == lax.rem(group + j, experts)
        member = jnp.sum(jnp.where(named, 1.0, 0.0), axis=1, keepdims=True)
        weight = jnp.sum(jnp.where(named, weight_ref[...], 0.0), axis=1, keepdims=True)
        rank = jnp.dot(upto, member.astype(BF16), preferred_element_type=F32)
        place = jnp.where(member > 0, rank - 1.0, -1.0).astype(jnp.int32)
        if j == 0:
            rows = jnp.concatenate([ref[:SLOTS] for ref in near_refs], axis=0)
        else:
            rows = back_refs[j - 1][...]
        slot = lax.broadcasted_iota(jnp.int32, (tok, rows.shape[0]), 1) % SLOTS
        chosen = jnp.where(slot == place, 1.0, 0.0).astype(BF16)
        term = weight * jnp.dot(chosen, rows, preferred_element_type=F32)
        mixed = term if mixed is None else mixed + term
    out_ref[...] = mixed.astype(BF16)


def on_device(tokens, expert_ids, combine, old_gate, old_up, old_down, move_plan):
    devices = lax.axis_size("expert")
    replicas = lax.axis_size("replica")
    experts = move_plan.shape[0]
    most = move_plan.shape[2]
    share = most // replicas
    width = tokens.shape[1]
    device = lax.axis_index("expert")
    group, position = device // GROUP, device % GROUP
    where = jnp.stack([group, position, lax.axis_index("replica")]).astype(jnp.int32)
    plan = jnp.transpose(move_plan, (1, 0, 2))
    weights = (old_gate, old_up, old_down)

    def shape(*dims, dtype=BF16):
        return jax.ShapeDtypeStruct(dims, dtype)

    def permute(block, target):
        return lax.ppermute(block, "expert", [(i, target(i)) for i in range(devices)])

    def migrate(block, survivor):
        route = [(GROUP * e + GROUP - 1, GROUP * e + survivor) for e in range(experts)]
        return lax.ppermute(block, "expert", route)

    parcels = pl.pallas_call(
        functools.partial(dispatch_kernel, experts),
        out_shape=[shape(SLOTS, width)] * experts,
        in_specs=[SMEM, VMEM, HBM],
        out_specs=[VMEM] * experts,
        scratch_shapes=[pltpu.VMEM(tokens.shape, BF16), pltpu.SemaphoreType.DMA],
        compiler_params=params(60),
        name="dispatch",
    )(where, expert_ids.T, tokens)

    chosen = pl.pallas_call(
        functools.partial(select_kernel, replicas),
        out_shape=[shape(3, share, width)] * (GROUP - 1),
        in_specs=[SMEM, VMEM, HBM, HBM, HBM, HBM],
        out_specs=[VMEM] * (GROUP - 1),
        scratch_shapes=[
            pltpu.VMEM((3,) + old_gate.shape, BF16),
            pltpu.SemaphoreType.DMA((3,)),
        ],
        compiler_params=params(60),
        cost_estimate=pl.CostEstimate(
            flops=4 * 10**9, bytes_accessed=8 * 10**6, transcendentals=0
        ),
        name="select",
    )(where, plan, *weights, parcels[0])

    across = [
        permute(parcels[j], lambda i: (i + GROUP * j) % devices) for j in range(1, experts)
    ]
    here = jnp.concatenate([parcels[0]] + across, axis=0)
    rows = [here] + [permute(here, lambda i: i ^ k) for k in (1, 2, 3)]

    landed = [migrate(chosen[p], p) for p in range(GROUP - 1)]
    arrived = lax.all_gather(landed[0] + landed[1] + landed[2], "replica", axis=1, tiled=True)

    step = min(experts * SLOTS, 32)
    row_spec = pl.BlockSpec((step, width), lambda i: (i, 0))
    whole_spec = pl.BlockSpec(old_gate.shape, lambda i: (0, 0))
    partial = pl.pallas_call(
        expert_kernel,
        grid=(experts * SLOTS // step,),
        out_shape=[shape(experts * SLOTS, width)] * GROUP,
        in_specs=[row_spec] * GROUP + [whole_spec] * 3,
        out_specs=[row_spec] * GROUP,
        compiler_params=params(),
        name="expert",
    )(*rows, *weights)
    near = [partial[0]] + [permute(partial[k], lambda i: i ^ k) for k in (1, 2, 3)]
    total = sum(block[SLOTS:].astype(F32) for block in near).astype(BF16)
    back = [
        permute(
            total[(j - 1) * SLOTS : j * SLOTS], lambda i: (i - GROUP * j) % devices
        )
        for j in range(1, experts)
    ]
    mixed = pl.pallas_call(
        functools.partial(combine_kernel, experts),
        out_shape=shape(tokens.shape[0], width),
        in_specs=[SMEM, VMEM, VMEM] + [VMEM] * (GROUP + experts - 1),
        out_specs=VMEM,
        compiler_params=params(),
        name="combine",
    )(where, expert_ids, combine, *near, *back)
    return mixed, arrived


def solution(mesh):
    placed = (
        P(("replica", "expert"), None),
        P(("replica", "expert"), None),
        P(("replica", "expert"), None),
        P("expert", None),
        P("expert", None),
        P("expert", None),
        P(),
    )
    return jax.shard_map(
        on_device,
        mesh=mesh,
        in_specs=placed,
        out_specs=(P(("replica", "expert"), None), P("replica", "expert", None)),
        check_vma=False,
    )
```

time: 78.5 us -> 67.8 us (0.86)
  the two profiles are of different devices: /device:TPU:1 before, /device:TPU:0 now
where the time goes in v3:
time: 67.8 us; the launch traced here: 67.5 us
  waiting for transfers between devices  29.8 us (44%)
  between operations  14.2 us (21%)
  starting transfers between devices  11.9 us (18%)
  Pallas kernels  7.52 us (11%)
  local copies, waits for them, and re-layouts  2.66 us (4%)
  other arithmetic  1.45 us (2%)
    ppermute x8, waiting for transfers between devices, permute(): lax.ppermute(block, 'expert', [(i, target(i)) for i in range(devices)])  17.8 us
    ppermute x8, starting transfers between devices, permute(): lax.ppermute(block, 'expert', [(i, target(i)) for i in range(devices)])  9.08 us
    ppermute x3, waiting for transfers between devices, migrate(): return lax.ppermute(block, 'expert', route)  8.83 us
    all_gather x1, waiting for transfers between devices, on_device(): lax.all_gather(landed[0] + landed[1] + landed[2], 'replica', axis=1, tile...  3.15 us
    ppermute x3, starting transfers between devices, migrate(): return lax.ppermute(block, 'expert', route)  2.78 us
    unnamed x20, local copies, waits for them, and re-layouts  2.66 us
    pallas_call x1, Pallas kernels, on_device(): pl.pallas_call(functools.partial(dispatch_kernel, experts), out_shape=[sh...  2.6 us
    pallas_call x1, Pallas kernels, on_device(): pl.pallas_call(functools.partial(combine_kernel, experts), out_shape=shap...  2.27 us
  transfers between devices with their start and end apart: 12, of which 8 were waited for; matrix products, arithmetic and copies ran while one was open for 0% of the time, Pallas kernels for 5%

profile of v3, /device:TPU:0, one launch (start us, length us, event | category | flops | bytes accessed | tf_op | source)
XLA Modules:
  0.0 67.5 jit_solution(1465849892588193088)
XLA Ops:
  7.2 0.0 all-gather.2.cloned.1.call-start
  7.2 0.7 pad_add_fusion.where_ref
  7.9 2.6 %dispatch.1 = (bf16[16,2048]{1,0:T(8,128)(2,1)}, bf16[16,2048]{1,0:T(8,128)(2,1)}) custom-call(s32[3]{0:T(128)} %pad_add_fusion.where_ref, s32[8,128]{1,0:T(8,128)} %bitcast.5, bf16[128,2048]{1,0:T(8,128)(2,1)} %tok_hbm.1), custom_call_target="tpu_custom_call" | custom-call | tf_op jit(solution)/shard_map/dispatch/pallas_call | solution.py:147
  10.5 0.0 copy-start.2
  10.5 1.7 %select.7 = (bf16[3,24,2048]{2,1,0:T(8,128)(2,1)}, bf16[3,24,2048]{2,1,0:T(8,128)(2,1)}, bf16[3,24,2048]{2,1,0:T(8,128)(2,1)}) custom-call(s32[3]{0:T(128)} %pad_add_fusion.where_ref, s32[3,2,96]{2,1,0:T(2,128)} %bitcast.6, bf16[192,2048]{1,0:T(8,128)(2,1)} %gate_hbm.1, bf16[192,2048]{1,0:T(8,128)(2,1)} %up_hbm.1, bf16[192,2048]{1,0:T(8,128)(2,1)} %down_hbm.1, ...), custom_call_target="tpu_custom_call" | custom-call | flops 4000000000 | bytes 8000000 | tf_op jit(solution)/shard_map/select/pallas_call | solution.py:157
  12.3 0.0 copy-start
  12.3 0.0 copy-start.1
  12.3 0.8 %collective-permute-start.10 = (bf16[3,24,2048]{2,1,0:T(8,128)(2,1)}, bf16[3,24,2048]{2,1,0:T(8,128)(2,1)S(1)}, u32[]{:S(2)}, u32[]{:S(2)}) collective-permute-start(bf16[3,24,2048]{2,1,0:T(8,128)(2,1)} %get-tuple-element.19), channel_id=1, source_target_pairs={{12,8},{28,24},{13,9},{29,25},{14,10},{30,26},{15,11},{31,27}} | collective-permute-start | bytes 884744 | tf_op jit(solution)/shard_map/ppermute | solution.py:145
  13.1 1.3 %collective-permute-start.8 = (bf16[3,24,2048]{2,1,0:T(8,128)(2,1)}, bf16[3,24,2048]{2,1,0:T(8,128)(2,1)S(1)}, u32[]{:S(2)}, u32[]{:S(2)}) collective-permute-start(bf16[3,24,2048]{2,1,0:T(8,128)(2,1)} %get-tuple-element.17), channel_id=1, source_target_pairs={{12,0},{28,16},{13,1},{29,17},{14,2},{30,18},{15,3},{31,19}} | collective-permute-start | bytes 884744 | tf_op jit(solution)/shard_map/ppermute | solution.py:145
  14.4 0.7 %collective-permute-start.9 = (bf16[3,24,2048]{2,1,0:T(8,128)(2,1)}, bf16[3,24,2048]{2,1,0:T(8,128)(2,1)S(1)}, u32[]{:S(2)}, u32[]{:S(2)}) collective-permute-start(bf16[3,24,2048]{2,1,0:T(8,128)(2,1)} %get-tuple-element.18), channel_id=1, source_target_pairs={{12,4},{28,20},{13,5},{29,21},{14,6},{30,22},{15,7},{31,23}} | collective-permute-start | bytes 884744 | tf_op jit(solution)/shard_map/ppermute | solution.py:145
  15.1 8.8 %collective-permute-done.8 = bf16[3,24,2048]{2,1,0:T(8,128)(2,1)S(1)} collective-permute-done((bf16[3,24,2048]{2,1,0:T(8,128)(2,1)}, bf16[3,24,2048]{2,1,0:T(8,128)(2,1)S(1)}, u32[]{:S(2)}, u32[]{:S(2)}) %collective-permute-start.8) | collective-permute-done | bytes 294944 | tf_op jit(solution)/shard_map/ppermute | solution.py:145
  23.9 0.8 %add_add_fusion = bf16[3,24,2048]{2,1,0:T(8,128)(2,1)} fusion(bf16[3,24,2048]{2,1,0:T(8,128)(2,1)S(1)} %collective-permute-done.10, bf16[3,24,2048]{2,1,0:T(8,128)(2,1)S(1)} %collective-permute-done.8, bf16[3,24,2048]{2,1,0:T(8,128)(2,1)S(1)} %collective-permute-done.9), kind=kLoop, calls=%fused_computation | loop fusion | flops 294912 | bytes 1179648 | tf_op jit(solution)/shard_map/add | solution.py:180
  24.7 0.0 all-gather.2.cloned.1.call-update
  24.7 1.6 %collective-permute-start = (bf16[16,2048]{1,0:T(8,128)(2,1)S(1)}, bf16[16,2048]{1,0:T(8,128)(2,1)S(1)}, u32[]{:S(2)}, u32[]{:S(2)}) collective-permute-start(bf16[16,2048]{1,0:T(8,128)(2,1)S(1)} %copy-done.7), channel_id=1, source_target_pairs={{0,16},{4,20},{8,24},{12,28},{16,0},{20,4},{24,8},{28,12},{1,17},{... | collective-permute-start | bytes 196616 | tf_op jit(solution)/shard_map/ppermute | solution.py:141
  26.3 2.7 %collective-permute-done = bf16[16,2048]{1,0:T(8,128)(2,1)S(1)} collective-permute-done((bf16[16,2048]{1,0:T(8,128)(2,1)S(1)}, bf16[16,2048]{1,0:T(8,128)(2,1)S(1)}, u32[]{:S(2)}, u32[]{:S(2)}) %collective-permute-start) | collective-permute-done | bytes 65568 | tf_op jit(solution)/shard_map/ppermute | solution.py:141
  29.1 0.0 copy-start.6
  29.1 1.9 %collective-permute-start.1 = (bf16[32,2048]{1,0:T(8,128)(2,1)S(1)}, bf16[32,2048]{1,0:T(8,128)(2,1)S(1)}, u32[]{:S(2)}, u32[]{:S(2)}) collective-permute-start(bf16[32,2048]{1,0:T(8,128)(2,1)S(1)} %constant_dynamic-update-slice_fusion.refs_0_), channel_id=1, source_target_pairs={{0,4},{4,0},{8,12},{12,8},{16,20},{20,16},{24,28},{28,24},{1,5},{5... | collective-permute-start | bytes 393224 | tf_op jit(solution)/shard_map/ppermute | solution.py:141
  31.0 1.4 %collective-permute-start.3 = (bf16[32,2048]{1,0:T(8,128)(2,1)S(1)}, bf16[32,2048]{1,0:T(8,128)(2,1)S(1)}, u32[]{:S(2)}, u32[]{:S(2)}) collective-permute-start(bf16[32,2048]{1,0:T(8,128)(2,1)S(1)} %constant_dynamic-update-slice_fusion.refs_0_), channel_id=1, source_target_pairs={{0,12},{4,8},{8,4},{12,0},{16,28},{20,24},{24,20},{28,16},{1,13},{... | collective-permute-start | bytes 393224 | tf_op jit(solution)/shard_map/ppermute | solution.py:141
  32.4 4.9 %collective-permute-done.2.refs_2_ = bf16[32,2048]{1,0:T(8,128)(2,1)S(1)} collective-permute-done((bf16[32,2048]{1,0:T(8,128)(2,1)S(1)}, bf16[32,2048]{1,0:T(8,128)(2,1)S(1)}, u32[]{:S(2)}, u32[]{:S(2)}) %collective-permute-start.2) | collective-permute-done | bytes 131104 | tf_op jit(solution)/shard_map/ppermute | solution.py:141
  37.3 1.1 %collective-permute-done.3.refs_3_ = bf16[32,2048]{1,0:T(8,128)(2,1)S(1)} collective-permute-done((bf16[32,2048]{1,0:T(8,128)(2,1)S(1)}, bf16[32,2048]{1,0:T(8,128)(2,1)S(1)}, u32[]{:S(2)}, u32[]{:S(2)}) %collective-permute-start.3) | collective-permute-done | bytes 131104 | tf_op jit(solution)/shard_map/ppermute | solution.py:141
  38.4 0.9 %expert.1 = (bf16[32,2048]{1,0:T(8,128)(2,1)S(1)}, bf16[32,2048]{1,0:T(8,128)(2,1)S(1)}, bf16[32,2048]{1,0:T(8,128)(2,1)S(1)}, bf16[32,2048]{1,0:T(8,128)(2,1)S(1)}) custom-call(bf16[32,2048]{1,0:T(8,128)(2,1)S(1)} %constant_dynamic-update-slice_fusion.refs_0_, bf16[32,2048]{1,0:T(8,128)(2,1)S(1)} %collective-permute-done.1.refs_1_, ...), custom_call_target="tpu_custom_call" | custom-call | tf_op jit(solution)/shard_map/expert/pallas_call | solution.py:185
  39.3 1.2 %collective-permute-start.4 = (bf16[32,2048]{1,0:T(8,128)(2,1)S(1)}, bf16[32,2048]{1,0:T(8,128)(2,1)S(1)}, u32[]{:S(2)}, u32[]{:S(2)}) collective-permute-start(bf16[32,2048]{1,0:T(8,128)(2,1)S(1)} %get-tuple-element.14), channel_id=1, source_target_pairs={{0,4},{4,0},{8,12},{12,8},{16,20},{20,16},{24,28},{28,24},{1,5},{5... | collective-permute-start | bytes 393224 | tf_op jit(solution)/shard_map/ppermute | solution.py:141
  40.5 1.4 %collective-permute-start.6 = (bf16[32,2048]{1,0:T(8,128)(2,1)S(1)}, bf16[32,2048]{1,0:T(8,128)(2,1)S(1)}, u32[]{:S(2)}, u32[]{:S(2)}) collective-permute-start(bf16[32,2048]{1,0:T(8,128)(2,1)S(1)} %get-tuple-element.16), channel_id=1, source_target_pairs={{0,12},{4,8},{8,4},{12,0},{16,28},{20,24},{24,20},{28,16},{1,13},{... | collective-permute-start | bytes 393224 | tf_op jit(solution)/shard_map/ppermute | solution.py:141
  41.9 4.9 %collective-permute-done.5.refs_2_ = bf16[32,2048]{1,0:T(8,128)(2,1)S(1)} collective-permute-done((bf16[32,2048]{1,0:T(8,128)(2,1)S(1)}, bf16[32,2048]{1,0:T(8,128)(2,1)S(1)}, u32[]{:S(2)}, u32[]{:S(2)}) %collective-permute-start.5) | collective-permute-done | bytes 131104 | tf_op jit(solution)/shard_map/ppermute | solution.py:141
  46.9 1.1 %collective-permute-done.6.refs_3_ = bf16[32,2048]{1,0:T(8,128)(2,1)S(1)} collective-permute-done((bf16[32,2048]{1,0:T(8,128)(2,1)S(1)}, bf16[32,2048]{1,0:T(8,128)(2,1)S(1)}, u32[]{:S(2)}, u32[]{:S(2)}) %collective-permute-start.6) | collective-permute-done | bytes 131104 | tf_op jit(solution)/shard_map/ppermute | solution.py:141
  47.9 1.6 %collective-permute-start.7 = (bf16[16,2048]{1,0:T(8,128)(2,1)S(1)}, bf16[16,2048]{1,0:T(8,128)(2,1)S(1)}, u32[]{:S(2)}, u32[]{:S(2)}) collective-permute-start(bf16[16,2048]{1,0:T(8,128)(2,1)S(1)} %add_convert_fusion), channel_id=1, source_target_pairs={{0,16},{4,20},{8,24},{12,28},{16,0},{20,4},{24,8},{28,12},{1,17},{... | collective-permute-start | bytes 196616 | tf_op jit(solution)/shard_map/ppermute | solution.py:141
  49.5 0.1 copy.9.ids_ref
  49.6 0.1 copy.10.weight_ref
  49.7 3.1 %collective-permute-done.7.refs_4_ = bf16[16,2048]{1,0:T(8,128)(2,1)S(1)} collective-permute-done((bf16[16,2048]{1,0:T(8,128)(2,1)S(1)}, bf16[16,2048]{1,0:T(8,128)(2,1)S(1)}, u32[]{:S(2)}, u32[]{:S(2)}) %collective-permute-start.7) | collective-permute-done | bytes 65568 | tf_op jit(solution)/shard_map/ppermute | solution.py:141
  52.9 2.3 %combine.1 = bf16[128,2048]{1,0:T(8,128)(2,1)} custom-call(s32[3]{0:T(128)S(1)} %copy-done.3, s32[128,8]{1,0:T(8,128)S(1)} %copy.9.ids_ref, f32[128,8]{1,0:T(8,128)S(1)} %copy.10.weight_ref, bf16[32,2048]{1,0:T(8,128)(2,1)S(1)} %get-tuple-element.13.refs_0_, bf16[32,2048]{1,0:T(8,128)(2,1)S(1)} %collective-permute-done.4.refs_1_, ...), custom_call_target="tpu_custom_call" | custom-call | tf_op jit(solution)/shard_map/combine/pallas_call | solution.py:202
  55.1 3.1 %all-gather.2.cloned.1.call-done = bf16[3,96,2048]{2,1,0:T(8,128)(2,1)} async-done(((bf16[3,24,2048]{2,1,0:T(8,128)(2,1)}), bf16[3,96,2048]{2,1,0:T(8,128)(2,1)}) %all-gather.2.cloned.1.call-update) | async-done | bytes 1179664 | tf_op jit(solution)/shard_map/all_gather | solution.py:180
  58.3 2.4 %copy.13 = bf16[3,96,2048]{2,1,0:T(8,128)(2,1)} copy(bf16[3,96,2048]{2,1,0:T(8,128)(2,1)} %all-gather.2.cloned.1.call-done) | data formatting | bytes 2359296
  (21 shorter events, 0.1 us)
Async XLA Ops:
  7.2 51.1 %all-gather.2.cloned.1.call-start = ((), (), s32[]{:S(2)}) async-start(), calls=%async_computation | async-start | bytes 1474560 | tf_op jit(solution)/shard_map/all_gather | solution.py:180
  10.5 14.2 %copy-start.7 = (bf16[16,2048]{1,0:T(8,128)(2,1)S(1)}, bf16[16,2048]{1,0:T(8,128)(2,1)}, u32[]{:S(2)}) copy-start(bf16[16,2048]{1,0:T(8,128)(2,1)} %get-tuple-element.12) | copy-start | bytes 196612
  10.5 15.8 %copy-start.4 = (bf16[16,2048]{1,0:T(8,128)(2,1)S(1)}, bf16[16,2048]{1,0:T(8,128)(2,1)}, u32[]{:S(2)}) copy-start(bf16[16,2048]{1,0:T(8,128)(2,1)} %get-tuple-element.11.after_ref) | copy-start | bytes 196612
  10.5 27.9 %copy-start.2 = (bf16[192,2048]{1,0:T(8,128)(2,1)S(1)}, bf16[192,2048]{1,0:T(8,128)(2,1)}, u32[]{:S(2)}) copy-start(bf16[192,2048]{1,0:T(8,128)(2,1)} %down_hbm.1) | copy-start | bytes 2359300
  12.3 26.1 %copy-start = (bf16[192,2048]{1,0:T(8,128)(2,1)S(1)}, bf16[192,2048]{1,0:T(8,128)(2,1)}, u32[]{:S(2)}) copy-start(bf16[192,2048]{1,0:T(8,128)(2,1)} %gate_hbm.1) | copy-start | bytes 2359300
  12.3 26.1 %copy-start.1 = (bf16[192,2048]{1,0:T(8,128)(2,1)S(1)}, bf16[192,2048]{1,0:T(8,128)(2,1)}, u32[]{:S(2)}) copy-start(bf16[192,2048]{1,0:T(8,128)(2,1)} %up_hbm.1) | copy-start | bytes 2359300
  12.3 2.8 %collective-permute-start.10 = (bf16[3,24,2048]{2,1,0:T(8,128)(2,1)}, bf16[3,24,2048]{2,1,0:T(8,128)(2,1)S(1)}, u32[]{:S(2)}, u32[]{:S(2)}) collective-permute-start(bf16[3,24,2048]{2,1,0:T(8,128)(2,1)} %get-tuple-element.19), channel_id=1, source_target_pairs={{12,8},{28,24},{13,9},{29,25},{14,10},{30,26},{15,11},{31,27}} | collective-permute-start | bytes 884744 | tf_op jit(solution)/shard_map/ppermute | solution.py:145
  13.1 10.8 %collective-permute-start.8 = (bf16[3,24,2048]{2,1,0:T(8,128)(2,1)}, bf16[3,24,2048]{2,1,0:T(8,128)(2,1)S(1)}, u32[]{:S(2)}, u32[]{:S(2)}) collective-permute-start(bf16[3,24,2048]{2,1,0:T(8,128)(2,1)} %get-tuple-element.17), channel_id=1, source_target_pairs={{12,0},{28,16},{13,1},{29,17},{14,2},{30,18},{15,3},{31,19}} | collective-permute-start | bytes 884744 | tf_op jit(solution)/shard_map/ppermute | solution.py:145
  14.4 9.5 %collective-permute-start.9 = (bf16[3,24,2048]{2,1,0:T(8,128)(2,1)}, bf16[3,24,2048]{2,1,0:T(8,128)(2,1)S(1)}, u32[]{:S(2)}, u32[]{:S(2)}) collective-permute-start(bf16[3,24,2048]{2,1,0:T(8,128)(2,1)} %get-tuple-element.18), channel_id=1, source_target_pairs={{12,4},{28,20},{13,5},{29,21},{14,6},{30,22},{15,7},{31,23}} | collective-permute-start | bytes 884744 | tf_op jit(solution)/shard_map/ppermute | solution.py:145
  24.7 4.3 %collective-permute-start = (bf16[16,2048]{1,0:T(8,128)(2,1)S(1)}, bf16[16,2048]{1,0:T(8,128)(2,1)S(1)}, u32[]{:S(2)}, u32[]{:S(2)}) collective-permute-start(bf16[16,2048]{1,0:T(8,128)(2,1)S(1)} %copy-done.7), channel_id=1, source_target_pairs={{0,16},{4,20},{8,24},{12,28},{16,0},{20,4},{24,8},{28,12},{1,17},{... | collective-permute-start | bytes 196616 | tf_op jit(solution)/shard_map/ppermute | solution.py:141
  29.1 20.5 %copy-start.5 = (s32[128,8]{0,1:T(8,128)S(1)}, s32[128,8]{0,1:T(8,128)}, u32[]{:S(2)}) copy-start(s32[128,8]{0,1:T(8,128)} %param.8) | copy-start | bytes 12292
  29.1 20.6 %copy-start.6 = (f32[128,8]{0,1:T(8,128)S(1)}, f32[128,8]{0,1:T(8,128)}, u32[]{:S(2)}) copy-start(f32[128,8]{0,1:T(8,128)} %param.9) | copy-start | bytes 12292
  29.1 23.8 %copy-start.3 = (s32[3]{0:T(128)S(1)}, s32[3]{0:T(128)}, u32[]{:S(2)}) copy-start(s32[3]{0:T(128)} %pad_add_fusion.where_ref) | copy-start | bytes 40
  29.1 3.3 %collective-permute-start.1 = (bf16[32,2048]{1,0:T(8,128)(2,1)S(1)}, bf16[32,2048]{1,0:T(8,128)(2,1)S(1)}, u32[]{:S(2)}, u32[]{:S(2)}) collective-permute-start(bf16[32,2048]{1,0:T(8,128)(2,1)S(1)} %constant_dynamic-update-slice_fusion.refs_0_), channel_id=1, source_target_pairs={{0,4},{4,0},{8,12},{12,8},{16,20},{20,16},{24,28},{28,24},{1,5},{5... | collective-permute-start | bytes 393224 | tf_op jit(solution)/shard_map/ppermute | solution.py:141
  31.0 6.4 %collective-permute-start.2 = (bf16[32,2048]{1,0:T(8,128)(2,1)S(1)}, bf16[32,2048]{1,0:T(8,128)(2,1)S(1)}, u32[]{:S(2)}, u32[]{:S(2)}) collective-permute-start(bf16[32,2048]{1,0:T(8,128)(2,1)S(1)} %constant_dynamic-update-slice_fusion.refs_0_), channel_id=1, source_target_pairs={{0,8},{4,12},{8,0},{12,4},{16,24},{20,28},{24,16},{28,20},{1,9},{5... | collective-permute-start | bytes 393224 | tf_op jit(solution)/shard_map/ppermute | solution.py:141
  31.0 7.4 %collective-permute-start.3 = (bf16[32,2048]{1,0:T(8,128)(2,1)S(1)}, bf16[32,2048]{1,0:T(8,128)(2,1)S(1)}, u32[]{:S(2)}, u32[]{:S(2)}) collective-permute-start(bf16[32,2048]{1,0:T(8,128)(2,1)S(1)} %constant_dynamic-update-slice_fusion.refs_0_), channel_id=1, source_target_pairs={{0,12},{4,8},{8,4},{12,0},{16,28},{20,24},{24,20},{28,16},{1,13},{... | collective-permute-start | bytes 393224 | tf_op jit(solution)/shard_map/ppermute | solution.py:141
  39.3 2.6 %collective-permute-start.4 = (bf16[32,2048]{1,0:T(8,128)(2,1)S(1)}, bf16[32,2048]{1,0:T(8,128)(2,1)S(1)}, u32[]{:S(2)}, u32[]{:S(2)}) collective-permute-start(bf16[32,2048]{1,0:T(8,128)(2,1)S(1)} %get-tuple-element.14), channel_id=1, source_target_pairs={{0,4},{4,0},{8,12},{12,8},{16,20},{20,16},{24,28},{28,24},{1,5},{5... | collective-permute-start | bytes 393224 | tf_op jit(solution)/shard_map/ppermute | solution.py:141
  40.5 6.4 %collective-permute-start.5 = (bf16[32,2048]{1,0:T(8,128)(2,1)S(1)}, bf16[32,2048]{1,0:T(8,128)(2,1)S(1)}, u32[]{:S(2)}, u32[]{:S(2)}) collective-permute-start(bf16[32,2048]{1,0:T(8,128)(2,1)S(1)} %get-tuple-element.15), channel_id=1, source_target_pairs={{0,8},{4,12},{8,0},{12,4},{16,24},{20,28},{24,16},{28,20},{1,9},{5... | collective-permute-start | bytes 393224 | tf_op jit(solution)/shard_map/ppermute | solution.py:141
  40.5 7.4 %collective-permute-start.6 = (bf16[32,2048]{1,0:T(8,128)(2,1)S(1)}, bf16[32,2048]{1,0:T(8,128)(2,1)S(1)}, u32[]{:S(2)}, u32[]{:S(2)}) collective-permute-start(bf16[32,2048]{1,0:T(8,128)(2,1)S(1)} %get-tuple-element.16), channel_id=1, source_target_pairs={{0,12},{4,8},{8,4},{12,0},{16,28},{20,24},{24,20},{28,16},{1,13},{... | collective-permute-start | bytes 393224 | tf_op jit(solution)/shard_map/ppermute | solution.py:141
  47.9 4.9 %collective-permute-start.7 = (bf16[16,2048]{1,0:T(8,128)(2,1)S(1)}, bf16[16,2048]{1,0:T(8,128)(2,1)S(1)}, u32[]{:S(2)}, u32[]{:S(2)}) collective-permute-start(bf16[16,2048]{1,0:T(8,128)(2,1)S(1)} %add_convert_fusion), channel_id=1, source_target_pairs={{0,16},{4,20},{8,24},{12,28},{16,0},{20,4},{24,8},{28,12},{1,17},{... | collective-permute-start | bytes 196616 | tf_op jit(solution)/shard_map/ppermute | solution.py:141
Sparse Core Ops, SparseCore 0:
  24.8 33.3 all-gather.1

commit v4 on v2

v4 whole, which is shorter than its diff:
```python
import functools

import jax
import jax.numpy as jnp
from jax import lax
from jax.experimental import pallas as pl
from jax.experimental.pallas import tpu as pltpu
from jax.sharding import PartitionSpec as P

CAP = 12
SLOTS = 16
GROUP = 4
BF16 = jnp.bfloat16
F32 = jnp.float32
VMEM = pl.BlockSpec(memory_space=pltpu.VMEM)
HBM = pl.BlockSpec(memory_space=pl.ANY)


def params():
    return pltpu.CompilerParams(vmem_limit_bytes=40 * 1024 * 1024)


def cost(microseconds):
    return pl.CostEstimate(
        flops=microseconds * 10**9, bytes_accessed=10**6, transcendentals=0
    )


def slot_matrix(ids, group, experts):
    tok = ids.shape[1]
    member = []
    for j in range(experts):
        expert = lax.rem(group + j, experts)
        named = jnp.where(ids == expert, 1.0, 0.0)
        member.append(jnp.sum(named, axis=0, keepdims=True))
    member = jnp.concatenate(member, axis=0)
    row = lax.broadcasted_iota(jnp.int32, (tok, tok), 0)
    col = lax.broadcasted_iota(jnp.int32, (tok, tok), 1)
    upto = jnp.where(row <= col, 1.0, 0.0).astype(BF16)
    rank = jnp.dot(member.astype(BF16), upto, preferred_element_type=F32)
    place = jnp.where(member > 0, rank - 1.0, -1.0).astype(jnp.int32)
    slot = lax.broadcasted_iota(jnp.int32, (SLOTS, tok), 0)
    blocks = [jnp.where(slot == place[j : j + 1, :], 1.0, 0.0) for j in range(experts)]
    return jnp.concatenate(blocks, axis=0)


def dispatch_kernel(experts, ids_ref, tok_ref, *out_refs):
    group = lax.axis_index("expert") // GROUP
    chosen = slot_matrix(ids_ref[...], group, experts).astype(BF16)
    rows = jnp.dot(chosen, tok_ref[...], preferred_element_type=F32).astype(BF16)
    for j, ref in enumerate(out_refs):
        ref[...] = rows[j * SLOTS : (j + 1) * SLOTS]


def select_kernel(wanted, plan_ref, gate_ref, up_ref, down_ref, *out_refs):
    device = lax.axis_index("expert")
    even = lax.axis_index("replica") % 2 == 0
    rows = gate_ref.shape[0]

    @pl.when(device % GROUP == GROUP - 1)
    def _():
        plans = []
        for survivor, first, count in wanted:
            plan = plan_ref[survivor, pl.ds(device // GROUP, 1), :]
            if first is None:
                plan = jnp.where(even, plan[:, :count], plan[:, count : 2 * count])
            else:
                plan = plan[:, first : first + count]
            plans.append(plan)
        total = sum(count for _, _, count in wanted)
        number = lax.broadcasted_iota(jnp.int32, (rows, total), 0)
        pick = jnp.where(number == jnp.concatenate(plans, axis=1), 1.0, 0.0).astype(BF16)
        for m, held_ref in enumerate((gate_ref, up_ref, down_ref)):
            found = lax.dot_general(
                pick, held_ref[...], (((0,), (0,)), ((), ())), preferred_element_type=F32
            ).astype(BF16)
            start = 0
            for (_, _, count), ref in zip(wanted, out_refs):
                ref[m] = found[start : start + count]
                start += count


def merge_kernel(part, shared_ref, swapped_ref, first_ref, second_ref, near_ref, out_ref, sems):
    position = lax.axis_index("expert") % GROUP
    parity = lax.axis_index("replica") % 2
    most = out_ref.shape[1]

    def move(pieces):
        copies = []
        for ref, first, count in pieces:
            for m in range(3):
                copies.append(
                    pltpu.make_async_copy(
                        ref.at[m], out_ref.at[m, pl.ds(first, count)], sems.at[len(copies)]
                    )
                )
        for copy in copies:
            copy.start()
        for copy in copies:
            copy.wait()

    for p, ref in ((0, first_ref), (1, second_ref)):
        for even in range(2):
            mine = position == 1 if p == 1 else jnp.logical_or(position == 0, position == 3)

            @pl.when(jnp.logical_and(mine, parity == even))
            def _():
                move(
                    [
                        (shared_ref, part * even, part),
                        (swapped_ref, part * (1 - even), part),
                        (ref, 2 * part, most - 2 * part),
                    ]
                )

    @pl.when(position == 2)
    def _():
        move([(near_ref, 0, most)])


def expert_kernel(mine_ref, other_ref, gate_ref, up_ref, down_ref, keep_ref, send_ref):
    rows = mine_ref.shape[0]
    x = jnp.concatenate([mine_ref[...], other_ref[...]], axis=0)
    numbers = (((1,), (1,)), ((), ()))
    gate_value = lax.dot_general(x, gate_ref[...], numbers, preferred_element_type=F32)
    up_value = lax.dot_general(x, up_ref[...], numbers, preferred_element_type=F32)
    hidden = (gate_value / (1.0 + jnp.exp(-gate_value)) * up_value).astype(BF16)
    partial = jnp.dot(hidden, down_ref[...], preferred_element_type=F32)
    keep_ref[...] = partial[:rows]
    send_ref[...] = partial[rows:].astype(BF16)


def combine_kernel(experts, ids_ref, weight_ref, *refs):
    piece_refs, out_ref = refs[:-1], refs[-1]
    ids = ids_ref[...]
    group = lax.axis_index("expert") // GROUP
    tok = ids.shape[0]
    each = len(piece_refs) // experts
    row = lax.broadcasted_iota(jnp.int32, (tok, tok), 0)
    col = lax.broadcasted_iota(jnp.int32, (tok, tok), 1)
    upto = jnp.where(col <= row, 1.0, 0.0).astype(BF16)
    slot = lax.broadcasted_iota(jnp.int32, (tok, each * SLOTS), 1) % SLOTS
    mixed = None
    for j in range(experts):
        named = ids == lax.rem(group + j, experts)
        member = jnp.sum(jnp.where(named, 1.0, 0.0), axis=1, keepdims=True)
        weight = jnp.sum(jnp.where(named, weight_ref[...], 0.0), axis=1, keepdims=True)
        rank = jnp.dot(upto, member.astype(BF16), preferred_element_type=F32)
        place = jnp.where(member > 0, rank - 1.0, -1.0).astype(jnp.int32)
        chosen = jnp.where(slot == place, 1.0, 0.0).astype(BF16)
        rows = [ref[...] for ref in piece_refs[j * each : (j + 1) * each]]
        found = jnp.dot(chosen, jnp.concatenate(rows, axis=0), preferred_element_type=F32)
        term = weight * found
        mixed = term if mixed is None else mixed + term
    out_ref[...] = mixed.astype(BF16)


def on_device(tokens, expert_ids, combine, old_gate, old_up, old_down, move_plan):
    devices = lax.axis_size("expert")
    replicas = lax.axis_size("replica")
    experts = move_plan.shape[0]
    most = move_plan.shape[2]
    width = tokens.shape[1]
    plan = jnp.transpose(move_plan, (1, 0, 2))
    weights = (old_gate, old_up, old_down)
    part = most // 3
    rest = most - 2 * part

    def shape(*dims, dtype=BF16):
        return jax.ShapeDtypeStruct(dims, dtype)

    def send(block, j, k):
        route = []
        for i in range(devices):
            g, p = i // GROUP, i % GROUP
            route.append((i, GROUP * ((g + j) % experts) + (p ^ k)))
        return lax.ppermute(block, "expert", route)

    def migrate(block, survivor):
        route = [(GROUP * e + GROUP - 1, GROUP * e + survivor) for e in range(experts)]
        return lax.ppermute(block, "expert", route)

    def swap(block):
        route = []
        for r in range(replicas):
            for i in range(devices):
                if i % GROUP < 2:
                    route.append((i * replicas + r, i * replicas + (r ^ 1)))
        return lax.ppermute(block, ("expert", "replica"), route)

    def select(wanted, held, name):
        return pl.pallas_call(
            functools.partial(select_kernel, wanted),
            out_shape=[shape(3, count, width) for _, _, count in wanted],
            in_specs=[VMEM] * 4,
            out_specs=[VMEM] * len(wanted),
            compiler_params=params(),
            cost_estimate=cost(2),
            name=name,
        )(plan, *held)

    parcels = pl.pallas_call(
        functools.partial(dispatch_kernel, experts),
        out_shape=[shape(SLOTS, width)] * experts,
        in_specs=[VMEM, VMEM],
        out_specs=[VMEM] * experts,
        compiler_params=params(),
        cost_estimate=cost(2),
        name="dispatch",
    )(expert_ids.T, tokens)

    pairs = [(j, k) for j in range(experts) for k in (0, 2)]
    mine = [parcels[0]] + [send(parcels[j], j, k) for j, k in pairs[1:]]
    mine = jnp.concatenate(mine, axis=0)
    other = send(mine, 0, 1)

    held, mine = lax.optimization_barrier((weights, mine))
    first = select([(0, None, part), (1, None, part)], held, "select_first")
    shared = [migrate(first[p], p) for p in range(2)]
    other, _ = lax.optimization_barrier((other, first))

    total = mine.shape[0]
    step = min(total, 64)
    row_spec = pl.BlockSpec((step, width), lambda i: (i, 0))
    whole_spec = pl.BlockSpec(old_gate.shape, lambda i: (0, 0))
    keep, give = pl.pallas_call(
        expert_kernel,
        grid=(total // step,),
        out_shape=[shape(total, width, dtype=F32), shape(total, width)],
        in_specs=[row_spec] * 2 + [whole_spec] * 3,
        out_specs=[row_spec] * 2,
        compiler_params=params(),
        cost_estimate=cost(4),
        name="expert",
    )(mine, other, *weights)
    taken = send(give, 0, 1)
    summed = (keep + taken.astype(F32)).astype(BF16)
    pieces = [summed[n * SLOTS : (n + 1) * SLOTS] for n in range(len(pairs))]
    back = [pieces[0]] + [
        send(block, -j, k) for (j, k), block in zip(pairs[1:], pieces[1:])
    ]

    held, shared, back = lax.optimization_barrier((weights, shared, back))
    shared = shared[0] + shared[1]
    swapped = swap(shared)
    last = select(
        [(0, 2 * part, rest), (1, 2 * part, rest), (2, 0, most)], held, "select_last"
    )
    straight = [migrate(last[p], p) for p in range(GROUP - 1)]

    mixed = pl.pallas_call(
        functools.partial(combine_kernel, experts),
        out_shape=shape(tokens.shape[0], width),
        in_specs=[VMEM, VMEM] + [VMEM] * len(back),
        out_specs=VMEM,
        compiler_params=params(),
        cost_estimate=cost(2),
        name="combine",
    )(expert_ids, combine, *back)

    arrived = pl.pallas_call(
        functools.partial(merge_kernel, part),
        out_shape=shape(3, most, width),
        in_specs=[HBM] * 5,
        out_specs=HBM,
        scratch_shapes=[pltpu.SemaphoreType.DMA((9,))],
        compiler_params=params(),
        name="merge",
    )(shared, swapped, *straight)
    return mixed, arrived


def solution(mesh):
    placed = (
        P(("replica", "expert"), None),
        P(("replica", "expert"), None),
        P(("replica", "expert"), None),
        P("expert", None),
        P("expert", None),
        P("expert", None),
        P(),
    )
    return jax.shard_map(
        on_device,
        mesh=mesh,
        in_specs=placed,
        out_specs=(P(("replica", "expert"), None), P("replica", "expert", None)),
        check_vma=False,
    )
```

time: 78.5 us -> 44.9 us (0.57)
  Pallas kernels: 23.9 us -> 5.23 us
  starting transfers between devices: 25.3 us -> 17.6 us
  waiting for transfers between devices: 22.5 us -> 18.9 us
  local copies, waits for them, and re-layouts: 4.82 us -> 1.99 us
    pallas_call x1, Pallas kernels: 13.7 us -> 1.08 us  [on_device(): pl.pallas_call(functools.partial(merge_kernel, part), out_shape=shape(3,...]
    ppermute x14 -> x8, waiting for transfers between devices: 19.2 us -> 7.26 us  [send(): return lax.ppermute(block, 'expert', route)]
    ppermute x5, waiting for transfers between devices: 2.03 us -> 11.6 us  [migrate(): return lax.ppermute(block, 'expert', route)]
    ppermute x14 -> x8, starting transfers between devices: 16.7 us -> 9.59 us  [send(): return lax.ppermute(block, 'expert', route)]
    unnamed x32 -> x21, local copies, waits for them, and re-layouts: 4.82 us -> 1.97 us
    pallas_call x2, Pallas kernels: 3.79 us -> 1.17 us  [select(): pl.pallas_call(functools.partial(select_kernel, wanted), out_shape=[shape...]
    pallas_call x1, Pallas kernels: 2.61 us -> 0.33 us  [on_device(): pl.pallas_call(functools.partial(dispatch_kernel, experts), out_shape=[sh...]
    ppermute x2 -> x1, waiting for transfers between devices: 1.31 us -> 0.01 us  [swap(): return lax.ppermute(block, ('expert', 'replica'), route)]
  transfers between devices with their start and end apart: 21 -> 14, of which waited for: 10 -> 6; matrix products, arithmetic and copies ran while one was open for 0% -> 1% of each run, Pallas kernels for 7% -> 4%
where the time goes in v4:
time: 44.9 us; the launch traced here: 44.6 us
  waiting for transfers between devices  18.9 us (42%)
  starting transfers between devices  17.6 us (39%)
  Pallas kernels  5.23 us (12%)
  local copies, waits for them, and re-layouts  1.99 us (4%)
  between operations  0.8 us (2%)
    ppermute x5, waiting for transfers between devices, migrate(): return lax.ppermute(block, 'expert', route)  11.6 us
    ppermute x8, starting transfers between devices, send(): return lax.ppermute(block, 'expert', route)  9.59 us
    ppermute x8, waiting for transfers between devices, send(): return lax.ppermute(block, 'expert', route)  7.26 us
    ppermute x5, starting transfers between devices, migrate(): return lax.ppermute(block, 'expert', route)  4.8 us
    ppermute x1, starting transfers between devices, swap(): return lax.ppermute(block, ('expert', 'replica'), route)  3.21 us
    unnamed x21, local copies, waits for them, and re-layouts  1.97 us
    pallas_call x1, Pallas kernels, on_device(): pl.pallas_call(functools.partial(combine_kernel, experts), out_shape=shap...  1.74 us
    pallas_call x2, Pallas kernels, select(): pl.pallas_call(functools.partial(select_kernel, wanted), out_shape=[shape...  1.17 us
  transfers between devices with their start and end apart: 14, of which 6 were waited for; matrix products, arithmetic and copies ran while one was open for 1% of the time, Pallas kernels for 4%

profile of v4, /device:TPU:1, one launch (start us, length us, event | category | flops | bytes accessed | tf_op | source)
XLA Modules:
  0.0 44.6 jit_solution(10511880056855554489)
XLA Ops:
  0.6 0.0 copy-start
  0.6 0.7 %copy-done = s32[128,8]{0,1:T(8,128)S(1)} copy-done((s32[128,8]{0,1:T(8,128)S(1)}, s32[128,8]{0,1:T(8,128)}, u32[]{:S(2)}) %copy-start) | copy-done | bytes 4120
  1.3 1.0 %copy-done.5 = bf16[128,2048]{1,0:T(8,128)(2,1)S(1)} copy-done((bf16[128,2048]{1,0:T(8,128)(2,1)S(1)}, bf16[128,2048]{1,0:T(8,128)(2,1)}, u32[]{:S(2)}) %copy-start.5) | copy-done | bytes 524312
  2.4 0.3 dispatch.1
  2.7 2.1 %collective-permute-start.1 = (bf16[16,2048]{1,0:T(8,128)(2,1)S(1)}, bf16[16,2048]{1,0:T(8,128)(2,1)S(1)}, u32[]{:S(2)}, u32[]{:S(2)}) collective-permute-start(bf16[16,2048]{1,0:T(8,128)(2,1)S(1)} %get-tuple-element.26), channel_id=1, source_target_pairs={{0,16},{4,20},{8,24},{12,28},{16,0},{20,4},{24,8},{28,12},{1,17},{... | collective-permute-start | bytes 196616 | tf_op jit(solution)/shard_map/ppermute | solution.py:177
  4.8 1.2 %collective-permute-start.2 = (bf16[16,2048]{1,0:T(8,128)(2,1)S(1)}, bf16[16,2048]{1,0:T(8,128)(2,1)S(1)}, u32[]{:S(2)}, u32[]{:S(2)}) collective-permute-start(bf16[16,2048]{1,0:T(8,128)(2,1)S(1)} %get-tuple-element.26), channel_id=1, source_target_pairs={{0,24},{4,28},{8,16},{12,20},{16,8},{20,12},{24,0},{28,4},{1,25},{... | collective-permute-start | bytes 196616 | tf_op jit(solution)/shard_map/ppermute | solution.py:177
  6.0 0.1 collective-permute-start
  6.1 3.8 %collective-permute-done = bf16[16,2048]{1,0:T(8,128)(2,1)S(1)} collective-permute-done((bf16[16,2048]{1,0:T(8,128)(2,1)S(1)}, bf16[16,2048]{1,0:T(8,128)(2,1)S(1)}, u32[]{:S(2)}, u32[]{:S(2)}) %collective-permute-start) | collective-permute-done | bytes 65568 | tf_op jit(solution)/shard_map/ppermute | solution.py:177
  9.9 0.0 collective-permute-done.1
  9.9 1.7 %collective-permute-start.5 = (bf16[64,2048]{1,0:T(8,128)(2,1)S(1)}, bf16[64,2048]{1,0:T(8,128)(2,1)S(1)}, u32[]{:S(2)}, u32[]{:S(2)}) collective-permute-start(bf16[64,2048]{1,0:T(8,128)(2,1)S(1)} %constant_dynamic-update-slice_fusion.mine_ref), channel_id=1, source_target_pairs={{0,4},{4,0},{8,12},{12,8},{16,20},{20,16},{24,28},{28,24},{1,5},{5... | collective-permute-start | bytes 786440 | tf_op jit(solution)/shard_map/ppermute | solution.py:177
  11.7 1.1 %collective-permute-done.5.other_ref = bf16[64,2048]{1,0:T(8,128)(2,1)S(1)} collective-permute-done((bf16[64,2048]{1,0:T(8,128)(2,1)S(1)}, bf16[64,2048]{1,0:T(8,128)(2,1)S(1)}, u32[]{:S(2)}, u32[]{:S(2)}) %collective-permute-start.5) | collective-permute-done | bytes 262176 | tf_op jit(solution)/shard_map/ppermute | solution.py:177
  12.8 0.9 %expert.1 = (f32[64,2048]{1,0:T(8,128)S(1)}, bf16[64,2048]{1,0:T(8,128)(2,1)S(1)}) custom-call(bf16[64,2048]{1,0:T(8,128)(2,1)S(1)} %constant_dynamic-update-slice_fusion.mine_ref, bf16[64,2048]{1,0:T(8,128)(2,1)S(1)} %collective-permute-done.5.other_ref, bf16[192,2048]{1,0:T(8,128)(2,1)S(1)} %copy-done.2, bf16[192,2048]{1,0:T(8,128)(2,1)S(1)} %copy-done.3, ...), custom_call_target="tpu_custom_call" | custom-call | flops 4000000000 | bytes 1000000 | tf_op jit(solution)/shard_map/expert/pallas_call | solution.py:226
  13.7 0.4 collective-permute-start.6
  14.1 0.7 %collective-permute-start.3 = (bf16[3,32,2048]{2,1,0:T(8,128)(2,1)S(1)}, bf16[3,32,2048]{2,1,0:T(8,128)(2,1)S(1)}, u32[]{:S(2)}, u32[]{:S(2)}) collective-permute-start(bf16[3,32,2048]{2,1,0:T(8,128)(2,1)S(1)} %get-tuple-element.30), channel_id=1, source_target_pairs={{12,0},{28,16},{13,1},{29,17},{14,2},{30,18},{15,3},{31,19}} | collective-permute-start | bytes 1179656 | tf_op jit(solution)/shard_map/ppermute | solution.py:181
  14.8 1.3 %collective-permute-start.4 = (bf16[3,32,2048]{2,1,0:T(8,128)(2,1)S(1)}, bf16[3,32,2048]{2,1,0:T(8,128)(2,1)S(1)}, u32[]{:S(2)}, u32[]{:S(2)}) collective-permute-start(bf16[3,32,2048]{2,1,0:T(8,128)(2,1)S(1)} %get-tuple-element.31), channel_id=1, source_target_pairs={{12,4},{28,20},{13,5},{29,21},{14,6},{30,22},{15,7},{31,23}} | collective-permute-start | bytes 1179656 | tf_op jit(solution)/shard_map/ppermute | solution.py:181
  16.2 2.8 %collective-permute-start.7 = (bf16[16,2048]{1,0:T(8,128)(2,1)S(1)}, bf16[16,2048]{1,0:T(8,128)(2,1)S(1)}, u32[]{:S(2)}, u32[]{:S(2)}) collective-permute-start(bf16[16,2048]{1,0:T(8,128)(2,1)S(1)} %get-tuple-element.50), channel_id=1, source_target_pairs={{0,8},{4,12},{8,0},{12,4},{16,24},{20,28},{24,16},{28,20},{1,9},{5... | collective-permute-start | bytes 196616 | tf_op jit(solution)/shard_map/ppermute | solution.py:177
  19.0 1.2 %collective-permute-start.8 = (bf16[16,2048]{1,0:T(8,128)(2,1)S(1)}, bf16[16,2048]{1,0:T(8,128)(2,1)S(1)}, u32[]{:S(2)}, u32[]{:S(2)}) collective-permute-start(bf16[16,2048]{1,0:T(8,128)(2,1)S(1)} %get-tuple-element.49), channel_id=1, source_target_pairs={{0,16},{4,20},{8,24},{12,28},{16,0},{20,4},{24,8},{28,12},{1,17},{... | collective-permute-start | bytes 196616 | tf_op jit(solution)/shard_map/ppermute | solution.py:177
  20.3 0.0 collective-permute-start.9
  20.3 8.0 %collective-permute-done.4 = bf16[3,32,2048]{2,1,0:T(8,128)(2,1)S(1)} collective-permute-done((bf16[3,32,2048]{2,1,0:T(8,128)(2,1)S(1)}, bf16[3,32,2048]{2,1,0:T(8,128)(2,1)S(1)}, u32[]{:S(2)}, u32[]{:S(2)}) %collective-permute-start.4) | collective-permute-done | bytes 393248 | tf_op jit(solution)/shard_map/ppermute | solution.py:181
  28.3 0.7 %collective-permute-done.7.refs_1_ = bf16[16,2048]{1,0:T(8,128)(2,1)S(1)} collective-permute-done((bf16[16,2048]{1,0:T(8,128)(2,1)S(1)}, bf16[16,2048]{1,0:T(8,128)(2,1)S(1)}, u32[]{:S(2)}, u32[]{:S(2)}) %collective-permute-start.7) | collective-permute-done | bytes 65568 | tf_op jit(solution)/shard_map/ppermute | solution.py:177
  29.0 1.7 %collective-permute-done.9.refs_3_ = bf16[16,2048]{1,0:T(8,128)(2,1)S(1)} collective-permute-done((bf16[16,2048]{1,0:T(8,128)(2,1)S(1)}, bf16[16,2048]{1,0:T(8,128)(2,1)S(1)}, u32[]{:S(2)}, u32[]{:S(2)}) %collective-permute-start.9) | collective-permute-done | bytes 65568 | tf_op jit(solution)/shard_map/ppermute | solution.py:177
  30.6 1.1 %select_last.1 = (bf16[3,32,2048]{2,1,0:T(8,128)(2,1)}, bf16[3,32,2048]{2,1,0:T(8,128)(2,1)S(1)}, bf16[3,96,2048]{2,1,0:T(8,128)(2,1)}) custom-call(s32[3,2,96]{2,1,0:T(2,128)S(1)} %bitcast.4, bf16[192,2048]{1,0:T(8,128)(2,1)S(1)} %copy-done.2, bf16[192,2048]{1,0:T(8,128)(2,1)S(1)} %copy-done.3, bf16[192,2048]{1,0:T(8,128)(2,1)S(1)} %copy-done.4), custom_call_target="tpu_custom_call" | custom-call | flops 2000000000 | bytes 1000000 | tf_op jit(solution)/shard_map/select_last/pallas_call | solution.py:192
  31.8 0.9 %collective-permute-start.13 = (bf16[3,96,2048]{2,1,0:T(8,128)(2,1)}, bf16[3,96,2048]{2,1,0:T(8,128)(2,1)S(1)}, u32[]{:S(2)}, u32[]{:S(2)}) collective-permute-start(bf16[3,96,2048]{2,1,0:T(8,128)(2,1)} %get-tuple-element.47), channel_id=1, source_target_pairs={{12,8},{28,24},{13,9},{29,25},{14,10},{30,26},{15,11},{31,27}} | collective-permute-start | bytes 3538952 | tf_op jit(solution)/shard_map/ppermute | solution.py:181
  32.7 0.7 %collective-permute-start.11 = (bf16[3,32,2048]{2,1,0:T(8,128)(2,1)}, bf16[3,32,2048]{2,1,0:T(8,128)(2,1)S(1)}, u32[]{:S(2)}, u32[]{:S(2)}) collective-permute-start(bf16[3,32,2048]{2,1,0:T(8,128)(2,1)} %get-tuple-element.45), channel_id=1, source_target_pairs={{12,0},{28,16},{13,1},{29,17},{14,2},{30,18},{15,3},{31,19}} | collective-permute-start | bytes 1179656 | tf_op jit(solution)/shard_map/ppermute | solution.py:181
  33.4 1.3 %collective-permute-start.12 = (bf16[3,32,2048]{2,1,0:T(8,128)(2,1)S(1)}, bf16[3,32,2048]{2,1,0:T(8,128)(2,1)S(1)}, u32[]{:S(2)}, u32[]{:S(2)}) collective-permute-start(bf16[3,32,2048]{2,1,0:T(8,128)(2,1)S(1)} %get-tuple-element.46), channel_id=1, source_target_pairs={{12,4},{28,20},{13,5},{29,21},{14,6},{30,22},{15,7},{31,23}} | collective-permute-start | bytes 1179656 | tf_op jit(solution)/shard_map/ppermute | solution.py:181
  34.7 0.1 add.7.shared_ref
  34.8 3.2 %collective-permute-start.10 = (bf16[3,32,2048]{2,1,0:T(8,128)(2,1)S(1)}, bf16[3,32,2048]{2,1,0:T(8,128)(2,1)S(1)}, u32[]{:S(2)}, u32[]{:S(2)}) collective-permute-start(bf16[3,32,2048]{2,1,0:T(8,128)(2,1)S(1)} %add.7.shared_ref), channel_id=1, source_target_pairs={{0,1},{4,5},{16,17},{20,21},{1,0},{5,4},{17,16},{21,20},{2,3},{6,7... | collective-permute-start | bytes 1179656 | tf_op jit(solution)/shard_map/ppermute | solution.py:189
  38.0 0.1 copy.9.ids_ref
  38.1 0.1 copy.10.weight_ref
  38.2 1.7 %combine.1 = bf16[128,2048]{1,0:T(8,128)(2,1)} custom-call(s32[128,8]{1,0:T(8,128)S(1)} %copy.9.ids_ref, f32[128,8]{1,0:T(8,128)S(1)} %copy.10.weight_ref, bf16[16,2048]{1,0:T(8,128)(2,1)S(1)} %get-tuple-element.36.refs_0_, bf16[16,2048]{1,0:T(8,128)(2,1)S(1)} %collective-permute-done.7.refs_1_, bf16[16,2048]{1,0:T(8,128)(2,1)S(1)} %collective-permute-done.8.refs_2_, ...), custom_call_target="tpu_custom_call" | custom-call | flops 2000000000 | bytes 1000000 | tf_op jit(solution)/shard_map/combine/pallas_call | solution.py:251
  39.9 3.6 %collective-permute-done.12.second_ref = bf16[3,32,2048]{2,1,0:T(8,128)(2,1)S(1)} collective-permute-done((bf16[3,32,2048]{2,1,0:T(8,128)(2,1)S(1)}, bf16[3,32,2048]{2,1,0:T(8,128)(2,1)S(1)}, u32[]{:S(2)}, u32[]{:S(2)}) %collective-permute-start.12) | collective-permute-done | bytes 393248 | tf_op jit(solution)/shard_map/ppermute | solution.py:181
  43.5 1.1 %merge.1 = bf16[3,96,2048]{2,1,0:T(8,128)(2,1)} custom-call(bf16[3,32,2048]{2,1,0:T(8,128)(2,1)S(1)} %add.7.shared_ref, bf16[3,32,2048]{2,1,0:T(8,128)(2,1)S(1)} %collective-permute-done.10.swapped_ref, bf16[3,32,2048]{2,1,0:T(8,128)(2,1)S(1)} %collective-permute-done.11.first_ref, bf16[3,32,2048]{2,1,0:T(8,128)(2,1)S(1)} %collective-permute-done.12.second_ref, ...), custom_call_target="tpu_custom_call" | custom-call | tf_op jit(solution)/shard_map/merge/pallas_call | solution.py:261
  (27 shorter events, 0.2 us)
Async XLA Ops:
  0.6 0.7 %copy-start = (s32[128,8]{0,1:T(8,128)S(1)}, s32[128,8]{0,1:T(8,128)}, u32[]{:S(2)}) copy-start(s32[128,8]{0,1:T(8,128)} %param.8) | copy-start | bytes 12292
  1.3 1.0 %copy-start.5 = (bf16[128,2048]{1,0:T(8,128)(2,1)S(1)}, bf16[128,2048]{1,0:T(8,128)(2,1)}, u32[]{:S(2)}) copy-start(bf16[128,2048]{1,0:T(8,128)(2,1)} %tok_ref.1) | copy-start | bytes 1572868
  2.4 9.3 %copy-start.2 = (bf16[192,2048]{1,0:T(8,128)(2,1)S(1)}, bf16[192,2048]{1,0:T(8,128)(2,1)}, u32[]{:S(2)}) copy-start(bf16[192,2048]{1,0:T(8,128)(2,1)} %gate_ref.3) | copy-start | bytes 2359300
  2.4 9.3 %copy-start.3 = (bf16[192,2048]{1,0:T(8,128)(2,1)S(1)}, bf16[192,2048]{1,0:T(8,128)(2,1)}, u32[]{:S(2)}) copy-start(bf16[192,2048]{1,0:T(8,128)(2,1)} %up_ref.3) | copy-start | bytes 2359300
  2.4 9.3 %copy-start.4 = (bf16[192,2048]{1,0:T(8,128)(2,1)S(1)}, bf16[192,2048]{1,0:T(8,128)(2,1)}, u32[]{:S(2)}) copy-start(bf16[192,2048]{1,0:T(8,128)(2,1)} %down_ref.3) | copy-start | bytes 2359300
  2.4 9.3 %copy-start.6 = (s32[2,3,96]{2,0,1:T(2,128)S(1)}, s32[2,3,96]{2,0,1:T(2,128)}, u32[]{:S(2)}) copy-start(s32[2,3,96]{2,0,1:T(2,128)} %param.13) | copy-start | bytes 6916
  2.7 7.2 %collective-permute-start.1 = (bf16[16,2048]{1,0:T(8,128)(2,1)S(1)}, bf16[16,2048]{1,0:T(8,128)(2,1)S(1)}, u32[]{:S(2)}, u32[]{:S(2)}) collective-permute-start(bf16[16,2048]{1,0:T(8,128)(2,1)S(1)} %get-tuple-element.26), channel_id=1, source_target_pairs={{0,16},{4,20},{8,24},{12,28},{16,0},{20,4},{24,8},{28,12},{1,17},{... | collective-permute-start | bytes 196616 | tf_op jit(solution)/shard_map/ppermute | solution.py:177
  4.8 5.1 %collective-permute-start.2 = (bf16[16,2048]{1,0:T(8,128)(2,1)S(1)}, bf16[16,2048]{1,0:T(8,128)(2,1)S(1)}, u32[]{:S(2)}, u32[]{:S(2)}) collective-permute-start(bf16[16,2048]{1,0:T(8,128)(2,1)S(1)} %get-tuple-element.26), channel_id=1, source_target_pairs={{0,24},{4,28},{8,16},{12,20},{16,8},{20,12},{24,0},{28,4},{1,25},{... | collective-permute-start | bytes 196616 | tf_op jit(solution)/shard_map/ppermute | solution.py:177
  6.0 3.9 %collective-permute-start = (bf16[16,2048]{1,0:T(8,128)(2,1)S(1)}, bf16[16,2048]{1,0:T(8,128)(2,1)S(1)}, u32[]{:S(2)}, u32[]{:S(2)}) collective-permute-start(bf16[16,2048]{1,0:T(8,128)(2,1)S(1)} %get-tuple-element.25), channel_id=1, source_target_pairs={{0,8},{4,12},{8,0},{12,4},{16,24},{20,28},{24,16},{28,20},{1,9},{5... | collective-permute-start | bytes 196616 | tf_op jit(solution)/shard_map/ppermute | solution.py:177
  9.9 2.8 %collective-permute-start.5 = (bf16[64,2048]{1,0:T(8,128)(2,1)S(1)}, bf16[64,2048]{1,0:T(8,128)(2,1)S(1)}, u32[]{:S(2)}, u32[]{:S(2)}) collective-permute-start(bf16[64,2048]{1,0:T(8,128)(2,1)S(1)} %constant_dynamic-update-slice_fusion.mine_ref), channel_id=1, source_target_pairs={{0,4},{4,0},{8,12},{12,8},{16,20},{20,16},{24,28},{28,24},{1,5},{5... | collective-permute-start | bytes 786440 | tf_op jit(solution)/shard_map/ppermute | solution.py:177
  13.7 2.4 %collective-permute-start.6 = (bf16[64,2048]{1,0:T(8,128)(2,1)S(1)}, bf16[64,2048]{1,0:T(8,128)(2,1)S(1)}, u32[]{:S(2)}, u32[]{:S(2)}) collective-permute-start(bf16[64,2048]{1,0:T(8,128)(2,1)S(1)} %get-tuple-element.35), channel_id=1, source_target_pairs={{0,4},{4,0},{8,12},{12,8},{16,20},{20,16},{24,28},{28,24},{1,5},{5... | collective-permute-start | bytes 786440 | tf_op jit(solution)/shard_map/ppermute | solution.py:177
  14.1 6.2 %collective-permute-start.3 = (bf16[3,32,2048]{2,1,0:T(8,128)(2,1)S(1)}, bf16[3,32,2048]{2,1,0:T(8,128)(2,1)S(1)}, u32[]{:S(2)}, u32[]{:S(2)}) collective-permute-start(bf16[3,32,2048]{2,1,0:T(8,128)(2,1)S(1)} %get-tuple-element.30), channel_id=1, source_target_pairs={{12,0},{28,16},{13,1},{29,17},{14,2},{30,18},{15,3},{31,19}} | collective-permute-start | bytes 1179656 | tf_op jit(solution)/shard_map/ppermute | solution.py:181
  14.8 13.5 %collective-permute-start.4 = (bf16[3,32,2048]{2,1,0:T(8,128)(2,1)S(1)}, bf16[3,32,2048]{2,1,0:T(8,128)(2,1)S(1)}, u32[]{:S(2)}, u32[]{:S(2)}) collective-permute-start(bf16[3,32,2048]{2,1,0:T(8,128)(2,1)S(1)} %get-tuple-element.31), channel_id=1, source_target_pairs={{12,4},{28,20},{13,5},{29,21},{14,6},{30,22},{15,7},{31,23}} | collective-permute-start | bytes 1179656 | tf_op jit(solution)/shard_map/ppermute | solution.py:181
  16.2 12.8 %collective-permute-start.7 = (bf16[16,2048]{1,0:T(8,128)(2,1)S(1)}, bf16[16,2048]{1,0:T(8,128)(2,1)S(1)}, u32[]{:S(2)}, u32[]{:S(2)}) collective-permute-start(bf16[16,2048]{1,0:T(8,128)(2,1)S(1)} %get-tuple-element.50), channel_id=1, source_target_pairs={{0,8},{4,12},{8,0},{12,4},{16,24},{20,28},{24,16},{28,20},{1,9},{5... | collective-permute-start | bytes 196616 | tf_op jit(solution)/shard_map/ppermute | solution.py:177
  19.0 10.0 %collective-permute-start.8 = (bf16[16,2048]{1,0:T(8,128)(2,1)S(1)}, bf16[16,2048]{1,0:T(8,128)(2,1)S(1)}, u32[]{:S(2)}, u32[]{:S(2)}) collective-permute-start(bf16[16,2048]{1,0:T(8,128)(2,1)S(1)} %get-tuple-element.49), channel_id=1, source_target_pairs={{0,16},{4,20},{8,24},{12,28},{16,0},{20,4},{24,8},{28,12},{1,17},{... | collective-permute-start | bytes 196616 | tf_op jit(solution)/shard_map/ppermute | solution.py:177
  20.3 10.4 %collective-permute-start.9 = (bf16[16,2048]{1,0:T(8,128)(2,1)S(1)}, bf16[16,2048]{1,0:T(8,128)(2,1)S(1)}, u32[]{:S(2)}, u32[]{:S(2)}) collective-permute-start(bf16[16,2048]{1,0:T(8,128)(2,1)S(1)} %get-tuple-element.48), channel_id=1, source_target_pairs={{0,24},{4,28},{8,16},{12,20},{16,8},{20,12},{24,0},{28,4},{1,25},{... | collective-permute-start | bytes 196616 | tf_op jit(solution)/shard_map/ppermute | solution.py:177
  31.8 6.2 %copy-start.1 = (s32[128,8]{0,1:T(8,128)S(1)}, s32[128,8]{0,1:T(8,128)}, u32[]{:S(2)}) copy-start(s32[128,8]{0,1:T(8,128)} %param.8) | copy-start | bytes 12292
  31.8 6.3 %copy-start.7 = (f32[128,8]{0,1:T(8,128)S(1)}, f32[128,8]{0,1:T(8,128)}, u32[]{:S(2)}) copy-start(f32[128,8]{0,1:T(8,128)} %param.9) | copy-start | bytes 12292
  31.8 11.7 %collective-permute-start.13 = (bf16[3,96,2048]{2,1,0:T(8,128)(2,1)}, bf16[3,96,2048]{2,1,0:T(8,128)(2,1)S(1)}, u32[]{:S(2)}, u32[]{:S(2)}) collective-permute-start(bf16[3,96,2048]{2,1,0:T(8,128)(2,1)} %get-tuple-element.47), channel_id=1, source_target_pairs={{12,8},{28,24},{13,9},{29,25},{14,10},{30,26},{15,11},{31,27}} | collective-permute-start | bytes 3538952 | tf_op jit(solution)/shard_map/ppermute | solution.py:181
  32.7 7.3 %collective-permute-start.11 = (bf16[3,32,2048]{2,1,0:T(8,128)(2,1)}, bf16[3,32,2048]{2,1,0:T(8,128)(2,1)S(1)}, u32[]{:S(2)}, u32[]{:S(2)}) collective-permute-start(bf16[3,32,2048]{2,1,0:T(8,128)(2,1)} %get-tuple-element.45), channel_id=1, source_target_pairs={{12,0},{28,16},{13,1},{29,17},{14,2},{30,18},{15,3},{31,19}} | collective-permute-start | bytes 1179656 | tf_op jit(solution)/shard_map/ppermute | solution.py:181
  33.4 10.2 %collective-permute-start.12 = (bf16[3,32,2048]{2,1,0:T(8,128)(2,1)S(1)}, bf16[3,32,2048]{2,1,0:T(8,128)(2,1)S(1)}, u32[]{:S(2)}, u32[]{:S(2)}) collective-permute-start(bf16[3,32,2048]{2,1,0:T(8,128)(2,1)S(1)} %get-tuple-element.46), channel_id=1, source_target_pairs={{12,4},{28,20},{13,5},{29,21},{14,6},{30,22},{15,7},{31,23}} | collective-permute-start | bytes 1179656 | tf_op jit(solution)/shard_map/ppermute | solution.py:181
  34.8 8.8 %collective-permute-start.10 = (bf16[3,32,2048]{2,1,0:T(8,128)(2,1)S(1)}, bf16[3,32,2048]{2,1,0:T(8,128)(2,1)S(1)}, u32[]{:S(2)}, u32[]{:S(2)}) collective-permute-start(bf16[3,32,2048]{2,1,0:T(8,128)(2,1)S(1)} %add.7.shared_ref), channel_id=1, source_target_pairs={{0,1},{4,5},{16,17},{20,21},{1,0},{5,4},{17,16},{21,20},{2,3},{6,7... | collective-permute-start | bytes 1179656 | tf_op jit(solution)/shard_map/ppermute | solution.py:189

commit v5 on v4

--- a/solution.py
+++ b/solution.py
@@ -22,7 +22,7 @@
 
 def cost(microseconds):
     return pl.CostEstimate(
-        flops=microseconds * 10**9, bytes_accessed=10**6, transcendentals=0
+        flops=microseconds * 10**9, bytes_accessed=10**4, transcendentals=0
     )
 
 
@@ -188,7 +188,7 @@
                     route.append((i * replicas + r, i * replicas + (r ^ 1)))
         return lax.ppermute(block, ("expert", "replica"), route)
 
-    def select(wanted, held, name):
+    def select(wanted, held):
         return pl.pallas_call(
             functools.partial(select_kernel, wanted),
             out_shape=[shape(3, count, width) for _, _, count in wanted],
@@ -196,7 +196,7 @@
             out_specs=[VMEM] * len(wanted),
             compiler_params=params(),
             cost_estimate=cost(2),
-            name=name,
+            name="select",
         )(plan, *held)
 
     parcels = pl.pallas_call(
@@ -211,13 +211,17 @@
 
     pairs = [(j, k) for j in range(experts) for k in (0, 2)]
     mine = [parcels[0]] + [send(parcels[j], j, k) for j, k in pairs[1:]]
+    held, parcels = lax.optimization_barrier((weights, parcels))
+    chosen = select(
+        [(0, None, part), (1, None, part)]
+        + [(0, 2 * part, rest), (1, 2 * part, rest), (2, 0, most)],
+        held,
+    )
+    mine, chosen = lax.optimization_barrier((mine, chosen))
     mine = jnp.concatenate(mine, axis=0)
     other = send(mine, 0, 1)
 
-    held, mine = lax.optimization_barrier((weights, mine))
-    first = select([(0, None, part), (1, None, part)], held, "select_first")
-    shared = [migrate(first[p], p) for p in range(2)]
-    other, _ = lax.optimization_barrier((other, first))
+    shared = [migrate(chosen[p], p) for p in range(2)]
 
     total = mine.shape[0]
     step = min(total, 64)
@@ -233,19 +237,16 @@
         cost_estimate=cost(4),
         name="expert",
     )(mine, other, *weights)
-    taken = send(give, 0, 1)
+    shared = shared[0] + shared[1]
+    taken, shared = lax.optimization_barrier((send(give, 0, 1), shared))
     summed = (keep + taken.astype(F32)).astype(BF16)
     pieces = [summed[n * SLOTS : (n + 1) * SLOTS] for n in range(len(pairs))]
     back = [pieces[0]] + [
         send(block, -j, k) for (j, k), block in zip(pairs[1:], pieces[1:])
     ]
 
-    held, shared, back = lax.optimization_barrier((weights, shared, back))
-    shared = shared[0] + shared[1]
     swapped = swap(shared)
-    last = select(
-        [(0, 2 * part, rest), (1, 2 * part, rest), (2, 0, most)], held, "select_last"
-    )
+    last, _ = lax.optimization_barrier((chosen[2:], summed))
     straight = [migrate(last[p], p) for p in range(GROUP - 1)]
 
     mixed = pl.pallas_call(
@@ -254,7 +255,7 @@
         in_specs=[VMEM, VMEM] + [VMEM] * len(back),
         out_specs=VMEM,
         compiler_params=params(),
-        cost_estimate=cost(2),
+        cost_estimate=cost(12),
         name="combine",
     )(expert_ids, combine, *back)
 

time: 44.9 us -> 42.6 us (0.949)
  starting transfers between devices: 17.6 us -> 15.7 us
  Pallas kernels: 5.23 us -> 4.1 us
  local copies, waits for them, and re-layouts: 1.99 us -> 2.66 us
    ppermute x8, waiting for transfers between devices: 7.26 us -> 3.74 us  [send(): return lax.ppermute(block, 'expert', route)]
    ppermute x5, waiting for transfers between devices: 11.6 us -> 14.2 us  [migrate(): return lax.ppermute(block, 'expert', route)]
    ppermute x8, starting transfers between devices: 9.59 us -> 7.81 us  [send(): return lax.ppermute(block, 'expert', route)]
    pallas_call x2 -> x1, Pallas kernels: 1.17 us -> 0.02 us  [select(): pl.pallas_call(functools.partial(select_kernel, wanted), out_shape=[shape...]
    ppermute x1, waiting for transfers between devices: 0.01 us -> 0.97 us  [swap(): return lax.ppermute(block, ('expert', 'replica'), route)]
    slice x1, local copies, waits for them, and re-layouts: 0.02 us -> 0.67 us  [on_device(): pieces = [summed[n * SLOTS:(n + 1) * SLOTS] for n in range(len(pairs))]]
    unnamed x21 -> x23, local copies, waits for them, and re-layouts: 1.97 us -> 1.98 us
  transfers between devices with their start and end apart: 14 -> 14, of which waited for: 6 -> 4; matrix products, arithmetic and copies ran while one was open for 1% -> 1% of each run, Pallas kernels for 4% -> 6%
where the time goes in v5:
time: 42.6 us; the launch traced here: 42.3 us
  waiting for transfers between devices  18.9 us (44%)
  starting transfers between devices  15.7 us (37%)
  Pallas kernels  4.1 us (10%)
  local copies, waits for them, and re-layouts  2.66 us (6%)
  between operations  0.85 us (2%)
    ppermute x5, waiting for transfers between devices, migrate(): return lax.ppermute(block, 'expert', route)  14.2 us
    ppermute x8, starting transfers between devices, send(): return lax.ppermute(block, 'expert', route)  7.81 us
    ppermute x5, starting transfers between devices, migrate(): return lax.ppermute(block, 'expert', route)  4.66 us
    ppermute x8, waiting for transfers between devices, send(): return lax.ppermute(block, 'expert', route)  3.74 us
    ppermute x1, starting transfers between devices, swap(): return lax.ppermute(block, ('expert', 'replica'), route)  3.2 us
    unnamed x23, local copies, waits for them, and re-layouts  1.98 us
    pallas_call x1, Pallas kernels, on_device(): pl.pallas_call(functools.partial(combine_kernel, experts), out_shape=shap...  1.75 us
    pallas_call x1, Pallas kernels, on_device(): pl.pallas_call(functools.partial(merge_kernel, part), out_shape=shape(3,...  1.08 us
  transfers between devices with their start and end apart: 14, of which 4 were waited for; matrix products, arithmetic and copies ran while one was open for 1% of the time, Pallas kernels for 6%

profile of v5, /device:TPU:1, one launch (start us, length us, event | category | flops | bytes accessed | tf_op | source)
XLA Modules:
  0.0 42.3 jit_solution(2159684708862467394)
XLA Ops:
  0.6 0.0 copy-start
  0.6 0.7 %copy-done = s32[128,8]{0,1:T(8,128)S(1)} copy-done((s32[128,8]{0,1:T(8,128)S(1)}, s32[128,8]{0,1:T(8,128)}, u32[]{:S(2)}) %copy-start) | copy-done | bytes 4120
  1.3 1.0 %copy-done.5 = bf16[128,2048]{1,0:T(8,128)(2,1)S(1)} copy-done((bf16[128,2048]{1,0:T(8,128)(2,1)S(1)}, bf16[128,2048]{1,0:T(8,128)(2,1)}, u32[]{:S(2)}) %copy-start.5) | copy-done | bytes 524312
  2.4 0.3 dispatch.1
  2.7 2.1 %collective-permute-start.1 = (bf16[16,2048]{1,0:T(8,128)(2,1)S(1)}, bf16[16,2048]{1,0:T(8,128)(2,1)S(1)}, u32[]{:S(2)}, u32[]{:S(2)}) collective-permute-start(bf16[16,2048]{1,0:T(8,128)(2,1)S(1)} %get-tuple-element.29), channel_id=1, source_target_pairs={{0,16},{4,20},{8,24},{12,28},{16,0},{20,4},{24,8},{28,12},{1,17},{... | collective-permute-start | bytes 196616 | tf_op jit(solution)/shard_map/ppermute | solution.py:177
  4.8 1.2 %collective-permute-start.2 = (bf16[16,2048]{1,0:T(8,128)(2,1)S(1)}, bf16[16,2048]{1,0:T(8,128)(2,1)S(1)}, u32[]{:S(2)}, u32[]{:S(2)}) collective-permute-start(bf16[16,2048]{1,0:T(8,128)(2,1)S(1)} %get-tuple-element.29), channel_id=1, source_target_pairs={{0,24},{4,28},{8,16},{12,20},{16,8},{20,12},{24,0},{28,4},{1,25},{... | collective-permute-start | bytes 196616 | tf_op jit(solution)/shard_map/ppermute | solution.py:177
  6.0 0.1 collective-permute-start
  6.2 0.0 copy-start.6
  6.2 3.7 %collective-permute-done = bf16[16,2048]{1,0:T(8,128)(2,1)S(1)} collective-permute-done((bf16[16,2048]{1,0:T(8,128)(2,1)S(1)}, bf16[16,2048]{1,0:T(8,128)(2,1)S(1)}, u32[]{:S(2)}, u32[]{:S(2)}) %collective-permute-start) | collective-permute-done | bytes 65568 | tf_op jit(solution)/shard_map/ppermute | solution.py:177
  9.9 1.7 %collective-permute-start.3 = (bf16[64,2048]{1,0:T(8,128)(2,1)S(1)}, bf16[64,2048]{1,0:T(8,128)(2,1)S(1)}, u32[]{:S(2)}, u32[]{:S(2)}) collective-permute-start(bf16[64,2048]{1,0:T(8,128)(2,1)S(1)} %constant_dynamic-update-slice_fusion.mine_ref), channel_id=1, source_target_pairs={{0,4},{4,0},{8,12},{12,8},{16,20},{20,16},{24,28},{28,24},{1,5},{5... | collective-permute-start | bytes 786440 | tf_op jit(solution)/shard_map/ppermute | solution.py:177
  11.6 0.7 %collective-permute-start.5 = (bf16[3,32,2048]{2,1,0:T(8,128)(2,1)S(1)}, bf16[3,32,2048]{2,1,0:T(8,128)(2,1)S(1)}, u32[]{:S(2)}, u32[]{:S(2)}) collective-permute-start(bf16[3,32,2048]{2,1,0:T(8,128)(2,1)S(1)} %get-tuple-element.44), channel_id=1, source_target_pairs={{12,0},{28,16},{13,1},{29,17},{14,2},{30,18},{15,3},{31,19}} | collective-permute-start | bytes 1179656 | tf_op jit(solution)/shard_map/ppermute | solution.py:181
  12.3 1.3 %collective-permute-start.6 = (bf16[3,32,2048]{2,1,0:T(8,128)(2,1)S(1)}, bf16[3,32,2048]{2,1,0:T(8,128)(2,1)S(1)}, u32[]{:S(2)}, u32[]{:S(2)}) collective-permute-start(bf16[3,32,2048]{2,1,0:T(8,128)(2,1)S(1)} %get-tuple-element.45), channel_id=1, source_target_pairs={{12,4},{28,20},{13,5},{29,21},{14,6},{30,22},{15,7},{31,23}} | collective-permute-start | bytes 1179656 | tf_op jit(solution)/shard_map/ppermute | solution.py:181
  13.6 0.9 %expert.1 = (f32[64,2048]{1,0:T(8,128)S(1)}, bf16[64,2048]{1,0:T(8,128)(2,1)S(1)}) custom-call(bf16[64,2048]{1,0:T(8,128)(2,1)S(1)} %constant_dynamic-update-slice_fusion.mine_ref, bf16[64,2048]{1,0:T(8,128)(2,1)S(1)} %collective-permute-done.3.other_ref, bf16[192,2048]{1,0:T(8,128)(2,1)S(1)} %copy-done.2, bf16[192,2048]{1,0:T(8,128)(2,1)S(1)} %copy-done.3, ...), custom_call_target="tpu_custom_call" | custom-call | flops 4000000000 | bytes 10000 | tf_op jit(solution)/shard_map/expert/pallas_call | solution.py:230
  14.6 0.0 copy-start.1
  14.6 0.0 copy-start.8
  14.6 0.1 collective-permute-start.4
  14.7 9.6 %collective-permute-done.6 = bf16[3,32,2048]{2,1,0:T(8,128)(2,1)S(1)} collective-permute-done((bf16[3,32,2048]{2,1,0:T(8,128)(2,1)S(1)}, bf16[3,32,2048]{2,1,0:T(8,128)(2,1)S(1)}, u32[]{:S(2)}, u32[]{:S(2)}) %collective-permute-start.6) | collective-permute-done | bytes 393248 | tf_op jit(solution)/shard_map/ppermute | solution.py:181
  24.3 0.1 add.6.shared_ref
  24.4 0.1 add_convert_fusion
  24.4 0.7 %fusion = (bf16[16,2048]{1,0:T(8,128)(2,1)}, bf16[16,2048]{1,0:T(8,128)(2,1)}, bf16[16,2048]{1,0:T(8,128)(2,1)}, bf16[16,2048]{1,0:T(8,128)(2,1)S(1)}) fusion(bf16[64,2048]{1,0:T(8,128)(2,1)S(1)} %add_convert_fusion), kind=kLoop, calls=%fused_computation.5 | loop fusion | bytes 524288 | tf_op jit(solution)/shard_map/slice | solution.py:243
  25.1 1.2 %collective-permute-start.8 = (bf16[16,2048]{1,0:T(8,128)(2,1)}, bf16[16,2048]{1,0:T(8,128)(2,1)S(1)}, u32[]{:S(2)}, u32[]{:S(2)}) collective-permute-start(bf16[16,2048]{1,0:T(8,128)(2,1)} %get-tuple-element.55), channel_id=1, source_target_pairs={{0,16},{4,20},{8,24},{12,28},{16,0},{20,4},{24,8},{28,12},{1,17},{... | collective-permute-start | bytes 196616 | tf_op jit(solution)/shard_map/ppermute | solution.py:177
  26.4 1.4 %collective-permute-start.9 = (bf16[16,2048]{1,0:T(8,128)(2,1)}, bf16[16,2048]{1,0:T(8,128)(2,1)S(1)}, u32[]{:S(2)}, u32[]{:S(2)}) collective-permute-start(bf16[16,2048]{1,0:T(8,128)(2,1)} %get-tuple-element.54), channel_id=1, source_target_pairs={{0,24},{4,28},{8,16},{12,20},{16,8},{20,12},{24,0},{28,4},{1,25},{... | collective-permute-start | bytes 196616 | tf_op jit(solution)/shard_map/ppermute | solution.py:177
  27.8 0.7 %collective-permute-start.13 = (bf16[3,96,2048]{2,1,0:T(8,128)(2,1)S(1)}, bf16[3,96,2048]{2,1,0:T(8,128)(2,1)S(1)}, u32[]{:S(2)}, u32[]{:S(2)}) collective-permute-start(bf16[3,96,2048]{2,1,0:T(8,128)(2,1)S(1)} %get-tuple-element.53), channel_id=1, source_target_pairs={{12,8},{28,24},{13,9},{29,25},{14,10},{30,26},{15,11},{31,27}} | collective-permute-start | bytes 3538952 | tf_op jit(solution)/shard_map/ppermute | solution.py:181
  28.5 0.1 copy.9.ids_ref
  28.6 0.1 copy.10.weight_ref
  28.7 0.7 %collective-permute-start.11 = (bf16[3,32,2048]{2,1,0:T(8,128)(2,1)}, bf16[3,32,2048]{2,1,0:T(8,128)(2,1)S(1)}, u32[]{:S(2)}, u32[]{:S(2)}) collective-permute-start(bf16[3,32,2048]{2,1,0:T(8,128)(2,1)} %copy-done.6), channel_id=1, source_target_pairs={{12,0},{28,16},{13,1},{29,17},{14,2},{30,18},{15,3},{31,19}} | collective-permute-start | bytes 1179656 | tf_op jit(solution)/shard_map/ppermute | solution.py:181
  29.4 1.3 %collective-permute-start.12 = (bf16[3,32,2048]{2,1,0:T(8,128)(2,1)S(1)}, bf16[3,32,2048]{2,1,0:T(8,128)(2,1)S(1)}, u32[]{:S(2)}, u32[]{:S(2)}) collective-permute-start(bf16[3,32,2048]{2,1,0:T(8,128)(2,1)S(1)} %get-tuple-element.52), channel_id=1, source_target_pairs={{12,4},{28,20},{13,5},{29,21},{14,6},{30,22},{15,7},{31,23}} | collective-permute-start | bytes 1179656 | tf_op jit(solution)/shard_map/ppermute | solution.py:181
  30.7 3.2 %collective-permute-start.10 = (bf16[3,32,2048]{2,1,0:T(8,128)(2,1)S(1)}, bf16[3,32,2048]{2,1,0:T(8,128)(2,1)S(1)}, u32[]{:S(2)}, u32[]{:S(2)}) collective-permute-start(bf16[3,32,2048]{2,1,0:T(8,128)(2,1)S(1)} %add.6.shared_ref), channel_id=1, source_target_pairs={{0,1},{4,5},{16,17},{20,21},{1,0},{5,4},{17,16},{21,20},{2,3},{6,7... | collective-permute-start | bytes 1179656 | tf_op jit(solution)/shard_map/ppermute | solution.py:189
  33.9 1.8 %combine.1 = bf16[128,2048]{1,0:T(8,128)(2,1)} custom-call(s32[128,8]{1,0:T(8,128)S(1)} %copy.9.ids_ref, f32[128,8]{1,0:T(8,128)S(1)} %copy.10.weight_ref, bf16[16,2048]{1,0:T(8,128)(2,1)S(1)} %get-tuple-element.57.refs_0_, bf16[16,2048]{1,0:T(8,128)(2,1)S(1)} %collective-permute-done.7.refs_1_, bf16[16,2048]{1,0:T(8,128)(2,1)S(1)} %collective-permute-done.8.refs_2_, ...), custom_call_target="tpu_custom_call" | custom-call | flops 12000000000 | bytes 10000 | tf_op jit(solution)/shard_map/combine/pallas_call | solution.py:252
  35.7 4.6 %collective-permute-done.12.second_ref = bf16[3,32,2048]{2,1,0:T(8,128)(2,1)S(1)} collective-permute-done((bf16[3,32,2048]{2,1,0:T(8,128)(2,1)S(1)}, bf16[3,32,2048]{2,1,0:T(8,128)(2,1)S(1)}, u32[]{:S(2)}, u32[]{:S(2)}) %collective-permute-start.12) | collective-permute-done | bytes 393248 | tf_op jit(solution)/shard_map/ppermute | solution.py:181
  40.3 1.0 %collective-permute-done.10.swapped_ref = bf16[3,32,2048]{2,1,0:T(8,128)(2,1)S(1)} collective-permute-done((bf16[3,32,2048]{2,1,0:T(8,128)(2,1)S(1)}, bf16[3,32,2048]{2,1,0:T(8,128)(2,1)S(1)}, u32[]{:S(2)}, u32[]{:S(2)}) %collective-permute-start.10) | collective-permute-done | bytes 393248 | tf_op jit(solution)/shard_map/ppermute | solution.py:189
  41.2 1.1 %merge.1 = bf16[3,96,2048]{2,1,0:T(8,128)(2,1)} custom-call(bf16[3,32,2048]{2,1,0:T(8,128)(2,1)S(1)} %add.6.shared_ref, bf16[3,32,2048]{2,1,0:T(8,128)(2,1)S(1)} %collective-permute-done.10.swapped_ref, bf16[3,32,2048]{2,1,0:T(8,128)(2,1)S(1)} %collective-permute-done.11.first_ref, bf16[3,32,2048]{2,1,0:T(8,128)(2,1)S(1)} %collective-permute-done.12.second_ref, ...), custom_call_target="tpu_custom_call" | custom-call | tf_op jit(solution)/shard_map/merge/pallas_call | solution.py:262
  (28 shorter events, 0.1 us)
Async XLA Ops:
  0.6 0.7 %copy-start = (s32[128,8]{0,1:T(8,128)S(1)}, s32[128,8]{0,1:T(8,128)}, u32[]{:S(2)}) copy-start(s32[128,8]{0,1:T(8,128)} %param.8) | copy-start | bytes 12292
  1.3 1.0 %copy-start.5 = (bf16[128,2048]{1,0:T(8,128)(2,1)S(1)}, bf16[128,2048]{1,0:T(8,128)(2,1)}, u32[]{:S(2)}) copy-start(bf16[128,2048]{1,0:T(8,128)(2,1)} %tok_ref.1) | copy-start | bytes 1572868
  2.4 3.7 %copy-start.2 = (bf16[192,2048]{1,0:T(8,128)(2,1)S(1)}, bf16[192,2048]{1,0:T(8,128)(2,1)}, u32[]{:S(2)}) copy-start(bf16[192,2048]{1,0:T(8,128)(2,1)} %gate_ref.2) | copy-start | bytes 2359300
  2.4 3.7 %copy-start.3 = (bf16[192,2048]{1,0:T(8,128)(2,1)S(1)}, bf16[192,2048]{1,0:T(8,128)(2,1)}, u32[]{:S(2)}) copy-start(bf16[192,2048]{1,0:T(8,128)(2,1)} %up_ref.2) | copy-start | bytes 2359300
  2.4 3.7 %copy-start.4 = (bf16[192,2048]{1,0:T(8,128)(2,1)S(1)}, bf16[192,2048]{1,0:T(8,128)(2,1)}, u32[]{:S(2)}) copy-start(bf16[192,2048]{1,0:T(8,128)(2,1)} %down_ref.2) | copy-start | bytes 2359300
  2.4 3.7 %copy-start.7 = (s32[2,3,96]{2,0,1:T(2,128)S(1)}, s32[2,3,96]{2,0,1:T(2,128)}, u32[]{:S(2)}) copy-start(s32[2,3,96]{2,0,1:T(2,128)} %param.13) | copy-start | bytes 6916
  2.7 7.2 %collective-permute-start.1 = (bf16[16,2048]{1,0:T(8,128)(2,1)S(1)}, bf16[16,2048]{1,0:T(8,128)(2,1)S(1)}, u32[]{:S(2)}, u32[]{:S(2)}) collective-permute-start(bf16[16,2048]{1,0:T(8,128)(2,1)S(1)} %get-tuple-element.29), channel_id=1, source_target_pairs={{0,16},{4,20},{8,24},{12,28},{16,0},{20,4},{24,8},{28,12},{1,17},{... | collective-permute-start | bytes 196616 | tf_op jit(solution)/shard_map/ppermute | solution.py:177
  4.8 5.0 %collective-permute-start.2 = (bf16[16,2048]{1,0:T(8,128)(2,1)S(1)}, bf16[16,2048]{1,0:T(8,128)(2,1)S(1)}, u32[]{:S(2)}, u32[]{:S(2)}) collective-permute-start(bf16[16,2048]{1,0:T(8,128)(2,1)S(1)} %get-tuple-element.29), channel_id=1, source_target_pairs={{0,24},{4,28},{8,16},{12,20},{16,8},{20,12},{24,0},{28,4},{1,25},{... | collective-permute-start | bytes 196616 | tf_op jit(solution)/shard_map/ppermute | solution.py:177
  6.0 3.9 %collective-permute-start = (bf16[16,2048]{1,0:T(8,128)(2,1)S(1)}, bf16[16,2048]{1,0:T(8,128)(2,1)S(1)}, u32[]{:S(2)}, u32[]{:S(2)}) collective-permute-start(bf16[16,2048]{1,0:T(8,128)(2,1)S(1)} %get-tuple-element.38), channel_id=1, source_target_pairs={{0,8},{4,12},{8,0},{12,4},{16,24},{20,28},{24,16},{28,20},{1,9},{5... | collective-permute-start | bytes 196616 | tf_op jit(solution)/shard_map/ppermute | solution.py:177
  6.2 8.4 %copy-start.6 = (bf16[3,32,2048]{2,1,0:T(8,128)(2,1)}, bf16[3,32,2048]{2,1,0:T(8,128)(2,1)S(1)}, u32[]{:S(2)}) copy-start(bf16[3,32,2048]{2,1,0:T(8,128)(2,1)S(1)} %get-tuple-element.51) | copy-start | bytes 1179652
  9.9 3.7 %collective-permute-start.3 = (bf16[64,2048]{1,0:T(8,128)(2,1)S(1)}, bf16[64,2048]{1,0:T(8,128)(2,1)S(1)}, u32[]{:S(2)}, u32[]{:S(2)}) collective-permute-start(bf16[64,2048]{1,0:T(8,128)(2,1)S(1)} %constant_dynamic-update-slice_fusion.mine_ref), channel_id=1, source_target_pairs={{0,4},{4,0},{8,12},{12,8},{16,20},{20,16},{24,28},{28,24},{1,5},{5... | collective-permute-start | bytes 786440 | tf_op jit(solution)/shard_map/ppermute | solution.py:177
  11.6 3.0 %collective-permute-start.5 = (bf16[3,32,2048]{2,1,0:T(8,128)(2,1)S(1)}, bf16[3,32,2048]{2,1,0:T(8,128)(2,1)S(1)}, u32[]{:S(2)}, u32[]{:S(2)}) collective-permute-start(bf16[3,32,2048]{2,1,0:T(8,128)(2,1)S(1)} %get-tuple-element.44), channel_id=1, source_target_pairs={{12,0},{28,16},{13,1},{29,17},{14,2},{30,18},{15,3},{31,19}} | collective-permute-start | bytes 1179656 | tf_op jit(solution)/shard_map/ppermute | solution.py:181
  12.3 12.0 %collective-permute-start.6 = (bf16[3,32,2048]{2,1,0:T(8,128)(2,1)S(1)}, bf16[3,32,2048]{2,1,0:T(8,128)(2,1)S(1)}, u32[]{:S(2)}, u32[]{:S(2)}) collective-permute-start(bf16[3,32,2048]{2,1,0:T(8,128)(2,1)S(1)} %get-tuple-element.45), channel_id=1, source_target_pairs={{12,4},{28,20},{13,5},{29,21},{14,6},{30,22},{15,7},{31,23}} | collective-permute-start | bytes 1179656 | tf_op jit(solution)/shard_map/ppermute | solution.py:181
  14.6 13.9 %copy-start.1 = (s32[128,8]{0,1:T(8,128)S(1)}, s32[128,8]{0,1:T(8,128)}, u32[]{:S(2)}) copy-start(s32[128,8]{0,1:T(8,128)} %param.8) | copy-start | bytes 12292
  14.6 14.0 %copy-start.8 = (f32[128,8]{0,1:T(8,128)S(1)}, f32[128,8]{0,1:T(8,128)}, u32[]{:S(2)}) copy-start(f32[128,8]{0,1:T(8,128)} %param.9) | copy-start | bytes 12292
  14.6 9.8 %collective-permute-start.4 = (bf16[64,2048]{1,0:T(8,128)(2,1)S(1)}, bf16[64,2048]{1,0:T(8,128)(2,1)S(1)}, u32[]{:S(2)}, u32[]{:S(2)}) collective-permute-start(bf16[64,2048]{1,0:T(8,128)(2,1)S(1)} %get-tuple-element.43), channel_id=1, source_target_pairs={{0,4},{4,0},{8,12},{12,8},{16,20},{20,16},{24,28},{28,24},{1,5},{5... | collective-permute-start | bytes 786440 | tf_op jit(solution)/shard_map/ppermute | solution.py:177
  25.1 4.3 %collective-permute-start.7 = (bf16[16,2048]{1,0:T(8,128)(2,1)}, bf16[16,2048]{1,0:T(8,128)(2,1)S(1)}, u32[]{:S(2)}, u32[]{:S(2)}) collective-permute-start(bf16[16,2048]{1,0:T(8,128)(2,1)} %get-tuple-element.56), channel_id=1, source_target_pairs={{0,8},{4,12},{8,0},{12,4},{16,24},{20,28},{24,16},{28,20},{1,9},{5... | collective-permute-start | bytes 196616 | tf_op jit(solution)/shard_map/ppermute | solution.py:177
  25.1 5.6 %collective-permute-start.8 = (bf16[16,2048]{1,0:T(8,128)(2,1)}, bf16[16,2048]{1,0:T(8,128)(2,1)S(1)}, u32[]{:S(2)}, u32[]{:S(2)}) collective-permute-start(bf16[16,2048]{1,0:T(8,128)(2,1)} %get-tuple-element.55), channel_id=1, source_target_pairs={{0,16},{4,20},{8,24},{12,28},{16,0},{20,4},{24,8},{28,12},{1,17},{... | collective-permute-start | bytes 196616 | tf_op jit(solution)/shard_map/ppermute | solution.py:177
  26.4 7.6 %collective-permute-start.9 = (bf16[16,2048]{1,0:T(8,128)(2,1)}, bf16[16,2048]{1,0:T(8,128)(2,1)S(1)}, u32[]{:S(2)}, u32[]{:S(2)}) collective-permute-start(bf16[16,2048]{1,0:T(8,128)(2,1)} %get-tuple-element.54), channel_id=1, source_target_pairs={{0,24},{4,28},{8,16},{12,20},{16,8},{20,12},{24,0},{28,4},{1,25},{... | collective-permute-start | bytes 196616 | tf_op jit(solution)/shard_map/ppermute | solution.py:177
  27.8 13.5 %collective-permute-start.13 = (bf16[3,96,2048]{2,1,0:T(8,128)(2,1)S(1)}, bf16[3,96,2048]{2,1,0:T(8,128)(2,1)S(1)}, u32[]{:S(2)}, u32[]{:S(2)}) collective-permute-start(bf16[3,96,2048]{2,1,0:T(8,128)(2,1)S(1)} %get-tuple-element.53), channel_id=1, source_target_pairs={{12,8},{28,24},{13,9},{29,25},{14,10},{30,26},{15,11},{31,27}} | collective-permute-start | bytes 3538952 | tf_op jit(solution)/shard_map/ppermute | solution.py:181
  28.7 7.0 %collective-permute-start.11 = (bf16[3,32,2048]{2,1,0:T(8,128)(2,1)}, bf16[3,32,2048]{2,1,0:T(8,128)(2,1)S(1)}, u32[]{:S(2)}, u32[]{:S(2)}) collective-permute-start(bf16[3,32,2048]{2,1,0:T(8,128)(2,1)} %copy-done.6), channel_id=1, source_target_pairs={{12,0},{28,16},{13,1},{29,17},{14,2},{30,18},{15,3},{31,19}} | collective-permute-start | bytes 1179656 | tf_op jit(solution)/shard_map/ppermute | solution.py:181
  29.4 10.9 %collective-permute-start.12 = (bf16[3,32,2048]{2,1,0:T(8,128)(2,1)S(1)}, bf16[3,32,2048]{2,1,0:T(8,128)(2,1)S(1)}, u32[]{:S(2)}, u32[]{:S(2)}) collective-permute-start(bf16[3,32,2048]{2,1,0:T(8,128)(2,1)S(1)} %get-tuple-element.52), channel_id=1, source_target_pairs={{12,4},{28,20},{13,5},{29,21},{14,6},{30,22},{15,7},{31,23}} | collective-permute-start | bytes 1179656 | tf_op jit(solution)/shard_map/ppermute | solution.py:181
  30.7 10.5 %collective-permute-start.10 = (bf16[3,32,2048]{2,1,0:T(8,128)(2,1)S(1)}, bf16[3,32,2048]{2,1,0:T(8,128)(2,1)S(1)}, u32[]{:S(2)}, u32[]{:S(2)}) collective-permute-start(bf16[3,32,2048]{2,1,0:T(8,128)(2,1)S(1)} %add.6.shared_ref), channel_id=1, source_target_pairs={{0,1},{4,5},{16,17},{20,21},{1,0},{5,4},{17,16},{21,20},{2,3},{6,7... | collective-permute-start | bytes 1179656 | tf_op jit(solution)/shard_map/ppermute | solution.py:189

commit v6 on v5

--- a/solution.py
+++ b/solution.py
@@ -80,42 +80,37 @@
                 start += count
 
 
-def merge_kernel(part, shared_ref, swapped_ref, first_ref, second_ref, near_ref, out_ref, sems):
+def merge_kernel(shared_ref, swapped_ref, straight_ref, near_ref, out_ref, sems):
     position = lax.axis_index("expert") % GROUP
     parity = lax.axis_index("replica") % 2
-    most = out_ref.shape[1]
+    half = shared_ref.shape[1]
 
     def move(pieces):
         copies = []
-        for ref, first, count in pieces:
+        for ref, first in pieces:
             for m in range(3):
+                rows = pl.ds(first, ref.shape[1])
                 copies.append(
-                    pltpu.make_async_copy(
-                        ref.at[m], out_ref.at[m, pl.ds(first, count)], sems.at[len(copies)]
-                    )
+                    pltpu.make_async_copy(ref.at[m], out_ref.at[m, rows], sems.at[len(copies)])
                 )
         for copy in copies:
             copy.start()
         for copy in copies:
             copy.wait()
 
-    for p, ref in ((0, first_ref), (1, second_ref)):
-        for even in range(2):
-            mine = position == 1 if p == 1 else jnp.logical_or(position == 0, position == 3)
-
-            @pl.when(jnp.logical_and(mine, parity == even))
-            def _():
-                move(
-                    [
-                        (shared_ref, part * even, part),
-                        (swapped_ref, part * (1 - even), part),
-                        (ref, 2 * part, most - 2 * part),
-                    ]
-                )
+    for even in range(2):
+
+        @pl.when(jnp.logical_and(position == 0, parity == even))
+        def _():
+            move([(shared_ref, half * even), (swapped_ref, half * (1 - even))])
+
+    @pl.when(jnp.logical_or(position == 1, position == 3))
+    def _():
+        move([(straight_ref, 0)])
 
     @pl.when(position == 2)
     def _():
-        move([(near_ref, 0, most)])
+        move([(near_ref, 0)])
 
 
 def expert_kernel(mine_ref, other_ref, gate_ref, up_ref, down_ref, keep_ref, send_ref):
@@ -163,8 +158,7 @@
     width = tokens.shape[1]
     plan = jnp.transpose(move_plan, (1, 0, 2))
     weights = (old_gate, old_up, old_down)
-    part = most // 3
-    rest = most - 2 * part
+    half = most // 2
 
     def shape(*dims, dtype=BF16):
         return jax.ShapeDtypeStruct(dims, dtype)
@@ -184,7 +178,7 @@
         route = []
         for r in range(replicas):
             for i in range(devices):
-                if i % GROUP < 2:
+                if i % GROUP == 0:
                     route.append((i * replicas + r, i * replicas + (r ^ 1)))
         return lax.ppermute(block, ("expert", "replica"), route)
 
@@ -212,17 +206,13 @@
     pairs = [(j, k) for j in range(experts) for k in (0, 2)]
     mine = [parcels[0]] + [send(parcels[j], j, k) for j, k in pairs[1:]]
     held, parcels = lax.optimization_barrier((weights, parcels))
-    chosen = select(
-        [(0, None, part), (1, None, part)]
-        + [(0, 2 * part, rest), (1, 2 * part, rest), (2, 0, most)],
-        held,
-    )
+    chosen = select([(0, None, half), (1, 0, most), (2, 0, most)], held)
     mine, chosen = lax.optimization_barrier((mine, chosen))
     mine = jnp.concatenate(mine, axis=0)
     other = send(mine, 0, 1)
 
-    shared = [migrate(chosen[p], p) for p in range(2)]
-
+    shared = migrate(chosen[0], 0)
+    straight = migrate(chosen[1], 1)
     total = mine.shape[0]
     step = min(total, 64)
     row_spec = pl.BlockSpec((step, width), lambda i: (i, 0))
@@ -234,10 +224,9 @@
         in_specs=[row_spec] * 2 + [whole_spec] * 3,
         out_specs=[row_spec] * 2,
         compiler_params=params(),
-        cost_estimate=cost(4),
+        cost_estimate=cost(0),
         name="expert",
     )(mine, other, *weights)
-    shared = shared[0] + shared[1]
     taken, shared = lax.optimization_barrier((send(give, 0, 1), shared))
     summed = (keep + taken.astype(F32)).astype(BF16)
     pieces = [summed[n * SLOTS : (n + 1) * SLOTS] for n in range(len(pairs))]
@@ -245,9 +234,10 @@
         send(block, -j, k) for (j, k), block in zip(pairs[1:], pieces[1:])
     ]
 
+    near, _ = lax.optimization_barrier((chosen[2], back[len(pairs) // 2]))
+    near = migrate(near, 2)
     swapped = swap(shared)
-    last, _ = lax.optimization_barrier((chosen[2:], summed))
-    straight = [migrate(last[p], p) for p in range(GROUP - 1)]
+    straight, back = lax.optimization_barrier((straight, back))
 
     mixed = pl.pallas_call(
         functools.partial(combine_kernel, experts),
@@ -260,14 +250,14 @@
     )(expert_ids, combine, *back)
 
     arrived = pl.pallas_call(
-        functools.partial(merge_kernel, part),
+        merge_kernel,
         out_shape=shape(3, most, width),
-        in_specs=[HBM] * 5,
+        in_specs=[HBM] * 4,
         out_specs=HBM,
-        scratch_shapes=[pltpu.SemaphoreType.DMA((9,))],
+        scratch_shapes=[pltpu.SemaphoreType.DMA((6,))],
         compiler_params=params(),
         name="merge",
-    )(shared, swapped, *straight)
+    )(shared, swapped, straight, near)
     return mixed, arrived
 
 

time: 42.6 us -> 41.5 us (0.974)
  the two profiles are of different devices: /device:TPU:1 before, /device:TPU:0 now
where the time goes in v6:
time: 41.5 us; the launch traced here: 40.9 us
  waiting for transfers between devices  17.9 us (43%)
  starting transfers between devices  14.6 us (35%)
  Pallas kernels  5.48 us (13%)
  local copies, waits for them, and re-layouts  2 us (5%)
  between operations  0.8 us (2%)
    ppermute x8, starting transfers between devices, send(): return lax.ppermute(block, 'expert', route)  8.39 us
    ppermute x1, waiting for transfers between devices, swap(): return lax.ppermute(block, ('expert', 'replica'), route)  6.5 us
    ppermute x3, waiting for transfers between devices, migrate(): return lax.ppermute(block, 'expert', route)  5.72 us
    ppermute x8, waiting for transfers between devices, send(): return lax.ppermute(block, 'expert', route)  5.68 us
    ppermute x1, starting transfers between devices, swap(): return lax.ppermute(block, ('expert', 'replica'), route)  3.48 us
    ppermute x3, starting transfers between devices, migrate(): return lax.ppermute(block, 'expert', route)  2.74 us
    unnamed x21, local copies, waits for them, and re-layouts  1.97 us
    pallas_call x1, Pallas kernels, on_device(): pl.pallas_call(functools.partial(combine_kernel, experts), out_shape=shap...  1.75 us
  transfers between devices with their start and end apart: 12, of which 6 were waited for; matrix products, arithmetic and copies ran while one was open for 1% of the time, Pallas kernels for 10%

profile of v6, /device:TPU:0, one launch (start us, length us, event | category | flops | bytes accessed | tf_op | source)
XLA Modules:
  0.0 40.9 jit_solution(7087233441460326417)
XLA Ops:
  0.6 0.0 copy-start.3
  0.6 0.7 %copy-done.3 = s32[128,8]{0,1:T(8,128)S(1)} copy-done((s32[128,8]{0,1:T(8,128)S(1)}, s32[128,8]{0,1:T(8,128)}, u32[]{:S(2)}) %copy-start.3) | copy-done | bytes 4120
  1.3 1.0 %copy-done.5 = bf16[128,2048]{1,0:T(8,128)(2,1)S(1)} copy-done((bf16[128,2048]{1,0:T(8,128)(2,1)S(1)}, bf16[128,2048]{1,0:T(8,128)(2,1)}, u32[]{:S(2)}) %copy-start.5) | copy-done | bytes 524312
  2.4 0.3 dispatch.1
  2.7 3.0 %collective-permute-start.1 = (bf16[16,2048]{1,0:T(8,128)(2,1)S(1)}, bf16[16,2048]{1,0:T(8,128)(2,1)S(1)}, u32[]{:S(2)}, u32[]{:S(2)}) collective-permute-start(bf16[16,2048]{1,0:T(8,128)(2,1)S(1)} %get-tuple-element.28), channel_id=1, source_target_pairs={{0,16},{4,20},{8,24},{12,28},{16,0},{20,4},{24,8},{28,12},{1,17},{... | collective-permute-start | bytes 196616 | tf_op jit(solution)/shard_map/ppermute | solution.py:171
  5.7 1.4 %collective-permute-start.2 = (bf16[16,2048]{1,0:T(8,128)(2,1)S(1)}, bf16[16,2048]{1,0:T(8,128)(2,1)S(1)}, u32[]{:S(2)}, u32[]{:S(2)}) collective-permute-start(bf16[16,2048]{1,0:T(8,128)(2,1)S(1)} %get-tuple-element.28), channel_id=1, source_target_pairs={{0,24},{4,28},{8,16},{12,20},{16,8},{20,12},{24,0},{28,4},{1,25},{... | collective-permute-start | bytes 196616 | tf_op jit(solution)/shard_map/ppermute | solution.py:171
  7.2 0.1 collective-permute-start
  7.3 1.4 %select.1 = (bf16[3,48,2048]{2,1,0:T(8,128)(2,1)S(1)}, bf16[3,96,2048]{2,1,0:T(8,128)(2,1)}, bf16[3,96,2048]{2,1,0:T(8,128)(2,1)}) custom-call(s32[3,2,96]{2,1,0:T(2,128)S(1)} %bitcast.3, bf16[192,2048]{1,0:T(8,128)(2,1)S(1)} %copy-done, bf16[192,2048]{1,0:T(8,128)(2,1)S(1)} %copy-done.1, bf16[192,2048]{1,0:T(8,128)(2,1)S(1)} %copy-done.2), custom_call_target="tpu_custom_call" | custom-call | flops 2000000000 | bytes 10000 | tf_op jit(solution)/shard_map/select/pallas_call | solution.py:186
  8.7 2.7 %collective-permute-done = bf16[16,2048]{1,0:T(8,128)(2,1)S(1)} collective-permute-done((bf16[16,2048]{1,0:T(8,128)(2,1)S(1)}, bf16[16,2048]{1,0:T(8,128)(2,1)S(1)}, u32[]{:S(2)}, u32[]{:S(2)}) %collective-permute-start) | collective-permute-done | bytes 65568 | tf_op jit(solution)/shard_map/ppermute | solution.py:171
  11.4 0.0 collective-permute-done.2
  11.5 1.3 %collective-permute-start.6 = (bf16[3,48,2048]{2,1,0:T(8,128)(2,1)S(1)}, bf16[3,48,2048]{2,1,0:T(8,128)(2,1)S(1)}, u32[]{:S(2)}, u32[]{:S(2)}) collective-permute-start(bf16[3,48,2048]{2,1,0:T(8,128)(2,1)S(1)} %get-tuple-element.42), channel_id=1, source_target_pairs={{12,0},{28,16},{13,1},{29,17},{14,2},{30,18},{15,3},{31,19}} | collective-permute-start | bytes 1769480 | tf_op jit(solution)/shard_map/ppermute | solution.py:175
  12.8 0.1 collective-permute-start.4
  12.9 1.5 %collective-permute-done.4.other_ref = bf16[64,2048]{1,0:T(8,128)(2,1)S(1)} collective-permute-done((bf16[64,2048]{1,0:T(8,128)(2,1)S(1)}, bf16[64,2048]{1,0:T(8,128)(2,1)S(1)}, u32[]{:S(2)}, u32[]{:S(2)}) %collective-permute-start.4) | collective-permute-done | bytes 262176 | tf_op jit(solution)/shard_map/ppermute | solution.py:171
  14.4 0.9 %expert.1 = (f32[64,2048]{1,0:T(8,128)S(1)}, bf16[64,2048]{1,0:T(8,128)(2,1)S(1)}) custom-call(bf16[64,2048]{1,0:T(8,128)(2,1)S(1)} %constant_dynamic-update-slice_fusion.mine_ref, bf16[64,2048]{1,0:T(8,128)(2,1)S(1)} %collective-permute-done.4.other_ref, bf16[192,2048]{1,0:T(8,128)(2,1)S(1)} %copy-done, bf16[192,2048]{1,0:T(8,128)(2,1)S(1)} %copy-done.1, ...), custom_call_target="tpu_custom_call" | custom-call | bytes 10000 | tf_op jit(solution)/shard_map/expert/pallas_call | solution.py:220
  15.3 0.0 copy-start.4
  15.3 0.0 copy-start.7
  15.3 0.2 collective-permute-start.5
  15.5 0.7 %collective-permute-start.3 = (bf16[3,96,2048]{2,1,0:T(8,128)(2,1)}, bf16[3,96,2048]{2,1,0:T(8,128)(2,1)S(1)}, u32[]{:S(2)}, u32[]{:S(2)}) collective-permute-start(bf16[3,96,2048]{2,1,0:T(8,128)(2,1)} %get-tuple-element.35), channel_id=1, source_target_pairs={{12,4},{28,20},{13,5},{29,21},{14,6},{30,22},{15,7},{31,23}} | collective-permute-start | bytes 3538952 | tf_op jit(solution)/shard_map/ppermute | solution.py:175
  16.3 0.7 %collective-permute-done.5 = bf16[64,2048]{1,0:T(8,128)(2,1)S(1)} collective-permute-done((bf16[64,2048]{1,0:T(8,128)(2,1)S(1)}, bf16[64,2048]{1,0:T(8,128)(2,1)S(1)}, u32[]{:S(2)}, u32[]{:S(2)}) %collective-permute-start.5) | collective-permute-done | bytes 262176 | tf_op jit(solution)/shard_map/ppermute | solution.py:171
  17.0 5.7 %collective-permute-done.6.shared_ref = bf16[3,48,2048]{2,1,0:T(8,128)(2,1)S(1)} collective-permute-done((bf16[3,48,2048]{2,1,0:T(8,128)(2,1)S(1)}, bf16[3,48,2048]{2,1,0:T(8,128)(2,1)S(1)}, u32[]{:S(2)}, u32[]{:S(2)}) %collective-permute-start.6) | collective-permute-done | bytes 589856 | tf_op jit(solution)/shard_map/ppermute | solution.py:175
  22.7 0.1 add_convert_fusion
  22.8 1.6 %collective-permute-start.8 = (bf16[16,2048]{1,0:T(8,128)(2,1)S(1)}, bf16[16,2048]{1,0:T(8,128)(2,1)S(1)}, u32[]{:S(2)}, u32[]{:S(2)}) collective-permute-start(bf16[16,2048]{1,0:T(8,128)(2,1)S(1)} %get-tuple-element.53), channel_id=1, source_target_pairs={{0,16},{4,20},{8,24},{12,28},{16,0},{20,4},{24,8},{28,12},{1,17},{... | collective-permute-start | bytes 196616 | tf_op jit(solution)/shard_map/ppermute | solution.py:171
  24.3 0.0 collective-permute-start.7
  24.3 2.0 %collective-permute-start.9 = (bf16[16,2048]{1,0:T(8,128)(2,1)S(1)}, bf16[16,2048]{1,0:T(8,128)(2,1)S(1)}, u32[]{:S(2)}, u32[]{:S(2)}) collective-permute-start(bf16[16,2048]{1,0:T(8,128)(2,1)S(1)} %get-tuple-element.52), channel_id=1, source_target_pairs={{0,24},{4,28},{8,16},{12,20},{16,8},{20,12},{24,0},{28,4},{1,25},{... | collective-permute-start | bytes 196616 | tf_op jit(solution)/shard_map/ppermute | solution.py:171
  26.3 0.8 %collective-permute-done.8.refs_2_ = bf16[16,2048]{1,0:T(8,128)(2,1)S(1)} collective-permute-done((bf16[16,2048]{1,0:T(8,128)(2,1)S(1)}, bf16[16,2048]{1,0:T(8,128)(2,1)S(1)}, u32[]{:S(2)}, u32[]{:S(2)}) %collective-permute-start.8) | collective-permute-done | bytes 65568 | tf_op jit(solution)/shard_map/ppermute | solution.py:171
  27.1 0.7 %collective-permute-start.11 = (bf16[3,96,2048]{2,1,0:T(8,128)(2,1)}, bf16[3,96,2048]{2,1,0:T(8,128)(2,1)S(1)}, u32[]{:S(2)}, u32[]{:S(2)}) collective-permute-start(bf16[3,96,2048]{2,1,0:T(8,128)(2,1)} %get-tuple-element.51), channel_id=1, source_target_pairs={{12,8},{28,24},{13,9},{29,25},{14,10},{30,26},{15,11},{31,27}} | collective-permute-start | bytes 3538952 | tf_op jit(solution)/shard_map/ppermute | solution.py:175
  27.8 0.1 copy.9.ids_ref
  27.9 0.1 copy.10.weight_ref
  28.0 3.5 %collective-permute-start.10 = (bf16[3,48,2048]{2,1,0:T(8,128)(2,1)S(1)}, bf16[3,48,2048]{2,1,0:T(8,128)(2,1)S(1)}, u32[]{:S(2)}, u32[]{:S(2)}) collective-permute-start(bf16[3,48,2048]{2,1,0:T(8,128)(2,1)S(1)} %collective-permute-done.6.shared_ref), channel_id=1, source_target_pairs={{0,1},{16,17},{1,0},{17,16},{2,3},{18,19},{3,2},{19,18}} | collective-permute-start | bytes 1769480 | tf_op jit(solution)/shard_map/ppermute | solution.py:183
  31.6 1.7 %combine.1 = bf16[128,2048]{1,0:T(8,128)(2,1)} custom-call(s32[128,8]{1,0:T(8,128)S(1)} %copy.9.ids_ref, f32[128,8]{1,0:T(8,128)S(1)} %copy.10.weight_ref, bf16[16,2048]{1,0:T(8,128)(2,1)S(1)} %get-tuple-element.44.refs_0_, bf16[16,2048]{1,0:T(8,128)(2,1)S(1)} %collective-permute-done.7.refs_1_, bf16[16,2048]{1,0:T(8,128)(2,1)S(1)} %collective-permute-done.8.refs_2_, ...), custom_call_target="tpu_custom_call" | custom-call | flops 12000000000 | bytes 10000 | tf_op jit(solution)/shard_map/combine/pallas_call | solution.py:242
  33.3 6.5 %collective-permute-done.10.swapped_ref = bf16[3,48,2048]{2,1,0:T(8,128)(2,1)S(1)} collective-permute-done((bf16[3,48,2048]{2,1,0:T(8,128)(2,1)S(1)}, bf16[3,48,2048]{2,1,0:T(8,128)(2,1)S(1)}, u32[]{:S(2)}, u32[]{:S(2)}) %collective-permute-start.10) | collective-permute-done | bytes 589856 | tf_op jit(solution)/shard_map/ppermute | solution.py:183
  39.8 1.1 %merge.1 = bf16[3,96,2048]{2,1,0:T(8,128)(2,1)} custom-call(bf16[3,48,2048]{2,1,0:T(8,128)(2,1)S(1)} %collective-permute-done.6.shared_ref, bf16[3,48,2048]{2,1,0:T(8,128)(2,1)S(1)} %collective-permute-done.10.swapped_ref, bf16[3,96,2048]{2,1,0:T(8,128)(2,1)S(1)} %collective-permute-done.3.straight_ref, bf16[3,96,2048]{2,1,0:T(8,128)(2,1)S(1)} %collective-permute-done.11.near_ref), custom_call_target="tpu_custom_call" | custom-call | tf_op jit(solution)/shard_map/merge/pallas_call | solution.py:252
  (21 shorter events, 0.1 us)
Async XLA Ops:
  0.6 0.7 %copy-start.3 = (s32[128,8]{0,1:T(8,128)S(1)}, s32[128,8]{0,1:T(8,128)}, u32[]{:S(2)}) copy-start(s32[128,8]{0,1:T(8,128)} %param.8) | copy-start | bytes 12292
  1.3 1.0 %copy-start.5 = (bf16[128,2048]{1,0:T(8,128)(2,1)S(1)}, bf16[128,2048]{1,0:T(8,128)(2,1)}, u32[]{:S(2)}) copy-start(bf16[128,2048]{1,0:T(8,128)(2,1)} %tok_ref.1) | copy-start | bytes 1572868
  2.4 4.9 %copy-start = (bf16[192,2048]{1,0:T(8,128)(2,1)S(1)}, bf16[192,2048]{1,0:T(8,128)(2,1)}, u32[]{:S(2)}) copy-start(bf16[192,2048]{1,0:T(8,128)(2,1)} %gate_ref.2) | copy-start | bytes 2359300
  2.4 4.9 %copy-start.1 = (bf16[192,2048]{1,0:T(8,128)(2,1)S(1)}, bf16[192,2048]{1,0:T(8,128)(2,1)}, u32[]{:S(2)}) copy-start(bf16[192,2048]{1,0:T(8,128)(2,1)} %up_ref.2) | copy-start | bytes 2359300
  2.4 4.9 %copy-start.2 = (bf16[192,2048]{1,0:T(8,128)(2,1)S(1)}, bf16[192,2048]{1,0:T(8,128)(2,1)}, u32[]{:S(2)}) copy-start(bf16[192,2048]{1,0:T(8,128)(2,1)} %down_ref.2) | copy-start | bytes 2359300
  2.4 4.9 %copy-start.6 = (s32[2,3,96]{2,0,1:T(2,128)S(1)}, s32[2,3,96]{2,0,1:T(2,128)}, u32[]{:S(2)}) copy-start(s32[2,3,96]{2,0,1:T(2,128)} %param.13) | copy-start | bytes 6916
  2.7 8.7 %collective-permute-start.1 = (bf16[16,2048]{1,0:T(8,128)(2,1)S(1)}, bf16[16,2048]{1,0:T(8,128)(2,1)S(1)}, u32[]{:S(2)}, u32[]{:S(2)}) collective-permute-start(bf16[16,2048]{1,0:T(8,128)(2,1)S(1)} %get-tuple-element.28), channel_id=1, source_target_pairs={{0,16},{4,20},{8,24},{12,28},{16,0},{20,4},{24,8},{28,12},{1,17},{... | collective-permute-start | bytes 196616 | tf_op jit(solution)/shard_map/ppermute | solution.py:171
  5.7 5.7 %collective-permute-start.2 = (bf16[16,2048]{1,0:T(8,128)(2,1)S(1)}, bf16[16,2048]{1,0:T(8,128)(2,1)S(1)}, u32[]{:S(2)}, u32[]{:S(2)}) collective-permute-start(bf16[16,2048]{1,0:T(8,128)(2,1)S(1)} %get-tuple-element.28), channel_id=1, source_target_pairs={{0,24},{4,28},{8,16},{12,20},{16,8},{20,12},{24,0},{28,4},{1,25},{... | collective-permute-start | bytes 196616 | tf_op jit(solution)/shard_map/ppermute | solution.py:171
  7.2 4.3 %collective-permute-start = (bf16[16,2048]{1,0:T(8,128)(2,1)S(1)}, bf16[16,2048]{1,0:T(8,128)(2,1)S(1)}, u32[]{:S(2)}, u32[]{:S(2)}) collective-permute-start(bf16[16,2048]{1,0:T(8,128)(2,1)S(1)} %get-tuple-element.36), channel_id=1, source_target_pairs={{0,8},{4,12},{8,0},{12,4},{16,24},{20,28},{24,16},{28,20},{1,9},{5... | collective-permute-start | bytes 196616 | tf_op jit(solution)/shard_map/ppermute | solution.py:171
  11.5 11.2 %collective-permute-start.6 = (bf16[3,48,2048]{2,1,0:T(8,128)(2,1)S(1)}, bf16[3,48,2048]{2,1,0:T(8,128)(2,1)S(1)}, u32[]{:S(2)}, u32[]{:S(2)}) collective-permute-start(bf16[3,48,2048]{2,1,0:T(8,128)(2,1)S(1)} %get-tuple-element.42), channel_id=1, source_target_pairs={{12,0},{28,16},{13,1},{29,17},{14,2},{30,18},{15,3},{31,19}} | collective-permute-start | bytes 1769480 | tf_op jit(solution)/shard_map/ppermute | solution.py:175
  12.8 1.6 %collective-permute-start.4 = (bf16[64,2048]{1,0:T(8,128)(2,1)S(1)}, bf16[64,2048]{1,0:T(8,128)(2,1)S(1)}, u32[]{:S(2)}, u32[]{:S(2)}) collective-permute-start(bf16[64,2048]{1,0:T(8,128)(2,1)S(1)} %constant_dynamic-update-slice_fusion.mine_ref), channel_id=1, source_target_pairs={{0,4},{4,0},{8,12},{12,8},{16,20},{20,16},{24,28},{28,24},{1,5},{5... | collective-permute-start | bytes 786440 | tf_op jit(solution)/shard_map/ppermute | solution.py:171
  15.3 12.5 %copy-start.4 = (s32[128,8]{0,1:T(8,128)S(1)}, s32[128,8]{0,1:T(8,128)}, u32[]{:S(2)}) copy-start(s32[128,8]{0,1:T(8,128)} %param.8) | copy-start | bytes 12292
  15.3 12.6 %copy-start.7 = (f32[128,8]{0,1:T(8,128)S(1)}, f32[128,8]{0,1:T(8,128)}, u32[]{:S(2)}) copy-start(f32[128,8]{0,1:T(8,128)} %param.9) | copy-start | bytes 12292
  15.3 1.6 %collective-permute-start.5 = (bf16[64,2048]{1,0:T(8,128)(2,1)S(1)}, bf16[64,2048]{1,0:T(8,128)(2,1)S(1)}, u32[]{:S(2)}, u32[]{:S(2)}) collective-permute-start(bf16[64,2048]{1,0:T(8,128)(2,1)S(1)} %get-tuple-element.41), channel_id=1, source_target_pairs={{0,4},{4,0},{8,12},{12,8},{16,20},{20,16},{24,28},{28,24},{1,5},{5... | collective-permute-start | bytes 786440 | tf_op jit(solution)/shard_map/ppermute | solution.py:171
  15.5 16.0 %collective-permute-start.3 = (bf16[3,96,2048]{2,1,0:T(8,128)(2,1)}, bf16[3,96,2048]{2,1,0:T(8,128)(2,1)S(1)}, u32[]{:S(2)}, u32[]{:S(2)}) collective-permute-start(bf16[3,96,2048]{2,1,0:T(8,128)(2,1)} %get-tuple-element.35), channel_id=1, source_target_pairs={{12,4},{28,20},{13,5},{29,21},{14,6},{30,22},{15,7},{31,23}} | collective-permute-start | bytes 3538952 | tf_op jit(solution)/shard_map/ppermute | solution.py:175
  22.8 4.3 %collective-permute-start.8 = (bf16[16,2048]{1,0:T(8,128)(2,1)S(1)}, bf16[16,2048]{1,0:T(8,128)(2,1)S(1)}, u32[]{:S(2)}, u32[]{:S(2)}) collective-permute-start(bf16[16,2048]{1,0:T(8,128)(2,1)S(1)} %get-tuple-element.53), channel_id=1, source_target_pairs={{0,16},{4,20},{8,24},{12,28},{16,0},{20,4},{24,8},{28,12},{1,17},{... | collective-permute-start | bytes 196616 | tf_op jit(solution)/shard_map/ppermute | solution.py:171
  24.3 7.2 %collective-permute-start.7 = (bf16[16,2048]{1,0:T(8,128)(2,1)S(1)}, bf16[16,2048]{1,0:T(8,128)(2,1)S(1)}, u32[]{:S(2)}, u32[]{:S(2)}) collective-permute-start(bf16[16,2048]{1,0:T(8,128)(2,1)S(1)} %get-tuple-element.54), channel_id=1, source_target_pairs={{0,8},{4,12},{8,0},{12,4},{16,24},{20,28},{24,16},{28,20},{1,9},{5... | collective-permute-start | bytes 196616 | tf_op jit(solution)/shard_map/ppermute | solution.py:171
  24.3 7.2 %collective-permute-start.9 = (bf16[16,2048]{1,0:T(8,128)(2,1)S(1)}, bf16[16,2048]{1,0:T(8,128)(2,1)S(1)}, u32[]{:S(2)}, u32[]{:S(2)}) collective-permute-start(bf16[16,2048]{1,0:T(8,128)(2,1)S(1)} %get-tuple-element.52), channel_id=1, source_target_pairs={{0,24},{4,28},{8,16},{12,20},{16,8},{20,12},{24,0},{28,4},{1,25},{... | collective-permute-start | bytes 196616 | tf_op jit(solution)/shard_map/ppermute | solution.py:171
  27.1 12.7 %collective-permute-start.11 = (bf16[3,96,2048]{2,1,0:T(8,128)(2,1)}, bf16[3,96,2048]{2,1,0:T(8,128)(2,1)S(1)}, u32[]{:S(2)}, u32[]{:S(2)}) collective-permute-start(bf16[3,96,2048]{2,1,0:T(8,128)(2,1)} %get-tuple-element.51), channel_id=1, source_target_pairs={{12,8},{28,24},{13,9},{29,25},{14,10},{30,26},{15,11},{31,27}} | collective-permute-start | bytes 3538952 | tf_op jit(solution)/shard_map/ppermute | solution.py:175
  28.0 11.8 %collective-permute-start.10 = (bf16[3,48,2048]{2,1,0:T(8,128)(2,1)S(1)}, bf16[3,48,2048]{2,1,0:T(8,128)(2,1)S(1)}, u32[]{:S(2)}, u32[]{:S(2)}) collective-permute-start(bf16[3,48,2048]{2,1,0:T(8,128)(2,1)S(1)} %collective-permute-done.6.shared_ref), channel_id=1, source_target_pairs={{0,1},{16,17},{1,0},{17,16},{2,3},{18,19},{3,2},{19,18}} | collective-permute-start | bytes 1769480 | tf_op jit(solution)/shard_map/ppermute | solution.py:183

commit v7 on v6

--- a/solution.py
+++ b/solution.py
@@ -8,7 +8,7 @@
 from jax.sharding import PartitionSpec as P
 
 CAP = 12
-SLOTS = 16
+PACK = 2 * CAP
 GROUP = 4
 BF16 = jnp.bfloat16
 F32 = jnp.float32
@@ -26,30 +26,32 @@
     )
 
 
-def slot_matrix(ids, group, experts):
+def token_places(ids, group, experts):
     tok = ids.shape[1]
     member = []
     for j in range(experts):
-        expert = lax.rem(group + j, experts)
-        named = jnp.where(ids == expert, 1.0, 0.0)
+        named = jnp.where(ids == lax.rem(group + j, experts), 1.0, 0.0)
         member.append(jnp.sum(named, axis=0, keepdims=True))
     member = jnp.concatenate(member, axis=0)
     row = lax.broadcasted_iota(jnp.int32, (tok, tok), 0)
     col = lax.broadcasted_iota(jnp.int32, (tok, tok), 1)
     upto = jnp.where(row <= col, 1.0, 0.0).astype(BF16)
     rank = jnp.dot(member.astype(BF16), upto, preferred_element_type=F32)
-    place = jnp.where(member > 0, rank - 1.0, -1.0).astype(jnp.int32)
-    slot = lax.broadcasted_iota(jnp.int32, (SLOTS, tok), 0)
-    blocks = [jnp.where(slot == place[j : j + 1, :], 1.0, 0.0) for j in range(experts)]
-    return jnp.concatenate(blocks, axis=0)
+    return jnp.where(member > 0, rank - 1.0, -PACK).astype(jnp.int32)
 
 
 def dispatch_kernel(experts, ids_ref, tok_ref, *out_refs):
     group = lax.axis_index("expert") // GROUP
-    chosen = slot_matrix(ids_ref[...], group, experts).astype(BF16)
-    rows = jnp.dot(chosen, tok_ref[...], preferred_element_type=F32).astype(BF16)
+    place = token_places(ids_ref[...], group, experts)
+    tok, half = tok_ref.shape[0], tok_ref.shape[1] // 2
+    slot = lax.broadcasted_iota(jnp.int32, (PACK, tok), 0)
     for j, ref in enumerate(out_refs):
-        ref[...] = rows[j * SLOTS : (j + 1) * SLOTS]
+        spot = place[j : j + 1, :]
+        left = jnp.where(jnp.logical_and(slot == spot, spot >= 0), 1.0, 0.0).astype(BF16)
+        right = jnp.where(slot == spot + CAP, 1.0, 0.0).astype(BF16)
+        rows = jnp.dot(left, tok_ref[:, :half], preferred_element_type=F32)
+        rows = rows + jnp.dot(right, tok_ref[:, half:], preferred_element_type=F32)
+        ref[...] = rows.astype(BF16)
 
 
 def select_kernel(wanted, plan_ref, gate_ref, up_ref, down_ref, *out_refs):
@@ -80,7 +82,7 @@
                 start += count
 
 
-def merge_kernel(shared_ref, swapped_ref, straight_ref, near_ref, out_ref, sems):
+def merge_kernel(shared_ref, swapped_ref, first_ref, second_ref, near_ref, out_ref, sems):
     position = lax.axis_index("expert") % GROUP
     parity = lax.axis_index("replica") % 2
     half = shared_ref.shape[1]
@@ -106,23 +108,34 @@
 
     @pl.when(jnp.logical_or(position == 1, position == 3))
     def _():
-        move([(straight_ref, 0)])
+        move([(first_ref, 0), (second_ref, first_ref.shape[1])])
 
     @pl.when(position == 2)
     def _():
         move([(near_ref, 0)])
 
 
-def expert_kernel(mine_ref, other_ref, gate_ref, up_ref, down_ref, keep_ref, send_ref):
-    rows = mine_ref.shape[0]
+def expert_kernel(mine_ref, other_ref, gate_ref, up_ref, down_ref, keep_ref, give_ref):
+    rows, half = mine_ref.shape
     x = jnp.concatenate([mine_ref[...], other_ref[...]], axis=0)
+    total = x.shape[0]
     numbers = (((1,), (1,)), ((), ()))
-    gate_value = lax.dot_general(x, gate_ref[...], numbers, preferred_element_type=F32)
-    up_value = lax.dot_general(x, up_ref[...], numbers, preferred_element_type=F32)
+
+    def project(ref):
+        left = lax.dot_general(x, ref[:, :half], numbers, preferred_element_type=F32)
+        right = lax.dot_general(x, ref[:, half:], numbers, preferred_element_type=F32)
+        return left + jnp.concatenate([right[CAP:], right[:CAP]], axis=0)
+
+    gate_value = project(gate_ref)
+    up_value = project(up_ref)
     hidden = (gate_value / (1.0 + jnp.exp(-gate_value)) * up_value).astype(BF16)
-    partial = jnp.dot(hidden, down_ref[...], preferred_element_type=F32)
+    left = jnp.dot(hidden, down_ref[:, :half], preferred_element_type=F32)
+    right = jnp.dot(hidden, down_ref[:, half:], preferred_element_type=F32)
+    right = jnp.concatenate([right[total - CAP :], right[: total - CAP]], axis=0)
+    row = lax.broadcasted_iota(jnp.int32, (total, half), 0)
+    partial = jnp.where(row % PACK < CAP, left, right)
     keep_ref[...] = partial[:rows]
-    send_ref[...] = partial[rows:].astype(BF16)
+    give_ref[...] = partial[rows:].astype(BF16)
 
 
 def combine_kernel(experts, ids_ref, weight_ref, *refs):
@@ -130,24 +143,25 @@
     ids = ids_ref[...]
     group = lax.axis_index("expert") // GROUP
     tok = ids.shape[0]
-    each = len(piece_refs) // experts
+    half = out_ref.shape[1] // 2
     row = lax.broadcasted_iota(jnp.int32, (tok, tok), 0)
     col = lax.broadcasted_iota(jnp.int32, (tok, tok), 1)
     upto = jnp.where(col <= row, 1.0, 0.0).astype(BF16)
-    slot = lax.broadcasted_iota(jnp.int32, (tok, each * SLOTS), 1) % SLOTS
-    mixed = None
+    slot = lax.broadcasted_iota(jnp.int32, (tok, PACK), 1)
+    mixed = [None, None]
     for j in range(experts):
         named = ids == lax.rem(group + j, experts)
         member = jnp.sum(jnp.where(named, 1.0, 0.0), axis=1, keepdims=True)
         weight = jnp.sum(jnp.where(named, weight_ref[...], 0.0), axis=1, keepdims=True)
         rank = jnp.dot(upto, member.astype(BF16), preferred_element_type=F32)
-        place = jnp.where(member > 0, rank - 1.0, -1.0).astype(jnp.int32)
-        chosen = jnp.where(slot == place, 1.0, 0.0).astype(BF16)
-        rows = [ref[...] for ref in piece_refs[j * each : (j + 1) * each]]
-        found = jnp.dot(chosen, jnp.concatenate(rows, axis=0), preferred_element_type=F32)
-        term = weight * found
-        mixed = term if mixed is None else mixed + term
-    out_ref[...] = mixed.astype(BF16)
+        place = jnp.where(member > 0, rank - 1.0, -PACK).astype(jnp.int32)
+        for side in range(2):
+            chosen = jnp.where(slot == place + side * CAP, 1.0, 0.0).astype(BF16)
+            found = jnp.dot(chosen, piece_refs[j][...], preferred_element_type=F32)
+            term = weight * found
+            mixed[side] = term if mixed[side] is None else mixed[side] + term
+    out_ref[:, :half] = mixed[0].astype(BF16)
+    out_ref[:, half:] = mixed[1].astype(BF16)
 
 
 def on_device(tokens, expert_ids, combine, old_gate, old_up, old_down, move_plan):
@@ -195,7 +209,7 @@
 
     parcels = pl.pallas_call(
         functools.partial(dispatch_kernel, experts),
-        out_shape=[shape(SLOTS, width)] * experts,
+        out_shape=[shape(PACK, width // 2)] * experts,
         in_specs=[VMEM, VMEM],
         out_specs=[VMEM] * experts,
         compiler_params=params(),
@@ -203,24 +217,26 @@
         name="dispatch",
     )(expert_ids.T, tokens)
 
-    pairs = [(j, k) for j in range(experts) for k in (0, 2)]
-    mine = [parcels[0]] + [send(parcels[j], j, k) for j, k in pairs[1:]]
-    held, parcels = lax.optimization_barrier((weights, parcels))
-    chosen = select([(0, None, half), (1, 0, most), (2, 0, most)], held)
-    mine, chosen = lax.optimization_barrier((mine, chosen))
-    mine = jnp.concatenate(mine, axis=0)
+    held, across = lax.optimization_barrier((weights, parcels[1]))
+    parcels = [parcels[0], across] + list(parcels[2:])
+    across = [send(parcels[j], j, 0) for j in range(1, experts)]
+    here = jnp.concatenate([parcels[0]] + across, axis=0)
+    chosen = select([(0, None, half), (1, 0, half), (1, half, most - half), (2, 0, most)], held)
+    here, chosen = lax.optimization_barrier((here, chosen))
+    mine = jnp.concatenate([here, send(here, 0, 2)], axis=0)
     other = send(mine, 0, 1)
 
     shared = migrate(chosen[0], 0)
-    straight = migrate(chosen[1], 1)
+    first = migrate(chosen[1], 1)
+
     total = mine.shape[0]
-    step = min(total, 64)
-    row_spec = pl.BlockSpec((step, width), lambda i: (i, 0))
+    step = min(total, 4 * PACK)
+    row_spec = pl.BlockSpec((step, width // 2), lambda i: (i, 0))
     whole_spec = pl.BlockSpec(old_gate.shape, lambda i: (0, 0))
     keep, give = pl.pallas_call(
         expert_kernel,
         grid=(total // step,),
-        out_shape=[shape(total, width, dtype=F32), shape(total, width)],
+        out_shape=[shape(total, width // 2, dtype=F32), shape(total, width // 2)],
         in_specs=[row_spec] * 2 + [whole_spec] * 3,
         out_specs=[row_spec] * 2,
         compiler_params=params(),
@@ -228,16 +244,18 @@
         name="expert",
     )(mine, other, *weights)
     taken, shared = lax.optimization_barrier((send(give, 0, 1), shared))
-    summed = (keep + taken.astype(F32)).astype(BF16)
-    pieces = [summed[n * SLOTS : (n + 1) * SLOTS] for n in range(len(pairs))]
-    back = [pieces[0]] + [
-        send(block, -j, k) for (j, k), block in zip(pairs[1:], pieces[1:])
-    ]
-
-    near, _ = lax.optimization_barrier((chosen[2], back[len(pairs) // 2]))
-    near = migrate(near, 2)
+    summed = keep + taken.astype(F32)
+    far = send(summed[total // 2 :].astype(BF16), 0, 2)
+
+    far, first = lax.optimization_barrier((far, first))
     swapped = swap(shared)
-    straight, back = lax.optimization_barrier((straight, back))
+    second = migrate(lax.optimization_barrier((chosen[2], summed))[0], 1)
+
+    summed = (summed[: total // 2] + far.astype(F32)).astype(BF16)
+    pieces = [summed[j * PACK : (j + 1) * PACK] for j in range(experts)]
+    back = [pieces[0]] + [send(pieces[j], -j, 0) for j in range(1, experts)]
+    near = migrate(lax.optimization_barrier((chosen[3], back))[0], 2)
+    back, swapped, second = lax.optimization_barrier((back, swapped, second))
 
     mixed = pl.pallas_call(
         functools.partial(combine_kernel, experts),
@@ -252,12 +270,12 @@
     arrived = pl.pallas_call(
         merge_kernel,
         out_shape=shape(3, most, width),
-        in_specs=[HBM] * 4,
+        in_specs=[HBM] * 5,
         out_specs=HBM,
         scratch_shapes=[pltpu.SemaphoreType.DMA((6,))],
         compiler_params=params(),
         name="merge",
-    )(shared, swapped, straight, near)
+    )(shared, swapped, first, second, near)
     return mixed, arrived
 
 

time: 41.5 us -> 42.5 us (1.024)
  the two profiles are of different devices: /device:TPU:0 before, /device:TPU:1 now
where the time goes in v7:
time: 42.5 us; the launch traced here: 42 us
  starting transfers between devices  16.2 us (38%)
  waiting for transfers between devices  11.9 us (28%)
  local copies, waits for them, and re-layouts  7.74 us (18%)
  Pallas kernels  5.38 us (13%)
  between operations  0.78 us (2%)
    ppermute x6, starting transfers between devices, send(): return lax.ppermute(block, 'expert', route)  11.5 us
    unnamed x29, local copies, waits for them, and re-layouts  7.1 us
    ppermute x4, waiting for transfers between devices, migrate(): return lax.ppermute(block, 'expert', route)  5.99 us
    ppermute x6, waiting for transfers between devices, send(): return lax.ppermute(block, 'expert', route)  5.89 us
    ppermute x4, starting transfers between devices, migrate(): return lax.ppermute(block, 'expert', route)  3.97 us
    pallas_call x1, Pallas kernels, on_device(): pl.pallas_call(functools.partial(combine_kernel, experts), out_shape=shap...  1.76 us
    pallas_call x1, Pallas kernels, select(): pl.pallas_call(functools.partial(select_kernel, wanted), out_shape=[shape...  1.23 us
    pallas_call x1, Pallas kernels, on_device(): pl.pallas_call(merge_kernel, out_shape=shape(3, most, width), in_specs=[H...  1.05 us
  transfers between devices with their start and end apart: 11, of which 6 were waited for; matrix products, arithmetic and copies ran while one was open for 5% of the time, Pallas kernels for 9%

profile of v7, /device:TPU:1, one launch (start us, length us, event | category | flops | bytes accessed | tf_op | source)
XLA Modules:
  0.0 42.0 jit_solution(15419998023673964195)
XLA Ops:
  0.6 0.7 %copy-done.6 = s32[128,8]{0,1:T(8,128)S(1)} copy-done((s32[128,8]{0,1:T(8,128)S(1)}, s32[128,8]{0,1:T(8,128)}, u32[]{:S(2)}) %copy-start.6) | copy-done | bytes 4120
  1.3 1.0 %copy-done.8 = bf16[128,2048]{1,0:T(8,128)(2,1)S(1)} copy-done((bf16[128,2048]{1,0:T(8,128)(2,1)S(1)}, bf16[128,2048]{1,0:T(8,128)(2,1)}, u32[]{:S(2)}) %copy-start.8) | copy-done | bytes 524312
  2.4 0.4 dispatch.1
  2.8 2.1 %collective-permute-start = (bf16[24,1024]{1,0:T(8,128)(2,1)S(1)}, bf16[24,1024]{1,0:T(8,128)(2,1)S(1)}, u32[]{:S(2)}, u32[]{:S(2)}) collective-permute-start(bf16[24,1024]{1,0:T(8,128)(2,1)S(1)} %get-tuple-element.31), channel_id=1, source_target_pairs={{0,16},{4,20},{8,24},{12,28},{16,0},{20,4},{24,8},{28,12},{1,17},{... | collective-permute-start | bytes 147464 | tf_op jit(solution)/shard_map/ppermute | solution.py:185
  4.9 1.2 %select.1 = (bf16[3,48,2048]{2,1,0:T(8,128)(2,1)S(1)}, bf16[3,48,2048]{2,1,0:T(8,128)(2,1)S(1)}, bf16[3,48,2048]{2,1,0:T(8,128)(2,1)}, bf16[3,96,2048]{2,1,0:T(8,128)(2,1)}) custom-call(s32[3,2,96]{2,1,0:T(2,128)S(1)} %bitcast.3, bf16[192,2048]{1,0:T(8,128)(2,1)S(1)} %copy-done, bf16[192,2048]{1,0:T(8,128)(2,1)S(1)} %copy-done.1, bf16[192,2048]{1,0:T(8,128)(2,1)S(1)} %copy-done.2), custom_call_target="tpu_custom_call" | custom-call | flops 2000000000 | bytes 10000 | tf_op jit(solution)/shard_map/select/pallas_call | solution.py:200
  6.2 0.2 collective-permute-done
  6.4 2.1 %collective-permute-start.1 = (bf16[48,1024]{1,0:T(8,128)(2,1)S(1)}, bf16[48,1024]{1,0:T(8,128)(2,1)S(1)}, u32[]{:S(2)}, u32[]{:S(2)}) collective-permute-start(bf16[48,1024]{1,0:T(8,128)(2,1)S(1)} %pad_maximum_fusion), channel_id=1, source_target_pairs={{0,8},{4,12},{8,0},{12,4},{16,24},{20,28},{24,16},{28,20},{1,9},{5... | collective-permute-start | bytes 294920 | tf_op jit(solution)/shard_map/ppermute | solution.py:185
  8.5 0.7 %collective-permute-start.4 = (bf16[3,48,2048]{2,1,0:T(8,128)(2,1)S(1)}, bf16[3,48,2048]{2,1,0:T(8,128)(2,1)S(1)}, u32[]{:S(2)}, u32[]{:S(2)}) collective-permute-start(bf16[3,48,2048]{2,1,0:T(8,128)(2,1)S(1)} %get-tuple-element.42), channel_id=1, source_target_pairs={{12,0},{28,16},{13,1},{29,17},{14,2},{30,18},{15,3},{31,19}} | collective-permute-start | bytes 1769480 | tf_op jit(solution)/shard_map/ppermute | solution.py:189
  9.2 1.3 %collective-permute-done.1 = bf16[48,1024]{1,0:T(8,128)(2,1)S(1)} collective-permute-done((bf16[48,1024]{1,0:T(8,128)(2,1)S(1)}, bf16[48,1024]{1,0:T(8,128)(2,1)S(1)}, u32[]{:S(2)}, u32[]{:S(2)}) %collective-permute-start.1) | collective-permute-done | bytes 98336 | tf_op jit(solution)/shard_map/ppermute | solution.py:185
  10.5 2.2 %collective-permute-start.2 = (bf16[96,1024]{1,0:T(8,128)(2,1)S(1)}, bf16[96,1024]{1,0:T(8,128)(2,1)S(1)}, u32[]{:S(2)}, u32[]{:S(2)}) collective-permute-start(bf16[96,1024]{1,0:T(8,128)(2,1)S(1)} %constant_dynamic-update-slice_fusion.mine_ref), channel_id=1, source_target_pairs={{0,4},{4,0},{8,12},{12,8},{16,20},{20,16},{24,28},{28,24},{1,5},{5... | collective-permute-start | bytes 589832 | tf_op jit(solution)/shard_map/ppermute | solution.py:185
  12.7 1.3 %collective-permute-start.6 = (bf16[3,48,2048]{2,1,0:T(8,128)(2,1)S(1)}, bf16[3,48,2048]{2,1,0:T(8,128)(2,1)S(1)}, u32[]{:S(2)}, u32[]{:S(2)}) collective-permute-start(bf16[3,48,2048]{2,1,0:T(8,128)(2,1)S(1)} %get-tuple-element.44), channel_id=1, source_target_pairs={{12,4},{28,20},{13,5},{29,21},{14,6},{30,22},{15,7},{31,23}} | collective-permute-start | bytes 1769480 | tf_op jit(solution)/shard_map/ppermute | solution.py:189
  14.0 0.9 %expert.1 = (f32[96,1024]{1,0:T(8,128)S(1)}, bf16[96,1024]{1,0:T(8,128)(2,1)S(1)}) custom-call(bf16[96,1024]{1,0:T(8,128)(2,1)S(1)} %constant_dynamic-update-slice_fusion.mine_ref, bf16[96,1024]{1,0:T(8,128)(2,1)S(1)} %collective-permute-done.2.other_ref, bf16[192,2048]{1,0:T(8,128)(2,1)S(1)} %copy-done, bf16[192,2048]{1,0:T(8,128)(2,1)S(1)} %copy-done.1, ...), custom_call_target="tpu_custom_call" | custom-call | bytes 10000 | tf_op jit(solution)/shard_map/expert/pallas_call | solution.py:236
  15.0 0.2 collective-permute-start.3
  15.2 1.3 %collective-permute-done.3 = bf16[96,1024]{1,0:T(8,128)(2,1)S(1)} collective-permute-done((bf16[96,1024]{1,0:T(8,128)(2,1)S(1)}, bf16[96,1024]{1,0:T(8,128)(2,1)S(1)}, u32[]{:S(2)}, u32[]{:S(2)}) %collective-permute-start.3) | collective-permute-done | bytes 196640 | tf_op jit(solution)/shard_map/ppermute | solution.py:185
  16.6 3.7 %collective-permute-start.5 = (bf16[48,1024]{1,0:T(8,128)(2,1)S(1)}, bf16[48,1024]{1,0:T(8,128)(2,1)S(1)}, u32[]{:S(2)}, u32[]{:S(2)}) collective-permute-start(bf16[48,1024]{1,0:T(8,128)(2,1)S(1)} %slice.25), channel_id=1, source_target_pairs={{0,8},{4,12},{8,0},{12,4},{16,24},{20,28},{24,16},{28,20},{1,9},{5... | collective-permute-start | bytes 294920 | tf_op jit(solution)/shard_map/ppermute | solution.py:185
  20.2 1.3 %collective-permute-start.9 = (bf16[3,48,2048]{2,1,0:T(8,128)(2,1)}, bf16[3,48,2048]{2,1,0:T(8,128)(2,1)S(1)}, u32[]{:S(2)}, u32[]{:S(2)}) collective-permute-start(bf16[3,48,2048]{2,1,0:T(8,128)(2,1)} %get-tuple-element.48), channel_id=1, source_target_pairs={{12,4},{28,20},{13,5},{29,21},{14,6},{30,22},{15,7},{31,23}} | collective-permute-start | bytes 1769480 | tf_op jit(solution)/shard_map/ppermute | solution.py:189
  21.5 0.7 %collective-permute-start.8 = (bf16[3,48,2048]{2,1,0:T(8,128)(2,1)S(1)}, bf16[3,48,2048]{2,1,0:T(8,128)(2,1)S(1)}, u32[]{:S(2)}, u32[]{:S(2)}) collective-permute-start(bf16[3,48,2048]{2,1,0:T(8,128)(2,1)S(1)} %collective-permute-done.4.shared_ref), channel_id=1, source_target_pairs={{0,1},{16,17},{1,0},{17,16},{2,3},{18,19},{3,2},{19,18}} | collective-permute-start | bytes 1769480 | tf_op jit(solution)/shard_map/ppermute | solution.py:197
  22.2 6.0 %collective-permute-done.6.first_ref = bf16[3,48,2048]{2,1,0:T(8,128)(2,1)S(1)} collective-permute-done((bf16[3,48,2048]{2,1,0:T(8,128)(2,1)S(1)}, bf16[3,48,2048]{2,1,0:T(8,128)(2,1)S(1)}, u32[]{:S(2)}, u32[]{:S(2)}) %collective-permute-start.6) | collective-permute-done | bytes 589856 | tf_op jit(solution)/shard_map/ppermute | solution.py:189
  28.2 1.1 %collective-permute-done.5 = bf16[48,1024]{1,0:T(8,128)(2,1)S(1)} collective-permute-done((bf16[48,1024]{1,0:T(8,128)(2,1)S(1)}, bf16[48,1024]{1,0:T(8,128)(2,1)S(1)}, u32[]{:S(2)}, u32[]{:S(2)}) %collective-permute-start.5) | collective-permute-done | bytes 98336 | tf_op jit(solution)/shard_map/ppermute | solution.py:185
  29.3 0.6 %fusion.1 = (bf16[24,1024]{1,0:T(8,128)(2,1)S(1)}, bf16[24,1024]{1,0:T(8,128)(2,1)}) fusion(bf16[48,1024]{1,0:T(8,128)(2,1)S(1)} %fusion), kind=kLoop, calls=%fused_computation.7 | loop fusion | bytes 196608 | tf_op jit(solution)/shard_map/slice | solution.py:255
  29.9 1.2 %collective-permute-start.7 = (bf16[24,1024]{1,0:T(8,128)(2,1)S(1)}, bf16[24,1024]{1,0:T(8,128)(2,1)S(1)}, u32[]{:S(2)}, u32[]{:S(2)}) collective-permute-start(bf16[24,1024]{1,0:T(8,128)(2,1)S(1)} %get-tuple-element.56), channel_id=1, source_target_pairs={{0,16},{4,20},{8,24},{12,28},{16,0},{20,4},{24,8},{28,12},{1,17},{... | collective-permute-start | bytes 147464 | tf_op jit(solution)/shard_map/ppermute | solution.py:185
  31.1 2.0 %collective-permute-done.7.refs_1_ = bf16[24,1024]{1,0:T(8,128)(2,1)S(1)} collective-permute-done((bf16[24,1024]{1,0:T(8,128)(2,1)S(1)}, bf16[24,1024]{1,0:T(8,128)(2,1)S(1)}, u32[]{:S(2)}, u32[]{:S(2)}) %collective-permute-start.7) | collective-permute-done | bytes 49184 | tf_op jit(solution)/shard_map/ppermute | solution.py:185
  33.1 0.6 %copy-done.9 = bf16[24,1024]{1,0:T(8,128)(2,1)} copy-done((bf16[24,1024]{1,0:T(8,128)(2,1)}, bf16[24,1024]{1,0:T(8,128)(2,1)S(1)}, u32[]{:S(2)}) %copy-start.9) | copy-done | bytes 49176
  33.7 0.7 %collective-permute-start.10 = (bf16[3,96,2048]{2,1,0:T(8,128)(2,1)}, bf16[3,96,2048]{2,1,0:T(8,128)(2,1)S(1)}, u32[]{:S(2)}, u32[]{:S(2)}) collective-permute-start(bf16[3,96,2048]{2,1,0:T(8,128)(2,1)} %get-tuple-element.55), channel_id=1, source_target_pairs={{12,8},{28,24},{13,9},{29,25},{14,10},{30,26},{15,11},{31,27}} | collective-permute-start | bytes 3538952 | tf_op jit(solution)/shard_map/ppermute | solution.py:189
  34.5 0.7 %copy.9.ids_ref = s32[128,8]{1,0:T(8,128)} copy(s32[128,8]{0,1:T(8,128)S(1)} %copy-done.7) | data formatting | bytes 8192 | tf_op args[1]
  35.2 0.7 %copy.10.weight_ref = f32[128,8]{1,0:T(8,128)} copy(f32[128,8]{0,1:T(8,128)S(1)} %copy-done.12) | data formatting | bytes 8192 | tf_op args[2]
  35.9 0.8 %copy-done.3 = s32[128,8]{1,0:T(8,128)S(1)} copy-done((s32[128,8]{1,0:T(8,128)S(1)}, s32[128,8]{1,0:T(8,128)}, u32[]{:S(2)}) %copy-start.3) | copy-done | bytes 4120
  36.8 0.8 %copy-done.4 = f32[128,8]{1,0:T(8,128)S(1)} copy-done((f32[128,8]{1,0:T(8,128)S(1)}, f32[128,8]{1,0:T(8,128)}, u32[]{:S(2)}) %copy-start.4) | copy-done | bytes 4120
  37.6 0.8 %copy-done.5 = bf16[24,1024]{1,0:T(8,128)(2,1)S(1)} copy-done((bf16[24,1024]{1,0:T(8,128)(2,1)S(1)}, bf16[24,1024]{1,0:T(8,128)(2,1)}, u32[]{:S(2)}) %copy-start.5) | copy-done | bytes 49176
  38.4 0.8 %copy-done.10 = bf16[24,1024]{1,0:T(8,128)(2,1)S(1)} copy-done((bf16[24,1024]{1,0:T(8,128)(2,1)S(1)}, bf16[24,1024]{1,0:T(8,128)(2,1)}, u32[]{:S(2)}) %copy-start.10) | copy-done | bytes 49176
  39.2 1.8 %combine.1 = bf16[128,2048]{1,0:T(8,128)(2,1)} custom-call(s32[128,8]{1,0:T(8,128)S(1)} %copy-done.3, f32[128,8]{1,0:T(8,128)S(1)} %copy-done.4, bf16[24,1024]{1,0:T(8,128)(2,1)S(1)} %copy-done.5, bf16[24,1024]{1,0:T(8,128)(2,1)S(1)} %copy-done.10), custom_call_target="tpu_custom_call" | custom-call | flops 12000000000 | bytes 10000 | tf_op jit(solution)/shard_map/combine/pallas_call | solution.py:260
  41.0 1.1 %merge.1 = bf16[3,96,2048]{2,1,0:T(8,128)(2,1)} custom-call(bf16[3,48,2048]{2,1,0:T(8,128)(2,1)S(1)} %collective-permute-done.4.shared_ref, bf16[3,48,2048]{2,1,0:T(8,128)(2,1)S(1)} %collective-permute-done.8.swapped_ref, bf16[3,48,2048]{2,1,0:T(8,128)(2,1)S(1)} %collective-permute-done.6.first_ref, ...), custom_call_target="tpu_custom_call" | custom-call | tf_op jit(solution)/shard_map/merge/pallas_call | solution.py:270
  (30 shorter events, 0.2 us)
Async XLA Ops:
  0.6 0.7 %copy-start.6 = (s32[128,8]{0,1:T(8,128)S(1)}, s32[128,8]{0,1:T(8,128)}, u32[]{:S(2)}) copy-start(s32[128,8]{0,1:T(8,128)} %param.8) | copy-start | bytes 12292
  1.3 1.0 %copy-start.8 = (bf16[128,2048]{1,0:T(8,128)(2,1)S(1)}, bf16[128,2048]{1,0:T(8,128)(2,1)}, u32[]{:S(2)}) copy-start(bf16[128,2048]{1,0:T(8,128)(2,1)} %tok_ref.1) | copy-start | bytes 1572868
  2.4 2.6 %copy-start = (bf16[192,2048]{1,0:T(8,128)(2,1)S(1)}, bf16[192,2048]{1,0:T(8,128)(2,1)}, u32[]{:S(2)}) copy-start(bf16[192,2048]{1,0:T(8,128)(2,1)} %gate_ref.2) | copy-start | bytes 2359300
  2.4 2.6 %copy-start.1 = (bf16[192,2048]{1,0:T(8,128)(2,1)S(1)}, bf16[192,2048]{1,0:T(8,128)(2,1)}, u32[]{:S(2)}) copy-start(bf16[192,2048]{1,0:T(8,128)(2,1)} %up_ref.2) | copy-start | bytes 2359300
  2.4 2.6 %copy-start.2 = (bf16[192,2048]{1,0:T(8,128)(2,1)S(1)}, bf16[192,2048]{1,0:T(8,128)(2,1)}, u32[]{:S(2)}) copy-start(bf16[192,2048]{1,0:T(8,128)(2,1)} %down_ref.2) | copy-start | bytes 2359300
  2.4 2.6 %copy-start.11 = (s32[2,3,96]{2,0,1:T(2,128)S(1)}, s32[2,3,96]{2,0,1:T(2,128)}, u32[]{:S(2)}) copy-start(s32[2,3,96]{2,0,1:T(2,128)} %param.13) | copy-start | bytes 6916
  2.8 3.6 %collective-permute-start = (bf16[24,1024]{1,0:T(8,128)(2,1)S(1)}, bf16[24,1024]{1,0:T(8,128)(2,1)S(1)}, u32[]{:S(2)}, u32[]{:S(2)}) collective-permute-start(bf16[24,1024]{1,0:T(8,128)(2,1)S(1)} %get-tuple-element.31), channel_id=1, source_target_pairs={{0,16},{4,20},{8,24},{12,28},{16,0},{20,4},{24,8},{28,12},{1,17},{... | collective-permute-start | bytes 147464 | tf_op jit(solution)/shard_map/ppermute | solution.py:185
  6.4 4.1 %collective-permute-start.1 = (bf16[48,1024]{1,0:T(8,128)(2,1)S(1)}, bf16[48,1024]{1,0:T(8,128)(2,1)S(1)}, u32[]{:S(2)}, u32[]{:S(2)}) collective-permute-start(bf16[48,1024]{1,0:T(8,128)(2,1)S(1)} %pad_maximum_fusion), channel_id=1, source_target_pairs={{0,8},{4,12},{8,0},{12,4},{16,24},{20,28},{24,16},{28,20},{1,9},{5... | collective-permute-start | bytes 294920 | tf_op jit(solution)/shard_map/ppermute | solution.py:185
  8.5 8.0 %collective-permute-start.4 = (bf16[3,48,2048]{2,1,0:T(8,128)(2,1)S(1)}, bf16[3,48,2048]{2,1,0:T(8,128)(2,1)S(1)}, u32[]{:S(2)}, u32[]{:S(2)}) collective-permute-start(bf16[3,48,2048]{2,1,0:T(8,128)(2,1)S(1)} %get-tuple-element.42), channel_id=1, source_target_pairs={{12,0},{28,16},{13,1},{29,17},{14,2},{30,18},{15,3},{31,19}} | collective-permute-start | bytes 1769480 | tf_op jit(solution)/shard_map/ppermute | solution.py:189
  10.5 3.5 %collective-permute-start.2 = (bf16[96,1024]{1,0:T(8,128)(2,1)S(1)}, bf16[96,1024]{1,0:T(8,128)(2,1)S(1)}, u32[]{:S(2)}, u32[]{:S(2)}) collective-permute-start(bf16[96,1024]{1,0:T(8,128)(2,1)S(1)} %constant_dynamic-update-slice_fusion.mine_ref), channel_id=1, source_target_pairs={{0,4},{4,0},{8,12},{12,8},{16,20},{20,16},{24,28},{28,24},{1,5},{5... | collective-permute-start | bytes 589832 | tf_op jit(solution)/shard_map/ppermute | solution.py:185
  12.7 15.5 %collective-permute-start.6 = (bf16[3,48,2048]{2,1,0:T(8,128)(2,1)S(1)}, bf16[3,48,2048]{2,1,0:T(8,128)(2,1)S(1)}, u32[]{:S(2)}, u32[]{:S(2)}) collective-permute-start(bf16[3,48,2048]{2,1,0:T(8,128)(2,1)S(1)} %get-tuple-element.44), channel_id=1, source_target_pairs={{12,4},{28,20},{13,5},{29,21},{14,6},{30,22},{15,7},{31,23}} | collective-permute-start | bytes 1769480 | tf_op jit(solution)/shard_map/ppermute | solution.py:189
  14.9 19.5 %copy-start.7 = (s32[128,8]{0,1:T(8,128)S(1)}, s32[128,8]{0,1:T(8,128)}, u32[]{:S(2)}) copy-start(s32[128,8]{0,1:T(8,128)} %param.8) | copy-start | bytes 12292
  15.0 20.3 %copy-start.12 = (f32[128,8]{0,1:T(8,128)S(1)}, f32[128,8]{0,1:T(8,128)}, u32[]{:S(2)}) copy-start(f32[128,8]{0,1:T(8,128)} %param.9) | copy-start | bytes 12292
  15.0 1.5 %collective-permute-start.3 = (bf16[96,1024]{1,0:T(8,128)(2,1)S(1)}, bf16[96,1024]{1,0:T(8,128)(2,1)S(1)}, u32[]{:S(2)}, u32[]{:S(2)}) collective-permute-start(bf16[96,1024]{1,0:T(8,128)(2,1)S(1)} %get-tuple-element.41), channel_id=1, source_target_pairs={{0,4},{4,0},{8,12},{12,8},{16,20},{20,16},{24,28},{28,24},{1,5},{5... | collective-permute-start | bytes 589832 | tf_op jit(solution)/shard_map/ppermute | solution.py:185
  16.6 12.7 %collective-permute-start.5 = (bf16[48,1024]{1,0:T(8,128)(2,1)S(1)}, bf16[48,1024]{1,0:T(8,128)(2,1)S(1)}, u32[]{:S(2)}, u32[]{:S(2)}) collective-permute-start(bf16[48,1024]{1,0:T(8,128)(2,1)S(1)} %slice.25), channel_id=1, source_target_pairs={{0,8},{4,12},{8,0},{12,4},{16,24},{20,28},{24,16},{28,20},{1,9},{5... | collective-permute-start | bytes 294920 | tf_op jit(solution)/shard_map/ppermute | solution.py:185
  20.2 15.7 %collective-permute-start.9 = (bf16[3,48,2048]{2,1,0:T(8,128)(2,1)}, bf16[3,48,2048]{2,1,0:T(8,128)(2,1)S(1)}, u32[]{:S(2)}, u32[]{:S(2)}) collective-permute-start(bf16[3,48,2048]{2,1,0:T(8,128)(2,1)} %get-tuple-element.48), channel_id=1, source_target_pairs={{12,4},{28,20},{13,5},{29,21},{14,6},{30,22},{15,7},{31,23}} | collective-permute-start | bytes 1769480 | tf_op jit(solution)/shard_map/ppermute | solution.py:189
  21.5 14.4 %collective-permute-start.8 = (bf16[3,48,2048]{2,1,0:T(8,128)(2,1)S(1)}, bf16[3,48,2048]{2,1,0:T(8,128)(2,1)S(1)}, u32[]{:S(2)}, u32[]{:S(2)}) collective-permute-start(bf16[3,48,2048]{2,1,0:T(8,128)(2,1)S(1)} %collective-permute-done.4.shared_ref), channel_id=1, source_target_pairs={{0,1},{16,17},{1,0},{17,16},{2,3},{18,19},{3,2},{19,18}} | collective-permute-start | bytes 1769480 | tf_op jit(solution)/shard_map/ppermute | solution.py:197
  29.9 3.2 %collective-permute-start.7 = (bf16[24,1024]{1,0:T(8,128)(2,1)S(1)}, bf16[24,1024]{1,0:T(8,128)(2,1)S(1)}, u32[]{:S(2)}, u32[]{:S(2)}) collective-permute-start(bf16[24,1024]{1,0:T(8,128)(2,1)S(1)} %get-tuple-element.56), channel_id=1, source_target_pairs={{0,16},{4,20},{8,24},{12,28},{16,0},{20,4},{24,8},{28,12},{1,17},{... | collective-permute-start | bytes 147464 | tf_op jit(solution)/shard_map/ppermute | solution.py:185
  33.1 0.6 %copy-start.9 = (bf16[24,1024]{1,0:T(8,128)(2,1)}, bf16[24,1024]{1,0:T(8,128)(2,1)S(1)}, u32[]{:S(2)}) copy-start(bf16[24,1024]{1,0:T(8,128)(2,1)S(1)} %collective-permute-done.7.refs_1_) | copy-start | bytes 147460
  33.7 7.2 %collective-permute-start.10 = (bf16[3,96,2048]{2,1,0:T(8,128)(2,1)}, bf16[3,96,2048]{2,1,0:T(8,128)(2,1)S(1)}, u32[]{:S(2)}, u32[]{:S(2)}) collective-permute-start(bf16[3,96,2048]{2,1,0:T(8,128)(2,1)} %get-tuple-element.55), channel_id=1, source_target_pairs={{12,8},{28,24},{13,9},{29,25},{14,10},{30,26},{15,11},{31,27}} | collective-permute-start | bytes 3538952 | tf_op jit(solution)/shard_map/ppermute | solution.py:189
  35.9 0.8 %copy-start.3 = (s32[128,8]{1,0:T(8,128)S(1)}, s32[128,8]{1,0:T(8,128)}, u32[]{:S(2)}) copy-start(s32[128,8]{1,0:T(8,128)} %copy.9.ids_ref) | copy-start | bytes 12292
  36.8 0.8 %copy-start.4 = (f32[128,8]{1,0:T(8,128)S(1)}, f32[128,8]{1,0:T(8,128)}, u32[]{:S(2)}) copy-start(f32[128,8]{1,0:T(8,128)} %copy.10.weight_ref) | copy-start | bytes 12292
  37.6 0.8 %copy-start.5 = (bf16[24,1024]{1,0:T(8,128)(2,1)S(1)}, bf16[24,1024]{1,0:T(8,128)(2,1)}, u32[]{:S(2)}) copy-start(bf16[24,1024]{1,0:T(8,128)(2,1)} %get-tuple-element.49.refs_0_) | copy-start | bytes 147460
  38.4 0.8 %copy-start.10 = (bf16[24,1024]{1,0:T(8,128)(2,1)S(1)}, bf16[24,1024]{1,0:T(8,128)(2,1)}, u32[]{:S(2)}) copy-start(bf16[24,1024]{1,0:T(8,128)(2,1)} %copy-done.9) | copy-start | bytes 147460

commit v8 on v7

--- a/solution.py
+++ b/solution.py
@@ -16,8 +16,8 @@
 HBM = pl.BlockSpec(memory_space=pl.ANY)
 
 
-def params():
-    return pltpu.CompilerParams(vmem_limit_bytes=40 * 1024 * 1024)
+def params(megabytes=16):
+    return pltpu.CompilerParams(vmem_limit_bytes=megabytes * 1024 * 1024)
 
 
 def cost(microseconds):
@@ -102,11 +102,11 @@
 
     for even in range(2):
 
-        @pl.when(jnp.logical_and(position == 0, parity == even))
+        @pl.when(jnp.logical_and(position == 1, parity == even))
         def _():
             move([(shared_ref, half * even), (swapped_ref, half * (1 - even))])
 
-    @pl.when(jnp.logical_or(position == 1, position == 3))
+    @pl.when(jnp.logical_or(position == 0, position == 3))
     def _():
         move([(first_ref, 0), (second_ref, first_ref.shape[1])])
 
@@ -192,7 +192,7 @@
         route = []
         for r in range(replicas):
             for i in range(devices):
-                if i % GROUP == 0:
+                if i % GROUP == 1:
                     route.append((i * replicas + r, i * replicas + (r ^ 1)))
         return lax.ppermute(block, ("expert", "replica"), route)
 
@@ -221,13 +221,13 @@
     parcels = [parcels[0], across] + list(parcels[2:])
     across = [send(parcels[j], j, 0) for j in range(1, experts)]
     here = jnp.concatenate([parcels[0]] + across, axis=0)
-    chosen = select([(0, None, half), (1, 0, half), (1, half, most - half), (2, 0, most)], held)
+    chosen = select([(1, None, half), (0, 0, half), (0, half, most - half), (2, 0, most)], held)
     here, chosen = lax.optimization_barrier((here, chosen))
     mine = jnp.concatenate([here, send(here, 0, 2)], axis=0)
     other = send(mine, 0, 1)
 
-    shared = migrate(chosen[0], 0)
-    first = migrate(chosen[1], 1)
+    shared = migrate(chosen[0], 1)
+    first = migrate(chosen[1], 0)
 
     total = mine.shape[0]
     step = min(total, 4 * PACK)
@@ -249,7 +249,7 @@
 
     far, first = lax.optimization_barrier((far, first))
     swapped = swap(shared)
-    second = migrate(lax.optimization_barrier((chosen[2], summed))[0], 1)
+    second = migrate(lax.optimization_barrier((chosen[2], summed))[0], 0)
 
     summed = (summed[: total // 2] + far.astype(F32)).astype(BF16)
     pieces = [summed[j * PACK : (j + 1) * PACK] for j in range(experts)]
@@ -262,7 +262,7 @@
         out_shape=shape(tokens.shape[0], width),
         in_specs=[VMEM, VMEM] + [VMEM] * len(back),
         out_specs=VMEM,
-        compiler_params=params(),
+        compiler_params=params(14 + experts),
         cost_estimate=cost(12),
         name="combine",
     )(expert_ids, combine, *back)

time: 42.5 us -> 41.6 us (0.979)
  the two profiles are of different devices: /device:TPU:1 before, /device:TPU:0 now
where the time goes in v8:
time: 41.6 us; the launch traced here: 41.2 us
  starting transfers between devices  13.8 us (33%)
  waiting for transfers between devices  13.4 us (32%)
  local copies, waits for them, and re-layouts  7.74 us (19%)
  Pallas kernels  5.36 us (13%)
  between operations  0.78 us (2%)
    ppermute x6, starting transfers between devices, send(): return lax.ppermute(block, 'expert', route)  9.11 us
    ppermute x6, waiting for transfers between devices, send(): return lax.ppermute(block, 'expert', route)  7.31 us
    unnamed x29, local copies, waits for them, and re-layouts  7.1 us
    ppermute x4, waiting for transfers between devices, migrate(): return lax.ppermute(block, 'expert', route)  6.11 us
    ppermute x4, starting transfers between devices, migrate(): return lax.ppermute(block, 'expert', route)  3.98 us
    pallas_call x1, Pallas kernels, on_device(): pl.pallas_call(functools.partial(combine_kernel, experts), out_shape=shap...  1.75 us
    pallas_call x1, Pallas kernels, select(): pl.pallas_call(functools.partial(select_kernel, wanted), out_shape=[shape...  1.23 us
    pallas_call x1, Pallas kernels, on_device(): pl.pallas_call(merge_kernel, out_shape=shape(3, most, width), in_specs=[H...  1.05 us
  transfers between devices with their start and end apart: 11, of which 6 were waited for; matrix products, arithmetic and copies ran while one was open for 5% of the time, Pallas kernels for 9%

profile of v8, /device:TPU:0, one launch (start us, length us, event | category | flops | bytes accessed | tf_op | source)
XLA Modules:
  0.0 41.2 jit_solution(13537245552442074468)
XLA Ops:
  0.6 0.7 %copy-done.6 = s32[128,8]{0,1:T(8,128)S(1)} copy-done((s32[128,8]{0,1:T(8,128)S(1)}, s32[128,8]{0,1:T(8,128)}, u32[]{:S(2)}) %copy-start.6) | copy-done | bytes 4120
  1.3 1.0 %copy-done.8 = bf16[128,2048]{1,0:T(8,128)(2,1)S(1)} copy-done((bf16[128,2048]{1,0:T(8,128)(2,1)S(1)}, bf16[128,2048]{1,0:T(8,128)(2,1)}, u32[]{:S(2)}) %copy-start.8) | copy-done | bytes 524312
  2.4 0.4 dispatch.1
  2.8 3.0 %collective-permute-start = (bf16[24,1024]{1,0:T(8,128)(2,1)S(1)}, bf16[24,1024]{1,0:T(8,128)(2,1)S(1)}, u32[]{:S(2)}, u32[]{:S(2)}) collective-permute-start(bf16[24,1024]{1,0:T(8,128)(2,1)S(1)} %get-tuple-element.31), channel_id=1, source_target_pairs={{0,16},{4,20},{8,24},{12,28},{16,0},{20,4},{24,8},{28,12},{1,17},{... | collective-permute-start | bytes 147464 | tf_op jit(solution)/shard_map/ppermute | solution.py:185
  5.8 1.2 %select.1 = (bf16[3,48,2048]{2,1,0:T(8,128)(2,1)S(1)}, bf16[3,48,2048]{2,1,0:T(8,128)(2,1)S(1)}, bf16[3,48,2048]{2,1,0:T(8,128)(2,1)}, bf16[3,96,2048]{2,1,0:T(8,128)(2,1)}) custom-call(s32[3,2,96]{2,1,0:T(2,128)S(1)} %bitcast.3, bf16[192,2048]{1,0:T(8,128)(2,1)S(1)} %copy-done, bf16[192,2048]{1,0:T(8,128)(2,1)S(1)} %copy-done.1, bf16[192,2048]{1,0:T(8,128)(2,1)S(1)} %copy-done.2), custom_call_target="tpu_custom_call" | custom-call | flops 2000000000 | bytes 10000 | tf_op jit(solution)/shard_map/select/pallas_call | solution.py:200
  7.1 0.8 %collective-permute-done = bf16[24,1024]{1,0:T(8,128)(2,1)S(1)} collective-permute-done((bf16[24,1024]{1,0:T(8,128)(2,1)S(1)}, bf16[24,1024]{1,0:T(8,128)(2,1)S(1)}, u32[]{:S(2)}, u32[]{:S(2)}) %collective-permute-start) | collective-permute-done | bytes 49184 | tf_op jit(solution)/shard_map/ppermute | solution.py:185
  7.9 2.1 %collective-permute-start.1 = (bf16[48,1024]{1,0:T(8,128)(2,1)S(1)}, bf16[48,1024]{1,0:T(8,128)(2,1)S(1)}, u32[]{:S(2)}, u32[]{:S(2)}) collective-permute-start(bf16[48,1024]{1,0:T(8,128)(2,1)S(1)} %pad_maximum_fusion), channel_id=1, source_target_pairs={{0,8},{4,12},{8,0},{12,4},{16,24},{20,28},{24,16},{28,20},{1,9},{5... | collective-permute-start | bytes 294920 | tf_op jit(solution)/shard_map/ppermute | solution.py:185
  10.0 0.7 %collective-permute-start.4 = (bf16[3,48,2048]{2,1,0:T(8,128)(2,1)S(1)}, bf16[3,48,2048]{2,1,0:T(8,128)(2,1)S(1)}, u32[]{:S(2)}, u32[]{:S(2)}) collective-permute-start(bf16[3,48,2048]{2,1,0:T(8,128)(2,1)S(1)} %get-tuple-element.42), channel_id=1, source_target_pairs={{12,4},{28,20},{13,5},{29,21},{14,6},{30,22},{15,7},{31,23}} | collective-permute-start | bytes 1769480 | tf_op jit(solution)/shard_map/ppermute | solution.py:189
  10.7 1.9 %collective-permute-done.1 = bf16[48,1024]{1,0:T(8,128)(2,1)S(1)} collective-permute-done((bf16[48,1024]{1,0:T(8,128)(2,1)S(1)}, bf16[48,1024]{1,0:T(8,128)(2,1)S(1)}, u32[]{:S(2)}, u32[]{:S(2)}) %collective-permute-start.1) | collective-permute-done | bytes 98336 | tf_op jit(solution)/shard_map/ppermute | solution.py:185
  12.6 0.1 collective-permute-start.2
  12.7 1.3 %collective-permute-start.6 = (bf16[3,48,2048]{2,1,0:T(8,128)(2,1)S(1)}, bf16[3,48,2048]{2,1,0:T(8,128)(2,1)S(1)}, u32[]{:S(2)}, u32[]{:S(2)}) collective-permute-start(bf16[3,48,2048]{2,1,0:T(8,128)(2,1)S(1)} %get-tuple-element.44), channel_id=1, source_target_pairs={{12,0},{28,16},{13,1},{29,17},{14,2},{30,18},{15,3},{31,19}} | collective-permute-start | bytes 1769480 | tf_op jit(solution)/shard_map/ppermute | solution.py:189
  14.0 0.1 collective-permute-done.2.other_ref
  14.1 0.9 %expert.1 = (f32[96,1024]{1,0:T(8,128)S(1)}, bf16[96,1024]{1,0:T(8,128)(2,1)S(1)}) custom-call(bf16[96,1024]{1,0:T(8,128)(2,1)S(1)} %constant_dynamic-update-slice_fusion.mine_ref, bf16[96,1024]{1,0:T(8,128)(2,1)S(1)} %collective-permute-done.2.other_ref, bf16[192,2048]{1,0:T(8,128)(2,1)S(1)} %copy-done, bf16[192,2048]{1,0:T(8,128)(2,1)S(1)} %copy-done.1, ...), custom_call_target="tpu_custom_call" | custom-call | bytes 10000 | tf_op jit(solution)/shard_map/expert/pallas_call | solution.py:236
  15.1 0.2 collective-permute-start.3
  15.3 1.3 %collective-permute-done.3 = bf16[96,1024]{1,0:T(8,128)(2,1)S(1)} collective-permute-done((bf16[96,1024]{1,0:T(8,128)(2,1)S(1)}, bf16[96,1024]{1,0:T(8,128)(2,1)S(1)}, u32[]{:S(2)}, u32[]{:S(2)}) %collective-permute-start.3) | collective-permute-done | bytes 196640 | tf_op jit(solution)/shard_map/ppermute | solution.py:185
  16.6 2.4 %collective-permute-start.5 = (bf16[48,1024]{1,0:T(8,128)(2,1)S(1)}, bf16[48,1024]{1,0:T(8,128)(2,1)S(1)}, u32[]{:S(2)}, u32[]{:S(2)}) collective-permute-start(bf16[48,1024]{1,0:T(8,128)(2,1)S(1)} %slice.25), channel_id=1, source_target_pairs={{0,8},{4,12},{8,0},{12,4},{16,24},{20,28},{24,16},{28,20},{1,9},{5... | collective-permute-start | bytes 294920 | tf_op jit(solution)/shard_map/ppermute | solution.py:185
  19.0 1.3 %collective-permute-start.9 = (bf16[3,48,2048]{2,1,0:T(8,128)(2,1)}, bf16[3,48,2048]{2,1,0:T(8,128)(2,1)S(1)}, u32[]{:S(2)}, u32[]{:S(2)}) collective-permute-start(bf16[3,48,2048]{2,1,0:T(8,128)(2,1)} %get-tuple-element.48), channel_id=1, source_target_pairs={{12,0},{28,16},{13,1},{29,17},{14,2},{30,18},{15,3},{31,19}} | collective-permute-start | bytes 1769480 | tf_op jit(solution)/shard_map/ppermute | solution.py:189
  20.3 0.7 %collective-permute-start.8 = (bf16[3,48,2048]{2,1,0:T(8,128)(2,1)S(1)}, bf16[3,48,2048]{2,1,0:T(8,128)(2,1)S(1)}, u32[]{:S(2)}, u32[]{:S(2)}) collective-permute-start(bf16[3,48,2048]{2,1,0:T(8,128)(2,1)S(1)} %collective-permute-done.4.shared_ref), channel_id=1, source_target_pairs={{4,5},{20,21},{5,4},{21,20},{6,7},{22,23},{7,6},{23,22}} | collective-permute-start | bytes 1769480 | tf_op jit(solution)/shard_map/ppermute | solution.py:197
  21.0 6.1 %collective-permute-done.6.first_ref = bf16[3,48,2048]{2,1,0:T(8,128)(2,1)S(1)} collective-permute-done((bf16[3,48,2048]{2,1,0:T(8,128)(2,1)S(1)}, bf16[3,48,2048]{2,1,0:T(8,128)(2,1)S(1)}, u32[]{:S(2)}, u32[]{:S(2)}) %collective-permute-start.6) | collective-permute-done | bytes 589856 | tf_op jit(solution)/shard_map/ppermute | solution.py:189
  27.1 0.6 %fusion.1 = (bf16[24,1024]{1,0:T(8,128)(2,1)S(1)}, bf16[24,1024]{1,0:T(8,128)(2,1)}) fusion(bf16[48,1024]{1,0:T(8,128)(2,1)S(1)} %fusion), kind=kLoop, calls=%fused_computation.7 | loop fusion | bytes 196608 | tf_op jit(solution)/shard_map/slice | solution.py:255
  27.8 1.4 %collective-permute-start.7 = (bf16[24,1024]{1,0:T(8,128)(2,1)S(1)}, bf16[24,1024]{1,0:T(8,128)(2,1)S(1)}, u32[]{:S(2)}, u32[]{:S(2)}) collective-permute-start(bf16[24,1024]{1,0:T(8,128)(2,1)S(1)} %get-tuple-element.56), channel_id=1, source_target_pairs={{0,16},{4,20},{8,24},{12,28},{16,0},{20,4},{24,8},{28,12},{1,17},{... | collective-permute-start | bytes 147464 | tf_op jit(solution)/shard_map/ppermute | solution.py:185
  29.1 3.1 %collective-permute-done.7.refs_1_ = bf16[24,1024]{1,0:T(8,128)(2,1)S(1)} collective-permute-done((bf16[24,1024]{1,0:T(8,128)(2,1)S(1)}, bf16[24,1024]{1,0:T(8,128)(2,1)S(1)}, u32[]{:S(2)}, u32[]{:S(2)}) %collective-permute-start.7) | collective-permute-done | bytes 49184 | tf_op jit(solution)/shard_map/ppermute | solution.py:185
  32.3 0.6 %copy-done.9 = bf16[24,1024]{1,0:T(8,128)(2,1)} copy-done((bf16[24,1024]{1,0:T(8,128)(2,1)}, bf16[24,1024]{1,0:T(8,128)(2,1)S(1)}, u32[]{:S(2)}) %copy-start.9) | copy-done | bytes 49176
  32.9 0.7 %collective-permute-start.10 = (bf16[3,96,2048]{2,1,0:T(8,128)(2,1)}, bf16[3,96,2048]{2,1,0:T(8,128)(2,1)S(1)}, u32[]{:S(2)}, u32[]{:S(2)}) collective-permute-start(bf16[3,96,2048]{2,1,0:T(8,128)(2,1)} %get-tuple-element.55), channel_id=1, source_target_pairs={{12,8},{28,24},{13,9},{29,25},{14,10},{30,26},{15,11},{31,27}} | collective-permute-start | bytes 3538952 | tf_op jit(solution)/shard_map/ppermute | solution.py:189
  33.6 0.7 %copy.9.ids_ref = s32[128,8]{1,0:T(8,128)} copy(s32[128,8]{0,1:T(8,128)S(1)} %copy-done.7) | data formatting | bytes 8192 | tf_op args[1]
  34.4 0.7 %copy.10.weight_ref = f32[128,8]{1,0:T(8,128)} copy(f32[128,8]{0,1:T(8,128)S(1)} %copy-done.12) | data formatting | bytes 8192 | tf_op args[2]
  35.1 0.8 %copy-done.3 = s32[128,8]{1,0:T(8,128)S(1)} copy-done((s32[128,8]{1,0:T(8,128)S(1)}, s32[128,8]{1,0:T(8,128)}, u32[]{:S(2)}) %copy-start.3) | copy-done | bytes 4120
  35.9 0.8 %copy-done.4 = f32[128,8]{1,0:T(8,128)S(1)} copy-done((f32[128,8]{1,0:T(8,128)S(1)}, f32[128,8]{1,0:T(8,128)}, u32[]{:S(2)}) %copy-start.4) | copy-done | bytes 4120
  36.8 0.8 %copy-done.5 = bf16[24,1024]{1,0:T(8,128)(2,1)S(1)} copy-done((bf16[24,1024]{1,0:T(8,128)(2,1)S(1)}, bf16[24,1024]{1,0:T(8,128)(2,1)}, u32[]{:S(2)}) %copy-start.5) | copy-done | bytes 49176
  37.6 0.8 %copy-done.10 = bf16[24,1024]{1,0:T(8,128)(2,1)S(1)} copy-done((bf16[24,1024]{1,0:T(8,128)(2,1)S(1)}, bf16[24,1024]{1,0:T(8,128)(2,1)}, u32[]{:S(2)}) %copy-start.10) | copy-done | bytes 49176
  38.4 1.8 %combine.1 = bf16[128,2048]{1,0:T(8,128)(2,1)} custom-call(s32[128,8]{1,0:T(8,128)S(1)} %copy-done.3, f32[128,8]{1,0:T(8,128)S(1)} %copy-done.4, bf16[24,1024]{1,0:T(8,128)(2,1)S(1)} %copy-done.5, bf16[24,1024]{1,0:T(8,128)(2,1)S(1)} %copy-done.10), custom_call_target="tpu_custom_call" | custom-call | flops 12000000000 | bytes 10000 | tf_op jit(solution)/shard_map/combine/pallas_call | solution.py:260
  40.1 1.1 %merge.1 = bf16[3,96,2048]{2,1,0:T(8,128)(2,1)} custom-call(bf16[3,48,2048]{2,1,0:T(8,128)(2,1)S(1)} %collective-permute-done.4.shared_ref, bf16[3,48,2048]{2,1,0:T(8,128)(2,1)S(1)} %collective-permute-done.8.swapped_ref, bf16[3,48,2048]{2,1,0:T(8,128)(2,1)S(1)} %collective-permute-done.6.first_ref, ...), custom_call_target="tpu_custom_call" | custom-call | tf_op jit(solution)/shard_map/merge/pallas_call | solution.py:270
  (30 shorter events, 0.2 us)
Async XLA Ops:
  0.6 0.7 %copy-start.6 = (s32[128,8]{0,1:T(8,128)S(1)}, s32[128,8]{0,1:T(8,128)}, u32[]{:S(2)}) copy-start(s32[128,8]{0,1:T(8,128)} %param.8) | copy-start | bytes 12292
  1.3 1.0 %copy-start.8 = (bf16[128,2048]{1,0:T(8,128)(2,1)S(1)}, bf16[128,2048]{1,0:T(8,128)(2,1)}, u32[]{:S(2)}) copy-start(bf16[128,2048]{1,0:T(8,128)(2,1)} %tok_ref.1) | copy-start | bytes 1572868
  2.4 3.5 %copy-start = (bf16[192,2048]{1,0:T(8,128)(2,1)S(1)}, bf16[192,2048]{1,0:T(8,128)(2,1)}, u32[]{:S(2)}) copy-start(bf16[192,2048]{1,0:T(8,128)(2,1)} %gate_ref.2) | copy-start | bytes 2359300
  2.4 3.5 %copy-start.1 = (bf16[192,2048]{1,0:T(8,128)(2,1)S(1)}, bf16[192,2048]{1,0:T(8,128)(2,1)}, u32[]{:S(2)}) copy-start(bf16[192,2048]{1,0:T(8,128)(2,1)} %up_ref.2) | copy-start | bytes 2359300
  2.4 3.5 %copy-start.2 = (bf16[192,2048]{1,0:T(8,128)(2,1)S(1)}, bf16[192,2048]{1,0:T(8,128)(2,1)}, u32[]{:S(2)}) copy-start(bf16[192,2048]{1,0:T(8,128)(2,1)} %down_ref.2) | copy-start | bytes 2359300
  2.4 3.5 %copy-start.11 = (s32[2,3,96]{2,0,1:T(2,128)S(1)}, s32[2,3,96]{2,0,1:T(2,128)}, u32[]{:S(2)}) copy-start(s32[2,3,96]{2,0,1:T(2,128)} %param.13) | copy-start | bytes 6916
  2.8 5.1 %collective-permute-start = (bf16[24,1024]{1,0:T(8,128)(2,1)S(1)}, bf16[24,1024]{1,0:T(8,128)(2,1)S(1)}, u32[]{:S(2)}, u32[]{:S(2)}) collective-permute-start(bf16[24,1024]{1,0:T(8,128)(2,1)S(1)} %get-tuple-element.31), channel_id=1, source_target_pairs={{0,16},{4,20},{8,24},{12,28},{16,0},{20,4},{24,8},{28,12},{1,17},{... | collective-permute-start | bytes 147464 | tf_op jit(solution)/shard_map/ppermute | solution.py:185
  7.9 4.7 %collective-permute-start.1 = (bf16[48,1024]{1,0:T(8,128)(2,1)S(1)}, bf16[48,1024]{1,0:T(8,128)(2,1)S(1)}, u32[]{:S(2)}, u32[]{:S(2)}) collective-permute-start(bf16[48,1024]{1,0:T(8,128)(2,1)S(1)} %pad_maximum_fusion), channel_id=1, source_target_pairs={{0,8},{4,12},{8,0},{12,4},{16,24},{20,28},{24,16},{28,20},{1,9},{5... | collective-permute-start | bytes 294920 | tf_op jit(solution)/shard_map/ppermute | solution.py:185
  10.0 6.6 %collective-permute-start.4 = (bf16[3,48,2048]{2,1,0:T(8,128)(2,1)S(1)}, bf16[3,48,2048]{2,1,0:T(8,128)(2,1)S(1)}, u32[]{:S(2)}, u32[]{:S(2)}) collective-permute-start(bf16[3,48,2048]{2,1,0:T(8,128)(2,1)S(1)} %get-tuple-element.42), channel_id=1, source_target_pairs={{12,4},{28,20},{13,5},{29,21},{14,6},{30,22},{15,7},{31,23}} | collective-permute-start | bytes 1769480 | tf_op jit(solution)/shard_map/ppermute | solution.py:189
  12.6 1.5 %collective-permute-start.2 = (bf16[96,1024]{1,0:T(8,128)(2,1)S(1)}, bf16[96,1024]{1,0:T(8,128)(2,1)S(1)}, u32[]{:S(2)}, u32[]{:S(2)}) collective-permute-start(bf16[96,1024]{1,0:T(8,128)(2,1)S(1)} %constant_dynamic-update-slice_fusion.mine_ref), channel_id=1, source_target_pairs={{0,4},{4,0},{8,12},{12,8},{16,20},{20,16},{24,28},{28,24},{1,5},{5... | collective-permute-start | bytes 589832 | tf_op jit(solution)/shard_map/ppermute | solution.py:185
  12.7 14.4 %collective-permute-start.6 = (bf16[3,48,2048]{2,1,0:T(8,128)(2,1)S(1)}, bf16[3,48,2048]{2,1,0:T(8,128)(2,1)S(1)}, u32[]{:S(2)}, u32[]{:S(2)}) collective-permute-start(bf16[3,48,2048]{2,1,0:T(8,128)(2,1)S(1)} %get-tuple-element.44), channel_id=1, source_target_pairs={{12,0},{28,16},{13,1},{29,17},{14,2},{30,18},{15,3},{31,19}} | collective-permute-start | bytes 1769480 | tf_op jit(solution)/shard_map/ppermute | solution.py:189
  15.0 18.6 %copy-start.7 = (s32[128,8]{0,1:T(8,128)S(1)}, s32[128,8]{0,1:T(8,128)}, u32[]{:S(2)}) copy-start(s32[128,8]{0,1:T(8,128)} %param.8) | copy-start | bytes 12292
  15.0 19.3 %copy-start.12 = (f32[128,8]{0,1:T(8,128)S(1)}, f32[128,8]{0,1:T(8,128)}, u32[]{:S(2)}) copy-start(f32[128,8]{0,1:T(8,128)} %param.9) | copy-start | bytes 12292
  15.1 1.5 %collective-permute-start.3 = (bf16[96,1024]{1,0:T(8,128)(2,1)S(1)}, bf16[96,1024]{1,0:T(8,128)(2,1)S(1)}, u32[]{:S(2)}, u32[]{:S(2)}) collective-permute-start(bf16[96,1024]{1,0:T(8,128)(2,1)S(1)} %get-tuple-element.41), channel_id=1, source_target_pairs={{0,4},{4,0},{8,12},{12,8},{16,20},{20,16},{24,28},{28,24},{1,5},{5... | collective-permute-start | bytes 589832 | tf_op jit(solution)/shard_map/ppermute | solution.py:185
  16.6 10.5 %collective-permute-start.5 = (bf16[48,1024]{1,0:T(8,128)(2,1)S(1)}, bf16[48,1024]{1,0:T(8,128)(2,1)S(1)}, u32[]{:S(2)}, u32[]{:S(2)}) collective-permute-start(bf16[48,1024]{1,0:T(8,128)(2,1)S(1)} %slice.25), channel_id=1, source_target_pairs={{0,8},{4,12},{8,0},{12,4},{16,24},{20,28},{24,16},{28,20},{1,9},{5... | collective-permute-start | bytes 294920 | tf_op jit(solution)/shard_map/ppermute | solution.py:185
  19.0 16.1 %collective-permute-start.9 = (bf16[3,48,2048]{2,1,0:T(8,128)(2,1)}, bf16[3,48,2048]{2,1,0:T(8,128)(2,1)S(1)}, u32[]{:S(2)}, u32[]{:S(2)}) collective-permute-start(bf16[3,48,2048]{2,1,0:T(8,128)(2,1)} %get-tuple-element.48), channel_id=1, source_target_pairs={{12,0},{28,16},{13,1},{29,17},{14,2},{30,18},{15,3},{31,19}} | collective-permute-start | bytes 1769480 | tf_op jit(solution)/shard_map/ppermute | solution.py:189
  20.3 14.8 %collective-permute-start.8 = (bf16[3,48,2048]{2,1,0:T(8,128)(2,1)S(1)}, bf16[3,48,2048]{2,1,0:T(8,128)(2,1)S(1)}, u32[]{:S(2)}, u32[]{:S(2)}) collective-permute-start(bf16[3,48,2048]{2,1,0:T(8,128)(2,1)S(1)} %collective-permute-done.4.shared_ref), channel_id=1, source_target_pairs={{4,5},{20,21},{5,4},{21,20},{6,7},{22,23},{7,6},{23,22}} | collective-permute-start | bytes 1769480 | tf_op jit(solution)/shard_map/ppermute | solution.py:197
  27.8 4.5 %collective-permute-start.7 = (bf16[24,1024]{1,0:T(8,128)(2,1)S(1)}, bf16[24,1024]{1,0:T(8,128)(2,1)S(1)}, u32[]{:S(2)}, u32[]{:S(2)}) collective-permute-start(bf16[24,1024]{1,0:T(8,128)(2,1)S(1)} %get-tuple-element.56), channel_id=1, source_target_pairs={{0,16},{4,20},{8,24},{12,28},{16,0},{20,4},{24,8},{28,12},{1,17},{... | collective-permute-start | bytes 147464 | tf_op jit(solution)/shard_map/ppermute | solution.py:185
  32.3 0.6 %copy-start.9 = (bf16[24,1024]{1,0:T(8,128)(2,1)}, bf16[24,1024]{1,0:T(8,128)(2,1)S(1)}, u32[]{:S(2)}) copy-start(bf16[24,1024]{1,0:T(8,128)(2,1)S(1)} %collective-permute-done.7.refs_1_) | copy-start | bytes 147460
  32.9 7.2 %collective-permute-start.10 = (bf16[3,96,2048]{2,1,0:T(8,128)(2,1)}, bf16[3,96,2048]{2,1,0:T(8,128)(2,1)S(1)}, u32[]{:S(2)}, u32[]{:S(2)}) collective-permute-start(bf16[3,96,2048]{2,1,0:T(8,128)(2,1)} %get-tuple-element.55), channel_id=1, source_target_pairs={{12,8},{28,24},{13,9},{29,25},{14,10},{30,26},{15,11},{31,27}} | collective-permute-start | bytes 3538952 | tf_op jit(solution)/shard_map/ppermute | solution.py:189
  35.1 0.8 %copy-start.3 = (s32[128,8]{1,0:T(8,128)S(1)}, s32[128,8]{1,0:T(8,128)}, u32[]{:S(2)}) copy-start(s32[128,8]{1,0:T(8,128)} %copy.9.ids_ref) | copy-start | bytes 12292
  35.9 0.8 %copy-start.4 = (f32[128,8]{1,0:T(8,128)S(1)}, f32[128,8]{1,0:T(8,128)}, u32[]{:S(2)}) copy-start(f32[128,8]{1,0:T(8,128)} %copy.10.weight_ref) | copy-start | bytes 12292
  36.8 0.8 %copy-start.5 = (bf16[24,1024]{1,0:T(8,128)(2,1)S(1)}, bf16[24,1024]{1,0:T(8,128)(2,1)}, u32[]{:S(2)}) copy-start(bf16[24,1024]{1,0:T(8,128)(2,1)} %get-tuple-element.49.refs_0_) | copy-start | bytes 147460
  37.6 0.8 %copy-start.10 = (bf16[24,1024]{1,0:T(8,128)(2,1)S(1)}, bf16[24,1024]{1,0:T(8,128)(2,1)}, u32[]{:S(2)}) copy-start(bf16[24,1024]{1,0:T(8,128)(2,1)} %copy-done.9) | copy-start | bytes 147460

commit v9 on v8

--- a/solution.py
+++ b/solution.py
@@ -13,7 +13,7 @@
 BF16 = jnp.bfloat16
 F32 = jnp.float32
 VMEM = pl.BlockSpec(memory_space=pltpu.VMEM)
-HBM = pl.BlockSpec(memory_space=pl.ANY)
+HBM = pl.BlockSpec(memory_space=pltpu.HBM)
 
 
 def params(megabytes=16):
@@ -40,11 +40,25 @@
     return jnp.where(member > 0, rank - 1.0, -PACK).astype(jnp.int32)
 
 
-def dispatch_kernel(experts, ids_ref, tok_ref, *out_refs):
+def dispatch_kernel(experts, ids_hbm, tok_hbm, *refs):
+    out_refs, (ids_ref, tok_ref, sems) = refs[:experts], refs[experts:]
+    tok, half = tok_ref.shape[0], tok_ref.shape[1] // 2
+    copies = [pltpu.make_async_copy(ids_hbm, ids_ref, sems.at[0])]
+    for side in range(2):
+        columns = pl.ds(side * half, half)
+        copies.append(
+            pltpu.make_async_copy(
+                tok_hbm.at[:, columns], tok_ref.at[:, columns], sems.at[side + 1]
+            )
+        )
+    for copy in copies:
+        copy.start()
     group = lax.axis_index("expert") // GROUP
+    copies[0].wait()
     place = token_places(ids_ref[...], group, experts)
-    tok, half = tok_ref.shape[0], tok_ref.shape[1] // 2
     slot = lax.broadcasted_iota(jnp.int32, (PACK, tok), 0)
+    copies[1].wait()
+    copies[2].wait()
     for j, ref in enumerate(out_refs):
         spot = place[j : j + 1, :]
         left = jnp.where(jnp.logical_and(slot == spot, spot >= 0), 1.0, 0.0).astype(BF16)
@@ -62,14 +76,14 @@
     @pl.when(device % GROUP == GROUP - 1)
     def _():
         plans = []
-        for survivor, first, count in wanted:
+        for survivor, count, first in wanted:
             plan = plan_ref[survivor, pl.ds(device // GROUP, 1), :]
             if first is None:
                 plan = jnp.where(even, plan[:, :count], plan[:, count : 2 * count])
             else:
                 plan = plan[:, first : first + count]
             plans.append(plan)
-        total = sum(count for _, _, count in wanted)
+        total = sum(count for _, count, _ in wanted)
         number = lax.broadcasted_iota(jnp.int32, (rows, total), 0)
         pick = jnp.where(number == jnp.concatenate(plans, axis=1), 1.0, 0.0).astype(BF16)
         for m, held_ref in enumerate((gate_ref, up_ref, down_ref)):
@@ -77,15 +91,15 @@
                 pick, held_ref[...], (((0,), (0,)), ((), ())), preferred_element_type=F32
             ).astype(BF16)
             start = 0
-            for (_, _, count), ref in zip(wanted, out_refs):
+            for (_, count, _), ref in zip(wanted, out_refs):
                 ref[m] = found[start : start + count]
                 start += count
 
 
-def merge_kernel(shared_ref, swapped_ref, first_ref, second_ref, near_ref, out_ref, sems):
+def merge_kernel(*refs):
+    shared_refs, swapped_refs, (straight_ref, near_ref, out_ref, sems) = refs[:2], refs[2:4], refs[4:]
     position = lax.axis_index("expert") % GROUP
     parity = lax.axis_index("replica") % 2
-    half = shared_ref.shape[1]
 
     def move(pieces):
         copies = []
@@ -100,15 +114,17 @@
         for copy in copies:
             copy.wait()
 
-    for even in range(2):
-
-        @pl.when(jnp.logical_and(position == 1, parity == even))
-        def _():
-            move([(shared_ref, half * even), (swapped_ref, half * (1 - even))])
-
-    @pl.when(jnp.logical_or(position == 0, position == 3))
-    def _():
-        move([(first_ref, 0), (second_ref, first_ref.shape[1])])
+    for p in range(2):
+        part = shared_refs[p].shape[1]
+        for even in range(2):
+            mine = position == 1 if p == 1 else jnp.logical_or(position == 0, position == 3)
+
+            @pl.when(jnp.logical_and(mine, parity == even))
+            def _():
+                pieces = [(shared_refs[p], part * even), (swapped_refs[p], part * (1 - even))]
+                if p == 0:
+                    pieces.append((straight_ref, 2 * part))
+                move(pieces)
 
     @pl.when(position == 2)
     def _():
@@ -142,23 +158,24 @@
     piece_refs, out_ref = refs[:-1], refs[-1]
     ids = ids_ref[...]
     group = lax.axis_index("expert") // GROUP
-    tok = ids.shape[0]
     half = out_ref.shape[1] // 2
-    row = lax.broadcasted_iota(jnp.int32, (tok, tok), 0)
-    col = lax.broadcasted_iota(jnp.int32, (tok, tok), 1)
-    upto = jnp.where(col <= row, 1.0, 0.0).astype(BF16)
-    slot = lax.broadcasted_iota(jnp.int32, (tok, PACK), 1)
+    place = token_places(ids, group, experts)
+    weights = []
+    for j in range(experts):
+        named = ids == lax.rem(group + j, experts)
+        weights.append(jnp.sum(jnp.where(named, weight_ref[...], 0.0), axis=0, keepdims=True))
+    weights = jnp.concatenate(weights, axis=0).T
+    slot = lax.broadcasted_iota(jnp.int32, (PACK, ids.shape[1]), 0)
+    numbers = (((0,), (0,)), ((), ()))
     mixed = [None, None]
     for j in range(experts):
-        named = ids == lax.rem(group + j, experts)
-        member = jnp.sum(jnp.where(named, 1.0, 0.0), axis=1, keepdims=True)
-        weight = jnp.sum(jnp.where(named, weight_ref[...], 0.0), axis=1, keepdims=True)
-        rank = jnp.dot(upto, member.astype(BF16), preferred_element_type=F32)
-        place = jnp.where(member > 0, rank - 1.0, -PACK).astype(jnp.int32)
+        spot = place[j : j + 1, :]
         for side in range(2):
-            chosen = jnp.where(slot == place + side * CAP, 1.0, 0.0).astype(BF16)
-            found = jnp.dot(chosen, piece_refs[j][...], preferred_element_type=F32)
-            term = weight * found
+            chosen = jnp.where(slot == spot + side * CAP, 1.0, 0.0).astype(BF16)
+            found = lax.dot_general(
+                chosen, piece_refs[j][...], numbers, preferred_element_type=F32
+            )
+            term = weights[:, j : j + 1] * found
             mixed[side] = term if mixed[side] is None else mixed[side] + term
     out_ref[:, :half] = mixed[0].astype(BF16)
     out_ref[:, half:] = mixed[1].astype(BF16)
@@ -173,6 +190,8 @@
     plan = jnp.transpose(move_plan, (1, 0, 2))
     weights = (old_gate, old_up, old_down)
     half = most // 2
+    part = most // 3
+    rest = most - 2 * part
 
     def shape(*dims, dtype=BF16):
         return jax.ShapeDtypeStruct(dims, dtype)
@@ -188,18 +207,18 @@
         route = [(GROUP * e + GROUP - 1, GROUP * e + survivor) for e in range(experts)]
         return lax.ppermute(block, "expert", route)
 
-    def swap(block):
+    def swap(block, survivor):
         route = []
         for r in range(replicas):
-            for i in range(devices):
-                if i % GROUP == 1:
-                    route.append((i * replicas + r, i * replicas + (r ^ 1)))
+            for e in range(experts):
+                i = GROUP * e + survivor
+                route.append((i * replicas + r, i * replicas + (r ^ 1)))
         return lax.ppermute(block, ("expert", "replica"), route)
 
     def select(wanted, held):
         return pl.pallas_call(
             functools.partial(select_kernel, wanted),
-            out_shape=[shape(3, count, width) for _, _, count in wanted],
+            out_shape=[shape(3, count, width) for _, count, _ in wanted],
             in_specs=[VMEM] * 4,
             out_specs=[VMEM] * len(wanted),
             compiler_params=params(),
@@ -210,24 +229,29 @@
     parcels = pl.pallas_call(
         functools.partial(dispatch_kernel, experts),
         out_shape=[shape(PACK, width // 2)] * experts,
-        in_specs=[VMEM, VMEM],
+        in_specs=[HBM, HBM],
         out_specs=[VMEM] * experts,
+        scratch_shapes=[
+            pltpu.VMEM(expert_ids.shape[::-1], jnp.int32),
+            pltpu.VMEM(tokens.shape, BF16),
+            pltpu.SemaphoreType.DMA((3,)),
+        ],
         compiler_params=params(),
         cost_estimate=cost(2),
         name="dispatch",
     )(expert_ids.T, tokens)
 
-    held, across = lax.optimization_barrier((weights, parcels[1]))
-    parcels = [parcels[0], across] + list(parcels[2:])
     across = [send(parcels[j], j, 0) for j in range(1, experts)]
     here = jnp.concatenate([parcels[0]] + across, axis=0)
-    chosen = select([(1, None, half), (0, 0, half), (0, half, most - half), (2, 0, most)], held)
-    here, chosen = lax.optimization_barrier((here, chosen))
-    mine = jnp.concatenate([here, send(here, 0, 2)], axis=0)
+    held, _ = lax.optimization_barrier((weights, here))
+    wanted = [(0, part, None), (1, half, None), (0, rest, 2 * part), (2, most, 0)]
+    chosen = select(wanted, held)
+    beside = send(here, 0, 2)
+    mine = jnp.concatenate([here, beside], axis=0)
     other = send(mine, 0, 1)
 
-    shared = migrate(chosen[0], 1)
-    first = migrate(chosen[1], 0)
+    shared = [migrate(chosen[p], p) for p in range(2)]
+    near = migrate(chosen[3], 2)
 
     total = mine.shape[0]
     step = min(total, 4 * PACK)
@@ -243,39 +267,37 @@
         cost_estimate=cost(0),
         name="expert",
     )(mine, other, *weights)
-    taken, shared = lax.optimization_barrier((send(give, 0, 1), shared))
+    taken, shared[1] = lax.optimization_barrier((send(give, 0, 1), shared[1]))
     summed = keep + taken.astype(F32)
     far = send(summed[total // 2 :].astype(BF16), 0, 2)
 
-    far, first = lax.optimization_barrier((far, first))
-    swapped = swap(shared)
-    second = migrate(lax.optimization_barrier((chosen[2], summed))[0], 0)
+    far, shared[0] = lax.optimization_barrier((far, shared[0]))
+    swapped = [swap(shared[p], p) for p in range(2)]
+    last, _ = lax.optimization_barrier((chosen[2], summed))
+    straight = migrate(last, 0)
 
     summed = (summed[: total // 2] + far.astype(F32)).astype(BF16)
     pieces = [summed[j * PACK : (j + 1) * PACK] for j in range(experts)]
     back = [pieces[0]] + [send(pieces[j], -j, 0) for j in range(1, experts)]
-    near = migrate(lax.optimization_barrier((chosen[3], back))[0], 2)
-    back, swapped, second = lax.optimization_barrier((back, swapped, second))
-
     mixed = pl.pallas_call(
         functools.partial(combine_kernel, experts),
         out_shape=shape(tokens.shape[0], width),
         in_specs=[VMEM, VMEM] + [VMEM] * len(back),
         out_specs=VMEM,
         compiler_params=params(14 + experts),
-        cost_estimate=cost(12),
+        cost_estimate=cost(2),
         name="combine",
-    )(expert_ids, combine, *back)
+    )(expert_ids.T, combine.T, *back)
 
     arrived = pl.pallas_call(
         merge_kernel,
         out_shape=shape(3, most, width),
-        in_specs=[HBM] * 5,
+        in_specs=[HBM] * 6,
         out_specs=HBM,
-        scratch_shapes=[pltpu.SemaphoreType.DMA((6,))],
+        scratch_shapes=[pltpu.SemaphoreType.DMA((9,))],
         compiler_params=params(),
         name="merge",
-    )(shared, swapped, first, second, near)
+    )(*shared, *swapped, straight, near)
     return mixed, arrived
 
 

time: 41.6 us -> 38.1 us (0.916)
  local copies, waits for them, and re-layouts: 7.74 us -> 1.79 us
  starting transfers between devices: 13.8 us -> 17.8 us
  Pallas kernels: 5.36 us -> 4 us
    unnamed x29 -> x17, local copies, waits for them, and re-layouts: 7.1 us -> 1.76 us
    ppermute x1 -> x2, starting transfers between devices: 0.7 us -> 4.88 us  [swap(): return lax.ppermute(block, ('expert', 'replica'), route)]
    ppermute x4, waiting for transfers between devices: 6.11 us -> 4.9 us  [migrate(): return lax.ppermute(block, 'expert', route)]
    pallas_call x1, Pallas kernels: 1.23 us -> 0.02 us  [select(): pl.pallas_call(functools.partial(select_kernel, wanted), out_shape=[shape...]
    ppermute x6, waiting for transfers between devices: 7.31 us -> 7.94 us  [send(): return lax.ppermute(block, 'expert', route)]
    slice x1, local copies, waits for them, and re-layouts: 0.62 us -> 0.01 us  [on_device(): pieces = [summed[j * PACK:(j + 1) * PACK] for j in range(experts)]]
    ppermute x1 -> x2, waiting for transfers between devices: 0.01 us -> 0.5 us  [swap(): return lax.ppermute(block, ('expert', 'replica'), route)]
  transfers between devices with their start and end apart: 11 -> 12, of which waited for: 6 -> 6; matrix products, arithmetic and copies ran while one was open for 5% -> 0% of each run, Pallas kernels for 9% -> 6%
where the time goes in v9:
time: 38.1 us; the launch traced here: 37.8 us
  starting transfers between devices  17.8 us (47%)
  waiting for transfers between devices  13.3 us (35%)
  Pallas kernels  4 us (10%)
  local copies, waits for them, and re-layouts  1.79 us (5%)
  between operations  0.81 us (2%)
    ppermute x6, starting transfers between devices, send(): return lax.ppermute(block, 'expert', route)  8.96 us
    ppermute x6, waiting for transfers between devices, send(): return lax.ppermute(block, 'expert', route)  7.94 us
    ppermute x4, waiting for transfers between devices, migrate(): return lax.ppermute(block, 'expert', route)  4.9 us
    ppermute x2, starting transfers between devices, swap(): return lax.ppermute(block, ('expert', 'replica'), route)  4.88 us
    ppermute x4, starting transfers between devices, migrate(): return lax.ppermute(block, 'expert', route)  3.99 us
    unnamed x17, local copies, waits for them, and re-layouts  1.76 us
    pallas_call x1, Pallas kernels, on_device(): pl.pallas_call(functools.partial(combine_kernel, experts), out_shape=shap...  1.45 us
    pallas_call x1, Pallas kernels, on_device(): pl.pallas_call(merge_kernel, out_shape=shape(3, most, width), in_specs=[H...  1.08 us
  transfers between devices with their start and end apart: 12, of which 6 were waited for; matrix products, arithmetic and copies ran while one was open for 0% of the time, Pallas kernels for 6%

profile of v9, /device:TPU:0, one launch (start us, length us, event | category | flops | bytes accessed | tf_op | source)
XLA Modules:
  0.0 37.8 jit_solution(11072833785095643210)
XLA Ops:
  0.6 1.0 %copy-done.3 = bf16[128,2048]{1,0:T(8,128)(2,1)S(1)} copy-done((bf16[128,2048]{1,0:T(8,128)(2,1)S(1)}, bf16[128,2048]{1,0:T(8,128)(2,1)}, u32[]{:S(2)}) %copy-start.3) | copy-done | bytes 524312
  1.7 0.7 %copy-done.4 = s32[128,8]{0,1:T(8,128)S(1)} copy-done((s32[128,8]{0,1:T(8,128)S(1)}, s32[128,8]{0,1:T(8,128)}, u32[]{:S(2)}) %copy-start.4) | copy-done | bytes 4120
  2.4 0.5 %dispatch.1 = (bf16[24,1024]{1,0:T(8,128)(2,1)S(1)}, bf16[24,1024]{1,0:T(8,128)(2,1)S(1)}) custom-call(s32[8,128]{1,0:T(8,128)S(1)} %bitcast.3, bf16[128,2048]{1,0:T(8,128)(2,1)S(1)} %copy-done.3), custom_call_target="tpu_custom_call" | custom-call | flops 2000000000 | bytes 10000 | tf_op jit(solution)/shard_map/dispatch/pallas_call | solution.py:229
  2.9 3.0 %collective-permute-start = (bf16[24,1024]{1,0:T(8,128)(2,1)S(1)}, bf16[24,1024]{1,0:T(8,128)(2,1)S(1)}, u32[]{:S(2)}, u32[]{:S(2)}) collective-permute-start(bf16[24,1024]{1,0:T(8,128)(2,1)S(1)} %get-tuple-element.19), channel_id=1, source_target_pairs={{0,16},{4,20},{8,24},{12,28},{16,0},{20,4},{24,8},{28,12},{1,17},{... | collective-permute-start | bytes 147464 | tf_op jit(solution)/shard_map/ppermute | solution.py:204
  5.9 2.1 %collective-permute-done = bf16[24,1024]{1,0:T(8,128)(2,1)S(1)} collective-permute-done((bf16[24,1024]{1,0:T(8,128)(2,1)S(1)}, bf16[24,1024]{1,0:T(8,128)(2,1)S(1)}, u32[]{:S(2)}, u32[]{:S(2)}) %collective-permute-start) | collective-permute-done | bytes 49184 | tf_op jit(solution)/shard_map/ppermute | solution.py:204
  8.0 2.1 %collective-permute-start.1 = (bf16[48,1024]{1,0:T(8,128)(2,1)S(1)}, bf16[48,1024]{1,0:T(8,128)(2,1)S(1)}, u32[]{:S(2)}, u32[]{:S(2)}) collective-permute-start(bf16[48,1024]{1,0:T(8,128)(2,1)S(1)} %get-tuple-element.36), channel_id=1, source_target_pairs={{0,8},{4,12},{8,0},{12,4},{16,24},{20,28},{24,16},{28,20},{1,9},{5... | collective-permute-start | bytes 294920 | tf_op jit(solution)/shard_map/ppermute | solution.py:204
  10.1 0.7 %collective-permute-start.4 = (bf16[3,48,2048]{2,1,0:T(8,128)(2,1)S(1)}, bf16[3,48,2048]{2,1,0:T(8,128)(2,1)S(1)}, u32[]{:S(2)}, u32[]{:S(2)}) collective-permute-start(bf16[3,48,2048]{2,1,0:T(8,128)(2,1)S(1)} %get-tuple-element.25), channel_id=1, source_target_pairs={{12,4},{28,20},{13,5},{29,21},{14,6},{30,22},{15,7},{31,23}} | collective-permute-start | bytes 1769480 | tf_op jit(solution)/shard_map/ppermute | solution.py:208
  10.8 1.9 %collective-permute-done.1 = bf16[48,1024]{1,0:T(8,128)(2,1)S(1)} collective-permute-done((bf16[48,1024]{1,0:T(8,128)(2,1)S(1)}, bf16[48,1024]{1,0:T(8,128)(2,1)S(1)}, u32[]{:S(2)}, u32[]{:S(2)}) %collective-permute-start.1) | collective-permute-done | bytes 98336 | tf_op jit(solution)/shard_map/ppermute | solution.py:204
  12.7 0.1 collective-permute-start.2
  12.8 1.4 %collective-permute-done.2.other_ref = bf16[96,1024]{1,0:T(8,128)(2,1)S(1)} collective-permute-done((bf16[96,1024]{1,0:T(8,128)(2,1)S(1)}, bf16[96,1024]{1,0:T(8,128)(2,1)S(1)}, u32[]{:S(2)}, u32[]{:S(2)}) %collective-permute-start.2) | collective-permute-done | bytes 196640 | tf_op jit(solution)/shard_map/ppermute | solution.py:204
  14.2 0.9 %expert.1 = (f32[96,1024]{1,0:T(8,128)S(1)}, bf16[96,1024]{1,0:T(8,128)(2,1)S(1)}) custom-call(bf16[96,1024]{1,0:T(8,128)(2,1)S(1)} %constant_dynamic-update-slice_fusion.2.mine_ref, bf16[96,1024]{1,0:T(8,128)(2,1)S(1)} %collective-permute-done.2.other_ref, bf16[192,2048]{1,0:T(8,128)(2,1)S(1)} %copy-done, bf16[192,2048]{1,0:T(8,128)(2,1)S(1)} %copy-done.1, ...), custom_call_target="tpu_custom_call" | custom-call | bytes 10000 | tf_op jit(solution)/shard_map/expert/pallas_call | solution.py:260
  15.1 0.0 copy-start.5
  15.2 0.0 copy-start.6
  15.2 0.2 collective-permute-start.3
  15.4 0.7 %collective-permute-start.11 = (bf16[3,96,2048]{2,1,0:T(8,128)(2,1)S(1)}, bf16[3,96,2048]{2,1,0:T(8,128)(2,1)S(1)}, u32[]{:S(2)}, u32[]{:S(2)}) collective-permute-start(bf16[3,96,2048]{2,1,0:T(8,128)(2,1)S(1)} %get-tuple-element.33), channel_id=1, source_target_pairs={{12,8},{28,24},{13,9},{29,25},{14,10},{30,26},{15,11},{31,27}} | collective-permute-start | bytes 3538952 | tf_op jit(solution)/shard_map/ppermute | solution.py:208
  16.1 1.3 %collective-permute-start.6 = (bf16[3,32,2048]{2,1,0:T(8,128)(2,1)S(1)}, bf16[3,32,2048]{2,1,0:T(8,128)(2,1)S(1)}, u32[]{:S(2)}, u32[]{:S(2)}) collective-permute-start(bf16[3,32,2048]{2,1,0:T(8,128)(2,1)S(1)} %get-tuple-element.27), channel_id=1, source_target_pairs={{12,0},{28,16},{13,1},{29,17},{14,2},{30,18},{15,3},{31,19}} | collective-permute-start | bytes 1179656 | tf_op jit(solution)/shard_map/ppermute | solution.py:208
  17.4 0.0 collective-permute-done.3
  17.4 0.0 collective-permute-done.4.refs_1_
  17.5 2.0 %collective-permute-start.5 = (bf16[48,1024]{1,0:T(8,128)(2,1)S(1)}, bf16[48,1024]{1,0:T(8,128)(2,1)S(1)}, u32[]{:S(2)}, u32[]{:S(2)}) collective-permute-start(bf16[48,1024]{1,0:T(8,128)(2,1)S(1)} %slice.25), channel_id=1, source_target_pairs={{0,8},{4,12},{8,0},{12,4},{16,24},{20,28},{24,16},{28,20},{1,9},{5... | collective-permute-start | bytes 294920 | tf_op jit(solution)/shard_map/ppermute | solution.py:204
  19.5 1.3 %collective-permute-start.10 = (bf16[3,32,2048]{2,1,0:T(8,128)(2,1)S(1)}, bf16[3,32,2048]{2,1,0:T(8,128)(2,1)S(1)}, u32[]{:S(2)}, u32[]{:S(2)}) collective-permute-start(bf16[3,32,2048]{2,1,0:T(8,128)(2,1)S(1)} %get-tuple-element.32), channel_id=1, source_target_pairs={{12,0},{28,16},{13,1},{29,17},{14,2},{30,18},{15,3},{31,19}} | collective-permute-start | bytes 1179656 | tf_op jit(solution)/shard_map/ppermute | solution.py:208
  20.8 0.7 %collective-permute-start.9 = (bf16[3,48,2048]{2,1,0:T(8,128)(2,1)S(1)}, bf16[3,48,2048]{2,1,0:T(8,128)(2,1)S(1)}, u32[]{:S(2)}, u32[]{:S(2)}) collective-permute-start(bf16[3,48,2048]{2,1,0:T(8,128)(2,1)S(1)} %collective-permute-done.4.refs_1_), channel_id=1, source_target_pairs={{4,5},{20,21},{5,4},{21,20},{6,7},{22,23},{7,6},{23,22}} | collective-permute-start | bytes 1769480 | tf_op jit(solution)/shard_map/ppermute | solution.py:216
  21.5 4.9 %collective-permute-done.6.refs_0_ = bf16[3,32,2048]{2,1,0:T(8,128)(2,1)S(1)} collective-permute-done((bf16[3,32,2048]{2,1,0:T(8,128)(2,1)S(1)}, bf16[3,32,2048]{2,1,0:T(8,128)(2,1)S(1)}, u32[]{:S(2)}, u32[]{:S(2)}) %collective-permute-start.6) | collective-permute-done | bytes 393248 | tf_op jit(solution)/shard_map/ppermute | solution.py:208
  26.4 0.0 collective-permute-done.5
  26.4 4.2 %collective-permute-start.8 = (bf16[3,32,2048]{2,1,0:T(8,128)(2,1)S(1)}, bf16[3,32,2048]{2,1,0:T(8,128)(2,1)S(1)}, u32[]{:S(2)}, u32[]{:S(2)}) collective-permute-start(bf16[3,32,2048]{2,1,0:T(8,128)(2,1)S(1)} %collective-permute-done.6.refs_0_), channel_id=1, source_target_pairs={{0,1},{16,17},{1,0},{17,16},{2,3},{18,19},{3,2},{19,18}} | collective-permute-start | bytes 1179656 | tf_op jit(solution)/shard_map/ppermute | solution.py:216
  30.6 1.6 %collective-permute-start.7 = (bf16[24,1024]{1,0:T(8,128)(2,1)S(1)}, bf16[24,1024]{1,0:T(8,128)(2,1)S(1)}, u32[]{:S(2)}, u32[]{:S(2)}) collective-permute-start(bf16[24,1024]{1,0:T(8,128)(2,1)S(1)} %get-tuple-element.34), channel_id=1, source_target_pairs={{0,16},{4,20},{8,24},{12,28},{16,0},{20,4},{24,8},{28,12},{1,17},{... | collective-permute-start | bytes 147464 | tf_op jit(solution)/shard_map/ppermute | solution.py:204
  32.2 2.6 %collective-permute-done.7.refs_1_ = bf16[24,1024]{1,0:T(8,128)(2,1)S(1)} collective-permute-done((bf16[24,1024]{1,0:T(8,128)(2,1)S(1)}, bf16[24,1024]{1,0:T(8,128)(2,1)S(1)}, u32[]{:S(2)}, u32[]{:S(2)}) %collective-permute-start.7) | collective-permute-done | bytes 49184 | tf_op jit(solution)/shard_map/ppermute | solution.py:204
  34.8 1.5 %combine.1 = bf16[128,2048]{1,0:T(8,128)(2,1)} custom-call(s32[8,128]{1,0:T(8,128)S(1)} %bitcast.4, f32[8,128]{1,0:T(8,128)S(1)} %bitcast.5, bf16[24,1024]{1,0:T(8,128)(2,1)S(1)} %get-tuple-element.35.refs_0_, bf16[24,1024]{1,0:T(8,128)(2,1)S(1)} %collective-permute-done.7.refs_1_), custom_call_target="tpu_custom_call" | custom-call | flops 2000000000 | bytes 10000 | tf_op jit(solution)/shard_map/combine/pallas_call | solution.py:282
  36.2 0.0 collective-permute-done.10.refs_4_
  36.2 0.5 %collective-permute-done.8.refs_2_ = bf16[3,32,2048]{2,1,0:T(8,128)(2,1)S(1)} collective-permute-done((bf16[3,32,2048]{2,1,0:T(8,128)(2,1)S(1)}, bf16[3,32,2048]{2,1,0:T(8,128)(2,1)S(1)}, u32[]{:S(2)}, u32[]{:S(2)}) %collective-permute-start.8) | collective-permute-done | bytes 393248 | tf_op jit(solution)/shard_map/ppermute | solution.py:216
  36.8 0.0 collective-permute-done.9.refs_3_
  36.8 0.0 collective-permute-done.11.refs_5_
  36.8 1.1 %merge.1 = bf16[3,96,2048]{2,1,0:T(8,128)(2,1)} custom-call(bf16[3,32,2048]{2,1,0:T(8,128)(2,1)S(1)} %collective-permute-done.6.refs_0_, bf16[3,48,2048]{2,1,0:T(8,128)(2,1)S(1)} %collective-permute-done.4.refs_1_, bf16[3,32,2048]{2,1,0:T(8,128)(2,1)S(1)} %collective-permute-done.8.refs_2_, bf16[3,48,2048]{2,1,0:T(8,128)(2,1)S(1)} %collective-permute-done.9.refs_3_, ...), custom_call_target="tpu_custom_call" | custom-call | tf_op jit(solution)/shard_map/merge/pallas_call | solution.py:292
  (20 shorter events, 0.2 us)
Async XLA Ops:
  0.6 1.0 %copy-start.3 = (bf16[128,2048]{1,0:T(8,128)(2,1)S(1)}, bf16[128,2048]{1,0:T(8,128)(2,1)}, u32[]{:S(2)}) copy-start(bf16[128,2048]{1,0:T(8,128)(2,1)} %tok_hbm.1) | copy-start | bytes 1572868
  1.7 0.7 %copy-start.4 = (s32[128,8]{0,1:T(8,128)S(1)}, s32[128,8]{0,1:T(8,128)}, u32[]{:S(2)}) copy-start(s32[128,8]{0,1:T(8,128)} %param.8) | copy-start | bytes 12292
  2.4 7.7 %copy-start = (bf16[192,2048]{1,0:T(8,128)(2,1)S(1)}, bf16[192,2048]{1,0:T(8,128)(2,1)}, u32[]{:S(2)}) copy-start(bf16[192,2048]{1,0:T(8,128)(2,1)} %gate_ref.2) | copy-start | bytes 2359300
  2.4 7.7 %copy-start.1 = (bf16[192,2048]{1,0:T(8,128)(2,1)S(1)}, bf16[192,2048]{1,0:T(8,128)(2,1)}, u32[]{:S(2)}) copy-start(bf16[192,2048]{1,0:T(8,128)(2,1)} %up_ref.2) | copy-start | bytes 2359300
  2.4 7.7 %copy-start.2 = (bf16[192,2048]{1,0:T(8,128)(2,1)S(1)}, bf16[192,2048]{1,0:T(8,128)(2,1)}, u32[]{:S(2)}) copy-start(bf16[192,2048]{1,0:T(8,128)(2,1)} %down_ref.2) | copy-start | bytes 2359300
  2.4 7.7 %copy-start.7 = (s32[2,3,96]{2,0,1:T(2,128)S(1)}, s32[2,3,96]{2,0,1:T(2,128)}, u32[]{:S(2)}) copy-start(s32[2,3,96]{2,0,1:T(2,128)} %param.13) | copy-start | bytes 6916
  2.9 5.1 %collective-permute-start = (bf16[24,1024]{1,0:T(8,128)(2,1)S(1)}, bf16[24,1024]{1,0:T(8,128)(2,1)S(1)}, u32[]{:S(2)}, u32[]{:S(2)}) collective-permute-start(bf16[24,1024]{1,0:T(8,128)(2,1)S(1)} %get-tuple-element.19), channel_id=1, source_target_pairs={{0,16},{4,20},{8,24},{12,28},{16,0},{20,4},{24,8},{28,12},{1,17},{... | collective-permute-start | bytes 147464 | tf_op jit(solution)/shard_map/ppermute | solution.py:204
  8.0 4.7 %collective-permute-start.1 = (bf16[48,1024]{1,0:T(8,128)(2,1)S(1)}, bf16[48,1024]{1,0:T(8,128)(2,1)S(1)}, u32[]{:S(2)}, u32[]{:S(2)}) collective-permute-start(bf16[48,1024]{1,0:T(8,128)(2,1)S(1)} %get-tuple-element.36), channel_id=1, source_target_pairs={{0,8},{4,12},{8,0},{12,4},{16,24},{20,28},{24,16},{28,20},{1,9},{5... | collective-permute-start | bytes 294920 | tf_op jit(solution)/shard_map/ppermute | solution.py:204
  10.1 7.3 %collective-permute-start.4 = (bf16[3,48,2048]{2,1,0:T(8,128)(2,1)S(1)}, bf16[3,48,2048]{2,1,0:T(8,128)(2,1)S(1)}, u32[]{:S(2)}, u32[]{:S(2)}) collective-permute-start(bf16[3,48,2048]{2,1,0:T(8,128)(2,1)S(1)} %get-tuple-element.25), channel_id=1, source_target_pairs={{12,4},{28,20},{13,5},{29,21},{14,6},{30,22},{15,7},{31,23}} | collective-permute-start | bytes 1769480 | tf_op jit(solution)/shard_map/ppermute | solution.py:208
  12.7 1.5 %collective-permute-start.2 = (bf16[96,1024]{1,0:T(8,128)(2,1)S(1)}, bf16[96,1024]{1,0:T(8,128)(2,1)S(1)}, u32[]{:S(2)}, u32[]{:S(2)}) collective-permute-start(bf16[96,1024]{1,0:T(8,128)(2,1)S(1)} %constant_dynamic-update-slice_fusion.2.mine_ref), channel_id=1, source_target_pairs={{0,4},{4,0},{8,12},{12,8},{16,20},{20,16},{24,28},{28,24},{1,5},{5... | collective-permute-start | bytes 589832 | tf_op jit(solution)/shard_map/ppermute | solution.py:204
  15.1 19.6 %copy-start.5 = (s32[128,8]{0,1:T(8,128)S(1)}, s32[128,8]{0,1:T(8,128)}, u32[]{:S(2)}) copy-start(s32[128,8]{0,1:T(8,128)} %param.8) | copy-start | bytes 12292
  15.2 19.6 %copy-start.6 = (f32[128,8]{0,1:T(8,128)S(1)}, f32[128,8]{0,1:T(8,128)}, u32[]{:S(2)}) copy-start(f32[128,8]{0,1:T(8,128)} %param.9) | copy-start | bytes 12292
  15.2 2.2 %collective-permute-start.3 = (bf16[96,1024]{1,0:T(8,128)(2,1)S(1)}, bf16[96,1024]{1,0:T(8,128)(2,1)S(1)}, u32[]{:S(2)}, u32[]{:S(2)}) collective-permute-start(bf16[96,1024]{1,0:T(8,128)(2,1)S(1)} %get-tuple-element.21), channel_id=1, source_target_pairs={{0,4},{4,0},{8,12},{12,8},{16,20},{20,16},{24,28},{28,24},{1,5},{5... | collective-permute-start | bytes 589832 | tf_op jit(solution)/shard_map/ppermute | solution.py:204
  15.4 21.4 %collective-permute-start.11 = (bf16[3,96,2048]{2,1,0:T(8,128)(2,1)S(1)}, bf16[3,96,2048]{2,1,0:T(8,128)(2,1)S(1)}, u32[]{:S(2)}, u32[]{:S(2)}) collective-permute-start(bf16[3,96,2048]{2,1,0:T(8,128)(2,1)S(1)} %get-tuple-element.33), channel_id=1, source_target_pairs={{12,8},{28,24},{13,9},{29,25},{14,10},{30,26},{15,11},{31,27}} | collective-permute-start | bytes 3538952 | tf_op jit(solution)/shard_map/ppermute | solution.py:208
  16.1 10.3 %collective-permute-start.6 = (bf16[3,32,2048]{2,1,0:T(8,128)(2,1)S(1)}, bf16[3,32,2048]{2,1,0:T(8,128)(2,1)S(1)}, u32[]{:S(2)}, u32[]{:S(2)}) collective-permute-start(bf16[3,32,2048]{2,1,0:T(8,128)(2,1)S(1)} %get-tuple-element.27), channel_id=1, source_target_pairs={{12,0},{28,16},{13,1},{29,17},{14,2},{30,18},{15,3},{31,19}} | collective-permute-start | bytes 1179656 | tf_op jit(solution)/shard_map/ppermute | solution.py:208
  17.5 8.9 %collective-permute-start.5 = (bf16[48,1024]{1,0:T(8,128)(2,1)S(1)}, bf16[48,1024]{1,0:T(8,128)(2,1)S(1)}, u32[]{:S(2)}, u32[]{:S(2)}) collective-permute-start(bf16[48,1024]{1,0:T(8,128)(2,1)S(1)} %slice.25), channel_id=1, source_target_pairs={{0,8},{4,12},{8,0},{12,4},{16,24},{20,28},{24,16},{28,20},{1,9},{5... | collective-permute-start | bytes 294920 | tf_op jit(solution)/shard_map/ppermute | solution.py:204
  19.5 16.7 %collective-permute-start.10 = (bf16[3,32,2048]{2,1,0:T(8,128)(2,1)S(1)}, bf16[3,32,2048]{2,1,0:T(8,128)(2,1)S(1)}, u32[]{:S(2)}, u32[]{:S(2)}) collective-permute-start(bf16[3,32,2048]{2,1,0:T(8,128)(2,1)S(1)} %get-tuple-element.32), channel_id=1, source_target_pairs={{12,0},{28,16},{13,1},{29,17},{14,2},{30,18},{15,3},{31,19}} | collective-permute-start | bytes 1179656 | tf_op jit(solution)/shard_map/ppermute | solution.py:208
  20.8 16.0 %collective-permute-start.9 = (bf16[3,48,2048]{2,1,0:T(8,128)(2,1)S(1)}, bf16[3,48,2048]{2,1,0:T(8,128)(2,1)S(1)}, u32[]{:S(2)}, u32[]{:S(2)}) collective-permute-start(bf16[3,48,2048]{2,1,0:T(8,128)(2,1)S(1)} %collective-permute-done.4.refs_1_), channel_id=1, source_target_pairs={{4,5},{20,21},{5,4},{21,20},{6,7},{22,23},{7,6},{23,22}} | collective-permute-start | bytes 1769480 | tf_op jit(solution)/shard_map/ppermute | solution.py:216
  26.4 10.4 %collective-permute-start.8 = (bf16[3,32,2048]{2,1,0:T(8,128)(2,1)S(1)}, bf16[3,32,2048]{2,1,0:T(8,128)(2,1)S(1)}, u32[]{:S(2)}, u32[]{:S(2)}) collective-permute-start(bf16[3,32,2048]{2,1,0:T(8,128)(2,1)S(1)} %collective-permute-done.6.refs_0_), channel_id=1, source_target_pairs={{0,1},{16,17},{1,0},{17,16},{2,3},{18,19},{3,2},{19,18}} | collective-permute-start | bytes 1179656 | tf_op jit(solution)/shard_map/ppermute | solution.py:216
  30.6 4.2 %collective-permute-start.7 = (bf16[24,1024]{1,0:T(8,128)(2,1)S(1)}, bf16[24,1024]{1,0:T(8,128)(2,1)S(1)}, u32[]{:S(2)}, u32[]{:S(2)}) collective-permute-start(bf16[24,1024]{1,0:T(8,128)(2,1)S(1)} %get-tuple-element.34), channel_id=1, source_target_pairs={{0,16},{4,20},{8,24},{12,28},{16,0},{20,4},{24,8},{28,12},{1,17},{... | collective-permute-start | bytes 147464 | tf_op jit(solution)/shard_map/ppermute | solution.py:204

commit v10 on v9

--- a/solution.py
+++ b/solution.py
@@ -96,10 +96,10 @@
                 start += count
 
 
-def merge_kernel(*refs):
-    shared_refs, swapped_refs, (straight_ref, near_ref, out_ref, sems) = refs[:2], refs[2:4], refs[4:]
+def merge_kernel(shared_ref, swapped_ref, first_ref, second_ref, near_ref, out_ref, sems):
     position = lax.axis_index("expert") % GROUP
     parity = lax.axis_index("replica") % 2
+    half = shared_ref.shape[1]
 
     def move(pieces):
         copies = []
@@ -114,17 +114,15 @@
         for copy in copies:
             copy.wait()
 
-    for p in range(2):
-        part = shared_refs[p].shape[1]
-        for even in range(2):
-            mine = position == 1 if p == 1 else jnp.logical_or(position == 0, position == 3)
-
-            @pl.when(jnp.logical_and(mine, parity == even))
-            def _():
-                pieces = [(shared_refs[p], part * even), (swapped_refs[p], part * (1 - even))]
-                if p == 0:
-                    pieces.append((straight_ref, 2 * part))
-                move(pieces)
+    for even in range(2):
+
+        @pl.when(jnp.logical_and(position == 1, parity == even))
+        def _():
+            move([(shared_ref, half * even), (swapped_ref, half * (1 - even))])
+
+    @pl.when(jnp.logical_or(position == 0, position == 3))
+    def _():
+        move([(first_ref, 0), (second_ref, first_ref.shape[1])])
 
     @pl.when(position == 2)
     def _():
@@ -167,14 +165,16 @@
     weights = jnp.concatenate(weights, axis=0).T
     slot = lax.broadcasted_iota(jnp.int32, (PACK, ids.shape[1]), 0)
     numbers = (((0,), (0,)), ((), ()))
+    each = len(piece_refs) // experts
     mixed = [None, None]
     for j in range(experts):
         spot = place[j : j + 1, :]
         for side in range(2):
             chosen = jnp.where(slot == spot + side * CAP, 1.0, 0.0).astype(BF16)
-            found = lax.dot_general(
-                chosen, piece_refs[j][...], numbers, preferred_element_type=F32
-            )
+            found = None
+            for ref in piece_refs[j * each : (j + 1) * each]:
+                part = lax.dot_general(chosen, ref[...], numbers, preferred_element_type=F32)
+                found = part if found is None else found + part
             term = weights[:, j : j + 1] * found
             mixed[side] = term if mixed[side] is None else mixed[side] + term
     out_ref[:, :half] = mixed[0].astype(BF16)
@@ -190,8 +190,7 @@
     plan = jnp.transpose(move_plan, (1, 0, 2))
     weights = (old_gate, old_up, old_down)
     half = most // 2
-    part = most // 3
-    rest = most - 2 * part
+    lead = most // 3
 
     def shape(*dims, dtype=BF16):
         return jax.ShapeDtypeStruct(dims, dtype)
@@ -241,17 +240,15 @@
         name="dispatch",
     )(expert_ids.T, tokens)
 
-    across = [send(parcels[j], j, 0) for j in range(1, experts)]
-    here = jnp.concatenate([parcels[0]] + across, axis=0)
-    held, _ = lax.optimization_barrier((weights, here))
-    wanted = [(0, part, None), (1, half, None), (0, rest, 2 * part), (2, most, 0)]
+    pairs = [(j, k) for j in range(experts) for k in (0, 2)]
+    mine = [parcels[0]] + [send(parcels[j], j, k) for j, k in pairs[1:]]
+    held, _ = lax.optimization_barrier((weights, parcels))
+    wanted = [(1, half, None), (0, lead, 0), (0, most - lead, lead), (2, most, 0)]
     chosen = select(wanted, held)
-    beside = send(here, 0, 2)
-    mine = jnp.concatenate([here, beside], axis=0)
+    shared = migrate(chosen[0], 1)
+    mine = jnp.concatenate(mine, axis=0)
     other = send(mine, 0, 1)
-
-    shared = [migrate(chosen[p], p) for p in range(2)]
-    near = migrate(chosen[3], 2)
+    first = migrate(chosen[1], 0)
 
     total = mine.shape[0]
     step = min(total, 4 * PACK)
@@ -267,37 +264,39 @@
         cost_estimate=cost(0),
         name="expert",
     )(mine, other, *weights)
-    taken, shared[1] = lax.optimization_barrier((send(give, 0, 1), shared[1]))
-    summed = keep + taken.astype(F32)
-    far = send(summed[total // 2 :].astype(BF16), 0, 2)
-
-    far, shared[0] = lax.optimization_barrier((far, shared[0]))
-    swapped = [swap(shared[p], p) for p in range(2)]
+    taken, shared = lax.optimization_barrier((send(give, 0, 1), shared))
+    summed = (keep + taken.astype(F32)).astype(BF16)
+    pieces = [summed[n * PACK : (n + 1) * PACK] for n in range(len(pairs))]
+    back = [pieces[0]] + [
+        send(block, -j, k) for (j, k), block in zip(pairs[1:], pieces[1:])
+    ]
+    beside = len(pairs) // 2
+    near, back[beside] = lax.optimization_barrier((chosen[3], back[beside]))
+    near = migrate(near, 2)
+    back, first = lax.optimization_barrier((back, first))
+    swapped = swap(shared, 1)
     last, _ = lax.optimization_barrier((chosen[2], summed))
-    straight = migrate(last, 0)
-
-    summed = (summed[: total // 2] + far.astype(F32)).astype(BF16)
-    pieces = [summed[j * PACK : (j + 1) * PACK] for j in range(experts)]
-    back = [pieces[0]] + [send(pieces[j], -j, 0) for j in range(1, experts)]
+    second = migrate(last, 0)
+
     mixed = pl.pallas_call(
         functools.partial(combine_kernel, experts),
         out_shape=shape(tokens.shape[0], width),
         in_specs=[VMEM, VMEM] + [VMEM] * len(back),
         out_specs=VMEM,
         compiler_params=params(14 + experts),
-        cost_estimate=cost(2),
+        cost_estimate=cost(14),
         name="combine",
     )(expert_ids.T, combine.T, *back)
 
     arrived = pl.pallas_call(
         merge_kernel,
         out_shape=shape(3, most, width),
-        in_specs=[HBM] * 6,
+        in_specs=[HBM] * 5,
         out_specs=HBM,
-        scratch_shapes=[pltpu.SemaphoreType.DMA((9,))],
+        scratch_shapes=[pltpu.SemaphoreType.DMA((6,))],
         compiler_params=params(),
         name="merge",
-    )(*shared, *swapped, straight, near)
+    )(shared, swapped, first, second, near)
     return mixed, arrived
 
 

time: 38.1 us -> 35.1 us (0.921)
  starting transfers between devices: 17.8 us -> 13.1 us
  waiting for transfers between devices: 13.3 us -> 14.9 us
    ppermute x4, waiting for transfers between devices: 4.9 us -> 10.2 us  [migrate(): return lax.ppermute(block, 'expert', route)]
    ppermute x2 -> x1, starting transfers between devices: 4.88 us -> 0.7 us  [swap(): return lax.ppermute(block, ('expert', 'replica'), route)]
    ppermute x6 -> x8, waiting for transfers between devices: 7.94 us -> 4.68 us  [send(): return lax.ppermute(block, 'expert', route)]
    ppermute x6 -> x8, starting transfers between devices: 8.96 us -> 8.4 us  [send(): return lax.ppermute(block, 'expert', route)]
    ppermute x2 -> x1, waiting for transfers between devices: 0.5 us -> 0.01 us  [swap(): return lax.ppermute(block, ('expert', 'replica'), route)]
    unnamed x17 -> x19, local copies, waits for them, and re-layouts: 1.76 us -> 1.76 us
  transfers between devices with their start and end apart: 12 -> 13, of which waited for: 6 -> 4; matrix products, arithmetic and copies ran while one was open for 0% -> 0% of each run, Pallas kernels for 6% -> 8%
where the time goes in v10:
time: 35.1 us; the launch traced here: 34.8 us
  waiting for transfers between devices  14.9 us (42%)
  starting transfers between devices  13.1 us (37%)
  Pallas kernels  4.24 us (12%)
  local copies, waits for them, and re-layouts  1.79 us (5%)
  between operations  0.84 us (2%)
    ppermute x4, waiting for transfers between devices, migrate(): return lax.ppermute(block, 'expert', route)  10.2 us
    ppermute x8, starting transfers between devices, send(): return lax.ppermute(block, 'expert', route)  8.4 us
    ppermute x8, waiting for transfers between devices, send(): return lax.ppermute(block, 'expert', route)  4.68 us
    ppermute x4, starting transfers between devices, migrate(): return lax.ppermute(block, 'expert', route)  3.98 us
    unnamed x19, local copies, waits for them, and re-layouts  1.76 us
    pallas_call x1, Pallas kernels, on_device(): pl.pallas_call(functools.partial(combine_kernel, experts), out_shape=shap...  1.72 us
    pallas_call x1, Pallas kernels, on_device(): pl.pallas_call(merge_kernel, out_shape=shape(3, most, width), in_specs=[H...  1.06 us
    pallas_call x1, Pallas kernels, on_device(): pl.pallas_call(expert_kernel, grid=(total // step,), out_shape=[shape(tot...  0.93 us
  transfers between devices with their start and end apart: 13, of which 4 were waited for; matrix products, arithmetic and copies ran while one was open for 0% of the time, Pallas kernels for 8%

profile of v10, /device:TPU:0, one launch (start us, length us, event | category | flops | bytes accessed | tf_op | source)
XLA Modules:
  0.0 34.8 jit_solution(10068374729966368881)
XLA Ops:
  0.6 1.0 %copy-done.3 = bf16[128,2048]{1,0:T(8,128)(2,1)S(1)} copy-done((bf16[128,2048]{1,0:T(8,128)(2,1)S(1)}, bf16[128,2048]{1,0:T(8,128)(2,1)}, u32[]{:S(2)}) %copy-start.3) | copy-done | bytes 524312
  1.7 0.7 %copy-done.4 = s32[128,8]{0,1:T(8,128)S(1)} copy-done((s32[128,8]{0,1:T(8,128)S(1)}, s32[128,8]{0,1:T(8,128)}, u32[]{:S(2)}) %copy-start.4) | copy-done | bytes 4120
  2.4 0.5 %dispatch.1 = (bf16[24,1024]{1,0:T(8,128)(2,1)S(1)}, bf16[24,1024]{1,0:T(8,128)(2,1)S(1)}) custom-call(s32[8,128]{1,0:T(8,128)S(1)} %bitcast.3, bf16[128,2048]{1,0:T(8,128)(2,1)S(1)} %copy-done.3), custom_call_target="tpu_custom_call" | custom-call | flops 2000000000 | bytes 10000 | tf_op jit(solution)/shard_map/dispatch/pallas_call | solution.py:228
  2.9 3.0 %collective-permute-start.1 = (bf16[24,1024]{1,0:T(8,128)(2,1)S(1)}, bf16[24,1024]{1,0:T(8,128)(2,1)S(1)}, u32[]{:S(2)}, u32[]{:S(2)}) collective-permute-start(bf16[24,1024]{1,0:T(8,128)(2,1)S(1)} %get-tuple-element.24), channel_id=1, source_target_pairs={{0,16},{4,20},{8,24},{12,28},{16,0},{20,4},{24,8},{28,12},{1,17},{... | collective-permute-start | bytes 147464 | tf_op jit(solution)/shard_map/ppermute | solution.py:203
  5.9 1.4 %collective-permute-start.2 = (bf16[24,1024]{1,0:T(8,128)(2,1)S(1)}, bf16[24,1024]{1,0:T(8,128)(2,1)S(1)}, u32[]{:S(2)}, u32[]{:S(2)}) collective-permute-start(bf16[24,1024]{1,0:T(8,128)(2,1)S(1)} %get-tuple-element.24), channel_id=1, source_target_pairs={{0,24},{4,28},{8,16},{12,20},{16,8},{20,12},{24,0},{28,4},{1,25},{... | collective-permute-start | bytes 147464 | tf_op jit(solution)/shard_map/ppermute | solution.py:203
  7.4 0.1 collective-permute-start
  7.5 0.7 %collective-permute-start.5 = (bf16[3,48,2048]{2,1,0:T(8,128)(2,1)S(1)}, bf16[3,48,2048]{2,1,0:T(8,128)(2,1)S(1)}, u32[]{:S(2)}, u32[]{:S(2)}) collective-permute-start(bf16[3,48,2048]{2,1,0:T(8,128)(2,1)S(1)} %get-tuple-element.30), channel_id=1, source_target_pairs={{12,4},{28,20},{13,5},{29,21},{14,6},{30,22},{15,7},{31,23}} | collective-permute-start | bytes 1769480 | tf_op jit(solution)/shard_map/ppermute | solution.py:207
  8.2 3.2 %collective-permute-done = bf16[24,1024]{1,0:T(8,128)(2,1)S(1)} collective-permute-done((bf16[24,1024]{1,0:T(8,128)(2,1)S(1)}, bf16[24,1024]{1,0:T(8,128)(2,1)S(1)}, u32[]{:S(2)}, u32[]{:S(2)}) %collective-permute-start) | collective-permute-done | bytes 49184 | tf_op jit(solution)/shard_map/ppermute | solution.py:203
  11.5 0.0 collective-permute-done.1
  11.5 0.0 collective-permute-done.2
  11.5 0.1 collective-permute-start.3
  11.6 1.4 %collective-permute-done.3.other_ref = bf16[96,1024]{1,0:T(8,128)(2,1)S(1)} collective-permute-done((bf16[96,1024]{1,0:T(8,128)(2,1)S(1)}, bf16[96,1024]{1,0:T(8,128)(2,1)S(1)}, u32[]{:S(2)}, u32[]{:S(2)}) %collective-permute-start.3) | collective-permute-done | bytes 196640 | tf_op jit(solution)/shard_map/ppermute | solution.py:203
  13.0 0.9 %expert.1 = (f32[96,1024]{1,0:T(8,128)S(1)}, bf16[96,1024]{1,0:T(8,128)(2,1)S(1)}) custom-call(bf16[96,1024]{1,0:T(8,128)(2,1)S(1)} %constant_dynamic-update-slice_fusion.mine_ref, bf16[96,1024]{1,0:T(8,128)(2,1)S(1)} %collective-permute-done.3.other_ref, bf16[192,2048]{1,0:T(8,128)(2,1)S(1)} %copy-done, bf16[192,2048]{1,0:T(8,128)(2,1)S(1)} %copy-done.1, ...), custom_call_target="tpu_custom_call" | custom-call | bytes 10000 | tf_op jit(solution)/shard_map/expert/pallas_call | solution.py:257
  13.9 0.0 copy-start.5
  14.0 0.0 copy-start.6
  14.0 0.2 collective-permute-start.4
  14.2 1.3 %collective-permute-start.9 = (bf16[3,32,2048]{2,1,0:T(8,128)(2,1)S(1)}, bf16[3,32,2048]{2,1,0:T(8,128)(2,1)S(1)}, u32[]{:S(2)}, u32[]{:S(2)}) collective-permute-start(bf16[3,32,2048]{2,1,0:T(8,128)(2,1)S(1)} %get-tuple-element.34), channel_id=1, source_target_pairs={{12,0},{28,16},{13,1},{29,17},{14,2},{30,18},{15,3},{31,19}} | collective-permute-start | bytes 1179656 | tf_op jit(solution)/shard_map/ppermute | solution.py:207
  15.5 0.0 collective-permute-done.4
  15.6 1.6 %collective-permute-start.7 = (bf16[24,1024]{1,0:T(8,128)(2,1)S(1)}, bf16[24,1024]{1,0:T(8,128)(2,1)S(1)}, u32[]{:S(2)}, u32[]{:S(2)}) collective-permute-start(bf16[24,1024]{1,0:T(8,128)(2,1)S(1)} %get-tuple-element.45), channel_id=1, source_target_pairs={{0,16},{4,20},{8,24},{12,28},{16,0},{20,4},{24,8},{28,12},{1,17},{... | collective-permute-start | bytes 147464 | tf_op jit(solution)/shard_map/ppermute | solution.py:203
  17.1 0.5 %collective-permute-start.6 = (bf16[24,1024]{1,0:T(8,128)(2,1)S(1)}, bf16[24,1024]{1,0:T(8,128)(2,1)S(1)}, u32[]{:S(2)}, u32[]{:S(2)}) collective-permute-start(bf16[24,1024]{1,0:T(8,128)(2,1)S(1)} %get-tuple-element.46), channel_id=1, source_target_pairs={{0,8},{4,12},{8,0},{12,4},{16,24},{20,28},{24,16},{28,20},{1,9},{5... | collective-permute-start | bytes 147464 | tf_op jit(solution)/shard_map/ppermute | solution.py:203
  17.7 1.4 %collective-permute-start.8 = (bf16[24,1024]{1,0:T(8,128)(2,1)S(1)}, bf16[24,1024]{1,0:T(8,128)(2,1)S(1)}, u32[]{:S(2)}, u32[]{:S(2)}) collective-permute-start(bf16[24,1024]{1,0:T(8,128)(2,1)S(1)} %get-tuple-element.44), channel_id=1, source_target_pairs={{0,24},{4,28},{8,16},{12,20},{16,8},{20,12},{24,0},{28,4},{1,25},{... | collective-permute-start | bytes 147464 | tf_op jit(solution)/shard_map/ppermute | solution.py:203
  19.1 1.3 %collective-permute-start.11 = (bf16[3,64,2048]{2,1,0:T(8,128)(2,1)S(1)}, bf16[3,64,2048]{2,1,0:T(8,128)(2,1)S(1)}, u32[]{:S(2)}, u32[]{:S(2)}) collective-permute-start(bf16[3,64,2048]{2,1,0:T(8,128)(2,1)S(1)} %get-tuple-element.42), channel_id=1, source_target_pairs={{12,0},{28,16},{13,1},{29,17},{14,2},{30,18},{15,3},{31,19}} | collective-permute-start | bytes 2359304 | tf_op jit(solution)/shard_map/ppermute | solution.py:207
  20.4 0.0 collective-permute-done.7.refs_2_
  20.4 0.7 %collective-permute-start.10 = (bf16[3,48,2048]{2,1,0:T(8,128)(2,1)S(1)}, bf16[3,48,2048]{2,1,0:T(8,128)(2,1)S(1)}, u32[]{:S(2)}, u32[]{:S(2)}) collective-permute-start(bf16[3,48,2048]{2,1,0:T(8,128)(2,1)S(1)} %collective-permute-done.5.shared_ref), channel_id=1, source_target_pairs={{4,5},{20,21},{5,4},{21,20},{6,7},{22,23},{7,6},{23,22}} | collective-permute-start | bytes 1769480 | tf_op jit(solution)/shard_map/ppermute | solution.py:215
  21.1 3.2 %collective-permute-done.9.first_ref = bf16[3,32,2048]{2,1,0:T(8,128)(2,1)S(1)} collective-permute-done((bf16[3,32,2048]{2,1,0:T(8,128)(2,1)S(1)}, bf16[3,32,2048]{2,1,0:T(8,128)(2,1)S(1)}, u32[]{:S(2)}, u32[]{:S(2)}) %collective-permute-start.9) | collective-permute-done | bytes 393248 | tf_op jit(solution)/shard_map/ppermute | solution.py:207
  24.3 0.7 %collective-permute-start.12 = (bf16[3,96,2048]{2,1,0:T(8,128)(2,1)S(1)}, bf16[3,96,2048]{2,1,0:T(8,128)(2,1)S(1)}, u32[]{:S(2)}, u32[]{:S(2)}) collective-permute-start(bf16[3,96,2048]{2,1,0:T(8,128)(2,1)S(1)} %get-tuple-element.43), channel_id=1, source_target_pairs={{12,8},{28,24},{13,9},{29,25},{14,10},{30,26},{15,11},{31,27}} | collective-permute-start | bytes 3538952 | tf_op jit(solution)/shard_map/ppermute | solution.py:207
  25.1 0.0 collective-permute-done.8.refs_3_
  25.1 1.7 %combine.1 = bf16[128,2048]{1,0:T(8,128)(2,1)} custom-call(s32[8,128]{1,0:T(8,128)S(1)} %bitcast.4, f32[8,128]{1,0:T(8,128)S(1)} %bitcast.5, bf16[24,1024]{1,0:T(8,128)(2,1)S(1)} %get-tuple-element.35.refs_0_, bf16[24,1024]{1,0:T(8,128)(2,1)S(1)} %collective-permute-done.6.refs_1_, bf16[24,1024]{1,0:T(8,128)(2,1)S(1)} %collective-permute-done.7.refs_2_, ...), custom_call_target="tpu_custom_call" | custom-call | flops 14000000000 | bytes 10000 | tf_op jit(solution)/shard_map/combine/pallas_call | solution.py:281
  26.8 0.0 collective-permute-done.10.swapped_ref
  26.8 7.0 %collective-permute-done.11.second_ref = bf16[3,64,2048]{2,1,0:T(8,128)(2,1)S(1)} collective-permute-done((bf16[3,64,2048]{2,1,0:T(8,128)(2,1)S(1)}, bf16[3,64,2048]{2,1,0:T(8,128)(2,1)S(1)}, u32[]{:S(2)}, u32[]{:S(2)}) %collective-permute-start.11) | collective-permute-done | bytes 786464 | tf_op jit(solution)/shard_map/ppermute | solution.py:207
  33.8 0.0 collective-permute-done.12.near_ref
  33.8 1.1 %merge.1 = bf16[3,96,2048]{2,1,0:T(8,128)(2,1)} custom-call(bf16[3,48,2048]{2,1,0:T(8,128)(2,1)S(1)} %collective-permute-done.5.shared_ref, bf16[3,48,2048]{2,1,0:T(8,128)(2,1)S(1)} %collective-permute-done.10.swapped_ref, bf16[3,32,2048]{2,1,0:T(8,128)(2,1)S(1)} %collective-permute-done.9.first_ref, ...), custom_call_target="tpu_custom_call" | custom-call | tf_op jit(solution)/shard_map/merge/pallas_call | solution.py:291
  (21 shorter events, 0.1 us)
Async XLA Ops:
  0.6 1.0 %copy-start.3 = (bf16[128,2048]{1,0:T(8,128)(2,1)S(1)}, bf16[128,2048]{1,0:T(8,128)(2,1)}, u32[]{:S(2)}) copy-start(bf16[128,2048]{1,0:T(8,128)(2,1)} %tok_hbm.1) | copy-start | bytes 1572868
  1.7 0.7 %copy-start.4 = (s32[128,8]{0,1:T(8,128)S(1)}, s32[128,8]{0,1:T(8,128)}, u32[]{:S(2)}) copy-start(s32[128,8]{0,1:T(8,128)} %param.8) | copy-start | bytes 12292
  2.4 5.1 %copy-start = (bf16[192,2048]{1,0:T(8,128)(2,1)S(1)}, bf16[192,2048]{1,0:T(8,128)(2,1)}, u32[]{:S(2)}) copy-start(bf16[192,2048]{1,0:T(8,128)(2,1)} %gate_ref.2) | copy-start | bytes 2359300
  2.4 5.1 %copy-start.1 = (bf16[192,2048]{1,0:T(8,128)(2,1)S(1)}, bf16[192,2048]{1,0:T(8,128)(2,1)}, u32[]{:S(2)}) copy-start(bf16[192,2048]{1,0:T(8,128)(2,1)} %up_ref.2) | copy-start | bytes 2359300
  2.4 5.1 %copy-start.2 = (bf16[192,2048]{1,0:T(8,128)(2,1)S(1)}, bf16[192,2048]{1,0:T(8,128)(2,1)}, u32[]{:S(2)}) copy-start(bf16[192,2048]{1,0:T(8,128)(2,1)} %down_ref.2) | copy-start | bytes 2359300
  2.4 5.1 %copy-start.7 = (s32[2,3,96]{2,0,1:T(2,128)S(1)}, s32[2,3,96]{2,0,1:T(2,128)}, u32[]{:S(2)}) copy-start(s32[2,3,96]{2,0,1:T(2,128)} %param.13) | copy-start | bytes 6916
  2.9 8.6 %collective-permute-start.1 = (bf16[24,1024]{1,0:T(8,128)(2,1)S(1)}, bf16[24,1024]{1,0:T(8,128)(2,1)S(1)}, u32[]{:S(2)}, u32[]{:S(2)}) collective-permute-start(bf16[24,1024]{1,0:T(8,128)(2,1)S(1)} %get-tuple-element.24), channel_id=1, source_target_pairs={{0,16},{4,20},{8,24},{12,28},{16,0},{20,4},{24,8},{28,12},{1,17},{... | collective-permute-start | bytes 147464 | tf_op jit(solution)/shard_map/ppermute | solution.py:203
  5.9 5.6 %collective-permute-start.2 = (bf16[24,1024]{1,0:T(8,128)(2,1)S(1)}, bf16[24,1024]{1,0:T(8,128)(2,1)S(1)}, u32[]{:S(2)}, u32[]{:S(2)}) collective-permute-start(bf16[24,1024]{1,0:T(8,128)(2,1)S(1)} %get-tuple-element.24), channel_id=1, source_target_pairs={{0,24},{4,28},{8,16},{12,20},{16,8},{20,12},{24,0},{28,4},{1,25},{... | collective-permute-start | bytes 147464 | tf_op jit(solution)/shard_map/ppermute | solution.py:203
  7.4 4.1 %collective-permute-start = (bf16[24,1024]{1,0:T(8,128)(2,1)S(1)}, bf16[24,1024]{1,0:T(8,128)(2,1)S(1)}, u32[]{:S(2)}, u32[]{:S(2)}) collective-permute-start(bf16[24,1024]{1,0:T(8,128)(2,1)S(1)} %get-tuple-element.23), channel_id=1, source_target_pairs={{0,8},{4,12},{8,0},{12,4},{16,24},{20,28},{24,16},{28,20},{1,9},{5... | collective-permute-start | bytes 147464 | tf_op jit(solution)/shard_map/ppermute | solution.py:203
  7.5 8.0 %collective-permute-start.5 = (bf16[3,48,2048]{2,1,0:T(8,128)(2,1)S(1)}, bf16[3,48,2048]{2,1,0:T(8,128)(2,1)S(1)}, u32[]{:S(2)}, u32[]{:S(2)}) collective-permute-start(bf16[3,48,2048]{2,1,0:T(8,128)(2,1)S(1)} %get-tuple-element.30), channel_id=1, source_target_pairs={{12,4},{28,20},{13,5},{29,21},{14,6},{30,22},{15,7},{31,23}} | collective-permute-start | bytes 1769480 | tf_op jit(solution)/shard_map/ppermute | solution.py:207
  11.5 1.5 %collective-permute-start.3 = (bf16[96,1024]{1,0:T(8,128)(2,1)S(1)}, bf16[96,1024]{1,0:T(8,128)(2,1)S(1)}, u32[]{:S(2)}, u32[]{:S(2)}) collective-permute-start(bf16[96,1024]{1,0:T(8,128)(2,1)S(1)} %constant_dynamic-update-slice_fusion.mine_ref), channel_id=1, source_target_pairs={{0,4},{4,0},{8,12},{12,8},{16,20},{20,16},{24,28},{28,24},{1,5},{5... | collective-permute-start | bytes 589832 | tf_op jit(solution)/shard_map/ppermute | solution.py:203
  13.9 11.1 %copy-start.5 = (s32[128,8]{0,1:T(8,128)S(1)}, s32[128,8]{0,1:T(8,128)}, u32[]{:S(2)}) copy-start(s32[128,8]{0,1:T(8,128)} %param.8) | copy-start | bytes 12292
  14.0 11.1 %copy-start.6 = (f32[128,8]{0,1:T(8,128)S(1)}, f32[128,8]{0,1:T(8,128)}, u32[]{:S(2)}) copy-start(f32[128,8]{0,1:T(8,128)} %param.9) | copy-start | bytes 12292
  14.0 1.5 %collective-permute-start.4 = (bf16[96,1024]{1,0:T(8,128)(2,1)S(1)}, bf16[96,1024]{1,0:T(8,128)(2,1)S(1)}, u32[]{:S(2)}, u32[]{:S(2)}) collective-permute-start(bf16[96,1024]{1,0:T(8,128)(2,1)S(1)} %get-tuple-element.26), channel_id=1, source_target_pairs={{0,4},{4,0},{8,12},{12,8},{16,20},{20,16},{24,28},{28,24},{1,5},{5... | collective-permute-start | bytes 589832 | tf_op jit(solution)/shard_map/ppermute | solution.py:203
  14.2 10.1 %collective-permute-start.9 = (bf16[3,32,2048]{2,1,0:T(8,128)(2,1)S(1)}, bf16[3,32,2048]{2,1,0:T(8,128)(2,1)S(1)}, u32[]{:S(2)}, u32[]{:S(2)}) collective-permute-start(bf16[3,32,2048]{2,1,0:T(8,128)(2,1)S(1)} %get-tuple-element.34), channel_id=1, source_target_pairs={{12,0},{28,16},{13,1},{29,17},{14,2},{30,18},{15,3},{31,19}} | collective-permute-start | bytes 1179656 | tf_op jit(solution)/shard_map/ppermute | solution.py:207
  15.6 4.8 %collective-permute-start.7 = (bf16[24,1024]{1,0:T(8,128)(2,1)S(1)}, bf16[24,1024]{1,0:T(8,128)(2,1)S(1)}, u32[]{:S(2)}, u32[]{:S(2)}) collective-permute-start(bf16[24,1024]{1,0:T(8,128)(2,1)S(1)} %get-tuple-element.45), channel_id=1, source_target_pairs={{0,16},{4,20},{8,24},{12,28},{16,0},{20,4},{24,8},{28,12},{1,17},{... | collective-permute-start | bytes 147464 | tf_op jit(solution)/shard_map/ppermute | solution.py:203
  17.1 7.9 %collective-permute-start.6 = (bf16[24,1024]{1,0:T(8,128)(2,1)S(1)}, bf16[24,1024]{1,0:T(8,128)(2,1)S(1)}, u32[]{:S(2)}, u32[]{:S(2)}) collective-permute-start(bf16[24,1024]{1,0:T(8,128)(2,1)S(1)} %get-tuple-element.46), channel_id=1, source_target_pairs={{0,8},{4,12},{8,0},{12,4},{16,24},{20,28},{24,16},{28,20},{1,9},{5... | collective-permute-start | bytes 147464 | tf_op jit(solution)/shard_map/ppermute | solution.py:203
  17.7 7.4 %collective-permute-start.8 = (bf16[24,1024]{1,0:T(8,128)(2,1)S(1)}, bf16[24,1024]{1,0:T(8,128)(2,1)S(1)}, u32[]{:S(2)}, u32[]{:S(2)}) collective-permute-start(bf16[24,1024]{1,0:T(8,128)(2,1)S(1)} %get-tuple-element.44), channel_id=1, source_target_pairs={{0,24},{4,28},{8,16},{12,20},{16,8},{20,12},{24,0},{28,4},{1,25},{... | collective-permute-start | bytes 147464 | tf_op jit(solution)/shard_map/ppermute | solution.py:203
  19.1 14.7 %collective-permute-start.11 = (bf16[3,64,2048]{2,1,0:T(8,128)(2,1)S(1)}, bf16[3,64,2048]{2,1,0:T(8,128)(2,1)S(1)}, u32[]{:S(2)}, u32[]{:S(2)}) collective-permute-start(bf16[3,64,2048]{2,1,0:T(8,128)(2,1)S(1)} %get-tuple-element.42), channel_id=1, source_target_pairs={{12,0},{28,16},{13,1},{29,17},{14,2},{30,18},{15,3},{31,19}} | collective-permute-start | bytes 2359304 | tf_op jit(solution)/shard_map/ppermute | solution.py:207
  20.4 6.4 %collective-permute-start.10 = (bf16[3,48,2048]{2,1,0:T(8,128)(2,1)S(1)}, bf16[3,48,2048]{2,1,0:T(8,128)(2,1)S(1)}, u32[]{:S(2)}, u32[]{:S(2)}) collective-permute-start(bf16[3,48,2048]{2,1,0:T(8,128)(2,1)S(1)} %collective-permute-done.5.shared_ref), channel_id=1, source_target_pairs={{4,5},{20,21},{5,4},{21,20},{6,7},{22,23},{7,6},{23,22}} | collective-permute-start | bytes 1769480 | tf_op jit(solution)/shard_map/ppermute | solution.py:215
  24.3 9.5 %collective-permute-start.12 = (bf16[3,96,2048]{2,1,0:T(8,128)(2,1)S(1)}, bf16[3,96,2048]{2,1,0:T(8,128)(2,1)S(1)}, u32[]{:S(2)}, u32[]{:S(2)}) collective-permute-start(bf16[3,96,2048]{2,1,0:T(8,128)(2,1)S(1)} %get-tuple-element.43), channel_id=1, source_target_pairs={{12,8},{28,24},{13,9},{29,25},{14,10},{30,26},{15,11},{31,27}} | collective-permute-start | bytes 3538952 | tf_op jit(solution)/shard_map/ppermute | solution.py:207

commit v11 on v10

--- a/solution.py
+++ b/solution.py
@@ -96,10 +96,10 @@
                 start += count
 
 
-def merge_kernel(shared_ref, swapped_ref, first_ref, second_ref, near_ref, out_ref, sems):
+def merge_kernel(*refs):
+    shared_refs, swapped_refs, (straight_ref, near_ref, out_ref, sems) = refs[:2], refs[2:4], refs[4:]
     position = lax.axis_index("expert") % GROUP
     parity = lax.axis_index("replica") % 2
-    half = shared_ref.shape[1]
 
     def move(pieces):
         copies = []
@@ -114,15 +114,17 @@
         for copy in copies:
             copy.wait()
 
-    for even in range(2):
-
-        @pl.when(jnp.logical_and(position == 1, parity == even))
-        def _():
-            move([(shared_ref, half * even), (swapped_ref, half * (1 - even))])
-
-    @pl.when(jnp.logical_or(position == 0, position == 3))
-    def _():
-        move([(first_ref, 0), (second_ref, first_ref.shape[1])])
+    for p in range(2):
+        part = shared_refs[p].shape[1]
+        for even in range(2):
+            mine = position == 1 if p == 1 else jnp.logical_or(position == 0, position == 3)
+
+            @pl.when(jnp.logical_and(mine, parity == even))
+            def _():
+                pieces = [(shared_refs[p], part * even), (swapped_refs[p], part * (1 - even))]
+                if p == 0:
+                    pieces.append((straight_ref, 2 * part))
+                move(pieces)
 
     @pl.when(position == 2)
     def _():
@@ -190,7 +192,7 @@
     plan = jnp.transpose(move_plan, (1, 0, 2))
     weights = (old_gate, old_up, old_down)
     half = most // 2
-    lead = most // 3
+    part = most // 6
 
     def shape(*dims, dtype=BF16):
         return jax.ShapeDtypeStruct(dims, dtype)
@@ -243,12 +245,11 @@
     pairs = [(j, k) for j in range(experts) for k in (0, 2)]
     mine = [parcels[0]] + [send(parcels[j], j, k) for j, k in pairs[1:]]
     held, _ = lax.optimization_barrier((weights, parcels))
-    wanted = [(1, half, None), (0, lead, 0), (0, most - lead, lead), (2, most, 0)]
+    wanted = [(0, part, None), (1, half, None), (0, most - 2 * part, 2 * part), (2, most, 0)]
     chosen = select(wanted, held)
-    shared = migrate(chosen[0], 1)
+    shared = [migrate(chosen[p], p) for p in range(2)]
     mine = jnp.concatenate(mine, axis=0)
     other = send(mine, 0, 1)
-    first = migrate(chosen[1], 0)
 
     total = mine.shape[0]
     step = min(total, 4 * PACK)
@@ -270,13 +271,14 @@
     back = [pieces[0]] + [
         send(block, -j, k) for (j, k), block in zip(pairs[1:], pieces[1:])
     ]
+    swapped = [None, swap(shared[1], 1)]
     beside = len(pairs) // 2
-    near, back[beside] = lax.optimization_barrier((chosen[3], back[beside]))
+    back[beside], near = lax.optimization_barrier((back[beside], chosen[3]))
     near = migrate(near, 2)
-    back, first = lax.optimization_barrier((back, first))
-    swapped = swap(shared, 1)
+    swapped[0] = swap(shared[0], 0)
     last, _ = lax.optimization_barrier((chosen[2], summed))
-    second = migrate(last, 0)
+    straight = migrate(last, 0)
+    back, swapped[1] = lax.optimization_barrier((back, swapped[1]))
 
     mixed = pl.pallas_call(
         functools.partial(combine_kernel, experts),
@@ -291,12 +293,12 @@
     arrived = pl.pallas_call(
         merge_kernel,
         out_shape=shape(3, most, width),
-        in_specs=[HBM] * 5,
+        in_specs=[HBM] * 6,
         out_specs=HBM,
-        scratch_shapes=[pltpu.SemaphoreType.DMA((6,))],
+        scratch_shapes=[pltpu.SemaphoreType.DMA((9,))],
         compiler_params=params(),
         name="merge",
-    )(shared, swapped, first, second, near)
+    )(*shared, *swapped, straight, near)
     return mixed, arrived
 
 

time: 35.1 us -> 39 us (1.11)
  starting transfers between devices: 13.1 us -> 16.6 us
    ppermute x1 -> x2, starting transfers between devices: 0.7 us -> 4.17 us  [swap(): return lax.ppermute(block, ('expert', 'replica'), route)]
    ppermute x1 -> x2, waiting for transfers between devices: 0.01 us -> 1.56 us  [swap(): return lax.ppermute(block, ('expert', 'replica'), route)]
    ppermute x8, waiting for transfers between devices: 4.68 us -> 3.36 us  [send(): return lax.ppermute(block, 'expert', route)]
  transfers between devices with their start and end apart: 13 -> 14, of which waited for: 4 -> 5; matrix products, arithmetic and copies ran while one was open for 0% -> 0% of each run, Pallas kernels for 8% -> 7%
where the time goes in v11:
time: 39 us; the launch traced here: 38.7 us
  starting transfers between devices  16.6 us (43%)
  waiting for transfers between devices  15.2 us (39%)
  Pallas kernels  4.27 us (11%)
  local copies, waits for them, and re-layouts  1.79 us (5%)
  between operations  0.85 us (2%)
    ppermute x4, waiting for transfers between devices, migrate(): return lax.ppermute(block, 'expert', route)  10.3 us
    ppermute x8, starting transfers between devices, send(): return lax.ppermute(block, 'expert', route)  8.4 us
    ppermute x2, starting transfers between devices, swap(): return lax.ppermute(block, ('expert', 'replica'), route)  4.17 us
    ppermute x4, starting transfers between devices, migrate(): return lax.ppermute(block, 'expert', route)  4.01 us
    ppermute x8, waiting for transfers between devices, send(): return lax.ppermute(block, 'expert', route)  3.36 us
    unnamed x19, local copies, waits for them, and re-layouts  1.76 us
    pallas_call x1, Pallas kernels, on_device(): pl.pallas_call(functools.partial(combine_kernel, experts), out_shape=shap...  1.72 us
    ppermute x2, waiting for transfers between devices, swap(): return lax.ppermute(block, ('expert', 'replica'), route)  1.56 us
  transfers between devices with their start and end apart: 14, of which 5 were waited for; matrix products, arithmetic and copies ran while one was open for 0% of the time, Pallas kernels for 7%

profile of v11, /device:TPU:0, one launch (start us, length us, event | category | flops | bytes accessed | tf_op | source)
XLA Modules:
  0.0 38.7 jit_solution(11292270150395043625)
XLA Ops:
  0.6 1.0 %copy-done.3 = bf16[128,2048]{1,0:T(8,128)(2,1)S(1)} copy-done((bf16[128,2048]{1,0:T(8,128)(2,1)S(1)}, bf16[128,2048]{1,0:T(8,128)(2,1)}, u32[]{:S(2)}) %copy-start.3) | copy-done | bytes 524312
  1.7 0.7 %copy-done.4 = s32[128,8]{0,1:T(8,128)S(1)} copy-done((s32[128,8]{0,1:T(8,128)S(1)}, s32[128,8]{0,1:T(8,128)}, u32[]{:S(2)}) %copy-start.4) | copy-done | bytes 4120
  2.4 0.5 %dispatch.1 = (bf16[24,1024]{1,0:T(8,128)(2,1)S(1)}, bf16[24,1024]{1,0:T(8,128)(2,1)S(1)}) custom-call(s32[8,128]{1,0:T(8,128)S(1)} %bitcast.3, bf16[128,2048]{1,0:T(8,128)(2,1)S(1)} %copy-done.3), custom_call_target="tpu_custom_call" | custom-call | flops 2000000000 | bytes 10000 | tf_op jit(solution)/shard_map/dispatch/pallas_call | solution.py:230
  2.9 3.0 %collective-permute-start.1 = (bf16[24,1024]{1,0:T(8,128)(2,1)S(1)}, bf16[24,1024]{1,0:T(8,128)(2,1)S(1)}, u32[]{:S(2)}, u32[]{:S(2)}) collective-permute-start(bf16[24,1024]{1,0:T(8,128)(2,1)S(1)} %get-tuple-element.25), channel_id=1, source_target_pairs={{0,16},{4,20},{8,24},{12,28},{16,0},{20,4},{24,8},{28,12},{1,17},{... | collective-permute-start | bytes 147464 | tf_op jit(solution)/shard_map/ppermute | solution.py:205
  5.9 1.4 %collective-permute-start.2 = (bf16[24,1024]{1,0:T(8,128)(2,1)S(1)}, bf16[24,1024]{1,0:T(8,128)(2,1)S(1)}, u32[]{:S(2)}, u32[]{:S(2)}) collective-permute-start(bf16[24,1024]{1,0:T(8,128)(2,1)S(1)} %get-tuple-element.25), channel_id=1, source_target_pairs={{0,24},{4,28},{8,16},{12,20},{16,8},{20,12},{24,0},{28,4},{1,25},{... | collective-permute-start | bytes 147464 | tf_op jit(solution)/shard_map/ppermute | solution.py:205
  7.4 0.1 collective-permute-start
  7.5 0.7 %collective-permute-start.6 = (bf16[3,48,2048]{2,1,0:T(8,128)(2,1)S(1)}, bf16[3,48,2048]{2,1,0:T(8,128)(2,1)S(1)}, u32[]{:S(2)}, u32[]{:S(2)}) collective-permute-start(bf16[3,48,2048]{2,1,0:T(8,128)(2,1)S(1)} %get-tuple-element.32), channel_id=1, source_target_pairs={{12,4},{28,20},{13,5},{29,21},{14,6},{30,22},{15,7},{31,23}} | collective-permute-start | bytes 1769480 | tf_op jit(solution)/shard_map/ppermute | solution.py:209
  8.2 3.2 %collective-permute-done = bf16[24,1024]{1,0:T(8,128)(2,1)S(1)} collective-permute-done((bf16[24,1024]{1,0:T(8,128)(2,1)S(1)}, bf16[24,1024]{1,0:T(8,128)(2,1)S(1)}, u32[]{:S(2)}, u32[]{:S(2)}) %collective-permute-start) | collective-permute-done | bytes 49184 | tf_op jit(solution)/shard_map/ppermute | solution.py:205
  11.5 0.0 collective-permute-done.1
  11.5 0.1 collective-permute-start.3
  11.6 1.3 %collective-permute-start.5 = (bf16[3,16,2048]{2,1,0:T(8,128)(2,1)S(1)}, bf16[3,16,2048]{2,1,0:T(8,128)(2,1)S(1)}, u32[]{:S(2)}, u32[]{:S(2)}) collective-permute-start(bf16[3,16,2048]{2,1,0:T(8,128)(2,1)S(1)} %get-tuple-element.31), channel_id=1, source_target_pairs={{12,0},{28,16},{13,1},{29,17},{14,2},{30,18},{15,3},{31,19}} | collective-permute-start | bytes 589832 | tf_op jit(solution)/shard_map/ppermute | solution.py:209
  12.9 0.1 collective-permute-done.3.other_ref
  13.0 0.9 %expert.1 = (f32[96,1024]{1,0:T(8,128)S(1)}, bf16[96,1024]{1,0:T(8,128)(2,1)S(1)}) custom-call(bf16[96,1024]{1,0:T(8,128)(2,1)S(1)} %constant_dynamic-update-slice_fusion.mine_ref, bf16[96,1024]{1,0:T(8,128)(2,1)S(1)} %collective-permute-done.3.other_ref, bf16[192,2048]{1,0:T(8,128)(2,1)S(1)} %copy-done, bf16[192,2048]{1,0:T(8,128)(2,1)S(1)} %copy-done.1, ...), custom_call_target="tpu_custom_call" | custom-call | bytes 10000 | tf_op jit(solution)/shard_map/expert/pallas_call | solution.py:258
  13.9 0.0 copy-start.5
  14.0 0.0 copy-start.6
  14.0 0.2 collective-permute-start.4
  14.2 5.9 %collective-permute-done.5.refs_0_ = bf16[3,16,2048]{2,1,0:T(8,128)(2,1)S(1)} collective-permute-done((bf16[3,16,2048]{2,1,0:T(8,128)(2,1)S(1)}, bf16[3,16,2048]{2,1,0:T(8,128)(2,1)S(1)}, u32[]{:S(2)}, u32[]{:S(2)}) %collective-permute-start.5) | collective-permute-done | bytes 196640 | tf_op jit(solution)/shard_map/ppermute | solution.py:209
  20.0 0.0 collective-permute-done.4
  20.0 0.0 collective-permute-done.6.refs_1_
  20.0 0.7 %collective-permute-start.10 = (bf16[3,48,2048]{2,1,0:T(8,128)(2,1)S(1)}, bf16[3,48,2048]{2,1,0:T(8,128)(2,1)S(1)}, u32[]{:S(2)}, u32[]{:S(2)}) collective-permute-start(bf16[3,48,2048]{2,1,0:T(8,128)(2,1)S(1)} %collective-permute-done.6.refs_1_), channel_id=1, source_target_pairs={{4,5},{20,21},{5,4},{21,20},{6,7},{22,23},{7,6},{23,22}} | collective-permute-start | bytes 1769480 | tf_op jit(solution)/shard_map/ppermute | solution.py:217
  20.8 1.6 %collective-permute-start.8 = (bf16[24,1024]{1,0:T(8,128)(2,1)S(1)}, bf16[24,1024]{1,0:T(8,128)(2,1)S(1)}, u32[]{:S(2)}, u32[]{:S(2)}) collective-permute-start(bf16[24,1024]{1,0:T(8,128)(2,1)S(1)} %get-tuple-element.47), channel_id=1, source_target_pairs={{0,16},{4,20},{8,24},{12,28},{16,0},{20,4},{24,8},{28,12},{1,17},{... | collective-permute-start | bytes 147464 | tf_op jit(solution)/shard_map/ppermute | solution.py:205
  22.4 0.0 collective-permute-start.7
  22.4 2.0 %collective-permute-start.9 = (bf16[24,1024]{1,0:T(8,128)(2,1)S(1)}, bf16[24,1024]{1,0:T(8,128)(2,1)S(1)}, u32[]{:S(2)}, u32[]{:S(2)}) collective-permute-start(bf16[24,1024]{1,0:T(8,128)(2,1)S(1)} %get-tuple-element.46), channel_id=1, source_target_pairs={{0,24},{4,28},{8,16},{12,20},{16,8},{20,12},{24,0},{28,4},{1,25},{... | collective-permute-start | bytes 147464 | tf_op jit(solution)/shard_map/ppermute | solution.py:205
  24.4 1.3 %collective-permute-start.12 = (bf16[3,64,2048]{2,1,0:T(8,128)(2,1)S(1)}, bf16[3,64,2048]{2,1,0:T(8,128)(2,1)S(1)}, u32[]{:S(2)}, u32[]{:S(2)}) collective-permute-start(bf16[3,64,2048]{2,1,0:T(8,128)(2,1)S(1)} %get-tuple-element.44), channel_id=1, source_target_pairs={{12,0},{28,16},{13,1},{29,17},{14,2},{30,18},{15,3},{31,19}} | collective-permute-start | bytes 2359304 | tf_op jit(solution)/shard_map/ppermute | solution.py:209
  25.6 0.0 collective-permute-done.8.refs_2_
  25.7 3.5 %collective-permute-start.11 = (bf16[3,16,2048]{2,1,0:T(8,128)(2,1)S(1)}, bf16[3,16,2048]{2,1,0:T(8,128)(2,1)S(1)}, u32[]{:S(2)}, u32[]{:S(2)}) collective-permute-start(bf16[3,16,2048]{2,1,0:T(8,128)(2,1)S(1)} %collective-permute-done.5.refs_0_), channel_id=1, source_target_pairs={{0,1},{16,17},{1,0},{17,16},{2,3},{18,19},{3,2},{19,18}} | collective-permute-start | bytes 589832 | tf_op jit(solution)/shard_map/ppermute | solution.py:217
  29.1 0.0 collective-permute-done.7.refs_1_
  29.1 0.7 %collective-permute-start.13 = (bf16[3,96,2048]{2,1,0:T(8,128)(2,1)S(1)}, bf16[3,96,2048]{2,1,0:T(8,128)(2,1)S(1)}, u32[]{:S(2)}, u32[]{:S(2)}) collective-permute-start(bf16[3,96,2048]{2,1,0:T(8,128)(2,1)S(1)} %get-tuple-element.45), channel_id=1, source_target_pairs={{12,8},{28,24},{13,9},{29,25},{14,10},{30,26},{15,11},{31,27}} | collective-permute-start | bytes 3538952 | tf_op jit(solution)/shard_map/ppermute | solution.py:209
  29.9 1.7 %combine.1 = bf16[128,2048]{1,0:T(8,128)(2,1)} custom-call(s32[8,128]{1,0:T(8,128)S(1)} %bitcast.4, f32[8,128]{1,0:T(8,128)S(1)} %bitcast.5, bf16[24,1024]{1,0:T(8,128)(2,1)S(1)} %get-tuple-element.37.refs_0_, bf16[24,1024]{1,0:T(8,128)(2,1)S(1)} %collective-permute-done.7.refs_1_, bf16[24,1024]{1,0:T(8,128)(2,1)S(1)} %collective-permute-done.8.refs_2_, ...), custom_call_target="tpu_custom_call" | custom-call | flops 14000000000 | bytes 10000 | tf_op jit(solution)/shard_map/combine/pallas_call | solution.py:283
  31.7 1.6 %collective-permute-done.11.refs_2_ = bf16[3,16,2048]{2,1,0:T(8,128)(2,1)S(1)} collective-permute-done((bf16[3,16,2048]{2,1,0:T(8,128)(2,1)S(1)}, bf16[3,16,2048]{2,1,0:T(8,128)(2,1)S(1)}, u32[]{:S(2)}, u32[]{:S(2)}) %collective-permute-start.11) | collective-permute-done | bytes 196640 | tf_op jit(solution)/shard_map/ppermute | solution.py:217
  33.2 4.4 %collective-permute-done.12.refs_4_ = bf16[3,64,2048]{2,1,0:T(8,128)(2,1)S(1)} collective-permute-done((bf16[3,64,2048]{2,1,0:T(8,128)(2,1)S(1)}, bf16[3,64,2048]{2,1,0:T(8,128)(2,1)S(1)}, u32[]{:S(2)}, u32[]{:S(2)}) %collective-permute-start.12) | collective-permute-done | bytes 786464 | tf_op jit(solution)/shard_map/ppermute | solution.py:209
  37.7 1.1 %merge.1 = bf16[3,96,2048]{2,1,0:T(8,128)(2,1)} custom-call(bf16[3,16,2048]{2,1,0:T(8,128)(2,1)S(1)} %collective-permute-done.5.refs_0_, bf16[3,48,2048]{2,1,0:T(8,128)(2,1)S(1)} %collective-permute-done.6.refs_1_, bf16[3,16,2048]{2,1,0:T(8,128)(2,1)S(1)} %collective-permute-done.11.refs_2_, bf16[3,48,2048]{2,1,0:T(8,128)(2,1)S(1)} %collective-permute-done.10.refs_3_, ...), custom_call_target="tpu_custom_call" | custom-call | tf_op jit(solution)/shard_map/merge/pallas_call | solution.py:293
  (23 shorter events, 0.1 us)
Async XLA Ops:
  0.6 1.0 %copy-start.3 = (bf16[128,2048]{1,0:T(8,128)(2,1)S(1)}, bf16[128,2048]{1,0:T(8,128)(2,1)}, u32[]{:S(2)}) copy-start(bf16[128,2048]{1,0:T(8,128)(2,1)} %tok_hbm.1) | copy-start | bytes 1572868
  1.7 0.7 %copy-start.4 = (s32[128,8]{0,1:T(8,128)S(1)}, s32[128,8]{0,1:T(8,128)}, u32[]{:S(2)}) copy-start(s32[128,8]{0,1:T(8,128)} %param.8) | copy-start | bytes 12292
  2.4 5.1 %copy-start = (bf16[192,2048]{1,0:T(8,128)(2,1)S(1)}, bf16[192,2048]{1,0:T(8,128)(2,1)}, u32[]{:S(2)}) copy-start(bf16[192,2048]{1,0:T(8,128)(2,1)} %gate_ref.2) | copy-start | bytes 2359300
  2.4 5.1 %copy-start.1 = (bf16[192,2048]{1,0:T(8,128)(2,1)S(1)}, bf16[192,2048]{1,0:T(8,128)(2,1)}, u32[]{:S(2)}) copy-start(bf16[192,2048]{1,0:T(8,128)(2,1)} %up_ref.2) | copy-start | bytes 2359300
  2.4 5.1 %copy-start.2 = (bf16[192,2048]{1,0:T(8,128)(2,1)S(1)}, bf16[192,2048]{1,0:T(8,128)(2,1)}, u32[]{:S(2)}) copy-start(bf16[192,2048]{1,0:T(8,128)(2,1)} %down_ref.2) | copy-start | bytes 2359300
  2.4 5.1 %copy-start.7 = (s32[2,3,96]{2,0,1:T(2,128)S(1)}, s32[2,3,96]{2,0,1:T(2,128)}, u32[]{:S(2)}) copy-start(s32[2,3,96]{2,0,1:T(2,128)} %param.13) | copy-start | bytes 6916
  2.9 8.6 %collective-permute-start.1 = (bf16[24,1024]{1,0:T(8,128)(2,1)S(1)}, bf16[24,1024]{1,0:T(8,128)(2,1)S(1)}, u32[]{:S(2)}, u32[]{:S(2)}) collective-permute-start(bf16[24,1024]{1,0:T(8,128)(2,1)S(1)} %get-tuple-element.25), channel_id=1, source_target_pairs={{0,16},{4,20},{8,24},{12,28},{16,0},{20,4},{24,8},{28,12},{1,17},{... | collective-permute-start | bytes 147464 | tf_op jit(solution)/shard_map/ppermute | solution.py:205
  5.9 5.6 %collective-permute-start.2 = (bf16[24,1024]{1,0:T(8,128)(2,1)S(1)}, bf16[24,1024]{1,0:T(8,128)(2,1)S(1)}, u32[]{:S(2)}, u32[]{:S(2)}) collective-permute-start(bf16[24,1024]{1,0:T(8,128)(2,1)S(1)} %get-tuple-element.25), channel_id=1, source_target_pairs={{0,24},{4,28},{8,16},{12,20},{16,8},{20,12},{24,0},{28,4},{1,25},{... | collective-permute-start | bytes 147464 | tf_op jit(solution)/shard_map/ppermute | solution.py:205
  7.4 4.1 %collective-permute-start = (bf16[24,1024]{1,0:T(8,128)(2,1)S(1)}, bf16[24,1024]{1,0:T(8,128)(2,1)S(1)}, u32[]{:S(2)}, u32[]{:S(2)}) collective-permute-start(bf16[24,1024]{1,0:T(8,128)(2,1)S(1)} %get-tuple-element.24), channel_id=1, source_target_pairs={{0,8},{4,12},{8,0},{12,4},{16,24},{20,28},{24,16},{28,20},{1,9},{5... | collective-permute-start | bytes 147464 | tf_op jit(solution)/shard_map/ppermute | solution.py:205
  7.5 12.5 %collective-permute-start.6 = (bf16[3,48,2048]{2,1,0:T(8,128)(2,1)S(1)}, bf16[3,48,2048]{2,1,0:T(8,128)(2,1)S(1)}, u32[]{:S(2)}, u32[]{:S(2)}) collective-permute-start(bf16[3,48,2048]{2,1,0:T(8,128)(2,1)S(1)} %get-tuple-element.32), channel_id=1, source_target_pairs={{12,4},{28,20},{13,5},{29,21},{14,6},{30,22},{15,7},{31,23}} | collective-permute-start | bytes 1769480 | tf_op jit(solution)/shard_map/ppermute | solution.py:209
  11.5 1.5 %collective-permute-start.3 = (bf16[96,1024]{1,0:T(8,128)(2,1)S(1)}, bf16[96,1024]{1,0:T(8,128)(2,1)S(1)}, u32[]{:S(2)}, u32[]{:S(2)}) collective-permute-start(bf16[96,1024]{1,0:T(8,128)(2,1)S(1)} %constant_dynamic-update-slice_fusion.mine_ref), channel_id=1, source_target_pairs={{0,4},{4,0},{8,12},{12,8},{16,20},{20,16},{24,28},{28,24},{1,5},{5... | collective-permute-start | bytes 589832 | tf_op jit(solution)/shard_map/ppermute | solution.py:205
  11.6 8.4 %collective-permute-start.5 = (bf16[3,16,2048]{2,1,0:T(8,128)(2,1)S(1)}, bf16[3,16,2048]{2,1,0:T(8,128)(2,1)S(1)}, u32[]{:S(2)}, u32[]{:S(2)}) collective-permute-start(bf16[3,16,2048]{2,1,0:T(8,128)(2,1)S(1)} %get-tuple-element.31), channel_id=1, source_target_pairs={{12,0},{28,16},{13,1},{29,17},{14,2},{30,18},{15,3},{31,19}} | collective-permute-start | bytes 589832 | tf_op jit(solution)/shard_map/ppermute | solution.py:209
  13.9 16.0 %copy-start.5 = (s32[128,8]{0,1:T(8,128)S(1)}, s32[128,8]{0,1:T(8,128)}, u32[]{:S(2)}) copy-start(s32[128,8]{0,1:T(8,128)} %param.8) | copy-start | bytes 12292
  14.0 16.0 %copy-start.6 = (f32[128,8]{0,1:T(8,128)S(1)}, f32[128,8]{0,1:T(8,128)}, u32[]{:S(2)}) copy-start(f32[128,8]{0,1:T(8,128)} %param.9) | copy-start | bytes 12292
  14.0 6.1 %collective-permute-start.4 = (bf16[96,1024]{1,0:T(8,128)(2,1)S(1)}, bf16[96,1024]{1,0:T(8,128)(2,1)S(1)}, u32[]{:S(2)}, u32[]{:S(2)}) collective-permute-start(bf16[96,1024]{1,0:T(8,128)(2,1)S(1)} %get-tuple-element.27), channel_id=1, source_target_pairs={{0,4},{4,0},{8,12},{12,8},{16,20},{20,16},{24,28},{28,24},{1,5},{5... | collective-permute-start | bytes 589832 | tf_op jit(solution)/shard_map/ppermute | solution.py:205
  20.0 9.9 %collective-permute-start.10 = (bf16[3,48,2048]{2,1,0:T(8,128)(2,1)S(1)}, bf16[3,48,2048]{2,1,0:T(8,128)(2,1)S(1)}, u32[]{:S(2)}, u32[]{:S(2)}) collective-permute-start(bf16[3,48,2048]{2,1,0:T(8,128)(2,1)S(1)} %collective-permute-done.6.refs_1_), channel_id=1, source_target_pairs={{4,5},{20,21},{5,4},{21,20},{6,7},{22,23},{7,6},{23,22}} | collective-permute-start | bytes 1769480 | tf_op jit(solution)/shard_map/ppermute | solution.py:217
  20.8 4.8 %collective-permute-start.8 = (bf16[24,1024]{1,0:T(8,128)(2,1)S(1)}, bf16[24,1024]{1,0:T(8,128)(2,1)S(1)}, u32[]{:S(2)}, u32[]{:S(2)}) collective-permute-start(bf16[24,1024]{1,0:T(8,128)(2,1)S(1)} %get-tuple-element.47), channel_id=1, source_target_pairs={{0,16},{4,20},{8,24},{12,28},{16,0},{20,4},{24,8},{28,12},{1,17},{... | collective-permute-start | bytes 147464 | tf_op jit(solution)/shard_map/ppermute | solution.py:205
  22.4 6.8 %collective-permute-start.7 = (bf16[24,1024]{1,0:T(8,128)(2,1)S(1)}, bf16[24,1024]{1,0:T(8,128)(2,1)S(1)}, u32[]{:S(2)}, u32[]{:S(2)}) collective-permute-start(bf16[24,1024]{1,0:T(8,128)(2,1)S(1)} %get-tuple-element.48), channel_id=1, source_target_pairs={{0,8},{4,12},{8,0},{12,4},{16,24},{20,28},{24,16},{28,20},{1,9},{5... | collective-permute-start | bytes 147464 | tf_op jit(solution)/shard_map/ppermute | solution.py:205
  22.4 7.5 %collective-permute-start.9 = (bf16[24,1024]{1,0:T(8,128)(2,1)S(1)}, bf16[24,1024]{1,0:T(8,128)(2,1)S(1)}, u32[]{:S(2)}, u32[]{:S(2)}) collective-permute-start(bf16[24,1024]{1,0:T(8,128)(2,1)S(1)} %get-tuple-element.46), channel_id=1, source_target_pairs={{0,24},{4,28},{8,16},{12,20},{16,8},{20,12},{24,0},{28,4},{1,25},{... | collective-permute-start | bytes 147464 | tf_op jit(solution)/shard_map/ppermute | solution.py:205
  24.4 13.3 %collective-permute-start.12 = (bf16[3,64,2048]{2,1,0:T(8,128)(2,1)S(1)}, bf16[3,64,2048]{2,1,0:T(8,128)(2,1)S(1)}, u32[]{:S(2)}, u32[]{:S(2)}) collective-permute-start(bf16[3,64,2048]{2,1,0:T(8,128)(2,1)S(1)} %get-tuple-element.44), channel_id=1, source_target_pairs={{12,0},{28,16},{13,1},{29,17},{14,2},{30,18},{15,3},{31,19}} | collective-permute-start | bytes 2359304 | tf_op jit(solution)/shard_map/ppermute | solution.py:209
  25.7 7.6 %collective-permute-start.11 = (bf16[3,16,2048]{2,1,0:T(8,128)(2,1)S(1)}, bf16[3,16,2048]{2,1,0:T(8,128)(2,1)S(1)}, u32[]{:S(2)}, u32[]{:S(2)}) collective-permute-start(bf16[3,16,2048]{2,1,0:T(8,128)(2,1)S(1)} %collective-permute-done.5.refs_0_), channel_id=1, source_target_pairs={{0,1},{16,17},{1,0},{17,16},{2,3},{18,19},{3,2},{19,18}} | collective-permute-start | bytes 589832 | tf_op jit(solution)/shard_map/ppermute | solution.py:217
  29.1 8.5 %collective-permute-start.13 = (bf16[3,96,2048]{2,1,0:T(8,128)(2,1)S(1)}, bf16[3,96,2048]{2,1,0:T(8,128)(2,1)S(1)}, u32[]{:S(2)}, u32[]{:S(2)}) collective-permute-start(bf16[3,96,2048]{2,1,0:T(8,128)(2,1)S(1)} %get-tuple-element.45), channel_id=1, source_target_pairs={{12,8},{28,24},{13,9},{29,25},{14,10},{30,26},{15,11},{31,27}} | collective-permute-start | bytes 3538952 | tf_op jit(solution)/shard_map/ppermute | solution.py:209

commit v12 on v11

--- a/solution.py
+++ b/solution.py
@@ -275,10 +275,10 @@
     beside = len(pairs) // 2
     back[beside], near = lax.optimization_barrier((back[beside], chosen[3]))
     near = migrate(near, 2)
+    back[1], shared[0] = lax.optimization_barrier((back[1], shared[0]))
     swapped[0] = swap(shared[0], 0)
-    last, _ = lax.optimization_barrier((chosen[2], summed))
-    straight = migrate(last, 0)
-    back, swapped[1] = lax.optimization_barrier((back, swapped[1]))
+    straight = migrate(chosen[2], 0)
+    back, swapped[1], straight = lax.optimization_barrier((back, swapped[1], straight))
 
     mixed = pl.pallas_call(
         functools.partial(combine_kernel, experts),

time: 39 us -> 36.7 us (0.941)
  waiting for transfers between devices: 15.2 us -> 12.9 us
    ppermute x4, waiting for transfers between devices: 10.3 us -> 4.57 us  [migrate(): return lax.ppermute(block, 'expert', route)]
    ppermute x8, waiting for transfers between devices: 3.36 us -> 6.06 us  [send(): return lax.ppermute(block, 'expert', route)]
    ppermute x2, waiting for transfers between devices: 1.56 us -> 2.3 us  [swap(): return lax.ppermute(block, ('expert', 'replica'), route)]
  transfers between devices with their start and end apart: 14 -> 14, of which waited for: 5 -> 6; matrix products, arithmetic and copies ran while one was open for 0% -> 0% of each run, Pallas kernels for 7% -> 7%
where the time goes in v12:
time: 36.7 us; the launch traced here: 36.4 us
  starting transfers between devices  16.6 us (45%)
  waiting for transfers between devices  12.9 us (35%)
  Pallas kernels  4.26 us (12%)
  local copies, waits for them, and re-layouts  1.79 us (5%)
  between operations  0.84 us (2%)
    ppermute x8, starting transfers between devices, send(): return lax.ppermute(block, 'expert', route)  8.4 us
    ppermute x8, waiting for transfers between devices, send(): return lax.ppermute(block, 'expert', route)  6.06 us
    ppermute x4, waiting for transfers between devices, migrate(): return lax.ppermute(block, 'expert', route)  4.57 us
    ppermute x2, starting transfers between devices, swap(): return lax.ppermute(block, ('expert', 'replica'), route)  4.18 us
    ppermute x4, starting transfers between devices, migrate(): return lax.ppermute(block, 'expert', route)  4 us
    ppermute x2, waiting for transfers between devices, swap(): return lax.ppermute(block, ('expert', 'replica'), route)  2.3 us
    unnamed x19, local copies, waits for them, and re-layouts  1.76 us
    pallas_call x1, Pallas kernels, on_device(): pl.pallas_call(functools.partial(combine_kernel, experts), out_shape=shap...  1.71 us
  transfers between devices with their start and end apart: 14, of which 6 were waited for; matrix products, arithmetic and copies ran while one was open for 0% of the time, Pallas kernels for 7%

profile of v12, /device:TPU:0, one launch (start us, length us, event | category | flops | bytes accessed | tf_op | source)
XLA Modules:
  0.0 36.4 jit_solution(8324469471212064587)
XLA Ops:
  0.6 1.0 %copy-done.3 = bf16[128,2048]{1,0:T(8,128)(2,1)S(1)} copy-done((bf16[128,2048]{1,0:T(8,128)(2,1)S(1)}, bf16[128,2048]{1,0:T(8,128)(2,1)}, u32[]{:S(2)}) %copy-start.3) | copy-done | bytes 524312
  1.7 0.7 %copy-done.4 = s32[128,8]{0,1:T(8,128)S(1)} copy-done((s32[128,8]{0,1:T(8,128)S(1)}, s32[128,8]{0,1:T(8,128)}, u32[]{:S(2)}) %copy-start.4) | copy-done | bytes 4120
  2.4 0.5 %dispatch.1 = (bf16[24,1024]{1,0:T(8,128)(2,1)S(1)}, bf16[24,1024]{1,0:T(8,128)(2,1)S(1)}) custom-call(s32[8,128]{1,0:T(8,128)S(1)} %bitcast.3, bf16[128,2048]{1,0:T(8,128)(2,1)S(1)} %copy-done.3), custom_call_target="tpu_custom_call" | custom-call | flops 2000000000 | bytes 10000 | tf_op jit(solution)/shard_map/dispatch/pallas_call | solution.py:230
  2.9 3.0 %collective-permute-start.1 = (bf16[24,1024]{1,0:T(8,128)(2,1)S(1)}, bf16[24,1024]{1,0:T(8,128)(2,1)S(1)}, u32[]{:S(2)}, u32[]{:S(2)}) collective-permute-start(bf16[24,1024]{1,0:T(8,128)(2,1)S(1)} %get-tuple-element.27), channel_id=1, source_target_pairs={{0,16},{4,20},{8,24},{12,28},{16,0},{20,4},{24,8},{28,12},{1,17},{... | collective-permute-start | bytes 147464 | tf_op jit(solution)/shard_map/ppermute | solution.py:205
  5.9 1.4 %collective-permute-start.2 = (bf16[24,1024]{1,0:T(8,128)(2,1)S(1)}, bf16[24,1024]{1,0:T(8,128)(2,1)S(1)}, u32[]{:S(2)}, u32[]{:S(2)}) collective-permute-start(bf16[24,1024]{1,0:T(8,128)(2,1)S(1)} %get-tuple-element.27), channel_id=1, source_target_pairs={{0,24},{4,28},{8,16},{12,20},{16,8},{20,12},{24,0},{28,4},{1,25},{... | collective-permute-start | bytes 147464 | tf_op jit(solution)/shard_map/ppermute | solution.py:205
  7.4 0.1 collective-permute-start
  7.5 0.7 %collective-permute-start.6 = (bf16[3,48,2048]{2,1,0:T(8,128)(2,1)S(1)}, bf16[3,48,2048]{2,1,0:T(8,128)(2,1)S(1)}, u32[]{:S(2)}, u32[]{:S(2)}) collective-permute-start(bf16[3,48,2048]{2,1,0:T(8,128)(2,1)S(1)} %get-tuple-element.34), channel_id=1, source_target_pairs={{12,4},{28,20},{13,5},{29,21},{14,6},{30,22},{15,7},{31,23}} | collective-permute-start | bytes 1769480 | tf_op jit(solution)/shard_map/ppermute | solution.py:209
  8.2 3.2 %collective-permute-done = bf16[24,1024]{1,0:T(8,128)(2,1)S(1)} collective-permute-done((bf16[24,1024]{1,0:T(8,128)(2,1)S(1)}, bf16[24,1024]{1,0:T(8,128)(2,1)S(1)}, u32[]{:S(2)}, u32[]{:S(2)}) %collective-permute-start) | collective-permute-done | bytes 49184 | tf_op jit(solution)/shard_map/ppermute | solution.py:205
  11.5 0.1 collective-permute-start.3
  11.6 1.3 %collective-permute-start.5 = (bf16[3,16,2048]{2,1,0:T(8,128)(2,1)S(1)}, bf16[3,16,2048]{2,1,0:T(8,128)(2,1)S(1)}, u32[]{:S(2)}, u32[]{:S(2)}) collective-permute-start(bf16[3,16,2048]{2,1,0:T(8,128)(2,1)S(1)} %get-tuple-element.33), channel_id=1, source_target_pairs={{12,0},{28,16},{13,1},{29,17},{14,2},{30,18},{15,3},{31,19}} | collective-permute-start | bytes 589832 | tf_op jit(solution)/shard_map/ppermute | solution.py:209
  12.9 0.1 collective-permute-done.3.other_ref
  13.0 0.9 %expert.1 = (f32[96,1024]{1,0:T(8,128)S(1)}, bf16[96,1024]{1,0:T(8,128)(2,1)S(1)}) custom-call(bf16[96,1024]{1,0:T(8,128)(2,1)S(1)} %constant_dynamic-update-slice_fusion.mine_ref, bf16[96,1024]{1,0:T(8,128)(2,1)S(1)} %collective-permute-done.3.other_ref, bf16[192,2048]{1,0:T(8,128)(2,1)S(1)} %copy-done, bf16[192,2048]{1,0:T(8,128)(2,1)S(1)} %copy-done.1, ...), custom_call_target="tpu_custom_call" | custom-call | bytes 10000 | tf_op jit(solution)/shard_map/expert/pallas_call | solution.py:258
  13.9 0.0 copy-start.5
  14.0 0.0 copy-start.6
  14.0 0.2 collective-permute-start.4
  14.2 1.3 %collective-permute-start.11 = (bf16[3,64,2048]{2,1,0:T(8,128)(2,1)S(1)}, bf16[3,64,2048]{2,1,0:T(8,128)(2,1)S(1)}, u32[]{:S(2)}, u32[]{:S(2)}) collective-permute-start(bf16[3,64,2048]{2,1,0:T(8,128)(2,1)S(1)} %get-tuple-element.41), channel_id=1, source_target_pairs={{12,0},{28,16},{13,1},{29,17},{14,2},{30,18},{15,3},{31,19}} | collective-permute-start | bytes 2359304 | tf_op jit(solution)/shard_map/ppermute | solution.py:209
  15.5 4.6 %collective-permute-done.5.refs_0_ = bf16[3,16,2048]{2,1,0:T(8,128)(2,1)S(1)} collective-permute-done((bf16[3,16,2048]{2,1,0:T(8,128)(2,1)S(1)}, bf16[3,16,2048]{2,1,0:T(8,128)(2,1)S(1)}, u32[]{:S(2)}, u32[]{:S(2)}) %collective-permute-start.5) | collective-permute-done | bytes 196640 | tf_op jit(solution)/shard_map/ppermute | solution.py:209
  20.0 0.0 collective-permute-done.4
  20.0 0.0 collective-permute-done.6.refs_1_
  20.0 0.7 %collective-permute-start.10 = (bf16[3,48,2048]{2,1,0:T(8,128)(2,1)S(1)}, bf16[3,48,2048]{2,1,0:T(8,128)(2,1)S(1)}, u32[]{:S(2)}, u32[]{:S(2)}) collective-permute-start(bf16[3,48,2048]{2,1,0:T(8,128)(2,1)S(1)} %collective-permute-done.6.refs_1_), channel_id=1, source_target_pairs={{4,5},{20,21},{5,4},{21,20},{6,7},{22,23},{7,6},{23,22}} | collective-permute-start | bytes 1769480 | tf_op jit(solution)/shard_map/ppermute | solution.py:217
  20.8 1.6 %collective-permute-start.8 = (bf16[24,1024]{1,0:T(8,128)(2,1)S(1)}, bf16[24,1024]{1,0:T(8,128)(2,1)S(1)}, u32[]{:S(2)}, u32[]{:S(2)}) collective-permute-start(bf16[24,1024]{1,0:T(8,128)(2,1)S(1)} %get-tuple-element.51), channel_id=1, source_target_pairs={{0,16},{4,20},{8,24},{12,28},{16,0},{20,4},{24,8},{28,12},{1,17},{... | collective-permute-start | bytes 147464 | tf_op jit(solution)/shard_map/ppermute | solution.py:205
  22.4 0.0 collective-permute-start.7
  22.4 2.0 %collective-permute-start.9 = (bf16[24,1024]{1,0:T(8,128)(2,1)S(1)}, bf16[24,1024]{1,0:T(8,128)(2,1)S(1)}, u32[]{:S(2)}, u32[]{:S(2)}) collective-permute-start(bf16[24,1024]{1,0:T(8,128)(2,1)S(1)} %get-tuple-element.50), channel_id=1, source_target_pairs={{0,24},{4,28},{8,16},{12,20},{16,8},{20,12},{24,0},{28,4},{1,25},{... | collective-permute-start | bytes 147464 | tf_op jit(solution)/shard_map/ppermute | solution.py:205
  24.4 0.6 %collective-permute-done.8.refs_2_ = bf16[24,1024]{1,0:T(8,128)(2,1)S(1)} collective-permute-done((bf16[24,1024]{1,0:T(8,128)(2,1)S(1)}, bf16[24,1024]{1,0:T(8,128)(2,1)S(1)}, u32[]{:S(2)}, u32[]{:S(2)}) %collective-permute-start.8) | collective-permute-done | bytes 49184 | tf_op jit(solution)/shard_map/ppermute | solution.py:205
  25.0 2.1 %collective-permute-done.7.refs_1_ = bf16[24,1024]{1,0:T(8,128)(2,1)S(1)} collective-permute-done((bf16[24,1024]{1,0:T(8,128)(2,1)S(1)}, bf16[24,1024]{1,0:T(8,128)(2,1)S(1)}, u32[]{:S(2)}, u32[]{:S(2)}) %collective-permute-start.7) | collective-permute-done | bytes 49184 | tf_op jit(solution)/shard_map/ppermute | solution.py:205
  27.1 0.7 %collective-permute-start.13 = (bf16[3,96,2048]{2,1,0:T(8,128)(2,1)S(1)}, bf16[3,96,2048]{2,1,0:T(8,128)(2,1)S(1)}, u32[]{:S(2)}, u32[]{:S(2)}) collective-permute-start(bf16[3,96,2048]{2,1,0:T(8,128)(2,1)S(1)} %get-tuple-element.49), channel_id=1, source_target_pairs={{12,8},{28,24},{13,9},{29,25},{14,10},{30,26},{15,11},{31,27}} | collective-permute-start | bytes 3538952 | tf_op jit(solution)/shard_map/ppermute | solution.py:209
  27.8 3.5 %collective-permute-start.12 = (bf16[3,16,2048]{2,1,0:T(8,128)(2,1)S(1)}, bf16[3,16,2048]{2,1,0:T(8,128)(2,1)S(1)}, u32[]{:S(2)}, u32[]{:S(2)}) collective-permute-start(bf16[3,16,2048]{2,1,0:T(8,128)(2,1)S(1)} %collective-permute-done.5.refs_0_), channel_id=1, source_target_pairs={{0,1},{16,17},{1,0},{17,16},{2,3},{18,19},{3,2},{19,18}} | collective-permute-start | bytes 589832 | tf_op jit(solution)/shard_map/ppermute | solution.py:217
  31.3 0.0 collective-permute-done.9.refs_3_
  31.3 0.0 collective-permute-done.10.refs_3_
  31.3 1.7 %combine.1 = bf16[128,2048]{1,0:T(8,128)(2,1)} custom-call(s32[8,128]{1,0:T(8,128)S(1)} %bitcast.4, f32[8,128]{1,0:T(8,128)S(1)} %bitcast.5, bf16[24,1024]{1,0:T(8,128)(2,1)S(1)} %get-tuple-element.42.refs_0_, bf16[24,1024]{1,0:T(8,128)(2,1)S(1)} %collective-permute-done.7.refs_1_, bf16[24,1024]{1,0:T(8,128)(2,1)S(1)} %collective-permute-done.8.refs_2_, ...), custom_call_target="tpu_custom_call" | custom-call | flops 14000000000 | bytes 10000 | tf_op jit(solution)/shard_map/combine/pallas_call | solution.py:283
  33.1 2.3 %collective-permute-done.12.refs_2_ = bf16[3,16,2048]{2,1,0:T(8,128)(2,1)S(1)} collective-permute-done((bf16[3,16,2048]{2,1,0:T(8,128)(2,1)S(1)}, bf16[3,16,2048]{2,1,0:T(8,128)(2,1)S(1)}, u32[]{:S(2)}, u32[]{:S(2)}) %collective-permute-start.12) | collective-permute-done | bytes 196640 | tf_op jit(solution)/shard_map/ppermute | solution.py:217
  35.4 1.1 %merge.1 = bf16[3,96,2048]{2,1,0:T(8,128)(2,1)} custom-call(bf16[3,16,2048]{2,1,0:T(8,128)(2,1)S(1)} %collective-permute-done.5.refs_0_, bf16[3,48,2048]{2,1,0:T(8,128)(2,1)S(1)} %collective-permute-done.6.refs_1_, bf16[3,16,2048]{2,1,0:T(8,128)(2,1)S(1)} %collective-permute-done.12.refs_2_, bf16[3,48,2048]{2,1,0:T(8,128)(2,1)S(1)} %collective-permute-done.10.refs_3_, ...), custom_call_target="tpu_custom_call" | custom-call | tf_op jit(solution)/shard_map/merge/pallas_call | solution.py:293
  (23 shorter events, 0.1 us)
Async XLA Ops:
  0.6 1.0 %copy-start.3 = (bf16[128,2048]{1,0:T(8,128)(2,1)S(1)}, bf16[128,2048]{1,0:T(8,128)(2,1)}, u32[]{:S(2)}) copy-start(bf16[128,2048]{1,0:T(8,128)(2,1)} %tok_hbm.1) | copy-start | bytes 1572868
  1.7 0.7 %copy-start.4 = (s32[128,8]{0,1:T(8,128)S(1)}, s32[128,8]{0,1:T(8,128)}, u32[]{:S(2)}) copy-start(s32[128,8]{0,1:T(8,128)} %param.8) | copy-start | bytes 12292
  2.4 5.1 %copy-start = (bf16[192,2048]{1,0:T(8,128)(2,1)S(1)}, bf16[192,2048]{1,0:T(8,128)(2,1)}, u32[]{:S(2)}) copy-start(bf16[192,2048]{1,0:T(8,128)(2,1)} %gate_ref.2) | copy-start | bytes 2359300
  2.4 5.1 %copy-start.1 = (bf16[192,2048]{1,0:T(8,128)(2,1)S(1)}, bf16[192,2048]{1,0:T(8,128)(2,1)}, u32[]{:S(2)}) copy-start(bf16[192,2048]{1,0:T(8,128)(2,1)} %up_ref.2) | copy-start | bytes 2359300
  2.4 5.1 %copy-start.2 = (bf16[192,2048]{1,0:T(8,128)(2,1)S(1)}, bf16[192,2048]{1,0:T(8,128)(2,1)}, u32[]{:S(2)}) copy-start(bf16[192,2048]{1,0:T(8,128)(2,1)} %down_ref.2) | copy-start | bytes 2359300
  2.4 5.1 %copy-start.7 = (s32[2,3,96]{2,0,1:T(2,128)S(1)}, s32[2,3,96]{2,0,1:T(2,128)}, u32[]{:S(2)}) copy-start(s32[2,3,96]{2,0,1:T(2,128)} %param.13) | copy-start | bytes 6916
  2.9 8.6 %collective-permute-start.1 = (bf16[24,1024]{1,0:T(8,128)(2,1)S(1)}, bf16[24,1024]{1,0:T(8,128)(2,1)S(1)}, u32[]{:S(2)}, u32[]{:S(2)}) collective-permute-start(bf16[24,1024]{1,0:T(8,128)(2,1)S(1)} %get-tuple-element.27), channel_id=1, source_target_pairs={{0,16},{4,20},{8,24},{12,28},{16,0},{20,4},{24,8},{28,12},{1,17},{... | collective-permute-start | bytes 147464 | tf_op jit(solution)/shard_map/ppermute | solution.py:205
  5.9 5.6 %collective-permute-start.2 = (bf16[24,1024]{1,0:T(8,128)(2,1)S(1)}, bf16[24,1024]{1,0:T(8,128)(2,1)S(1)}, u32[]{:S(2)}, u32[]{:S(2)}) collective-permute-start(bf16[24,1024]{1,0:T(8,128)(2,1)S(1)} %get-tuple-element.27), channel_id=1, source_target_pairs={{0,24},{4,28},{8,16},{12,20},{16,8},{20,12},{24,0},{28,4},{1,25},{... | collective-permute-start | bytes 147464 | tf_op jit(solution)/shard_map/ppermute | solution.py:205
  7.4 4.1 %collective-permute-start = (bf16[24,1024]{1,0:T(8,128)(2,1)S(1)}, bf16[24,1024]{1,0:T(8,128)(2,1)S(1)}, u32[]{:S(2)}, u32[]{:S(2)}) collective-permute-start(bf16[24,1024]{1,0:T(8,128)(2,1)S(1)} %get-tuple-element.26), channel_id=1, source_target_pairs={{0,8},{4,12},{8,0},{12,4},{16,24},{20,28},{24,16},{28,20},{1,9},{5... | collective-permute-start | bytes 147464 | tf_op jit(solution)/shard_map/ppermute | solution.py:205
  7.5 12.5 %collective-permute-start.6 = (bf16[3,48,2048]{2,1,0:T(8,128)(2,1)S(1)}, bf16[3,48,2048]{2,1,0:T(8,128)(2,1)S(1)}, u32[]{:S(2)}, u32[]{:S(2)}) collective-permute-start(bf16[3,48,2048]{2,1,0:T(8,128)(2,1)S(1)} %get-tuple-element.34), channel_id=1, source_target_pairs={{12,4},{28,20},{13,5},{29,21},{14,6},{30,22},{15,7},{31,23}} | collective-permute-start | bytes 1769480 | tf_op jit(solution)/shard_map/ppermute | solution.py:209
  11.5 1.5 %collective-permute-start.3 = (bf16[96,1024]{1,0:T(8,128)(2,1)S(1)}, bf16[96,1024]{1,0:T(8,128)(2,1)S(1)}, u32[]{:S(2)}, u32[]{:S(2)}) collective-permute-start(bf16[96,1024]{1,0:T(8,128)(2,1)S(1)} %constant_dynamic-update-slice_fusion.mine_ref), channel_id=1, source_target_pairs={{0,4},{4,0},{8,12},{12,8},{16,20},{20,16},{24,28},{28,24},{1,5},{5... | collective-permute-start | bytes 589832 | tf_op jit(solution)/shard_map/ppermute | solution.py:205
  11.6 8.4 %collective-permute-start.5 = (bf16[3,16,2048]{2,1,0:T(8,128)(2,1)S(1)}, bf16[3,16,2048]{2,1,0:T(8,128)(2,1)S(1)}, u32[]{:S(2)}, u32[]{:S(2)}) collective-permute-start(bf16[3,16,2048]{2,1,0:T(8,128)(2,1)S(1)} %get-tuple-element.33), channel_id=1, source_target_pairs={{12,0},{28,16},{13,1},{29,17},{14,2},{30,18},{15,3},{31,19}} | collective-permute-start | bytes 589832 | tf_op jit(solution)/shard_map/ppermute | solution.py:209
  13.9 17.4 %copy-start.5 = (s32[128,8]{0,1:T(8,128)S(1)}, s32[128,8]{0,1:T(8,128)}, u32[]{:S(2)}) copy-start(s32[128,8]{0,1:T(8,128)} %param.8) | copy-start | bytes 12292
  14.0 17.4 %copy-start.6 = (f32[128,8]{0,1:T(8,128)S(1)}, f32[128,8]{0,1:T(8,128)}, u32[]{:S(2)}) copy-start(f32[128,8]{0,1:T(8,128)} %param.9) | copy-start | bytes 12292
  14.0 6.1 %collective-permute-start.4 = (bf16[96,1024]{1,0:T(8,128)(2,1)S(1)}, bf16[96,1024]{1,0:T(8,128)(2,1)S(1)}, u32[]{:S(2)}, u32[]{:S(2)}) collective-permute-start(bf16[96,1024]{1,0:T(8,128)(2,1)S(1)} %get-tuple-element.29), channel_id=1, source_target_pairs={{0,4},{4,0},{8,12},{12,8},{16,20},{20,16},{24,28},{28,24},{1,5},{5... | collective-permute-start | bytes 589832 | tf_op jit(solution)/shard_map/ppermute | solution.py:205
  14.2 17.1 %collective-permute-start.11 = (bf16[3,64,2048]{2,1,0:T(8,128)(2,1)S(1)}, bf16[3,64,2048]{2,1,0:T(8,128)(2,1)S(1)}, u32[]{:S(2)}, u32[]{:S(2)}) collective-permute-start(bf16[3,64,2048]{2,1,0:T(8,128)(2,1)S(1)} %get-tuple-element.41), channel_id=1, source_target_pairs={{12,0},{28,16},{13,1},{29,17},{14,2},{30,18},{15,3},{31,19}} | collective-permute-start | bytes 2359304 | tf_op jit(solution)/shard_map/ppermute | solution.py:209
  20.0 11.3 %collective-permute-start.10 = (bf16[3,48,2048]{2,1,0:T(8,128)(2,1)S(1)}, bf16[3,48,2048]{2,1,0:T(8,128)(2,1)S(1)}, u32[]{:S(2)}, u32[]{:S(2)}) collective-permute-start(bf16[3,48,2048]{2,1,0:T(8,128)(2,1)S(1)} %collective-permute-done.6.refs_1_), channel_id=1, source_target_pairs={{4,5},{20,21},{5,4},{21,20},{6,7},{22,23},{7,6},{23,22}} | collective-permute-start | bytes 1769480 | tf_op jit(solution)/shard_map/ppermute | solution.py:217
  20.8 4.2 %collective-permute-start.8 = (bf16[24,1024]{1,0:T(8,128)(2,1)S(1)}, bf16[24,1024]{1,0:T(8,128)(2,1)S(1)}, u32[]{:S(2)}, u32[]{:S(2)}) collective-permute-start(bf16[24,1024]{1,0:T(8,128)(2,1)S(1)} %get-tuple-element.51), channel_id=1, source_target_pairs={{0,16},{4,20},{8,24},{12,28},{16,0},{20,4},{24,8},{28,12},{1,17},{... | collective-permute-start | bytes 147464 | tf_op jit(solution)/shard_map/ppermute | solution.py:205
  22.4 4.7 %collective-permute-start.7 = (bf16[24,1024]{1,0:T(8,128)(2,1)S(1)}, bf16[24,1024]{1,0:T(8,128)(2,1)S(1)}, u32[]{:S(2)}, u32[]{:S(2)}) collective-permute-start(bf16[24,1024]{1,0:T(8,128)(2,1)S(1)} %get-tuple-element.52), channel_id=1, source_target_pairs={{0,8},{4,12},{8,0},{12,4},{16,24},{20,28},{24,16},{28,20},{1,9},{5... | collective-permute-start | bytes 147464 | tf_op jit(solution)/shard_map/ppermute | solution.py:205
  22.4 8.9 %collective-permute-start.9 = (bf16[24,1024]{1,0:T(8,128)(2,1)S(1)}, bf16[24,1024]{1,0:T(8,128)(2,1)S(1)}, u32[]{:S(2)}, u32[]{:S(2)}) collective-permute-start(bf16[24,1024]{1,0:T(8,128)(2,1)S(1)} %get-tuple-element.50), channel_id=1, source_target_pairs={{0,24},{4,28},{8,16},{12,20},{16,8},{20,12},{24,0},{28,4},{1,25},{... | collective-permute-start | bytes 147464 | tf_op jit(solution)/shard_map/ppermute | solution.py:205
  27.1 8.3 %collective-permute-start.13 = (bf16[3,96,2048]{2,1,0:T(8,128)(2,1)S(1)}, bf16[3,96,2048]{2,1,0:T(8,128)(2,1)S(1)}, u32[]{:S(2)}, u32[]{:S(2)}) collective-permute-start(bf16[3,96,2048]{2,1,0:T(8,128)(2,1)S(1)} %get-tuple-element.49), channel_id=1, source_target_pairs={{12,8},{28,24},{13,9},{29,25},{14,10},{30,26},{15,11},{31,27}} | collective-permute-start | bytes 3538952 | tf_op jit(solution)/shard_map/ppermute | solution.py:209
  27.8 7.6 %collective-permute-start.12 = (bf16[3,16,2048]{2,1,0:T(8,128)(2,1)S(1)}, bf16[3,16,2048]{2,1,0:T(8,128)(2,1)S(1)}, u32[]{:S(2)}, u32[]{:S(2)}) collective-permute-start(bf16[3,16,2048]{2,1,0:T(8,128)(2,1)S(1)} %collective-permute-done.5.refs_0_), channel_id=1, source_target_pairs={{0,1},{16,17},{1,0},{17,16},{2,3},{18,19},{3,2},{19,18}} | collective-permute-start | bytes 589832 | tf_op jit(solution)/shard_map/ppermute | solution.py:217

commit v13 on v12

--- a/solution.py
+++ b/solution.py
@@ -9,6 +9,7 @@
 
 CAP = 12
 PACK = 2 * CAP
+STRIDE = 32
 GROUP = 4
 BF16 = jnp.bfloat16
 F32 = jnp.float32
@@ -22,7 +23,7 @@
 
 def cost(microseconds):
     return pl.CostEstimate(
-        flops=microseconds * 10**9, bytes_accessed=10**4, transcendentals=0
+        flops=int(microseconds * 10**9), bytes_accessed=10**4, transcendentals=0
     )
 
 
@@ -96,24 +97,24 @@
                 start += count
 
 
-def merge_kernel(*refs):
-    shared_refs, swapped_refs, (straight_ref, near_ref, out_ref, sems) = refs[:2], refs[2:4], refs[4:]
+def place_rows(pieces, out_ref, sems):
+    copies = []
+    for ref, first in pieces:
+        for m in range(3):
+            rows = pl.ds(first, ref.shape[1])
+            copies.append(
+                pltpu.make_async_copy(ref.at[m], out_ref.at[m, rows], sems.at[len(copies)])
+            )
+    for copy in copies:
+        copy.start()
+    for copy in copies:
+        copy.wait()
+
+
+def early_kernel(*refs):
+    shared_refs, swapped_refs, (out_ref, sems) = refs[:2], refs[2:4], refs[4:]
     position = lax.axis_index("expert") % GROUP
     parity = lax.axis_index("replica") % 2
-
-    def move(pieces):
-        copies = []
-        for ref, first in pieces:
-            for m in range(3):
-                rows = pl.ds(first, ref.shape[1])
-                copies.append(
-                    pltpu.make_async_copy(ref.at[m], out_ref.at[m, rows], sems.at[len(copies)])
-                )
-        for copy in copies:
-            copy.start()
-        for copy in copies:
-            copy.wait()
-
     for p in range(2):
         part = shared_refs[p].shape[1]
         for even in range(2):
@@ -122,13 +123,19 @@
             @pl.when(jnp.logical_and(mine, parity == even))
             def _():
                 pieces = [(shared_refs[p], part * even), (swapped_refs[p], part * (1 - even))]
-                if p == 0:
-                    pieces.append((straight_ref, 2 * part))
-                move(pieces)
+                place_rows(pieces, out_ref, sems)
+
+
+def late_kernel(early_ref, straight_ref, near_ref, out_ref, sems):
+    position = lax.axis_index("expert") % GROUP
+
+    @pl.when(jnp.logical_or(position == 0, position == 3))
+    def _():
+        place_rows([(straight_ref, out_ref.shape[1] - straight_ref.shape[1])], out_ref, sems)
 
     @pl.when(position == 2)
     def _():
-        move([(near_ref, 0)])
+        place_rows([(near_ref, 0)], out_ref, sems)
 
 
 def expert_kernel(mine_ref, other_ref, gate_ref, up_ref, down_ref, keep_ref, give_ref):
@@ -155,32 +162,31 @@
 
 
 def combine_kernel(experts, ids_ref, weight_ref, *refs):
-    piece_refs, out_ref = refs[:-1], refs[-1]
+    piece_refs, (out_ref, rows_ref) = refs[:-2], refs[-2:]
     ids = ids_ref[...]
     group = lax.axis_index("expert") // GROUP
     half = out_ref.shape[1] // 2
+    each = len(piece_refs) // experts
     place = token_places(ids, group, experts)
-    weights = []
+    slot = lax.broadcasted_iota(jnp.int32, (STRIDE, ids.shape[1]), 0)
+    numbers = (((0,), (0,)), ((), ()))
+    rows_ref[...] = jnp.zeros_like(rows_ref)
+    for n, ref in enumerate(piece_refs):
+        rows_ref[n * STRIDE : n * STRIDE + PACK, :] = ref[...]
+    scaled = [[], []]
     for j in range(experts):
         named = ids == lax.rem(group + j, experts)
-        weights.append(jnp.sum(jnp.where(named, weight_ref[...], 0.0), axis=0, keepdims=True))
-    weights = jnp.concatenate(weights, axis=0).T
-    slot = lax.broadcasted_iota(jnp.int32, (PACK, ids.shape[1]), 0)
-    numbers = (((0,), (0,)), ((), ()))
-    each = len(piece_refs) // experts
-    mixed = [None, None]
-    for j in range(experts):
-        spot = place[j : j + 1, :]
+        weight = jnp.sum(jnp.where(named, weight_ref[...], 0.0), axis=0, keepdims=True)
         for side in range(2):
-            chosen = jnp.where(slot == spot + side * CAP, 1.0, 0.0).astype(BF16)
-            found = None
-            for ref in piece_refs[j * each : (j + 1) * each]:
-                part = lax.dot_general(chosen, ref[...], numbers, preferred_element_type=F32)
-                found = part if found is None else found + part
-            term = weights[:, j : j + 1] * found
-            mixed[side] = term if mixed[side] is None else mixed[side] + term
-    out_ref[:, :half] = mixed[0].astype(BF16)
-    out_ref[:, half:] = mixed[1].astype(BF16)
+            chosen = jnp.where(slot == place[j : j + 1, :] + side * CAP, weight, 0.0)
+            scaled[side] += [chosen] * each
+    for side in range(2):
+        chosen = jnp.concatenate(scaled[side], axis=0)
+        high = chosen.astype(BF16)
+        low = (chosen - high.astype(F32)).astype(BF16)
+        mixed = lax.dot_general(high, rows_ref[...], numbers, preferred_element_type=F32)
+        mixed = mixed + lax.dot_general(low, rows_ref[...], numbers, preferred_element_type=F32)
+        out_ref[:, side * half : (side + 1) * half] = mixed.astype(BF16)
 
 
 def on_device(tokens, expert_ids, combine, old_gate, old_up, old_down, move_plan):
@@ -268,37 +274,48 @@
     taken, shared = lax.optimization_barrier((send(give, 0, 1), shared))
     summed = (keep + taken.astype(F32)).astype(BF16)
     pieces = [summed[n * PACK : (n + 1) * PACK] for n in range(len(pairs))]
-    back = [pieces[0]] + [
-        send(block, -j, k) for (j, k), block in zip(pairs[1:], pieces[1:])
-    ]
-    swapped = [None, swap(shared[1], 1)]
-    beside = len(pairs) // 2
-    back[beside], near = lax.optimization_barrier((back[beside], chosen[3]))
+    back = pieces[:1] + [send(pieces[1], 0, 2)]
+    for n in range(2, len(pairs), 2):
+        beside = send(pieces[n], -pairs[n][0], 0)
+        beside, across = lax.optimization_barrier((beside, pieces[n + 1]))
+        back += [beside, send(across, -pairs[n][0], 2)]
+    swapped = [swap(shared[p], p) for p in range(2)]
+    swapped[1], near = lax.optimization_barrier((swapped[1], chosen[3]))
     near = migrate(near, 2)
-    back[1], shared[0] = lax.optimization_barrier((back[1], shared[0]))
-    swapped[0] = swap(shared[0], 0)
     straight = migrate(chosen[2], 0)
-    back, swapped[1], straight = lax.optimization_barrier((back, swapped[1], straight))
+
+    early = pl.pallas_call(
+        early_kernel,
+        out_shape=shape(3, most, width),
+        in_specs=[HBM] * 4,
+        out_specs=HBM,
+        scratch_shapes=[pltpu.SemaphoreType.DMA((6,))],
+        compiler_params=params(),
+        name="early",
+    )(*shared, *swapped)
+    back, early, straight = lax.optimization_barrier((back, early, straight))
 
     mixed = pl.pallas_call(
         functools.partial(combine_kernel, experts),
         out_shape=shape(tokens.shape[0], width),
         in_specs=[VMEM, VMEM] + [VMEM] * len(back),
         out_specs=VMEM,
+        scratch_shapes=[pltpu.VMEM((len(back) * STRIDE, width // 2), BF16)],
         compiler_params=params(14 + experts),
-        cost_estimate=cost(14),
+        cost_estimate=cost(12.3),
         name="combine",
     )(expert_ids.T, combine.T, *back)
 
     arrived = pl.pallas_call(
-        merge_kernel,
+        late_kernel,
         out_shape=shape(3, most, width),
-        in_specs=[HBM] * 6,
+        in_specs=[HBM] * 3,
         out_specs=HBM,
-        scratch_shapes=[pltpu.SemaphoreType.DMA((9,))],
+        input_output_aliases={0: 0},
+        scratch_shapes=[pltpu.SemaphoreType.DMA((3,))],
         compiler_params=params(),
-        name="merge",
-    )(*shared, *swapped, straight, near)
+        name="late",
+    )(early, straight, near)
     return mixed, arrived
 
 

time: 36.7 us -> 36.1 us (0.984)
  starting transfers between devices: 16.6 us -> 14.8 us
  waiting for transfers between devices: 12.9 us -> 13.8 us
    ppermute x8, waiting for transfers between devices: 6.06 us -> 8.05 us  [send(): return lax.ppermute(block, 'expert', route)]
    ppermute x8, starting transfers between devices: 8.4 us -> 6.47 us  [send(): return lax.ppermute(block, 'expert', route)]
    ppermute x2, waiting for transfers between devices: 2.3 us -> 1.12 us  [swap(): return lax.ppermute(block, ('expert', 'replica'), route)]
    pallas_call x1 -> x2, Pallas kernels: 1.08 us -> 1.69 us  [the longest x1 0.9 us: on_device(): pl.pallas_call(late_kernel, out_shape=shape(3, most, width), in_specs=[HB...]
  transfers between devices with their start and end apart: 14 -> 14, of which waited for: 6 -> 6; matrix products, arithmetic and copies ran while one was open for 0% -> 0% of each run, Pallas kernels for 7% -> 9%
where the time goes in v13:
time: 36.1 us; the launch traced here: 35.8 us
  starting transfers between devices  14.8 us (41%)
  waiting for transfers between devices  13.8 us (38%)
  Pallas kernels  4.57 us (13%)
  local copies, waits for them, and re-layouts  1.78 us (5%)
  between operations  0.82 us (2%)
    ppermute x8, waiting for transfers between devices, send(): return lax.ppermute(block, 'expert', route)  8.05 us
    ppermute x8, starting transfers between devices, send(): return lax.ppermute(block, 'expert', route)  6.47 us
    ppermute x4, waiting for transfers between devices, migrate(): return lax.ppermute(block, 'expert', route)  4.6 us
    ppermute x2, starting transfers between devices, swap(): return lax.ppermute(block, ('expert', 'replica'), route)  4.17 us
    ppermute x4, starting transfers between devices, migrate(): return lax.ppermute(block, 'expert', route)  4.14 us
    unnamed x19, local copies, waits for them, and re-layouts  1.76 us
    pallas_call x1, Pallas kernels, on_device(): pl.pallas_call(functools.partial(combine_kernel, experts), out_shape=shap...  1.42 us
    ppermute x2, waiting for transfers between devices, swap(): return lax.ppermute(block, ('expert', 'replica'), route)  1.12 us
  transfers between devices with their start and end apart: 14, of which 6 were waited for; matrix products, arithmetic and copies ran while one was open for 0% of the time, Pallas kernels for 9%

profile of v13, /device:TPU:0, one launch (start us, length us, event | category | flops | bytes accessed | tf_op | source)
XLA Modules:
  0.0 35.8 jit_solution(4764777837796465328)
XLA Ops:
  0.6 1.0 %copy-done.3 = bf16[128,2048]{1,0:T(8,128)(2,1)S(1)} copy-done((bf16[128,2048]{1,0:T(8,128)(2,1)S(1)}, bf16[128,2048]{1,0:T(8,128)(2,1)}, u32[]{:S(2)}) %copy-start.3) | copy-done | bytes 524312
  1.7 0.7 %copy-done.4 = s32[128,8]{0,1:T(8,128)S(1)} copy-done((s32[128,8]{0,1:T(8,128)S(1)}, s32[128,8]{0,1:T(8,128)}, u32[]{:S(2)}) %copy-start.4) | copy-done | bytes 4120
  2.4 0.5 %dispatch.1 = (bf16[24,1024]{1,0:T(8,128)(2,1)S(1)}, bf16[24,1024]{1,0:T(8,128)(2,1)S(1)}) custom-call(s32[8,128]{1,0:T(8,128)S(1)} %bitcast.3, bf16[128,2048]{1,0:T(8,128)(2,1)S(1)} %copy-done.3), custom_call_target="tpu_custom_call" | custom-call | flops 2000000000 | bytes 10000 | tf_op jit(solution)/shard_map/dispatch/pallas_call | solution.py:236
  2.9 4.0 %collective-permute-start.2 = (bf16[24,1024]{1,0:T(8,128)(2,1)S(1)}, bf16[24,1024]{1,0:T(8,128)(2,1)S(1)}, u32[]{:S(2)}, u32[]{:S(2)}) collective-permute-start(bf16[24,1024]{1,0:T(8,128)(2,1)S(1)} %get-tuple-element.27), channel_id=1, source_target_pairs={{0,24},{4,28},{8,16},{12,20},{16,8},{20,12},{24,0},{28,4},{1,25},{... | collective-permute-start | bytes 147464 | tf_op jit(solution)/shard_map/ppermute | solution.py:211
  6.9 0.5 %collective-permute-start.1 = (bf16[24,1024]{1,0:T(8,128)(2,1)S(1)}, bf16[24,1024]{1,0:T(8,128)(2,1)S(1)}, u32[]{:S(2)}, u32[]{:S(2)}) collective-permute-start(bf16[24,1024]{1,0:T(8,128)(2,1)S(1)} %get-tuple-element.27), channel_id=1, source_target_pairs={{0,16},{4,20},{8,24},{12,28},{16,0},{20,4},{24,8},{28,12},{1,17},{... | collective-permute-start | bytes 147464 | tf_op jit(solution)/shard_map/ppermute | solution.py:211
  7.4 0.1 collective-permute-start
  7.5 0.7 %collective-permute-start.6 = (bf16[3,48,2048]{2,1,0:T(8,128)(2,1)S(1)}, bf16[3,48,2048]{2,1,0:T(8,128)(2,1)S(1)}, u32[]{:S(2)}, u32[]{:S(2)}) collective-permute-start(bf16[3,48,2048]{2,1,0:T(8,128)(2,1)S(1)} %get-tuple-element.34), channel_id=1, source_target_pairs={{12,4},{28,20},{13,5},{29,21},{14,6},{30,22},{15,7},{31,23}} | collective-permute-start | bytes 1769480 | tf_op jit(solution)/shard_map/ppermute | solution.py:215
  8.3 3.2 %collective-permute-done = bf16[24,1024]{1,0:T(8,128)(2,1)S(1)} collective-permute-done((bf16[24,1024]{1,0:T(8,128)(2,1)S(1)}, bf16[24,1024]{1,0:T(8,128)(2,1)S(1)}, u32[]{:S(2)}, u32[]{:S(2)}) %collective-permute-start) | collective-permute-done | bytes 49184 | tf_op jit(solution)/shard_map/ppermute | solution.py:211
  11.5 0.0 collective-permute-done.1
  11.5 0.0 collective-permute-done.2
  11.5 0.1 collective-permute-start.3
  11.6 1.3 %collective-permute-start.5 = (bf16[3,16,2048]{2,1,0:T(8,128)(2,1)S(1)}, bf16[3,16,2048]{2,1,0:T(8,128)(2,1)S(1)}, u32[]{:S(2)}, u32[]{:S(2)}) collective-permute-start(bf16[3,16,2048]{2,1,0:T(8,128)(2,1)S(1)} %get-tuple-element.33), channel_id=1, source_target_pairs={{12,0},{28,16},{13,1},{29,17},{14,2},{30,18},{15,3},{31,19}} | collective-permute-start | bytes 589832 | tf_op jit(solution)/shard_map/ppermute | solution.py:215
  12.9 0.1 collective-permute-done.3.other_ref
  13.0 0.9 %expert.1 = (f32[96,1024]{1,0:T(8,128)S(1)}, bf16[96,1024]{1,0:T(8,128)(2,1)S(1)}) custom-call(bf16[96,1024]{1,0:T(8,128)(2,1)S(1)} %constant_dynamic-update-slice_fusion.mine_ref, bf16[96,1024]{1,0:T(8,128)(2,1)S(1)} %collective-permute-done.3.other_ref, bf16[192,2048]{1,0:T(8,128)(2,1)S(1)} %copy-done, bf16[192,2048]{1,0:T(8,128)(2,1)S(1)} %copy-done.1, ...), custom_call_target="tpu_custom_call" | custom-call | bytes 10000 | tf_op jit(solution)/shard_map/expert/pallas_call | solution.py:264
  13.9 0.2 collective-permute-start.4
  14.1 1.3 %collective-permute-start.12 = (bf16[3,64,2048]{2,1,0:T(8,128)(2,1)S(1)}, bf16[3,64,2048]{2,1,0:T(8,128)(2,1)S(1)}, u32[]{:S(2)}, u32[]{:S(2)}) collective-permute-start(bf16[3,64,2048]{2,1,0:T(8,128)(2,1)S(1)} %get-tuple-element.42), channel_id=1, source_target_pairs={{12,0},{28,16},{13,1},{29,17},{14,2},{30,18},{15,3},{31,19}} | collective-permute-start | bytes 2359304 | tf_op jit(solution)/shard_map/ppermute | solution.py:215
  15.4 4.6 %collective-permute-done.5.refs_0_ = bf16[3,16,2048]{2,1,0:T(8,128)(2,1)S(1)} collective-permute-done((bf16[3,16,2048]{2,1,0:T(8,128)(2,1)S(1)}, bf16[3,16,2048]{2,1,0:T(8,128)(2,1)S(1)}, u32[]{:S(2)}, u32[]{:S(2)}) %collective-permute-start.5) | collective-permute-done | bytes 196640 | tf_op jit(solution)/shard_map/ppermute | solution.py:215
  20.0 0.0 collective-permute-done.4
  20.0 0.7 %collective-permute-start.11 = (bf16[3,48,2048]{2,1,0:T(8,128)(2,1)S(1)}, bf16[3,48,2048]{2,1,0:T(8,128)(2,1)S(1)}, u32[]{:S(2)}, u32[]{:S(2)}) collective-permute-start(bf16[3,48,2048]{2,1,0:T(8,128)(2,1)S(1)} %collective-permute-done.6.refs_1_), channel_id=1, source_target_pairs={{4,5},{20,21},{5,4},{21,20},{6,7},{22,23},{7,6},{23,22}} | collective-permute-start | bytes 1769480 | tf_op jit(solution)/shard_map/ppermute | solution.py:223
  20.7 3.5 %collective-permute-start.10 = (bf16[3,16,2048]{2,1,0:T(8,128)(2,1)S(1)}, bf16[3,16,2048]{2,1,0:T(8,128)(2,1)S(1)}, u32[]{:S(2)}, u32[]{:S(2)}) collective-permute-start(bf16[3,16,2048]{2,1,0:T(8,128)(2,1)S(1)} %collective-permute-done.5.refs_0_), channel_id=1, source_target_pairs={{0,1},{16,17},{1,0},{17,16},{2,3},{18,19},{3,2},{19,18}} | collective-permute-start | bytes 589832 | tf_op jit(solution)/shard_map/ppermute | solution.py:223
  24.3 1.6 %collective-permute-start.8 = (bf16[24,1024]{1,0:T(8,128)(2,1)S(1)}, bf16[24,1024]{1,0:T(8,128)(2,1)S(1)}, u32[]{:S(2)}, u32[]{:S(2)}) collective-permute-start(bf16[24,1024]{1,0:T(8,128)(2,1)S(1)} %get-tuple-element.51), channel_id=1, source_target_pairs={{0,16},{4,20},{8,24},{12,28},{16,0},{20,4},{24,8},{28,12},{1,17},{... | collective-permute-start | bytes 147464 | tf_op jit(solution)/shard_map/ppermute | solution.py:211
  25.9 2.6 %collective-permute-done.8.refs_2_ = bf16[24,1024]{1,0:T(8,128)(2,1)S(1)} collective-permute-done((bf16[24,1024]{1,0:T(8,128)(2,1)S(1)}, bf16[24,1024]{1,0:T(8,128)(2,1)S(1)}, u32[]{:S(2)}, u32[]{:S(2)}) %collective-permute-start.8) | collective-permute-done | bytes 49184 | tf_op jit(solution)/shard_map/ppermute | solution.py:211
  28.4 0.0 collective-permute-start.9
  28.4 0.0 collective-permute-done.11.refs_3_
  28.5 0.0 copy-start.6
  28.5 0.9 %collective-permute-start.13 = (bf16[3,96,2048]{2,1,0:T(8,128)(2,1)S(1)}, bf16[3,96,2048]{2,1,0:T(8,128)(2,1)S(1)}, u32[]{:S(2)}, u32[]{:S(2)}) collective-permute-start(bf16[3,96,2048]{2,1,0:T(8,128)(2,1)S(1)} %get-tuple-element.49), channel_id=1, source_target_pairs={{12,8},{28,24},{13,9},{29,25},{14,10},{30,26},{15,11},{31,27}} | collective-permute-start | bytes 3538952 | tf_op jit(solution)/shard_map/ppermute | solution.py:215
  29.3 1.1 %collective-permute-done.10.refs_2_ = bf16[3,16,2048]{2,1,0:T(8,128)(2,1)S(1)} collective-permute-done((bf16[3,16,2048]{2,1,0:T(8,128)(2,1)S(1)}, bf16[3,16,2048]{2,1,0:T(8,128)(2,1)S(1)}, u32[]{:S(2)}, u32[]{:S(2)}) %collective-permute-start.10) | collective-permute-done | bytes 196640 | tf_op jit(solution)/shard_map/ppermute | solution.py:223
  30.5 0.8 %early.1.early_ref = bf16[3,96,2048]{2,1,0:T(8,128)(2,1)} custom-call(bf16[3,16,2048]{2,1,0:T(8,128)(2,1)S(1)} %collective-permute-done.5.refs_0_, bf16[3,48,2048]{2,1,0:T(8,128)(2,1)S(1)} %collective-permute-done.6.refs_1_, bf16[3,16,2048]{2,1,0:T(8,128)(2,1)S(1)} %collective-permute-done.10.refs_2_, bf16[3,48,2048]{2,1,0:T(8,128)(2,1)S(1)} %collective-permute-done.11.refs_3_), custom_call_target="tpu_custom_call" | custom-call | tf_op jit(solution)/shard_map/early/pallas_call | solution.py:287
  31.3 0.0 collective-permute-done.7.refs_1_
  31.3 2.2 %collective-permute-done.9.refs_3_ = bf16[24,1024]{1,0:T(8,128)(2,1)S(1)} collective-permute-done((bf16[24,1024]{1,0:T(8,128)(2,1)S(1)}, bf16[24,1024]{1,0:T(8,128)(2,1)S(1)}, u32[]{:S(2)}, u32[]{:S(2)}) %collective-permute-start.9) | collective-permute-done | bytes 49184 | tf_op jit(solution)/shard_map/ppermute | solution.py:211
  33.4 1.4 %combine.1 = bf16[128,2048]{1,0:T(8,128)(2,1)} custom-call(s32[8,128]{1,0:T(8,128)S(1)} %bitcast.4, f32[8,128]{1,0:T(8,128)S(1)} %bitcast.5, bf16[24,1024]{1,0:T(8,128)(2,1)S(1)} %get-tuple-element.43.refs_0_, bf16[24,1024]{1,0:T(8,128)(2,1)S(1)} %collective-permute-done.7.refs_1_, bf16[24,1024]{1,0:T(8,128)(2,1)S(1)} %collective-permute-done.8.refs_2_, ...), custom_call_target="tpu_custom_call" | custom-call | flops 12300000256 | bytes 10000 | tf_op jit(solution)/shard_map/combine/pallas_call | solution.py:298
  34.9 0.9 %late.1 = bf16[3,96,2048]{2,1,0:T(8,128)(2,1)} custom-call(bf16[3,96,2048]{2,1,0:T(8,128)(2,1)} %early.1.early_ref, bf16[3,64,2048]{2,1,0:T(8,128)(2,1)S(1)} %collective-permute-done.12.straight_ref, bf16[3,96,2048]{2,1,0:T(8,128)(2,1)S(1)} %collective-permute-done.13.near_ref), custom_call_target="tpu_custom_call", output_to_operand_aliasing={{}: (0, {})} | custom-call | tf_op jit(solution)/shard_map/late/pallas_call | solution.py:309
  (24 shorter events, 0.1 us)
Async XLA Ops:
  0.6 1.0 %copy-start.3 = (bf16[128,2048]{1,0:T(8,128)(2,1)S(1)}, bf16[128,2048]{1,0:T(8,128)(2,1)}, u32[]{:S(2)}) copy-start(bf16[128,2048]{1,0:T(8,128)(2,1)} %tok_hbm.1) | copy-start | bytes 1572868
  1.7 0.7 %copy-start.4 = (s32[128,8]{0,1:T(8,128)S(1)}, s32[128,8]{0,1:T(8,128)}, u32[]{:S(2)}) copy-start(s32[128,8]{0,1:T(8,128)} %param.8) | copy-start | bytes 12292
  2.4 5.1 %copy-start = (bf16[192,2048]{1,0:T(8,128)(2,1)S(1)}, bf16[192,2048]{1,0:T(8,128)(2,1)}, u32[]{:S(2)}) copy-start(bf16[192,2048]{1,0:T(8,128)(2,1)} %gate_ref.2) | copy-start | bytes 2359300
  2.4 5.1 %copy-start.1 = (bf16[192,2048]{1,0:T(8,128)(2,1)S(1)}, bf16[192,2048]{1,0:T(8,128)(2,1)}, u32[]{:S(2)}) copy-start(bf16[192,2048]{1,0:T(8,128)(2,1)} %up_ref.2) | copy-start | bytes 2359300
  2.4 5.1 %copy-start.2 = (bf16[192,2048]{1,0:T(8,128)(2,1)S(1)}, bf16[192,2048]{1,0:T(8,128)(2,1)}, u32[]{:S(2)}) copy-start(bf16[192,2048]{1,0:T(8,128)(2,1)} %down_ref.2) | copy-start | bytes 2359300
  2.4 5.1 %copy-start.7 = (s32[2,3,96]{2,0,1:T(2,128)S(1)}, s32[2,3,96]{2,0,1:T(2,128)}, u32[]{:S(2)}) copy-start(s32[2,3,96]{2,0,1:T(2,128)} %param.13) | copy-start | bytes 6916
  2.9 8.6 %collective-permute-start.2 = (bf16[24,1024]{1,0:T(8,128)(2,1)S(1)}, bf16[24,1024]{1,0:T(8,128)(2,1)S(1)}, u32[]{:S(2)}, u32[]{:S(2)}) collective-permute-start(bf16[24,1024]{1,0:T(8,128)(2,1)S(1)} %get-tuple-element.27), channel_id=1, source_target_pairs={{0,24},{4,28},{8,16},{12,20},{16,8},{20,12},{24,0},{28,4},{1,25},{... | collective-permute-start | bytes 147464 | tf_op jit(solution)/shard_map/ppermute | solution.py:211
  6.9 4.6 %collective-permute-start.1 = (bf16[24,1024]{1,0:T(8,128)(2,1)S(1)}, bf16[24,1024]{1,0:T(8,128)(2,1)S(1)}, u32[]{:S(2)}, u32[]{:S(2)}) collective-permute-start(bf16[24,1024]{1,0:T(8,128)(2,1)S(1)} %get-tuple-element.27), channel_id=1, source_target_pairs={{0,16},{4,20},{8,24},{12,28},{16,0},{20,4},{24,8},{28,12},{1,17},{... | collective-permute-start | bytes 147464 | tf_op jit(solution)/shard_map/ppermute | solution.py:211
  7.4 4.1 %collective-permute-start = (bf16[24,1024]{1,0:T(8,128)(2,1)S(1)}, bf16[24,1024]{1,0:T(8,128)(2,1)S(1)}, u32[]{:S(2)}, u32[]{:S(2)}) collective-permute-start(bf16[24,1024]{1,0:T(8,128)(2,1)S(1)} %get-tuple-element.26), channel_id=1, source_target_pairs={{0,8},{4,12},{8,0},{12,4},{16,24},{20,28},{24,16},{28,20},{1,9},{5... | collective-permute-start | bytes 147464 | tf_op jit(solution)/shard_map/ppermute | solution.py:211
  7.5 12.5 %collective-permute-start.6 = (bf16[3,48,2048]{2,1,0:T(8,128)(2,1)S(1)}, bf16[3,48,2048]{2,1,0:T(8,128)(2,1)S(1)}, u32[]{:S(2)}, u32[]{:S(2)}) collective-permute-start(bf16[3,48,2048]{2,1,0:T(8,128)(2,1)S(1)} %get-tuple-element.34), channel_id=1, source_target_pairs={{12,4},{28,20},{13,5},{29,21},{14,6},{30,22},{15,7},{31,23}} | collective-permute-start | bytes 1769480 | tf_op jit(solution)/shard_map/ppermute | solution.py:215
  11.5 1.5 %collective-permute-start.3 = (bf16[96,1024]{1,0:T(8,128)(2,1)S(1)}, bf16[96,1024]{1,0:T(8,128)(2,1)S(1)}, u32[]{:S(2)}, u32[]{:S(2)}) collective-permute-start(bf16[96,1024]{1,0:T(8,128)(2,1)S(1)} %constant_dynamic-update-slice_fusion.mine_ref), channel_id=1, source_target_pairs={{0,4},{4,0},{8,12},{12,8},{16,20},{20,16},{24,28},{28,24},{1,5},{5... | collective-permute-start | bytes 589832 | tf_op jit(solution)/shard_map/ppermute | solution.py:211
  11.6 8.4 %collective-permute-start.5 = (bf16[3,16,2048]{2,1,0:T(8,128)(2,1)S(1)}, bf16[3,16,2048]{2,1,0:T(8,128)(2,1)S(1)}, u32[]{:S(2)}, u32[]{:S(2)}) collective-permute-start(bf16[3,16,2048]{2,1,0:T(8,128)(2,1)S(1)} %get-tuple-element.33), channel_id=1, source_target_pairs={{12,0},{28,16},{13,1},{29,17},{14,2},{30,18},{15,3},{31,19}} | collective-permute-start | bytes 589832 | tf_op jit(solution)/shard_map/ppermute | solution.py:215
  13.9 6.1 %collective-permute-start.4 = (bf16[96,1024]{1,0:T(8,128)(2,1)S(1)}, bf16[96,1024]{1,0:T(8,128)(2,1)S(1)}, u32[]{:S(2)}, u32[]{:S(2)}) collective-permute-start(bf16[96,1024]{1,0:T(8,128)(2,1)S(1)} %get-tuple-element.29), channel_id=1, source_target_pairs={{0,4},{4,0},{8,12},{12,8},{16,20},{20,16},{24,28},{28,24},{1,5},{5... | collective-permute-start | bytes 589832 | tf_op jit(solution)/shard_map/ppermute | solution.py:211
  14.1 19.3 %collective-permute-start.12 = (bf16[3,64,2048]{2,1,0:T(8,128)(2,1)S(1)}, bf16[3,64,2048]{2,1,0:T(8,128)(2,1)S(1)}, u32[]{:S(2)}, u32[]{:S(2)}) collective-permute-start(bf16[3,64,2048]{2,1,0:T(8,128)(2,1)S(1)} %get-tuple-element.42), channel_id=1, source_target_pairs={{12,0},{28,16},{13,1},{29,17},{14,2},{30,18},{15,3},{31,19}} | collective-permute-start | bytes 2359304 | tf_op jit(solution)/shard_map/ppermute | solution.py:215
  20.0 8.4 %collective-permute-start.11 = (bf16[3,48,2048]{2,1,0:T(8,128)(2,1)S(1)}, bf16[3,48,2048]{2,1,0:T(8,128)(2,1)S(1)}, u32[]{:S(2)}, u32[]{:S(2)}) collective-permute-start(bf16[3,48,2048]{2,1,0:T(8,128)(2,1)S(1)} %collective-permute-done.6.refs_1_), channel_id=1, source_target_pairs={{4,5},{20,21},{5,4},{21,20},{6,7},{22,23},{7,6},{23,22}} | collective-permute-start | bytes 1769480 | tf_op jit(solution)/shard_map/ppermute | solution.py:223
  20.7 9.7 %collective-permute-start.10 = (bf16[3,16,2048]{2,1,0:T(8,128)(2,1)S(1)}, bf16[3,16,2048]{2,1,0:T(8,128)(2,1)S(1)}, u32[]{:S(2)}, u32[]{:S(2)}) collective-permute-start(bf16[3,16,2048]{2,1,0:T(8,128)(2,1)S(1)} %collective-permute-done.5.refs_0_), channel_id=1, source_target_pairs={{0,1},{16,17},{1,0},{17,16},{2,3},{18,19},{3,2},{19,18}} | collective-permute-start | bytes 589832 | tf_op jit(solution)/shard_map/ppermute | solution.py:223
  24.3 4.2 %collective-permute-start.8 = (bf16[24,1024]{1,0:T(8,128)(2,1)S(1)}, bf16[24,1024]{1,0:T(8,128)(2,1)S(1)}, u32[]{:S(2)}, u32[]{:S(2)}) collective-permute-start(bf16[24,1024]{1,0:T(8,128)(2,1)S(1)} %get-tuple-element.51), channel_id=1, source_target_pairs={{0,16},{4,20},{8,24},{12,28},{16,0},{20,4},{24,8},{28,12},{1,17},{... | collective-permute-start | bytes 147464 | tf_op jit(solution)/shard_map/ppermute | solution.py:211
  25.9 5.4 %collective-permute-start.7 = (bf16[24,1024]{1,0:T(8,128)(2,1)S(1)}, bf16[24,1024]{1,0:T(8,128)(2,1)S(1)}, u32[]{:S(2)}, u32[]{:S(2)}) collective-permute-start(bf16[24,1024]{1,0:T(8,128)(2,1)S(1)} %get-tuple-element.52), channel_id=1, source_target_pairs={{0,8},{4,12},{8,0},{12,4},{16,24},{20,28},{24,16},{28,20},{1,9},{5... | collective-permute-start | bytes 147464 | tf_op jit(solution)/shard_map/ppermute | solution.py:211
  28.4 5.0 %collective-permute-start.9 = (bf16[24,1024]{1,0:T(8,128)(2,1)S(1)}, bf16[24,1024]{1,0:T(8,128)(2,1)S(1)}, u32[]{:S(2)}, u32[]{:S(2)}) collective-permute-start(bf16[24,1024]{1,0:T(8,128)(2,1)S(1)} %get-tuple-element.37), channel_id=1, source_target_pairs={{0,24},{4,28},{8,16},{12,20},{16,8},{20,12},{24,0},{28,4},{1,25},{... | collective-permute-start | bytes 147464 | tf_op jit(solution)/shard_map/ppermute | solution.py:211
  28.4 5.0 %copy-start.5 = (s32[128,8]{0,1:T(8,128)S(1)}, s32[128,8]{0,1:T(8,128)}, u32[]{:S(2)}) copy-start(s32[128,8]{0,1:T(8,128)} %param.8) | copy-start | bytes 12292
  28.5 5.0 %copy-start.6 = (f32[128,8]{0,1:T(8,128)S(1)}, f32[128,8]{0,1:T(8,128)}, u32[]{:S(2)}) copy-start(f32[128,8]{0,1:T(8,128)} %param.9) | copy-start | bytes 12292
  28.5 6.4 %collective-permute-start.13 = (bf16[3,96,2048]{2,1,0:T(8,128)(2,1)S(1)}, bf16[3,96,2048]{2,1,0:T(8,128)(2,1)S(1)}, u32[]{:S(2)}, u32[]{:S(2)}) collective-permute-start(bf16[3,96,2048]{2,1,0:T(8,128)(2,1)S(1)} %get-tuple-element.49), channel_id=1, source_target_pairs={{12,8},{28,24},{13,9},{29,25},{14,10},{30,26},{15,11},{31,27}} | collective-permute-start | bytes 3538952 | tf_op jit(solution)/shard_map/ppermute | solution.py:215

commit v14 on v13

--- a/solution.py
+++ b/solution.py
@@ -41,25 +41,11 @@
     return jnp.where(member > 0, rank - 1.0, -PACK).astype(jnp.int32)
 
 
-def dispatch_kernel(experts, ids_hbm, tok_hbm, *refs):
-    out_refs, (ids_ref, tok_ref, sems) = refs[:experts], refs[experts:]
+def dispatch_kernel(experts, ids_ref, tok_ref, begun_ref, *out_refs):
+    group = lax.axis_index("expert") // GROUP
+    place = token_places(ids_ref[...], group, experts)
     tok, half = tok_ref.shape[0], tok_ref.shape[1] // 2
-    copies = [pltpu.make_async_copy(ids_hbm, ids_ref, sems.at[0])]
-    for side in range(2):
-        columns = pl.ds(side * half, half)
-        copies.append(
-            pltpu.make_async_copy(
-                tok_hbm.at[:, columns], tok_ref.at[:, columns], sems.at[side + 1]
-            )
-        )
-    for copy in copies:
-        copy.start()
-    group = lax.axis_index("expert") // GROUP
-    copies[0].wait()
-    place = token_places(ids_ref[...], group, experts)
     slot = lax.broadcasted_iota(jnp.int32, (PACK, tok), 0)
-    copies[1].wait()
-    copies[2].wait()
     for j, ref in enumerate(out_refs):
         spot = place[j : j + 1, :]
         left = jnp.where(jnp.logical_and(slot == spot, spot >= 0), 1.0, 0.0).astype(BF16)
@@ -111,19 +97,15 @@
         copy.wait()
 
 
-def early_kernel(*refs):
-    shared_refs, swapped_refs, (out_ref, sems) = refs[:2], refs[2:4], refs[4:]
+def early_kernel(shared_ref, swapped_ref, out_ref, sems):
     position = lax.axis_index("expert") % GROUP
     parity = lax.axis_index("replica") % 2
-    for p in range(2):
-        part = shared_refs[p].shape[1]
-        for even in range(2):
-            mine = position == 1 if p == 1 else jnp.logical_or(position == 0, position == 3)
-
-            @pl.when(jnp.logical_and(mine, parity == even))
-            def _():
-                pieces = [(shared_refs[p], part * even), (swapped_refs[p], part * (1 - even))]
-                place_rows(pieces, out_ref, sems)
+    half = shared_ref.shape[1]
+    for even in range(2):
+
+        @pl.when(jnp.logical_and(position == 1, parity == even))
+        def _():
+            place_rows([(shared_ref, half * even), (swapped_ref, half * (1 - even))], out_ref, sems)
 
 
 def late_kernel(early_ref, straight_ref, near_ref, out_ref, sems):
@@ -131,11 +113,15 @@
 
     @pl.when(jnp.logical_or(position == 0, position == 3))
     def _():
-        place_rows([(straight_ref, out_ref.shape[1] - straight_ref.shape[1])], out_ref, sems)
+        place_rows([(straight_ref, 0)], out_ref, sems)
 
     @pl.when(position == 2)
     def _():
         place_rows([(near_ref, 0)], out_ref, sems)
+
+
+def begin_kernel(out_ref):
+    out_ref[...] = jnp.zeros_like(out_ref)
 
 
 def expert_kernel(mine_ref, other_ref, gate_ref, up_ref, down_ref, keep_ref, give_ref):
@@ -198,7 +184,6 @@
     plan = jnp.transpose(move_plan, (1, 0, 2))
     weights = (old_gate, old_up, old_down)
     half = most // 2
-    part = most // 6
 
     def shape(*dims, dtype=BF16):
         return jax.ShapeDtypeStruct(dims, dtype)
@@ -233,27 +218,30 @@
             name="select",
         )(plan, *held)
 
+    begun = pl.pallas_call(
+        begin_kernel,
+        out_shape=shape(8, 128, dtype=F32),
+        out_specs=VMEM,
+        cost_estimate=cost(5),
+        name="begin",
+    )()
     parcels = pl.pallas_call(
         functools.partial(dispatch_kernel, experts),
         out_shape=[shape(PACK, width // 2)] * experts,
-        in_specs=[HBM, HBM],
+        in_specs=[VMEM, VMEM, HBM],
         out_specs=[VMEM] * experts,
-        scratch_shapes=[
-            pltpu.VMEM(expert_ids.shape[::-1], jnp.int32),
-            pltpu.VMEM(tokens.shape, BF16),
-            pltpu.SemaphoreType.DMA((3,)),
-        ],
         compiler_params=params(),
         cost_estimate=cost(2),
         name="dispatch",
-    )(expert_ids.T, tokens)
+    )(expert_ids.T, tokens, begun)
 
     pairs = [(j, k) for j in range(experts) for k in (0, 2)]
     mine = [parcels[0]] + [send(parcels[j], j, k) for j, k in pairs[1:]]
     held, _ = lax.optimization_barrier((weights, parcels))
-    wanted = [(0, part, None), (1, half, None), (0, most - 2 * part, 2 * part), (2, most, 0)]
+    wanted = [(1, half, None), (0, most, 0), (2, most, 0)]
     chosen = select(wanted, held)
-    shared = [migrate(chosen[p], p) for p in range(2)]
+    shared = migrate(chosen[0], 1)
+    straight = migrate(chosen[1], 0)
     mine = jnp.concatenate(mine, axis=0)
     other = send(mine, 0, 1)
 
@@ -274,25 +262,22 @@
     taken, shared = lax.optimization_barrier((send(give, 0, 1), shared))
     summed = (keep + taken.astype(F32)).astype(BF16)
     pieces = [summed[n * PACK : (n + 1) * PACK] for n in range(len(pairs))]
-    back = pieces[:1] + [send(pieces[1], 0, 2)]
-    for n in range(2, len(pairs), 2):
-        beside = send(pieces[n], -pairs[n][0], 0)
-        beside, across = lax.optimization_barrier((beside, pieces[n + 1]))
-        back += [beside, send(across, -pairs[n][0], 2)]
-    swapped = [swap(shared[p], p) for p in range(2)]
-    swapped[1], near = lax.optimization_barrier((swapped[1], chosen[3]))
+    back = [pieces[0]] + [
+        send(block, -j, k) for (j, k), block in zip(pairs[1:], pieces[1:])
+    ]
+    swapped = swap(shared, 1)
+    swapped, near = lax.optimization_barrier((swapped, chosen[2]))
     near = migrate(near, 2)
-    straight = migrate(chosen[2], 0)
 
     early = pl.pallas_call(
         early_kernel,
         out_shape=shape(3, most, width),
-        in_specs=[HBM] * 4,
+        in_specs=[HBM] * 2,
         out_specs=HBM,
         scratch_shapes=[pltpu.SemaphoreType.DMA((6,))],
         compiler_params=params(),
         name="early",
-    )(*shared, *swapped)
+    )(shared, swapped)
     back, early, straight = lax.optimization_barrier((back, early, straight))
 
     mixed = pl.pallas_call(

time: 36.1 us -> 34.2 us (0.947)
  starting transfers between devices: 14.8 us -> 12 us
  waiting for transfers between devices: 13.8 us -> 15.5 us
  local copies, waits for them, and re-layouts: 1.78 us -> 1.19 us
    ppermute x4 -> x3, waiting for transfers between devices: 4.6 us -> 8.6 us  [migrate(): return lax.ppermute(block, 'expert', route)]
    ppermute x2 -> x1, starting transfers between devices: 4.17 us -> 0.69 us  [swap(): return lax.ppermute(block, ('expert', 'replica'), route)]
    ppermute x8, starting transfers between devices: 6.47 us -> 8.43 us  [send(): return lax.ppermute(block, 'expert', route)]
    ppermute x4 -> x3, starting transfers between devices: 4.14 us -> 2.85 us  [migrate(): return lax.ppermute(block, 'expert', route)]
    ppermute x8, waiting for transfers between devices: 8.05 us -> 6.86 us  [send(): return lax.ppermute(block, 'expert', route)]
    ppermute x2 -> x1, waiting for transfers between devices: 1.12 us -> 0.01 us  [swap(): return lax.ppermute(block, ('expert', 'replica'), route)]
    pallas_call x1, Pallas kernels: 0.79 us -> 0.09 us  [on_device(): pl.pallas_call(early_kernel, out_shape=shape(3, most, width), in_specs=[H...]
    pallas_call x0 -> x1, Pallas kernels: none -> 0.6 us  [on_device(): pl.pallas_call(begin_kernel, out_shape=shape(8, 128, dtype=F32), out_spec...]
  transfers between devices with their start and end apart: 14 -> 12, of which waited for: 6 -> 7; matrix products, arithmetic and copies ran while one was open for 0% -> 0% of each run, Pallas kernels for 9% -> 7%
where the time goes in v14:
time: 34.2 us; the launch traced here: 33.9 us
  waiting for transfers between devices  15.5 us (45%)
  starting transfers between devices  12 us (35%)
  Pallas kernels  4.48 us (13%)
  local copies, waits for them, and re-layouts  1.19 us (3%)
  between operations  0.78 us (2%)
    ppermute x3, waiting for transfers between devices, migrate(): return lax.ppermute(block, 'expert', route)  8.6 us
    ppermute x8, starting transfers between devices, send(): return lax.ppermute(block, 'expert', route)  8.43 us
    ppermute x8, waiting for transfers between devices, send(): return lax.ppermute(block, 'expert', route)  6.86 us
    ppermute x3, starting transfers between devices, migrate(): return lax.ppermute(block, 'expert', route)  2.85 us
    pallas_call x1, Pallas kernels, on_device(): pl.pallas_call(functools.partial(combine_kernel, experts), out_shape=shap...  1.41 us
    unnamed x19, local copies, waits for them, and re-layouts  1.17 us
    pallas_call x1, Pallas kernels, on_device(): pl.pallas_call(late_kernel, out_shape=shape(3, most, width), in_specs=[HB...  1.03 us
    pallas_call x1, Pallas kernels, on_device(): pl.pallas_call(expert_kernel, grid=(total // step,), out_shape=[shape(tot...  0.93 us
  transfers between devices with their start and end apart: 12, of which 7 were waited for; matrix products, arithmetic and copies ran while one was open for 0% of the time, Pallas kernels for 7%

profile of v14, /device:TPU:0, one launch (start us, length us, event | category | flops | bytes accessed | tf_op | source)
XLA Modules:
  0.0 33.9 jit_solution(155347917906821394)
XLA Ops:
  0.6 0.6 %begin.1.begun_ref = f32[8,128]{1,0:T(8,128)} custom-call(), custom_call_target="tpu_custom_call" | custom-call | flops 5000000000 | bytes 10000 | tf_op jit(solution)/shard_map/begin/pallas_call | solution.py:221
  1.2 0.1 copy-done.4
  1.3 0.4 %copy-done.3 = bf16[128,2048]{1,0:T(8,128)(2,1)S(1)} copy-done((bf16[128,2048]{1,0:T(8,128)(2,1)S(1)}, bf16[128,2048]{1,0:T(8,128)(2,1)}, u32[]{:S(2)}) %copy-start.3) | copy-done | bytes 524312
  1.7 0.7 %copy-done.7 = f32[8,128]{1,0:T(8,128)S(1)} copy-done((f32[8,128]{1,0:T(8,128)S(1)}, f32[8,128]{1,0:T(8,128)}, u32[]{:S(2)}) %copy-start.7) | copy-done | bytes 4120
  2.4 0.4 %dispatch.1 = (bf16[24,1024]{1,0:T(8,128)(2,1)S(1)}, bf16[24,1024]{1,0:T(8,128)(2,1)S(1)}) custom-call(s32[8,128]{1,0:T(8,128)S(1)} %bitcast.3, bf16[128,2048]{1,0:T(8,128)(2,1)S(1)} %copy-done.3, f32[8,128]{1,0:T(8,128)S(1)} %copy-done.7), custom_call_target="tpu_custom_call" | custom-call | flops 2000000000 | bytes 10000 | tf_op jit(solution)/shard_map/dispatch/pallas_call | solution.py:228
  2.8 4.0 %collective-permute-start.2 = (bf16[24,1024]{1,0:T(8,128)(2,1)S(1)}, bf16[24,1024]{1,0:T(8,128)(2,1)S(1)}, u32[]{:S(2)}, u32[]{:S(2)}) collective-permute-start(bf16[24,1024]{1,0:T(8,128)(2,1)S(1)} %get-tuple-element.23), channel_id=1, source_target_pairs={{0,24},{4,28},{8,16},{12,20},{16,8},{20,12},{24,0},{28,4},{1,25},{... | collective-permute-start | bytes 147464 | tf_op jit(solution)/shard_map/ppermute | solution.py:196
  6.8 0.5 %collective-permute-start.1 = (bf16[24,1024]{1,0:T(8,128)(2,1)S(1)}, bf16[24,1024]{1,0:T(8,128)(2,1)S(1)}, u32[]{:S(2)}, u32[]{:S(2)}) collective-permute-start(bf16[24,1024]{1,0:T(8,128)(2,1)S(1)} %get-tuple-element.23), channel_id=1, source_target_pairs={{0,16},{4,20},{8,24},{12,28},{16,0},{20,4},{24,8},{28,12},{1,17},{... | collective-permute-start | bytes 147464 | tf_op jit(solution)/shard_map/ppermute | solution.py:196
  7.3 0.1 collective-permute-start
  7.4 0.7 %collective-permute-start.5 = (bf16[3,48,2048]{2,1,0:T(8,128)(2,1)S(1)}, bf16[3,48,2048]{2,1,0:T(8,128)(2,1)S(1)}, u32[]{:S(2)}, u32[]{:S(2)}) collective-permute-start(bf16[3,48,2048]{2,1,0:T(8,128)(2,1)S(1)} %get-tuple-element.29), channel_id=1, source_target_pairs={{12,4},{28,20},{13,5},{29,21},{14,6},{30,22},{15,7},{31,23}} | collective-permute-start | bytes 1769480 | tf_op jit(solution)/shard_map/ppermute | solution.py:200
  8.2 1.3 %collective-permute-start.10 = (bf16[3,96,2048]{2,1,0:T(8,128)(2,1)S(1)}, bf16[3,96,2048]{2,1,0:T(8,128)(2,1)S(1)}, u32[]{:S(2)}, u32[]{:S(2)}) collective-permute-start(bf16[3,96,2048]{2,1,0:T(8,128)(2,1)S(1)} %get-tuple-element.34), channel_id=1, source_target_pairs={{12,0},{28,16},{13,1},{29,17},{14,2},{30,18},{15,3},{31,19}} | collective-permute-start | bytes 3538952 | tf_op jit(solution)/shard_map/ppermute | solution.py:200
  9.5 1.9 %collective-permute-done = bf16[24,1024]{1,0:T(8,128)(2,1)S(1)} collective-permute-done((bf16[24,1024]{1,0:T(8,128)(2,1)S(1)}, bf16[24,1024]{1,0:T(8,128)(2,1)S(1)}, u32[]{:S(2)}, u32[]{:S(2)}) %collective-permute-start) | collective-permute-done | bytes 49184 | tf_op jit(solution)/shard_map/ppermute | solution.py:196
  11.4 0.0 collective-permute-done.1
  11.4 0.0 collective-permute-done.2
  11.4 0.1 collective-permute-start.3
  11.5 1.4 %collective-permute-done.3.other_ref = bf16[96,1024]{1,0:T(8,128)(2,1)S(1)} collective-permute-done((bf16[96,1024]{1,0:T(8,128)(2,1)S(1)}, bf16[96,1024]{1,0:T(8,128)(2,1)S(1)}, u32[]{:S(2)}, u32[]{:S(2)}) %collective-permute-start.3) | collective-permute-done | bytes 196640 | tf_op jit(solution)/shard_map/ppermute | solution.py:196
  12.9 0.9 %expert.1 = (f32[96,1024]{1,0:T(8,128)S(1)}, bf16[96,1024]{1,0:T(8,128)(2,1)S(1)}) custom-call(bf16[96,1024]{1,0:T(8,128)(2,1)S(1)} %constant_dynamic-update-slice_fusion.mine_ref, bf16[96,1024]{1,0:T(8,128)(2,1)S(1)} %collective-permute-done.3.other_ref, bf16[192,2048]{1,0:T(8,128)(2,1)S(1)} %copy-done, bf16[192,2048]{1,0:T(8,128)(2,1)S(1)} %copy-done.1, ...), custom_call_target="tpu_custom_call" | custom-call | bytes 10000 | tf_op jit(solution)/shard_map/expert/pallas_call | solution.py:252
  13.8 0.2 collective-permute-start.4
  14.0 1.3 %collective-permute-done.4 = bf16[96,1024]{1,0:T(8,128)(2,1)S(1)} collective-permute-done((bf16[96,1024]{1,0:T(8,128)(2,1)S(1)}, bf16[96,1024]{1,0:T(8,128)(2,1)S(1)}, u32[]{:S(2)}, u32[]{:S(2)}) %collective-permute-start.4) | collective-permute-done | bytes 196640 | tf_op jit(solution)/shard_map/ppermute | solution.py:196
  15.4 0.0 collective-permute-done.5.shared_ref
  15.4 0.7 %collective-permute-start.9 = (bf16[3,48,2048]{2,1,0:T(8,128)(2,1)S(1)}, bf16[3,48,2048]{2,1,0:T(8,128)(2,1)S(1)}, u32[]{:S(2)}, u32[]{:S(2)}) collective-permute-start(bf16[3,48,2048]{2,1,0:T(8,128)(2,1)S(1)} %collective-permute-done.5.shared_ref), channel_id=1, source_target_pairs={{4,5},{20,21},{5,4},{21,20},{6,7},{22,23},{7,6},{23,22}} | collective-permute-start | bytes 1769480 | tf_op jit(solution)/shard_map/ppermute | solution.py:208
  16.1 0.1 add_convert_fusion
  16.1 2.0 %collective-permute-start.8 = (bf16[24,1024]{1,0:T(8,128)(2,1)S(1)}, bf16[24,1024]{1,0:T(8,128)(2,1)S(1)}, u32[]{:S(2)}, u32[]{:S(2)}) collective-permute-start(bf16[24,1024]{1,0:T(8,128)(2,1)S(1)} %get-tuple-element.42), channel_id=1, source_target_pairs={{0,24},{4,28},{8,16},{12,20},{16,8},{20,12},{24,0},{28,4},{1,25},{... | collective-permute-start | bytes 147464 | tf_op jit(solution)/shard_map/ppermute | solution.py:196
  18.1 0.1 collective-permute-start.7
  18.3 1.4 %collective-permute-start.6 = (bf16[24,1024]{1,0:T(8,128)(2,1)S(1)}, bf16[24,1024]{1,0:T(8,128)(2,1)S(1)}, u32[]{:S(2)}, u32[]{:S(2)}) collective-permute-start(bf16[24,1024]{1,0:T(8,128)(2,1)S(1)} %get-tuple-element.44), channel_id=1, source_target_pairs={{0,8},{4,12},{8,0},{12,4},{16,24},{20,28},{24,16},{28,20},{1,9},{5... | collective-permute-start | bytes 147464 | tf_op jit(solution)/shard_map/ppermute | solution.py:196
  19.7 0.9 %collective-permute-start.11 = (bf16[3,96,2048]{2,1,0:T(8,128)(2,1)S(1)}, bf16[3,96,2048]{2,1,0:T(8,128)(2,1)S(1)}, u32[]{:S(2)}, u32[]{:S(2)}) collective-permute-start(bf16[3,96,2048]{2,1,0:T(8,128)(2,1)S(1)} %get-tuple-element.41), channel_id=1, source_target_pairs={{12,8},{28,24},{13,9},{29,25},{14,10},{30,26},{15,11},{31,27}} | collective-permute-start | bytes 3538952 | tf_op jit(solution)/shard_map/ppermute | solution.py:200
  20.6 0.1 early.1.early_ref
  20.7 1.1 %collective-permute-done.8.refs_3_ = bf16[24,1024]{1,0:T(8,128)(2,1)S(1)} collective-permute-done((bf16[24,1024]{1,0:T(8,128)(2,1)S(1)}, bf16[24,1024]{1,0:T(8,128)(2,1)S(1)}, u32[]{:S(2)}, u32[]{:S(2)}) %collective-permute-start.8) | collective-permute-done | bytes 49184 | tf_op jit(solution)/shard_map/ppermute | solution.py:196
  21.8 0.5 %collective-permute-done.7.refs_2_ = bf16[24,1024]{1,0:T(8,128)(2,1)S(1)} collective-permute-done((bf16[24,1024]{1,0:T(8,128)(2,1)S(1)}, bf16[24,1024]{1,0:T(8,128)(2,1)S(1)}, u32[]{:S(2)}, u32[]{:S(2)}) %collective-permute-start.7) | collective-permute-done | bytes 49184 | tf_op jit(solution)/shard_map/ppermute | solution.py:196
  22.3 0.6 %collective-permute-done.6.refs_1_ = bf16[24,1024]{1,0:T(8,128)(2,1)S(1)} collective-permute-done((bf16[24,1024]{1,0:T(8,128)(2,1)S(1)}, bf16[24,1024]{1,0:T(8,128)(2,1)S(1)}, u32[]{:S(2)}, u32[]{:S(2)}) %collective-permute-start.6) | collective-permute-done | bytes 49184 | tf_op jit(solution)/shard_map/ppermute | solution.py:196
  22.9 8.6 %collective-permute-done.10.straight_ref = bf16[3,96,2048]{2,1,0:T(8,128)(2,1)S(1)} collective-permute-done((bf16[3,96,2048]{2,1,0:T(8,128)(2,1)S(1)}, bf16[3,96,2048]{2,1,0:T(8,128)(2,1)S(1)}, u32[]{:S(2)}, u32[]{:S(2)}) %collective-permute-start.10) | collective-permute-done | bytes 1179680 | tf_op jit(solution)/shard_map/ppermute | solution.py:200
  31.5 1.4 %combine.1 = bf16[128,2048]{1,0:T(8,128)(2,1)} custom-call(s32[8,128]{1,0:T(8,128)S(1)} %bitcast.4, f32[8,128]{1,0:T(8,128)S(1)} %bitcast.5, bf16[24,1024]{1,0:T(8,128)(2,1)S(1)} %get-tuple-element.35.refs_0_, bf16[24,1024]{1,0:T(8,128)(2,1)S(1)} %collective-permute-done.6.refs_1_, bf16[24,1024]{1,0:T(8,128)(2,1)S(1)} %collective-permute-done.7.refs_2_, ...), custom_call_target="tpu_custom_call" | custom-call | flops 12300000256 | bytes 10000 | tf_op jit(solution)/shard_map/combine/pallas_call | solution.py:283
  32.9 1.0 %late.1 = bf16[3,96,2048]{2,1,0:T(8,128)(2,1)} custom-call(bf16[3,96,2048]{2,1,0:T(8,128)(2,1)} %early.1.early_ref, bf16[3,96,2048]{2,1,0:T(8,128)(2,1)S(1)} %collective-permute-done.10.straight_ref, bf16[3,96,2048]{2,1,0:T(8,128)(2,1)S(1)} %collective-permute-done.11.near_ref), custom_call_target="tpu_custom_call", output_to_operand_aliasing={{}: (0, {})} | custom-call | tf_op jit(solution)/shard_map/late/pallas_call | solution.py:294
  (21 shorter events, 0.1 us)
Async XLA Ops:
  0.6 0.7 %copy-start.4 = (s32[128,8]{0,1:T(8,128)S(1)}, s32[128,8]{0,1:T(8,128)}, u32[]{:S(2)}) copy-start(s32[128,8]{0,1:T(8,128)} %param.8) | copy-start | bytes 12292
  0.6 1.1 %copy-start.3 = (bf16[128,2048]{1,0:T(8,128)(2,1)S(1)}, bf16[128,2048]{1,0:T(8,128)(2,1)}, u32[]{:S(2)}) copy-start(bf16[128,2048]{1,0:T(8,128)(2,1)} %tok_ref.1) | copy-start | bytes 1572868
  1.7 0.7 %copy-start.7 = (f32[8,128]{1,0:T(8,128)S(1)}, f32[8,128]{1,0:T(8,128)}, u32[]{:S(2)}) copy-start(f32[8,128]{1,0:T(8,128)} %begin.1.begun_ref) | copy-start | bytes 12292
  2.4 5.0 %copy-start = (bf16[192,2048]{1,0:T(8,128)(2,1)S(1)}, bf16[192,2048]{1,0:T(8,128)(2,1)}, u32[]{:S(2)}) copy-start(bf16[192,2048]{1,0:T(8,128)(2,1)} %gate_ref.2) | copy-start | bytes 2359300
  2.4 5.0 %copy-start.1 = (bf16[192,2048]{1,0:T(8,128)(2,1)S(1)}, bf16[192,2048]{1,0:T(8,128)(2,1)}, u32[]{:S(2)}) copy-start(bf16[192,2048]{1,0:T(8,128)(2,1)} %up_ref.2) | copy-start | bytes 2359300
  2.4 5.0 %copy-start.2 = (bf16[192,2048]{1,0:T(8,128)(2,1)S(1)}, bf16[192,2048]{1,0:T(8,128)(2,1)}, u32[]{:S(2)}) copy-start(bf16[192,2048]{1,0:T(8,128)(2,1)} %down_ref.2) | copy-start | bytes 2359300
  2.4 5.0 %copy-start.6 = (s32[2,3,96]{2,0,1:T(2,128)S(1)}, s32[2,3,96]{2,0,1:T(2,128)}, u32[]{:S(2)}) copy-start(s32[2,3,96]{2,0,1:T(2,128)} %param.13) | copy-start | bytes 6916
  2.8 8.6 %collective-permute-start.2 = (bf16[24,1024]{1,0:T(8,128)(2,1)S(1)}, bf16[24,1024]{1,0:T(8,128)(2,1)S(1)}, u32[]{:S(2)}, u32[]{:S(2)}) collective-permute-start(bf16[24,1024]{1,0:T(8,128)(2,1)S(1)} %get-tuple-element.23), channel_id=1, source_target_pairs={{0,24},{4,28},{8,16},{12,20},{16,8},{20,12},{24,0},{28,4},{1,25},{... | collective-permute-start | bytes 147464 | tf_op jit(solution)/shard_map/ppermute | solution.py:196
  6.8 4.6 %collective-permute-start.1 = (bf16[24,1024]{1,0:T(8,128)(2,1)S(1)}, bf16[24,1024]{1,0:T(8,128)(2,1)S(1)}, u32[]{:S(2)}, u32[]{:S(2)}) collective-permute-start(bf16[24,1024]{1,0:T(8,128)(2,1)S(1)} %get-tuple-element.23), channel_id=1, source_target_pairs={{0,16},{4,20},{8,24},{12,28},{16,0},{20,4},{24,8},{28,12},{1,17},{... | collective-permute-start | bytes 147464 | tf_op jit(solution)/shard_map/ppermute | solution.py:196
  7.3 4.1 %collective-permute-start = (bf16[24,1024]{1,0:T(8,128)(2,1)S(1)}, bf16[24,1024]{1,0:T(8,128)(2,1)S(1)}, u32[]{:S(2)}, u32[]{:S(2)}) collective-permute-start(bf16[24,1024]{1,0:T(8,128)(2,1)S(1)} %get-tuple-element.22), channel_id=1, source_target_pairs={{0,8},{4,12},{8,0},{12,4},{16,24},{20,28},{24,16},{28,20},{1,9},{5... | collective-permute-start | bytes 147464 | tf_op jit(solution)/shard_map/ppermute | solution.py:196
  7.4 7.9 %collective-permute-start.5 = (bf16[3,48,2048]{2,1,0:T(8,128)(2,1)S(1)}, bf16[3,48,2048]{2,1,0:T(8,128)(2,1)S(1)}, u32[]{:S(2)}, u32[]{:S(2)}) collective-permute-start(bf16[3,48,2048]{2,1,0:T(8,128)(2,1)S(1)} %get-tuple-element.29), channel_id=1, source_target_pairs={{12,4},{28,20},{13,5},{29,21},{14,6},{30,22},{15,7},{31,23}} | collective-permute-start | bytes 1769480 | tf_op jit(solution)/shard_map/ppermute | solution.py:200
  8.2 23.3 %collective-permute-start.10 = (bf16[3,96,2048]{2,1,0:T(8,128)(2,1)S(1)}, bf16[3,96,2048]{2,1,0:T(8,128)(2,1)S(1)}, u32[]{:S(2)}, u32[]{:S(2)}) collective-permute-start(bf16[3,96,2048]{2,1,0:T(8,128)(2,1)S(1)} %get-tuple-element.34), channel_id=1, source_target_pairs={{12,0},{28,16},{13,1},{29,17},{14,2},{30,18},{15,3},{31,19}} | collective-permute-start | bytes 3538952 | tf_op jit(solution)/shard_map/ppermute | solution.py:200
  11.4 1.5 %collective-permute-start.3 = (bf16[96,1024]{1,0:T(8,128)(2,1)S(1)}, bf16[96,1024]{1,0:T(8,128)(2,1)S(1)}, u32[]{:S(2)}, u32[]{:S(2)}) collective-permute-start(bf16[96,1024]{1,0:T(8,128)(2,1)S(1)} %constant_dynamic-update-slice_fusion.mine_ref), channel_id=1, source_target_pairs={{0,4},{4,0},{8,12},{12,8},{16,20},{20,16},{24,28},{28,24},{1,5},{5... | collective-permute-start | bytes 589832 | tf_op jit(solution)/shard_map/ppermute | solution.py:196
  13.8 1.5 %collective-permute-start.4 = (bf16[96,1024]{1,0:T(8,128)(2,1)S(1)}, bf16[96,1024]{1,0:T(8,128)(2,1)S(1)}, u32[]{:S(2)}, u32[]{:S(2)}) collective-permute-start(bf16[96,1024]{1,0:T(8,128)(2,1)S(1)} %get-tuple-element.25), channel_id=1, source_target_pairs={{0,4},{4,0},{8,12},{12,8},{16,20},{20,16},{24,28},{28,24},{1,5},{5... | collective-permute-start | bytes 589832 | tf_op jit(solution)/shard_map/ppermute | solution.py:196
  15.4 4.3 %collective-permute-start.9 = (bf16[3,48,2048]{2,1,0:T(8,128)(2,1)S(1)}, bf16[3,48,2048]{2,1,0:T(8,128)(2,1)S(1)}, u32[]{:S(2)}, u32[]{:S(2)}) collective-permute-start(bf16[3,48,2048]{2,1,0:T(8,128)(2,1)S(1)} %collective-permute-done.5.shared_ref), channel_id=1, source_target_pairs={{4,5},{20,21},{5,4},{21,20},{6,7},{22,23},{7,6},{23,22}} | collective-permute-start | bytes 1769480 | tf_op jit(solution)/shard_map/ppermute | solution.py:208
  16.1 5.6 %collective-permute-start.8 = (bf16[24,1024]{1,0:T(8,128)(2,1)S(1)}, bf16[24,1024]{1,0:T(8,128)(2,1)S(1)}, u32[]{:S(2)}, u32[]{:S(2)}) collective-permute-start(bf16[24,1024]{1,0:T(8,128)(2,1)S(1)} %get-tuple-element.42), channel_id=1, source_target_pairs={{0,24},{4,28},{8,16},{12,20},{16,8},{20,12},{24,0},{28,4},{1,25},{... | collective-permute-start | bytes 147464 | tf_op jit(solution)/shard_map/ppermute | solution.py:196
  18.1 4.1 %collective-permute-start.7 = (bf16[24,1024]{1,0:T(8,128)(2,1)S(1)}, bf16[24,1024]{1,0:T(8,128)(2,1)S(1)}, u32[]{:S(2)}, u32[]{:S(2)}) collective-permute-start(bf16[24,1024]{1,0:T(8,128)(2,1)S(1)} %get-tuple-element.43), channel_id=1, source_target_pairs={{0,16},{4,20},{8,24},{12,28},{16,0},{20,4},{24,8},{28,12},{1,17},{... | collective-permute-start | bytes 147464 | tf_op jit(solution)/shard_map/ppermute | solution.py:196
  18.3 4.6 %collective-permute-start.6 = (bf16[24,1024]{1,0:T(8,128)(2,1)S(1)}, bf16[24,1024]{1,0:T(8,128)(2,1)S(1)}, u32[]{:S(2)}, u32[]{:S(2)}) collective-permute-start(bf16[24,1024]{1,0:T(8,128)(2,1)S(1)} %get-tuple-element.44), channel_id=1, source_target_pairs={{0,8},{4,12},{8,0},{12,4},{16,24},{20,28},{24,16},{28,20},{1,9},{5... | collective-permute-start | bytes 147464 | tf_op jit(solution)/shard_map/ppermute | solution.py:196
  19.7 11.8 %copy-start.5 = (f32[128,8]{0,1:T(8,128)S(1)}, f32[128,8]{0,1:T(8,128)}, u32[]{:S(2)}) copy-start(f32[128,8]{0,1:T(8,128)} %param.9) | copy-start | bytes 12292
  19.7 13.2 %collective-permute-start.11 = (bf16[3,96,2048]{2,1,0:T(8,128)(2,1)S(1)}, bf16[3,96,2048]{2,1,0:T(8,128)(2,1)S(1)}, u32[]{:S(2)}, u32[]{:S(2)}) collective-permute-start(bf16[3,96,2048]{2,1,0:T(8,128)(2,1)S(1)} %get-tuple-element.41), channel_id=1, source_target_pairs={{12,8},{28,24},{13,9},{29,25},{14,10},{30,26},{15,11},{31,27}} | collective-permute-start | bytes 3538952 | tf_op jit(solution)/shard_map/ppermute | solution.py:200

commit v15 on v14

--- a/solution.py
+++ b/solution.py
@@ -23,7 +23,7 @@
 
 def cost(microseconds):
     return pl.CostEstimate(
-        flops=int(microseconds * 10**9), bytes_accessed=10**4, transcendentals=0
+        flops=microseconds * 10**9, bytes_accessed=10**4, transcendentals=0
     )
 
 
@@ -97,7 +97,7 @@
         copy.wait()
 
 
-def early_kernel(shared_ref, swapped_ref, out_ref, sems):
+def early_kernel(shared_ref, swapped_ref, first_ref, near_ref, out_ref, sems):
     position = lax.axis_index("expert") % GROUP
     parity = lax.axis_index("replica") % 2
     half = shared_ref.shape[1]
@@ -107,17 +107,21 @@
         def _():
             place_rows([(shared_ref, half * even), (swapped_ref, half * (1 - even))], out_ref, sems)
 
-
-def late_kernel(early_ref, straight_ref, near_ref, out_ref, sems):
-    position = lax.axis_index("expert") % GROUP
-
     @pl.when(jnp.logical_or(position == 0, position == 3))
     def _():
-        place_rows([(straight_ref, 0)], out_ref, sems)
+        place_rows([(first_ref, 0)], out_ref, sems)
 
     @pl.when(position == 2)
     def _():
         place_rows([(near_ref, 0)], out_ref, sems)
+
+
+def late_kernel(early_ref, second_ref, out_ref, sems):
+    position = lax.axis_index("expert") % GROUP
+
+    @pl.when(jnp.logical_or(position == 0, position == 3))
+    def _():
+        place_rows([(second_ref, out_ref.shape[1] - second_ref.shape[1])], out_ref, sems)
 
 
 def begin_kernel(out_ref):
@@ -184,6 +188,7 @@
     plan = jnp.transpose(move_plan, (1, 0, 2))
     weights = (old_gate, old_up, old_down)
     half = most // 2
+    lead = most // 3 * 2
 
     def shape(*dims, dtype=BF16):
         return jax.ShapeDtypeStruct(dims, dtype)
@@ -238,10 +243,11 @@
     pairs = [(j, k) for j in range(experts) for k in (0, 2)]
     mine = [parcels[0]] + [send(parcels[j], j, k) for j, k in pairs[1:]]
     held, _ = lax.optimization_barrier((weights, parcels))
-    wanted = [(1, half, None), (0, most, 0), (2, most, 0)]
+    wanted = [(1, half, None), (0, lead, 0), (0, most - lead, lead), (2, most, 0)]
     chosen = select(wanted, held)
     shared = migrate(chosen[0], 1)
-    straight = migrate(chosen[1], 0)
+    first = migrate(chosen[1], 0)
+    near = migrate(chosen[3], 2)
     mine = jnp.concatenate(mine, axis=0)
     other = send(mine, 0, 1)
 
@@ -266,19 +272,21 @@
         send(block, -j, k) for (j, k), block in zip(pairs[1:], pieces[1:])
     ]
     swapped = swap(shared, 1)
-    swapped, near = lax.optimization_barrier((swapped, chosen[2]))
-    near = migrate(near, 2)
+    beside = len(pairs) // 2
+    back[beside], near = lax.optimization_barrier((back[beside], near))
+    last, _ = lax.optimization_barrier((chosen[2], summed))
+    second = migrate(last, 0)
 
     early = pl.pallas_call(
         early_kernel,
         out_shape=shape(3, most, width),
-        in_specs=[HBM] * 2,
+        in_specs=[HBM] * 4,
         out_specs=HBM,
         scratch_shapes=[pltpu.SemaphoreType.DMA((6,))],
         compiler_params=params(),
         name="early",
-    )(shared, swapped)
-    back, early, straight = lax.optimization_barrier((back, early, straight))
+    )(shared, swapped, first, near)
+    back, early = lax.optimization_barrier((back, early))
 
     mixed = pl.pallas_call(
         functools.partial(combine_kernel, experts),
@@ -287,20 +295,20 @@
         out_specs=VMEM,
         scratch_shapes=[pltpu.VMEM((len(back) * STRIDE, width // 2), BF16)],
         compiler_params=params(14 + experts),
-        cost_estimate=cost(12.3),
+        cost_estimate=cost(5),
         name="combine",
     )(expert_ids.T, combine.T, *back)
 
     arrived = pl.pallas_call(
         late_kernel,
         out_shape=shape(3, most, width),
-        in_specs=[HBM] * 3,
+        in_specs=[HBM] * 2,
         out_specs=HBM,
         input_output_aliases={0: 0},
         scratch_shapes=[pltpu.SemaphoreType.DMA((3,))],
         compiler_params=params(),
         name="late",
-    )(early, straight, near)
+    )(early, second)
     return mixed, arrived
 
 

time: 34.2 us -> 34.7 us (1.015)
  waiting for transfers between devices: 15.5 us -> 11.6 us
  starting transfers between devices: 12 us -> 15.8 us
  Pallas kernels: 4.48 us -> 5.06 us
    ppermute x8, waiting for transfers between devices: 6.86 us -> 4.36 us  [send(): return lax.ppermute(block, 'expert', route)]
    ppermute x8, starting transfers between devices: 8.43 us -> 10.9 us  [send(): return lax.ppermute(block, 'expert', route)]
    ppermute x3 -> x4, waiting for transfers between devices: 8.6 us -> 7.21 us  [migrate(): return lax.ppermute(block, 'expert', route)]
    ppermute x3 -> x4, starting transfers between devices: 2.85 us -> 4.13 us  [migrate(): return lax.ppermute(block, 'expert', route)]
    pallas_call x1, Pallas kernels: 0.09 us -> 0.93 us  [on_device(): pl.pallas_call(early_kernel, out_shape=shape(3, most, width), in_specs=[H...]
  transfers between devices with their start and end apart: 12 -> 13, of which waited for: 7 -> 5; matrix products, arithmetic and copies ran while one was open for 0% -> 0% of each run, Pallas kernels for 7% -> 10%
where the time goes in v15:
time: 34.7 us; the launch traced here: 34.4 us
  starting transfers between devices  15.8 us (46%)
  waiting for transfers between devices  11.6 us (33%)
  Pallas kernels  5.06 us (15%)
  local copies, waits for them, and re-layouts  1.19 us (3%)
  between operations  0.82 us (2%)
    ppermute x8, starting transfers between devices, send(): return lax.ppermute(block, 'expert', route)  10.9 us
    ppermute x4, waiting for transfers between devices, migrate(): return lax.ppermute(block, 'expert', route)  7.21 us
    ppermute x8, waiting for transfers between devices, send(): return lax.ppermute(block, 'expert', route)  4.36 us
    ppermute x4, starting transfers between devices, migrate(): return lax.ppermute(block, 'expert', route)  4.13 us
    pallas_call x1, Pallas kernels, on_device(): pl.pallas_call(functools.partial(combine_kernel, experts), out_shape=shap...  1.41 us
    unnamed x19, local copies, waits for them, and re-layouts  1.17 us
    pallas_call x1, Pallas kernels, on_device(): pl.pallas_call(early_kernel, out_shape=shape(3, most, width), in_specs=[H...  0.93 us
    pallas_call x1, Pallas kernels, on_device(): pl.pallas_call(expert_kernel, grid=(total // step,), out_shape=[shape(tot...  0.93 us
  transfers between devices with their start and end apart: 13, of which 5 were waited for; matrix products, arithmetic and copies ran while one was open for 0% of the time, Pallas kernels for 10%

profile of v15, /device:TPU:0, one launch (start us, length us, event | category | flops | bytes accessed | tf_op | source)
XLA Modules:
  0.0 34.4 jit_solution(3005381723244276103)
XLA Ops:
  0.6 0.6 %begin.1.begun_ref = f32[8,128]{1,0:T(8,128)} custom-call(), custom_call_target="tpu_custom_call" | custom-call | flops 5000000000 | bytes 10000 | tf_op jit(solution)/shard_map/begin/pallas_call | solution.py:226
  1.2 0.1 copy-done.4
  1.3 0.4 %copy-done.3 = bf16[128,2048]{1,0:T(8,128)(2,1)S(1)} copy-done((bf16[128,2048]{1,0:T(8,128)(2,1)S(1)}, bf16[128,2048]{1,0:T(8,128)(2,1)}, u32[]{:S(2)}) %copy-start.3) | copy-done | bytes 524312
  1.7 0.7 %copy-done.7 = f32[8,128]{1,0:T(8,128)S(1)} copy-done((f32[8,128]{1,0:T(8,128)S(1)}, f32[8,128]{1,0:T(8,128)}, u32[]{:S(2)}) %copy-start.7) | copy-done | bytes 4120
  2.4 0.4 %dispatch.1 = (bf16[24,1024]{1,0:T(8,128)(2,1)S(1)}, bf16[24,1024]{1,0:T(8,128)(2,1)S(1)}) custom-call(s32[8,128]{1,0:T(8,128)S(1)} %bitcast.3, bf16[128,2048]{1,0:T(8,128)(2,1)S(1)} %copy-done.3, f32[8,128]{1,0:T(8,128)S(1)} %copy-done.7), custom_call_target="tpu_custom_call" | custom-call | flops 2000000000 | bytes 10000 | tf_op jit(solution)/shard_map/dispatch/pallas_call | solution.py:233
  2.8 4.0 %collective-permute-start.2 = (bf16[24,1024]{1,0:T(8,128)(2,1)S(1)}, bf16[24,1024]{1,0:T(8,128)(2,1)S(1)}, u32[]{:S(2)}, u32[]{:S(2)}) collective-permute-start(bf16[24,1024]{1,0:T(8,128)(2,1)S(1)} %get-tuple-element.24), channel_id=1, source_target_pairs={{0,24},{4,28},{8,16},{12,20},{16,8},{20,12},{24,0},{28,4},{1,25},{... | collective-permute-start | bytes 147464 | tf_op jit(solution)/shard_map/ppermute | solution.py:201
  6.8 0.5 %collective-permute-start.1 = (bf16[24,1024]{1,0:T(8,128)(2,1)S(1)}, bf16[24,1024]{1,0:T(8,128)(2,1)S(1)}, u32[]{:S(2)}, u32[]{:S(2)}) collective-permute-start(bf16[24,1024]{1,0:T(8,128)(2,1)S(1)} %get-tuple-element.24), channel_id=1, source_target_pairs={{0,16},{4,20},{8,24},{12,28},{16,0},{20,4},{24,8},{28,12},{1,17},{... | collective-permute-start | bytes 147464 | tf_op jit(solution)/shard_map/ppermute | solution.py:201
  7.3 0.1 collective-permute-start
  7.4 0.7 %collective-permute-start.5 = (bf16[3,48,2048]{2,1,0:T(8,128)(2,1)S(1)}, bf16[3,48,2048]{2,1,0:T(8,128)(2,1)S(1)}, u32[]{:S(2)}, u32[]{:S(2)}) collective-permute-start(bf16[3,48,2048]{2,1,0:T(8,128)(2,1)S(1)} %get-tuple-element.30), channel_id=1, source_target_pairs={{12,4},{28,20},{13,5},{29,21},{14,6},{30,22},{15,7},{31,23}} | collective-permute-start | bytes 1769480 | tf_op jit(solution)/shard_map/ppermute | solution.py:205
  8.2 0.7 %collective-permute-start.8 = (bf16[3,96,2048]{2,1,0:T(8,128)(2,1)S(1)}, bf16[3,96,2048]{2,1,0:T(8,128)(2,1)S(1)}, u32[]{:S(2)}, u32[]{:S(2)}) collective-permute-start(bf16[3,96,2048]{2,1,0:T(8,128)(2,1)S(1)} %get-tuple-element.32), channel_id=1, source_target_pairs={{12,8},{28,24},{13,9},{29,25},{14,10},{30,26},{15,11},{31,27}} | collective-permute-start | bytes 3538952 | tf_op jit(solution)/shard_map/ppermute | solution.py:205
  8.9 2.4 %collective-permute-done = bf16[24,1024]{1,0:T(8,128)(2,1)S(1)} collective-permute-done((bf16[24,1024]{1,0:T(8,128)(2,1)S(1)}, bf16[24,1024]{1,0:T(8,128)(2,1)S(1)}, u32[]{:S(2)}, u32[]{:S(2)}) %collective-permute-start) | collective-permute-done | bytes 49184 | tf_op jit(solution)/shard_map/ppermute | solution.py:201
  11.4 0.0 collective-permute-done.2
  11.4 0.1 collective-permute-start.3
  11.5 1.4 %collective-permute-done.3.other_ref = bf16[96,1024]{1,0:T(8,128)(2,1)S(1)} collective-permute-done((bf16[96,1024]{1,0:T(8,128)(2,1)S(1)}, bf16[96,1024]{1,0:T(8,128)(2,1)S(1)}, u32[]{:S(2)}, u32[]{:S(2)}) %collective-permute-start.3) | collective-permute-done | bytes 196640 | tf_op jit(solution)/shard_map/ppermute | solution.py:201
  12.9 0.9 %expert.1 = (f32[96,1024]{1,0:T(8,128)S(1)}, bf16[96,1024]{1,0:T(8,128)(2,1)S(1)}) custom-call(bf16[96,1024]{1,0:T(8,128)(2,1)S(1)} %constant_dynamic-update-slice_fusion.mine_ref, bf16[96,1024]{1,0:T(8,128)(2,1)S(1)} %collective-permute-done.3.other_ref, bf16[192,2048]{1,0:T(8,128)(2,1)S(1)} %copy-done, bf16[192,2048]{1,0:T(8,128)(2,1)S(1)} %copy-done.1, ...), custom_call_target="tpu_custom_call" | custom-call | bytes 10000 | tf_op jit(solution)/shard_map/expert/pallas_call | solution.py:258
  13.8 0.2 collective-permute-start.4
  14.0 1.3 %collective-permute-start.11 = (bf16[3,64,2048]{2,1,0:T(8,128)(2,1)S(1)}, bf16[3,64,2048]{2,1,0:T(8,128)(2,1)S(1)}, u32[]{:S(2)}, u32[]{:S(2)}) collective-permute-start(bf16[3,64,2048]{2,1,0:T(8,128)(2,1)S(1)} %get-tuple-element.35), channel_id=1, source_target_pairs={{12,0},{28,16},{13,1},{29,17},{14,2},{30,18},{15,3},{31,19}} | collective-permute-start | bytes 2359304 | tf_op jit(solution)/shard_map/ppermute | solution.py:205
  15.3 0.0 collective-permute-done.4
  15.4 0.0 collective-permute-done.5.shared_ref
  15.4 0.7 %collective-permute-start.10 = (bf16[3,48,2048]{2,1,0:T(8,128)(2,1)S(1)}, bf16[3,48,2048]{2,1,0:T(8,128)(2,1)S(1)}, u32[]{:S(2)}, u32[]{:S(2)}) collective-permute-start(bf16[3,48,2048]{2,1,0:T(8,128)(2,1)S(1)} %collective-permute-done.5.shared_ref), channel_id=1, source_target_pairs={{4,5},{20,21},{5,4},{21,20},{6,7},{22,23},{7,6},{23,22}} | collective-permute-start | bytes 1769480 | tf_op jit(solution)/shard_map/ppermute | solution.py:213
  16.1 1.6 %collective-permute-start.7 = (bf16[24,1024]{1,0:T(8,128)(2,1)S(1)}, bf16[24,1024]{1,0:T(8,128)(2,1)S(1)}, u32[]{:S(2)}, u32[]{:S(2)}) collective-permute-start(bf16[24,1024]{1,0:T(8,128)(2,1)S(1)} %get-tuple-element.45), channel_id=1, source_target_pairs={{0,16},{4,20},{8,24},{12,28},{16,0},{20,4},{24,8},{28,12},{1,17},{... | collective-permute-start | bytes 147464 | tf_op jit(solution)/shard_map/ppermute | solution.py:201
  17.7 2.1 %collective-permute-start.9 = (bf16[24,1024]{1,0:T(8,128)(2,1)S(1)}, bf16[24,1024]{1,0:T(8,128)(2,1)S(1)}, u32[]{:S(2)}, u32[]{:S(2)}) collective-permute-start(bf16[24,1024]{1,0:T(8,128)(2,1)S(1)} %get-tuple-element.44), channel_id=1, source_target_pairs={{0,24},{4,28},{8,16},{12,20},{16,8},{20,12},{24,0},{28,4},{1,25},{... | collective-permute-start | bytes 147464 | tf_op jit(solution)/shard_map/ppermute | solution.py:201
  19.8 0.5 %collective-permute-done.7.refs_2_ = bf16[24,1024]{1,0:T(8,128)(2,1)S(1)} collective-permute-done((bf16[24,1024]{1,0:T(8,128)(2,1)S(1)}, bf16[24,1024]{1,0:T(8,128)(2,1)S(1)}, u32[]{:S(2)}, u32[]{:S(2)}) %collective-permute-start.7) | collective-permute-done | bytes 49184 | tf_op jit(solution)/shard_map/ppermute | solution.py:201
  20.3 2.4 %collective-permute-start.6 = (bf16[24,1024]{1,0:T(8,128)(2,1)S(1)}, bf16[24,1024]{1,0:T(8,128)(2,1)S(1)}, u32[]{:S(2)}, u32[]{:S(2)}) collective-permute-start(bf16[24,1024]{1,0:T(8,128)(2,1)S(1)} %get-tuple-element.46), channel_id=1, source_target_pairs={{0,8},{4,12},{8,0},{12,4},{16,24},{20,28},{24,16},{28,20},{1,9},{5... | collective-permute-start | bytes 147464 | tf_op jit(solution)/shard_map/ppermute | solution.py:201
  22.7 1.4 %collective-permute-start.12 = (bf16[3,32,2048]{2,1,0:T(8,128)(2,1)S(1)}, bf16[3,32,2048]{2,1,0:T(8,128)(2,1)S(1)}, u32[]{:S(2)}, u32[]{:S(2)}) collective-permute-start(bf16[3,32,2048]{2,1,0:T(8,128)(2,1)S(1)} %get-tuple-element.43), channel_id=1, source_target_pairs={{12,0},{28,16},{13,1},{29,17},{14,2},{30,18},{15,3},{31,19}} | collective-permute-start | bytes 1179656 | tf_op jit(solution)/shard_map/ppermute | solution.py:205
  24.1 4.3 %collective-permute-done.11.first_ref = bf16[3,64,2048]{2,1,0:T(8,128)(2,1)S(1)} collective-permute-done((bf16[3,64,2048]{2,1,0:T(8,128)(2,1)S(1)}, bf16[3,64,2048]{2,1,0:T(8,128)(2,1)S(1)}, u32[]{:S(2)}, u32[]{:S(2)}) %collective-permute-start.11) | collective-permute-done | bytes 786464 | tf_op jit(solution)/shard_map/ppermute | solution.py:205
  28.4 0.0 collective-permute-done.10.swapped_ref
  28.4 0.9 %early.1.early_ref = bf16[3,96,2048]{2,1,0:T(8,128)(2,1)} custom-call(bf16[3,48,2048]{2,1,0:T(8,128)(2,1)S(1)} %collective-permute-done.5.shared_ref, bf16[3,48,2048]{2,1,0:T(8,128)(2,1)S(1)} %collective-permute-done.10.swapped_ref, bf16[3,64,2048]{2,1,0:T(8,128)(2,1)S(1)} %collective-permute-done.11.first_ref, ...), custom_call_target="tpu_custom_call" | custom-call | tf_op jit(solution)/shard_map/early/pallas_call | solution.py:280
  29.3 0.0 collective-permute-done.9.refs_3_
  29.4 1.4 %combine.1 = bf16[128,2048]{1,0:T(8,128)(2,1)} custom-call(s32[8,128]{1,0:T(8,128)S(1)} %bitcast.4, f32[8,128]{1,0:T(8,128)S(1)} %bitcast.5, bf16[24,1024]{1,0:T(8,128)(2,1)S(1)} %get-tuple-element.37.refs_0_, bf16[24,1024]{1,0:T(8,128)(2,1)S(1)} %collective-permute-done.6.refs_1_, bf16[24,1024]{1,0:T(8,128)(2,1)S(1)} %collective-permute-done.7.refs_2_, ...), custom_call_target="tpu_custom_call" | custom-call | flops 5000000000 | bytes 10000 | tf_op jit(solution)/shard_map/combine/pallas_call | solution.py:291
  30.8 2.9 %collective-permute-done.12.second_ref = bf16[3,32,2048]{2,1,0:T(8,128)(2,1)S(1)} collective-permute-done((bf16[3,32,2048]{2,1,0:T(8,128)(2,1)S(1)}, bf16[3,32,2048]{2,1,0:T(8,128)(2,1)S(1)}, u32[]{:S(2)}, u32[]{:S(2)}) %collective-permute-start.12) | collective-permute-done | bytes 393248 | tf_op jit(solution)/shard_map/ppermute | solution.py:205
  33.7 0.8 %late.1 = bf16[3,96,2048]{2,1,0:T(8,128)(2,1)} custom-call(bf16[3,96,2048]{2,1,0:T(8,128)(2,1)} %early.1.early_ref, bf16[3,32,2048]{2,1,0:T(8,128)(2,1)S(1)} %collective-permute-done.12.second_ref), custom_call_target="tpu_custom_call", output_to_operand_aliasing={{}: (0, {})} | custom-call | tf_op jit(solution)/shard_map/late/pallas_call | solution.py:302
  (23 shorter events, 0.1 us)
Async XLA Ops:
  0.6 0.7 %copy-start.4 = (s32[128,8]{0,1:T(8,128)S(1)}, s32[128,8]{0,1:T(8,128)}, u32[]{:S(2)}) copy-start(s32[128,8]{0,1:T(8,128)} %param.8) | copy-start | bytes 12292
  0.6 1.1 %copy-start.3 = (bf16[128,2048]{1,0:T(8,128)(2,1)S(1)}, bf16[128,2048]{1,0:T(8,128)(2,1)}, u32[]{:S(2)}) copy-start(bf16[128,2048]{1,0:T(8,128)(2,1)} %tok_ref.1) | copy-start | bytes 1572868
  1.7 0.7 %copy-start.7 = (f32[8,128]{1,0:T(8,128)S(1)}, f32[8,128]{1,0:T(8,128)}, u32[]{:S(2)}) copy-start(f32[8,128]{1,0:T(8,128)} %begin.1.begun_ref) | copy-start | bytes 12292
  2.4 5.0 %copy-start = (bf16[192,2048]{1,0:T(8,128)(2,1)S(1)}, bf16[192,2048]{1,0:T(8,128)(2,1)}, u32[]{:S(2)}) copy-start(bf16[192,2048]{1,0:T(8,128)(2,1)} %gate_ref.2) | copy-start | bytes 2359300
  2.4 5.0 %copy-start.1 = (bf16[192,2048]{1,0:T(8,128)(2,1)S(1)}, bf16[192,2048]{1,0:T(8,128)(2,1)}, u32[]{:S(2)}) copy-start(bf16[192,2048]{1,0:T(8,128)(2,1)} %up_ref.2) | copy-start | bytes 2359300
  2.4 5.0 %copy-start.2 = (bf16[192,2048]{1,0:T(8,128)(2,1)S(1)}, bf16[192,2048]{1,0:T(8,128)(2,1)}, u32[]{:S(2)}) copy-start(bf16[192,2048]{1,0:T(8,128)(2,1)} %down_ref.2) | copy-start | bytes 2359300
  2.4 5.0 %copy-start.6 = (s32[2,3,96]{2,0,1:T(2,128)S(1)}, s32[2,3,96]{2,0,1:T(2,128)}, u32[]{:S(2)}) copy-start(s32[2,3,96]{2,0,1:T(2,128)} %param.13) | copy-start | bytes 6916
  2.8 8.6 %collective-permute-start.2 = (bf16[24,1024]{1,0:T(8,128)(2,1)S(1)}, bf16[24,1024]{1,0:T(8,128)(2,1)S(1)}, u32[]{:S(2)}, u32[]{:S(2)}) collective-permute-start(bf16[24,1024]{1,0:T(8,128)(2,1)S(1)} %get-tuple-element.24), channel_id=1, source_target_pairs={{0,24},{4,28},{8,16},{12,20},{16,8},{20,12},{24,0},{28,4},{1,25},{... | collective-permute-start | bytes 147464 | tf_op jit(solution)/shard_map/ppermute | solution.py:201
  6.8 4.6 %collective-permute-start.1 = (bf16[24,1024]{1,0:T(8,128)(2,1)S(1)}, bf16[24,1024]{1,0:T(8,128)(2,1)S(1)}, u32[]{:S(2)}, u32[]{:S(2)}) collective-permute-start(bf16[24,1024]{1,0:T(8,128)(2,1)S(1)} %get-tuple-element.24), channel_id=1, source_target_pairs={{0,16},{4,20},{8,24},{12,28},{16,0},{20,4},{24,8},{28,12},{1,17},{... | collective-permute-start | bytes 147464 | tf_op jit(solution)/shard_map/ppermute | solution.py:201
  7.3 4.1 %collective-permute-start = (bf16[24,1024]{1,0:T(8,128)(2,1)S(1)}, bf16[24,1024]{1,0:T(8,128)(2,1)S(1)}, u32[]{:S(2)}, u32[]{:S(2)}) collective-permute-start(bf16[24,1024]{1,0:T(8,128)(2,1)S(1)} %get-tuple-element.23), channel_id=1, source_target_pairs={{0,8},{4,12},{8,0},{12,4},{16,24},{20,28},{24,16},{28,20},{1,9},{5... | collective-permute-start | bytes 147464 | tf_op jit(solution)/shard_map/ppermute | solution.py:201
  7.4 7.9 %collective-permute-start.5 = (bf16[3,48,2048]{2,1,0:T(8,128)(2,1)S(1)}, bf16[3,48,2048]{2,1,0:T(8,128)(2,1)S(1)}, u32[]{:S(2)}, u32[]{:S(2)}) collective-permute-start(bf16[3,48,2048]{2,1,0:T(8,128)(2,1)S(1)} %get-tuple-element.30), channel_id=1, source_target_pairs={{12,4},{28,20},{13,5},{29,21},{14,6},{30,22},{15,7},{31,23}} | collective-permute-start | bytes 1769480 | tf_op jit(solution)/shard_map/ppermute | solution.py:205
  8.2 14.5 %collective-permute-start.8 = (bf16[3,96,2048]{2,1,0:T(8,128)(2,1)S(1)}, bf16[3,96,2048]{2,1,0:T(8,128)(2,1)S(1)}, u32[]{:S(2)}, u32[]{:S(2)}) collective-permute-start(bf16[3,96,2048]{2,1,0:T(8,128)(2,1)S(1)} %get-tuple-element.32), channel_id=1, source_target_pairs={{12,8},{28,24},{13,9},{29,25},{14,10},{30,26},{15,11},{31,27}} | collective-permute-start | bytes 3538952 | tf_op jit(solution)/shard_map/ppermute | solution.py:205
  11.4 1.5 %collective-permute-start.3 = (bf16[96,1024]{1,0:T(8,128)(2,1)S(1)}, bf16[96,1024]{1,0:T(8,128)(2,1)S(1)}, u32[]{:S(2)}, u32[]{:S(2)}) collective-permute-start(bf16[96,1024]{1,0:T(8,128)(2,1)S(1)} %constant_dynamic-update-slice_fusion.mine_ref), channel_id=1, source_target_pairs={{0,4},{4,0},{8,12},{12,8},{16,20},{20,16},{24,28},{28,24},{1,5},{5... | collective-permute-start | bytes 589832 | tf_op jit(solution)/shard_map/ppermute | solution.py:201
  13.8 1.5 %collective-permute-start.4 = (bf16[96,1024]{1,0:T(8,128)(2,1)S(1)}, bf16[96,1024]{1,0:T(8,128)(2,1)S(1)}, u32[]{:S(2)}, u32[]{:S(2)}) collective-permute-start(bf16[96,1024]{1,0:T(8,128)(2,1)S(1)} %get-tuple-element.26), channel_id=1, source_target_pairs={{0,4},{4,0},{8,12},{12,8},{16,20},{20,16},{24,28},{28,24},{1,5},{5... | collective-permute-start | bytes 589832 | tf_op jit(solution)/shard_map/ppermute | solution.py:201
  14.0 14.3 %collective-permute-start.11 = (bf16[3,64,2048]{2,1,0:T(8,128)(2,1)S(1)}, bf16[3,64,2048]{2,1,0:T(8,128)(2,1)S(1)}, u32[]{:S(2)}, u32[]{:S(2)}) collective-permute-start(bf16[3,64,2048]{2,1,0:T(8,128)(2,1)S(1)} %get-tuple-element.35), channel_id=1, source_target_pairs={{12,0},{28,16},{13,1},{29,17},{14,2},{30,18},{15,3},{31,19}} | collective-permute-start | bytes 2359304 | tf_op jit(solution)/shard_map/ppermute | solution.py:205
  15.4 13.0 %collective-permute-start.10 = (bf16[3,48,2048]{2,1,0:T(8,128)(2,1)S(1)}, bf16[3,48,2048]{2,1,0:T(8,128)(2,1)S(1)}, u32[]{:S(2)}, u32[]{:S(2)}) collective-permute-start(bf16[3,48,2048]{2,1,0:T(8,128)(2,1)S(1)} %collective-permute-done.5.shared_ref), channel_id=1, source_target_pairs={{4,5},{20,21},{5,4},{21,20},{6,7},{22,23},{7,6},{23,22}} | collective-permute-start | bytes 1769480 | tf_op jit(solution)/shard_map/ppermute | solution.py:213
  16.1 4.2 %collective-permute-start.7 = (bf16[24,1024]{1,0:T(8,128)(2,1)S(1)}, bf16[24,1024]{1,0:T(8,128)(2,1)S(1)}, u32[]{:S(2)}, u32[]{:S(2)}) collective-permute-start(bf16[24,1024]{1,0:T(8,128)(2,1)S(1)} %get-tuple-element.45), channel_id=1, source_target_pairs={{0,16},{4,20},{8,24},{12,28},{16,0},{20,4},{24,8},{28,12},{1,17},{... | collective-permute-start | bytes 147464 | tf_op jit(solution)/shard_map/ppermute | solution.py:201
  17.7 11.6 %collective-permute-start.9 = (bf16[24,1024]{1,0:T(8,128)(2,1)S(1)}, bf16[24,1024]{1,0:T(8,128)(2,1)S(1)}, u32[]{:S(2)}, u32[]{:S(2)}) collective-permute-start(bf16[24,1024]{1,0:T(8,128)(2,1)S(1)} %get-tuple-element.44), channel_id=1, source_target_pairs={{0,24},{4,28},{8,16},{12,20},{16,8},{20,12},{24,0},{28,4},{1,25},{... | collective-permute-start | bytes 147464 | tf_op jit(solution)/shard_map/ppermute | solution.py:201
  20.3 9.1 %collective-permute-start.6 = (bf16[24,1024]{1,0:T(8,128)(2,1)S(1)}, bf16[24,1024]{1,0:T(8,128)(2,1)S(1)}, u32[]{:S(2)}, u32[]{:S(2)}) collective-permute-start(bf16[24,1024]{1,0:T(8,128)(2,1)S(1)} %get-tuple-element.46), channel_id=1, source_target_pairs={{0,8},{4,12},{8,0},{12,4},{16,24},{20,28},{24,16},{28,20},{1,9},{5... | collective-permute-start | bytes 147464 | tf_op jit(solution)/shard_map/ppermute | solution.py:201
  22.7 6.7 %copy-start.5 = (f32[128,8]{0,1:T(8,128)S(1)}, f32[128,8]{0,1:T(8,128)}, u32[]{:S(2)}) copy-start(f32[128,8]{0,1:T(8,128)} %param.9) | copy-start | bytes 12292
  22.7 11.0 %collective-permute-start.12 = (bf16[3,32,2048]{2,1,0:T(8,128)(2,1)S(1)}, bf16[3,32,2048]{2,1,0:T(8,128)(2,1)S(1)}, u32[]{:S(2)}, u32[]{:S(2)}) collective-permute-start(bf16[3,32,2048]{2,1,0:T(8,128)(2,1)S(1)} %get-tuple-element.43), channel_id=1, source_target_pairs={{12,0},{28,16},{13,1},{29,17},{14,2},{30,18},{15,3},{31,19}} | collective-permute-start | bytes 1179656 | tf_op jit(solution)/shard_map/ppermute | solution.py:205

commit v16 on v15

--- a/solution.py
+++ b/solution.py
@@ -188,7 +188,7 @@
     plan = jnp.transpose(move_plan, (1, 0, 2))
     weights = (old_gate, old_up, old_down)
     half = most // 2
-    lead = most // 3 * 2
+    lead = most // 6 * 5
 
     def shape(*dims, dtype=BF16):
         return jax.ShapeDtypeStruct(dims, dtype)
@@ -295,7 +295,7 @@
         out_specs=VMEM,
         scratch_shapes=[pltpu.VMEM((len(back) * STRIDE, width // 2), BF16)],
         compiler_params=params(14 + experts),
-        cost_estimate=cost(5),
+        cost_estimate=cost(3),
         name="combine",
     )(expert_ids.T, combine.T, *back)
 

time: 34.7 us -> 33.5 us (0.965)
  waiting for transfers between devices: 11.6 us -> 10.2 us
    ppermute x4, waiting for transfers between devices: 7.21 us -> 6.04 us  [migrate(): return lax.ppermute(block, 'expert', route)]
  transfers between devices with their start and end apart: 13 -> 13, of which waited for: 5 -> 6; matrix products, arithmetic and copies ran while one was open for 0% -> 0% of each run, Pallas kernels for 10% -> 10%
where the time goes in v16:
time: 33.5 us; the launch traced here: 33.2 us
  starting transfers between devices  15.9 us (47%)
  waiting for transfers between devices  10.2 us (30%)
  Pallas kernels  5.06 us (15%)
  local copies, waits for them, and re-layouts  1.19 us (4%)
  between operations  0.81 us (2%)
    ppermute x8, starting transfers between devices, send(): return lax.ppermute(block, 'expert', route)  11.1 us
    ppermute x4, waiting for transfers between devices, migrate(): return lax.ppermute(block, 'expert', route)  6.04 us
    ppermute x8, waiting for transfers between devices, send(): return lax.ppermute(block, 'expert', route)  4.17 us
    ppermute x4, starting transfers between devices, migrate(): return lax.ppermute(block, 'expert', route)  4.14 us
    pallas_call x1, Pallas kernels, on_device(): pl.pallas_call(functools.partial(combine_kernel, experts), out_shape=shap...  1.43 us
    unnamed x19, local copies, waits for them, and re-layouts  1.17 us
    pallas_call x1, Pallas kernels, on_device(): pl.pallas_call(early_kernel, out_shape=shape(3, most, width), in_specs=[H...  0.99 us
    pallas_call x1, Pallas kernels, on_device(): pl.pallas_call(expert_kernel, grid=(total // step,), out_shape=[shape(tot...  0.92 us
  transfers between devices with their start and end apart: 13, of which 6 were waited for; matrix products, arithmetic and copies ran while one was open for 0% of the time, Pallas kernels for 10%

profile of v16, /device:TPU:0, one launch (start us, length us, event | category | flops | bytes accessed | tf_op | source)
XLA Modules:
  0.0 33.2 jit_solution(1491025284729432114)
XLA Ops:
  0.6 0.6 %begin.1.begun_ref = f32[8,128]{1,0:T(8,128)} custom-call(), custom_call_target="tpu_custom_call" | custom-call | flops 5000000000 | bytes 10000 | tf_op jit(solution)/shard_map/begin/pallas_call | solution.py:226
  1.2 0.1 copy-done.4
  1.3 0.4 %copy-done.3 = bf16[128,2048]{1,0:T(8,128)(2,1)S(1)} copy-done((bf16[128,2048]{1,0:T(8,128)(2,1)S(1)}, bf16[128,2048]{1,0:T(8,128)(2,1)}, u32[]{:S(2)}) %copy-start.3) | copy-done | bytes 524312
  1.7 0.7 %copy-done.7 = f32[8,128]{1,0:T(8,128)S(1)} copy-done((f32[8,128]{1,0:T(8,128)S(1)}, f32[8,128]{1,0:T(8,128)}, u32[]{:S(2)}) %copy-start.7) | copy-done | bytes 4120
  2.4 0.4 %dispatch.1 = (bf16[24,1024]{1,0:T(8,128)(2,1)S(1)}, bf16[24,1024]{1,0:T(8,128)(2,1)S(1)}) custom-call(s32[8,128]{1,0:T(8,128)S(1)} %bitcast.3, bf16[128,2048]{1,0:T(8,128)(2,1)S(1)} %copy-done.3, f32[8,128]{1,0:T(8,128)S(1)} %copy-done.7), custom_call_target="tpu_custom_call" | custom-call | flops 2000000000 | bytes 10000 | tf_op jit(solution)/shard_map/dispatch/pallas_call | solution.py:233
  2.8 4.0 %collective-permute-start.2 = (bf16[24,1024]{1,0:T(8,128)(2,1)S(1)}, bf16[24,1024]{1,0:T(8,128)(2,1)S(1)}, u32[]{:S(2)}, u32[]{:S(2)}) collective-permute-start(bf16[24,1024]{1,0:T(8,128)(2,1)S(1)} %get-tuple-element.24), channel_id=1, source_target_pairs={{0,24},{4,28},{8,16},{12,20},{16,8},{20,12},{24,0},{28,4},{1,25},{... | collective-permute-start | bytes 147464 | tf_op jit(solution)/shard_map/ppermute | solution.py:201
  6.8 0.5 %collective-permute-start.1 = (bf16[24,1024]{1,0:T(8,128)(2,1)S(1)}, bf16[24,1024]{1,0:T(8,128)(2,1)S(1)}, u32[]{:S(2)}, u32[]{:S(2)}) collective-permute-start(bf16[24,1024]{1,0:T(8,128)(2,1)S(1)} %get-tuple-element.24), channel_id=1, source_target_pairs={{0,16},{4,20},{8,24},{12,28},{16,0},{20,4},{24,8},{28,12},{1,17},{... | collective-permute-start | bytes 147464 | tf_op jit(solution)/shard_map/ppermute | solution.py:201
  7.3 0.1 collective-permute-start
  7.4 0.7 %collective-permute-start.5 = (bf16[3,48,2048]{2,1,0:T(8,128)(2,1)S(1)}, bf16[3,48,2048]{2,1,0:T(8,128)(2,1)S(1)}, u32[]{:S(2)}, u32[]{:S(2)}) collective-permute-start(bf16[3,48,2048]{2,1,0:T(8,128)(2,1)S(1)} %get-tuple-element.30), channel_id=1, source_target_pairs={{12,4},{28,20},{13,5},{29,21},{14,6},{30,22},{15,7},{31,23}} | collective-permute-start | bytes 1769480 | tf_op jit(solution)/shard_map/ppermute | solution.py:205
  8.2 0.7 %collective-permute-start.8 = (bf16[3,96,2048]{2,1,0:T(8,128)(2,1)S(1)}, bf16[3,96,2048]{2,1,0:T(8,128)(2,1)S(1)}, u32[]{:S(2)}, u32[]{:S(2)}) collective-permute-start(bf16[3,96,2048]{2,1,0:T(8,128)(2,1)S(1)} %get-tuple-element.32), channel_id=1, source_target_pairs={{12,8},{28,24},{13,9},{29,25},{14,10},{30,26},{15,11},{31,27}} | collective-permute-start | bytes 3538952 | tf_op jit(solution)/shard_map/ppermute | solution.py:205
  8.9 2.4 %collective-permute-done = bf16[24,1024]{1,0:T(8,128)(2,1)S(1)} collective-permute-done((bf16[24,1024]{1,0:T(8,128)(2,1)S(1)}, bf16[24,1024]{1,0:T(8,128)(2,1)S(1)}, u32[]{:S(2)}, u32[]{:S(2)}) %collective-permute-start) | collective-permute-done | bytes 49184 | tf_op jit(solution)/shard_map/ppermute | solution.py:201
  11.4 0.0 collective-permute-done.1
  11.4 0.0 collective-permute-done.2
  11.4 0.1 collective-permute-start.3
  11.5 1.3 %collective-permute-start.11 = (bf16[3,80,2048]{2,1,0:T(8,128)(2,1)S(1)}, bf16[3,80,2048]{2,1,0:T(8,128)(2,1)S(1)}, u32[]{:S(2)}, u32[]{:S(2)}) collective-permute-start(bf16[3,80,2048]{2,1,0:T(8,128)(2,1)S(1)} %get-tuple-element.35), channel_id=1, source_target_pairs={{12,0},{28,16},{13,1},{29,17},{14,2},{30,18},{15,3},{31,19}} | collective-permute-start | bytes 2949128 | tf_op jit(solution)/shard_map/ppermute | solution.py:205
  12.8 0.1 collective-permute-done.3.other_ref
  12.9 0.9 %expert.1 = (f32[96,1024]{1,0:T(8,128)S(1)}, bf16[96,1024]{1,0:T(8,128)(2,1)S(1)}) custom-call(bf16[96,1024]{1,0:T(8,128)(2,1)S(1)} %constant_dynamic-update-slice_fusion.mine_ref, bf16[96,1024]{1,0:T(8,128)(2,1)S(1)} %collective-permute-done.3.other_ref, bf16[192,2048]{1,0:T(8,128)(2,1)S(1)} %copy-done, bf16[192,2048]{1,0:T(8,128)(2,1)S(1)} %copy-done.1, ...), custom_call_target="tpu_custom_call" | custom-call | bytes 10000 | tf_op jit(solution)/shard_map/expert/pallas_call | solution.py:258
  13.8 0.2 collective-permute-start.4
  14.0 1.3 %collective-permute-done.4 = bf16[96,1024]{1,0:T(8,128)(2,1)S(1)} collective-permute-done((bf16[96,1024]{1,0:T(8,128)(2,1)S(1)}, bf16[96,1024]{1,0:T(8,128)(2,1)S(1)}, u32[]{:S(2)}, u32[]{:S(2)}) %collective-permute-start.4) | collective-permute-done | bytes 196640 | tf_op jit(solution)/shard_map/ppermute | solution.py:201
  15.3 0.0 collective-permute-done.5.shared_ref
  15.4 0.7 %collective-permute-start.10 = (bf16[3,48,2048]{2,1,0:T(8,128)(2,1)S(1)}, bf16[3,48,2048]{2,1,0:T(8,128)(2,1)S(1)}, u32[]{:S(2)}, u32[]{:S(2)}) collective-permute-start(bf16[3,48,2048]{2,1,0:T(8,128)(2,1)S(1)} %collective-permute-done.5.shared_ref), channel_id=1, source_target_pairs={{4,5},{20,21},{5,4},{21,20},{6,7},{22,23},{7,6},{23,22}} | collective-permute-start | bytes 1769480 | tf_op jit(solution)/shard_map/ppermute | solution.py:213
  16.1 1.6 %collective-permute-start.7 = (bf16[24,1024]{1,0:T(8,128)(2,1)S(1)}, bf16[24,1024]{1,0:T(8,128)(2,1)S(1)}, u32[]{:S(2)}, u32[]{:S(2)}) collective-permute-start(bf16[24,1024]{1,0:T(8,128)(2,1)S(1)} %get-tuple-element.45), channel_id=1, source_target_pairs={{0,16},{4,20},{8,24},{12,28},{16,0},{20,4},{24,8},{28,12},{1,17},{... | collective-permute-start | bytes 147464 | tf_op jit(solution)/shard_map/ppermute | solution.py:201
  17.7 2.3 %collective-permute-start.9 = (bf16[24,1024]{1,0:T(8,128)(2,1)S(1)}, bf16[24,1024]{1,0:T(8,128)(2,1)S(1)}, u32[]{:S(2)}, u32[]{:S(2)}) collective-permute-start(bf16[24,1024]{1,0:T(8,128)(2,1)S(1)} %get-tuple-element.44), channel_id=1, source_target_pairs={{0,24},{4,28},{8,16},{12,20},{16,8},{20,12},{24,0},{28,4},{1,25},{... | collective-permute-start | bytes 147464 | tf_op jit(solution)/shard_map/ppermute | solution.py:201
  20.0 0.3 collective-permute-done.7.refs_2_
  20.3 2.3 %collective-permute-start.6 = (bf16[24,1024]{1,0:T(8,128)(2,1)S(1)}, bf16[24,1024]{1,0:T(8,128)(2,1)S(1)}, u32[]{:S(2)}, u32[]{:S(2)}) collective-permute-start(bf16[24,1024]{1,0:T(8,128)(2,1)S(1)} %get-tuple-element.46), channel_id=1, source_target_pairs={{0,8},{4,12},{8,0},{12,4},{16,24},{20,28},{24,16},{28,20},{1,9},{5... | collective-permute-start | bytes 147464 | tf_op jit(solution)/shard_map/ppermute | solution.py:201
  22.6 0.0 collective-permute-done.8.near_ref
  22.6 1.4 %collective-permute-start.12 = (bf16[3,16,2048]{2,1,0:T(8,128)(2,1)S(1)}, bf16[3,16,2048]{2,1,0:T(8,128)(2,1)S(1)}, u32[]{:S(2)}, u32[]{:S(2)}) collective-permute-start(bf16[3,16,2048]{2,1,0:T(8,128)(2,1)S(1)} %get-tuple-element.43), channel_id=1, source_target_pairs={{12,0},{28,16},{13,1},{29,17},{14,2},{30,18},{15,3},{31,19}} | collective-permute-start | bytes 589832 | tf_op jit(solution)/shard_map/ppermute | solution.py:205
  24.0 5.3 %collective-permute-done.11.first_ref = bf16[3,80,2048]{2,1,0:T(8,128)(2,1)S(1)} collective-permute-done((bf16[3,80,2048]{2,1,0:T(8,128)(2,1)S(1)}, bf16[3,80,2048]{2,1,0:T(8,128)(2,1)S(1)}, u32[]{:S(2)}, u32[]{:S(2)}) %collective-permute-start.11) | collective-permute-done | bytes 983072 | tf_op jit(solution)/shard_map/ppermute | solution.py:205
  29.4 1.0 %early.1.early_ref = bf16[3,96,2048]{2,1,0:T(8,128)(2,1)} custom-call(bf16[3,48,2048]{2,1,0:T(8,128)(2,1)S(1)} %collective-permute-done.5.shared_ref, bf16[3,48,2048]{2,1,0:T(8,128)(2,1)S(1)} %collective-permute-done.10.swapped_ref, bf16[3,80,2048]{2,1,0:T(8,128)(2,1)S(1)} %collective-permute-done.11.first_ref, ...), custom_call_target="tpu_custom_call" | custom-call | tf_op jit(solution)/shard_map/early/pallas_call | solution.py:280
  30.4 1.4 %combine.1 = bf16[128,2048]{1,0:T(8,128)(2,1)} custom-call(s32[8,128]{1,0:T(8,128)S(1)} %bitcast.4, f32[8,128]{1,0:T(8,128)S(1)} %bitcast.5, bf16[24,1024]{1,0:T(8,128)(2,1)S(1)} %get-tuple-element.37.refs_0_, bf16[24,1024]{1,0:T(8,128)(2,1)S(1)} %collective-permute-done.6.refs_1_, bf16[24,1024]{1,0:T(8,128)(2,1)S(1)} %collective-permute-done.7.refs_2_, ...), custom_call_target="tpu_custom_call" | custom-call | flops 3000000000 | bytes 10000 | tf_op jit(solution)/shard_map/combine/pallas_call | solution.py:291
  31.8 0.7 %collective-permute-done.12.second_ref = bf16[3,16,2048]{2,1,0:T(8,128)(2,1)S(1)} collective-permute-done((bf16[3,16,2048]{2,1,0:T(8,128)(2,1)S(1)}, bf16[3,16,2048]{2,1,0:T(8,128)(2,1)S(1)}, u32[]{:S(2)}, u32[]{:S(2)}) %collective-permute-start.12) | collective-permute-done | bytes 196640 | tf_op jit(solution)/shard_map/ppermute | solution.py:205
  32.5 0.7 %late.1 = bf16[3,96,2048]{2,1,0:T(8,128)(2,1)} custom-call(bf16[3,96,2048]{2,1,0:T(8,128)(2,1)} %early.1.early_ref, bf16[3,16,2048]{2,1,0:T(8,128)(2,1)S(1)} %collective-permute-done.12.second_ref), custom_call_target="tpu_custom_call", output_to_operand_aliasing={{}: (0, {})} | custom-call | tf_op jit(solution)/shard_map/late/pallas_call | solution.py:302
  (23 shorter events, 0.1 us)
Async XLA Ops:
  0.6 0.7 %copy-start.4 = (s32[128,8]{0,1:T(8,128)S(1)}, s32[128,8]{0,1:T(8,128)}, u32[]{:S(2)}) copy-start(s32[128,8]{0,1:T(8,128)} %param.8) | copy-start | bytes 12292
  0.6 1.1 %copy-start.3 = (bf16[128,2048]{1,0:T(8,128)(2,1)S(1)}, bf16[128,2048]{1,0:T(8,128)(2,1)}, u32[]{:S(2)}) copy-start(bf16[128,2048]{1,0:T(8,128)(2,1)} %tok_ref.1) | copy-start | bytes 1572868
  1.7 0.7 %copy-start.7 = (f32[8,128]{1,0:T(8,128)S(1)}, f32[8,128]{1,0:T(8,128)}, u32[]{:S(2)}) copy-start(f32[8,128]{1,0:T(8,128)} %begin.1.begun_ref) | copy-start | bytes 12292
  2.4 5.0 %copy-start = (bf16[192,2048]{1,0:T(8,128)(2,1)S(1)}, bf16[192,2048]{1,0:T(8,128)(2,1)}, u32[]{:S(2)}) copy-start(bf16[192,2048]{1,0:T(8,128)(2,1)} %gate_ref.2) | copy-start | bytes 2359300
  2.4 5.0 %copy-start.1 = (bf16[192,2048]{1,0:T(8,128)(2,1)S(1)}, bf16[192,2048]{1,0:T(8,128)(2,1)}, u32[]{:S(2)}) copy-start(bf16[192,2048]{1,0:T(8,128)(2,1)} %up_ref.2) | copy-start | bytes 2359300
  2.4 5.0 %copy-start.2 = (bf16[192,2048]{1,0:T(8,128)(2,1)S(1)}, bf16[192,2048]{1,0:T(8,128)(2,1)}, u32[]{:S(2)}) copy-start(bf16[192,2048]{1,0:T(8,128)(2,1)} %down_ref.2) | copy-start | bytes 2359300
  2.4 5.0 %copy-start.6 = (s32[2,3,96]{2,0,1:T(2,128)S(1)}, s32[2,3,96]{2,0,1:T(2,128)}, u32[]{:S(2)}) copy-start(s32[2,3,96]{2,0,1:T(2,128)} %param.13) | copy-start | bytes 6916
  2.8 8.6 %collective-permute-start.2 = (bf16[24,1024]{1,0:T(8,128)(2,1)S(1)}, bf16[24,1024]{1,0:T(8,128)(2,1)S(1)}, u32[]{:S(2)}, u32[]{:S(2)}) collective-permute-start(bf16[24,1024]{1,0:T(8,128)(2,1)S(1)} %get-tuple-element.24), channel_id=1, source_target_pairs={{0,24},{4,28},{8,16},{12,20},{16,8},{20,12},{24,0},{28,4},{1,25},{... | collective-permute-start | bytes 147464 | tf_op jit(solution)/shard_map/ppermute | solution.py:201
  6.8 4.6 %collective-permute-start.1 = (bf16[24,1024]{1,0:T(8,128)(2,1)S(1)}, bf16[24,1024]{1,0:T(8,128)(2,1)S(1)}, u32[]{:S(2)}, u32[]{:S(2)}) collective-permute-start(bf16[24,1024]{1,0:T(8,128)(2,1)S(1)} %get-tuple-element.24), channel_id=1, source_target_pairs={{0,16},{4,20},{8,24},{12,28},{16,0},{20,4},{24,8},{28,12},{1,17},{... | collective-permute-start | bytes 147464 | tf_op jit(solution)/shard_map/ppermute | solution.py:201
  7.3 4.1 %collective-permute-start = (bf16[24,1024]{1,0:T(8,128)(2,1)S(1)}, bf16[24,1024]{1,0:T(8,128)(2,1)S(1)}, u32[]{:S(2)}, u32[]{:S(2)}) collective-permute-start(bf16[24,1024]{1,0:T(8,128)(2,1)S(1)} %get-tuple-element.23), channel_id=1, source_target_pairs={{0,8},{4,12},{8,0},{12,4},{16,24},{20,28},{24,16},{28,20},{1,9},{5... | collective-permute-start | bytes 147464 | tf_op jit(solution)/shard_map/ppermute | solution.py:201
  7.4 7.9 %collective-permute-start.5 = (bf16[3,48,2048]{2,1,0:T(8,128)(2,1)S(1)}, bf16[3,48,2048]{2,1,0:T(8,128)(2,1)S(1)}, u32[]{:S(2)}, u32[]{:S(2)}) collective-permute-start(bf16[3,48,2048]{2,1,0:T(8,128)(2,1)S(1)} %get-tuple-element.30), channel_id=1, source_target_pairs={{12,4},{28,20},{13,5},{29,21},{14,6},{30,22},{15,7},{31,23}} | collective-permute-start | bytes 1769480 | tf_op jit(solution)/shard_map/ppermute | solution.py:205
  8.2 14.5 %collective-permute-start.8 = (bf16[3,96,2048]{2,1,0:T(8,128)(2,1)S(1)}, bf16[3,96,2048]{2,1,0:T(8,128)(2,1)S(1)}, u32[]{:S(2)}, u32[]{:S(2)}) collective-permute-start(bf16[3,96,2048]{2,1,0:T(8,128)(2,1)S(1)} %get-tuple-element.32), channel_id=1, source_target_pairs={{12,8},{28,24},{13,9},{29,25},{14,10},{30,26},{15,11},{31,27}} | collective-permute-start | bytes 3538952 | tf_op jit(solution)/shard_map/ppermute | solution.py:205
  11.4 1.5 %collective-permute-start.3 = (bf16[96,1024]{1,0:T(8,128)(2,1)S(1)}, bf16[96,1024]{1,0:T(8,128)(2,1)S(1)}, u32[]{:S(2)}, u32[]{:S(2)}) collective-permute-start(bf16[96,1024]{1,0:T(8,128)(2,1)S(1)} %constant_dynamic-update-slice_fusion.mine_ref), channel_id=1, source_target_pairs={{0,4},{4,0},{8,12},{12,8},{16,20},{20,16},{24,28},{28,24},{1,5},{5... | collective-permute-start | bytes 589832 | tf_op jit(solution)/shard_map/ppermute | solution.py:201
  11.5 17.9 %collective-permute-start.11 = (bf16[3,80,2048]{2,1,0:T(8,128)(2,1)S(1)}, bf16[3,80,2048]{2,1,0:T(8,128)(2,1)S(1)}, u32[]{:S(2)}, u32[]{:S(2)}) collective-permute-start(bf16[3,80,2048]{2,1,0:T(8,128)(2,1)S(1)} %get-tuple-element.35), channel_id=1, source_target_pairs={{12,0},{28,16},{13,1},{29,17},{14,2},{30,18},{15,3},{31,19}} | collective-permute-start | bytes 2949128 | tf_op jit(solution)/shard_map/ppermute | solution.py:205
  13.8 1.5 %collective-permute-start.4 = (bf16[96,1024]{1,0:T(8,128)(2,1)S(1)}, bf16[96,1024]{1,0:T(8,128)(2,1)S(1)}, u32[]{:S(2)}, u32[]{:S(2)}) collective-permute-start(bf16[96,1024]{1,0:T(8,128)(2,1)S(1)} %get-tuple-element.26), channel_id=1, source_target_pairs={{0,4},{4,0},{8,12},{12,8},{16,20},{20,16},{24,28},{28,24},{1,5},{5... | collective-permute-start | bytes 589832 | tf_op jit(solution)/shard_map/ppermute | solution.py:201
  15.4 14.0 %collective-permute-start.10 = (bf16[3,48,2048]{2,1,0:T(8,128)(2,1)S(1)}, bf16[3,48,2048]{2,1,0:T(8,128)(2,1)S(1)}, u32[]{:S(2)}, u32[]{:S(2)}) collective-permute-start(bf16[3,48,2048]{2,1,0:T(8,128)(2,1)S(1)} %collective-permute-done.5.shared_ref), channel_id=1, source_target_pairs={{4,5},{20,21},{5,4},{21,20},{6,7},{22,23},{7,6},{23,22}} | collective-permute-start | bytes 1769480 | tf_op jit(solution)/shard_map/ppermute | solution.py:213
  16.1 4.2 %collective-permute-start.7 = (bf16[24,1024]{1,0:T(8,128)(2,1)S(1)}, bf16[24,1024]{1,0:T(8,128)(2,1)S(1)}, u32[]{:S(2)}, u32[]{:S(2)}) collective-permute-start(bf16[24,1024]{1,0:T(8,128)(2,1)S(1)} %get-tuple-element.45), channel_id=1, source_target_pairs={{0,16},{4,20},{8,24},{12,28},{16,0},{20,4},{24,8},{28,12},{1,17},{... | collective-permute-start | bytes 147464 | tf_op jit(solution)/shard_map/ppermute | solution.py:201
  17.7 12.7 %collective-permute-start.9 = (bf16[24,1024]{1,0:T(8,128)(2,1)S(1)}, bf16[24,1024]{1,0:T(8,128)(2,1)S(1)}, u32[]{:S(2)}, u32[]{:S(2)}) collective-permute-start(bf16[24,1024]{1,0:T(8,128)(2,1)S(1)} %get-tuple-element.44), channel_id=1, source_target_pairs={{0,24},{4,28},{8,16},{12,20},{16,8},{20,12},{24,0},{28,4},{1,25},{... | collective-permute-start | bytes 147464 | tf_op jit(solution)/shard_map/ppermute | solution.py:201
  20.3 10.1 %collective-permute-start.6 = (bf16[24,1024]{1,0:T(8,128)(2,1)S(1)}, bf16[24,1024]{1,0:T(8,128)(2,1)S(1)}, u32[]{:S(2)}, u32[]{:S(2)}) collective-permute-start(bf16[24,1024]{1,0:T(8,128)(2,1)S(1)} %get-tuple-element.46), channel_id=1, source_target_pairs={{0,8},{4,12},{8,0},{12,4},{16,24},{20,28},{24,16},{28,20},{1,9},{5... | collective-permute-start | bytes 147464 | tf_op jit(solution)/shard_map/ppermute | solution.py:201
  22.6 7.8 %copy-start.5 = (f32[128,8]{0,1:T(8,128)S(1)}, f32[128,8]{0,1:T(8,128)}, u32[]{:S(2)}) copy-start(f32[128,8]{0,1:T(8,128)} %param.9) | copy-start | bytes 12292
  22.6 9.9 %collective-permute-start.12 = (bf16[3,16,2048]{2,1,0:T(8,128)(2,1)S(1)}, bf16[3,16,2048]{2,1,0:T(8,128)(2,1)S(1)}, u32[]{:S(2)}, u32[]{:S(2)}) collective-permute-start(bf16[3,16,2048]{2,1,0:T(8,128)(2,1)S(1)} %get-tuple-element.43), channel_id=1, source_target_pairs={{12,0},{28,16},{13,1},{29,17},{14,2},{30,18},{15,3},{31,19}} | collective-permute-start | bytes 589832 | tf_op jit(solution)/shard_map/ppermute | solution.py:205

commit v17 on v16

--- a/solution.py
+++ b/solution.py
@@ -15,6 +15,7 @@
 F32 = jnp.float32
 VMEM = pl.BlockSpec(memory_space=pltpu.VMEM)
 HBM = pl.BlockSpec(memory_space=pltpu.HBM)
+ANY = pl.BlockSpec(memory_space=pl.ANY)
 
 
 def params(megabytes=16):
@@ -41,7 +42,7 @@
     return jnp.where(member > 0, rank - 1.0, -PACK).astype(jnp.int32)
 
 
-def dispatch_kernel(experts, ids_ref, tok_ref, begun_ref, *out_refs):
+def dispatch_kernel(experts, ids_ref, tok_ref, begun_hbm, *out_refs):
     group = lax.axis_index("expert") // GROUP
     place = token_places(ids_ref[...], group, experts)
     tok, half = tok_ref.shape[0], tok_ref.shape[1] // 2
@@ -97,31 +98,34 @@
         copy.wait()
 
 
-def early_kernel(shared_ref, swapped_ref, first_ref, near_ref, out_ref, sems):
+def early_kernel(swapped_ref, near_ref, shared_ref, own_ref, out_ref, sems):
     position = lax.axis_index("expert") % GROUP
     parity = lax.axis_index("replica") % 2
-    half = shared_ref.shape[1]
+    half, part = shared_ref.shape[1], own_ref.shape[1]
     for even in range(2):
 
         @pl.when(jnp.logical_and(position == 1, parity == even))
         def _():
             place_rows([(shared_ref, half * even), (swapped_ref, half * (1 - even))], out_ref, sems)
 
-    @pl.when(jnp.logical_or(position == 0, position == 3))
-    def _():
-        place_rows([(first_ref, 0)], out_ref, sems)
+        @pl.when(jnp.logical_and(position % 3 == 0, parity == even))
+        def _():
+            place_rows([(own_ref, part * even)], out_ref, sems)
 
     @pl.when(position == 2)
     def _():
         place_rows([(near_ref, 0)], out_ref, sems)
 
 
-def late_kernel(early_ref, second_ref, out_ref, sems):
+def late_kernel(early_ref, straight_ref, swapped_ref, out_ref, sems):
     position = lax.axis_index("expert") % GROUP
-
-    @pl.when(jnp.logical_or(position == 0, position == 3))
-    def _():
-        place_rows([(second_ref, out_ref.shape[1] - second_ref.shape[1])], out_ref, sems)
+    parity = lax.axis_index("replica") % 2
+    part = swapped_ref.shape[1]
+    for even in range(2):
+
+        @pl.when(jnp.logical_and(position % 3 == 0, parity == even))
+        def _():
+            place_rows([(straight_ref, 2 * part), (swapped_ref, part * (1 - even))], out_ref, sems)
 
 
 def begin_kernel(out_ref):
@@ -188,7 +192,7 @@
     plan = jnp.transpose(move_plan, (1, 0, 2))
     weights = (old_gate, old_up, old_down)
     half = most // 2
-    lead = most // 6 * 5
+    part = most // 6
 
     def shape(*dims, dtype=BF16):
         return jax.ShapeDtypeStruct(dims, dtype)
@@ -233,7 +237,7 @@
     parcels = pl.pallas_call(
         functools.partial(dispatch_kernel, experts),
         out_shape=[shape(PACK, width // 2)] * experts,
-        in_specs=[VMEM, VMEM, HBM],
+        in_specs=[VMEM, VMEM, ANY],
         out_specs=[VMEM] * experts,
         compiler_params=params(),
         cost_estimate=cost(2),
@@ -243,10 +247,10 @@
     pairs = [(j, k) for j in range(experts) for k in (0, 2)]
     mine = [parcels[0]] + [send(parcels[j], j, k) for j, k in pairs[1:]]
     held, _ = lax.optimization_barrier((weights, parcels))
-    wanted = [(1, half, None), (0, lead, 0), (0, most - lead, lead), (2, most, 0)]
+    wanted = [(0, part, None), (1, half, None), (0, most - 2 * part, 2 * part), (2, most, 0)]
     chosen = select(wanted, held)
-    shared = migrate(chosen[0], 1)
-    first = migrate(chosen[1], 0)
+    shared = [migrate(chosen[p], p) for p in range(2)]
+    straight = migrate(chosen[2], 0)
     near = migrate(chosen[3], 2)
     mine = jnp.concatenate(mine, axis=0)
     other = send(mine, 0, 1)
@@ -271,11 +275,9 @@
     back = [pieces[0]] + [
         send(block, -j, k) for (j, k), block in zip(pairs[1:], pieces[1:])
     ]
-    swapped = swap(shared, 1)
+    swapped = [swap(shared[p], p) for p in range(2)]
     beside = len(pairs) // 2
     back[beside], near = lax.optimization_barrier((back[beside], near))
-    last, _ = lax.optimization_barrier((chosen[2], summed))
-    second = migrate(last, 0)
 
     early = pl.pallas_call(
         early_kernel,
@@ -285,8 +287,8 @@
         scratch_shapes=[pltpu.SemaphoreType.DMA((6,))],
         compiler_params=params(),
         name="early",
-    )(shared, swapped, first, near)
-    back, early = lax.optimization_barrier((back, early))
+    )(swapped[1], near, shared[1], shared[0])
+    back, early, straight = lax.optimization_barrier((back, early, straight))
 
     mixed = pl.pallas_call(
         functools.partial(combine_kernel, experts),
@@ -302,13 +304,13 @@
     arrived = pl.pallas_call(
         late_kernel,
         out_shape=shape(3, most, width),
-        in_specs=[HBM] * 2,
+        in_specs=[HBM] * 3,
         out_specs=HBM,
         input_output_aliases={0: 0},
-        scratch_shapes=[pltpu.SemaphoreType.DMA((3,))],
+        scratch_shapes=[pltpu.SemaphoreType.DMA((6,))],
         compiler_params=params(),
         name="late",
-    )(early, second)
+    )(early, straight, swapped[0])
     return mixed, arrived
 
 

time: 33.5 us -> 33.7 us (level)
  waiting for transfers between devices: 10.2 us -> 11.6 us
  starting transfers between devices: 15.9 us -> 14.6 us
    ppermute x8, starting transfers between devices: 11.1 us -> 6.43 us  [send(): return lax.ppermute(block, 'expert', route)]
    ppermute x1 -> x2, starting transfers between devices: 0.69 us -> 4.18 us  [swap(): return lax.ppermute(block, ('expert', 'replica'), route)]
    ppermute x8, waiting for transfers between devices: 4.17 us -> 6.47 us  [send(): return lax.ppermute(block, 'expert', route)]
    ppermute x4, waiting for transfers between devices: 6.04 us -> 4.59 us  [migrate(): return lax.ppermute(block, 'expert', route)]
    ppermute x1 -> x2, waiting for transfers between devices: 0.01 us -> 0.57 us  [swap(): return lax.ppermute(block, ('expert', 'replica'), route)]
  transfers between devices with their start and end apart: 13 -> 14, of which waited for: 6 -> 6; matrix products, arithmetic and copies ran while one was open for 0% -> 0% of each run, Pallas kernels for 10% -> 9%
where the time goes in v17:
time: 33.7 us; the launch traced here: 33.4 us
  starting transfers between devices  14.6 us (43%)
  waiting for transfers between devices  11.6 us (34%)
  Pallas kernels  5.11 us (15%)
  local copies, waits for them, and re-layouts  1.19 us (4%)
  between operations  0.82 us (2%)
    ppermute x8, waiting for transfers between devices, send(): return lax.ppermute(block, 'expert', route)  6.47 us
    ppermute x8, starting transfers between devices, send(): return lax.ppermute(block, 'expert', route)  6.43 us
    ppermute x4, waiting for transfers between devices, migrate(): return lax.ppermute(block, 'expert', route)  4.59 us
    ppermute x2, starting transfers between devices, swap(): return lax.ppermute(block, ('expert', 'replica'), route)  4.18 us
    ppermute x4, starting transfers between devices, migrate(): return lax.ppermute(block, 'expert', route)  4.01 us
    pallas_call x1, Pallas kernels, on_device(): pl.pallas_call(functools.partial(combine_kernel, experts), out_shape=shap...  1.42 us
    unnamed x19, local copies, waits for them, and re-layouts  1.17 us
    pallas_call x1, Pallas kernels, on_device(): pl.pallas_call(late_kernel, out_shape=shape(3, most, width), in_specs=[HB...  0.98 us
  transfers between devices with their start and end apart: 14, of which 6 were waited for; matrix products, arithmetic and copies ran while one was open for 0% of the time, Pallas kernels for 9%

profile of v17, /device:TPU:0, one launch (start us, length us, event | category | flops | bytes accessed | tf_op | source)
XLA Modules:
  0.0 33.4 jit_solution(11085209165647813054)
XLA Ops:
  0.6 0.6 %begin.1.begun_hbm = f32[8,128]{1,0:T(8,128)} custom-call(), custom_call_target="tpu_custom_call" | custom-call | flops 5000000000 | bytes 10000 | tf_op jit(solution)/shard_map/begin/pallas_call | solution.py:230
  1.2 0.1 copy-done.4
  1.3 0.4 %copy-done.3 = bf16[128,2048]{1,0:T(8,128)(2,1)S(1)} copy-done((bf16[128,2048]{1,0:T(8,128)(2,1)S(1)}, bf16[128,2048]{1,0:T(8,128)(2,1)}, u32[]{:S(2)}) %copy-start.3) | copy-done | bytes 524312
  1.7 0.7 %copy-done.7 = f32[8,128]{1,0:T(8,128)S(1)} copy-done((f32[8,128]{1,0:T(8,128)S(1)}, f32[8,128]{1,0:T(8,128)}, u32[]{:S(2)}) %copy-start.7) | copy-done | bytes 4120
  2.4 0.4 %dispatch.1 = (bf16[24,1024]{1,0:T(8,128)(2,1)S(1)}, bf16[24,1024]{1,0:T(8,128)(2,1)S(1)}) custom-call(s32[8,128]{1,0:T(8,128)S(1)} %bitcast.3, bf16[128,2048]{1,0:T(8,128)(2,1)S(1)} %copy-done.3, f32[8,128]{1,0:T(8,128)S(1)} %copy-done.7), custom_call_target="tpu_custom_call" | custom-call | flops 2000000000 | bytes 10000 | tf_op jit(solution)/shard_map/dispatch/pallas_call | solution.py:237
  2.8 3.0 %collective-permute-start.1 = (bf16[24,1024]{1,0:T(8,128)(2,1)S(1)}, bf16[24,1024]{1,0:T(8,128)(2,1)S(1)}, u32[]{:S(2)}, u32[]{:S(2)}) collective-permute-start(bf16[24,1024]{1,0:T(8,128)(2,1)S(1)} %get-tuple-element.25), channel_id=1, source_target_pairs={{0,16},{4,20},{8,24},{12,28},{16,0},{20,4},{24,8},{28,12},{1,17},{... | collective-permute-start | bytes 147464 | tf_op jit(solution)/shard_map/ppermute | solution.py:205
  5.8 1.4 %collective-permute-start.2 = (bf16[24,1024]{1,0:T(8,128)(2,1)S(1)}, bf16[24,1024]{1,0:T(8,128)(2,1)S(1)}, u32[]{:S(2)}, u32[]{:S(2)}) collective-permute-start(bf16[24,1024]{1,0:T(8,128)(2,1)S(1)} %get-tuple-element.25), channel_id=1, source_target_pairs={{0,24},{4,28},{8,16},{12,20},{16,8},{20,12},{24,0},{28,4},{1,25},{... | collective-permute-start | bytes 147464 | tf_op jit(solution)/shard_map/ppermute | solution.py:205
  7.3 0.1 collective-permute-start
  7.4 0.7 %collective-permute-start.6 = (bf16[3,48,2048]{2,1,0:T(8,128)(2,1)S(1)}, bf16[3,48,2048]{2,1,0:T(8,128)(2,1)S(1)}, u32[]{:S(2)}, u32[]{:S(2)}) collective-permute-start(bf16[3,48,2048]{2,1,0:T(8,128)(2,1)S(1)} %get-tuple-element.32), channel_id=1, source_target_pairs={{12,4},{28,20},{13,5},{29,21},{14,6},{30,22},{15,7},{31,23}} | collective-permute-start | bytes 1769480 | tf_op jit(solution)/shard_map/ppermute | solution.py:209
  8.1 0.7 %collective-permute-start.9 = (bf16[3,96,2048]{2,1,0:T(8,128)(2,1)S(1)}, bf16[3,96,2048]{2,1,0:T(8,128)(2,1)S(1)}, u32[]{:S(2)}, u32[]{:S(2)}) collective-permute-start(bf16[3,96,2048]{2,1,0:T(8,128)(2,1)S(1)} %get-tuple-element.34), channel_id=1, source_target_pairs={{12,8},{28,24},{13,9},{29,25},{14,10},{30,26},{15,11},{31,27}} | collective-permute-start | bytes 3538952 | tf_op jit(solution)/shard_map/ppermute | solution.py:209
  8.9 2.5 %collective-permute-done = bf16[24,1024]{1,0:T(8,128)(2,1)S(1)} collective-permute-done((bf16[24,1024]{1,0:T(8,128)(2,1)S(1)}, bf16[24,1024]{1,0:T(8,128)(2,1)S(1)}, u32[]{:S(2)}, u32[]{:S(2)}) %collective-permute-start) | collective-permute-done | bytes 49184 | tf_op jit(solution)/shard_map/ppermute | solution.py:205
  11.4 0.1 collective-permute-start.3
  11.5 1.3 %collective-permute-start.5 = (bf16[3,16,2048]{2,1,0:T(8,128)(2,1)S(1)}, bf16[3,16,2048]{2,1,0:T(8,128)(2,1)S(1)}, u32[]{:S(2)}, u32[]{:S(2)}) collective-permute-start(bf16[3,16,2048]{2,1,0:T(8,128)(2,1)S(1)} %get-tuple-element.31), channel_id=1, source_target_pairs={{12,0},{28,16},{13,1},{29,17},{14,2},{30,18},{15,3},{31,19}} | collective-permute-start | bytes 589832 | tf_op jit(solution)/shard_map/ppermute | solution.py:209
  12.8 0.1 collective-permute-done.3.other_ref
  12.9 0.9 %expert.1 = (f32[96,1024]{1,0:T(8,128)S(1)}, bf16[96,1024]{1,0:T(8,128)(2,1)S(1)}) custom-call(bf16[96,1024]{1,0:T(8,128)(2,1)S(1)} %constant_dynamic-update-slice_fusion.mine_ref, bf16[96,1024]{1,0:T(8,128)(2,1)S(1)} %collective-permute-done.3.other_ref, bf16[192,2048]{1,0:T(8,128)(2,1)S(1)} %copy-done, bf16[192,2048]{1,0:T(8,128)(2,1)S(1)} %copy-done.1, ...), custom_call_target="tpu_custom_call" | custom-call | bytes 10000 | tf_op jit(solution)/shard_map/expert/pallas_call | solution.py:262
  13.8 0.2 collective-permute-start.4
  14.0 1.3 %collective-permute-start.12 = (bf16[3,64,2048]{2,1,0:T(8,128)(2,1)S(1)}, bf16[3,64,2048]{2,1,0:T(8,128)(2,1)S(1)}, u32[]{:S(2)}, u32[]{:S(2)}) collective-permute-start(bf16[3,64,2048]{2,1,0:T(8,128)(2,1)S(1)} %get-tuple-element.39), channel_id=1, source_target_pairs={{12,0},{28,16},{13,1},{29,17},{14,2},{30,18},{15,3},{31,19}} | collective-permute-start | bytes 2359304 | tf_op jit(solution)/shard_map/ppermute | solution.py:209
  15.3 4.6 %collective-permute-done.5.own_ref = bf16[3,16,2048]{2,1,0:T(8,128)(2,1)S(1)} collective-permute-done((bf16[3,16,2048]{2,1,0:T(8,128)(2,1)S(1)}, bf16[3,16,2048]{2,1,0:T(8,128)(2,1)S(1)}, u32[]{:S(2)}, u32[]{:S(2)}) %collective-permute-start.5) | collective-permute-done | bytes 196640 | tf_op jit(solution)/shard_map/ppermute | solution.py:209
  19.9 0.0 collective-permute-done.4
  19.9 0.0 collective-permute-done.6.shared_ref
  19.9 0.7 %collective-permute-start.11 = (bf16[3,48,2048]{2,1,0:T(8,128)(2,1)S(1)}, bf16[3,48,2048]{2,1,0:T(8,128)(2,1)S(1)}, u32[]{:S(2)}, u32[]{:S(2)}) collective-permute-start(bf16[3,48,2048]{2,1,0:T(8,128)(2,1)S(1)} %collective-permute-done.6.shared_ref), channel_id=1, source_target_pairs={{4,5},{20,21},{5,4},{21,20},{6,7},{22,23},{7,6},{23,22}} | collective-permute-start | bytes 1769480 | tf_op jit(solution)/shard_map/ppermute | solution.py:217
  20.7 1.6 %collective-permute-start.8 = (bf16[24,1024]{1,0:T(8,128)(2,1)S(1)}, bf16[24,1024]{1,0:T(8,128)(2,1)S(1)}, u32[]{:S(2)}, u32[]{:S(2)}) collective-permute-start(bf16[24,1024]{1,0:T(8,128)(2,1)S(1)} %get-tuple-element.47), channel_id=1, source_target_pairs={{0,16},{4,20},{8,24},{12,28},{16,0},{20,4},{24,8},{28,12},{1,17},{... | collective-permute-start | bytes 147464 | tf_op jit(solution)/shard_map/ppermute | solution.py:205
  22.3 2.6 %collective-permute-done.8.refs_2_ = bf16[24,1024]{1,0:T(8,128)(2,1)S(1)} collective-permute-done((bf16[24,1024]{1,0:T(8,128)(2,1)S(1)}, bf16[24,1024]{1,0:T(8,128)(2,1)S(1)}, u32[]{:S(2)}, u32[]{:S(2)}) %collective-permute-start.8) | collective-permute-done | bytes 49184 | tf_op jit(solution)/shard_map/ppermute | solution.py:205
  24.9 0.0 collective-permute-start.10
  24.9 0.0 collective-permute-done.9.near_ref
  24.9 3.5 %collective-permute-start.13 = (bf16[3,16,2048]{2,1,0:T(8,128)(2,1)S(1)}, bf16[3,16,2048]{2,1,0:T(8,128)(2,1)S(1)}, u32[]{:S(2)}, u32[]{:S(2)}) collective-permute-start(bf16[3,16,2048]{2,1,0:T(8,128)(2,1)S(1)} %collective-permute-done.5.own_ref), channel_id=1, source_target_pairs={{0,1},{16,17},{1,0},{17,16},{2,3},{18,19},{3,2},{19,18}} | collective-permute-start | bytes 589832 | tf_op jit(solution)/shard_map/ppermute | solution.py:217
  28.4 0.8 %early.1.early_ref = bf16[3,96,2048]{2,1,0:T(8,128)(2,1)} custom-call(bf16[3,48,2048]{2,1,0:T(8,128)(2,1)S(1)} %collective-permute-done.11.swapped_ref, bf16[3,96,2048]{2,1,0:T(8,128)(2,1)S(1)} %collective-permute-done.9.near_ref, bf16[3,48,2048]{2,1,0:T(8,128)(2,1)S(1)} %collective-permute-done.6.shared_ref, ...), custom_call_target="tpu_custom_call" | custom-call | tf_op jit(solution)/shard_map/early/pallas_call | solution.py:282
  29.1 0.0 collective-permute-done.7.refs_1_
  29.1 1.3 %collective-permute-done.10.refs_3_ = bf16[24,1024]{1,0:T(8,128)(2,1)S(1)} collective-permute-done((bf16[24,1024]{1,0:T(8,128)(2,1)S(1)}, bf16[24,1024]{1,0:T(8,128)(2,1)S(1)}, u32[]{:S(2)}, u32[]{:S(2)}) %collective-permute-start.10) | collective-permute-done | bytes 49184 | tf_op jit(solution)/shard_map/ppermute | solution.py:205
  30.4 1.4 %combine.1 = bf16[128,2048]{1,0:T(8,128)(2,1)} custom-call(s32[8,128]{1,0:T(8,128)S(1)} %bitcast.4, f32[8,128]{1,0:T(8,128)S(1)} %bitcast.5, bf16[24,1024]{1,0:T(8,128)(2,1)S(1)} %get-tuple-element.40.refs_0_, bf16[24,1024]{1,0:T(8,128)(2,1)S(1)} %collective-permute-done.7.refs_1_, bf16[24,1024]{1,0:T(8,128)(2,1)S(1)} %collective-permute-done.8.refs_2_, ...), custom_call_target="tpu_custom_call" | custom-call | flops 3000000000 | bytes 10000 | tf_op jit(solution)/shard_map/combine/pallas_call | solution.py:293
  31.9 0.6 %collective-permute-done.13.swapped_ref = bf16[3,16,2048]{2,1,0:T(8,128)(2,1)S(1)} collective-permute-done((bf16[3,16,2048]{2,1,0:T(8,128)(2,1)S(1)}, bf16[3,16,2048]{2,1,0:T(8,128)(2,1)S(1)}, u32[]{:S(2)}, u32[]{:S(2)}) %collective-permute-start.13) | collective-permute-done | bytes 196640 | tf_op jit(solution)/shard_map/ppermute | solution.py:217
  32.4 1.0 %late.1 = bf16[3,96,2048]{2,1,0:T(8,128)(2,1)} custom-call(bf16[3,96,2048]{2,1,0:T(8,128)(2,1)} %early.1.early_ref, bf16[3,64,2048]{2,1,0:T(8,128)(2,1)S(1)} %collective-permute-done.12.straight_ref, bf16[3,16,2048]{2,1,0:T(8,128)(2,1)S(1)} %collective-permute-done.13.swapped_ref), custom_call_target="tpu_custom_call", output_to_operand_aliasing={{}: (0, {})} | custom-call | tf_op jit(solution)/shard_map/late/pallas_call | solution.py:304
  (25 shorter events, 0.1 us)
Async XLA Ops:
  0.6 0.7 %copy-start.4 = (s32[128,8]{0,1:T(8,128)S(1)}, s32[128,8]{0,1:T(8,128)}, u32[]{:S(2)}) copy-start(s32[128,8]{0,1:T(8,128)} %param.8) | copy-start | bytes 12292
  0.6 1.1 %copy-start.3 = (bf16[128,2048]{1,0:T(8,128)(2,1)S(1)}, bf16[128,2048]{1,0:T(8,128)(2,1)}, u32[]{:S(2)}) copy-start(bf16[128,2048]{1,0:T(8,128)(2,1)} %tok_ref.1) | copy-start | bytes 1572868
  1.7 0.7 %copy-start.7 = (f32[8,128]{1,0:T(8,128)S(1)}, f32[8,128]{1,0:T(8,128)}, u32[]{:S(2)}) copy-start(f32[8,128]{1,0:T(8,128)} %begin.1.begun_hbm) | copy-start | bytes 12292
  2.4 5.0 %copy-start = (bf16[192,2048]{1,0:T(8,128)(2,1)S(1)}, bf16[192,2048]{1,0:T(8,128)(2,1)}, u32[]{:S(2)}) copy-start(bf16[192,2048]{1,0:T(8,128)(2,1)} %gate_ref.2) | copy-start | bytes 2359300
  2.4 5.0 %copy-start.1 = (bf16[192,2048]{1,0:T(8,128)(2,1)S(1)}, bf16[192,2048]{1,0:T(8,128)(2,1)}, u32[]{:S(2)}) copy-start(bf16[192,2048]{1,0:T(8,128)(2,1)} %up_ref.2) | copy-start | bytes 2359300
  2.4 5.0 %copy-start.2 = (bf16[192,2048]{1,0:T(8,128)(2,1)S(1)}, bf16[192,2048]{1,0:T(8,128)(2,1)}, u32[]{:S(2)}) copy-start(bf16[192,2048]{1,0:T(8,128)(2,1)} %down_ref.2) | copy-start | bytes 2359300
  2.4 5.0 %copy-start.6 = (s32[2,3,96]{2,0,1:T(2,128)S(1)}, s32[2,3,96]{2,0,1:T(2,128)}, u32[]{:S(2)}) copy-start(s32[2,3,96]{2,0,1:T(2,128)} %param.13) | copy-start | bytes 6916
  2.8 8.6 %collective-permute-start.1 = (bf16[24,1024]{1,0:T(8,128)(2,1)S(1)}, bf16[24,1024]{1,0:T(8,128)(2,1)S(1)}, u32[]{:S(2)}, u32[]{:S(2)}) collective-permute-start(bf16[24,1024]{1,0:T(8,128)(2,1)S(1)} %get-tuple-element.25), channel_id=1, source_target_pairs={{0,16},{4,20},{8,24},{12,28},{16,0},{20,4},{24,8},{28,12},{1,17},{... | collective-permute-start | bytes 147464 | tf_op jit(solution)/shard_map/ppermute | solution.py:205
  5.8 5.6 %collective-permute-start.2 = (bf16[24,1024]{1,0:T(8,128)(2,1)S(1)}, bf16[24,1024]{1,0:T(8,128)(2,1)S(1)}, u32[]{:S(2)}, u32[]{:S(2)}) collective-permute-start(bf16[24,1024]{1,0:T(8,128)(2,1)S(1)} %get-tuple-element.25), channel_id=1, source_target_pairs={{0,24},{4,28},{8,16},{12,20},{16,8},{20,12},{24,0},{28,4},{1,25},{... | collective-permute-start | bytes 147464 | tf_op jit(solution)/shard_map/ppermute | solution.py:205
  7.3 4.1 %collective-permute-start = (bf16[24,1024]{1,0:T(8,128)(2,1)S(1)}, bf16[24,1024]{1,0:T(8,128)(2,1)S(1)}, u32[]{:S(2)}, u32[]{:S(2)}) collective-permute-start(bf16[24,1024]{1,0:T(8,128)(2,1)S(1)} %get-tuple-element.24), channel_id=1, source_target_pairs={{0,8},{4,12},{8,0},{12,4},{16,24},{20,28},{24,16},{28,20},{1,9},{5... | collective-permute-start | bytes 147464 | tf_op jit(solution)/shard_map/ppermute | solution.py:205
  7.4 12.5 %collective-permute-start.6 = (bf16[3,48,2048]{2,1,0:T(8,128)(2,1)S(1)}, bf16[3,48,2048]{2,1,0:T(8,128)(2,1)S(1)}, u32[]{:S(2)}, u32[]{:S(2)}) collective-permute-start(bf16[3,48,2048]{2,1,0:T(8,128)(2,1)S(1)} %get-tuple-element.32), channel_id=1, source_target_pairs={{12,4},{28,20},{13,5},{29,21},{14,6},{30,22},{15,7},{31,23}} | collective-permute-start | bytes 1769480 | tf_op jit(solution)/shard_map/ppermute | solution.py:209
  8.1 16.7 %collective-permute-start.9 = (bf16[3,96,2048]{2,1,0:T(8,128)(2,1)S(1)}, bf16[3,96,2048]{2,1,0:T(8,128)(2,1)S(1)}, u32[]{:S(2)}, u32[]{:S(2)}) collective-permute-start(bf16[3,96,2048]{2,1,0:T(8,128)(2,1)S(1)} %get-tuple-element.34), channel_id=1, source_target_pairs={{12,8},{28,24},{13,9},{29,25},{14,10},{30,26},{15,11},{31,27}} | collective-permute-start | bytes 3538952 | tf_op jit(solution)/shard_map/ppermute | solution.py:209
  11.4 1.5 %collective-permute-start.3 = (bf16[96,1024]{1,0:T(8,128)(2,1)S(1)}, bf16[96,1024]{1,0:T(8,128)(2,1)S(1)}, u32[]{:S(2)}, u32[]{:S(2)}) collective-permute-start(bf16[96,1024]{1,0:T(8,128)(2,1)S(1)} %constant_dynamic-update-slice_fusion.mine_ref), channel_id=1, source_target_pairs={{0,4},{4,0},{8,12},{12,8},{16,20},{20,16},{24,28},{28,24},{1,5},{5... | collective-permute-start | bytes 589832 | tf_op jit(solution)/shard_map/ppermute | solution.py:205
  11.5 8.4 %collective-permute-start.5 = (bf16[3,16,2048]{2,1,0:T(8,128)(2,1)S(1)}, bf16[3,16,2048]{2,1,0:T(8,128)(2,1)S(1)}, u32[]{:S(2)}, u32[]{:S(2)}) collective-permute-start(bf16[3,16,2048]{2,1,0:T(8,128)(2,1)S(1)} %get-tuple-element.31), channel_id=1, source_target_pairs={{12,0},{28,16},{13,1},{29,17},{14,2},{30,18},{15,3},{31,19}} | collective-permute-start | bytes 589832 | tf_op jit(solution)/shard_map/ppermute | solution.py:209
  13.8 6.1 %collective-permute-start.4 = (bf16[96,1024]{1,0:T(8,128)(2,1)S(1)}, bf16[96,1024]{1,0:T(8,128)(2,1)S(1)}, u32[]{:S(2)}, u32[]{:S(2)}) collective-permute-start(bf16[96,1024]{1,0:T(8,128)(2,1)S(1)} %get-tuple-element.27), channel_id=1, source_target_pairs={{0,4},{4,0},{8,12},{12,8},{16,20},{20,16},{24,28},{28,24},{1,5},{5... | collective-permute-start | bytes 589832 | tf_op jit(solution)/shard_map/ppermute | solution.py:205
  14.0 16.4 %collective-permute-start.12 = (bf16[3,64,2048]{2,1,0:T(8,128)(2,1)S(1)}, bf16[3,64,2048]{2,1,0:T(8,128)(2,1)S(1)}, u32[]{:S(2)}, u32[]{:S(2)}) collective-permute-start(bf16[3,64,2048]{2,1,0:T(8,128)(2,1)S(1)} %get-tuple-element.39), channel_id=1, source_target_pairs={{12,0},{28,16},{13,1},{29,17},{14,2},{30,18},{15,3},{31,19}} | collective-permute-start | bytes 2359304 | tf_op jit(solution)/shard_map/ppermute | solution.py:209
  19.9 8.4 %collective-permute-start.11 = (bf16[3,48,2048]{2,1,0:T(8,128)(2,1)S(1)}, bf16[3,48,2048]{2,1,0:T(8,128)(2,1)S(1)}, u32[]{:S(2)}, u32[]{:S(2)}) collective-permute-start(bf16[3,48,2048]{2,1,0:T(8,128)(2,1)S(1)} %collective-permute-done.6.shared_ref), channel_id=1, source_target_pairs={{4,5},{20,21},{5,4},{21,20},{6,7},{22,23},{7,6},{23,22}} | collective-permute-start | bytes 1769480 | tf_op jit(solution)/shard_map/ppermute | solution.py:217
  20.7 4.2 %collective-permute-start.8 = (bf16[24,1024]{1,0:T(8,128)(2,1)S(1)}, bf16[24,1024]{1,0:T(8,128)(2,1)S(1)}, u32[]{:S(2)}, u32[]{:S(2)}) collective-permute-start(bf16[24,1024]{1,0:T(8,128)(2,1)S(1)} %get-tuple-element.47), channel_id=1, source_target_pairs={{0,16},{4,20},{8,24},{12,28},{16,0},{20,4},{24,8},{28,12},{1,17},{... | collective-permute-start | bytes 147464 | tf_op jit(solution)/shard_map/ppermute | solution.py:205
  22.3 6.9 %collective-permute-start.7 = (bf16[24,1024]{1,0:T(8,128)(2,1)S(1)}, bf16[24,1024]{1,0:T(8,128)(2,1)S(1)}, u32[]{:S(2)}, u32[]{:S(2)}) collective-permute-start(bf16[24,1024]{1,0:T(8,128)(2,1)S(1)} %get-tuple-element.48), channel_id=1, source_target_pairs={{0,8},{4,12},{8,0},{12,4},{16,24},{20,28},{24,16},{28,20},{1,9},{5... | collective-permute-start | bytes 147464 | tf_op jit(solution)/shard_map/ppermute | solution.py:205
  24.9 5.6 %copy-start.5 = (f32[128,8]{0,1:T(8,128)S(1)}, f32[128,8]{0,1:T(8,128)}, u32[]{:S(2)}) copy-start(f32[128,8]{0,1:T(8,128)} %param.9) | copy-start | bytes 12292
  24.9 5.6 %collective-permute-start.10 = (bf16[24,1024]{1,0:T(8,128)(2,1)S(1)}, bf16[24,1024]{1,0:T(8,128)(2,1)S(1)}, u32[]{:S(2)}, u32[]{:S(2)}) collective-permute-start(bf16[24,1024]{1,0:T(8,128)(2,1)S(1)} %get-tuple-element.46), channel_id=1, source_target_pairs={{0,24},{4,28},{8,16},{12,20},{16,8},{20,12},{24,0},{28,4},{1,25},{... | collective-permute-start | bytes 147464 | tf_op jit(solution)/shard_map/ppermute | solution.py:205
  24.9 7.6 %collective-permute-start.13 = (bf16[3,16,2048]{2,1,0:T(8,128)(2,1)S(1)}, bf16[3,16,2048]{2,1,0:T(8,128)(2,1)S(1)}, u32[]{:S(2)}, u32[]{:S(2)}) collective-permute-start(bf16[3,16,2048]{2,1,0:T(8,128)(2,1)S(1)} %collective-permute-done.5.own_ref), channel_id=1, source_target_pairs={{0,1},{16,17},{1,0},{17,16},{2,3},{18,19},{3,2},{19,18}} | collective-permute-start | bytes 589832 | tf_op jit(solution)/shard_map/ppermute | solution.py:217

commit v18 on v16

--- a/solution.py
+++ b/solution.py
@@ -41,7 +41,7 @@
     return jnp.where(member > 0, rank - 1.0, -PACK).astype(jnp.int32)
 
 
-def dispatch_kernel(experts, ids_ref, tok_ref, begun_ref, *out_refs):
+def dispatch_kernel(experts, ids_ref, tok_ref, *out_refs):
     group = lax.axis_index("expert") // GROUP
     place = token_places(ids_ref[...], group, experts)
     tok, half = tok_ref.shape[0], tok_ref.shape[1] // 2
@@ -116,7 +116,7 @@
         place_rows([(near_ref, 0)], out_ref, sems)
 
 
-def late_kernel(early_ref, second_ref, out_ref, sems):
+def late_kernel(early_ref, second_ref, begun_ref, out_ref, sems):
     position = lax.axis_index("expert") % GROUP
 
     @pl.when(jnp.logical_or(position == 0, position == 3))
@@ -230,21 +230,25 @@
         cost_estimate=cost(5),
         name="begin",
     )()
+    ids, begun = lax.optimization_barrier((expert_ids.T, begun))
     parcels = pl.pallas_call(
         functools.partial(dispatch_kernel, experts),
         out_shape=[shape(PACK, width // 2)] * experts,
-        in_specs=[VMEM, VMEM, HBM],
+        in_specs=[VMEM, VMEM],
         out_specs=[VMEM] * experts,
         compiler_params=params(),
         cost_estimate=cost(2),
         name="dispatch",
-    )(expert_ids.T, tokens, begun)
+    )(ids, tokens)
 
     pairs = [(j, k) for j in range(experts) for k in (0, 2)]
-    mine = [parcels[0]] + [send(parcels[j], j, k) for j, k in pairs[1:]]
     held, _ = lax.optimization_barrier((weights, parcels))
     wanted = [(1, half, None), (0, lead, 0), (0, most - lead, lead), (2, most, 0)]
     chosen = select(wanted, held)
+    after, _ = lax.optimization_barrier((parcels, chosen))
+    mine = [parcels[0]]
+    for j, k in pairs[1:]:
+        mine.append(send(parcels[j] if k else after[j], j, k))
     shared = migrate(chosen[0], 1)
     first = migrate(chosen[1], 0)
     near = migrate(chosen[3], 2)
@@ -302,13 +306,13 @@
     arrived = pl.pallas_call(
         late_kernel,
         out_shape=shape(3, most, width),
-        in_specs=[HBM] * 2,
+        in_specs=[HBM] * 3,
         out_specs=HBM,
         input_output_aliases={0: 0},
         scratch_shapes=[pltpu.SemaphoreType.DMA((3,))],
         compiler_params=params(),
         name="late",
-    )(early, second)
+    )(early, second, begun)
     return mixed, arrived
 
 

time: 33.5 us -> 33 us (0.985)
  local copies, waits for them, and re-layouts: 1.19 us -> 0.51 us
    ppermute x8, waiting for transfers between devices: 4.17 us -> 5.63 us  [send(): return lax.ppermute(block, 'expert', route)]
    ppermute x4, waiting for transfers between devices: 6.04 us -> 4.75 us  [migrate(): return lax.ppermute(block, 'expert', route)]
    unnamed x19, local copies, waits for them, and re-layouts: 1.17 us -> 0.49 us
  transfers between devices with their start and end apart: 13 -> 13, of which waited for: 6 -> 7; matrix products, arithmetic and copies ran while one was open for 0% -> 0% of each run, Pallas kernels for 10% -> 10%
where the time goes in v18:
time: 33 us; the launch traced here: 32.8 us
  starting transfers between devices  16 us (48%)
  waiting for transfers between devices  10.4 us (32%)
  Pallas kernels  5.05 us (15%)
  between operations  0.8 us (2%)
  local copies, waits for them, and re-layouts  0.51 us (2%)
    ppermute x8, starting transfers between devices, send(): return lax.ppermute(block, 'expert', route)  11.3 us
    ppermute x8, waiting for transfers between devices, send(): return lax.ppermute(block, 'expert', route)  5.63 us
    ppermute x4, waiting for transfers between devices, migrate(): return lax.ppermute(block, 'expert', route)  4.75 us
    ppermute x4, starting transfers between devices, migrate(): return lax.ppermute(block, 'expert', route)  4.01 us
    pallas_call x1, Pallas kernels, on_device(): pl.pallas_call(functools.partial(combine_kernel, experts), out_shape=shap...  1.42 us
    pallas_call x1, Pallas kernels, on_device(): pl.pallas_call(early_kernel, out_shape=shape(3, most, width), in_specs=[H...  0.99 us
    pallas_call x1, Pallas kernels, on_device(): pl.pallas_call(expert_kernel, grid=(total // step,), out_shape=[shape(tot...  0.92 us
    pallas_call x1, Pallas kernels, on_device(): pl.pallas_call(late_kernel, out_shape=shape(3, most, width), in_specs=[HB...  0.7 us
  transfers between devices with their start and end apart: 13, of which 7 were waited for; matrix products, arithmetic and copies ran while one was open for 0% of the time, Pallas kernels for 10%

profile of v18, /device:TPU:0, one launch (start us, length us, event | category | flops | bytes accessed | tf_op | source)
XLA Modules:
  0.0 32.8 jit_solution(15944728184072133473)
XLA Ops:
  0.6 0.6 %begin.1.begun_ref = f32[8,128]{1,0:T(8,128)} custom-call(), custom_call_target="tpu_custom_call" | custom-call | flops 5000000000 | bytes 10000 | tf_op jit(solution)/shard_map/begin/pallas_call | solution.py:226
  1.2 0.1 copy-done.5
  1.3 0.4 %copy-done.4 = bf16[128,2048]{1,0:T(8,128)(2,1)S(1)} copy-done((bf16[128,2048]{1,0:T(8,128)(2,1)S(1)}, bf16[128,2048]{1,0:T(8,128)(2,1)}, u32[]{:S(2)}) %copy-start.4) | copy-done | bytes 524312
  1.7 0.4 %dispatch.1 = (bf16[24,1024]{1,0:T(8,128)(2,1)S(1)}, bf16[24,1024]{1,0:T(8,128)(2,1)S(1)}) custom-call(s32[8,128]{1,0:T(8,128)S(1)} %bitcast.3, bf16[128,2048]{1,0:T(8,128)(2,1)S(1)} %copy-done.4), custom_call_target="tpu_custom_call" | custom-call | flops 2000000000 | bytes 10000 | tf_op jit(solution)/shard_map/dispatch/pallas_call | solution.py:234
  2.1 4.0 %collective-permute-start.2 = (bf16[24,1024]{1,0:T(8,128)(2,1)S(1)}, bf16[24,1024]{1,0:T(8,128)(2,1)S(1)}, u32[]{:S(2)}, u32[]{:S(2)}) collective-permute-start(bf16[24,1024]{1,0:T(8,128)(2,1)S(1)} %get-tuple-element.36), channel_id=1, source_target_pairs={{0,24},{4,28},{8,16},{12,20},{16,8},{20,12},{24,0},{28,4},{1,25},{... | collective-permute-start | bytes 147464 | tf_op jit(solution)/shard_map/ppermute | solution.py:201
  6.1 0.5 %collective-permute-start = (bf16[24,1024]{1,0:T(8,128)(2,1)S(1)}, bf16[24,1024]{1,0:T(8,128)(2,1)S(1)}, u32[]{:S(2)}, u32[]{:S(2)}) collective-permute-start(bf16[24,1024]{1,0:T(8,128)(2,1)S(1)} %get-tuple-element.27), channel_id=1, source_target_pairs={{0,8},{4,12},{8,0},{12,4},{16,24},{20,28},{24,16},{28,20},{1,9},{5... | collective-permute-start | bytes 147464 | tf_op jit(solution)/shard_map/ppermute | solution.py:201
  6.7 0.7 %collective-permute-start.5 = (bf16[3,48,2048]{2,1,0:T(8,128)(2,1)S(1)}, bf16[3,48,2048]{2,1,0:T(8,128)(2,1)S(1)}, u32[]{:S(2)}, u32[]{:S(2)}) collective-permute-start(bf16[3,48,2048]{2,1,0:T(8,128)(2,1)S(1)} %get-tuple-element.32), channel_id=1, source_target_pairs={{12,4},{28,20},{13,5},{29,21},{14,6},{30,22},{15,7},{31,23}} | collective-permute-start | bytes 1769480 | tf_op jit(solution)/shard_map/ppermute | solution.py:205
  7.4 0.7 %collective-permute-start.8 = (bf16[3,96,2048]{2,1,0:T(8,128)(2,1)S(1)}, bf16[3,96,2048]{2,1,0:T(8,128)(2,1)S(1)}, u32[]{:S(2)}, u32[]{:S(2)}) collective-permute-start(bf16[3,96,2048]{2,1,0:T(8,128)(2,1)S(1)} %get-tuple-element.35), channel_id=1, source_target_pairs={{12,8},{28,24},{13,9},{29,25},{14,10},{30,26},{15,11},{31,27}} | collective-permute-start | bytes 3538952 | tf_op jit(solution)/shard_map/ppermute | solution.py:205
  8.1 0.2 collective-permute-start.1
  8.3 1.9 %collective-permute-done = bf16[24,1024]{1,0:T(8,128)(2,1)S(1)} collective-permute-done((bf16[24,1024]{1,0:T(8,128)(2,1)S(1)}, bf16[24,1024]{1,0:T(8,128)(2,1)S(1)}, u32[]{:S(2)}, u32[]{:S(2)}) %collective-permute-start) | collective-permute-done | bytes 49184 | tf_op jit(solution)/shard_map/ppermute | solution.py:201
  10.2 2.1 %collective-permute-done.1 = bf16[24,1024]{1,0:T(8,128)(2,1)S(1)} collective-permute-done((bf16[24,1024]{1,0:T(8,128)(2,1)S(1)}, bf16[24,1024]{1,0:T(8,128)(2,1)S(1)}, u32[]{:S(2)}, u32[]{:S(2)}) %collective-permute-start.1) | collective-permute-done | bytes 49184 | tf_op jit(solution)/shard_map/ppermute | solution.py:201
  12.3 0.0 collective-permute-done.2
  12.3 0.1 collective-permute-start.3
  12.4 1.3 %collective-permute-start.11 = (bf16[3,80,2048]{2,1,0:T(8,128)(2,1)S(1)}, bf16[3,80,2048]{2,1,0:T(8,128)(2,1)S(1)}, u32[]{:S(2)}, u32[]{:S(2)}) collective-permute-start(bf16[3,80,2048]{2,1,0:T(8,128)(2,1)S(1)} %get-tuple-element.33), channel_id=1, source_target_pairs={{12,0},{28,16},{13,1},{29,17},{14,2},{30,18},{15,3},{31,19}} | collective-permute-start | bytes 2949128 | tf_op jit(solution)/shard_map/ppermute | solution.py:205
  13.7 0.1 collective-permute-done.3.other_ref
  13.8 0.9 %expert.1 = (f32[96,1024]{1,0:T(8,128)S(1)}, bf16[96,1024]{1,0:T(8,128)(2,1)S(1)}) custom-call(bf16[96,1024]{1,0:T(8,128)(2,1)S(1)} %constant_dynamic-update-slice_fusion.mine_ref, bf16[96,1024]{1,0:T(8,128)(2,1)S(1)} %collective-permute-done.3.other_ref, bf16[192,2048]{1,0:T(8,128)(2,1)S(1)} %copy-done, bf16[192,2048]{1,0:T(8,128)(2,1)S(1)} %copy-done.1, ...), custom_call_target="tpu_custom_call" | custom-call | bytes 10000 | tf_op jit(solution)/shard_map/expert/pallas_call | solution.py:262
  14.7 0.2 collective-permute-start.4
  14.9 1.3 %collective-permute-done.4 = bf16[96,1024]{1,0:T(8,128)(2,1)S(1)} collective-permute-done((bf16[96,1024]{1,0:T(8,128)(2,1)S(1)}, bf16[96,1024]{1,0:T(8,128)(2,1)S(1)}, u32[]{:S(2)}, u32[]{:S(2)}) %collective-permute-start.4) | collective-permute-done | bytes 196640 | tf_op jit(solution)/shard_map/ppermute | solution.py:201
  16.2 0.0 collective-permute-done.5.shared_ref
  16.2 0.7 %collective-permute-start.10 = (bf16[3,48,2048]{2,1,0:T(8,128)(2,1)S(1)}, bf16[3,48,2048]{2,1,0:T(8,128)(2,1)S(1)}, u32[]{:S(2)}, u32[]{:S(2)}) collective-permute-start(bf16[3,48,2048]{2,1,0:T(8,128)(2,1)S(1)} %collective-permute-done.5.shared_ref), channel_id=1, source_target_pairs={{4,5},{20,21},{5,4},{21,20},{6,7},{22,23},{7,6},{23,22}} | collective-permute-start | bytes 1769480 | tf_op jit(solution)/shard_map/ppermute | solution.py:213
  17.0 0.2 collective-permute-start.7
  17.2 3.8 %collective-permute-start.9 = (bf16[24,1024]{1,0:T(8,128)(2,1)S(1)}, bf16[24,1024]{1,0:T(8,128)(2,1)S(1)}, u32[]{:S(2)}, u32[]{:S(2)}) collective-permute-start(bf16[24,1024]{1,0:T(8,128)(2,1)S(1)} %get-tuple-element.50), channel_id=1, source_target_pairs={{0,24},{4,28},{8,16},{12,20},{16,8},{20,12},{24,0},{28,4},{1,25},{... | collective-permute-start | bytes 147464 | tf_op jit(solution)/shard_map/ppermute | solution.py:201
  20.9 0.2 collective-permute-done.7.refs_2_
  21.2 2.4 %collective-permute-start.6 = (bf16[24,1024]{1,0:T(8,128)(2,1)S(1)}, bf16[24,1024]{1,0:T(8,128)(2,1)S(1)}, u32[]{:S(2)}, u32[]{:S(2)}) collective-permute-start(bf16[24,1024]{1,0:T(8,128)(2,1)S(1)} %get-tuple-element.52), channel_id=1, source_target_pairs={{0,8},{4,12},{8,0},{12,4},{16,24},{20,28},{24,16},{28,20},{1,9},{5... | collective-permute-start | bytes 147464 | tf_op jit(solution)/shard_map/ppermute | solution.py:201
  23.6 1.3 %collective-permute-start.12 = (bf16[3,16,2048]{2,1,0:T(8,128)(2,1)S(1)}, bf16[3,16,2048]{2,1,0:T(8,128)(2,1)S(1)}, u32[]{:S(2)}, u32[]{:S(2)}) collective-permute-start(bf16[3,16,2048]{2,1,0:T(8,128)(2,1)S(1)} %get-tuple-element.48), channel_id=1, source_target_pairs={{12,0},{28,16},{13,1},{29,17},{14,2},{30,18},{15,3},{31,19}} | collective-permute-start | bytes 589832 | tf_op jit(solution)/shard_map/ppermute | solution.py:205
  24.9 4.0 %collective-permute-done.11.first_ref = bf16[3,80,2048]{2,1,0:T(8,128)(2,1)S(1)} collective-permute-done((bf16[3,80,2048]{2,1,0:T(8,128)(2,1)S(1)}, bf16[3,80,2048]{2,1,0:T(8,128)(2,1)S(1)}, u32[]{:S(2)}, u32[]{:S(2)}) %collective-permute-start.11) | collective-permute-done | bytes 983072 | tf_op jit(solution)/shard_map/ppermute | solution.py:205
  28.9 0.0 collective-permute-done.10.swapped_ref
  28.9 1.0 %early.1.early_ref = bf16[3,96,2048]{2,1,0:T(8,128)(2,1)} custom-call(bf16[3,48,2048]{2,1,0:T(8,128)(2,1)S(1)} %collective-permute-done.5.shared_ref, bf16[3,48,2048]{2,1,0:T(8,128)(2,1)S(1)} %collective-permute-done.10.swapped_ref, bf16[3,80,2048]{2,1,0:T(8,128)(2,1)S(1)} %collective-permute-done.11.first_ref, ...), custom_call_target="tpu_custom_call" | custom-call | tf_op jit(solution)/shard_map/early/pallas_call | solution.py:284
  29.9 0.0 collective-permute-done.9.refs_3_
  29.9 1.4 %combine.1 = bf16[128,2048]{1,0:T(8,128)(2,1)} custom-call(s32[8,128]{1,0:T(8,128)S(1)} %bitcast.4, f32[8,128]{1,0:T(8,128)S(1)} %bitcast.5, bf16[24,1024]{1,0:T(8,128)(2,1)S(1)} %get-tuple-element.43.refs_0_, bf16[24,1024]{1,0:T(8,128)(2,1)S(1)} %collective-permute-done.6.refs_1_, bf16[24,1024]{1,0:T(8,128)(2,1)S(1)} %collective-permute-done.7.refs_2_, ...), custom_call_target="tpu_custom_call" | custom-call | flops 3000000000 | bytes 10000 | tf_op jit(solution)/shard_map/combine/pallas_call | solution.py:295
  31.4 0.7 %collective-permute-done.12.second_ref = bf16[3,16,2048]{2,1,0:T(8,128)(2,1)S(1)} collective-permute-done((bf16[3,16,2048]{2,1,0:T(8,128)(2,1)S(1)}, bf16[3,16,2048]{2,1,0:T(8,128)(2,1)S(1)}, u32[]{:S(2)}, u32[]{:S(2)}) %collective-permute-start.12) | collective-permute-done | bytes 196640 | tf_op jit(solution)/shard_map/ppermute | solution.py:205
  32.1 0.7 %late.1 = bf16[3,96,2048]{2,1,0:T(8,128)(2,1)} custom-call(bf16[3,96,2048]{2,1,0:T(8,128)(2,1)} %early.1.early_ref, bf16[3,16,2048]{2,1,0:T(8,128)(2,1)S(1)} %collective-permute-done.12.second_ref, f32[8,128]{1,0:T(8,128)S(1)} %copy-done.3), custom_call_target="tpu_custom_call", output_to_operand_aliasing={{}: (0, {})} | custom-call | tf_op jit(solution)/shard_map/late/pallas_call | solution.py:306
  (23 shorter events, 0.1 us)
Async XLA Ops:
  0.6 0.7 %copy-start.5 = (s32[128,8]{0,1:T(8,128)S(1)}, s32[128,8]{0,1:T(8,128)}, u32[]{:S(2)}) copy-start(s32[128,8]{0,1:T(8,128)} %param.8) | copy-start | bytes 12292
  0.6 1.1 %copy-start.4 = (bf16[128,2048]{1,0:T(8,128)(2,1)S(1)}, bf16[128,2048]{1,0:T(8,128)(2,1)}, u32[]{:S(2)}) copy-start(bf16[128,2048]{1,0:T(8,128)(2,1)} %tok_ref.1) | copy-start | bytes 1572868
  1.7 4.9 %copy-start = (bf16[192,2048]{1,0:T(8,128)(2,1)S(1)}, bf16[192,2048]{1,0:T(8,128)(2,1)}, u32[]{:S(2)}) copy-start(bf16[192,2048]{1,0:T(8,128)(2,1)} %gate_ref.2) | copy-start | bytes 2359300
  1.7 4.9 %copy-start.1 = (bf16[192,2048]{1,0:T(8,128)(2,1)S(1)}, bf16[192,2048]{1,0:T(8,128)(2,1)}, u32[]{:S(2)}) copy-start(bf16[192,2048]{1,0:T(8,128)(2,1)} %up_ref.2) | copy-start | bytes 2359300
  1.7 4.9 %copy-start.2 = (bf16[192,2048]{1,0:T(8,128)(2,1)S(1)}, bf16[192,2048]{1,0:T(8,128)(2,1)}, u32[]{:S(2)}) copy-start(bf16[192,2048]{1,0:T(8,128)(2,1)} %down_ref.2) | copy-start | bytes 2359300
  1.7 4.9 %copy-start.7 = (s32[2,3,96]{2,0,1:T(2,128)S(1)}, s32[2,3,96]{2,0,1:T(2,128)}, u32[]{:S(2)}) copy-start(s32[2,3,96]{2,0,1:T(2,128)} %param.13) | copy-start | bytes 6916
  2.1 10.2 %collective-permute-start.2 = (bf16[24,1024]{1,0:T(8,128)(2,1)S(1)}, bf16[24,1024]{1,0:T(8,128)(2,1)S(1)}, u32[]{:S(2)}, u32[]{:S(2)}) collective-permute-start(bf16[24,1024]{1,0:T(8,128)(2,1)S(1)} %get-tuple-element.36), channel_id=1, source_target_pairs={{0,24},{4,28},{8,16},{12,20},{16,8},{20,12},{24,0},{28,4},{1,25},{... | collective-permute-start | bytes 147464 | tf_op jit(solution)/shard_map/ppermute | solution.py:201
  6.1 4.1 %collective-permute-start = (bf16[24,1024]{1,0:T(8,128)(2,1)S(1)}, bf16[24,1024]{1,0:T(8,128)(2,1)S(1)}, u32[]{:S(2)}, u32[]{:S(2)}) collective-permute-start(bf16[24,1024]{1,0:T(8,128)(2,1)S(1)} %get-tuple-element.27), channel_id=1, source_target_pairs={{0,8},{4,12},{8,0},{12,4},{16,24},{20,28},{24,16},{28,20},{1,9},{5... | collective-permute-start | bytes 147464 | tf_op jit(solution)/shard_map/ppermute | solution.py:201
  6.7 9.6 %collective-permute-start.5 = (bf16[3,48,2048]{2,1,0:T(8,128)(2,1)S(1)}, bf16[3,48,2048]{2,1,0:T(8,128)(2,1)S(1)}, u32[]{:S(2)}, u32[]{:S(2)}) collective-permute-start(bf16[3,48,2048]{2,1,0:T(8,128)(2,1)S(1)} %get-tuple-element.32), channel_id=1, source_target_pairs={{12,4},{28,20},{13,5},{29,21},{14,6},{30,22},{15,7},{31,23}} | collective-permute-start | bytes 1769480 | tf_op jit(solution)/shard_map/ppermute | solution.py:205
  7.4 16.2 %collective-permute-start.8 = (bf16[3,96,2048]{2,1,0:T(8,128)(2,1)S(1)}, bf16[3,96,2048]{2,1,0:T(8,128)(2,1)S(1)}, u32[]{:S(2)}, u32[]{:S(2)}) collective-permute-start(bf16[3,96,2048]{2,1,0:T(8,128)(2,1)S(1)} %get-tuple-element.35), channel_id=1, source_target_pairs={{12,8},{28,24},{13,9},{29,25},{14,10},{30,26},{15,11},{31,27}} | collective-permute-start | bytes 3538952 | tf_op jit(solution)/shard_map/ppermute | solution.py:205
  8.1 4.2 %collective-permute-start.1 = (bf16[24,1024]{1,0:T(8,128)(2,1)S(1)}, bf16[24,1024]{1,0:T(8,128)(2,1)S(1)}, u32[]{:S(2)}, u32[]{:S(2)}) collective-permute-start(bf16[24,1024]{1,0:T(8,128)(2,1)S(1)} %get-tuple-element.36), channel_id=1, source_target_pairs={{0,16},{4,20},{8,24},{12,28},{16,0},{20,4},{24,8},{28,12},{1,17},{... | collective-permute-start | bytes 147464 | tf_op jit(solution)/shard_map/ppermute | solution.py:201
  12.3 1.5 %collective-permute-start.3 = (bf16[96,1024]{1,0:T(8,128)(2,1)S(1)}, bf16[96,1024]{1,0:T(8,128)(2,1)S(1)}, u32[]{:S(2)}, u32[]{:S(2)}) collective-permute-start(bf16[96,1024]{1,0:T(8,128)(2,1)S(1)} %constant_dynamic-update-slice_fusion.mine_ref), channel_id=1, source_target_pairs={{0,4},{4,0},{8,12},{12,8},{16,20},{20,16},{24,28},{28,24},{1,5},{5... | collective-permute-start | bytes 589832 | tf_op jit(solution)/shard_map/ppermute | solution.py:201
  12.4 16.5 %collective-permute-start.11 = (bf16[3,80,2048]{2,1,0:T(8,128)(2,1)S(1)}, bf16[3,80,2048]{2,1,0:T(8,128)(2,1)S(1)}, u32[]{:S(2)}, u32[]{:S(2)}) collective-permute-start(bf16[3,80,2048]{2,1,0:T(8,128)(2,1)S(1)} %get-tuple-element.33), channel_id=1, source_target_pairs={{12,0},{28,16},{13,1},{29,17},{14,2},{30,18},{15,3},{31,19}} | collective-permute-start | bytes 2949128 | tf_op jit(solution)/shard_map/ppermute | solution.py:205
  14.7 1.5 %collective-permute-start.4 = (bf16[96,1024]{1,0:T(8,128)(2,1)S(1)}, bf16[96,1024]{1,0:T(8,128)(2,1)S(1)}, u32[]{:S(2)}, u32[]{:S(2)}) collective-permute-start(bf16[96,1024]{1,0:T(8,128)(2,1)S(1)} %get-tuple-element.38), channel_id=1, source_target_pairs={{0,4},{4,0},{8,12},{12,8},{16,20},{20,16},{24,28},{28,24},{1,5},{5... | collective-permute-start | bytes 589832 | tf_op jit(solution)/shard_map/ppermute | solution.py:201
  16.2 12.7 %collective-permute-start.10 = (bf16[3,48,2048]{2,1,0:T(8,128)(2,1)S(1)}, bf16[3,48,2048]{2,1,0:T(8,128)(2,1)S(1)}, u32[]{:S(2)}, u32[]{:S(2)}) collective-permute-start(bf16[3,48,2048]{2,1,0:T(8,128)(2,1)S(1)} %collective-permute-done.5.shared_ref), channel_id=1, source_target_pairs={{4,5},{20,21},{5,4},{21,20},{6,7},{22,23},{7,6},{23,22}} | collective-permute-start | bytes 1769480 | tf_op jit(solution)/shard_map/ppermute | solution.py:213
  17.0 4.2 %collective-permute-start.7 = (bf16[24,1024]{1,0:T(8,128)(2,1)S(1)}, bf16[24,1024]{1,0:T(8,128)(2,1)S(1)}, u32[]{:S(2)}, u32[]{:S(2)}) collective-permute-start(bf16[24,1024]{1,0:T(8,128)(2,1)S(1)} %get-tuple-element.51), channel_id=1, source_target_pairs={{0,16},{4,20},{8,24},{12,28},{16,0},{20,4},{24,8},{28,12},{1,17},{... | collective-permute-start | bytes 147464 | tf_op jit(solution)/shard_map/ppermute | solution.py:201
  17.2 12.7 %collective-permute-start.9 = (bf16[24,1024]{1,0:T(8,128)(2,1)S(1)}, bf16[24,1024]{1,0:T(8,128)(2,1)S(1)}, u32[]{:S(2)}, u32[]{:S(2)}) collective-permute-start(bf16[24,1024]{1,0:T(8,128)(2,1)S(1)} %get-tuple-element.50), channel_id=1, source_target_pairs={{0,24},{4,28},{8,16},{12,20},{16,8},{20,12},{24,0},{28,4},{1,25},{... | collective-permute-start | bytes 147464 | tf_op jit(solution)/shard_map/ppermute | solution.py:201
  21.2 8.8 %copy-start.6 = (f32[128,8]{0,1:T(8,128)S(1)}, f32[128,8]{0,1:T(8,128)}, u32[]{:S(2)}) copy-start(f32[128,8]{0,1:T(8,128)} %param.9) | copy-start | bytes 12292
  21.2 8.8 %collective-permute-start.6 = (bf16[24,1024]{1,0:T(8,128)(2,1)S(1)}, bf16[24,1024]{1,0:T(8,128)(2,1)S(1)}, u32[]{:S(2)}, u32[]{:S(2)}) collective-permute-start(bf16[24,1024]{1,0:T(8,128)(2,1)S(1)} %get-tuple-element.52), channel_id=1, source_target_pairs={{0,8},{4,12},{8,0},{12,4},{16,24},{20,28},{24,16},{28,20},{1,9},{5... | collective-permute-start | bytes 147464 | tf_op jit(solution)/shard_map/ppermute | solution.py:201
  23.6 8.5 %collective-permute-start.12 = (bf16[3,16,2048]{2,1,0:T(8,128)(2,1)S(1)}, bf16[3,16,2048]{2,1,0:T(8,128)(2,1)S(1)}, u32[]{:S(2)}, u32[]{:S(2)}) collective-permute-start(bf16[3,16,2048]{2,1,0:T(8,128)(2,1)S(1)} %get-tuple-element.48), channel_id=1, source_target_pairs={{12,0},{28,16},{13,1},{29,17},{14,2},{30,18},{15,3},{31,19}} | collective-permute-start | bytes 589832 | tf_op jit(solution)/shard_map/ppermute | solution.py:205
  29.9 2.1 %copy-start.3 = (f32[8,128]{1,0:T(8,128)S(1)}, f32[8,128]{1,0:T(8,128)}, u32[]{:S(2)}) copy-start(f32[8,128]{1,0:T(8,128)} %begin.1.begun_ref) | copy-start | bytes 12292

commit v19 on v14

--- a/solution.py
+++ b/solution.py
@@ -41,7 +41,7 @@
     return jnp.where(member > 0, rank - 1.0, -PACK).astype(jnp.int32)
 
 
-def dispatch_kernel(experts, ids_ref, tok_ref, begun_ref, *out_refs):
+def dispatch_kernel(experts, ids_ref, tok_ref, *out_refs):
     group = lax.axis_index("expert") // GROUP
     place = token_places(ids_ref[...], group, experts)
     tok, half = tok_ref.shape[0], tok_ref.shape[1] // 2
@@ -108,7 +108,7 @@
             place_rows([(shared_ref, half * even), (swapped_ref, half * (1 - even))], out_ref, sems)
 
 
-def late_kernel(early_ref, straight_ref, near_ref, out_ref, sems):
+def late_kernel(early_ref, straight_ref, near_ref, begun_ref, out_ref, sems):
     position = lax.axis_index("expert") % GROUP
 
     @pl.when(jnp.logical_or(position == 0, position == 3))
@@ -147,31 +147,37 @@
     give_ref[...] = partial[rows:].astype(BF16)
 
 
-def combine_kernel(experts, ids_ref, weight_ref, *refs):
-    piece_refs, (out_ref, rows_ref) = refs[:-2], refs[-2:]
+def weigh_kernel(experts, ids_ref, weight_ref, out_ref):
     ids = ids_ref[...]
     group = lax.axis_index("expert") // GROUP
-    half = out_ref.shape[1] // 2
-    each = len(piece_refs) // experts
     place = token_places(ids, group, experts)
+    each = out_ref.shape[2] // STRIDE // experts
     slot = lax.broadcasted_iota(jnp.int32, (STRIDE, ids.shape[1]), 0)
-    numbers = (((0,), (0,)), ((), ()))
-    rows_ref[...] = jnp.zeros_like(rows_ref)
-    for n, ref in enumerate(piece_refs):
-        rows_ref[n * STRIDE : n * STRIDE + PACK, :] = ref[...]
-    scaled = [[], []]
     for j in range(experts):
         named = ids == lax.rem(group + j, experts)
         weight = jnp.sum(jnp.where(named, weight_ref[...], 0.0), axis=0, keepdims=True)
         for side in range(2):
             chosen = jnp.where(slot == place[j : j + 1, :] + side * CAP, weight, 0.0)
-            scaled[side] += [chosen] * each
+            high = chosen.astype(BF16)
+            low = (chosen - high.astype(F32)).astype(BF16)
+            for n in range(j * each, (j + 1) * each):
+                out_ref[side, 0, n * STRIDE : (n + 1) * STRIDE, :] = high
+                out_ref[side, 1, n * STRIDE : (n + 1) * STRIDE, :] = low
+
+
+def combine_kernel(scaled_ref, *refs):
+    piece_refs, (out_ref, rows_ref) = refs[:-2], refs[-2:]
+    half = out_ref.shape[1] // 2
+    numbers = (((0,), (0,)), ((), ()))
+    for n, ref in enumerate(piece_refs):
+        rows_ref[n * STRIDE : n * STRIDE + PACK, :] = ref[...]
+        rows_ref[n * STRIDE + PACK : (n + 1) * STRIDE, :] = jnp.zeros((STRIDE - PACK, half), BF16)
+    rows = rows_ref[...]
     for side in range(2):
-        chosen = jnp.concatenate(scaled[side], axis=0)
-        high = chosen.astype(BF16)
-        low = (chosen - high.astype(F32)).astype(BF16)
-        mixed = lax.dot_general(high, rows_ref[...], numbers, preferred_element_type=F32)
-        mixed = mixed + lax.dot_general(low, rows_ref[...], numbers, preferred_element_type=F32)
+        mixed = lax.dot_general(scaled_ref[side, 0], rows, numbers, preferred_element_type=F32)
+        mixed = mixed + lax.dot_general(
+            scaled_ref[side, 1], rows, numbers, preferred_element_type=F32
+        )
         out_ref[:, side * half : (side + 1) * half] = mixed.astype(BF16)
 
 
@@ -225,21 +231,25 @@
         cost_estimate=cost(5),
         name="begin",
     )()
+    ids, begun = lax.optimization_barrier((expert_ids.T, begun))
     parcels = pl.pallas_call(
         functools.partial(dispatch_kernel, experts),
         out_shape=[shape(PACK, width // 2)] * experts,
-        in_specs=[VMEM, VMEM, HBM],
+        in_specs=[VMEM, VMEM],
         out_specs=[VMEM] * experts,
         compiler_params=params(),
         cost_estimate=cost(2),
         name="dispatch",
-    )(expert_ids.T, tokens, begun)
+    )(ids, tokens)
 
     pairs = [(j, k) for j in range(experts) for k in (0, 2)]
-    mine = [parcels[0]] + [send(parcels[j], j, k) for j, k in pairs[1:]]
     held, _ = lax.optimization_barrier((weights, parcels))
     wanted = [(1, half, None), (0, most, 0), (2, most, 0)]
     chosen = select(wanted, held)
+    after, _ = lax.optimization_barrier((parcels, chosen))
+    mine = [parcels[0]]
+    for j, k in pairs[1:]:
+        mine.append(send(parcels[j] if k else after[j], j, k))
     shared = migrate(chosen[0], 1)
     straight = migrate(chosen[1], 0)
     mine = jnp.concatenate(mine, axis=0)
@@ -269,6 +279,16 @@
     swapped, near = lax.optimization_barrier((swapped, chosen[2]))
     near = migrate(near, 2)
 
+    scaled = pl.pallas_call(
+        functools.partial(weigh_kernel, experts),
+        out_shape=shape(2, 2, len(back) * STRIDE, tokens.shape[0]),
+        in_specs=[VMEM, VMEM],
+        out_specs=VMEM,
+        compiler_params=params(),
+        name="weigh",
+    )(expert_ids.T, combine.T)
+    swapped, scaled = lax.optimization_barrier((swapped, scaled))
+
     early = pl.pallas_call(
         early_kernel,
         out_shape=shape(3, most, width),
@@ -281,26 +301,26 @@
     back, early, straight = lax.optimization_barrier((back, early, straight))
 
     mixed = pl.pallas_call(
-        functools.partial(combine_kernel, experts),
+        combine_kernel,
         out_shape=shape(tokens.shape[0], width),
-        in_specs=[VMEM, VMEM] + [VMEM] * len(back),
+        in_specs=[VMEM] + [VMEM] * len(back),
         out_specs=VMEM,
         scratch_shapes=[pltpu.VMEM((len(back) * STRIDE, width // 2), BF16)],
-        compiler_params=params(14 + experts),
+        compiler_params=params(),
         cost_estimate=cost(12.3),
         name="combine",
-    )(expert_ids.T, combine.T, *back)
+    )(scaled, *back)
 
     arrived = pl.pallas_call(
         late_kernel,
         out_shape=shape(3, most, width),
-        in_specs=[HBM] * 3,
+        in_specs=[HBM] * 4,
         out_specs=HBM,
         input_output_aliases={0: 0},
         scratch_shapes=[pltpu.SemaphoreType.DMA((3,))],
         compiler_params=params(),
         name="late",
-    )(early, straight, near)
+    )(early, straight, near, begun)
     return mixed, arrived
 
 

time: 34.2 us -> 33.1 us (0.968)
  local copies, waits for them, and re-layouts: 1.19 us -> 0.52 us
  waiting for transfers between devices: 15.5 us -> 15.1 us
    ppermute x3, waiting for transfers between devices: 8.6 us -> 5.47 us  [migrate(): return lax.ppermute(block, 'expert', route)]
    ppermute x8, waiting for transfers between devices: 6.86 us -> 9.66 us  [send(): return lax.ppermute(block, 'expert', route)]
    unnamed x19, local copies, waits for them, and re-layouts: 1.17 us -> 0.5 us
    pallas_call x1 -> x2, Pallas kernels: 1.41 us -> 1.41 us  [the longest x1 1.25 us: on_device(): pl.pallas_call(combine_kernel, out_shape=shape(tokens.shape[0], width), i...]
  transfers between devices with their start and end apart: 12 -> 12, of which waited for: 7 -> 8; matrix products, arithmetic and copies ran while one was open for 0% -> 0% of each run, Pallas kernels for 7% -> 7%
where the time goes in v19:
time: 33.1 us; the launch traced here: 32.9 us
  waiting for transfers between devices  15.1 us (46%)
  starting transfers between devices  11.9 us (36%)
  Pallas kernels  4.47 us (14%)
  between operations  0.78 us (2%)
  local copies, waits for them, and re-layouts  0.52 us (2%)
    ppermute x8, waiting for transfers between devices, send(): return lax.ppermute(block, 'expert', route)  9.66 us
    ppermute x8, starting transfers between devices, send(): return lax.ppermute(block, 'expert', route)  8.5 us
    ppermute x3, waiting for transfers between devices, migrate(): return lax.ppermute(block, 'expert', route)  5.47 us
    ppermute x3, starting transfers between devices, migrate(): return lax.ppermute(block, 'expert', route)  2.72 us
    pallas_call x1, Pallas kernels, on_device(): pl.pallas_call(combine_kernel, out_shape=shape(tokens.shape[0], width), i...  1.25 us
    pallas_call x1, Pallas kernels, on_device(): pl.pallas_call(late_kernel, out_shape=shape(3, most, width), in_specs=[HB...  1.03 us
    pallas_call x1, Pallas kernels, on_device(): pl.pallas_call(expert_kernel, grid=(total // step,), out_shape=[shape(tot...  0.92 us
    ppermute x1, starting transfers between devices, swap(): return lax.ppermute(block, ('expert', 'replica'), route)  0.69 us
  transfers between devices with their start and end apart: 12, of which 8 were waited for; matrix products, arithmetic and copies ran while one was open for 0% of the time, Pallas kernels for 7%

profile of v19, /device:TPU:0, one launch (start us, length us, event | category | flops | bytes accessed | tf_op | source)
XLA Modules:
  0.0 32.9 jit_solution(11896907628495692597)
XLA Ops:
  0.6 0.6 %begin.1.begun_ref = f32[8,128]{1,0:T(8,128)} custom-call(), custom_call_target="tpu_custom_call" | custom-call | flops 5000000000 | bytes 10000 | tf_op jit(solution)/shard_map/begin/pallas_call | solution.py:227
  1.2 0.1 copy-done.3
  1.3 0.4 %copy-done.6 = bf16[128,2048]{1,0:T(8,128)(2,1)S(1)} copy-done((bf16[128,2048]{1,0:T(8,128)(2,1)S(1)}, bf16[128,2048]{1,0:T(8,128)(2,1)}, u32[]{:S(2)}) %copy-start.6) | copy-done | bytes 524312
  1.7 0.4 %dispatch.1 = (bf16[24,1024]{1,0:T(8,128)(2,1)S(1)}, bf16[24,1024]{1,0:T(8,128)(2,1)S(1)}) custom-call(s32[8,128]{1,0:T(8,128)S(1)} %bitcast.3, bf16[128,2048]{1,0:T(8,128)(2,1)S(1)} %copy-done.6), custom_call_target="tpu_custom_call" | custom-call | flops 2000000000 | bytes 10000 | tf_op jit(solution)/shard_map/dispatch/pallas_call | solution.py:235
  2.1 4.0 %collective-permute-start.2 = (bf16[24,1024]{1,0:T(8,128)(2,1)S(1)}, bf16[24,1024]{1,0:T(8,128)(2,1)S(1)}, u32[]{:S(2)}, u32[]{:S(2)}) collective-permute-start(bf16[24,1024]{1,0:T(8,128)(2,1)S(1)} %get-tuple-element.36), channel_id=1, source_target_pairs={{0,24},{4,28},{8,16},{12,20},{16,8},{20,12},{24,0},{28,4},{1,25},{... | collective-permute-start | bytes 147464 | tf_op jit(solution)/shard_map/ppermute | solution.py:202
  6.1 0.5 %collective-permute-start = (bf16[24,1024]{1,0:T(8,128)(2,1)S(1)}, bf16[24,1024]{1,0:T(8,128)(2,1)S(1)}, u32[]{:S(2)}, u32[]{:S(2)}) collective-permute-start(bf16[24,1024]{1,0:T(8,128)(2,1)S(1)} %get-tuple-element.28), channel_id=1, source_target_pairs={{0,8},{4,12},{8,0},{12,4},{16,24},{20,28},{24,16},{28,20},{1,9},{5... | collective-permute-start | bytes 147464 | tf_op jit(solution)/shard_map/ppermute | solution.py:202
  6.7 0.7 %collective-permute-start.5 = (bf16[3,48,2048]{2,1,0:T(8,128)(2,1)S(1)}, bf16[3,48,2048]{2,1,0:T(8,128)(2,1)S(1)}, u32[]{:S(2)}, u32[]{:S(2)}) collective-permute-start(bf16[3,48,2048]{2,1,0:T(8,128)(2,1)S(1)} %get-tuple-element.33), channel_id=1, source_target_pairs={{12,4},{28,20},{13,5},{29,21},{14,6},{30,22},{15,7},{31,23}} | collective-permute-start | bytes 1769480 | tf_op jit(solution)/shard_map/ppermute | solution.py:206
  7.4 1.3 %collective-permute-start.10 = (bf16[3,96,2048]{2,1,0:T(8,128)(2,1)S(1)}, bf16[3,96,2048]{2,1,0:T(8,128)(2,1)S(1)}, u32[]{:S(2)}, u32[]{:S(2)}) collective-permute-start(bf16[3,96,2048]{2,1,0:T(8,128)(2,1)S(1)} %get-tuple-element.34), channel_id=1, source_target_pairs={{12,0},{28,16},{13,1},{29,17},{14,2},{30,18},{15,3},{31,19}} | collective-permute-start | bytes 3538952 | tf_op jit(solution)/shard_map/ppermute | solution.py:206
  8.7 0.2 collective-permute-start.1
  8.8 1.3 %collective-permute-done = bf16[24,1024]{1,0:T(8,128)(2,1)S(1)} collective-permute-done((bf16[24,1024]{1,0:T(8,128)(2,1)S(1)}, bf16[24,1024]{1,0:T(8,128)(2,1)S(1)}, u32[]{:S(2)}, u32[]{:S(2)}) %collective-permute-start) | collective-permute-done | bytes 49184 | tf_op jit(solution)/shard_map/ppermute | solution.py:202
  10.2 2.6 %collective-permute-done.1 = bf16[24,1024]{1,0:T(8,128)(2,1)S(1)} collective-permute-done((bf16[24,1024]{1,0:T(8,128)(2,1)S(1)}, bf16[24,1024]{1,0:T(8,128)(2,1)S(1)}, u32[]{:S(2)}, u32[]{:S(2)}) %collective-permute-start.1) | collective-permute-done | bytes 49184 | tf_op jit(solution)/shard_map/ppermute | solution.py:202
  12.8 0.0 collective-permute-done.2
  12.8 0.1 collective-permute-start.3
  12.9 1.4 %collective-permute-done.3.other_ref = bf16[96,1024]{1,0:T(8,128)(2,1)S(1)} collective-permute-done((bf16[96,1024]{1,0:T(8,128)(2,1)S(1)}, bf16[96,1024]{1,0:T(8,128)(2,1)S(1)}, u32[]{:S(2)}, u32[]{:S(2)}) %collective-permute-start.3) | collective-permute-done | bytes 196640 | tf_op jit(solution)/shard_map/ppermute | solution.py:202
  14.3 0.9 %expert.1 = (f32[96,1024]{1,0:T(8,128)S(1)}, bf16[96,1024]{1,0:T(8,128)(2,1)S(1)}) custom-call(bf16[96,1024]{1,0:T(8,128)(2,1)S(1)} %constant_dynamic-update-slice_fusion.mine_ref, bf16[96,1024]{1,0:T(8,128)(2,1)S(1)} %collective-permute-done.3.other_ref, bf16[192,2048]{1,0:T(8,128)(2,1)S(1)} %copy-done, bf16[192,2048]{1,0:T(8,128)(2,1)S(1)} %copy-done.1, ...), custom_call_target="tpu_custom_call" | custom-call | bytes 10000 | tf_op jit(solution)/shard_map/expert/pallas_call | solution.py:262
  15.3 0.0 copy-start.4
  15.3 0.2 collective-permute-start.4
  15.5 1.3 %collective-permute-done.4 = bf16[96,1024]{1,0:T(8,128)(2,1)S(1)} collective-permute-done((bf16[96,1024]{1,0:T(8,128)(2,1)S(1)}, bf16[96,1024]{1,0:T(8,128)(2,1)S(1)}, u32[]{:S(2)}, u32[]{:S(2)}) %collective-permute-start.4) | collective-permute-done | bytes 196640 | tf_op jit(solution)/shard_map/ppermute | solution.py:202
  16.8 0.7 %collective-permute-start.6 = (bf16[3,48,2048]{2,1,0:T(8,128)(2,1)S(1)}, bf16[3,48,2048]{2,1,0:T(8,128)(2,1)S(1)}, u32[]{:S(2)}, u32[]{:S(2)}) collective-permute-start(bf16[3,48,2048]{2,1,0:T(8,128)(2,1)S(1)} %collective-permute-done.5.shared_ref), channel_id=1, source_target_pairs={{4,5},{20,21},{5,4},{21,20},{6,7},{22,23},{7,6},{23,22}} | collective-permute-start | bytes 1769480 | tf_op jit(solution)/shard_map/ppermute | solution.py:214
  17.5 0.1 add_convert_fusion
  17.6 1.1 %collective-permute-start.9 = (bf16[24,1024]{1,0:T(8,128)(2,1)S(1)}, bf16[24,1024]{1,0:T(8,128)(2,1)S(1)}, u32[]{:S(2)}, u32[]{:S(2)}) collective-permute-start(bf16[24,1024]{1,0:T(8,128)(2,1)S(1)} %get-tuple-element.52), channel_id=1, source_target_pairs={{0,24},{4,28},{8,16},{12,20},{16,8},{20,12},{24,0},{28,4},{1,25},{... | collective-permute-start | bytes 147464 | tf_op jit(solution)/shard_map/ppermute | solution.py:202
  18.7 1.7 %collective-permute-start.8 = (bf16[24,1024]{1,0:T(8,128)(2,1)S(1)}, bf16[24,1024]{1,0:T(8,128)(2,1)S(1)}, u32[]{:S(2)}, u32[]{:S(2)}) collective-permute-start(bf16[24,1024]{1,0:T(8,128)(2,1)S(1)} %get-tuple-element.53), channel_id=1, source_target_pairs={{0,16},{4,20},{8,24},{12,28},{16,0},{20,4},{24,8},{28,12},{1,17},{... | collective-permute-start | bytes 147464 | tf_op jit(solution)/shard_map/ppermute | solution.py:202
  20.4 0.7 %collective-permute-start.7 = (bf16[24,1024]{1,0:T(8,128)(2,1)S(1)}, bf16[24,1024]{1,0:T(8,128)(2,1)S(1)}, u32[]{:S(2)}, u32[]{:S(2)}) collective-permute-start(bf16[24,1024]{1,0:T(8,128)(2,1)S(1)} %get-tuple-element.54), channel_id=1, source_target_pairs={{0,8},{4,12},{8,0},{12,4},{16,24},{20,28},{24,16},{28,20},{1,9},{5... | collective-permute-start | bytes 147464 | tf_op jit(solution)/shard_map/ppermute | solution.py:202
  21.1 0.7 %collective-permute-start.11 = (bf16[3,96,2048]{2,1,0:T(8,128)(2,1)S(1)}, bf16[3,96,2048]{2,1,0:T(8,128)(2,1)S(1)}, u32[]{:S(2)}, u32[]{:S(2)}) collective-permute-start(bf16[3,96,2048]{2,1,0:T(8,128)(2,1)S(1)} %get-tuple-element.50), channel_id=1, source_target_pairs={{12,8},{28,24},{13,9},{29,25},{14,10},{30,26},{15,11},{31,27}} | collective-permute-start | bytes 3538952 | tf_op jit(solution)/shard_map/ppermute | solution.py:206
  21.9 0.2 weigh.1.scaled_ref
  22.0 0.1 early.1.early_ref
  22.1 1.1 %collective-permute-done.9.refs_3_ = bf16[24,1024]{1,0:T(8,128)(2,1)S(1)} collective-permute-done((bf16[24,1024]{1,0:T(8,128)(2,1)S(1)}, bf16[24,1024]{1,0:T(8,128)(2,1)S(1)}, u32[]{:S(2)}, u32[]{:S(2)}) %collective-permute-start.9) | collective-permute-done | bytes 49184 | tf_op jit(solution)/shard_map/ppermute | solution.py:202
  23.2 0.3 collective-permute-done.8.refs_2_
  23.5 1.6 %collective-permute-done.7.refs_1_ = bf16[24,1024]{1,0:T(8,128)(2,1)S(1)} collective-permute-done((bf16[24,1024]{1,0:T(8,128)(2,1)S(1)}, bf16[24,1024]{1,0:T(8,128)(2,1)S(1)}, u32[]{:S(2)}, u32[]{:S(2)}) %collective-permute-start.7) | collective-permute-done | bytes 49184 | tf_op jit(solution)/shard_map/ppermute | solution.py:202
  25.1 5.5 %collective-permute-done.10.straight_ref = bf16[3,96,2048]{2,1,0:T(8,128)(2,1)S(1)} collective-permute-done((bf16[3,96,2048]{2,1,0:T(8,128)(2,1)S(1)}, bf16[3,96,2048]{2,1,0:T(8,128)(2,1)S(1)}, u32[]{:S(2)}, u32[]{:S(2)}) %collective-permute-start.10) | collective-permute-done | bytes 1179680 | tf_op jit(solution)/shard_map/ppermute | solution.py:206
  30.6 1.2 %combine.1 = bf16[128,2048]{1,0:T(8,128)(2,1)} custom-call(bf16[2,2,128,128]{3,2,1,0:T(8,128)(2,1)S(1)} %weigh.1.scaled_ref, bf16[24,1024]{1,0:T(8,128)(2,1)S(1)} %get-tuple-element.44.refs_0_, bf16[24,1024]{1,0:T(8,128)(2,1)S(1)} %collective-permute-done.7.refs_1_, bf16[24,1024]{1,0:T(8,128)(2,1)S(1)} %collective-permute-done.8.refs_2_, ...), custom_call_target="tpu_custom_call" | custom-call | flops 12300000256 | bytes 10000 | tf_op jit(solution)/shard_map/combine/pallas_call | solution.py:303
  31.8 1.0 %late.1 = bf16[3,96,2048]{2,1,0:T(8,128)(2,1)} custom-call(bf16[3,96,2048]{2,1,0:T(8,128)(2,1)} %early.1.early_ref, bf16[3,96,2048]{2,1,0:T(8,128)(2,1)S(1)} %collective-permute-done.10.straight_ref, bf16[3,96,2048]{2,1,0:T(8,128)(2,1)S(1)} %collective-permute-done.11.near_ref, f32[8,128]{1,0:T(8,128)S(1)} %copy-done.5), custom_call_target="tpu_custom_call", output_to_operand_aliasing={{}: (0, {})} | custom-call | tf_op jit(solution)/shard_map/late/pallas_call | solution.py:314
  (22 shorter events, 0.1 us)
Async XLA Ops:
  0.6 0.7 %copy-start.3 = (s32[128,8]{0,1:T(8,128)S(1)}, s32[128,8]{0,1:T(8,128)}, u32[]{:S(2)}) copy-start(s32[128,8]{0,1:T(8,128)} %param.8) | copy-start | bytes 12292
  0.6 1.1 %copy-start.6 = (bf16[128,2048]{1,0:T(8,128)(2,1)S(1)}, bf16[128,2048]{1,0:T(8,128)(2,1)}, u32[]{:S(2)}) copy-start(bf16[128,2048]{1,0:T(8,128)(2,1)} %tok_ref.1) | copy-start | bytes 1572868
  1.7 4.9 %copy-start = (bf16[192,2048]{1,0:T(8,128)(2,1)S(1)}, bf16[192,2048]{1,0:T(8,128)(2,1)}, u32[]{:S(2)}) copy-start(bf16[192,2048]{1,0:T(8,128)(2,1)} %gate_ref.2) | copy-start | bytes 2359300
  1.7 4.9 %copy-start.1 = (bf16[192,2048]{1,0:T(8,128)(2,1)S(1)}, bf16[192,2048]{1,0:T(8,128)(2,1)}, u32[]{:S(2)}) copy-start(bf16[192,2048]{1,0:T(8,128)(2,1)} %up_ref.2) | copy-start | bytes 2359300
  1.7 4.9 %copy-start.2 = (bf16[192,2048]{1,0:T(8,128)(2,1)S(1)}, bf16[192,2048]{1,0:T(8,128)(2,1)}, u32[]{:S(2)}) copy-start(bf16[192,2048]{1,0:T(8,128)(2,1)} %down_ref.2) | copy-start | bytes 2359300
  1.7 4.9 %copy-start.7 = (s32[2,3,96]{2,0,1:T(2,128)S(1)}, s32[2,3,96]{2,0,1:T(2,128)}, u32[]{:S(2)}) copy-start(s32[2,3,96]{2,0,1:T(2,128)} %param.13) | copy-start | bytes 6916
  2.1 10.7 %collective-permute-start.2 = (bf16[24,1024]{1,0:T(8,128)(2,1)S(1)}, bf16[24,1024]{1,0:T(8,128)(2,1)S(1)}, u32[]{:S(2)}, u32[]{:S(2)}) collective-permute-start(bf16[24,1024]{1,0:T(8,128)(2,1)S(1)} %get-tuple-element.36), channel_id=1, source_target_pairs={{0,24},{4,28},{8,16},{12,20},{16,8},{20,12},{24,0},{28,4},{1,25},{... | collective-permute-start | bytes 147464 | tf_op jit(solution)/shard_map/ppermute | solution.py:202
  6.1 4.1 %collective-permute-start = (bf16[24,1024]{1,0:T(8,128)(2,1)S(1)}, bf16[24,1024]{1,0:T(8,128)(2,1)S(1)}, u32[]{:S(2)}, u32[]{:S(2)}) collective-permute-start(bf16[24,1024]{1,0:T(8,128)(2,1)S(1)} %get-tuple-element.28), channel_id=1, source_target_pairs={{0,8},{4,12},{8,0},{12,4},{16,24},{20,28},{24,16},{28,20},{1,9},{5... | collective-permute-start | bytes 147464 | tf_op jit(solution)/shard_map/ppermute | solution.py:202
  6.7 10.1 %collective-permute-start.5 = (bf16[3,48,2048]{2,1,0:T(8,128)(2,1)S(1)}, bf16[3,48,2048]{2,1,0:T(8,128)(2,1)S(1)}, u32[]{:S(2)}, u32[]{:S(2)}) collective-permute-start(bf16[3,48,2048]{2,1,0:T(8,128)(2,1)S(1)} %get-tuple-element.33), channel_id=1, source_target_pairs={{12,4},{28,20},{13,5},{29,21},{14,6},{30,22},{15,7},{31,23}} | collective-permute-start | bytes 1769480 | tf_op jit(solution)/shard_map/ppermute | solution.py:206
  7.4 23.2 %collective-permute-start.10 = (bf16[3,96,2048]{2,1,0:T(8,128)(2,1)S(1)}, bf16[3,96,2048]{2,1,0:T(8,128)(2,1)S(1)}, u32[]{:S(2)}, u32[]{:S(2)}) collective-permute-start(bf16[3,96,2048]{2,1,0:T(8,128)(2,1)S(1)} %get-tuple-element.34), channel_id=1, source_target_pairs={{12,0},{28,16},{13,1},{29,17},{14,2},{30,18},{15,3},{31,19}} | collective-permute-start | bytes 3538952 | tf_op jit(solution)/shard_map/ppermute | solution.py:206
  8.7 4.2 %collective-permute-start.1 = (bf16[24,1024]{1,0:T(8,128)(2,1)S(1)}, bf16[24,1024]{1,0:T(8,128)(2,1)S(1)}, u32[]{:S(2)}, u32[]{:S(2)}) collective-permute-start(bf16[24,1024]{1,0:T(8,128)(2,1)S(1)} %get-tuple-element.36), channel_id=1, source_target_pairs={{0,16},{4,20},{8,24},{12,28},{16,0},{20,4},{24,8},{28,12},{1,17},{... | collective-permute-start | bytes 147464 | tf_op jit(solution)/shard_map/ppermute | solution.py:202
  12.8 1.5 %collective-permute-start.3 = (bf16[96,1024]{1,0:T(8,128)(2,1)S(1)}, bf16[96,1024]{1,0:T(8,128)(2,1)S(1)}, u32[]{:S(2)}, u32[]{:S(2)}) collective-permute-start(bf16[96,1024]{1,0:T(8,128)(2,1)S(1)} %constant_dynamic-update-slice_fusion.mine_ref), channel_id=1, source_target_pairs={{0,4},{4,0},{8,12},{12,8},{16,20},{20,16},{24,28},{28,24},{1,5},{5... | collective-permute-start | bytes 589832 | tf_op jit(solution)/shard_map/ppermute | solution.py:202
  15.3 6.6 %copy-start.4 = (f32[128,8]{0,1:T(8,128)S(1)}, f32[128,8]{0,1:T(8,128)}, u32[]{:S(2)}) copy-start(f32[128,8]{0,1:T(8,128)} %param.9) | copy-start | bytes 12292
  15.3 1.5 %collective-permute-start.4 = (bf16[96,1024]{1,0:T(8,128)(2,1)S(1)}, bf16[96,1024]{1,0:T(8,128)(2,1)S(1)}, u32[]{:S(2)}, u32[]{:S(2)}) collective-permute-start(bf16[96,1024]{1,0:T(8,128)(2,1)S(1)} %get-tuple-element.37), channel_id=1, source_target_pairs={{0,4},{4,0},{8,12},{12,8},{16,20},{20,16},{24,28},{28,24},{1,5},{5... | collective-permute-start | bytes 589832 | tf_op jit(solution)/shard_map/ppermute | solution.py:202
  16.8 4.3 %collective-permute-start.6 = (bf16[3,48,2048]{2,1,0:T(8,128)(2,1)S(1)}, bf16[3,48,2048]{2,1,0:T(8,128)(2,1)S(1)}, u32[]{:S(2)}, u32[]{:S(2)}) collective-permute-start(bf16[3,48,2048]{2,1,0:T(8,128)(2,1)S(1)} %collective-permute-done.5.shared_ref), channel_id=1, source_target_pairs={{4,5},{20,21},{5,4},{21,20},{6,7},{22,23},{7,6},{23,22}} | collective-permute-start | bytes 1769480 | tf_op jit(solution)/shard_map/ppermute | solution.py:214
  17.6 5.6 %collective-permute-start.9 = (bf16[24,1024]{1,0:T(8,128)(2,1)S(1)}, bf16[24,1024]{1,0:T(8,128)(2,1)S(1)}, u32[]{:S(2)}, u32[]{:S(2)}) collective-permute-start(bf16[24,1024]{1,0:T(8,128)(2,1)S(1)} %get-tuple-element.52), channel_id=1, source_target_pairs={{0,24},{4,28},{8,16},{12,20},{16,8},{20,12},{24,0},{28,4},{1,25},{... | collective-permute-start | bytes 147464 | tf_op jit(solution)/shard_map/ppermute | solution.py:202
  18.7 4.8 %collective-permute-start.8 = (bf16[24,1024]{1,0:T(8,128)(2,1)S(1)}, bf16[24,1024]{1,0:T(8,128)(2,1)S(1)}, u32[]{:S(2)}, u32[]{:S(2)}) collective-permute-start(bf16[24,1024]{1,0:T(8,128)(2,1)S(1)} %get-tuple-element.53), channel_id=1, source_target_pairs={{0,16},{4,20},{8,24},{12,28},{16,0},{20,4},{24,8},{28,12},{1,17},{... | collective-permute-start | bytes 147464 | tf_op jit(solution)/shard_map/ppermute | solution.py:202
  20.4 4.7 %collective-permute-start.7 = (bf16[24,1024]{1,0:T(8,128)(2,1)S(1)}, bf16[24,1024]{1,0:T(8,128)(2,1)S(1)}, u32[]{:S(2)}, u32[]{:S(2)}) collective-permute-start(bf16[24,1024]{1,0:T(8,128)(2,1)S(1)} %get-tuple-element.54), channel_id=1, source_target_pairs={{0,8},{4,12},{8,0},{12,4},{16,24},{20,28},{24,16},{28,20},{1,9},{5... | collective-permute-start | bytes 147464 | tf_op jit(solution)/shard_map/ppermute | solution.py:202
  21.1 10.7 %collective-permute-start.11 = (bf16[3,96,2048]{2,1,0:T(8,128)(2,1)S(1)}, bf16[3,96,2048]{2,1,0:T(8,128)(2,1)S(1)}, u32[]{:S(2)}, u32[]{:S(2)}) collective-permute-start(bf16[3,96,2048]{2,1,0:T(8,128)(2,1)S(1)} %get-tuple-element.50), channel_id=1, source_target_pairs={{12,8},{28,24},{13,9},{29,25},{14,10},{30,26},{15,11},{31,27}} | collective-permute-start | bytes 3538952 | tf_op jit(solution)/shard_map/ppermute | solution.py:206
  30.6 1.3 %copy-start.5 = (f32[8,128]{1,0:T(8,128)S(1)}, f32[8,128]{1,0:T(8,128)}, u32[]{:S(2)}) copy-start(f32[8,128]{1,0:T(8,128)} %begin.1.begun_ref) | copy-start | bytes 12292

commit v20 on v19

--- a/solution.py
+++ b/solution.py
@@ -108,14 +108,8 @@
             place_rows([(shared_ref, half * even), (swapped_ref, half * (1 - even))], out_ref, sems)
 
 
-def late_kernel(early_ref, straight_ref, near_ref, begun_ref, out_ref, sems):
-    position = lax.axis_index("expert") % GROUP
-
-    @pl.when(jnp.logical_or(position == 0, position == 3))
-    def _():
-        place_rows([(straight_ref, 0)], out_ref, sems)
-
-    @pl.when(position == 2)
+def late_kernel(filled_ref, near_ref, begun_ref, out_ref, sems):
+    @pl.when(lax.axis_index("expert") % GROUP == 2)
     def _():
         place_rows([(near_ref, 0)], out_ref, sems)
 
@@ -166,19 +160,38 @@
 
 
 def combine_kernel(scaled_ref, *refs):
-    piece_refs, (out_ref, rows_ref) = refs[:-2], refs[-2:]
+    piece_refs, (straight_ref, early_ref, out_ref, arrived_ref) = refs[:-7], refs[-7:-3]
+    rows_ref, mixed_ref, sems = refs[-3:]
     half = out_ref.shape[1] // 2
     numbers = (((0,), (0,)), ((), ()))
+    direct = lax.axis_index("expert") % GROUP % 3 == 0
+    fill = pltpu.make_async_copy(straight_ref, arrived_ref, sems.at[2])
+
+    @pl.when(direct)
+    def _():
+        fill.start()
+
     for n, ref in enumerate(piece_refs):
         rows_ref[n * STRIDE : n * STRIDE + PACK, :] = ref[...]
         rows_ref[n * STRIDE + PACK : (n + 1) * STRIDE, :] = jnp.zeros((STRIDE - PACK, half), BF16)
     rows = rows_ref[...]
+    copies = []
     for side in range(2):
         mixed = lax.dot_general(scaled_ref[side, 0], rows, numbers, preferred_element_type=F32)
         mixed = mixed + lax.dot_general(
             scaled_ref[side, 1], rows, numbers, preferred_element_type=F32
         )
-        out_ref[:, side * half : (side + 1) * half] = mixed.astype(BF16)
+        columns = pl.ds(side * half, half)
+        mixed_ref[:, columns] = mixed.astype(BF16)
+        copy = pltpu.make_async_copy(mixed_ref.at[:, columns], out_ref.at[:, columns], sems.at[side])
+        copy.start()
+        copies.append(copy)
+    for copy in copies:
+        copy.wait()
+
+    @pl.when(direct)
+    def _():
+        fill.wait()
 
 
 def on_device(tokens, expert_ids, combine, old_gate, old_up, old_down, move_plan):
@@ -300,27 +313,32 @@
     )(shared, swapped)
     back, early, straight = lax.optimization_barrier((back, early, straight))
 
-    mixed = pl.pallas_call(
+    mixed, filled = pl.pallas_call(
         combine_kernel,
-        out_shape=shape(tokens.shape[0], width),
-        in_specs=[VMEM] + [VMEM] * len(back),
-        out_specs=VMEM,
-        scratch_shapes=[pltpu.VMEM((len(back) * STRIDE, width // 2), BF16)],
+        out_shape=[shape(tokens.shape[0], width), shape(3, most, width)],
+        in_specs=[VMEM] * (len(back) + 1) + [HBM] * 2,
+        out_specs=[HBM] * 2,
+        input_output_aliases={len(back) + 2: 1},
+        scratch_shapes=[
+            pltpu.VMEM((len(back) * STRIDE, width // 2), BF16),
+            pltpu.VMEM((tokens.shape[0], width), BF16),
+            pltpu.SemaphoreType.DMA((3,)),
+        ],
         compiler_params=params(),
         cost_estimate=cost(12.3),
         name="combine",
-    )(scaled, *back)
+    )(scaled, *back, straight, early)
 
     arrived = pl.pallas_call(
         late_kernel,
         out_shape=shape(3, most, width),
-        in_specs=[HBM] * 4,
+        in_specs=[HBM] * 3,
         out_specs=HBM,
         input_output_aliases={0: 0},
         scratch_shapes=[pltpu.SemaphoreType.DMA((3,))],
         compiler_params=params(),
         name="late",
-    )(early, straight, near, begun)
+    )(filled, near, begun)
     return mixed, arrived
 
 

time: 33.1 us -> 32.5 us (0.982)
  Pallas kernels: 4.47 us -> 3.64 us
    pallas_call x1, Pallas kernels: 1.03 us -> 0.05 us  [on_device(): pl.pallas_call(late_kernel, out_shape=shape(3, most, width), in_specs=[HB...]
  transfers between devices with their start and end apart: 12 -> 12, of which waited for: 8 -> 8; matrix products, arithmetic and copies ran while one was open for 0% -> 0% of each run, Pallas kernels for 7% -> 8%
where the time goes in v20:
time: 32.5 us; the launch traced here: 32 us
  waiting for transfers between devices  15.1 us (46%)
  starting transfers between devices  11.9 us (37%)
  Pallas kernels  3.64 us (11%)
  between operations  0.8 us (2%)
  local copies, waits for them, and re-layouts  0.52 us (2%)
    ppermute x8, waiting for transfers between devices, send(): return lax.ppermute(block, 'expert', route)  9.66 us
    ppermute x8, starting transfers between devices, send(): return lax.ppermute(block, 'expert', route)  8.5 us
    ppermute x3, waiting for transfers between devices, migrate(): return lax.ppermute(block, 'expert', route)  5.48 us
    ppermute x3, starting transfers between devices, migrate(): return lax.ppermute(block, 'expert', route)  2.72 us
    pallas_call x1, Pallas kernels, on_device(): pl.pallas_call(combine_kernel, out_shape=[shape(tokens.shape[0], width),...  1.39 us
    pallas_call x1, Pallas kernels, on_device(): pl.pallas_call(expert_kernel, grid=(total // step,), out_shape=[shape(tot...  0.92 us
    ppermute x1, starting transfers between devices, swap(): return lax.ppermute(block, ('expert', 'replica'), route)  0.69 us
  transfers between devices with their start and end apart: 12, of which 8 were waited for; matrix products, arithmetic and copies ran while one was open for 0% of the time, Pallas kernels for 8%

profile of v20, /device:TPU:0, one launch (start us, length us, event | category | flops | bytes accessed | tf_op | source)
XLA Modules:
  0.0 32.0 jit_solution(4243134698657267118)
XLA Ops:
  0.6 0.6 %begin.1.begun_ref = f32[8,128]{1,0:T(8,128)} custom-call(), custom_call_target="tpu_custom_call" | custom-call | flops 5000000000 | bytes 10000 | tf_op jit(solution)/shard_map/begin/pallas_call | solution.py:240
  1.2 0.1 copy-done.3
  1.3 0.4 %copy-done.6 = bf16[128,2048]{1,0:T(8,128)(2,1)S(1)} copy-done((bf16[128,2048]{1,0:T(8,128)(2,1)S(1)}, bf16[128,2048]{1,0:T(8,128)(2,1)}, u32[]{:S(2)}) %copy-start.6) | copy-done | bytes 524312
  1.7 0.4 %dispatch.1 = (bf16[24,1024]{1,0:T(8,128)(2,1)S(1)}, bf16[24,1024]{1,0:T(8,128)(2,1)S(1)}) custom-call(s32[8,128]{1,0:T(8,128)S(1)} %bitcast.3, bf16[128,2048]{1,0:T(8,128)(2,1)S(1)} %copy-done.6), custom_call_target="tpu_custom_call" | custom-call | flops 2000000000 | bytes 10000 | tf_op jit(solution)/shard_map/dispatch/pallas_call | solution.py:248
  2.1 4.0 %collective-permute-start.2 = (bf16[24,1024]{1,0:T(8,128)(2,1)S(1)}, bf16[24,1024]{1,0:T(8,128)(2,1)S(1)}, u32[]{:S(2)}, u32[]{:S(2)}) collective-permute-start(bf16[24,1024]{1,0:T(8,128)(2,1)S(1)} %get-tuple-element.38), channel_id=1, source_target_pairs={{0,24},{4,28},{8,16},{12,20},{16,8},{20,12},{24,0},{28,4},{1,25},{... | collective-permute-start | bytes 147464 | tf_op jit(solution)/shard_map/ppermute | solution.py:215
  6.1 0.5 %collective-permute-start = (bf16[24,1024]{1,0:T(8,128)(2,1)S(1)}, bf16[24,1024]{1,0:T(8,128)(2,1)S(1)}, u32[]{:S(2)}, u32[]{:S(2)}) collective-permute-start(bf16[24,1024]{1,0:T(8,128)(2,1)S(1)} %get-tuple-element.30), channel_id=1, source_target_pairs={{0,8},{4,12},{8,0},{12,4},{16,24},{20,28},{24,16},{28,20},{1,9},{5... | collective-permute-start | bytes 147464 | tf_op jit(solution)/shard_map/ppermute | solution.py:215
  6.7 0.7 %collective-permute-start.5 = (bf16[3,48,2048]{2,1,0:T(8,128)(2,1)S(1)}, bf16[3,48,2048]{2,1,0:T(8,128)(2,1)S(1)}, u32[]{:S(2)}, u32[]{:S(2)}) collective-permute-start(bf16[3,48,2048]{2,1,0:T(8,128)(2,1)S(1)} %get-tuple-element.35), channel_id=1, source_target_pairs={{12,4},{28,20},{13,5},{29,21},{14,6},{30,22},{15,7},{31,23}} | collective-permute-start | bytes 1769480 | tf_op jit(solution)/shard_map/ppermute | solution.py:219
  7.4 1.3 %collective-permute-start.10 = (bf16[3,96,2048]{2,1,0:T(8,128)(2,1)S(1)}, bf16[3,96,2048]{2,1,0:T(8,128)(2,1)S(1)}, u32[]{:S(2)}, u32[]{:S(2)}) collective-permute-start(bf16[3,96,2048]{2,1,0:T(8,128)(2,1)S(1)} %get-tuple-element.36), channel_id=1, source_target_pairs={{12,0},{28,16},{13,1},{29,17},{14,2},{30,18},{15,3},{31,19}} | collective-permute-start | bytes 3538952 | tf_op jit(solution)/shard_map/ppermute | solution.py:219
  8.7 0.2 collective-permute-start.1
  8.8 1.3 %collective-permute-done = bf16[24,1024]{1,0:T(8,128)(2,1)S(1)} collective-permute-done((bf16[24,1024]{1,0:T(8,128)(2,1)S(1)}, bf16[24,1024]{1,0:T(8,128)(2,1)S(1)}, u32[]{:S(2)}, u32[]{:S(2)}) %collective-permute-start) | collective-permute-done | bytes 49184 | tf_op jit(solution)/shard_map/ppermute | solution.py:215
  10.2 2.6 %collective-permute-done.1 = bf16[24,1024]{1,0:T(8,128)(2,1)S(1)} collective-permute-done((bf16[24,1024]{1,0:T(8,128)(2,1)S(1)}, bf16[24,1024]{1,0:T(8,128)(2,1)S(1)}, u32[]{:S(2)}, u32[]{:S(2)}) %collective-permute-start.1) | collective-permute-done | bytes 49184 | tf_op jit(solution)/shard_map/ppermute | solution.py:215
  12.8 0.0 collective-permute-done.2
  12.8 0.1 collective-permute-start.3
  12.9 1.4 %collective-permute-done.3.other_ref = bf16[96,1024]{1,0:T(8,128)(2,1)S(1)} collective-permute-done((bf16[96,1024]{1,0:T(8,128)(2,1)S(1)}, bf16[96,1024]{1,0:T(8,128)(2,1)S(1)}, u32[]{:S(2)}, u32[]{:S(2)}) %collective-permute-start.3) | collective-permute-done | bytes 196640 | tf_op jit(solution)/shard_map/ppermute | solution.py:215
  14.3 0.9 %expert.1 = (f32[96,1024]{1,0:T(8,128)S(1)}, bf16[96,1024]{1,0:T(8,128)(2,1)S(1)}) custom-call(bf16[96,1024]{1,0:T(8,128)(2,1)S(1)} %constant_dynamic-update-slice_fusion.mine_ref, bf16[96,1024]{1,0:T(8,128)(2,1)S(1)} %collective-permute-done.3.other_ref, bf16[192,2048]{1,0:T(8,128)(2,1)S(1)} %copy-done, bf16[192,2048]{1,0:T(8,128)(2,1)S(1)} %copy-done.1, ...), custom_call_target="tpu_custom_call" | custom-call | bytes 10000 | tf_op jit(solution)/shard_map/expert/pallas_call | solution.py:275
  15.3 0.0 copy-start.4
  15.3 0.2 collective-permute-start.4
  15.5 1.3 %collective-permute-done.4 = bf16[96,1024]{1,0:T(8,128)(2,1)S(1)} collective-permute-done((bf16[96,1024]{1,0:T(8,128)(2,1)S(1)}, bf16[96,1024]{1,0:T(8,128)(2,1)S(1)}, u32[]{:S(2)}, u32[]{:S(2)}) %collective-permute-start.4) | collective-permute-done | bytes 196640 | tf_op jit(solution)/shard_map/ppermute | solution.py:215
  16.8 0.7 %collective-permute-start.6 = (bf16[3,48,2048]{2,1,0:T(8,128)(2,1)S(1)}, bf16[3,48,2048]{2,1,0:T(8,128)(2,1)S(1)}, u32[]{:S(2)}, u32[]{:S(2)}) collective-permute-start(bf16[3,48,2048]{2,1,0:T(8,128)(2,1)S(1)} %collective-permute-done.5.shared_ref), channel_id=1, source_target_pairs={{4,5},{20,21},{5,4},{21,20},{6,7},{22,23},{7,6},{23,22}} | collective-permute-start | bytes 1769480 | tf_op jit(solution)/shard_map/ppermute | solution.py:227
  17.6 1.1 %collective-permute-start.9 = (bf16[24,1024]{1,0:T(8,128)(2,1)S(1)}, bf16[24,1024]{1,0:T(8,128)(2,1)S(1)}, u32[]{:S(2)}, u32[]{:S(2)}) collective-permute-start(bf16[24,1024]{1,0:T(8,128)(2,1)S(1)} %get-tuple-element.56), channel_id=1, source_target_pairs={{0,24},{4,28},{8,16},{12,20},{16,8},{20,12},{24,0},{28,4},{1,25},{... | collective-permute-start | bytes 147464 | tf_op jit(solution)/shard_map/ppermute | solution.py:215
  18.7 1.7 %collective-permute-start.8 = (bf16[24,1024]{1,0:T(8,128)(2,1)S(1)}, bf16[24,1024]{1,0:T(8,128)(2,1)S(1)}, u32[]{:S(2)}, u32[]{:S(2)}) collective-permute-start(bf16[24,1024]{1,0:T(8,128)(2,1)S(1)} %get-tuple-element.57), channel_id=1, source_target_pairs={{0,16},{4,20},{8,24},{12,28},{16,0},{20,4},{24,8},{28,12},{1,17},{... | collective-permute-start | bytes 147464 | tf_op jit(solution)/shard_map/ppermute | solution.py:215
  20.4 0.7 %collective-permute-start.7 = (bf16[24,1024]{1,0:T(8,128)(2,1)S(1)}, bf16[24,1024]{1,0:T(8,128)(2,1)S(1)}, u32[]{:S(2)}, u32[]{:S(2)}) collective-permute-start(bf16[24,1024]{1,0:T(8,128)(2,1)S(1)} %get-tuple-element.58), channel_id=1, source_target_pairs={{0,8},{4,12},{8,0},{12,4},{16,24},{20,28},{24,16},{28,20},{1,9},{5... | collective-permute-start | bytes 147464 | tf_op jit(solution)/shard_map/ppermute | solution.py:215
  21.1 0.0 collective-permute-done.6.swapped_ref
  21.1 0.7 %collective-permute-start.11 = (bf16[3,96,2048]{2,1,0:T(8,128)(2,1)S(1)}, bf16[3,96,2048]{2,1,0:T(8,128)(2,1)S(1)}, u32[]{:S(2)}, u32[]{:S(2)}) collective-permute-start(bf16[3,96,2048]{2,1,0:T(8,128)(2,1)S(1)} %get-tuple-element.54), channel_id=1, source_target_pairs={{12,8},{28,24},{13,9},{29,25},{14,10},{30,26},{15,11},{31,27}} | collective-permute-start | bytes 3538952 | tf_op jit(solution)/shard_map/ppermute | solution.py:219
  21.9 0.2 weigh.1.scaled_ref
  22.0 0.1 early.1.refs_5_
  22.1 1.1 %collective-permute-done.9.refs_3_ = bf16[24,1024]{1,0:T(8,128)(2,1)S(1)} collective-permute-done((bf16[24,1024]{1,0:T(8,128)(2,1)S(1)}, bf16[24,1024]{1,0:T(8,128)(2,1)S(1)}, u32[]{:S(2)}, u32[]{:S(2)}) %collective-permute-start.9) | collective-permute-done | bytes 49184 | tf_op jit(solution)/shard_map/ppermute | solution.py:215
  23.2 0.3 collective-permute-done.8.refs_2_
  23.5 1.6 %collective-permute-done.7.refs_1_ = bf16[24,1024]{1,0:T(8,128)(2,1)S(1)} collective-permute-done((bf16[24,1024]{1,0:T(8,128)(2,1)S(1)}, bf16[24,1024]{1,0:T(8,128)(2,1)S(1)}, u32[]{:S(2)}, u32[]{:S(2)}) %collective-permute-start.7) | collective-permute-done | bytes 49184 | tf_op jit(solution)/shard_map/ppermute | solution.py:215
  25.1 5.5 %collective-permute-done.10.refs_4_ = bf16[3,96,2048]{2,1,0:T(8,128)(2,1)S(1)} collective-permute-done((bf16[3,96,2048]{2,1,0:T(8,128)(2,1)S(1)}, bf16[3,96,2048]{2,1,0:T(8,128)(2,1)S(1)}, u32[]{:S(2)}, u32[]{:S(2)}) %collective-permute-start.10) | collective-permute-done | bytes 1179680 | tf_op jit(solution)/shard_map/ppermute | solution.py:219
  30.6 1.4 %combine.1 = (bf16[128,2048]{1,0:T(8,128)(2,1)}, bf16[3,96,2048]{2,1,0:T(8,128)(2,1)}) custom-call(bf16[2,2,128,128]{3,2,1,0:T(8,128)(2,1)S(1)} %weigh.1.scaled_ref, bf16[24,1024]{1,0:T(8,128)(2,1)S(1)} %get-tuple-element.46.refs_0_, bf16[24,1024]{1,0:T(8,128)(2,1)S(1)} %collective-permute-done.7.refs_1_, ...), custom_call_target="tpu_custom_call", output_to_operand_aliasing={{1}: (6, {})} | custom-call | flops 12300000256 | bytes 10000 | tf_op jit(solution)/shard_map/combine/pallas_call | solution.py:316
  32.0 0.1 late.1
  (22 shorter events, 0.1 us)
Async XLA Ops:
  0.6 0.7 %copy-start.3 = (s32[128,8]{0,1:T(8,128)S(1)}, s32[128,8]{0,1:T(8,128)}, u32[]{:S(2)}) copy-start(s32[128,8]{0,1:T(8,128)} %param.8) | copy-start | bytes 12292
  0.6 1.1 %copy-start.6 = (bf16[128,2048]{1,0:T(8,128)(2,1)S(1)}, bf16[128,2048]{1,0:T(8,128)(2,1)}, u32[]{:S(2)}) copy-start(bf16[128,2048]{1,0:T(8,128)(2,1)} %tok_ref.1) | copy-start | bytes 1572868
  1.7 4.9 %copy-start = (bf16[192,2048]{1,0:T(8,128)(2,1)S(1)}, bf16[192,2048]{1,0:T(8,128)(2,1)}, u32[]{:S(2)}) copy-start(bf16[192,2048]{1,0:T(8,128)(2,1)} %gate_ref.2) | copy-start | bytes 2359300
  1.7 4.9 %copy-start.1 = (bf16[192,2048]{1,0:T(8,128)(2,1)S(1)}, bf16[192,2048]{1,0:T(8,128)(2,1)}, u32[]{:S(2)}) copy-start(bf16[192,2048]{1,0:T(8,128)(2,1)} %up_ref.2) | copy-start | bytes 2359300
  1.7 4.9 %copy-start.2 = (bf16[192,2048]{1,0:T(8,128)(2,1)S(1)}, bf16[192,2048]{1,0:T(8,128)(2,1)}, u32[]{:S(2)}) copy-start(bf16[192,2048]{1,0:T(8,128)(2,1)} %down_ref.2) | copy-start | bytes 2359300
  1.7 4.9 %copy-start.7 = (s32[2,3,96]{2,0,1:T(2,128)S(1)}, s32[2,3,96]{2,0,1:T(2,128)}, u32[]{:S(2)}) copy-start(s32[2,3,96]{2,0,1:T(2,128)} %param.13) | copy-start | bytes 6916
  2.1 10.7 %collective-permute-start.2 = (bf16[24,1024]{1,0:T(8,128)(2,1)S(1)}, bf16[24,1024]{1,0:T(8,128)(2,1)S(1)}, u32[]{:S(2)}, u32[]{:S(2)}) collective-permute-start(bf16[24,1024]{1,0:T(8,128)(2,1)S(1)} %get-tuple-element.38), channel_id=1, source_target_pairs={{0,24},{4,28},{8,16},{12,20},{16,8},{20,12},{24,0},{28,4},{1,25},{... | collective-permute-start | bytes 147464 | tf_op jit(solution)/shard_map/ppermute | solution.py:215
  6.1 4.1 %collective-permute-start = (bf16[24,1024]{1,0:T(8,128)(2,1)S(1)}, bf16[24,1024]{1,0:T(8,128)(2,1)S(1)}, u32[]{:S(2)}, u32[]{:S(2)}) collective-permute-start(bf16[24,1024]{1,0:T(8,128)(2,1)S(1)} %get-tuple-element.30), channel_id=1, source_target_pairs={{0,8},{4,12},{8,0},{12,4},{16,24},{20,28},{24,16},{28,20},{1,9},{5... | collective-permute-start | bytes 147464 | tf_op jit(solution)/shard_map/ppermute | solution.py:215
  6.7 10.1 %collective-permute-start.5 = (bf16[3,48,2048]{2,1,0:T(8,128)(2,1)S(1)}, bf16[3,48,2048]{2,1,0:T(8,128)(2,1)S(1)}, u32[]{:S(2)}, u32[]{:S(2)}) collective-permute-start(bf16[3,48,2048]{2,1,0:T(8,128)(2,1)S(1)} %get-tuple-element.35), channel_id=1, source_target_pairs={{12,4},{28,20},{13,5},{29,21},{14,6},{30,22},{15,7},{31,23}} | collective-permute-start | bytes 1769480 | tf_op jit(solution)/shard_map/ppermute | solution.py:219
  7.4 23.2 %collective-permute-start.10 = (bf16[3,96,2048]{2,1,0:T(8,128)(2,1)S(1)}, bf16[3,96,2048]{2,1,0:T(8,128)(2,1)S(1)}, u32[]{:S(2)}, u32[]{:S(2)}) collective-permute-start(bf16[3,96,2048]{2,1,0:T(8,128)(2,1)S(1)} %get-tuple-element.36), channel_id=1, source_target_pairs={{12,0},{28,16},{13,1},{29,17},{14,2},{30,18},{15,3},{31,19}} | collective-permute-start | bytes 3538952 | tf_op jit(solution)/shard_map/ppermute | solution.py:219
  8.7 4.2 %collective-permute-start.1 = (bf16[24,1024]{1,0:T(8,128)(2,1)S(1)}, bf16[24,1024]{1,0:T(8,128)(2,1)S(1)}, u32[]{:S(2)}, u32[]{:S(2)}) collective-permute-start(bf16[24,1024]{1,0:T(8,128)(2,1)S(1)} %get-tuple-element.38), channel_id=1, source_target_pairs={{0,16},{4,20},{8,24},{12,28},{16,0},{20,4},{24,8},{28,12},{1,17},{... | collective-permute-start | bytes 147464 | tf_op jit(solution)/shard_map/ppermute | solution.py:215
  12.8 1.5 %collective-permute-start.3 = (bf16[96,1024]{1,0:T(8,128)(2,1)S(1)}, bf16[96,1024]{1,0:T(8,128)(2,1)S(1)}, u32[]{:S(2)}, u32[]{:S(2)}) collective-permute-start(bf16[96,1024]{1,0:T(8,128)(2,1)S(1)} %constant_dynamic-update-slice_fusion.mine_ref), channel_id=1, source_target_pairs={{0,4},{4,0},{8,12},{12,8},{16,20},{20,16},{24,28},{28,24},{1,5},{5... | collective-permute-start | bytes 589832 | tf_op jit(solution)/shard_map/ppermute | solution.py:215
  15.3 6.6 %copy-start.4 = (f32[128,8]{0,1:T(8,128)S(1)}, f32[128,8]{0,1:T(8,128)}, u32[]{:S(2)}) copy-start(f32[128,8]{0,1:T(8,128)} %param.9) | copy-start | bytes 12292
  15.3 1.5 %collective-permute-start.4 = (bf16[96,1024]{1,0:T(8,128)(2,1)S(1)}, bf16[96,1024]{1,0:T(8,128)(2,1)S(1)}, u32[]{:S(2)}, u32[]{:S(2)}) collective-permute-start(bf16[96,1024]{1,0:T(8,128)(2,1)S(1)} %get-tuple-element.39), channel_id=1, source_target_pairs={{0,4},{4,0},{8,12},{12,8},{16,20},{20,16},{24,28},{28,24},{1,5},{5... | collective-permute-start | bytes 589832 | tf_op jit(solution)/shard_map/ppermute | solution.py:215
  16.8 4.3 %collective-permute-start.6 = (bf16[3,48,2048]{2,1,0:T(8,128)(2,1)S(1)}, bf16[3,48,2048]{2,1,0:T(8,128)(2,1)S(1)}, u32[]{:S(2)}, u32[]{:S(2)}) collective-permute-start(bf16[3,48,2048]{2,1,0:T(8,128)(2,1)S(1)} %collective-permute-done.5.shared_ref), channel_id=1, source_target_pairs={{4,5},{20,21},{5,4},{21,20},{6,7},{22,23},{7,6},{23,22}} | collective-permute-start | bytes 1769480 | tf_op jit(solution)/shard_map/ppermute | solution.py:227
  17.6 5.6 %collective-permute-start.9 = (bf16[24,1024]{1,0:T(8,128)(2,1)S(1)}, bf16[24,1024]{1,0:T(8,128)(2,1)S(1)}, u32[]{:S(2)}, u32[]{:S(2)}) collective-permute-start(bf16[24,1024]{1,0:T(8,128)(2,1)S(1)} %get-tuple-element.56), channel_id=1, source_target_pairs={{0,24},{4,28},{8,16},{12,20},{16,8},{20,12},{24,0},{28,4},{1,25},{... | collective-permute-start | bytes 147464 | tf_op jit(solution)/shard_map/ppermute | solution.py:215
  18.7 4.8 %collective-permute-start.8 = (bf16[24,1024]{1,0:T(8,128)(2,1)S(1)}, bf16[24,1024]{1,0:T(8,128)(2,1)S(1)}, u32[]{:S(2)}, u32[]{:S(2)}) collective-permute-start(bf16[24,1024]{1,0:T(8,128)(2,1)S(1)} %get-tuple-element.57), channel_id=1, source_target_pairs={{0,16},{4,20},{8,24},{12,28},{16,0},{20,4},{24,8},{28,12},{1,17},{... | collective-permute-start | bytes 147464 | tf_op jit(solution)/shard_map/ppermute | solution.py:215
  20.4 4.7 %collective-permute-start.7 = (bf16[24,1024]{1,0:T(8,128)(2,1)S(1)}, bf16[24,1024]{1,0:T(8,128)(2,1)S(1)}, u32[]{:S(2)}, u32[]{:S(2)}) collective-permute-start(bf16[24,1024]{1,0:T(8,128)(2,1)S(1)} %get-tuple-element.58), channel_id=1, source_target_pairs={{0,8},{4,12},{8,0},{12,4},{16,24},{20,28},{24,16},{28,20},{1,9},{5... | collective-permute-start | bytes 147464 | tf_op jit(solution)/shard_map/ppermute | solution.py:215
  21.1 10.8 %collective-permute-start.11 = (bf16[3,96,2048]{2,1,0:T(8,128)(2,1)S(1)}, bf16[3,96,2048]{2,1,0:T(8,128)(2,1)S(1)}, u32[]{:S(2)}, u32[]{:S(2)}) collective-permute-start(bf16[3,96,2048]{2,1,0:T(8,128)(2,1)S(1)} %get-tuple-element.54), channel_id=1, source_target_pairs={{12,8},{28,24},{13,9},{29,25},{14,10},{30,26},{15,11},{31,27}} | collective-permute-start | bytes 3538952 | tf_op jit(solution)/shard_map/ppermute | solution.py:219
  30.6 1.4 %copy-start.5 = (f32[8,128]{1,0:T(8,128)S(1)}, f32[8,128]{1,0:T(8,128)}, u32[]{:S(2)}) copy-start(f32[8,128]{1,0:T(8,128)} %begin.1.begun_ref) | copy-start | bytes 12292

commit v21 on v20

--- a/solution.py
+++ b/solution.py
@@ -63,24 +63,24 @@
     @pl.when(device % GROUP == GROUP - 1)
     def _():
         plans = []
-        for survivor, count, first in wanted:
+        for survivor, count, first in sum(wanted, []):
             plan = plan_ref[survivor, pl.ds(device // GROUP, 1), :]
             if first is None:
                 plan = jnp.where(even, plan[:, :count], plan[:, count : 2 * count])
             else:
                 plan = plan[:, first : first + count]
             plans.append(plan)
-        total = sum(count for _, count, _ in wanted)
-        number = lax.broadcasted_iota(jnp.int32, (rows, total), 0)
-        pick = jnp.where(number == jnp.concatenate(plans, axis=1), 1.0, 0.0).astype(BF16)
+        plan = jnp.concatenate(plans, axis=1)
+        number = lax.broadcasted_iota(jnp.int32, (rows, plan.shape[1]), 0)
+        pick = jnp.where(number == plan, 1.0, 0.0).astype(BF16)
         for m, held_ref in enumerate((gate_ref, up_ref, down_ref)):
             found = lax.dot_general(
                 pick, held_ref[...], (((0,), (0,)), ((), ())), preferred_element_type=F32
             ).astype(BF16)
             start = 0
-            for (_, count, _), ref in zip(wanted, out_refs):
-                ref[m] = found[start : start + count]
-                start += count
+            for ref in out_refs:
+                ref[m] = found[start : start + ref.shape[1]]
+                start += ref.shape[1]
 
 
 def place_rows(pieces, out_ref, sems):
@@ -97,7 +97,7 @@
         copy.wait()
 
 
-def early_kernel(shared_ref, swapped_ref, out_ref, sems):
+def early_kernel(shared_ref, swapped_ref, beside_ref, relayed_ref, out_ref, sems):
     position = lax.axis_index("expert") % GROUP
     parity = lax.axis_index("replica") % 2
     half = shared_ref.shape[1]
@@ -107,11 +107,20 @@
         def _():
             place_rows([(shared_ref, half * even), (swapped_ref, half * (1 - even))], out_ref, sems)
 
+    @pl.when(position == 2)
+    def _():
+        rows = beside_ref.shape[1] - relayed_ref.shape[1]
+        place_rows([(beside_ref.at[:, pl.ds(0, rows)], 0)], out_ref, sems)
+
+    @pl.when(position % 3 == 0)
+    def _():
+        place_rows([(relayed_ref, out_ref.shape[1] - relayed_ref.shape[1])], out_ref, sems)
+
 
 def late_kernel(filled_ref, near_ref, begun_ref, out_ref, sems):
     @pl.when(lax.axis_index("expert") % GROUP == 2)
     def _():
-        place_rows([(near_ref, 0)], out_ref, sems)
+        place_rows([(near_ref, out_ref.shape[1] - near_ref.shape[1])], out_ref, sems)
 
 
 def begin_kernel(out_ref):
@@ -165,7 +174,8 @@
     half = out_ref.shape[1] // 2
     numbers = (((0,), (0,)), ((), ()))
     direct = lax.axis_index("expert") % GROUP % 3 == 0
-    fill = pltpu.make_async_copy(straight_ref, arrived_ref, sems.at[2])
+    rows_at = pl.ds(0, straight_ref.shape[1])
+    fill = pltpu.make_async_copy(straight_ref, arrived_ref.at[:, rows_at], sems.at[2])
 
     @pl.when(direct)
     def _():
@@ -203,6 +213,8 @@
     plan = jnp.transpose(move_plan, (1, 0, 2))
     weights = (old_gate, old_up, old_down)
     half = most // 2
+    lead = most // 6 * 5
+    ahead = half - (most - lead)
 
     def shape(*dims, dtype=BF16):
         return jax.ShapeDtypeStruct(dims, dtype)
@@ -214,8 +226,8 @@
             route.append((i, GROUP * ((g + j) % experts) + (p ^ k)))
         return lax.ppermute(block, "expert", route)
 
-    def migrate(block, survivor):
-        route = [(GROUP * e + GROUP - 1, GROUP * e + survivor) for e in range(experts)]
+    def migrate(block, survivor, source=GROUP - 1):
+        route = [(GROUP * e + source, GROUP * e + survivor) for e in range(experts)]
         return lax.ppermute(block, "expert", route)
 
     def swap(block, survivor):
@@ -229,7 +241,7 @@
     def select(wanted, held):
         return pl.pallas_call(
             functools.partial(select_kernel, wanted),
-            out_shape=[shape(3, count, width) for _, count, _ in wanted],
+            out_shape=[shape(3, sum(piece[1] for piece in part), width) for part in wanted],
             in_specs=[VMEM] * 4,
             out_specs=[VMEM] * len(wanted),
             compiler_params=params(),
@@ -257,7 +269,12 @@
 
     pairs = [(j, k) for j in range(experts) for k in (0, 2)]
     held, _ = lax.optimization_barrier((weights, parcels))
-    wanted = [(1, half, None), (0, most, 0), (2, most, 0)]
+    wanted = [
+        [(1, half, None)],
+        [(0, lead, 0)],
+        [(2, ahead, 0), (0, most - lead, lead)],
+        [(2, most - ahead, ahead)],
+    ]
     chosen = select(wanted, held)
     after, _ = lax.optimization_barrier((parcels, chosen))
     mine = [parcels[0]]
@@ -265,6 +282,7 @@
         mine.append(send(parcels[j] if k else after[j], j, k))
     shared = migrate(chosen[0], 1)
     straight = migrate(chosen[1], 0)
+    beside = migrate(chosen[2], 2)
     mine = jnp.concatenate(mine, axis=0)
     other = send(mine, 0, 1)
 
@@ -282,14 +300,15 @@
         cost_estimate=cost(0),
         name="expert",
     )(mine, other, *weights)
-    taken, shared = lax.optimization_barrier((send(give, 0, 1), shared))
+    taken, shared, beside = lax.optimization_barrier((send(give, 0, 1), shared, beside))
     summed = (keep + taken.astype(F32)).astype(BF16)
     pieces = [summed[n * PACK : (n + 1) * PACK] for n in range(len(pairs))]
-    back = [pieces[0]] + [
-        send(block, -j, k) for (j, k), block in zip(pairs[1:], pieces[1:])
-    ]
+    back = [send(block, -j, k) for (j, k), block in zip(pairs[2:], pieces[2:])]
+    back[0], across = lax.optimization_barrier((back[0], pieces[1]))
+    back = [pieces[0], send(across, 0, 2)] + back
     swapped = swap(shared, 1)
-    swapped, near = lax.optimization_barrier((swapped, chosen[2]))
+    relayed = migrate(beside[:, ahead:], 0, GROUP - 2)
+    swapped, near = lax.optimization_barrier((swapped, chosen[3]))
     near = migrate(near, 2)
 
     scaled = pl.pallas_call(
@@ -305,12 +324,12 @@
     early = pl.pallas_call(
         early_kernel,
         out_shape=shape(3, most, width),
-        in_specs=[HBM] * 2,
+        in_specs=[HBM] * 4,
         out_specs=HBM,
         scratch_shapes=[pltpu.SemaphoreType.DMA((6,))],
         compiler_params=params(),
         name="early",
-    )(shared, swapped)
+    )(shared, swapped, beside, relayed)
     back, early, straight = lax.optimization_barrier((back, early, straight))
 
     mixed, filled = pl.pallas_call(
@@ -325,7 +344,7 @@
             pltpu.SemaphoreType.DMA((3,)),
         ],
         compiler_params=params(),
-        cost_estimate=cost(12.3),
+        cost_estimate=cost(8.7),
         name="combine",
     )(scaled, *back, straight, early)
 

time: 32.5 us -> 33 us (1.015)
  waiting for transfers between devices: 15.1 us -> 9.19 us
  starting transfers between devices: 11.9 us -> 17.6 us
  Pallas kernels: 3.64 us -> 4.21 us
    ppermute x8, starting transfers between devices: 8.5 us -> 12.3 us  [send(): return lax.ppermute(block, 'expert', route)]
    ppermute x3 -> x5, waiting for transfers between devices: 5.48 us -> 2.4 us  [migrate(): return lax.ppermute(block, 'expert', route)]
    ppermute x8, waiting for transfers between devices: 9.66 us -> 6.79 us  [send(): return lax.ppermute(block, 'expert', route)]
    ppermute x3 -> x5, starting transfers between devices: 2.72 us -> 4.69 us  [migrate(): return lax.ppermute(block, 'expert', route)]
    pallas_call x1, Pallas kernels: 0.09 us -> 0.72 us  [on_device(): pl.pallas_call(early_kernel, out_shape=shape(3, most, width), in_specs=[H...]
  transfers between devices with their start and end apart: 12 -> 14, of which waited for: 8 -> 8; matrix products, arithmetic and copies ran while one was open for 0% -> 0% of each run, Pallas kernels for 8% -> 10%
where the time goes in v21:
time: 33 us; the launch traced here: 32.5 us
  starting transfers between devices  17.6 us (53%)
  waiting for transfers between devices  9.19 us (28%)
  Pallas kernels  4.21 us (13%)
  between operations  0.83 us (3%)
  local copies, waits for them, and re-layouts  0.52 us (2%)
    ppermute x8, starting transfers between devices, send(): return lax.ppermute(block, 'expert', route)  12.3 us
    ppermute x8, waiting for transfers between devices, send(): return lax.ppermute(block, 'expert', route)  6.79 us
    ppermute x5, starting transfers between devices, migrate(): return lax.ppermute(block, 'expert', route)  4.69 us
    ppermute x5, waiting for transfers between devices, migrate(): return lax.ppermute(block, 'expert', route)  2.4 us
    pallas_call x1, Pallas kernels, on_device(): pl.pallas_call(combine_kernel, out_shape=[shape(tokens.shape[0], width),...  1.32 us
    pallas_call x1, Pallas kernels, on_device(): pl.pallas_call(expert_kernel, grid=(total // step,), out_shape=[shape(tot...  0.93 us
    pallas_call x1, Pallas kernels, on_device(): pl.pallas_call(early_kernel, out_shape=shape(3, most, width), in_specs=[H...  0.72 us
    ppermute x1, starting transfers between devices, swap(): return lax.ppermute(block, ('expert', 'replica'), route)  0.69 us
  transfers between devices with their start and end apart: 14, of which 8 were waited for; matrix products, arithmetic and copies ran while one was open for 0% of the time, Pallas kernels for 10%

profile of v21, /device:TPU:0, one launch (start us, length us, event | category | flops | bytes accessed | tf_op | source)
XLA Modules:
  0.0 32.5 jit_solution(12773501247177740577)
XLA Ops:
  0.6 0.6 %begin.1.begun_ref = f32[8,128]{1,0:T(8,128)} custom-call(), custom_call_target="tpu_custom_call" | custom-call | flops 5000000000 | bytes 10000 | tf_op jit(solution)/shard_map/begin/pallas_call | solution.py:252
  1.2 0.1 copy-done.4
  1.3 0.4 %copy-done.6 = bf16[128,2048]{1,0:T(8,128)(2,1)S(1)} copy-done((bf16[128,2048]{1,0:T(8,128)(2,1)S(1)}, bf16[128,2048]{1,0:T(8,128)(2,1)}, u32[]{:S(2)}) %copy-start.6) | copy-done | bytes 524312
  1.7 0.4 %dispatch.1 = (bf16[24,1024]{1,0:T(8,128)(2,1)S(1)}, bf16[24,1024]{1,0:T(8,128)(2,1)S(1)}) custom-call(s32[8,128]{1,0:T(8,128)S(1)} %bitcast.3, bf16[128,2048]{1,0:T(8,128)(2,1)S(1)} %copy-done.6), custom_call_target="tpu_custom_call" | custom-call | flops 2000000000 | bytes 10000 | tf_op jit(solution)/shard_map/dispatch/pallas_call | solution.py:260
  2.1 4.0 %collective-permute-start.2 = (bf16[24,1024]{1,0:T(8,128)(2,1)S(1)}, bf16[24,1024]{1,0:T(8,128)(2,1)S(1)}, u32[]{:S(2)}, u32[]{:S(2)}) collective-permute-start(bf16[24,1024]{1,0:T(8,128)(2,1)S(1)} %get-tuple-element.43), channel_id=1, source_target_pairs={{0,24},{4,28},{8,16},{12,20},{16,8},{20,12},{24,0},{28,4},{1,25},{... | collective-permute-start | bytes 147464 | tf_op jit(solution)/shard_map/ppermute | solution.py:227
  6.1 0.5 %collective-permute-start = (bf16[24,1024]{1,0:T(8,128)(2,1)S(1)}, bf16[24,1024]{1,0:T(8,128)(2,1)S(1)}, u32[]{:S(2)}, u32[]{:S(2)}) collective-permute-start(bf16[24,1024]{1,0:T(8,128)(2,1)S(1)} %get-tuple-element.34), channel_id=1, source_target_pairs={{0,8},{4,12},{8,0},{12,4},{16,24},{20,28},{24,16},{28,20},{1,9},{5... | collective-permute-start | bytes 147464 | tf_op jit(solution)/shard_map/ppermute | solution.py:227
  6.7 0.7 %collective-permute-start.5 = (bf16[3,48,2048]{2,1,0:T(8,128)(2,1)S(1)}, bf16[3,48,2048]{2,1,0:T(8,128)(2,1)S(1)}, u32[]{:S(2)}, u32[]{:S(2)}) collective-permute-start(bf16[3,48,2048]{2,1,0:T(8,128)(2,1)S(1)} %get-tuple-element.39), channel_id=1, source_target_pairs={{12,4},{28,20},{13,5},{29,21},{14,6},{30,22},{15,7},{31,23}} | collective-permute-start | bytes 1769480 | tf_op jit(solution)/shard_map/ppermute | solution.py:231
  7.4 0.7 %collective-permute-start.6 = (bf16[3,48,2048]{2,1,0:T(8,128)(2,1)S(1)}, bf16[3,48,2048]{2,1,0:T(8,128)(2,1)S(1)}, u32[]{:S(2)}, u32[]{:S(2)}) collective-permute-start(bf16[3,48,2048]{2,1,0:T(8,128)(2,1)S(1)} %get-tuple-element.41), channel_id=1, source_target_pairs={{12,8},{28,24},{13,9},{29,25},{14,10},{30,26},{15,11},{31,27}} | collective-permute-start | bytes 1769480 | tf_op jit(solution)/shard_map/ppermute | solution.py:231
  8.1 0.2 collective-permute-start.1
  8.2 1.9 %collective-permute-done = bf16[24,1024]{1,0:T(8,128)(2,1)S(1)} collective-permute-done((bf16[24,1024]{1,0:T(8,128)(2,1)S(1)}, bf16[24,1024]{1,0:T(8,128)(2,1)S(1)}, u32[]{:S(2)}, u32[]{:S(2)}) %collective-permute-start) | collective-permute-done | bytes 49184 | tf_op jit(solution)/shard_map/ppermute | solution.py:227
  10.2 2.1 %collective-permute-done.1 = bf16[24,1024]{1,0:T(8,128)(2,1)S(1)} collective-permute-done((bf16[24,1024]{1,0:T(8,128)(2,1)S(1)}, bf16[24,1024]{1,0:T(8,128)(2,1)S(1)}, u32[]{:S(2)}, u32[]{:S(2)}) %collective-permute-start.1) | collective-permute-done | bytes 49184 | tf_op jit(solution)/shard_map/ppermute | solution.py:227
  12.2 0.1 collective-permute-start.3
  12.3 1.3 %collective-permute-start.12 = (bf16[3,80,2048]{2,1,0:T(8,128)(2,1)S(1)}, bf16[3,80,2048]{2,1,0:T(8,128)(2,1)S(1)}, u32[]{:S(2)}, u32[]{:S(2)}) collective-permute-start(bf16[3,80,2048]{2,1,0:T(8,128)(2,1)S(1)} %get-tuple-element.40), channel_id=1, source_target_pairs={{12,0},{28,16},{13,1},{29,17},{14,2},{30,18},{15,3},{31,19}} | collective-permute-start | bytes 2949128 | tf_op jit(solution)/shard_map/ppermute | solution.py:231
  13.6 0.1 collective-permute-done.3.other_ref
  13.8 0.9 %expert.1 = (f32[96,1024]{1,0:T(8,128)S(1)}, bf16[96,1024]{1,0:T(8,128)(2,1)S(1)}) custom-call(bf16[96,1024]{1,0:T(8,128)(2,1)S(1)} %constant_dynamic-update-slice_fusion.mine_ref, bf16[96,1024]{1,0:T(8,128)(2,1)S(1)} %collective-permute-done.3.other_ref, bf16[192,2048]{1,0:T(8,128)(2,1)S(1)} %copy-done, bf16[192,2048]{1,0:T(8,128)(2,1)S(1)} %copy-done.1, ...), custom_call_target="tpu_custom_call" | custom-call | bytes 10000 | tf_op jit(solution)/shard_map/expert/pallas_call | solution.py:293
  14.7 0.2 collective-permute-start.4
  14.9 1.3 %collective-permute-done.4 = bf16[96,1024]{1,0:T(8,128)(2,1)S(1)} collective-permute-done((bf16[96,1024]{1,0:T(8,128)(2,1)S(1)}, bf16[96,1024]{1,0:T(8,128)(2,1)S(1)}, u32[]{:S(2)}, u32[]{:S(2)}) %collective-permute-start.4) | collective-permute-done | bytes 196640 | tf_op jit(solution)/shard_map/ppermute | solution.py:227
  16.2 0.7 %collective-permute-start.7 = (bf16[3,48,2048]{2,1,0:T(8,128)(2,1)S(1)}, bf16[3,48,2048]{2,1,0:T(8,128)(2,1)S(1)}, u32[]{:S(2)}, u32[]{:S(2)}) collective-permute-start(bf16[3,48,2048]{2,1,0:T(8,128)(2,1)S(1)} %collective-permute-done.5.shared_ref), channel_id=1, source_target_pairs={{4,5},{20,21},{5,4},{21,20},{6,7},{22,23},{7,6},{23,22}} | collective-permute-start | bytes 1769480 | tf_op jit(solution)/shard_map/ppermute | solution.py:239
  16.9 1.3 %collective-permute-start.11 = (bf16[3,16,2048]{2,1,0:T(8,128)(2,1)S(1)}, bf16[3,16,2048]{2,1,0:T(8,128)(2,1)S(1)}, u32[]{:S(2)}, u32[]{:S(2)}) collective-permute-start(bf16[3,16,2048]{2,1,0:T(8,128)(2,1)S(1)} %slice.19), channel_id=1, source_target_pairs={{8,0},{24,16},{9,1},{25,17},{10,2},{26,18},{11,3},{27,19}} | collective-permute-start | bytes 589832 | tf_op jit(solution)/shard_map/ppermute | solution.py:231
  18.2 0.1 add_convert_fusion
  18.3 0.2 collective-permute-start.8
  18.5 4.0 %collective-permute-start.10 = (bf16[24,1024]{1,0:T(8,128)(2,1)S(1)}, bf16[24,1024]{1,0:T(8,128)(2,1)S(1)}, u32[]{:S(2)}, u32[]{:S(2)}) collective-permute-start(bf16[24,1024]{1,0:T(8,128)(2,1)S(1)} %get-tuple-element.64), channel_id=1, source_target_pairs={{0,24},{4,28},{8,16},{12,20},{16,8},{20,12},{24,0},{28,4},{1,25},{... | collective-permute-start | bytes 147464 | tf_op jit(solution)/shard_map/ppermute | solution.py:227
  22.5 3.2 %collective-permute-start.9 = (bf16[24,1024]{1,0:T(8,128)(2,1)S(1)}, bf16[24,1024]{1,0:T(8,128)(2,1)S(1)}, u32[]{:S(2)}, u32[]{:S(2)}) collective-permute-start(bf16[24,1024]{1,0:T(8,128)(2,1)S(1)} %get-tuple-element.50), channel_id=1, source_target_pairs={{0,8},{4,12},{8,0},{12,4},{16,24},{20,28},{24,16},{28,20},{1,9},{5... | collective-permute-start | bytes 147464 | tf_op jit(solution)/shard_map/ppermute | solution.py:227
  25.6 0.2 weigh.1.scaled_ref
  25.8 0.7 %collective-permute-start.13 = (bf16[3,64,2048]{2,1,0:T(8,128)(2,1)S(1)}, bf16[3,64,2048]{2,1,0:T(8,128)(2,1)S(1)}, u32[]{:S(2)}, u32[]{:S(2)}) collective-permute-start(bf16[3,64,2048]{2,1,0:T(8,128)(2,1)S(1)} %get-tuple-element.62), channel_id=1, source_target_pairs={{12,8},{28,24},{13,9},{29,25},{14,10},{30,26},{15,11},{31,27}} | collective-permute-start | bytes 2359304 | tf_op jit(solution)/shard_map/ppermute | solution.py:231
  26.5 0.1 collective-permute-done.11.relayed_ref
  26.7 0.7 %early.1.refs_5_ = bf16[3,96,2048]{2,1,0:T(8,128)(2,1)} custom-call(bf16[3,48,2048]{2,1,0:T(8,128)(2,1)S(1)} %collective-permute-done.5.shared_ref, bf16[3,48,2048]{2,1,0:T(8,128)(2,1)S(1)} %collective-permute-done.7.swapped_ref, bf16[3,48,2048]{2,1,0:T(8,128)(2,1)S(1)} %collective-permute-done.6.beside_ref, ...), custom_call_target="tpu_custom_call" | custom-call | tf_op jit(solution)/shard_map/early/pallas_call | solution.py:324
  27.4 0.1 collective-permute-done.10.refs_3_
  27.5 1.3 %collective-permute-done.9.refs_1_ = bf16[24,1024]{1,0:T(8,128)(2,1)S(1)} collective-permute-done((bf16[24,1024]{1,0:T(8,128)(2,1)S(1)}, bf16[24,1024]{1,0:T(8,128)(2,1)S(1)}, u32[]{:S(2)}, u32[]{:S(2)}) %collective-permute-start.9) | collective-permute-done | bytes 49184 | tf_op jit(solution)/shard_map/ppermute | solution.py:227
  28.8 2.3 %collective-permute-done.12.refs_4_ = bf16[3,80,2048]{2,1,0:T(8,128)(2,1)S(1)} collective-permute-done((bf16[3,80,2048]{2,1,0:T(8,128)(2,1)S(1)}, bf16[3,80,2048]{2,1,0:T(8,128)(2,1)S(1)}, u32[]{:S(2)}, u32[]{:S(2)}) %collective-permute-start.12) | collective-permute-done | bytes 983072 | tf_op jit(solution)/shard_map/ppermute | solution.py:231
  31.0 1.3 %combine.1 = (bf16[128,2048]{1,0:T(8,128)(2,1)}, bf16[3,96,2048]{2,1,0:T(8,128)(2,1)}) custom-call(bf16[2,2,128,128]{3,2,1,0:T(8,128)(2,1)S(1)} %weigh.1.scaled_ref, bf16[24,1024]{1,0:T(8,128)(2,1)S(1)} %get-tuple-element.54.refs_0_, bf16[24,1024]{1,0:T(8,128)(2,1)S(1)} %collective-permute-done.9.refs_1_, ...), custom_call_target="tpu_custom_call", output_to_operand_aliasing={{1}: (6, {})} | custom-call | flops 8700000256 | bytes 10000 | tf_op jit(solution)/shard_map/combine/pallas_call | solution.py:335
  32.4 0.1 late.1
  (27 shorter events, 0.1 us)
Async XLA Ops:
  0.6 0.7 %copy-start.4 = (s32[128,8]{0,1:T(8,128)S(1)}, s32[128,8]{0,1:T(8,128)}, u32[]{:S(2)}) copy-start(s32[128,8]{0,1:T(8,128)} %param.8) | copy-start | bytes 12292
  0.6 1.1 %copy-start.6 = (bf16[128,2048]{1,0:T(8,128)(2,1)S(1)}, bf16[128,2048]{1,0:T(8,128)(2,1)}, u32[]{:S(2)}) copy-start(bf16[128,2048]{1,0:T(8,128)(2,1)} %tok_ref.1) | copy-start | bytes 1572868
  1.7 4.9 %copy-start = (bf16[192,2048]{1,0:T(8,128)(2,1)S(1)}, bf16[192,2048]{1,0:T(8,128)(2,1)}, u32[]{:S(2)}) copy-start(bf16[192,2048]{1,0:T(8,128)(2,1)} %gate_ref.2) | copy-start | bytes 2359300
  1.7 4.9 %copy-start.1 = (bf16[192,2048]{1,0:T(8,128)(2,1)S(1)}, bf16[192,2048]{1,0:T(8,128)(2,1)}, u32[]{:S(2)}) copy-start(bf16[192,2048]{1,0:T(8,128)(2,1)} %up_ref.2) | copy-start | bytes 2359300
  1.7 4.9 %copy-start.2 = (bf16[192,2048]{1,0:T(8,128)(2,1)S(1)}, bf16[192,2048]{1,0:T(8,128)(2,1)}, u32[]{:S(2)}) copy-start(bf16[192,2048]{1,0:T(8,128)(2,1)} %down_ref.2) | copy-start | bytes 2359300
  1.7 4.9 %copy-start.7 = (s32[2,3,96]{2,0,1:T(2,128)S(1)}, s32[2,3,96]{2,0,1:T(2,128)}, u32[]{:S(2)}) copy-start(s32[2,3,96]{2,0,1:T(2,128)} %param.13) | copy-start | bytes 6916
  2.1 10.1 %collective-permute-start.2 = (bf16[24,1024]{1,0:T(8,128)(2,1)S(1)}, bf16[24,1024]{1,0:T(8,128)(2,1)S(1)}, u32[]{:S(2)}, u32[]{:S(2)}) collective-permute-start(bf16[24,1024]{1,0:T(8,128)(2,1)S(1)} %get-tuple-element.43), channel_id=1, source_target_pairs={{0,24},{4,28},{8,16},{12,20},{16,8},{20,12},{24,0},{28,4},{1,25},{... | collective-permute-start | bytes 147464 | tf_op jit(solution)/shard_map/ppermute | solution.py:227
  6.1 4.1 %collective-permute-start = (bf16[24,1024]{1,0:T(8,128)(2,1)S(1)}, bf16[24,1024]{1,0:T(8,128)(2,1)S(1)}, u32[]{:S(2)}, u32[]{:S(2)}) collective-permute-start(bf16[24,1024]{1,0:T(8,128)(2,1)S(1)} %get-tuple-element.34), channel_id=1, source_target_pairs={{0,8},{4,12},{8,0},{12,4},{16,24},{20,28},{24,16},{28,20},{1,9},{5... | collective-permute-start | bytes 147464 | tf_op jit(solution)/shard_map/ppermute | solution.py:227
  6.7 9.6 %collective-permute-start.5 = (bf16[3,48,2048]{2,1,0:T(8,128)(2,1)S(1)}, bf16[3,48,2048]{2,1,0:T(8,128)(2,1)S(1)}, u32[]{:S(2)}, u32[]{:S(2)}) collective-permute-start(bf16[3,48,2048]{2,1,0:T(8,128)(2,1)S(1)} %get-tuple-element.39), channel_id=1, source_target_pairs={{12,4},{28,20},{13,5},{29,21},{14,6},{30,22},{15,7},{31,23}} | collective-permute-start | bytes 1769480 | tf_op jit(solution)/shard_map/ppermute | solution.py:231
  7.4 8.9 %collective-permute-start.6 = (bf16[3,48,2048]{2,1,0:T(8,128)(2,1)S(1)}, bf16[3,48,2048]{2,1,0:T(8,128)(2,1)S(1)}, u32[]{:S(2)}, u32[]{:S(2)}) collective-permute-start(bf16[3,48,2048]{2,1,0:T(8,128)(2,1)S(1)} %get-tuple-element.41), channel_id=1, source_target_pairs={{12,8},{28,24},{13,9},{29,25},{14,10},{30,26},{15,11},{31,27}} | collective-permute-start | bytes 1769480 | tf_op jit(solution)/shard_map/ppermute | solution.py:231
  8.1 4.2 %collective-permute-start.1 = (bf16[24,1024]{1,0:T(8,128)(2,1)S(1)}, bf16[24,1024]{1,0:T(8,128)(2,1)S(1)}, u32[]{:S(2)}, u32[]{:S(2)}) collective-permute-start(bf16[24,1024]{1,0:T(8,128)(2,1)S(1)} %get-tuple-element.43), channel_id=1, source_target_pairs={{0,16},{4,20},{8,24},{12,28},{16,0},{20,4},{24,8},{28,12},{1,17},{... | collective-permute-start | bytes 147464 | tf_op jit(solution)/shard_map/ppermute | solution.py:227
  12.2 1.5 %collective-permute-start.3 = (bf16[96,1024]{1,0:T(8,128)(2,1)S(1)}, bf16[96,1024]{1,0:T(8,128)(2,1)S(1)}, u32[]{:S(2)}, u32[]{:S(2)}) collective-permute-start(bf16[96,1024]{1,0:T(8,128)(2,1)S(1)} %constant_dynamic-update-slice_fusion.mine_ref), channel_id=1, source_target_pairs={{0,4},{4,0},{8,12},{12,8},{16,20},{20,16},{24,28},{28,24},{1,5},{5... | collective-permute-start | bytes 589832 | tf_op jit(solution)/shard_map/ppermute | solution.py:227
  12.3 18.7 %collective-permute-start.12 = (bf16[3,80,2048]{2,1,0:T(8,128)(2,1)S(1)}, bf16[3,80,2048]{2,1,0:T(8,128)(2,1)S(1)}, u32[]{:S(2)}, u32[]{:S(2)}) collective-permute-start(bf16[3,80,2048]{2,1,0:T(8,128)(2,1)S(1)} %get-tuple-element.40), channel_id=1, source_target_pairs={{12,0},{28,16},{13,1},{29,17},{14,2},{30,18},{15,3},{31,19}} | collective-permute-start | bytes 2949128 | tf_op jit(solution)/shard_map/ppermute | solution.py:231
  14.7 11.0 %copy-start.5 = (f32[128,8]{0,1:T(8,128)S(1)}, f32[128,8]{0,1:T(8,128)}, u32[]{:S(2)}) copy-start(f32[128,8]{0,1:T(8,128)} %param.9) | copy-start | bytes 12292
  14.7 1.5 %collective-permute-start.4 = (bf16[96,1024]{1,0:T(8,128)(2,1)S(1)}, bf16[96,1024]{1,0:T(8,128)(2,1)S(1)}, u32[]{:S(2)}, u32[]{:S(2)}) collective-permute-start(bf16[96,1024]{1,0:T(8,128)(2,1)S(1)} %get-tuple-element.44), channel_id=1, source_target_pairs={{0,4},{4,0},{8,12},{12,8},{16,20},{20,16},{24,28},{28,24},{1,5},{5... | collective-permute-start | bytes 589832 | tf_op jit(solution)/shard_map/ppermute | solution.py:227
  16.2 9.6 %collective-permute-start.7 = (bf16[3,48,2048]{2,1,0:T(8,128)(2,1)S(1)}, bf16[3,48,2048]{2,1,0:T(8,128)(2,1)S(1)}, u32[]{:S(2)}, u32[]{:S(2)}) collective-permute-start(bf16[3,48,2048]{2,1,0:T(8,128)(2,1)S(1)} %collective-permute-done.5.shared_ref), channel_id=1, source_target_pairs={{4,5},{20,21},{5,4},{21,20},{6,7},{22,23},{7,6},{23,22}} | collective-permute-start | bytes 1769480 | tf_op jit(solution)/shard_map/ppermute | solution.py:239
  16.9 9.7 %collective-permute-start.11 = (bf16[3,16,2048]{2,1,0:T(8,128)(2,1)S(1)}, bf16[3,16,2048]{2,1,0:T(8,128)(2,1)S(1)}, u32[]{:S(2)}, u32[]{:S(2)}) collective-permute-start(bf16[3,16,2048]{2,1,0:T(8,128)(2,1)S(1)} %slice.19), channel_id=1, source_target_pairs={{8,0},{24,16},{9,1},{25,17},{10,2},{26,18},{11,3},{27,19}} | collective-permute-start | bytes 589832 | tf_op jit(solution)/shard_map/ppermute | solution.py:231
  18.3 4.2 %collective-permute-start.8 = (bf16[24,1024]{1,0:T(8,128)(2,1)S(1)}, bf16[24,1024]{1,0:T(8,128)(2,1)S(1)}, u32[]{:S(2)}, u32[]{:S(2)}) collective-permute-start(bf16[24,1024]{1,0:T(8,128)(2,1)S(1)} %get-tuple-element.66), channel_id=1, source_target_pairs={{0,16},{4,20},{8,24},{12,28},{16,0},{20,4},{24,8},{28,12},{1,17},{... | collective-permute-start | bytes 147464 | tf_op jit(solution)/shard_map/ppermute | solution.py:227
  18.5 9.0 %collective-permute-start.10 = (bf16[24,1024]{1,0:T(8,128)(2,1)S(1)}, bf16[24,1024]{1,0:T(8,128)(2,1)S(1)}, u32[]{:S(2)}, u32[]{:S(2)}) collective-permute-start(bf16[24,1024]{1,0:T(8,128)(2,1)S(1)} %get-tuple-element.64), channel_id=1, source_target_pairs={{0,24},{4,28},{8,16},{12,20},{16,8},{20,12},{24,0},{28,4},{1,25},{... | collective-permute-start | bytes 147464 | tf_op jit(solution)/shard_map/ppermute | solution.py:227
  22.5 6.3 %collective-permute-start.9 = (bf16[24,1024]{1,0:T(8,128)(2,1)S(1)}, bf16[24,1024]{1,0:T(8,128)(2,1)S(1)}, u32[]{:S(2)}, u32[]{:S(2)}) collective-permute-start(bf16[24,1024]{1,0:T(8,128)(2,1)S(1)} %get-tuple-element.50), channel_id=1, source_target_pairs={{0,8},{4,12},{8,0},{12,4},{16,24},{20,28},{24,16},{28,20},{1,9},{5... | collective-permute-start | bytes 147464 | tf_op jit(solution)/shard_map/ppermute | solution.py:227
  25.8 6.6 %collective-permute-start.13 = (bf16[3,64,2048]{2,1,0:T(8,128)(2,1)S(1)}, bf16[3,64,2048]{2,1,0:T(8,128)(2,1)S(1)}, u32[]{:S(2)}, u32[]{:S(2)}) collective-permute-start(bf16[3,64,2048]{2,1,0:T(8,128)(2,1)S(1)} %get-tuple-element.62), channel_id=1, source_target_pairs={{12,8},{28,24},{13,9},{29,25},{14,10},{30,26},{15,11},{31,27}} | collective-permute-start | bytes 2359304 | tf_op jit(solution)/shard_map/ppermute | solution.py:231
  31.0 1.3 %copy-start.3 = (f32[8,128]{1,0:T(8,128)S(1)}, f32[8,128]{1,0:T(8,128)}, u32[]{:S(2)}) copy-start(f32[8,128]{1,0:T(8,128)} %begin.1.begun_ref) | copy-start | bytes 12292

commit v22 on v20

--- a/solution.py
+++ b/solution.py
@@ -145,25 +145,26 @@
     ids = ids_ref[...]
     group = lax.axis_index("expert") // GROUP
     place = token_places(ids, group, experts)
-    each = out_ref.shape[2] // STRIDE // experts
+    each = out_ref.shape[3] // STRIDE // experts
     slot = lax.broadcasted_iota(jnp.int32, (STRIDE, ids.shape[1]), 0)
+    chosen = [[], []]
     for j in range(experts):
         named = ids == lax.rem(group + j, experts)
         weight = jnp.sum(jnp.where(named, weight_ref[...], 0.0), axis=0, keepdims=True)
         for side in range(2):
-            chosen = jnp.where(slot == place[j : j + 1, :] + side * CAP, weight, 0.0)
-            high = chosen.astype(BF16)
-            low = (chosen - high.astype(F32)).astype(BF16)
-            for n in range(j * each, (j + 1) * each):
-                out_ref[side, 0, n * STRIDE : (n + 1) * STRIDE, :] = high
-                out_ref[side, 1, n * STRIDE : (n + 1) * STRIDE, :] = low
+            block = jnp.where(slot == place[j : j + 1, :] + side * CAP, weight, 0.0)
+            chosen[side] += [block] * each
+    for side in range(2):
+        scaled = jnp.concatenate(chosen[side], axis=0).T
+        high = scaled.astype(BF16)
+        out_ref[side, 0] = high
+        out_ref[side, 1] = (scaled - high.astype(F32)).astype(BF16)
 
 
 def combine_kernel(scaled_ref, *refs):
-    piece_refs, (straight_ref, early_ref, out_ref, arrived_ref) = refs[:-7], refs[-7:-3]
-    rows_ref, mixed_ref, sems = refs[-3:]
+    piece_refs, (straight_ref, early_ref, out_ref, arrived_ref) = refs[:-6], refs[-6:-2]
+    mixed_ref, sems = refs[-2:]
     half = out_ref.shape[1] // 2
-    numbers = (((0,), (0,)), ((), ()))
     direct = lax.axis_index("expert") % GROUP % 3 == 0
     fill = pltpu.make_async_copy(straight_ref, arrived_ref, sems.at[2])
 
@@ -171,16 +172,15 @@
     def _():
         fill.start()
 
-    for n, ref in enumerate(piece_refs):
-        rows_ref[n * STRIDE : n * STRIDE + PACK, :] = ref[...]
-        rows_ref[n * STRIDE + PACK : (n + 1) * STRIDE, :] = jnp.zeros((STRIDE - PACK, half), BF16)
-    rows = rows_ref[...]
+    blank = jnp.zeros((STRIDE - PACK, half), F32)
+    rows = []
+    for ref in piece_refs:
+        rows += [ref[...].astype(F32), blank]
+    rows = jnp.concatenate(rows, axis=0).astype(BF16)
     copies = []
     for side in range(2):
-        mixed = lax.dot_general(scaled_ref[side, 0], rows, numbers, preferred_element_type=F32)
-        mixed = mixed + lax.dot_general(
-            scaled_ref[side, 1], rows, numbers, preferred_element_type=F32
-        )
+        mixed = jnp.dot(scaled_ref[side, 0], rows, preferred_element_type=F32)
+        mixed = mixed + jnp.dot(scaled_ref[side, 1], rows, preferred_element_type=F32)
         columns = pl.ds(side * half, half)
         mixed_ref[:, columns] = mixed.astype(BF16)
         copy = pltpu.make_async_copy(mixed_ref.at[:, columns], out_ref.at[:, columns], sems.at[side])
@@ -294,7 +294,7 @@
 
     scaled = pl.pallas_call(
         functools.partial(weigh_kernel, experts),
-        out_shape=shape(2, 2, len(back) * STRIDE, tokens.shape[0]),
+        out_shape=shape(2, 2, tokens.shape[0], len(back) * STRIDE),
         in_specs=[VMEM, VMEM],
         out_specs=VMEM,
         compiler_params=params(),
@@ -320,7 +320,6 @@
         out_specs=[HBM] * 2,
         input_output_aliases={len(back) + 2: 1},
         scratch_shapes=[
-            pltpu.VMEM((len(back) * STRIDE, width // 2), BF16),
             pltpu.VMEM((tokens.shape[0], width), BF16),
             pltpu.SemaphoreType.DMA((3,)),
         ],

time: 32.5 us -> 32.5 us (level)
  transfers between devices with their start and end apart: 12 -> 12, of which waited for: 8 -> 8; matrix products, arithmetic and copies ran while one was open for 0% -> 0% of each run, Pallas kernels for 8% -> 9%
where the time goes in v22:
time: 32.5 us; the launch traced here: 32.1 us
  waiting for transfers between devices  15.1 us (46%)
  starting transfers between devices  11.9 us (37%)
  Pallas kernels  3.81 us (12%)
  between operations  0.8 us (2%)
  local copies, waits for them, and re-layouts  0.52 us (2%)
    ppermute x8, waiting for transfers between devices, send(): return lax.ppermute(block, 'expert', route)  9.57 us
    ppermute x8, starting transfers between devices, send(): return lax.ppermute(block, 'expert', route)  8.5 us
    ppermute x3, waiting for transfers between devices, migrate(): return lax.ppermute(block, 'expert', route)  5.48 us
    ppermute x3, starting transfers between devices, migrate(): return lax.ppermute(block, 'expert', route)  2.72 us
    pallas_call x1, Pallas kernels, on_device(): pl.pallas_call(combine_kernel, out_shape=[shape(tokens.shape[0], width),...  1.47 us
    pallas_call x1, Pallas kernels, on_device(): pl.pallas_call(expert_kernel, grid=(total // step,), out_shape=[shape(tot...  0.92 us
    ppermute x1, starting transfers between devices, swap(): return lax.ppermute(block, ('expert', 'replica'), route)  0.69 us
  transfers between devices with their start and end apart: 12, of which 8 were waited for; matrix products, arithmetic and copies ran while one was open for 0% of the time, Pallas kernels for 9%

profile of v22, /device:TPU:0, one launch (start us, length us, event | category | flops | bytes accessed | tf_op | source)
XLA Modules:
  0.0 32.1 jit_solution(14350191379326325178)
XLA Ops:
  0.6 0.6 %begin.1.begun_ref = f32[8,128]{1,0:T(8,128)} custom-call(), custom_call_target="tpu_custom_call" | custom-call | flops 5000000000 | bytes 10000 | tf_op jit(solution)/shard_map/begin/pallas_call | solution.py:240
  1.2 0.1 copy-done.3
  1.3 0.4 %copy-done.6 = bf16[128,2048]{1,0:T(8,128)(2,1)S(1)} copy-done((bf16[128,2048]{1,0:T(8,128)(2,1)S(1)}, bf16[128,2048]{1,0:T(8,128)(2,1)}, u32[]{:S(2)}) %copy-start.6) | copy-done | bytes 524312
  1.7 0.4 %dispatch.1 = (bf16[24,1024]{1,0:T(8,128)(2,1)S(1)}, bf16[24,1024]{1,0:T(8,128)(2,1)S(1)}) custom-call(s32[8,128]{1,0:T(8,128)S(1)} %bitcast.3, bf16[128,2048]{1,0:T(8,128)(2,1)S(1)} %copy-done.6), custom_call_target="tpu_custom_call" | custom-call | flops 2000000000 | bytes 10000 | tf_op jit(solution)/shard_map/dispatch/pallas_call | solution.py:248
  2.1 4.0 %collective-permute-start.2 = (bf16[24,1024]{1,0:T(8,128)(2,1)S(1)}, bf16[24,1024]{1,0:T(8,128)(2,1)S(1)}, u32[]{:S(2)}, u32[]{:S(2)}) collective-permute-start(bf16[24,1024]{1,0:T(8,128)(2,1)S(1)} %get-tuple-element.38), channel_id=1, source_target_pairs={{0,24},{4,28},{8,16},{12,20},{16,8},{20,12},{24,0},{28,4},{1,25},{... | collective-permute-start | bytes 147464 | tf_op jit(solution)/shard_map/ppermute | solution.py:215
  6.1 0.5 %collective-permute-start = (bf16[24,1024]{1,0:T(8,128)(2,1)S(1)}, bf16[24,1024]{1,0:T(8,128)(2,1)S(1)}, u32[]{:S(2)}, u32[]{:S(2)}) collective-permute-start(bf16[24,1024]{1,0:T(8,128)(2,1)S(1)} %get-tuple-element.30), channel_id=1, source_target_pairs={{0,8},{4,12},{8,0},{12,4},{16,24},{20,28},{24,16},{28,20},{1,9},{5... | collective-permute-start | bytes 147464 | tf_op jit(solution)/shard_map/ppermute | solution.py:215
  6.7 0.7 %collective-permute-start.5 = (bf16[3,48,2048]{2,1,0:T(8,128)(2,1)S(1)}, bf16[3,48,2048]{2,1,0:T(8,128)(2,1)S(1)}, u32[]{:S(2)}, u32[]{:S(2)}) collective-permute-start(bf16[3,48,2048]{2,1,0:T(8,128)(2,1)S(1)} %get-tuple-element.35), channel_id=1, source_target_pairs={{12,4},{28,20},{13,5},{29,21},{14,6},{30,22},{15,7},{31,23}} | collective-permute-start | bytes 1769480 | tf_op jit(solution)/shard_map/ppermute | solution.py:219
  7.4 1.3 %collective-permute-start.10 = (bf16[3,96,2048]{2,1,0:T(8,128)(2,1)S(1)}, bf16[3,96,2048]{2,1,0:T(8,128)(2,1)S(1)}, u32[]{:S(2)}, u32[]{:S(2)}) collective-permute-start(bf16[3,96,2048]{2,1,0:T(8,128)(2,1)S(1)} %get-tuple-element.36), channel_id=1, source_target_pairs={{12,0},{28,16},{13,1},{29,17},{14,2},{30,18},{15,3},{31,19}} | collective-permute-start | bytes 3538952 | tf_op jit(solution)/shard_map/ppermute | solution.py:219
  8.7 0.2 collective-permute-start.1
  8.8 1.3 %collective-permute-done = bf16[24,1024]{1,0:T(8,128)(2,1)S(1)} collective-permute-done((bf16[24,1024]{1,0:T(8,128)(2,1)S(1)}, bf16[24,1024]{1,0:T(8,128)(2,1)S(1)}, u32[]{:S(2)}, u32[]{:S(2)}) %collective-permute-start) | collective-permute-done | bytes 49184 | tf_op jit(solution)/shard_map/ppermute | solution.py:215
  10.2 2.6 %collective-permute-done.1 = bf16[24,1024]{1,0:T(8,128)(2,1)S(1)} collective-permute-done((bf16[24,1024]{1,0:T(8,128)(2,1)S(1)}, bf16[24,1024]{1,0:T(8,128)(2,1)S(1)}, u32[]{:S(2)}, u32[]{:S(2)}) %collective-permute-start.1) | collective-permute-done | bytes 49184 | tf_op jit(solution)/shard_map/ppermute | solution.py:215
  12.8 0.1 collective-permute-start.3
  12.9 1.4 %collective-permute-done.3.other_ref = bf16[96,1024]{1,0:T(8,128)(2,1)S(1)} collective-permute-done((bf16[96,1024]{1,0:T(8,128)(2,1)S(1)}, bf16[96,1024]{1,0:T(8,128)(2,1)S(1)}, u32[]{:S(2)}, u32[]{:S(2)}) %collective-permute-start.3) | collective-permute-done | bytes 196640 | tf_op jit(solution)/shard_map/ppermute | solution.py:215
  14.3 0.9 %expert.1 = (f32[96,1024]{1,0:T(8,128)S(1)}, bf16[96,1024]{1,0:T(8,128)(2,1)S(1)}) custom-call(bf16[96,1024]{1,0:T(8,128)(2,1)S(1)} %constant_dynamic-update-slice_fusion.mine_ref, bf16[96,1024]{1,0:T(8,128)(2,1)S(1)} %collective-permute-done.3.other_ref, bf16[192,2048]{1,0:T(8,128)(2,1)S(1)} %copy-done, bf16[192,2048]{1,0:T(8,128)(2,1)S(1)} %copy-done.1, ...), custom_call_target="tpu_custom_call" | custom-call | bytes 10000 | tf_op jit(solution)/shard_map/expert/pallas_call | solution.py:275
  15.3 0.0 copy-start.4
  15.3 0.2 collective-permute-start.4
  15.5 1.3 %collective-permute-done.4 = bf16[96,1024]{1,0:T(8,128)(2,1)S(1)} collective-permute-done((bf16[96,1024]{1,0:T(8,128)(2,1)S(1)}, bf16[96,1024]{1,0:T(8,128)(2,1)S(1)}, u32[]{:S(2)}, u32[]{:S(2)}) %collective-permute-start.4) | collective-permute-done | bytes 196640 | tf_op jit(solution)/shard_map/ppermute | solution.py:215
  16.8 0.0 collective-permute-done.5.shared_ref
  16.8 0.7 %collective-permute-start.6 = (bf16[3,48,2048]{2,1,0:T(8,128)(2,1)S(1)}, bf16[3,48,2048]{2,1,0:T(8,128)(2,1)S(1)}, u32[]{:S(2)}, u32[]{:S(2)}) collective-permute-start(bf16[3,48,2048]{2,1,0:T(8,128)(2,1)S(1)} %collective-permute-done.5.shared_ref), channel_id=1, source_target_pairs={{4,5},{20,21},{5,4},{21,20},{6,7},{22,23},{7,6},{23,22}} | collective-permute-start | bytes 1769480 | tf_op jit(solution)/shard_map/ppermute | solution.py:227
  17.6 1.1 %collective-permute-start.9 = (bf16[24,1024]{1,0:T(8,128)(2,1)S(1)}, bf16[24,1024]{1,0:T(8,128)(2,1)S(1)}, u32[]{:S(2)}, u32[]{:S(2)}) collective-permute-start(bf16[24,1024]{1,0:T(8,128)(2,1)S(1)} %get-tuple-element.56), channel_id=1, source_target_pairs={{0,24},{4,28},{8,16},{12,20},{16,8},{20,12},{24,0},{28,4},{1,25},{... | collective-permute-start | bytes 147464 | tf_op jit(solution)/shard_map/ppermute | solution.py:215
  18.7 1.7 %collective-permute-start.8 = (bf16[24,1024]{1,0:T(8,128)(2,1)S(1)}, bf16[24,1024]{1,0:T(8,128)(2,1)S(1)}, u32[]{:S(2)}, u32[]{:S(2)}) collective-permute-start(bf16[24,1024]{1,0:T(8,128)(2,1)S(1)} %get-tuple-element.57), channel_id=1, source_target_pairs={{0,16},{4,20},{8,24},{12,28},{16,0},{20,4},{24,8},{28,12},{1,17},{... | collective-permute-start | bytes 147464 | tf_op jit(solution)/shard_map/ppermute | solution.py:215
  20.4 0.7 %collective-permute-start.7 = (bf16[24,1024]{1,0:T(8,128)(2,1)S(1)}, bf16[24,1024]{1,0:T(8,128)(2,1)S(1)}, u32[]{:S(2)}, u32[]{:S(2)}) collective-permute-start(bf16[24,1024]{1,0:T(8,128)(2,1)S(1)} %get-tuple-element.58), channel_id=1, source_target_pairs={{0,8},{4,12},{8,0},{12,4},{16,24},{20,28},{24,16},{28,20},{1,9},{5... | collective-permute-start | bytes 147464 | tf_op jit(solution)/shard_map/ppermute | solution.py:215
  21.1 0.0 collective-permute-done.6.swapped_ref
  21.1 0.7 %collective-permute-start.11 = (bf16[3,96,2048]{2,1,0:T(8,128)(2,1)S(1)}, bf16[3,96,2048]{2,1,0:T(8,128)(2,1)S(1)}, u32[]{:S(2)}, u32[]{:S(2)}) collective-permute-start(bf16[3,96,2048]{2,1,0:T(8,128)(2,1)S(1)} %get-tuple-element.54), channel_id=1, source_target_pairs={{12,8},{28,24},{13,9},{29,25},{14,10},{30,26},{15,11},{31,27}} | collective-permute-start | bytes 3538952 | tf_op jit(solution)/shard_map/ppermute | solution.py:219
  21.9 0.3 weigh.1.scaled_ref
  22.1 0.1 early.1.refs_5_
  22.2 1.0 %collective-permute-done.9.refs_3_ = bf16[24,1024]{1,0:T(8,128)(2,1)S(1)} collective-permute-done((bf16[24,1024]{1,0:T(8,128)(2,1)S(1)}, bf16[24,1024]{1,0:T(8,128)(2,1)S(1)}, u32[]{:S(2)}, u32[]{:S(2)}) %collective-permute-start.9) | collective-permute-done | bytes 49184 | tf_op jit(solution)/shard_map/ppermute | solution.py:215
  23.2 0.3 collective-permute-done.8.refs_2_
  23.5 1.6 %collective-permute-done.7.refs_1_ = bf16[24,1024]{1,0:T(8,128)(2,1)S(1)} collective-permute-done((bf16[24,1024]{1,0:T(8,128)(2,1)S(1)}, bf16[24,1024]{1,0:T(8,128)(2,1)S(1)}, u32[]{:S(2)}, u32[]{:S(2)}) %collective-permute-start.7) | collective-permute-done | bytes 49184 | tf_op jit(solution)/shard_map/ppermute | solution.py:215
  25.1 5.5 %collective-permute-done.10.refs_4_ = bf16[3,96,2048]{2,1,0:T(8,128)(2,1)S(1)} collective-permute-done((bf16[3,96,2048]{2,1,0:T(8,128)(2,1)S(1)}, bf16[3,96,2048]{2,1,0:T(8,128)(2,1)S(1)}, u32[]{:S(2)}, u32[]{:S(2)}) %collective-permute-start.10) | collective-permute-done | bytes 1179680 | tf_op jit(solution)/shard_map/ppermute | solution.py:219
  30.6 1.5 %combine.1 = (bf16[128,2048]{1,0:T(8,128)(2,1)}, bf16[3,96,2048]{2,1,0:T(8,128)(2,1)}) custom-call(bf16[2,2,128,128]{3,2,1,0:T(8,128)(2,1)S(1)} %weigh.1.scaled_ref, bf16[24,1024]{1,0:T(8,128)(2,1)S(1)} %get-tuple-element.46.refs_0_, bf16[24,1024]{1,0:T(8,128)(2,1)S(1)} %collective-permute-done.7.refs_1_, ...), custom_call_target="tpu_custom_call", output_to_operand_aliasing={{1}: (6, {})} | custom-call | flops 12300000256 | bytes 10000 | tf_op jit(solution)/shard_map/combine/pallas_call | solution.py:316
  32.1 0.1 late.1
  (22 shorter events, 0.1 us)
Async XLA Ops:
  0.6 0.7 %copy-start.3 = (s32[128,8]{0,1:T(8,128)S(1)}, s32[128,8]{0,1:T(8,128)}, u32[]{:S(2)}) copy-start(s32[128,8]{0,1:T(8,128)} %param.8) | copy-start | bytes 12292
  0.6 1.1 %copy-start.6 = (bf16[128,2048]{1,0:T(8,128)(2,1)S(1)}, bf16[128,2048]{1,0:T(8,128)(2,1)}, u32[]{:S(2)}) copy-start(bf16[128,2048]{1,0:T(8,128)(2,1)} %tok_ref.1) | copy-start | bytes 1572868
  1.7 4.9 %copy-start = (bf16[192,2048]{1,0:T(8,128)(2,1)S(1)}, bf16[192,2048]{1,0:T(8,128)(2,1)}, u32[]{:S(2)}) copy-start(bf16[192,2048]{1,0:T(8,128)(2,1)} %gate_ref.2) | copy-start | bytes 2359300
  1.7 4.9 %copy-start.1 = (bf16[192,2048]{1,0:T(8,128)(2,1)S(1)}, bf16[192,2048]{1,0:T(8,128)(2,1)}, u32[]{:S(2)}) copy-start(bf16[192,2048]{1,0:T(8,128)(2,1)} %up_ref.2) | copy-start | bytes 2359300
  1.7 4.9 %copy-start.2 = (bf16[192,2048]{1,0:T(8,128)(2,1)S(1)}, bf16[192,2048]{1,0:T(8,128)(2,1)}, u32[]{:S(2)}) copy-start(bf16[192,2048]{1,0:T(8,128)(2,1)} %down_ref.2) | copy-start | bytes 2359300
  1.7 4.9 %copy-start.7 = (s32[2,3,96]{2,0,1:T(2,128)S(1)}, s32[2,3,96]{2,0,1:T(2,128)}, u32[]{:S(2)}) copy-start(s32[2,3,96]{2,0,1:T(2,128)} %param.13) | copy-start | bytes 6916
  2.1 10.7 %collective-permute-start.2 = (bf16[24,1024]{1,0:T(8,128)(2,1)S(1)}, bf16[24,1024]{1,0:T(8,128)(2,1)S(1)}, u32[]{:S(2)}, u32[]{:S(2)}) collective-permute-start(bf16[24,1024]{1,0:T(8,128)(2,1)S(1)} %get-tuple-element.38), channel_id=1, source_target_pairs={{0,24},{4,28},{8,16},{12,20},{16,8},{20,12},{24,0},{28,4},{1,25},{... | collective-permute-start | bytes 147464 | tf_op jit(solution)/shard_map/ppermute | solution.py:215
  6.1 4.1 %collective-permute-start = (bf16[24,1024]{1,0:T(8,128)(2,1)S(1)}, bf16[24,1024]{1,0:T(8,128)(2,1)S(1)}, u32[]{:S(2)}, u32[]{:S(2)}) collective-permute-start(bf16[24,1024]{1,0:T(8,128)(2,1)S(1)} %get-tuple-element.30), channel_id=1, source_target_pairs={{0,8},{4,12},{8,0},{12,4},{16,24},{20,28},{24,16},{28,20},{1,9},{5... | collective-permute-start | bytes 147464 | tf_op jit(solution)/shard_map/ppermute | solution.py:215
  6.7 10.1 %collective-permute-start.5 = (bf16[3,48,2048]{2,1,0:T(8,128)(2,1)S(1)}, bf16[3,48,2048]{2,1,0:T(8,128)(2,1)S(1)}, u32[]{:S(2)}, u32[]{:S(2)}) collective-permute-start(bf16[3,48,2048]{2,1,0:T(8,128)(2,1)S(1)} %get-tuple-element.35), channel_id=1, source_target_pairs={{12,4},{28,20},{13,5},{29,21},{14,6},{30,22},{15,7},{31,23}} | collective-permute-start | bytes 1769480 | tf_op jit(solution)/shard_map/ppermute | solution.py:219
  7.4 23.2 %collective-permute-start.10 = (bf16[3,96,2048]{2,1,0:T(8,128)(2,1)S(1)}, bf16[3,96,2048]{2,1,0:T(8,128)(2,1)S(1)}, u32[]{:S(2)}, u32[]{:S(2)}) collective-permute-start(bf16[3,96,2048]{2,1,0:T(8,128)(2,1)S(1)} %get-tuple-element.36), channel_id=1, source_target_pairs={{12,0},{28,16},{13,1},{29,17},{14,2},{30,18},{15,3},{31,19}} | collective-permute-start | bytes 3538952 | tf_op jit(solution)/shard_map/ppermute | solution.py:219
  8.7 4.2 %collective-permute-start.1 = (bf16[24,1024]{1,0:T(8,128)(2,1)S(1)}, bf16[24,1024]{1,0:T(8,128)(2,1)S(1)}, u32[]{:S(2)}, u32[]{:S(2)}) collective-permute-start(bf16[24,1024]{1,0:T(8,128)(2,1)S(1)} %get-tuple-element.38), channel_id=1, source_target_pairs={{0,16},{4,20},{8,24},{12,28},{16,0},{20,4},{24,8},{28,12},{1,17},{... | collective-permute-start | bytes 147464 | tf_op jit(solution)/shard_map/ppermute | solution.py:215
  12.8 1.5 %collective-permute-start.3 = (bf16[96,1024]{1,0:T(8,128)(2,1)S(1)}, bf16[96,1024]{1,0:T(8,128)(2,1)S(1)}, u32[]{:S(2)}, u32[]{:S(2)}) collective-permute-start(bf16[96,1024]{1,0:T(8,128)(2,1)S(1)} %constant_dynamic-update-slice_fusion.mine_ref), channel_id=1, source_target_pairs={{0,4},{4,0},{8,12},{12,8},{16,20},{20,16},{24,28},{28,24},{1,5},{5... | collective-permute-start | bytes 589832 | tf_op jit(solution)/shard_map/ppermute | solution.py:215
  15.3 6.6 %copy-start.4 = (f32[128,8]{0,1:T(8,128)S(1)}, f32[128,8]{0,1:T(8,128)}, u32[]{:S(2)}) copy-start(f32[128,8]{0,1:T(8,128)} %param.9) | copy-start | bytes 12292
  15.3 1.5 %collective-permute-start.4 = (bf16[96,1024]{1,0:T(8,128)(2,1)S(1)}, bf16[96,1024]{1,0:T(8,128)(2,1)S(1)}, u32[]{:S(2)}, u32[]{:S(2)}) collective-permute-start(bf16[96,1024]{1,0:T(8,128)(2,1)S(1)} %get-tuple-element.39), channel_id=1, source_target_pairs={{0,4},{4,0},{8,12},{12,8},{16,20},{20,16},{24,28},{28,24},{1,5},{5... | collective-permute-start | bytes 589832 | tf_op jit(solution)/shard_map/ppermute | solution.py:215
  16.8 4.3 %collective-permute-start.6 = (bf16[3,48,2048]{2,1,0:T(8,128)(2,1)S(1)}, bf16[3,48,2048]{2,1,0:T(8,128)(2,1)S(1)}, u32[]{:S(2)}, u32[]{:S(2)}) collective-permute-start(bf16[3,48,2048]{2,1,0:T(8,128)(2,1)S(1)} %collective-permute-done.5.shared_ref), channel_id=1, source_target_pairs={{4,5},{20,21},{5,4},{21,20},{6,7},{22,23},{7,6},{23,22}} | collective-permute-start | bytes 1769480 | tf_op jit(solution)/shard_map/ppermute | solution.py:227
  17.6 5.6 %collective-permute-start.9 = (bf16[24,1024]{1,0:T(8,128)(2,1)S(1)}, bf16[24,1024]{1,0:T(8,128)(2,1)S(1)}, u32[]{:S(2)}, u32[]{:S(2)}) collective-permute-start(bf16[24,1024]{1,0:T(8,128)(2,1)S(1)} %get-tuple-element.56), channel_id=1, source_target_pairs={{0,24},{4,28},{8,16},{12,20},{16,8},{20,12},{24,0},{28,4},{1,25},{... | collective-permute-start | bytes 147464 | tf_op jit(solution)/shard_map/ppermute | solution.py:215
  18.7 4.8 %collective-permute-start.8 = (bf16[24,1024]{1,0:T(8,128)(2,1)S(1)}, bf16[24,1024]{1,0:T(8,128)(2,1)S(1)}, u32[]{:S(2)}, u32[]{:S(2)}) collective-permute-start(bf16[24,1024]{1,0:T(8,128)(2,1)S(1)} %get-tuple-element.57), channel_id=1, source_target_pairs={{0,16},{4,20},{8,24},{12,28},{16,0},{20,4},{24,8},{28,12},{1,17},{... | collective-permute-start | bytes 147464 | tf_op jit(solution)/shard_map/ppermute | solution.py:215
  20.4 4.7 %collective-permute-start.7 = (bf16[24,1024]{1,0:T(8,128)(2,1)S(1)}, bf16[24,1024]{1,0:T(8,128)(2,1)S(1)}, u32[]{:S(2)}, u32[]{:S(2)}) collective-permute-start(bf16[24,1024]{1,0:T(8,128)(2,1)S(1)} %get-tuple-element.58), channel_id=1, source_target_pairs={{0,8},{4,12},{8,0},{12,4},{16,24},{20,28},{24,16},{28,20},{1,9},{5... | collective-permute-start | bytes 147464 | tf_op jit(solution)/shard_map/ppermute | solution.py:215
  21.1 10.9 %collective-permute-start.11 = (bf16[3,96,2048]{2,1,0:T(8,128)(2,1)S(1)}, bf16[3,96,2048]{2,1,0:T(8,128)(2,1)S(1)}, u32[]{:S(2)}, u32[]{:S(2)}) collective-permute-start(bf16[3,96,2048]{2,1,0:T(8,128)(2,1)S(1)} %get-tuple-element.54), channel_id=1, source_target_pairs={{12,8},{28,24},{13,9},{29,25},{14,10},{30,26},{15,11},{31,27}} | collective-permute-start | bytes 3538952 | tf_op jit(solution)/shard_map/ppermute | solution.py:219
  30.6 1.5 %copy-start.5 = (f32[8,128]{1,0:T(8,128)S(1)}, f32[8,128]{1,0:T(8,128)}, u32[]{:S(2)}) copy-start(f32[8,128]{1,0:T(8,128)} %begin.1.begun_ref) | copy-start | bytes 12292

commit v23 on v22

--- a/solution.py
+++ b/solution.py
@@ -257,9 +257,10 @@
 
     pairs = [(j, k) for j in range(experts) for k in (0, 2)]
     held, _ = lax.optimization_barrier((weights, parcels))
-    wanted = [(1, half, None), (0, most, 0), (2, most, 0)]
-    chosen = select(wanted, held)
-    after, _ = lax.optimization_barrier((parcels, chosen))
+    chosen = list(select([(1, half, None)], held))
+    held, _ = lax.optimization_barrier((weights, chosen))
+    chosen += select([(0, most, 0), (2, most, 0)], held)
+    after, _ = lax.optimization_barrier((parcels, chosen[0]))
     mine = [parcels[0]]
     for j, k in pairs[1:]:
         mine.append(send(parcels[j] if k else after[j], j, k))

time: 32.5 us -> 32.3 us (level)
    ppermute x8, waiting for transfers between devices: 9.57 us -> 8.78 us  [send(): return lax.ppermute(block, 'expert', route)]
    ppermute x3, waiting for transfers between devices: 5.48 us -> 6.13 us  [migrate(): return lax.ppermute(block, 'expert', route)]
where the time goes in v23:
time: 32.3 us; the launch traced here: 32 us
  waiting for transfers between devices  14.9 us (46%)
  starting transfers between devices  11.9 us (37%)
  Pallas kernels  3.82 us (12%)
  between operations  0.81 us (3%)
  local copies, waits for them, and re-layouts  0.52 us (2%)
    ppermute x8, waiting for transfers between devices, send(): return lax.ppermute(block, 'expert', route)  8.78 us
    ppermute x8, starting transfers between devices, send(): return lax.ppermute(block, 'expert', route)  8.49 us
    ppermute x3, waiting for transfers between devices, migrate(): return lax.ppermute(block, 'expert', route)  6.13 us
    ppermute x3, starting transfers between devices, migrate(): return lax.ppermute(block, 'expert', route)  2.7 us
    pallas_call x1, Pallas kernels, on_device(): pl.pallas_call(combine_kernel, out_shape=[shape(tokens.shape[0], width),...  1.48 us
    pallas_call x1, Pallas kernels, on_device(): pl.pallas_call(expert_kernel, grid=(total // step,), out_shape=[shape(tot...  0.93 us
    ppermute x1, starting transfers between devices, swap(): return lax.ppermute(block, ('expert', 'replica'), route)  0.69 us
  transfers between devices with their start and end apart: 12, of which 8 were waited for; matrix products, arithmetic and copies ran while one was open for 0% of the time, Pallas kernels for 9%

profile of v23, /device:TPU:0, one launch (start us, length us, event | category | flops | bytes accessed | tf_op | source)
XLA Modules:
  0.0 32.0 jit_solution(15630303912700707638)
XLA Ops:
  0.6 0.6 %begin.1.begun_ref = f32[8,128]{1,0:T(8,128)} custom-call(), custom_call_target="tpu_custom_call" | custom-call | flops 5000000000 | bytes 10000 | tf_op jit(solution)/shard_map/begin/pallas_call | solution.py:240
  1.2 0.1 copy-done.3
  1.3 0.4 %copy-done.6 = bf16[128,2048]{1,0:T(8,128)(2,1)S(1)} copy-done((bf16[128,2048]{1,0:T(8,128)(2,1)S(1)}, bf16[128,2048]{1,0:T(8,128)(2,1)}, u32[]{:S(2)}) %copy-start.6) | copy-done | bytes 524312
  1.7 0.4 %dispatch.1 = (bf16[24,1024]{1,0:T(8,128)(2,1)S(1)}, bf16[24,1024]{1,0:T(8,128)(2,1)S(1)}) custom-call(s32[8,128]{1,0:T(8,128)S(1)} %bitcast.3, bf16[128,2048]{1,0:T(8,128)(2,1)S(1)} %copy-done.6), custom_call_target="tpu_custom_call" | custom-call | flops 2000000000 | bytes 10000 | tf_op jit(solution)/shard_map/dispatch/pallas_call | solution.py:248
  2.1 4.0 %collective-permute-start.2 = (bf16[24,1024]{1,0:T(8,128)(2,1)S(1)}, bf16[24,1024]{1,0:T(8,128)(2,1)S(1)}, u32[]{:S(2)}, u32[]{:S(2)}) collective-permute-start(bf16[24,1024]{1,0:T(8,128)(2,1)S(1)} %get-tuple-element.37), channel_id=1, source_target_pairs={{0,24},{4,28},{8,16},{12,20},{16,8},{20,12},{24,0},{28,4},{1,25},{... | collective-permute-start | bytes 147464 | tf_op jit(solution)/shard_map/ppermute | solution.py:215
  6.1 0.5 %collective-permute-start = (bf16[24,1024]{1,0:T(8,128)(2,1)S(1)}, bf16[24,1024]{1,0:T(8,128)(2,1)S(1)}, u32[]{:S(2)}, u32[]{:S(2)}) collective-permute-start(bf16[24,1024]{1,0:T(8,128)(2,1)S(1)} %get-tuple-element.32), channel_id=1, source_target_pairs={{0,8},{4,12},{8,0},{12,4},{16,24},{20,28},{24,16},{28,20},{1,9},{5... | collective-permute-start | bytes 147464 | tf_op jit(solution)/shard_map/ppermute | solution.py:215
  6.6 0.7 %collective-permute-start.5 = (bf16[3,48,2048]{2,1,0:T(8,128)(2,1)S(1)}, bf16[3,48,2048]{2,1,0:T(8,128)(2,1)S(1)}, u32[]{:S(2)}, u32[]{:S(2)}) collective-permute-start(bf16[3,48,2048]{2,1,0:T(8,128)(2,1)S(1)} %select.2), channel_id=1, source_target_pairs={{12,4},{28,20},{13,5},{29,21},{14,6},{30,22},{15,7},{31,23}} | collective-permute-start | bytes 1769480 | tf_op jit(solution)/shard_map/ppermute | solution.py:219
  7.4 0.2 collective-permute-start.1
  7.5 1.3 %collective-permute-start.10 = (bf16[3,96,2048]{2,1,0:T(8,128)(2,1)S(1)}, bf16[3,96,2048]{2,1,0:T(8,128)(2,1)S(1)}, u32[]{:S(2)}, u32[]{:S(2)}) collective-permute-start(bf16[3,96,2048]{2,1,0:T(8,128)(2,1)S(1)} %get-tuple-element.49), channel_id=1, source_target_pairs={{12,0},{28,16},{13,1},{29,17},{14,2},{30,18},{15,3},{31,19}} | collective-permute-start | bytes 3538952 | tf_op jit(solution)/shard_map/ppermute | solution.py:219
  8.8 1.3 %collective-permute-done = bf16[24,1024]{1,0:T(8,128)(2,1)S(1)} collective-permute-done((bf16[24,1024]{1,0:T(8,128)(2,1)S(1)}, bf16[24,1024]{1,0:T(8,128)(2,1)S(1)}, u32[]{:S(2)}, u32[]{:S(2)}) %collective-permute-start) | collective-permute-done | bytes 49184 | tf_op jit(solution)/shard_map/ppermute | solution.py:215
  10.2 1.3 %collective-permute-done.1 = bf16[24,1024]{1,0:T(8,128)(2,1)S(1)} collective-permute-done((bf16[24,1024]{1,0:T(8,128)(2,1)S(1)}, bf16[24,1024]{1,0:T(8,128)(2,1)S(1)}, u32[]{:S(2)}, u32[]{:S(2)}) %collective-permute-start.1) | collective-permute-done | bytes 49184 | tf_op jit(solution)/shard_map/ppermute | solution.py:215
  11.5 0.0 collective-permute-done.2
  11.5 0.1 collective-permute-start.3
  11.6 1.4 %collective-permute-done.3.other_ref = bf16[96,1024]{1,0:T(8,128)(2,1)S(1)} collective-permute-done((bf16[96,1024]{1,0:T(8,128)(2,1)S(1)}, bf16[96,1024]{1,0:T(8,128)(2,1)S(1)}, u32[]{:S(2)}, u32[]{:S(2)}) %collective-permute-start.3) | collective-permute-done | bytes 196640 | tf_op jit(solution)/shard_map/ppermute | solution.py:215
  13.0 0.9 %expert.1 = (f32[96,1024]{1,0:T(8,128)S(1)}, bf16[96,1024]{1,0:T(8,128)(2,1)S(1)}) custom-call(bf16[96,1024]{1,0:T(8,128)(2,1)S(1)} %constant_dynamic-update-slice_fusion.mine_ref, bf16[96,1024]{1,0:T(8,128)(2,1)S(1)} %collective-permute-done.3.other_ref, bf16[192,2048]{1,0:T(8,128)(2,1)S(1)} %copy-done, bf16[192,2048]{1,0:T(8,128)(2,1)S(1)} %copy-done.1, ...), custom_call_target="tpu_custom_call" | custom-call | bytes 10000 | tf_op jit(solution)/shard_map/expert/pallas_call | solution.py:276
  14.0 0.0 copy-start.4
  14.0 0.2 collective-permute-start.4
  14.2 1.3 %collective-permute-done.4 = bf16[96,1024]{1,0:T(8,128)(2,1)S(1)} collective-permute-done((bf16[96,1024]{1,0:T(8,128)(2,1)S(1)}, bf16[96,1024]{1,0:T(8,128)(2,1)S(1)}, u32[]{:S(2)}, u32[]{:S(2)}) %collective-permute-start.4) | collective-permute-done | bytes 196640 | tf_op jit(solution)/shard_map/ppermute | solution.py:215
  15.5 0.0 collective-permute-done.5.shared_ref
  15.5 0.7 %collective-permute-start.6 = (bf16[3,48,2048]{2,1,0:T(8,128)(2,1)S(1)}, bf16[3,48,2048]{2,1,0:T(8,128)(2,1)S(1)}, u32[]{:S(2)}, u32[]{:S(2)}) collective-permute-start(bf16[3,48,2048]{2,1,0:T(8,128)(2,1)S(1)} %collective-permute-done.5.shared_ref), channel_id=1, source_target_pairs={{4,5},{20,21},{5,4},{21,20},{6,7},{22,23},{7,6},{23,22}} | collective-permute-start | bytes 1769480 | tf_op jit(solution)/shard_map/ppermute | solution.py:227
  16.3 1.7 %collective-permute-start.9 = (bf16[24,1024]{1,0:T(8,128)(2,1)S(1)}, bf16[24,1024]{1,0:T(8,128)(2,1)S(1)}, u32[]{:S(2)}, u32[]{:S(2)}) collective-permute-start(bf16[24,1024]{1,0:T(8,128)(2,1)S(1)} %get-tuple-element.60), channel_id=1, source_target_pairs={{0,24},{4,28},{8,16},{12,20},{16,8},{20,12},{24,0},{28,4},{1,25},{... | collective-permute-start | bytes 147464 | tf_op jit(solution)/shard_map/ppermute | solution.py:215
  18.0 1.6 %collective-permute-start.8 = (bf16[24,1024]{1,0:T(8,128)(2,1)S(1)}, bf16[24,1024]{1,0:T(8,128)(2,1)S(1)}, u32[]{:S(2)}, u32[]{:S(2)}) collective-permute-start(bf16[24,1024]{1,0:T(8,128)(2,1)S(1)} %get-tuple-element.61), channel_id=1, source_target_pairs={{0,16},{4,20},{8,24},{12,28},{16,0},{20,4},{24,8},{28,12},{1,17},{... | collective-permute-start | bytes 147464 | tf_op jit(solution)/shard_map/ppermute | solution.py:215
  19.6 0.2 collective-permute-start.7
  19.8 0.7 %collective-permute-start.11 = (bf16[3,96,2048]{2,1,0:T(8,128)(2,1)S(1)}, bf16[3,96,2048]{2,1,0:T(8,128)(2,1)S(1)}, u32[]{:S(2)}, u32[]{:S(2)}) collective-permute-start(bf16[3,96,2048]{2,1,0:T(8,128)(2,1)S(1)} %get-tuple-element.58), channel_id=1, source_target_pairs={{12,8},{28,24},{13,9},{29,25},{14,10},{30,26},{15,11},{31,27}} | collective-permute-start | bytes 3538952 | tf_op jit(solution)/shard_map/ppermute | solution.py:219
  20.6 0.3 weigh.1.scaled_ref
  20.8 0.1 early.1.refs_5_
  20.9 1.0 %collective-permute-done.9.refs_3_ = bf16[24,1024]{1,0:T(8,128)(2,1)S(1)} collective-permute-done((bf16[24,1024]{1,0:T(8,128)(2,1)S(1)}, bf16[24,1024]{1,0:T(8,128)(2,1)S(1)}, u32[]{:S(2)}, u32[]{:S(2)}) %collective-permute-start.9) | collective-permute-done | bytes 49184 | tf_op jit(solution)/shard_map/ppermute | solution.py:215
  21.9 0.3 %collective-permute-done.8.refs_2_ = bf16[24,1024]{1,0:T(8,128)(2,1)S(1)} collective-permute-done((bf16[24,1024]{1,0:T(8,128)(2,1)S(1)}, bf16[24,1024]{1,0:T(8,128)(2,1)S(1)}, u32[]{:S(2)}, u32[]{:S(2)}) %collective-permute-start.8) | collective-permute-done | bytes 49184 | tf_op jit(solution)/shard_map/ppermute | solution.py:215
  22.3 2.0 %collective-permute-done.7.refs_1_ = bf16[24,1024]{1,0:T(8,128)(2,1)S(1)} collective-permute-done((bf16[24,1024]{1,0:T(8,128)(2,1)S(1)}, bf16[24,1024]{1,0:T(8,128)(2,1)S(1)}, u32[]{:S(2)}, u32[]{:S(2)}) %collective-permute-start.7) | collective-permute-done | bytes 49184 | tf_op jit(solution)/shard_map/ppermute | solution.py:215
  24.3 6.1 %collective-permute-done.10.refs_4_ = bf16[3,96,2048]{2,1,0:T(8,128)(2,1)S(1)} collective-permute-done((bf16[3,96,2048]{2,1,0:T(8,128)(2,1)S(1)}, bf16[3,96,2048]{2,1,0:T(8,128)(2,1)S(1)}, u32[]{:S(2)}, u32[]{:S(2)}) %collective-permute-start.10) | collective-permute-done | bytes 1179680 | tf_op jit(solution)/shard_map/ppermute | solution.py:219
  30.4 1.5 %combine.1 = (bf16[128,2048]{1,0:T(8,128)(2,1)}, bf16[3,96,2048]{2,1,0:T(8,128)(2,1)}) custom-call(bf16[2,2,128,128]{3,2,1,0:T(8,128)(2,1)S(1)} %weigh.1.scaled_ref, bf16[24,1024]{1,0:T(8,128)(2,1)S(1)} %get-tuple-element.50.refs_0_, bf16[24,1024]{1,0:T(8,128)(2,1)S(1)} %collective-permute-done.7.refs_1_, ...), custom_call_target="tpu_custom_call", output_to_operand_aliasing={{1}: (6, {})} | custom-call | flops 12300000256 | bytes 10000 | tf_op jit(solution)/shard_map/combine/pallas_call | solution.py:317
  31.9 0.1 late.1
  (23 shorter events, 0.1 us)
Async XLA Ops:
  0.6 0.7 %copy-start.3 = (s32[128,8]{0,1:T(8,128)S(1)}, s32[128,8]{0,1:T(8,128)}, u32[]{:S(2)}) copy-start(s32[128,8]{0,1:T(8,128)} %param.8) | copy-start | bytes 12292
  0.6 1.1 %copy-start.6 = (bf16[128,2048]{1,0:T(8,128)(2,1)S(1)}, bf16[128,2048]{1,0:T(8,128)(2,1)}, u32[]{:S(2)}) copy-start(bf16[128,2048]{1,0:T(8,128)(2,1)} %tok_ref.1) | copy-start | bytes 1572868
  1.7 4.9 %copy-start = (bf16[192,2048]{1,0:T(8,128)(2,1)S(1)}, bf16[192,2048]{1,0:T(8,128)(2,1)}, u32[]{:S(2)}) copy-start(bf16[192,2048]{1,0:T(8,128)(2,1)} %gate_ref.3) | copy-start | bytes 2359300
  1.7 4.9 %copy-start.1 = (bf16[192,2048]{1,0:T(8,128)(2,1)S(1)}, bf16[192,2048]{1,0:T(8,128)(2,1)}, u32[]{:S(2)}) copy-start(bf16[192,2048]{1,0:T(8,128)(2,1)} %up_ref.3) | copy-start | bytes 2359300
  1.7 4.9 %copy-start.2 = (bf16[192,2048]{1,0:T(8,128)(2,1)S(1)}, bf16[192,2048]{1,0:T(8,128)(2,1)}, u32[]{:S(2)}) copy-start(bf16[192,2048]{1,0:T(8,128)(2,1)} %down_ref.3) | copy-start | bytes 2359300
  1.7 4.9 %copy-start.7 = (s32[2,3,96]{2,0,1:T(2,128)S(1)}, s32[2,3,96]{2,0,1:T(2,128)}, u32[]{:S(2)}) copy-start(s32[2,3,96]{2,0,1:T(2,128)} %param.13) | copy-start | bytes 6916
  2.1 9.4 %collective-permute-start.2 = (bf16[24,1024]{1,0:T(8,128)(2,1)S(1)}, bf16[24,1024]{1,0:T(8,128)(2,1)S(1)}, u32[]{:S(2)}, u32[]{:S(2)}) collective-permute-start(bf16[24,1024]{1,0:T(8,128)(2,1)S(1)} %get-tuple-element.37), channel_id=1, source_target_pairs={{0,24},{4,28},{8,16},{12,20},{16,8},{20,12},{24,0},{28,4},{1,25},{... | collective-permute-start | bytes 147464 | tf_op jit(solution)/shard_map/ppermute | solution.py:215
  6.1 4.1 %collective-permute-start = (bf16[24,1024]{1,0:T(8,128)(2,1)S(1)}, bf16[24,1024]{1,0:T(8,128)(2,1)S(1)}, u32[]{:S(2)}, u32[]{:S(2)}) collective-permute-start(bf16[24,1024]{1,0:T(8,128)(2,1)S(1)} %get-tuple-element.32), channel_id=1, source_target_pairs={{0,8},{4,12},{8,0},{12,4},{16,24},{20,28},{24,16},{28,20},{1,9},{5... | collective-permute-start | bytes 147464 | tf_op jit(solution)/shard_map/ppermute | solution.py:215
  6.6 8.9 %collective-permute-start.5 = (bf16[3,48,2048]{2,1,0:T(8,128)(2,1)S(1)}, bf16[3,48,2048]{2,1,0:T(8,128)(2,1)S(1)}, u32[]{:S(2)}, u32[]{:S(2)}) collective-permute-start(bf16[3,48,2048]{2,1,0:T(8,128)(2,1)S(1)} %select.2), channel_id=1, source_target_pairs={{12,4},{28,20},{13,5},{29,21},{14,6},{30,22},{15,7},{31,23}} | collective-permute-start | bytes 1769480 | tf_op jit(solution)/shard_map/ppermute | solution.py:219
  7.4 4.2 %collective-permute-start.1 = (bf16[24,1024]{1,0:T(8,128)(2,1)S(1)}, bf16[24,1024]{1,0:T(8,128)(2,1)S(1)}, u32[]{:S(2)}, u32[]{:S(2)}) collective-permute-start(bf16[24,1024]{1,0:T(8,128)(2,1)S(1)} %get-tuple-element.37), channel_id=1, source_target_pairs={{0,16},{4,20},{8,24},{12,28},{16,0},{20,4},{24,8},{28,12},{1,17},{... | collective-permute-start | bytes 147464 | tf_op jit(solution)/shard_map/ppermute | solution.py:215
  7.5 22.9 %collective-permute-start.10 = (bf16[3,96,2048]{2,1,0:T(8,128)(2,1)S(1)}, bf16[3,96,2048]{2,1,0:T(8,128)(2,1)S(1)}, u32[]{:S(2)}, u32[]{:S(2)}) collective-permute-start(bf16[3,96,2048]{2,1,0:T(8,128)(2,1)S(1)} %get-tuple-element.49), channel_id=1, source_target_pairs={{12,0},{28,16},{13,1},{29,17},{14,2},{30,18},{15,3},{31,19}} | collective-permute-start | bytes 3538952 | tf_op jit(solution)/shard_map/ppermute | solution.py:219
  11.5 1.5 %collective-permute-start.3 = (bf16[96,1024]{1,0:T(8,128)(2,1)S(1)}, bf16[96,1024]{1,0:T(8,128)(2,1)S(1)}, u32[]{:S(2)}, u32[]{:S(2)}) collective-permute-start(bf16[96,1024]{1,0:T(8,128)(2,1)S(1)} %constant_dynamic-update-slice_fusion.mine_ref), channel_id=1, source_target_pairs={{0,4},{4,0},{8,12},{12,8},{16,20},{20,16},{24,28},{28,24},{1,5},{5... | collective-permute-start | bytes 589832 | tf_op jit(solution)/shard_map/ppermute | solution.py:215
  14.0 6.6 %copy-start.4 = (f32[128,8]{0,1:T(8,128)S(1)}, f32[128,8]{0,1:T(8,128)}, u32[]{:S(2)}) copy-start(f32[128,8]{0,1:T(8,128)} %param.9) | copy-start | bytes 12292
  14.0 1.5 %collective-permute-start.4 = (bf16[96,1024]{1,0:T(8,128)(2,1)S(1)}, bf16[96,1024]{1,0:T(8,128)(2,1)S(1)}, u32[]{:S(2)}, u32[]{:S(2)}) collective-permute-start(bf16[96,1024]{1,0:T(8,128)(2,1)S(1)} %get-tuple-element.38), channel_id=1, source_target_pairs={{0,4},{4,0},{8,12},{12,8},{16,20},{20,16},{24,28},{28,24},{1,5},{5... | collective-permute-start | bytes 589832 | tf_op jit(solution)/shard_map/ppermute | solution.py:215
  15.5 4.3 %collective-permute-start.6 = (bf16[3,48,2048]{2,1,0:T(8,128)(2,1)S(1)}, bf16[3,48,2048]{2,1,0:T(8,128)(2,1)S(1)}, u32[]{:S(2)}, u32[]{:S(2)}) collective-permute-start(bf16[3,48,2048]{2,1,0:T(8,128)(2,1)S(1)} %collective-permute-done.5.shared_ref), channel_id=1, source_target_pairs={{4,5},{20,21},{5,4},{21,20},{6,7},{22,23},{7,6},{23,22}} | collective-permute-start | bytes 1769480 | tf_op jit(solution)/shard_map/ppermute | solution.py:227
  16.3 5.6 %collective-permute-start.9 = (bf16[24,1024]{1,0:T(8,128)(2,1)S(1)}, bf16[24,1024]{1,0:T(8,128)(2,1)S(1)}, u32[]{:S(2)}, u32[]{:S(2)}) collective-permute-start(bf16[24,1024]{1,0:T(8,128)(2,1)S(1)} %get-tuple-element.60), channel_id=1, source_target_pairs={{0,24},{4,28},{8,16},{12,20},{16,8},{20,12},{24,0},{28,4},{1,25},{... | collective-permute-start | bytes 147464 | tf_op jit(solution)/shard_map/ppermute | solution.py:215
  18.0 4.3 %collective-permute-start.8 = (bf16[24,1024]{1,0:T(8,128)(2,1)S(1)}, bf16[24,1024]{1,0:T(8,128)(2,1)S(1)}, u32[]{:S(2)}, u32[]{:S(2)}) collective-permute-start(bf16[24,1024]{1,0:T(8,128)(2,1)S(1)} %get-tuple-element.61), channel_id=1, source_target_pairs={{0,16},{4,20},{8,24},{12,28},{16,0},{20,4},{24,8},{28,12},{1,17},{... | collective-permute-start | bytes 147464 | tf_op jit(solution)/shard_map/ppermute | solution.py:215
  19.6 4.7 %collective-permute-start.7 = (bf16[24,1024]{1,0:T(8,128)(2,1)S(1)}, bf16[24,1024]{1,0:T(8,128)(2,1)S(1)}, u32[]{:S(2)}, u32[]{:S(2)}) collective-permute-start(bf16[24,1024]{1,0:T(8,128)(2,1)S(1)} %get-tuple-element.62), channel_id=1, source_target_pairs={{0,8},{4,12},{8,0},{12,4},{16,24},{20,28},{24,16},{28,20},{1,9},{5... | collective-permute-start | bytes 147464 | tf_op jit(solution)/shard_map/ppermute | solution.py:215
  19.8 12.1 %collective-permute-start.11 = (bf16[3,96,2048]{2,1,0:T(8,128)(2,1)S(1)}, bf16[3,96,2048]{2,1,0:T(8,128)(2,1)S(1)}, u32[]{:S(2)}, u32[]{:S(2)}) collective-permute-start(bf16[3,96,2048]{2,1,0:T(8,128)(2,1)S(1)} %get-tuple-element.58), channel_id=1, source_target_pairs={{12,8},{28,24},{13,9},{29,25},{14,10},{30,26},{15,11},{31,27}} | collective-permute-start | bytes 3538952 | tf_op jit(solution)/shard_map/ppermute | solution.py:219
  30.4 1.5 %copy-start.5 = (f32[8,128]{1,0:T(8,128)S(1)}, f32[8,128]{1,0:T(8,128)}, u32[]{:S(2)}) copy-start(f32[8,128]{1,0:T(8,128)} %begin.1.begun_ref) | copy-start | bytes 12292

commit v24 on v23

--- a/solution.py
+++ b/solution.py
@@ -145,7 +145,7 @@
     ids = ids_ref[...]
     group = lax.axis_index("expert") // GROUP
     place = token_places(ids, group, experts)
-    each = out_ref.shape[3] // STRIDE // experts
+    each = out_ref.shape[2] // 2 // STRIDE // experts
     slot = lax.broadcasted_iota(jnp.int32, (STRIDE, ids.shape[1]), 0)
     chosen = [[], []]
     for j in range(experts):
@@ -157,8 +157,8 @@
     for side in range(2):
         scaled = jnp.concatenate(chosen[side], axis=0).T
         high = scaled.astype(BF16)
-        out_ref[side, 0] = high
-        out_ref[side, 1] = (scaled - high.astype(F32)).astype(BF16)
+        low = (scaled - high.astype(F32)).astype(BF16)
+        out_ref[side] = jnp.concatenate([high, low], axis=1)
 
 
 def combine_kernel(scaled_ref, *refs):
@@ -166,21 +166,25 @@
     mixed_ref, sems = refs[-2:]
     half = out_ref.shape[1] // 2
     direct = lax.axis_index("expert") % GROUP % 3 == 0
-    fill = pltpu.make_async_copy(straight_ref, arrived_ref, sems.at[2])
+    fills = [
+        pltpu.make_async_copy(straight_ref.at[m], arrived_ref.at[m], sems.at[2 + m])
+        for m in range(3)
+    ]
 
     @pl.when(direct)
     def _():
-        fill.start()
+        for fill in fills:
+            fill.start()
 
     blank = jnp.zeros((STRIDE - PACK, half), F32)
     rows = []
     for ref in piece_refs:
         rows += [ref[...].astype(F32), blank]
     rows = jnp.concatenate(rows, axis=0).astype(BF16)
+    rows = jnp.concatenate([rows, rows], axis=0)
     copies = []
     for side in range(2):
-        mixed = jnp.dot(scaled_ref[side, 0], rows, preferred_element_type=F32)
-        mixed = mixed + jnp.dot(scaled_ref[side, 1], rows, preferred_element_type=F32)
+        mixed = jnp.dot(scaled_ref[side], rows, preferred_element_type=F32)
         columns = pl.ds(side * half, half)
         mixed_ref[:, columns] = mixed.astype(BF16)
         copy = pltpu.make_async_copy(mixed_ref.at[:, columns], out_ref.at[:, columns], sems.at[side])
@@ -191,7 +195,8 @@
 
     @pl.when(direct)
     def _():
-        fill.wait()
+        for fill in fills:
+            fill.wait()
 
 
 def on_device(tokens, expert_ids, combine, old_gate, old_up, old_down, move_plan):
@@ -295,7 +300,7 @@
 
     scaled = pl.pallas_call(
         functools.partial(weigh_kernel, experts),
-        out_shape=shape(2, 2, tokens.shape[0], len(back) * STRIDE),
+        out_shape=shape(2, tokens.shape[0], 2 * len(back) * STRIDE),
         in_specs=[VMEM, VMEM],
         out_specs=VMEM,
         compiler_params=params(),
@@ -322,7 +327,7 @@
         input_output_aliases={len(back) + 2: 1},
         scratch_shapes=[
             pltpu.VMEM((tokens.shape[0], width), BF16),
-            pltpu.SemaphoreType.DMA((3,)),
+            pltpu.SemaphoreType.DMA((5,)),
         ],
         compiler_params=params(),
         cost_estimate=cost(12.3),

time: 32.3 us -> 32.2 us (level)
  transfers between devices with their start and end apart: 12 -> 12, of which waited for: 8 -> 8; matrix products, arithmetic and copies ran while one was open for 0% -> 0% of each run, Pallas kernels for 9% -> 8%
where the time goes in v24:
time: 32.2 us; the launch traced here: 31.9 us
  waiting for transfers between devices  14.9 us (46%)
  starting transfers between devices  11.9 us (37%)
  Pallas kernels  3.73 us (12%)
  between operations  0.81 us (3%)
  local copies, waits for them, and re-layouts  0.52 us (2%)
    ppermute x8, waiting for transfers between devices, send(): return lax.ppermute(block, 'expert', route)  8.78 us
    ppermute x8, starting transfers between devices, send(): return lax.ppermute(block, 'expert', route)  8.49 us
    ppermute x3, waiting for transfers between devices, migrate(): return lax.ppermute(block, 'expert', route)  6.13 us
    ppermute x3, starting transfers between devices, migrate(): return lax.ppermute(block, 'expert', route)  2.7 us
    pallas_call x1, Pallas kernels, on_device(): pl.pallas_call(combine_kernel, out_shape=[shape(tokens.shape[0], width),...  1.39 us
    pallas_call x1, Pallas kernels, on_device(): pl.pallas_call(expert_kernel, grid=(total // step,), out_shape=[shape(tot...  0.93 us
    ppermute x1, starting transfers between devices, swap(): return lax.ppermute(block, ('expert', 'replica'), route)  0.69 us
  transfers between devices with their start and end apart: 12, of which 8 were waited for; matrix products, arithmetic and copies ran while one was open for 0% of the time, Pallas kernels for 8%

profile of v24, /device:TPU:0, one launch (start us, length us, event | category | flops | bytes accessed | tf_op | source)
XLA Modules:
  0.0 31.9 jit_solution(16127149913800042569)
XLA Ops:
  0.6 0.6 %begin.1.begun_ref = f32[8,128]{1,0:T(8,128)} custom-call(), custom_call_target="tpu_custom_call" | custom-call | flops 5000000000 | bytes 10000 | tf_op jit(solution)/shard_map/begin/pallas_call | solution.py:245
  1.2 0.1 copy-done.3
  1.3 0.4 %copy-done.6 = bf16[128,2048]{1,0:T(8,128)(2,1)S(1)} copy-done((bf16[128,2048]{1,0:T(8,128)(2,1)S(1)}, bf16[128,2048]{1,0:T(8,128)(2,1)}, u32[]{:S(2)}) %copy-start.6) | copy-done | bytes 524312
  1.7 0.4 %dispatch.1 = (bf16[24,1024]{1,0:T(8,128)(2,1)S(1)}, bf16[24,1024]{1,0:T(8,128)(2,1)S(1)}) custom-call(s32[8,128]{1,0:T(8,128)S(1)} %bitcast.3, bf16[128,2048]{1,0:T(8,128)(2,1)S(1)} %copy-done.6), custom_call_target="tpu_custom_call" | custom-call | flops 2000000000 | bytes 10000 | tf_op jit(solution)/shard_map/dispatch/pallas_call | solution.py:253
  2.1 4.0 %collective-permute-start.2 = (bf16[24,1024]{1,0:T(8,128)(2,1)S(1)}, bf16[24,1024]{1,0:T(8,128)(2,1)S(1)}, u32[]{:S(2)}, u32[]{:S(2)}) collective-permute-start(bf16[24,1024]{1,0:T(8,128)(2,1)S(1)} %get-tuple-element.37), channel_id=1, source_target_pairs={{0,24},{4,28},{8,16},{12,20},{16,8},{20,12},{24,0},{28,4},{1,25},{... | collective-permute-start | bytes 147464 | tf_op jit(solution)/shard_map/ppermute | solution.py:220
  6.1 0.5 %collective-permute-start = (bf16[24,1024]{1,0:T(8,128)(2,1)S(1)}, bf16[24,1024]{1,0:T(8,128)(2,1)S(1)}, u32[]{:S(2)}, u32[]{:S(2)}) collective-permute-start(bf16[24,1024]{1,0:T(8,128)(2,1)S(1)} %get-tuple-element.32), channel_id=1, source_target_pairs={{0,8},{4,12},{8,0},{12,4},{16,24},{20,28},{24,16},{28,20},{1,9},{5... | collective-permute-start | bytes 147464 | tf_op jit(solution)/shard_map/ppermute | solution.py:220
  6.6 0.7 %collective-permute-start.5 = (bf16[3,48,2048]{2,1,0:T(8,128)(2,1)S(1)}, bf16[3,48,2048]{2,1,0:T(8,128)(2,1)S(1)}, u32[]{:S(2)}, u32[]{:S(2)}) collective-permute-start(bf16[3,48,2048]{2,1,0:T(8,128)(2,1)S(1)} %select.2), channel_id=1, source_target_pairs={{12,4},{28,20},{13,5},{29,21},{14,6},{30,22},{15,7},{31,23}} | collective-permute-start | bytes 1769480 | tf_op jit(solution)/shard_map/ppermute | solution.py:224
  7.4 0.2 collective-permute-start.1
  7.5 1.3 %collective-permute-start.10 = (bf16[3,96,2048]{2,1,0:T(8,128)(2,1)S(1)}, bf16[3,96,2048]{2,1,0:T(8,128)(2,1)S(1)}, u32[]{:S(2)}, u32[]{:S(2)}) collective-permute-start(bf16[3,96,2048]{2,1,0:T(8,128)(2,1)S(1)} %get-tuple-element.49), channel_id=1, source_target_pairs={{12,0},{28,16},{13,1},{29,17},{14,2},{30,18},{15,3},{31,19}} | collective-permute-start | bytes 3538952 | tf_op jit(solution)/shard_map/ppermute | solution.py:224
  8.8 1.3 %collective-permute-done = bf16[24,1024]{1,0:T(8,128)(2,1)S(1)} collective-permute-done((bf16[24,1024]{1,0:T(8,128)(2,1)S(1)}, bf16[24,1024]{1,0:T(8,128)(2,1)S(1)}, u32[]{:S(2)}, u32[]{:S(2)}) %collective-permute-start) | collective-permute-done | bytes 49184 | tf_op jit(solution)/shard_map/ppermute | solution.py:220
  10.2 1.3 %collective-permute-done.1 = bf16[24,1024]{1,0:T(8,128)(2,1)S(1)} collective-permute-done((bf16[24,1024]{1,0:T(8,128)(2,1)S(1)}, bf16[24,1024]{1,0:T(8,128)(2,1)S(1)}, u32[]{:S(2)}, u32[]{:S(2)}) %collective-permute-start.1) | collective-permute-done | bytes 49184 | tf_op jit(solution)/shard_map/ppermute | solution.py:220
  11.5 0.0 collective-permute-done.2
  11.5 0.1 collective-permute-start.3
  11.6 1.4 %collective-permute-done.3.other_ref = bf16[96,1024]{1,0:T(8,128)(2,1)S(1)} collective-permute-done((bf16[96,1024]{1,0:T(8,128)(2,1)S(1)}, bf16[96,1024]{1,0:T(8,128)(2,1)S(1)}, u32[]{:S(2)}, u32[]{:S(2)}) %collective-permute-start.3) | collective-permute-done | bytes 196640 | tf_op jit(solution)/shard_map/ppermute | solution.py:220
  13.0 0.9 %expert.1 = (f32[96,1024]{1,0:T(8,128)S(1)}, bf16[96,1024]{1,0:T(8,128)(2,1)S(1)}) custom-call(bf16[96,1024]{1,0:T(8,128)(2,1)S(1)} %constant_dynamic-update-slice_fusion.mine_ref, bf16[96,1024]{1,0:T(8,128)(2,1)S(1)} %collective-permute-done.3.other_ref, bf16[192,2048]{1,0:T(8,128)(2,1)S(1)} %copy-done, bf16[192,2048]{1,0:T(8,128)(2,1)S(1)} %copy-done.1, ...), custom_call_target="tpu_custom_call" | custom-call | bytes 10000 | tf_op jit(solution)/shard_map/expert/pallas_call | solution.py:281
  14.0 0.0 copy-start.4
  14.0 0.2 collective-permute-start.4
  14.2 1.3 %collective-permute-done.4 = bf16[96,1024]{1,0:T(8,128)(2,1)S(1)} collective-permute-done((bf16[96,1024]{1,0:T(8,128)(2,1)S(1)}, bf16[96,1024]{1,0:T(8,128)(2,1)S(1)}, u32[]{:S(2)}, u32[]{:S(2)}) %collective-permute-start.4) | collective-permute-done | bytes 196640 | tf_op jit(solution)/shard_map/ppermute | solution.py:220
  15.5 0.0 collective-permute-done.5.shared_ref
  15.5 0.7 %collective-permute-start.6 = (bf16[3,48,2048]{2,1,0:T(8,128)(2,1)S(1)}, bf16[3,48,2048]{2,1,0:T(8,128)(2,1)S(1)}, u32[]{:S(2)}, u32[]{:S(2)}) collective-permute-start(bf16[3,48,2048]{2,1,0:T(8,128)(2,1)S(1)} %collective-permute-done.5.shared_ref), channel_id=1, source_target_pairs={{4,5},{20,21},{5,4},{21,20},{6,7},{22,23},{7,6},{23,22}} | collective-permute-start | bytes 1769480 | tf_op jit(solution)/shard_map/ppermute | solution.py:232
  16.3 1.7 %collective-permute-start.9 = (bf16[24,1024]{1,0:T(8,128)(2,1)S(1)}, bf16[24,1024]{1,0:T(8,128)(2,1)S(1)}, u32[]{:S(2)}, u32[]{:S(2)}) collective-permute-start(bf16[24,1024]{1,0:T(8,128)(2,1)S(1)} %get-tuple-element.60), channel_id=1, source_target_pairs={{0,24},{4,28},{8,16},{12,20},{16,8},{20,12},{24,0},{28,4},{1,25},{... | collective-permute-start | bytes 147464 | tf_op jit(solution)/shard_map/ppermute | solution.py:220
  18.0 1.6 %collective-permute-start.8 = (bf16[24,1024]{1,0:T(8,128)(2,1)S(1)}, bf16[24,1024]{1,0:T(8,128)(2,1)S(1)}, u32[]{:S(2)}, u32[]{:S(2)}) collective-permute-start(bf16[24,1024]{1,0:T(8,128)(2,1)S(1)} %get-tuple-element.61), channel_id=1, source_target_pairs={{0,16},{4,20},{8,24},{12,28},{16,0},{20,4},{24,8},{28,12},{1,17},{... | collective-permute-start | bytes 147464 | tf_op jit(solution)/shard_map/ppermute | solution.py:220
  19.6 0.2 collective-permute-start.7
  19.8 0.7 %collective-permute-start.11 = (bf16[3,96,2048]{2,1,0:T(8,128)(2,1)S(1)}, bf16[3,96,2048]{2,1,0:T(8,128)(2,1)S(1)}, u32[]{:S(2)}, u32[]{:S(2)}) collective-permute-start(bf16[3,96,2048]{2,1,0:T(8,128)(2,1)S(1)} %get-tuple-element.58), channel_id=1, source_target_pairs={{12,8},{28,24},{13,9},{29,25},{14,10},{30,26},{15,11},{31,27}} | collective-permute-start | bytes 3538952 | tf_op jit(solution)/shard_map/ppermute | solution.py:224
  20.6 0.3 weigh.1.scaled_ref
  20.8 0.1 early.1.refs_5_
  20.9 1.0 %collective-permute-done.9.refs_3_ = bf16[24,1024]{1,0:T(8,128)(2,1)S(1)} collective-permute-done((bf16[24,1024]{1,0:T(8,128)(2,1)S(1)}, bf16[24,1024]{1,0:T(8,128)(2,1)S(1)}, u32[]{:S(2)}, u32[]{:S(2)}) %collective-permute-start.9) | collective-permute-done | bytes 49184 | tf_op jit(solution)/shard_map/ppermute | solution.py:220
  21.9 0.3 %collective-permute-done.8.refs_2_ = bf16[24,1024]{1,0:T(8,128)(2,1)S(1)} collective-permute-done((bf16[24,1024]{1,0:T(8,128)(2,1)S(1)}, bf16[24,1024]{1,0:T(8,128)(2,1)S(1)}, u32[]{:S(2)}, u32[]{:S(2)}) %collective-permute-start.8) | collective-permute-done | bytes 49184 | tf_op jit(solution)/shard_map/ppermute | solution.py:220
  22.3 2.0 %collective-permute-done.7.refs_1_ = bf16[24,1024]{1,0:T(8,128)(2,1)S(1)} collective-permute-done((bf16[24,1024]{1,0:T(8,128)(2,1)S(1)}, bf16[24,1024]{1,0:T(8,128)(2,1)S(1)}, u32[]{:S(2)}, u32[]{:S(2)}) %collective-permute-start.7) | collective-permute-done | bytes 49184 | tf_op jit(solution)/shard_map/ppermute | solution.py:220
  24.3 6.1 %collective-permute-done.10.refs_4_ = bf16[3,96,2048]{2,1,0:T(8,128)(2,1)S(1)} collective-permute-done((bf16[3,96,2048]{2,1,0:T(8,128)(2,1)S(1)}, bf16[3,96,2048]{2,1,0:T(8,128)(2,1)S(1)}, u32[]{:S(2)}, u32[]{:S(2)}) %collective-permute-start.10) | collective-permute-done | bytes 1179680 | tf_op jit(solution)/shard_map/ppermute | solution.py:224
  30.4 1.4 %combine.1 = (bf16[128,2048]{1,0:T(8,128)(2,1)}, bf16[3,96,2048]{2,1,0:T(8,128)(2,1)}) custom-call(bf16[2,128,256]{2,1,0:T(8,128)(2,1)S(1)} %weigh.1.scaled_ref, bf16[24,1024]{1,0:T(8,128)(2,1)S(1)} %get-tuple-element.50.refs_0_, bf16[24,1024]{1,0:T(8,128)(2,1)S(1)} %collective-permute-done.7.refs_1_, ...), custom_call_target="tpu_custom_call", output_to_operand_aliasing={{1}: (6, {})} | custom-call | flops 12300000256 | bytes 10000 | tf_op jit(solution)/shard_map/combine/pallas_call | solution.py:322
  31.8 0.1 late.1
  (23 shorter events, 0.1 us)
Async XLA Ops:
  0.6 0.7 %copy-start.3 = (s32[128,8]{0,1:T(8,128)S(1)}, s32[128,8]{0,1:T(8,128)}, u32[]{:S(2)}) copy-start(s32[128,8]{0,1:T(8,128)} %param.8) | copy-start | bytes 12292
  0.6 1.1 %copy-start.6 = (bf16[128,2048]{1,0:T(8,128)(2,1)S(1)}, bf16[128,2048]{1,0:T(8,128)(2,1)}, u32[]{:S(2)}) copy-start(bf16[128,2048]{1,0:T(8,128)(2,1)} %tok_ref.1) | copy-start | bytes 1572868
  1.7 4.9 %copy-start = (bf16[192,2048]{1,0:T(8,128)(2,1)S(1)}, bf16[192,2048]{1,0:T(8,128)(2,1)}, u32[]{:S(2)}) copy-start(bf16[192,2048]{1,0:T(8,128)(2,1)} %gate_ref.3) | copy-start | bytes 2359300
  1.7 4.9 %copy-start.1 = (bf16[192,2048]{1,0:T(8,128)(2,1)S(1)}, bf16[192,2048]{1,0:T(8,128)(2,1)}, u32[]{:S(2)}) copy-start(bf16[192,2048]{1,0:T(8,128)(2,1)} %up_ref.3) | copy-start | bytes 2359300
  1.7 4.9 %copy-start.2 = (bf16[192,2048]{1,0:T(8,128)(2,1)S(1)}, bf16[192,2048]{1,0:T(8,128)(2,1)}, u32[]{:S(2)}) copy-start(bf16[192,2048]{1,0:T(8,128)(2,1)} %down_ref.3) | copy-start | bytes 2359300
  1.7 4.9 %copy-start.7 = (s32[2,3,96]{2,0,1:T(2,128)S(1)}, s32[2,3,96]{2,0,1:T(2,128)}, u32[]{:S(2)}) copy-start(s32[2,3,96]{2,0,1:T(2,128)} %param.13) | copy-start | bytes 6916
  2.1 9.4 %collective-permute-start.2 = (bf16[24,1024]{1,0:T(8,128)(2,1)S(1)}, bf16[24,1024]{1,0:T(8,128)(2,1)S(1)}, u32[]{:S(2)}, u32[]{:S(2)}) collective-permute-start(bf16[24,1024]{1,0:T(8,128)(2,1)S(1)} %get-tuple-element.37), channel_id=1, source_target_pairs={{0,24},{4,28},{8,16},{12,20},{16,8},{20,12},{24,0},{28,4},{1,25},{... | collective-permute-start | bytes 147464 | tf_op jit(solution)/shard_map/ppermute | solution.py:220
  6.1 4.1 %collective-permute-start = (bf16[24,1024]{1,0:T(8,128)(2,1)S(1)}, bf16[24,1024]{1,0:T(8,128)(2,1)S(1)}, u32[]{:S(2)}, u32[]{:S(2)}) collective-permute-start(bf16[24,1024]{1,0:T(8,128)(2,1)S(1)} %get-tuple-element.32), channel_id=1, source_target_pairs={{0,8},{4,12},{8,0},{12,4},{16,24},{20,28},{24,16},{28,20},{1,9},{5... | collective-permute-start | bytes 147464 | tf_op jit(solution)/shard_map/ppermute | solution.py:220
  6.6 8.9 %collective-permute-start.5 = (bf16[3,48,2048]{2,1,0:T(8,128)(2,1)S(1)}, bf16[3,48,2048]{2,1,0:T(8,128)(2,1)S(1)}, u32[]{:S(2)}, u32[]{:S(2)}) collective-permute-start(bf16[3,48,2048]{2,1,0:T(8,128)(2,1)S(1)} %select.2), channel_id=1, source_target_pairs={{12,4},{28,20},{13,5},{29,21},{14,6},{30,22},{15,7},{31,23}} | collective-permute-start | bytes 1769480 | tf_op jit(solution)/shard_map/ppermute | solution.py:224
  7.4 4.2 %collective-permute-start.1 = (bf16[24,1024]{1,0:T(8,128)(2,1)S(1)}, bf16[24,1024]{1,0:T(8,128)(2,1)S(1)}, u32[]{:S(2)}, u32[]{:S(2)}) collective-permute-start(bf16[24,1024]{1,0:T(8,128)(2,1)S(1)} %get-tuple-element.37), channel_id=1, source_target_pairs={{0,16},{4,20},{8,24},{12,28},{16,0},{20,4},{24,8},{28,12},{1,17},{... | collective-permute-start | bytes 147464 | tf_op jit(solution)/shard_map/ppermute | solution.py:220
  7.5 22.9 %collective-permute-start.10 = (bf16[3,96,2048]{2,1,0:T(8,128)(2,1)S(1)}, bf16[3,96,2048]{2,1,0:T(8,128)(2,1)S(1)}, u32[]{:S(2)}, u32[]{:S(2)}) collective-permute-start(bf16[3,96,2048]{2,1,0:T(8,128)(2,1)S(1)} %get-tuple-element.49), channel_id=1, source_target_pairs={{12,0},{28,16},{13,1},{29,17},{14,2},{30,18},{15,3},{31,19}} | collective-permute-start | bytes 3538952 | tf_op jit(solution)/shard_map/ppermute | solution.py:224
  11.5 1.5 %collective-permute-start.3 = (bf16[96,1024]{1,0:T(8,128)(2,1)S(1)}, bf16[96,1024]{1,0:T(8,128)(2,1)S(1)}, u32[]{:S(2)}, u32[]{:S(2)}) collective-permute-start(bf16[96,1024]{1,0:T(8,128)(2,1)S(1)} %constant_dynamic-update-slice_fusion.mine_ref), channel_id=1, source_target_pairs={{0,4},{4,0},{8,12},{12,8},{16,20},{20,16},{24,28},{28,24},{1,5},{5... | collective-permute-start | bytes 589832 | tf_op jit(solution)/shard_map/ppermute | solution.py:220
  14.0 6.6 %copy-start.4 = (f32[128,8]{0,1:T(8,128)S(1)}, f32[128,8]{0,1:T(8,128)}, u32[]{:S(2)}) copy-start(f32[128,8]{0,1:T(8,128)} %param.9) | copy-start | bytes 12292
  14.0 1.5 %collective-permute-start.4 = (bf16[96,1024]{1,0:T(8,128)(2,1)S(1)}, bf16[96,1024]{1,0:T(8,128)(2,1)S(1)}, u32[]{:S(2)}, u32[]{:S(2)}) collective-permute-start(bf16[96,1024]{1,0:T(8,128)(2,1)S(1)} %get-tuple-element.38), channel_id=1, source_target_pairs={{0,4},{4,0},{8,12},{12,8},{16,20},{20,16},{24,28},{28,24},{1,5},{5... | collective-permute-start | bytes 589832 | tf_op jit(solution)/shard_map/ppermute | solution.py:220
  15.5 4.3 %collective-permute-start.6 = (bf16[3,48,2048]{2,1,0:T(8,128)(2,1)S(1)}, bf16[3,48,2048]{2,1,0:T(8,128)(2,1)S(1)}, u32[]{:S(2)}, u32[]{:S(2)}) collective-permute-start(bf16[3,48,2048]{2,1,0:T(8,128)(2,1)S(1)} %collective-permute-done.5.shared_ref), channel_id=1, source_target_pairs={{4,5},{20,21},{5,4},{21,20},{6,7},{22,23},{7,6},{23,22}} | collective-permute-start | bytes 1769480 | tf_op jit(solution)/shard_map/ppermute | solution.py:232
  16.3 5.6 %collective-permute-start.9 = (bf16[24,1024]{1,0:T(8,128)(2,1)S(1)}, bf16[24,1024]{1,0:T(8,128)(2,1)S(1)}, u32[]{:S(2)}, u32[]{:S(2)}) collective-permute-start(bf16[24,1024]{1,0:T(8,128)(2,1)S(1)} %get-tuple-element.60), channel_id=1, source_target_pairs={{0,24},{4,28},{8,16},{12,20},{16,8},{20,12},{24,0},{28,4},{1,25},{... | collective-permute-start | bytes 147464 | tf_op jit(solution)/shard_map/ppermute | solution.py:220
  18.0 4.3 %collective-permute-start.8 = (bf16[24,1024]{1,0:T(8,128)(2,1)S(1)}, bf16[24,1024]{1,0:T(8,128)(2,1)S(1)}, u32[]{:S(2)}, u32[]{:S(2)}) collective-permute-start(bf16[24,1024]{1,0:T(8,128)(2,1)S(1)} %get-tuple-element.61), channel_id=1, source_target_pairs={{0,16},{4,20},{8,24},{12,28},{16,0},{20,4},{24,8},{28,12},{1,17},{... | collective-permute-start | bytes 147464 | tf_op jit(solution)/shard_map/ppermute | solution.py:220
  19.6 4.7 %collective-permute-start.7 = (bf16[24,1024]{1,0:T(8,128)(2,1)S(1)}, bf16[24,1024]{1,0:T(8,128)(2,1)S(1)}, u32[]{:S(2)}, u32[]{:S(2)}) collective-permute-start(bf16[24,1024]{1,0:T(8,128)(2,1)S(1)} %get-tuple-element.62), channel_id=1, source_target_pairs={{0,8},{4,12},{8,0},{12,4},{16,24},{20,28},{24,16},{28,20},{1,9},{5... | collective-permute-start | bytes 147464 | tf_op jit(solution)/shard_map/ppermute | solution.py:220
  19.8 12.0 %collective-permute-start.11 = (bf16[3,96,2048]{2,1,0:T(8,128)(2,1)S(1)}, bf16[3,96,2048]{2,1,0:T(8,128)(2,1)S(1)}, u32[]{:S(2)}, u32[]{:S(2)}) collective-permute-start(bf16[3,96,2048]{2,1,0:T(8,128)(2,1)S(1)} %get-tuple-element.58), channel_id=1, source_target_pairs={{12,8},{28,24},{13,9},{29,25},{14,10},{30,26},{15,11},{31,27}} | collective-permute-start | bytes 3538952 | tf_op jit(solution)/shard_map/ppermute | solution.py:224
  30.4 1.4 %copy-start.5 = (f32[8,128]{1,0:T(8,128)S(1)}, f32[8,128]{1,0:T(8,128)}, u32[]{:S(2)}) copy-start(f32[8,128]{1,0:T(8,128)} %begin.1.begun_ref) | copy-start | bytes 12292

commit v25 on v24

--- a/solution.py
+++ b/solution.py
@@ -183,11 +183,13 @@
     rows = jnp.concatenate(rows, axis=0).astype(BF16)
     rows = jnp.concatenate([rows, rows], axis=0)
     copies = []
-    for side in range(2):
-        mixed = jnp.dot(scaled_ref[side], rows, preferred_element_type=F32)
-        columns = pl.ds(side * half, half)
-        mixed_ref[:, columns] = mixed.astype(BF16)
-        copy = pltpu.make_async_copy(mixed_ref.at[:, columns], out_ref.at[:, columns], sems.at[side])
+    tok = out_ref.shape[0] // 2
+    for n in range(2):
+        span = pl.ds(n * tok, tok)
+        for side in range(2):
+            mixed = jnp.dot(scaled_ref[side, span], rows, preferred_element_type=F32)
+            mixed_ref[span, side * half : (side + 1) * half] = mixed.astype(BF16)
+        copy = pltpu.make_async_copy(mixed_ref.at[span], out_ref.at[span], sems.at[n])
         copy.start()
         copies.append(copy)
     for copy in copies:

time: 32.2 us -> 32.4 us (level)
  no operation moved by 1% of the time
where the time goes in v25:
time: 32.4 us; the launch traced here: 31.8 us
  waiting for transfers between devices  14.9 us (46%)
  starting transfers between devices  11.9 us (37%)
  Pallas kernels  3.63 us (11%)
  between operations  0.81 us (2%)
  local copies, waits for them, and re-layouts  0.52 us (2%)
    ppermute x8, waiting for transfers between devices, send(): return lax.ppermute(block, 'expert', route)  8.78 us
    ppermute x8, starting transfers between devices, send(): return lax.ppermute(block, 'expert', route)  8.49 us
    ppermute x3, waiting for transfers between devices, migrate(): return lax.ppermute(block, 'expert', route)  6.13 us
    ppermute x3, starting transfers between devices, migrate(): return lax.ppermute(block, 'expert', route)  2.7 us
    pallas_call x1, Pallas kernels, on_device(): pl.pallas_call(combine_kernel, out_shape=[shape(tokens.shape[0], width),...  1.29 us
    pallas_call x1, Pallas kernels, on_device(): pl.pallas_call(expert_kernel, grid=(total // step,), out_shape=[shape(tot...  0.93 us
    ppermute x1, starting transfers between devices, swap(): return lax.ppermute(block, ('expert', 'replica'), route)  0.69 us
  transfers between devices with their start and end apart: 12, of which 8 were waited for; matrix products, arithmetic and copies ran while one was open for 0% of the time, Pallas kernels for 8%

profile of v25, /device:TPU:0, one launch (start us, length us, event | category | flops | bytes accessed | tf_op | source)
XLA Modules:
  0.0 31.8 jit_solution(4949949427362636177)
XLA Ops:
  0.6 0.6 %begin.1.begun_ref = f32[8,128]{1,0:T(8,128)} custom-call(), custom_call_target="tpu_custom_call" | custom-call | flops 5000000000 | bytes 10000 | tf_op jit(solution)/shard_map/begin/pallas_call | solution.py:247
  1.2 0.1 copy-done.3
  1.3 0.4 %copy-done.6 = bf16[128,2048]{1,0:T(8,128)(2,1)S(1)} copy-done((bf16[128,2048]{1,0:T(8,128)(2,1)S(1)}, bf16[128,2048]{1,0:T(8,128)(2,1)}, u32[]{:S(2)}) %copy-start.6) | copy-done | bytes 524312
  1.7 0.4 %dispatch.1 = (bf16[24,1024]{1,0:T(8,128)(2,1)S(1)}, bf16[24,1024]{1,0:T(8,128)(2,1)S(1)}) custom-call(s32[8,128]{1,0:T(8,128)S(1)} %bitcast.3, bf16[128,2048]{1,0:T(8,128)(2,1)S(1)} %copy-done.6), custom_call_target="tpu_custom_call" | custom-call | flops 2000000000 | bytes 10000 | tf_op jit(solution)/shard_map/dispatch/pallas_call | solution.py:255
  2.1 4.0 %collective-permute-start.2 = (bf16[24,1024]{1,0:T(8,128)(2,1)S(1)}, bf16[24,1024]{1,0:T(8,128)(2,1)S(1)}, u32[]{:S(2)}, u32[]{:S(2)}) collective-permute-start(bf16[24,1024]{1,0:T(8,128)(2,1)S(1)} %get-tuple-element.37), channel_id=1, source_target_pairs={{0,24},{4,28},{8,16},{12,20},{16,8},{20,12},{24,0},{28,4},{1,25},{... | collective-permute-start | bytes 147464 | tf_op jit(solution)/shard_map/ppermute | solution.py:222
  6.1 0.5 %collective-permute-start = (bf16[24,1024]{1,0:T(8,128)(2,1)S(1)}, bf16[24,1024]{1,0:T(8,128)(2,1)S(1)}, u32[]{:S(2)}, u32[]{:S(2)}) collective-permute-start(bf16[24,1024]{1,0:T(8,128)(2,1)S(1)} %get-tuple-element.32), channel_id=1, source_target_pairs={{0,8},{4,12},{8,0},{12,4},{16,24},{20,28},{24,16},{28,20},{1,9},{5... | collective-permute-start | bytes 147464 | tf_op jit(solution)/shard_map/ppermute | solution.py:222
  6.6 0.7 %collective-permute-start.5 = (bf16[3,48,2048]{2,1,0:T(8,128)(2,1)S(1)}, bf16[3,48,2048]{2,1,0:T(8,128)(2,1)S(1)}, u32[]{:S(2)}, u32[]{:S(2)}) collective-permute-start(bf16[3,48,2048]{2,1,0:T(8,128)(2,1)S(1)} %select.2), channel_id=1, source_target_pairs={{12,4},{28,20},{13,5},{29,21},{14,6},{30,22},{15,7},{31,23}} | collective-permute-start | bytes 1769480 | tf_op jit(solution)/shard_map/ppermute | solution.py:226
  7.4 0.2 collective-permute-start.1
  7.5 1.3 %collective-permute-start.10 = (bf16[3,96,2048]{2,1,0:T(8,128)(2,1)S(1)}, bf16[3,96,2048]{2,1,0:T(8,128)(2,1)S(1)}, u32[]{:S(2)}, u32[]{:S(2)}) collective-permute-start(bf16[3,96,2048]{2,1,0:T(8,128)(2,1)S(1)} %get-tuple-element.49), channel_id=1, source_target_pairs={{12,0},{28,16},{13,1},{29,17},{14,2},{30,18},{15,3},{31,19}} | collective-permute-start | bytes 3538952 | tf_op jit(solution)/shard_map/ppermute | solution.py:226
  8.8 1.3 %collective-permute-done = bf16[24,1024]{1,0:T(8,128)(2,1)S(1)} collective-permute-done((bf16[24,1024]{1,0:T(8,128)(2,1)S(1)}, bf16[24,1024]{1,0:T(8,128)(2,1)S(1)}, u32[]{:S(2)}, u32[]{:S(2)}) %collective-permute-start) | collective-permute-done | bytes 49184 | tf_op jit(solution)/shard_map/ppermute | solution.py:222
  10.2 1.3 %collective-permute-done.1 = bf16[24,1024]{1,0:T(8,128)(2,1)S(1)} collective-permute-done((bf16[24,1024]{1,0:T(8,128)(2,1)S(1)}, bf16[24,1024]{1,0:T(8,128)(2,1)S(1)}, u32[]{:S(2)}, u32[]{:S(2)}) %collective-permute-start.1) | collective-permute-done | bytes 49184 | tf_op jit(solution)/shard_map/ppermute | solution.py:222
  11.5 0.0 collective-permute-done.2
  11.5 0.1 collective-permute-start.3
  11.6 1.4 %collective-permute-done.3.other_ref = bf16[96,1024]{1,0:T(8,128)(2,1)S(1)} collective-permute-done((bf16[96,1024]{1,0:T(8,128)(2,1)S(1)}, bf16[96,1024]{1,0:T(8,128)(2,1)S(1)}, u32[]{:S(2)}, u32[]{:S(2)}) %collective-permute-start.3) | collective-permute-done | bytes 196640 | tf_op jit(solution)/shard_map/ppermute | solution.py:222
  13.0 0.9 %expert.1 = (f32[96,1024]{1,0:T(8,128)S(1)}, bf16[96,1024]{1,0:T(8,128)(2,1)S(1)}) custom-call(bf16[96,1024]{1,0:T(8,128)(2,1)S(1)} %constant_dynamic-update-slice_fusion.mine_ref, bf16[96,1024]{1,0:T(8,128)(2,1)S(1)} %collective-permute-done.3.other_ref, bf16[192,2048]{1,0:T(8,128)(2,1)S(1)} %copy-done, bf16[192,2048]{1,0:T(8,128)(2,1)S(1)} %copy-done.1, ...), custom_call_target="tpu_custom_call" | custom-call | bytes 10000 | tf_op jit(solution)/shard_map/expert/pallas_call | solution.py:283
  14.0 0.0 copy-start.4
  14.0 0.2 collective-permute-start.4
  14.2 1.3 %collective-permute-done.4 = bf16[96,1024]{1,0:T(8,128)(2,1)S(1)} collective-permute-done((bf16[96,1024]{1,0:T(8,128)(2,1)S(1)}, bf16[96,1024]{1,0:T(8,128)(2,1)S(1)}, u32[]{:S(2)}, u32[]{:S(2)}) %collective-permute-start.4) | collective-permute-done | bytes 196640 | tf_op jit(solution)/shard_map/ppermute | solution.py:222
  15.5 0.0 collective-permute-done.5.shared_ref
  15.5 0.7 %collective-permute-start.6 = (bf16[3,48,2048]{2,1,0:T(8,128)(2,1)S(1)}, bf16[3,48,2048]{2,1,0:T(8,128)(2,1)S(1)}, u32[]{:S(2)}, u32[]{:S(2)}) collective-permute-start(bf16[3,48,2048]{2,1,0:T(8,128)(2,1)S(1)} %collective-permute-done.5.shared_ref), channel_id=1, source_target_pairs={{4,5},{20,21},{5,4},{21,20},{6,7},{22,23},{7,6},{23,22}} | collective-permute-start | bytes 1769480 | tf_op jit(solution)/shard_map/ppermute | solution.py:234
  16.3 1.7 %collective-permute-start.9 = (bf16[24,1024]{1,0:T(8,128)(2,1)S(1)}, bf16[24,1024]{1,0:T(8,128)(2,1)S(1)}, u32[]{:S(2)}, u32[]{:S(2)}) collective-permute-start(bf16[24,1024]{1,0:T(8,128)(2,1)S(1)} %get-tuple-element.60), channel_id=1, source_target_pairs={{0,24},{4,28},{8,16},{12,20},{16,8},{20,12},{24,0},{28,4},{1,25},{... | collective-permute-start | bytes 147464 | tf_op jit(solution)/shard_map/ppermute | solution.py:222
  18.0 1.6 %collective-permute-start.8 = (bf16[24,1024]{1,0:T(8,128)(2,1)S(1)}, bf16[24,1024]{1,0:T(8,128)(2,1)S(1)}, u32[]{:S(2)}, u32[]{:S(2)}) collective-permute-start(bf16[24,1024]{1,0:T(8,128)(2,1)S(1)} %get-tuple-element.61), channel_id=1, source_target_pairs={{0,16},{4,20},{8,24},{12,28},{16,0},{20,4},{24,8},{28,12},{1,17},{... | collective-permute-start | bytes 147464 | tf_op jit(solution)/shard_map/ppermute | solution.py:222
  19.6 0.2 collective-permute-start.7
  19.8 0.7 %collective-permute-start.11 = (bf16[3,96,2048]{2,1,0:T(8,128)(2,1)S(1)}, bf16[3,96,2048]{2,1,0:T(8,128)(2,1)S(1)}, u32[]{:S(2)}, u32[]{:S(2)}) collective-permute-start(bf16[3,96,2048]{2,1,0:T(8,128)(2,1)S(1)} %get-tuple-element.58), channel_id=1, source_target_pairs={{12,8},{28,24},{13,9},{29,25},{14,10},{30,26},{15,11},{31,27}} | collective-permute-start | bytes 3538952 | tf_op jit(solution)/shard_map/ppermute | solution.py:226
  20.6 0.3 weigh.1.scaled_ref
  20.8 0.1 early.1.refs_5_
  20.9 1.0 %collective-permute-done.9.refs_3_ = bf16[24,1024]{1,0:T(8,128)(2,1)S(1)} collective-permute-done((bf16[24,1024]{1,0:T(8,128)(2,1)S(1)}, bf16[24,1024]{1,0:T(8,128)(2,1)S(1)}, u32[]{:S(2)}, u32[]{:S(2)}) %collective-permute-start.9) | collective-permute-done | bytes 49184 | tf_op jit(solution)/shard_map/ppermute | solution.py:222
  21.9 0.3 %collective-permute-done.8.refs_2_ = bf16[24,1024]{1,0:T(8,128)(2,1)S(1)} collective-permute-done((bf16[24,1024]{1,0:T(8,128)(2,1)S(1)}, bf16[24,1024]{1,0:T(8,128)(2,1)S(1)}, u32[]{:S(2)}, u32[]{:S(2)}) %collective-permute-start.8) | collective-permute-done | bytes 49184 | tf_op jit(solution)/shard_map/ppermute | solution.py:222
  22.3 2.0 %collective-permute-done.7.refs_1_ = bf16[24,1024]{1,0:T(8,128)(2,1)S(1)} collective-permute-done((bf16[24,1024]{1,0:T(8,128)(2,1)S(1)}, bf16[24,1024]{1,0:T(8,128)(2,1)S(1)}, u32[]{:S(2)}, u32[]{:S(2)}) %collective-permute-start.7) | collective-permute-done | bytes 49184 | tf_op jit(solution)/shard_map/ppermute | solution.py:222
  24.3 6.1 %collective-permute-done.10.refs_4_ = bf16[3,96,2048]{2,1,0:T(8,128)(2,1)S(1)} collective-permute-done((bf16[3,96,2048]{2,1,0:T(8,128)(2,1)S(1)}, bf16[3,96,2048]{2,1,0:T(8,128)(2,1)S(1)}, u32[]{:S(2)}, u32[]{:S(2)}) %collective-permute-start.10) | collective-permute-done | bytes 1179680 | tf_op jit(solution)/shard_map/ppermute | solution.py:226
  30.4 1.3 %combine.1 = (bf16[128,2048]{1,0:T(8,128)(2,1)}, bf16[3,96,2048]{2,1,0:T(8,128)(2,1)}) custom-call(bf16[2,128,256]{2,1,0:T(8,128)(2,1)S(1)} %weigh.1.scaled_ref, bf16[24,1024]{1,0:T(8,128)(2,1)S(1)} %get-tuple-element.50.refs_0_, bf16[24,1024]{1,0:T(8,128)(2,1)S(1)} %collective-permute-done.7.refs_1_, ...), custom_call_target="tpu_custom_call", output_to_operand_aliasing={{1}: (6, {})} | custom-call | flops 12300000256 | bytes 10000 | tf_op jit(solution)/shard_map/combine/pallas_call | solution.py:324
  31.7 0.1 late.1
  (23 shorter events, 0.1 us)
Async XLA Ops:
  0.6 0.7 %copy-start.3 = (s32[128,8]{0,1:T(8,128)S(1)}, s32[128,8]{0,1:T(8,128)}, u32[]{:S(2)}) copy-start(s32[128,8]{0,1:T(8,128)} %param.8) | copy-start | bytes 12292
  0.6 1.1 %copy-start.6 = (bf16[128,2048]{1,0:T(8,128)(2,1)S(1)}, bf16[128,2048]{1,0:T(8,128)(2,1)}, u32[]{:S(2)}) copy-start(bf16[128,2048]{1,0:T(8,128)(2,1)} %tok_ref.1) | copy-start | bytes 1572868
  1.7 4.9 %copy-start = (bf16[192,2048]{1,0:T(8,128)(2,1)S(1)}, bf16[192,2048]{1,0:T(8,128)(2,1)}, u32[]{:S(2)}) copy-start(bf16[192,2048]{1,0:T(8,128)(2,1)} %gate_ref.3) | copy-start | bytes 2359300
  1.7 4.9 %copy-start.1 = (bf16[192,2048]{1,0:T(8,128)(2,1)S(1)}, bf16[192,2048]{1,0:T(8,128)(2,1)}, u32[]{:S(2)}) copy-start(bf16[192,2048]{1,0:T(8,128)(2,1)} %up_ref.3) | copy-start | bytes 2359300
  1.7 4.9 %copy-start.2 = (bf16[192,2048]{1,0:T(8,128)(2,1)S(1)}, bf16[192,2048]{1,0:T(8,128)(2,1)}, u32[]{:S(2)}) copy-start(bf16[192,2048]{1,0:T(8,128)(2,1)} %down_ref.3) | copy-start | bytes 2359300
  1.7 4.9 %copy-start.7 = (s32[2,3,96]{2,0,1:T(2,128)S(1)}, s32[2,3,96]{2,0,1:T(2,128)}, u32[]{:S(2)}) copy-start(s32[2,3,96]{2,0,1:T(2,128)} %param.13) | copy-start | bytes 6916
  2.1 9.4 %collective-permute-start.2 = (bf16[24,1024]{1,0:T(8,128)(2,1)S(1)}, bf16[24,1024]{1,0:T(8,128)(2,1)S(1)}, u32[]{:S(2)}, u32[]{:S(2)}) collective-permute-start(bf16[24,1024]{1,0:T(8,128)(2,1)S(1)} %get-tuple-element.37), channel_id=1, source_target_pairs={{0,24},{4,28},{8,16},{12,20},{16,8},{20,12},{24,0},{28,4},{1,25},{... | collective-permute-start | bytes 147464 | tf_op jit(solution)/shard_map/ppermute | solution.py:222
  6.1 4.1 %collective-permute-start = (bf16[24,1024]{1,0:T(8,128)(2,1)S(1)}, bf16[24,1024]{1,0:T(8,128)(2,1)S(1)}, u32[]{:S(2)}, u32[]{:S(2)}) collective-permute-start(bf16[24,1024]{1,0:T(8,128)(2,1)S(1)} %get-tuple-element.32), channel_id=1, source_target_pairs={{0,8},{4,12},{8,0},{12,4},{16,24},{20,28},{24,16},{28,20},{1,9},{5... | collective-permute-start | bytes 147464 | tf_op jit(solution)/shard_map/ppermute | solution.py:222
  6.6 8.9 %collective-permute-start.5 = (bf16[3,48,2048]{2,1,0:T(8,128)(2,1)S(1)}, bf16[3,48,2048]{2,1,0:T(8,128)(2,1)S(1)}, u32[]{:S(2)}, u32[]{:S(2)}) collective-permute-start(bf16[3,48,2048]{2,1,0:T(8,128)(2,1)S(1)} %select.2), channel_id=1, source_target_pairs={{12,4},{28,20},{13,5},{29,21},{14,6},{30,22},{15,7},{31,23}} | collective-permute-start | bytes 1769480 | tf_op jit(solution)/shard_map/ppermute | solution.py:226
  7.4 4.2 %collective-permute-start.1 = (bf16[24,1024]{1,0:T(8,128)(2,1)S(1)}, bf16[24,1024]{1,0:T(8,128)(2,1)S(1)}, u32[]{:S(2)}, u32[]{:S(2)}) collective-permute-start(bf16[24,1024]{1,0:T(8,128)(2,1)S(1)} %get-tuple-element.37), channel_id=1, source_target_pairs={{0,16},{4,20},{8,24},{12,28},{16,0},{20,4},{24,8},{28,12},{1,17},{... | collective-permute-start | bytes 147464 | tf_op jit(solution)/shard_map/ppermute | solution.py:222
  7.5 22.9 %collective-permute-start.10 = (bf16[3,96,2048]{2,1,0:T(8,128)(2,1)S(1)}, bf16[3,96,2048]{2,1,0:T(8,128)(2,1)S(1)}, u32[]{:S(2)}, u32[]{:S(2)}) collective-permute-start(bf16[3,96,2048]{2,1,0:T(8,128)(2,1)S(1)} %get-tuple-element.49), channel_id=1, source_target_pairs={{12,0},{28,16},{13,1},{29,17},{14,2},{30,18},{15,3},{31,19}} | collective-permute-start | bytes 3538952 | tf_op jit(solution)/shard_map/ppermute | solution.py:226
  11.5 1.5 %collective-permute-start.3 = (bf16[96,1024]{1,0:T(8,128)(2,1)S(1)}, bf16[96,1024]{1,0:T(8,128)(2,1)S(1)}, u32[]{:S(2)}, u32[]{:S(2)}) collective-permute-start(bf16[96,1024]{1,0:T(8,128)(2,1)S(1)} %constant_dynamic-update-slice_fusion.mine_ref), channel_id=1, source_target_pairs={{0,4},{4,0},{8,12},{12,8},{16,20},{20,16},{24,28},{28,24},{1,5},{5... | collective-permute-start | bytes 589832 | tf_op jit(solution)/shard_map/ppermute | solution.py:222
  14.0 6.6 %copy-start.4 = (f32[128,8]{0,1:T(8,128)S(1)}, f32[128,8]{0,1:T(8,128)}, u32[]{:S(2)}) copy-start(f32[128,8]{0,1:T(8,128)} %param.9) | copy-start | bytes 12292
  14.0 1.5 %collective-permute-start.4 = (bf16[96,1024]{1,0:T(8,128)(2,1)S(1)}, bf16[96,1024]{1,0:T(8,128)(2,1)S(1)}, u32[]{:S(2)}, u32[]{:S(2)}) collective-permute-start(bf16[96,1024]{1,0:T(8,128)(2,1)S(1)} %get-tuple-element.38), channel_id=1, source_target_pairs={{0,4},{4,0},{8,12},{12,8},{16,20},{20,16},{24,28},{28,24},{1,5},{5... | collective-permute-start | bytes 589832 | tf_op jit(solution)/shard_map/ppermute | solution.py:222
  15.5 4.3 %collective-permute-start.6 = (bf16[3,48,2048]{2,1,0:T(8,128)(2,1)S(1)}, bf16[3,48,2048]{2,1,0:T(8,128)(2,1)S(1)}, u32[]{:S(2)}, u32[]{:S(2)}) collective-permute-start(bf16[3,48,2048]{2,1,0:T(8,128)(2,1)S(1)} %collective-permute-done.5.shared_ref), channel_id=1, source_target_pairs={{4,5},{20,21},{5,4},{21,20},{6,7},{22,23},{7,6},{23,22}} | collective-permute-start | bytes 1769480 | tf_op jit(solution)/shard_map/ppermute | solution.py:234
  16.3 5.6 %collective-permute-start.9 = (bf16[24,1024]{1,0:T(8,128)(2,1)S(1)}, bf16[24,1024]{1,0:T(8,128)(2,1)S(1)}, u32[]{:S(2)}, u32[]{:S(2)}) collective-permute-start(bf16[24,1024]{1,0:T(8,128)(2,1)S(1)} %get-tuple-element.60), channel_id=1, source_target_pairs={{0,24},{4,28},{8,16},{12,20},{16,8},{20,12},{24,0},{28,4},{1,25},{... | collective-permute-start | bytes 147464 | tf_op jit(solution)/shard_map/ppermute | solution.py:222
  18.0 4.3 %collective-permute-start.8 = (bf16[24,1024]{1,0:T(8,128)(2,1)S(1)}, bf16[24,1024]{1,0:T(8,128)(2,1)S(1)}, u32[]{:S(2)}, u32[]{:S(2)}) collective-permute-start(bf16[24,1024]{1,0:T(8,128)(2,1)S(1)} %get-tuple-element.61), channel_id=1, source_target_pairs={{0,16},{4,20},{8,24},{12,28},{16,0},{20,4},{24,8},{28,12},{1,17},{... | collective-permute-start | bytes 147464 | tf_op jit(solution)/shard_map/ppermute | solution.py:222
  19.6 4.7 %collective-permute-start.7 = (bf16[24,1024]{1,0:T(8,128)(2,1)S(1)}, bf16[24,1024]{1,0:T(8,128)(2,1)S(1)}, u32[]{:S(2)}, u32[]{:S(2)}) collective-permute-start(bf16[24,1024]{1,0:T(8,128)(2,1)S(1)} %get-tuple-element.62), channel_id=1, source_target_pairs={{0,8},{4,12},{8,0},{12,4},{16,24},{20,28},{24,16},{28,20},{1,9},{5... | collective-permute-start | bytes 147464 | tf_op jit(solution)/shard_map/ppermute | solution.py:222
  19.8 11.9 %collective-permute-start.11 = (bf16[3,96,2048]{2,1,0:T(8,128)(2,1)S(1)}, bf16[3,96,2048]{2,1,0:T(8,128)(2,1)S(1)}, u32[]{:S(2)}, u32[]{:S(2)}) collective-permute-start(bf16[3,96,2048]{2,1,0:T(8,128)(2,1)S(1)} %get-tuple-element.58), channel_id=1, source_target_pairs={{12,8},{28,24},{13,9},{29,25},{14,10},{30,26},{15,11},{31,27}} | collective-permute-start | bytes 3538952 | tf_op jit(solution)/shard_map/ppermute | solution.py:226
  30.4 1.3 %copy-start.5 = (f32[8,128]{1,0:T(8,128)S(1)}, f32[8,128]{1,0:T(8,128)}, u32[]{:S(2)}) copy-start(f32[8,128]{1,0:T(8,128)} %begin.1.begun_ref) | copy-start | bytes 12292

commit v26 on v24

--- a/solution.py
+++ b/solution.py
@@ -268,7 +268,7 @@
     after, _ = lax.optimization_barrier((parcels, chosen[0]))
     mine = [parcels[0]]
     for j, k in pairs[1:]:
-        mine.append(send(parcels[j] if k else after[j], j, k))
+        mine.append(send(after[j] if j else parcels[j], j, k))
     shared = migrate(chosen[0], 1)
     straight = migrate(chosen[1], 0)
     mine = jnp.concatenate(mine, axis=0)

time: 32.2 us -> 34.4 us (1.068)
  the two profiles are of different devices: /device:TPU:0 before, /device:TPU:1 now
where the time goes in v26:
time: 34.4 us; the launch traced here: 34.2 us
  starting transfers between devices  15.5 us (45%)
  waiting for transfers between devices  12.9 us (38%)
  Pallas kernels  4.42 us (13%)
  between operations  0.84 us (2%)
  local copies, waits for them, and re-layouts  0.52 us (2%)
    ppermute x8, starting transfers between devices, send(): return lax.ppermute(block, 'expert', route)  9.53 us
    ppermute x8, waiting for transfers between devices, send(): return lax.ppermute(block, 'expert', route)  5.11 us
    ppermute x1, waiting for transfers between devices, swap(): return lax.ppermute(block, ('expert', 'replica'), route)  4.92 us
    ppermute x1, starting transfers between devices, swap(): return lax.ppermute(block, ('expert', 'replica'), route)  3.19 us
    ppermute x3, waiting for transfers between devices, migrate(): return lax.ppermute(block, 'expert', route)  2.9 us
    ppermute x3, starting transfers between devices, migrate(): return lax.ppermute(block, 'expert', route)  2.74 us
    pallas_call x1, Pallas kernels, on_device(): pl.pallas_call(combine_kernel, out_shape=[shape(tokens.shape[0], width),...  1.08 us
    pallas_call x1, Pallas kernels, on_device(): pl.pallas_call(early_kernel, out_shape=shape(3, most, width), in_specs=[H...  1.07 us
  transfers between devices with their start and end apart: 12, of which 6 were waited for; matrix products, arithmetic and copies ran while one was open for 0% of the time, Pallas kernels for 10%

profile of v26, /device:TPU:1, one launch (start us, length us, event | category | flops | bytes accessed | tf_op | source)
XLA Modules:
  0.0 34.2 jit_solution(5813036686191187146)
XLA Ops:
  0.6 0.6 %begin.1.begun_ref = f32[8,128]{1,0:T(8,128)} custom-call(), custom_call_target="tpu_custom_call" | custom-call | flops 5000000000 | bytes 10000 | tf_op jit(solution)/shard_map/begin/pallas_call | solution.py:245
  1.2 0.1 copy-done.3
  1.3 0.4 %copy-done.6 = bf16[128,2048]{1,0:T(8,128)(2,1)S(1)} copy-done((bf16[128,2048]{1,0:T(8,128)(2,1)S(1)}, bf16[128,2048]{1,0:T(8,128)(2,1)}, u32[]{:S(2)}) %copy-start.6) | copy-done | bytes 524312
  1.7 0.4 %dispatch.1 = (bf16[24,1024]{1,0:T(8,128)(2,1)S(1)}, bf16[24,1024]{1,0:T(8,128)(2,1)S(1)}) custom-call(s32[8,128]{1,0:T(8,128)S(1)} %bitcast.3, bf16[128,2048]{1,0:T(8,128)(2,1)S(1)} %copy-done.6), custom_call_target="tpu_custom_call" | custom-call | flops 2000000000 | bytes 10000 | tf_op jit(solution)/shard_map/dispatch/pallas_call | solution.py:253
  2.1 2.1 %collective-permute-start = (bf16[24,1024]{1,0:T(8,128)(2,1)S(1)}, bf16[24,1024]{1,0:T(8,128)(2,1)S(1)}, u32[]{:S(2)}, u32[]{:S(2)}) collective-permute-start(bf16[24,1024]{1,0:T(8,128)(2,1)S(1)} %get-tuple-element.32), channel_id=1, source_target_pairs={{0,8},{4,12},{8,0},{12,4},{16,24},{20,28},{24,16},{28,20},{1,9},{5... | collective-permute-start | bytes 147464 | tf_op jit(solution)/shard_map/ppermute | solution.py:220
  4.3 2.7 %collective-permute-start.2 = (bf16[24,1024]{1,0:T(8,128)(2,1)S(1)}, bf16[24,1024]{1,0:T(8,128)(2,1)S(1)}, u32[]{:S(2)}, u32[]{:S(2)}) collective-permute-start(bf16[24,1024]{1,0:T(8,128)(2,1)S(1)} %get-tuple-element.37), channel_id=1, source_target_pairs={{0,24},{4,28},{8,16},{12,20},{16,8},{20,12},{24,0},{28,4},{1,25},{... | collective-permute-start | bytes 147464 | tf_op jit(solution)/shard_map/ppermute | solution.py:220
  7.0 0.2 collective-permute-start.1
  7.2 1.3 %collective-permute-start.5 = (bf16[3,48,2048]{2,1,0:T(8,128)(2,1)S(1)}, bf16[3,48,2048]{2,1,0:T(8,128)(2,1)S(1)}, u32[]{:S(2)}, u32[]{:S(2)}) collective-permute-start(bf16[3,48,2048]{2,1,0:T(8,128)(2,1)S(1)} %select.2), channel_id=1, source_target_pairs={{12,4},{28,20},{13,5},{29,21},{14,6},{30,22},{15,7},{31,23}} | collective-permute-start | bytes 1769480 | tf_op jit(solution)/shard_map/ppermute | solution.py:224
  8.6 0.7 %collective-permute-start.10 = (bf16[3,96,2048]{2,1,0:T(8,128)(2,1)S(1)}, bf16[3,96,2048]{2,1,0:T(8,128)(2,1)S(1)}, u32[]{:S(2)}, u32[]{:S(2)}) collective-permute-start(bf16[3,96,2048]{2,1,0:T(8,128)(2,1)S(1)} %get-tuple-element.49), channel_id=1, source_target_pairs={{12,0},{28,16},{13,1},{29,17},{14,2},{30,18},{15,3},{31,19}} | collective-permute-start | bytes 3538952 | tf_op jit(solution)/shard_map/ppermute | solution.py:224
  9.3 0.0 collective-permute-done
  9.3 0.8 %collective-permute-done.1 = bf16[24,1024]{1,0:T(8,128)(2,1)S(1)} collective-permute-done((bf16[24,1024]{1,0:T(8,128)(2,1)S(1)}, bf16[24,1024]{1,0:T(8,128)(2,1)S(1)}, u32[]{:S(2)}, u32[]{:S(2)}) %collective-permute-start.1) | collective-permute-done | bytes 49184 | tf_op jit(solution)/shard_map/ppermute | solution.py:220
  10.1 0.0 collective-permute-done.2
  10.1 1.3 %collective-permute-start.3 = (bf16[96,1024]{1,0:T(8,128)(2,1)S(1)}, bf16[96,1024]{1,0:T(8,128)(2,1)S(1)}, u32[]{:S(2)}, u32[]{:S(2)}) collective-permute-start(bf16[96,1024]{1,0:T(8,128)(2,1)S(1)} %constant_dynamic-update-slice_fusion.mine_ref), channel_id=1, source_target_pairs={{0,4},{4,0},{8,12},{12,8},{16,20},{20,16},{24,28},{28,24},{1,5},{5... | collective-permute-start | bytes 589832 | tf_op jit(solution)/shard_map/ppermute | solution.py:220
  11.4 1.1 %collective-permute-done.3.other_ref = bf16[96,1024]{1,0:T(8,128)(2,1)S(1)} collective-permute-done((bf16[96,1024]{1,0:T(8,128)(2,1)S(1)}, bf16[96,1024]{1,0:T(8,128)(2,1)S(1)}, u32[]{:S(2)}, u32[]{:S(2)}) %collective-permute-start.3) | collective-permute-done | bytes 196640 | tf_op jit(solution)/shard_map/ppermute | solution.py:220
  12.5 0.9 %expert.1 = (f32[96,1024]{1,0:T(8,128)S(1)}, bf16[96,1024]{1,0:T(8,128)(2,1)S(1)}) custom-call(bf16[96,1024]{1,0:T(8,128)(2,1)S(1)} %constant_dynamic-update-slice_fusion.mine_ref, bf16[96,1024]{1,0:T(8,128)(2,1)S(1)} %collective-permute-done.3.other_ref, bf16[192,2048]{1,0:T(8,128)(2,1)S(1)} %copy-done, bf16[192,2048]{1,0:T(8,128)(2,1)S(1)} %copy-done.1, ...), custom_call_target="tpu_custom_call" | custom-call | bytes 10000 | tf_op jit(solution)/shard_map/expert/pallas_call | solution.py:281
  13.4 0.0 copy-start.4
  13.5 0.4 %collective-permute-start.4 = (bf16[96,1024]{1,0:T(8,128)(2,1)S(1)}, bf16[96,1024]{1,0:T(8,128)(2,1)S(1)}, u32[]{:S(2)}, u32[]{:S(2)}) collective-permute-start(bf16[96,1024]{1,0:T(8,128)(2,1)S(1)} %get-tuple-element.38), channel_id=1, source_target_pairs={{0,4},{4,0},{8,12},{12,8},{16,20},{20,16},{24,28},{28,24},{1,5},{5... | collective-permute-start | bytes 589832 | tf_op jit(solution)/shard_map/ppermute | solution.py:220
  13.9 1.1 %collective-permute-done.4 = bf16[96,1024]{1,0:T(8,128)(2,1)S(1)} collective-permute-done((bf16[96,1024]{1,0:T(8,128)(2,1)S(1)}, bf16[96,1024]{1,0:T(8,128)(2,1)S(1)}, u32[]{:S(2)}, u32[]{:S(2)}) %collective-permute-start.4) | collective-permute-done | bytes 196640 | tf_op jit(solution)/shard_map/ppermute | solution.py:220
  15.0 2.9 %collective-permute-done.5.shared_ref = bf16[3,48,2048]{2,1,0:T(8,128)(2,1)S(1)} collective-permute-done((bf16[3,48,2048]{2,1,0:T(8,128)(2,1)S(1)}, bf16[3,48,2048]{2,1,0:T(8,128)(2,1)S(1)}, u32[]{:S(2)}, u32[]{:S(2)}) %collective-permute-start.5) | collective-permute-done | bytes 589856 | tf_op jit(solution)/shard_map/ppermute | solution.py:224
  17.9 3.2 %collective-permute-start.6 = (bf16[3,48,2048]{2,1,0:T(8,128)(2,1)S(1)}, bf16[3,48,2048]{2,1,0:T(8,128)(2,1)S(1)}, u32[]{:S(2)}, u32[]{:S(2)}) collective-permute-start(bf16[3,48,2048]{2,1,0:T(8,128)(2,1)S(1)} %collective-permute-done.5.shared_ref), channel_id=1, source_target_pairs={{4,5},{20,21},{5,4},{21,20},{6,7},{22,23},{7,6},{23,22}} | collective-permute-start | bytes 1769480 | tf_op jit(solution)/shard_map/ppermute | solution.py:232
  21.1 0.1 collective-permute-start.9
  21.2 1.3 %collective-permute-start.8 = (bf16[24,1024]{1,0:T(8,128)(2,1)S(1)}, bf16[24,1024]{1,0:T(8,128)(2,1)S(1)}, u32[]{:S(2)}, u32[]{:S(2)}) collective-permute-start(bf16[24,1024]{1,0:T(8,128)(2,1)S(1)} %get-tuple-element.61), channel_id=1, source_target_pairs={{0,16},{4,20},{8,24},{12,28},{16,0},{20,4},{24,8},{28,12},{1,17},{... | collective-permute-start | bytes 147464 | tf_op jit(solution)/shard_map/ppermute | solution.py:220
  22.5 1.3 %collective-permute-start.7 = (bf16[24,1024]{1,0:T(8,128)(2,1)S(1)}, bf16[24,1024]{1,0:T(8,128)(2,1)S(1)}, u32[]{:S(2)}, u32[]{:S(2)}) collective-permute-start(bf16[24,1024]{1,0:T(8,128)(2,1)S(1)} %get-tuple-element.62), channel_id=1, source_target_pairs={{0,8},{4,12},{8,0},{12,4},{16,24},{20,28},{24,16},{28,20},{1,9},{5... | collective-permute-start | bytes 147464 | tf_op jit(solution)/shard_map/ppermute | solution.py:220
  23.8 4.9 %collective-permute-done.6.swapped_ref = bf16[3,48,2048]{2,1,0:T(8,128)(2,1)S(1)} collective-permute-done((bf16[3,48,2048]{2,1,0:T(8,128)(2,1)S(1)}, bf16[3,48,2048]{2,1,0:T(8,128)(2,1)S(1)}, u32[]{:S(2)}, u32[]{:S(2)}) %collective-permute-start.6) | collective-permute-done | bytes 589856 | tf_op jit(solution)/shard_map/ppermute | solution.py:232
  28.8 0.7 %collective-permute-start.11 = (bf16[3,96,2048]{2,1,0:T(8,128)(2,1)S(1)}, bf16[3,96,2048]{2,1,0:T(8,128)(2,1)S(1)}, u32[]{:S(2)}, u32[]{:S(2)}) collective-permute-start(bf16[3,96,2048]{2,1,0:T(8,128)(2,1)S(1)} %get-tuple-element.58), channel_id=1, source_target_pairs={{12,8},{28,24},{13,9},{29,25},{14,10},{30,26},{15,11},{31,27}} | collective-permute-start | bytes 3538952 | tf_op jit(solution)/shard_map/ppermute | solution.py:224
  29.5 0.3 weigh.1.scaled_ref
  29.8 1.1 %early.1.refs_5_ = bf16[3,96,2048]{2,1,0:T(8,128)(2,1)} custom-call(bf16[3,48,2048]{2,1,0:T(8,128)(2,1)S(1)} %collective-permute-done.5.shared_ref, bf16[3,48,2048]{2,1,0:T(8,128)(2,1)S(1)} %collective-permute-done.6.swapped_ref), custom_call_target="tpu_custom_call" | custom-call | tf_op jit(solution)/shard_map/early/pallas_call | solution.py:311
  30.8 2.2 %collective-permute-done.9.refs_3_ = bf16[24,1024]{1,0:T(8,128)(2,1)S(1)} collective-permute-done((bf16[24,1024]{1,0:T(8,128)(2,1)S(1)}, bf16[24,1024]{1,0:T(8,128)(2,1)S(1)}, u32[]{:S(2)}, u32[]{:S(2)}) %collective-permute-start.9) | collective-permute-done | bytes 49184 | tf_op jit(solution)/shard_map/ppermute | solution.py:220
  33.0 0.0 collective-permute-done.8.refs_2_
  33.0 0.0 collective-permute-done.7.refs_1_
  33.1 1.1 %combine.1 = (bf16[128,2048]{1,0:T(8,128)(2,1)}, bf16[3,96,2048]{2,1,0:T(8,128)(2,1)}) custom-call(bf16[2,128,256]{2,1,0:T(8,128)(2,1)S(1)} %weigh.1.scaled_ref, bf16[24,1024]{1,0:T(8,128)(2,1)S(1)} %get-tuple-element.50.refs_0_, bf16[24,1024]{1,0:T(8,128)(2,1)S(1)} %collective-permute-done.7.refs_1_, ...), custom_call_target="tpu_custom_call", output_to_operand_aliasing={{1}: (6, {})} | custom-call | flops 12300000256 | bytes 10000 | tf_op jit(solution)/shard_map/combine/pallas_call | solution.py:322
  34.2 0.1 late.1
  (23 shorter events, 0.2 us)
Async XLA Ops:
  0.6 0.7 %copy-start.3 = (s32[128,8]{0,1:T(8,128)S(1)}, s32[128,8]{0,1:T(8,128)}, u32[]{:S(2)}) copy-start(s32[128,8]{0,1:T(8,128)} %param.8) | copy-start | bytes 12292
  0.6 1.1 %copy-start.6 = (bf16[128,2048]{1,0:T(8,128)(2,1)S(1)}, bf16[128,2048]{1,0:T(8,128)(2,1)}, u32[]{:S(2)}) copy-start(bf16[128,2048]{1,0:T(8,128)(2,1)} %tok_ref.1) | copy-start | bytes 1572868
  1.7 2.5 %copy-start = (bf16[192,2048]{1,0:T(8,128)(2,1)S(1)}, bf16[192,2048]{1,0:T(8,128)(2,1)}, u32[]{:S(2)}) copy-start(bf16[192,2048]{1,0:T(8,128)(2,1)} %gate_ref.3) | copy-start | bytes 2359300
  1.7 2.5 %copy-start.1 = (bf16[192,2048]{1,0:T(8,128)(2,1)S(1)}, bf16[192,2048]{1,0:T(8,128)(2,1)}, u32[]{:S(2)}) copy-start(bf16[192,2048]{1,0:T(8,128)(2,1)} %up_ref.3) | copy-start | bytes 2359300
  1.7 2.5 %copy-start.2 = (bf16[192,2048]{1,0:T(8,128)(2,1)S(1)}, bf16[192,2048]{1,0:T(8,128)(2,1)}, u32[]{:S(2)}) copy-start(bf16[192,2048]{1,0:T(8,128)(2,1)} %down_ref.3) | copy-start | bytes 2359300
  1.7 2.5 %copy-start.7 = (s32[2,3,96]{2,0,1:T(2,128)S(1)}, s32[2,3,96]{2,0,1:T(2,128)}, u32[]{:S(2)}) copy-start(s32[2,3,96]{2,0,1:T(2,128)} %param.13) | copy-start | bytes 6916
  2.1 7.2 %collective-permute-start = (bf16[24,1024]{1,0:T(8,128)(2,1)S(1)}, bf16[24,1024]{1,0:T(8,128)(2,1)S(1)}, u32[]{:S(2)}, u32[]{:S(2)}) collective-permute-start(bf16[24,1024]{1,0:T(8,128)(2,1)S(1)} %get-tuple-element.32), channel_id=1, source_target_pairs={{0,8},{4,12},{8,0},{12,4},{16,24},{20,28},{24,16},{28,20},{1,9},{5... | collective-permute-start | bytes 147464 | tf_op jit(solution)/shard_map/ppermute | solution.py:220
  4.3 5.9 %collective-permute-start.2 = (bf16[24,1024]{1,0:T(8,128)(2,1)S(1)}, bf16[24,1024]{1,0:T(8,128)(2,1)S(1)}, u32[]{:S(2)}, u32[]{:S(2)}) collective-permute-start(bf16[24,1024]{1,0:T(8,128)(2,1)S(1)} %get-tuple-element.37), channel_id=1, source_target_pairs={{0,24},{4,28},{8,16},{12,20},{16,8},{20,12},{24,0},{28,4},{1,25},{... | collective-permute-start | bytes 147464 | tf_op jit(solution)/shard_map/ppermute | solution.py:220
  7.0 3.1 %collective-permute-start.1 = (bf16[24,1024]{1,0:T(8,128)(2,1)S(1)}, bf16[24,1024]{1,0:T(8,128)(2,1)S(1)}, u32[]{:S(2)}, u32[]{:S(2)}) collective-permute-start(bf16[24,1024]{1,0:T(8,128)(2,1)S(1)} %get-tuple-element.37), channel_id=1, source_target_pairs={{0,16},{4,20},{8,24},{12,28},{16,0},{20,4},{24,8},{28,12},{1,17},{... | collective-permute-start | bytes 147464 | tf_op jit(solution)/shard_map/ppermute | solution.py:220
  7.2 10.6 %collective-permute-start.5 = (bf16[3,48,2048]{2,1,0:T(8,128)(2,1)S(1)}, bf16[3,48,2048]{2,1,0:T(8,128)(2,1)S(1)}, u32[]{:S(2)}, u32[]{:S(2)}) collective-permute-start(bf16[3,48,2048]{2,1,0:T(8,128)(2,1)S(1)} %select.2), channel_id=1, source_target_pairs={{12,4},{28,20},{13,5},{29,21},{14,6},{30,22},{15,7},{31,23}} | collective-permute-start | bytes 1769480 | tf_op jit(solution)/shard_map/ppermute | solution.py:224
  8.6 24.5 %collective-permute-start.10 = (bf16[3,96,2048]{2,1,0:T(8,128)(2,1)S(1)}, bf16[3,96,2048]{2,1,0:T(8,128)(2,1)S(1)}, u32[]{:S(2)}, u32[]{:S(2)}) collective-permute-start(bf16[3,96,2048]{2,1,0:T(8,128)(2,1)S(1)} %get-tuple-element.49), channel_id=1, source_target_pairs={{12,0},{28,16},{13,1},{29,17},{14,2},{30,18},{15,3},{31,19}} | collective-permute-start | bytes 3538952 | tf_op jit(solution)/shard_map/ppermute | solution.py:224
  10.1 2.4 %collective-permute-start.3 = (bf16[96,1024]{1,0:T(8,128)(2,1)S(1)}, bf16[96,1024]{1,0:T(8,128)(2,1)S(1)}, u32[]{:S(2)}, u32[]{:S(2)}) collective-permute-start(bf16[96,1024]{1,0:T(8,128)(2,1)S(1)} %constant_dynamic-update-slice_fusion.mine_ref), channel_id=1, source_target_pairs={{0,4},{4,0},{8,12},{12,8},{16,20},{20,16},{24,28},{28,24},{1,5},{5... | collective-permute-start | bytes 589832 | tf_op jit(solution)/shard_map/ppermute | solution.py:220
  13.4 16.1 %copy-start.4 = (f32[128,8]{0,1:T(8,128)S(1)}, f32[128,8]{0,1:T(8,128)}, u32[]{:S(2)}) copy-start(f32[128,8]{0,1:T(8,128)} %param.9) | copy-start | bytes 12292
  13.5 1.5 %collective-permute-start.4 = (bf16[96,1024]{1,0:T(8,128)(2,1)S(1)}, bf16[96,1024]{1,0:T(8,128)(2,1)S(1)}, u32[]{:S(2)}, u32[]{:S(2)}) collective-permute-start(bf16[96,1024]{1,0:T(8,128)(2,1)S(1)} %get-tuple-element.38), channel_id=1, source_target_pairs={{0,4},{4,0},{8,12},{12,8},{16,20},{20,16},{24,28},{28,24},{1,5},{5... | collective-permute-start | bytes 589832 | tf_op jit(solution)/shard_map/ppermute | solution.py:220
  17.9 10.9 %collective-permute-start.6 = (bf16[3,48,2048]{2,1,0:T(8,128)(2,1)S(1)}, bf16[3,48,2048]{2,1,0:T(8,128)(2,1)S(1)}, u32[]{:S(2)}, u32[]{:S(2)}) collective-permute-start(bf16[3,48,2048]{2,1,0:T(8,128)(2,1)S(1)} %collective-permute-done.5.shared_ref), channel_id=1, source_target_pairs={{4,5},{20,21},{5,4},{21,20},{6,7},{22,23},{7,6},{23,22}} | collective-permute-start | bytes 1769480 | tf_op jit(solution)/shard_map/ppermute | solution.py:232
  21.1 11.9 %collective-permute-start.9 = (bf16[24,1024]{1,0:T(8,128)(2,1)S(1)}, bf16[24,1024]{1,0:T(8,128)(2,1)S(1)}, u32[]{:S(2)}, u32[]{:S(2)}) collective-permute-start(bf16[24,1024]{1,0:T(8,128)(2,1)S(1)} %get-tuple-element.60), channel_id=1, source_target_pairs={{0,24},{4,28},{8,16},{12,20},{16,8},{20,12},{24,0},{28,4},{1,25},{... | collective-permute-start | bytes 147464 | tf_op jit(solution)/shard_map/ppermute | solution.py:220
  21.2 11.8 %collective-permute-start.8 = (bf16[24,1024]{1,0:T(8,128)(2,1)S(1)}, bf16[24,1024]{1,0:T(8,128)(2,1)S(1)}, u32[]{:S(2)}, u32[]{:S(2)}) collective-permute-start(bf16[24,1024]{1,0:T(8,128)(2,1)S(1)} %get-tuple-element.61), channel_id=1, source_target_pairs={{0,16},{4,20},{8,24},{12,28},{16,0},{20,4},{24,8},{28,12},{1,17},{... | collective-permute-start | bytes 147464 | tf_op jit(solution)/shard_map/ppermute | solution.py:220
  22.5 10.5 %collective-permute-start.7 = (bf16[24,1024]{1,0:T(8,128)(2,1)S(1)}, bf16[24,1024]{1,0:T(8,128)(2,1)S(1)}, u32[]{:S(2)}, u32[]{:S(2)}) collective-permute-start(bf16[24,1024]{1,0:T(8,128)(2,1)S(1)} %get-tuple-element.62), channel_id=1, source_target_pairs={{0,8},{4,12},{8,0},{12,4},{16,24},{20,28},{24,16},{28,20},{1,9},{5... | collective-permute-start | bytes 147464 | tf_op jit(solution)/shard_map/ppermute | solution.py:220
  28.8 5.4 %collective-permute-start.11 = (bf16[3,96,2048]{2,1,0:T(8,128)(2,1)S(1)}, bf16[3,96,2048]{2,1,0:T(8,128)(2,1)S(1)}, u32[]{:S(2)}, u32[]{:S(2)}) collective-permute-start(bf16[3,96,2048]{2,1,0:T(8,128)(2,1)S(1)} %get-tuple-element.58), channel_id=1, source_target_pairs={{12,8},{28,24},{13,9},{29,25},{14,10},{30,26},{15,11},{31,27}} | collective-permute-start | bytes 3538952 | tf_op jit(solution)/shard_map/ppermute | solution.py:224
  33.0 1.1 %copy-start.5 = (f32[8,128]{1,0:T(8,128)S(1)}, f32[8,128]{1,0:T(8,128)}, u32[]{:S(2)}) copy-start(f32[8,128]{1,0:T(8,128)} %begin.1.begun_ref) | copy-start | bytes 12292
